TPU v7x, 32 devices: a whole 2x2x4 slice. The times are simulated.
32 devices in a mesh: pipe: 2 (over x), expert: 16 (over z, y, core).
Axes of the slice: x: 2, y: 2, z: 4, core: 2. Of those that a mesh axis runs over, the one named last changes fastest.
Arguments:
- acts: bfloat16 [2, 2048, 3584], P('pipe', 'expert'), may hold values from -6 to 6
- grad_out: bfloat16 [2, 2048, 3584], P('pipe', 'expert'), may hold values from -6 to 6
- expert_ids: int32 [2, 2048, 2], P('pipe', 'expert'), may hold values from 0 to 7, all different within a row; in each aligned block of 64 rows (0 to 63, 64 to 127, ..., all dimensions but the last counted through in order) at most 24 rows name the same one
- route_weights: float32 [2, 2048, 2], P('pipe', 'expert'), may hold values from 0.1 to 1
- w_gate: bfloat16 [2, 3584, 8192], P('pipe', None, 'expert'), may hold values from -0.09375 to 0.09375
- w_up: bfloat16 [2, 3584, 8192], P('pipe', None, 'expert'), may hold values from -0.09375 to 0.09375
- w_down: bfloat16 [2, 8192, 3584], P('pipe', 'expert'), may hold values from -0.1875 to 0.1875
Outputs:
- out_acts: bfloat16 [2, 2048, 3584], P('pipe', 'expert')
- grad_acts: bfloat16 [2, 2048, 3584], P('pipe', 'expert')
- grad_gate: bfloat16 [2, 3584, 4096], P('pipe', None, 'expert')
- grad_up: bfloat16 [2, 3584, 4096], P('pipe', None, 'expert')
- grad_down: bfloat16 [2, 4096, 3584], P('pipe', 'expert')
Inputs may be any that keep to these rules, and one draw needn't show every extreme that they name: `expert_ids`: in each aligned block of 64 rows of one rank (one micro-batch of one device), no expert is named by more than 24 rows; the 2 experts of a row differ.
All inputs are finite; a program needn't handle non-finite values.
Results may differ from a plain program's by a relative error of at most 0.0072.
Values may be sent and summed in bfloat16 or wider, within the bound.
No kernel may reach another device: no remote copies, remote signals or barrier semaphores. Data moves between devices by JAX's collectives and lax.ppermute only.
A program may use at most 192 MiB of HBM per device.

v0:
```python
import jax
import jax.numpy as jnp
from jax import lax
from jax.sharding import PartitionSpec as P

TOPK = 2
MB = 2
TOK_MB = 64


def expert_half(rows_in, rows_grad, gate_weight, up_weight, down_weight):
    pre_gate = jnp.dot(rows_in, gate_weight, preferred_element_type=jnp.float32)
    pre_up = jnp.dot(rows_in, up_weight, preferred_element_type=jnp.float32)
    sigma = jax.nn.sigmoid(pre_gate)
    active = pre_gate * sigma
    hidden = (active * pre_up).astype(jnp.bfloat16)
    part_out = jnp.dot(hidden, down_weight, preferred_element_type=jnp.float32).astype(jnp.bfloat16)
    hidden_grad = lax.dot_general(
        rows_grad, down_weight, (((1,), (1,)), ((), ())), preferred_element_type=jnp.float32
    )
    gate_grad = (hidden_grad * pre_up * sigma * (1.0 + pre_gate * (1.0 - sigma))).astype(
        jnp.bfloat16
    )
    up_grad = (hidden_grad * active).astype(jnp.bfloat16)
    part_input = lax.dot_general(
        gate_grad, gate_weight, (((1,), (1,)), ((), ())), preferred_element_type=jnp.float32
    )
    part_input = part_input + lax.dot_general(
        up_grad, up_weight, (((1,), (1,)), ((), ())), preferred_element_type=jnp.float32
    )
    grad_gate = lax.dot_general(
        rows_in, gate_grad, (((0,), (0,)), ((), ())), preferred_element_type=jnp.float32
    )
    grad_up = lax.dot_general(
        rows_in, up_grad, (((0,), (0,)), ((), ())), preferred_element_type=jnp.float32
    )
    grad_down = lax.dot_general(
        hidden, rows_grad, (((0,), (0,)), ((), ())), preferred_element_type=jnp.float32
    )
    return (part_out, part_input.astype(jnp.bfloat16), grad_gate, grad_up, grad_down)


def flip_blocks(array, block_count):
    shaped = array.reshape((block_count, array.shape[0] // block_count) + array.shape[1:])
    return jnp.flip(shaped, axis=0).reshape(array.shape)


def on_device(acts, grad_out, expert_ids, route_weights, w_gate, w_up, w_down):
    token_rows = acts[0]
    grad_rows = grad_out[0]
    choice_ids = expert_ids[0]
    choice_gain = route_weights[0]
    gate_weight = w_gate[0]
    up_weight = w_up[0]
    down_weight = w_down[0]
    groups = lax.axis_size("expert")
    expert_count = groups // 2
    capacity = 3 * TOPK * TOK_MB // (2 * expert_count)
    slot_count = expert_count * capacity
    model_width = gate_weight.shape[0]
    unit_count = gate_weight.shape[1]
    rows_dims = (((0,), (0,)), ((), ()))
    slot_dims = (((1,), (0,)), ((), ()))
    slot_range = jnp.arange(slot_count, dtype=jnp.int32)
    expert_range = jnp.arange(expert_count, dtype=jnp.int32)
    acc_gate = jnp.zeros((model_width, unit_count), jnp.float32)
    acc_up = jnp.zeros((model_width, unit_count), jnp.float32)
    acc_down = jnp.zeros((unit_count, model_width), jnp.float32)
    out_pieces = []
    input_pieces = []
    for batch_index in range(MB):
        first_row = batch_index * TOK_MB
        batch_tokens = token_rows[first_row : first_row + TOK_MB]
        batch_grads = grad_rows[first_row : first_row + TOK_MB]
        batch_ids = choice_ids[first_row : first_row + TOK_MB]
        batch_gain = choice_gain[first_row : first_row + TOK_MB]
        flat_ids = batch_ids.reshape(-1)
        member = (flat_ids[:, None] == expert_range[None, :]).astype(jnp.int32)
        running = jnp.cumsum(member, axis=0) - 1
        slot_rank = jnp.sum(member * running, axis=1)
        target = (flat_ids * capacity + slot_rank).reshape(TOK_MB, TOPK)
        matches = (target[:, :, None] == slot_range[None, None, :]).astype(jnp.float32)
        placing = jnp.sum(matches, axis=1)
        weighting = jnp.sum(matches * batch_gain[:, :, None], axis=1)
        slot_tokens = lax.dot_general(
            placing.astype(jnp.bfloat16),
            batch_tokens,
            rows_dims,
            preferred_element_type=jnp.float32,
        ).astype(jnp.bfloat16)
        slot_grads = lax.dot_general(
            weighting,
            batch_grads.astype(jnp.float32),
            rows_dims,
            precision=lax.Precision.HIGHEST,
            preferred_element_type=jnp.float32,
        ).astype(jnp.bfloat16)
        send_tokens = jnp.repeat(
            slot_tokens.reshape(expert_count, capacity, model_width), 2, axis=0
        )
        send_grads = jnp.repeat(slot_grads.reshape(expert_count, capacity, model_width), 2, axis=0)
        recv_tokens, recv_grads = (
            lax.all_to_all(send_tokens, "expert", split_axis=0, concat_axis=0, tiled=True),
            lax.all_to_all(send_grads, "expert", split_axis=0, concat_axis=0, tiled=True),
        )
        part_out, part_input, grad_g, grad_u, grad_d = expert_half(
            recv_tokens.reshape(groups * capacity, model_width),
            recv_grads.reshape(groups * capacity, model_width),
            gate_weight,
            up_weight,
            down_weight,
        )
        back_out, back_input = (
            lax.all_to_all(
                part_out.reshape(groups, capacity, model_width),
                "expert",
                split_axis=0,
                concat_axis=0,
                tiled=True,
            ),
            lax.all_to_all(
                part_input.reshape(groups, capacity, model_width),
                "expert",
                split_axis=0,
                concat_axis=0,
                tiled=True,
            ),
        )
        slot_out = (
            jnp.sum(
                back_out.reshape(expert_count, 2, capacity, model_width).astype(jnp.float32), axis=1
            )
            .astype(jnp.bfloat16)
            .reshape(slot_count, model_width)
        )
        slot_input = (
            jnp.sum(
                back_input.reshape(expert_count, 2, capacity, model_width).astype(jnp.float32),
                axis=1,
            )
            .astype(jnp.bfloat16)
            .reshape(slot_count, model_width)
        )
        acc_gate = acc_gate + grad_g
        acc_up = acc_up + grad_u
        acc_down = acc_down + grad_d
        batch_out = lax.dot_general(
            weighting,
            slot_out.astype(jnp.float32),
            slot_dims,
            precision=lax.Precision.HIGHEST,
            preferred_element_type=jnp.float32,
        )
        batch_input = lax.dot_general(
            placing,
            slot_input.astype(jnp.float32),
            slot_dims,
            precision=lax.Precision.HIGHEST,
            preferred_element_type=jnp.float32,
        )
        out_pieces.append(batch_out.astype(jnp.bfloat16))
        input_pieces.append(batch_input.astype(jnp.bfloat16))
    local_gate = acc_gate.astype(jnp.bfloat16)
    local_up = acc_up.astype(jnp.bfloat16)
    local_down = acc_down.astype(jnp.bfloat16)
    rank_index = lax.axis_index("pipe")
    rank_count = lax.axis_size("pipe")
    kept_half = (rank_index >= rank_count // 2).astype(jnp.int32)
    half_units = unit_count // 2
    own_gate = lax.dynamic_slice_in_dim(local_gate, kept_half * half_units, half_units, 1)
    own_up = lax.dynamic_slice_in_dim(local_up, kept_half * half_units, half_units, 1)
    own_down = lax.dynamic_slice_in_dim(local_down, kept_half * half_units, half_units, 0)
    carried = (
        lax.dynamic_slice_in_dim(local_gate, (1 - kept_half) * half_units, half_units, 1),
        lax.dynamic_slice_in_dim(local_up, (1 - kept_half) * half_units, half_units, 1),
        lax.dynamic_slice_in_dim(local_down, (1 - kept_half) * half_units, half_units, 0),
    )
    spread = (
        lax.all_to_all(carried[0], "pipe", split_axis=0, concat_axis=0, tiled=True),
        lax.all_to_all(carried[1], "pipe", split_axis=0, concat_axis=0, tiled=True),
        lax.all_to_all(carried[2], "pipe", split_axis=0, concat_axis=0, tiled=True),
    )
    flipped = (
        flip_blocks(spread[0], rank_count),
        flip_blocks(spread[1], rank_count),
        flip_blocks(spread[2], rank_count),
    )
    carried = (
        lax.all_to_all(flipped[0], "pipe", split_axis=0, concat_axis=0, tiled=True),
        lax.all_to_all(flipped[1], "pipe", split_axis=0, concat_axis=0, tiled=True),
        lax.all_to_all(flipped[2], "pipe", split_axis=0, concat_axis=0, tiled=True),
    )
    grad_gate = (own_gate.astype(jnp.float32) + carried[0].astype(jnp.float32)).astype(jnp.bfloat16)
    grad_up = (own_up.astype(jnp.float32) + carried[1].astype(jnp.float32)).astype(jnp.bfloat16)
    grad_down = (own_down.astype(jnp.float32) + carried[2].astype(jnp.float32)).astype(jnp.bfloat16)
    out_acts = jnp.concatenate(out_pieces, axis=0)[None]
    grad_acts = jnp.concatenate(input_pieces, axis=0)[None]
    return (out_acts, grad_acts, grad_gate[None], grad_up[None], grad_down[None])


def solution(mesh):
    placed = (
        P("pipe", "expert", None),
        P("pipe", "expert", None),
        P("pipe", "expert", None),
        P("pipe", "expert", None),
        P("pipe", None, "expert"),
        P("pipe", None, "expert"),
        P("pipe", "expert", None),
    )
    return jax.shard_map(
        on_device,
        mesh=mesh,
        in_specs=placed,
        out_specs=(
            P("pipe", "expert", None),
            P("pipe", "expert", None),
            P("pipe", None, "expert"),
            P("pipe", None, "expert"),
            P("pipe", "expert", None),
        ),
        check_vma=False,
    )
```

profile of v0, /device:TPU:0, one launch (start us, length us, event | category | flops | bytes accessed | tf_op | source)
XLA Modules:
  0.0 716.1 jit_solution(3539927835582135330)
XLA Ops:
  9.0 7.4 %all-to-all-start = ((bf16[16,24,3584]{2,1,0:T(8,128)(2,1)}), bf16[16,24,3584]{2,1,0:T(8,128)(2,1)S(1)}, u32[]{:S(2)}, u32[]{:S(2)}) async-start(bf16[16,24,3584]{2,1,0:T(8,128)(2,1)} %bitcast.147), calls=%async_computation | async-start | bytes 5505024 | tf_op jit(solution)/shard_map/all_to_all | solution.py:103
  19.8 49.1 %all-to-all-done = bf16[16,24,3584]{2,1,0:T(8,128)(2,1)S(1)} async-done(((bf16[16,24,3584]{2,1,0:T(8,128)(2,1)}), bf16[16,24,3584]{2,1,0:T(8,128)(2,1)S(1)}, u32[]{:S(2)}, u32[]{:S(2)}) %all-to-all-start) | async-done | bytes 2752544 | tf_op jit(solution)/shard_map/all_to_all | solution.py:103
  73.0 13.9 %all-to-all-start.4 = ((bf16[16,24,3584]{2,1,0:T(8,128)(2,1)}), bf16[16,24,3584]{2,1,0:T(8,128)(2,1)}, u32[]{:S(2)}, u32[]{:S(2)}) async-start(bf16[16,24,3584]{2,1,0:T(8,128)(2,1)} %bitcast.148), calls=%async_computation.4 | async-start | bytes 5505024 | tf_op jit(solution)/shard_map/all_to_all | solution.py:104
  88.5 51.0 %all-to-all-done.4 = bf16[16,24,3584]{2,1,0:T(8,128)(2,1)} async-done(((bf16[16,24,3584]{2,1,0:T(8,128)(2,1)}), bf16[16,24,3584]{2,1,0:T(8,128)(2,1)}, u32[]{:S(2)}, u32[]{:S(2)}) %all-to-all-start.4) | async-done | bytes 2752544 | tf_op jit(solution)/shard_map/all_to_all | solution.py:104
  141.3 13.8 %all-to-all-start.2 = ((bf16[16,24,3584]{2,1,0:T(8,128)(2,1)}), bf16[16,24,3584]{2,1,0:T(8,128)(2,1)S(1)}, u32[]{:S(2)}, u32[]{:S(2)}) async-start(bf16[16,24,3584]{2,1,0:T(8,128)(2,1)} %bitcast.146), calls=%async_computation.2 | async-start | bytes 5505024 | tf_op jit(solution)/shard_map/all_to_all | solution.py:103
  158.5 49.1 %all-to-all-done.2 = bf16[16,24,3584]{2,1,0:T(8,128)(2,1)S(1)} async-done(((bf16[16,24,3584]{2,1,0:T(8,128)(2,1)}), bf16[16,24,3584]{2,1,0:T(8,128)(2,1)S(1)}, u32[]{:S(2)}, u32[]{:S(2)}) %all-to-all-start.2) | async-done | bytes 2752544 | tf_op jit(solution)/shard_map/all_to_all | solution.py:103
  210.8 14.1 %all-to-all-start.6 = ((bf16[16,24,3584]{2,1,0:T(8,128)(2,1)}), bf16[16,24,3584]{2,1,0:T(8,128)(2,1)}, u32[]{:S(2)}, u32[]{:S(2)}) async-start(bf16[16,24,3584]{2,1,0:T(8,128)(2,1)} %bitcast.143), calls=%async_computation.6 | async-start | bytes 5505024 | tf_op jit(solution)/shard_map/all_to_all | solution.py:104
  235.4 7.0 fusion.45
  247.4 30.1 %all-to-all-done.6 = bf16[16,24,3584]{2,1,0:T(8,128)(2,1)} async-done(((bf16[16,24,3584]{2,1,0:T(8,128)(2,1)}), bf16[16,24,3584]{2,1,0:T(8,128)(2,1)}, u32[]{:S(2)}, u32[]{:S(2)}) %all-to-all-start.6) | async-done | bytes 2752544 | tf_op jit(solution)/shard_map/all_to_all | solution.py:104
  277.5 6.0 multiply_convert_fusion
  283.5 6.1 add_convert_fusion
  292.8 4.9 all-to-all-start.12
  303.9 5.1 fusion.43
  310.4 10.7 %all-to-all-done.12 = bf16[2,128,3584]{2,1,0:T(8,128)(2,1)} async-done(((bf16[2,128,3584]{2,1,0:T(8,128)(2,1)}), bf16[2,128,3584]{2,1,0:T(8,128)(2,1)}, u32[]{:S(2)}, u32[]{:S(2)}) %all-to-all-start.12) | async-done | bytes 1835040 | tf_op jit(solution)/shard_map/all_to_all | solution.py:181
  321.1 4.7 all-to-all-start.10
  325.8 5.3 add_convert_fusion.2
  334.3 14.0 %all-to-all-done.10 = bf16[2,1792,256]{2,1,0:T(8,128)(2,1)} async-done(((bf16[2,1792,256]{2,1,0:T(8,128)(2,1)}), bf16[2,1792,256]{2,1,0:T(8,128)(2,1)}, u32[]{:S(2)}, u32[]{:S(2)}) %all-to-all-start.10) | async-done | bytes 1835040 | tf_op jit(solution)/shard_map/all_to_all | solution.py:180
  354.8 18.7 %all-to-all-done.8 = bf16[2,1792,256]{2,1,0:T(8,128)(2,1)S(1)} async-done(((bf16[2,1792,256]{2,1,0:T(8,128)(2,1)}), bf16[2,1792,256]{2,1,0:T(8,128)(2,1)S(1)}, u32[]{:S(2)}, u32[]{:S(2)}) %all-to-all-start.8) | async-done | bytes 1835040 | tf_op jit(solution)/shard_map/all_to_all | solution.py:179
  381.0 17.8 %all-to-all-done.13 = bf16[2,128,3584]{2,1,0:T(8,128)(2,1)} async-done(((bf16[2,128,3584]{2,1,0:T(8,128)(2,1)}), bf16[2,128,3584]{2,1,0:T(8,128)(2,1)}, u32[]{:S(2)}, u32[]{:S(2)}) %all-to-all-start.13) | async-done | bytes 1835040 | tf_op jit(solution)/shard_map/all_to_all | solution.py:191
  398.9 4.7 all-to-all-start.11
  405.0 18.4 %all-to-all-done.11 = bf16[2,1792,256]{2,1,0:T(8,128)(2,1)} async-done(((bf16[2,1792,256]{2,1,0:T(8,128)(2,1)}), bf16[2,1792,256]{2,1,0:T(8,128)(2,1)}, u32[]{:S(2)}, u32[]{:S(2)}) %all-to-all-start.11) | async-done | bytes 1835040 | tf_op jit(solution)/shard_map/all_to_all | solution.py:190
  434.1 11.7 %all-to-all-done.9 = bf16[2,1792,256]{2,1,0:T(8,128)(2,1)S(1)} async-done(((bf16[2,1792,256]{2,1,0:T(8,128)(2,1)}), bf16[2,1792,256]{2,1,0:T(8,128)(2,1)S(1)}, u32[]{:S(2)}, u32[]{:S(2)}) %all-to-all-start.9) | async-done | bytes 1835040 | tf_op jit(solution)/shard_map/all_to_all | solution.py:189
  447.1 11.3 %all-to-all-start.5 = ((bf16[16,24,3584]{2,1,0:T(8,128)(2,1)}), bf16[16,24,3584]{2,1,0:T(8,128)(2,1)S(1)}, u32[]{:S(2)}, u32[]{:S(2)}) async-start(bf16[16,24,3584]{2,1,0:T(8,128)(2,1)} %bitcast.144), calls=%async_computation.5 | async-start | bytes 5505024 | tf_op jit(solution)/shard_map/all_to_all | solution.py:121
  465.3 45.5 %all-to-all-done.5 = bf16[16,24,3584]{2,1,0:T(8,128)(2,1)S(1)} async-done(((bf16[16,24,3584]{2,1,0:T(8,128)(2,1)}), bf16[16,24,3584]{2,1,0:T(8,128)(2,1)S(1)}, u32[]{:S(2)}, u32[]{:S(2)}) %all-to-all-start.5) | async-done | bytes 2752544 | tf_op jit(solution)/shard_map/all_to_all | solution.py:121
  510.8 14.0 %all-to-all-start.7 = ((bf16[16,24,3584]{2,1,0:T(8,128)(2,1)}), bf16[16,24,3584]{2,1,0:T(8,128)(2,1)}, u32[]{:S(2)}, u32[]{:S(2)}) async-start(bf16[16,24,3584]{2,1,0:T(8,128)(2,1)} %bitcast.145), calls=%async_computation.7 | async-start | bytes 5505024 | tf_op jit(solution)/shard_map/all_to_all | solution.py:121
  524.9 5.2 convolution_convert_fusion.1
  530.1 47.4 %all-to-all-done.7 = bf16[16,24,3584]{2,1,0:T(8,128)(2,1)} async-done(((bf16[16,24,3584]{2,1,0:T(8,128)(2,1)}), bf16[16,24,3584]{2,1,0:T(8,128)(2,1)}, u32[]{:S(2)}, u32[]{:S(2)}) %all-to-all-start.7) | async-done | bytes 2752544 | tf_op jit(solution)/shard_map/all_to_all | solution.py:121
  577.4 14.0 %all-to-all-start.1 = ((bf16[16,24,3584]{2,1,0:T(8,128)(2,1)}), bf16[16,24,3584]{2,1,0:T(8,128)(2,1)}, u32[]{:S(2)}, u32[]{:S(2)}) async-start(bf16[16,24,3584]{2,1,0:T(8,128)(2,1)} %bitcast.161), calls=%async_computation.1 | async-start | bytes 5505024 | tf_op jit(solution)/shard_map/all_to_all | solution.py:114
  591.5 5.1 convolution_convert_fusion
  596.6 47.4 %all-to-all-done.1 = bf16[16,24,3584]{2,1,0:T(8,128)(2,1)} async-done(((bf16[16,24,3584]{2,1,0:T(8,128)(2,1)}), bf16[16,24,3584]{2,1,0:T(8,128)(2,1)}, u32[]{:S(2)}, u32[]{:S(2)}) %all-to-all-start.1) | async-done | bytes 2752544 | tf_op jit(solution)/shard_map/all_to_all | solution.py:114
  644.0 13.9 %all-to-all-start.3 = ((bf16[16,24,3584]{2,1,0:T(8,128)(2,1)}), bf16[16,24,3584]{2,1,0:T(8,128)(2,1)}, u32[]{:S(2)}, u32[]{:S(2)}) async-start(bf16[16,24,3584]{2,1,0:T(8,128)(2,1)} %bitcast.160), calls=%async_computation.3 | async-start | bytes 5505024 | tf_op jit(solution)/shard_map/all_to_all | solution.py:114
  674.8 35.7 %all-to-all-done.3 = bf16[16,24,3584]{2,1,0:T(8,128)(2,1)} async-done(((bf16[16,24,3584]{2,1,0:T(8,128)(2,1)}), bf16[16,24,3584]{2,1,0:T(8,128)(2,1)}, u32[]{:S(2)}, u32[]{:S(2)}) %all-to-all-start.3) | async-done | bytes 2752544 | tf_op jit(solution)/shard_map/all_to_all | solution.py:114
  (119 shorter events, 110.9 us)
Async XLA Ops:
  5.1 11.3 %copy-start.21 = (f32[64,192]{1,0:T(8,128)}, f32[64,192]{1,0:T(8,128)S(1)}, u32[]{:S(2)}) copy-start(f32[64,192]{1,0:T(8,128)S(1)} %get-tuple-element.21) | copy-start | bytes 147460
  5.1 81.8 %copy-start.23 = (f32[64,192]{1,0:T(8,128)}, f32[64,192]{1,0:T(8,128)S(1)}, u32[]{:S(2)}) copy-start(f32[64,192]{1,0:T(8,128)S(1)} %get-tuple-element.7) | copy-start | bytes 147460
  5.1 150.0 %copy-start.19 = (f32[64,192]{1,0:T(8,128)}, f32[64,192]{1,0:T(8,128)S(1)}, u32[]{:S(2)}) copy-start(f32[64,192]{1,0:T(8,128)S(1)} %get-tuple-element.8) | copy-start | bytes 147460
  9.0 59.9 %all-to-all-start = ((bf16[16,24,3584]{2,1,0:T(8,128)(2,1)}), bf16[16,24,3584]{2,1,0:T(8,128)(2,1)S(1)}, u32[]{:S(2)}, u32[]{:S(2)}) async-start(bf16[16,24,3584]{2,1,0:T(8,128)(2,1)} %bitcast.147), calls=%async_computation | async-start | bytes 5505024 | tf_op jit(solution)/shard_map/all_to_all | solution.py:103
  68.9 4.1 copy-start.4
  73.0 66.5 %all-to-all-start.4 = ((bf16[16,24,3584]{2,1,0:T(8,128)(2,1)}), bf16[16,24,3584]{2,1,0:T(8,128)(2,1)}, u32[]{:S(2)}, u32[]{:S(2)}) async-start(bf16[16,24,3584]{2,1,0:T(8,128)(2,1)} %bitcast.148), calls=%async_computation.4 | async-start | bytes 5505024 | tf_op jit(solution)/shard_map/all_to_all | solution.py:104
  141.3 66.4 %all-to-all-start.2 = ((bf16[16,24,3584]{2,1,0:T(8,128)(2,1)}), bf16[16,24,3584]{2,1,0:T(8,128)(2,1)S(1)}, u32[]{:S(2)}, u32[]{:S(2)}) async-start(bf16[16,24,3584]{2,1,0:T(8,128)(2,1)} %bitcast.146), calls=%async_computation.2 | async-start | bytes 5505024 | tf_op jit(solution)/shard_map/all_to_all | solution.py:103
  210.8 66.6 %all-to-all-start.6 = ((bf16[16,24,3584]{2,1,0:T(8,128)(2,1)}), bf16[16,24,3584]{2,1,0:T(8,128)(2,1)}, u32[]{:S(2)}, u32[]{:S(2)}) async-start(bf16[16,24,3584]{2,1,0:T(8,128)(2,1)} %bitcast.143), calls=%async_computation.6 | async-start | bytes 5505024 | tf_op jit(solution)/shard_map/all_to_all | solution.py:104
  224.9 4.6 copy-start.5
  224.9 4.8 copy-start.8
  235.4 7.1 copy-start.27
  235.4 7.1 copy-start.9
  283.5 6.2 copy-start.17
  292.8 28.2 %all-to-all-start.12 = ((bf16[2,128,3584]{2,1,0:T(8,128)(2,1)}), bf16[2,128,3584]{2,1,0:T(8,128)(2,1)}, u32[]{:S(2)}, u32[]{:S(2)}) async-start(bf16[2,128,3584]{2,1,0:T(8,128)(2,1)} %bitcast.151), calls=%async_computation.12 | async-start | bytes 3670016 | tf_op jit(solution)/shard_map/all_to_all | solution.py:181
  297.8 3.9 copy-start.14
  303.9 5.1 copy-start
  321.1 27.2 %all-to-all-start.10 = ((bf16[2,1792,256]{2,1,0:T(8,128)(2,1)}), bf16[2,1792,256]{2,1,0:T(8,128)(2,1)}, u32[]{:S(2)}, u32[]{:S(2)}) async-start(bf16[2,1792,256]{2,1,0:T(8,128)(2,1)} %bitcast.149), calls=%async_computation.10 | async-start | bytes 3670016 | tf_op jit(solution)/shard_map/all_to_all | solution.py:180
  348.3 25.2 %all-to-all-start.8 = ((bf16[2,1792,256]{2,1,0:T(8,128)(2,1)}), bf16[2,1792,256]{2,1,0:T(8,128)(2,1)S(1)}, u32[]{:S(2)}, u32[]{:S(2)}) async-start(bf16[2,1792,256]{2,1,0:T(8,128)(2,1)} %bitcast.150), calls=%async_computation.8 | async-start | bytes 3670016 | tf_op jit(solution)/shard_map/all_to_all | solution.py:179
  373.5 25.4 %all-to-all-start.13 = ((bf16[2,128,3584]{2,1,0:T(8,128)(2,1)}), bf16[2,128,3584]{2,1,0:T(8,128)(2,1)}, u32[]{:S(2)}, u32[]{:S(2)}) async-start(bf16[2,128,3584]{2,1,0:T(8,128)(2,1)} %all_to_all.78), calls=%async_computation.13 | async-start | bytes 3670016 | tf_op jit(solution)/shard_map/all_to_all | solution.py:191
  398.9 24.5 %all-to-all-start.11 = ((bf16[2,1792,256]{2,1,0:T(8,128)(2,1)}), bf16[2,1792,256]{2,1,0:T(8,128)(2,1)}, u32[]{:S(2)}, u32[]{:S(2)}) async-start(bf16[2,1792,256]{2,1,0:T(8,128)(2,1)} %all_to_all.74), calls=%async_computation.11 | async-start | bytes 3670016 | tf_op jit(solution)/shard_map/all_to_all | solution.py:190
  423.4 22.5 %all-to-all-start.9 = ((bf16[2,1792,256]{2,1,0:T(8,128)(2,1)}), bf16[2,1792,256]{2,1,0:T(8,128)(2,1)S(1)}, u32[]{:S(2)}, u32[]{:S(2)}) async-start(bf16[2,1792,256]{2,1,0:T(8,128)(2,1)} %all_to_all.70), calls=%async_computation.9 | async-start | bytes 3670016 | tf_op jit(solution)/shard_map/all_to_all | solution.py:189
  445.8 12.5 %copy-start.16 = (bf16[384,512]{1,0:T(8,128)(2,1)S(1)}, bf16[384,512]{1,0:T(8,128)(2,1)}, u32[]{:S(2)}) copy-start(bf16[384,512]{1,0:T(8,128)(2,1)} %get-tuple-element.13) | copy-start | bytes 1179652
  447.1 63.8 %all-to-all-start.5 = ((bf16[16,24,3584]{2,1,0:T(8,128)(2,1)}), bf16[16,24,3584]{2,1,0:T(8,128)(2,1)S(1)}, u32[]{:S(2)}, u32[]{:S(2)}) async-start(bf16[16,24,3584]{2,1,0:T(8,128)(2,1)} %bitcast.144), calls=%async_computation.5 | async-start | bytes 5505024 | tf_op jit(solution)/shard_map/all_to_all | solution.py:121
  458.3 3.8 copy-start.11
  458.3 3.8 copy-start.15
  510.8 14.0 %copy-start.28 = (bf16[384,512]{1,0:T(8,128)(2,1)S(1)}, bf16[384,512]{1,0:T(8,128)(2,1)}, u32[]{:S(2)}) copy-start(bf16[384,512]{1,0:T(8,128)(2,1)} %copy-done.27) | copy-start | bytes 1179652
  510.8 66.6 %all-to-all-start.7 = ((bf16[16,24,3584]{2,1,0:T(8,128)(2,1)}), bf16[16,24,3584]{2,1,0:T(8,128)(2,1)}, u32[]{:S(2)}, u32[]{:S(2)}) async-start(bf16[16,24,3584]{2,1,0:T(8,128)(2,1)} %bitcast.145), calls=%async_computation.7 | async-start | bytes 5505024 | tf_op jit(solution)/shard_map/all_to_all | solution.py:121
  577.4 14.0 %copy-start.18 = (bf16[384,512]{1,0:T(8,128)(2,1)S(1)}, bf16[384,512]{1,0:T(8,128)(2,1)}, u32[]{:S(2)}) copy-start(bf16[384,512]{1,0:T(8,128)(2,1)} %copy-done.17) | copy-start | bytes 1179652
  577.4 66.6 %all-to-all-start.1 = ((bf16[16,24,3584]{2,1,0:T(8,128)(2,1)}), bf16[16,24,3584]{2,1,0:T(8,128)(2,1)}, u32[]{:S(2)}, u32[]{:S(2)}) async-start(bf16[16,24,3584]{2,1,0:T(8,128)(2,1)} %bitcast.161), calls=%async_computation.1 | async-start | bytes 5505024 | tf_op jit(solution)/shard_map/all_to_all | solution.py:114
  644.0 66.5 %all-to-all-start.3 = ((bf16[16,24,3584]{2,1,0:T(8,128)(2,1)}), bf16[16,24,3584]{2,1,0:T(8,128)(2,1)}, u32[]{:S(2)}, u32[]{:S(2)}) async-start(bf16[16,24,3584]{2,1,0:T(8,128)(2,1)} %bitcast.160), calls=%async_computation.3 | async-start | bytes 5505024 | tf_op jit(solution)/shard_map/all_to_all | solution.py:114
  658.0 3.9 copy-start.1
  674.0 38.9 %copy-start.20 = (f32[64,192]{1,0:T(8,128)S(1)}, f32[64,192]{1,0:T(8,128)}, u32[]{:S(2)}) copy-start(f32[64,192]{1,0:T(8,128)} %copy-done.19) | copy-start | bytes 147460
  (12 other events, 27.7 us)
where the time goes:
time: 730 us; the launch traced here: 716 us
  waiting for transfers between devices  447 us (61%)
  starting transfers between devices  129 us (18%)
  matrix products  87.9 us (12%)
  local copies, waits for them, and re-layouts  30.6 us (4%)
  other arithmetic  20.3 us (3%)
    all_to_all x2, waiting for transfers between devices, on_device(): lax.all_to_all(send_tokens, 'expert', split_axis=0, concat_axis=0, tiled=...  98.3 us
    all_to_all x2, waiting for transfers between devices, on_device(): lax.all_to_all(part_input.reshape(groups, capacity, model_width), 'expert...  92.9 us
    all_to_all x2, waiting for transfers between devices, on_device(): lax.all_to_all(part_out.reshape(groups, capacity, model_width), 'expert',...  83.2 us
    all_to_all x2, waiting for transfers between devices, on_device(): lax.all_to_all(send_grads, 'expert', split_axis=0, concat_axis=0, tiled=T...  81.1 us
    all_to_all x2, starting transfers between devices, on_device(): lax.all_to_all(send_grads, 'expert', split_axis=0, concat_axis=0, tiled=T...  28 us
    all_to_all x2, starting transfers between devices, on_device(): lax.all_to_all(part_out.reshape(groups, capacity, model_width), 'expert',...  27.9 us
    all_to_all x2, starting transfers between devices, on_device(): lax.all_to_all(part_input.reshape(groups, capacity, model_width), 'expert...  25.3 us
    all_to_all x2, starting transfers between devices, on_device(): lax.all_to_all(send_tokens, 'expert', split_axis=0, concat_axis=0, tiled=...  21.2 us
  transfers between devices with their start and end apart: 14, of which 14 were waited for; matrix products, arithmetic and copies ran while one was open for 13% of the time, Pallas kernels for 0%

commit v1 on v0

v1 whole, which is shorter than its diff:
```python
import jax
import jax.numpy as jnp
from jax import lax
from jax.sharding import PartitionSpec as P

TOPK = 2
MB = 2
TOK_MB = 64
F32 = jnp.float32
BF16 = jnp.bfloat16


def dot(a, b, dims):
    return lax.dot_general(a, b, (dims, ((), ())), preferred_element_type=F32)


def route(ids, gain, expert_count, capacity):
    flat_ids = ids.reshape(-1)
    member = (flat_ids[:, None] == jnp.arange(expert_count, dtype=jnp.int32)[None, :]).astype(jnp.int32)
    running = jnp.cumsum(member, axis=0) - 1
    slot_rank = jnp.sum(member * running, axis=1)
    target = (flat_ids * capacity + slot_rank).reshape(ids.shape)
    slots = jnp.arange(expert_count * capacity, dtype=jnp.int32)
    matches = (target[:, :, None] == slots[None, None, :]).astype(F32)
    placing = jnp.sum(matches, axis=1).astype(BF16)
    weighting = jnp.sum(matches * gain[:, :, None], axis=1)
    return placing, weighting, jnp.sum(weighting, axis=0)


def on_device(acts, grad_out, expert_ids, route_weights, w_gate, w_up, w_down):
    gate_weight, up_weight, down_weight = w_gate[0], w_up[0], w_down[0]
    devices = lax.axis_size("expert")
    chips = devices // 2
    capacity = 3 * TOPK * TOK_MB // (2 * chips)
    slot_count = chips * capacity
    width = gate_weight.shape[0]
    half_units = gate_weight.shape[1] // 2
    same_core = [[2 * chip + core for chip in range(chips)] for core in range(2)]
    other_core = [(i, i ^ 1) for i in range(devices)]

    def across(blocks):
        moved = lax.all_to_all(
            blocks.reshape(chips, capacity, width),
            "expert",
            split_axis=0,
            concat_axis=0,
            axis_index_groups=same_core,
            tiled=True,
        )
        return moved.reshape(slot_count, width)

    def swap(rows):
        return lax.ppermute(rows, "expert", other_core)

    rows_in, rows_grad, hiddens, gate_grads, up_grads = [], [], [], [], []
    routes, outs, inputs = [], [], []
    for b in range(MB):
        rows = slice(b * TOK_MB, (b + 1) * TOK_MB)
        placing, weighting, slot_gain = route(
            expert_ids[0, rows], route_weights[0, rows], chips, capacity
        )
        routes.append((placing, weighting))
        tokens = dot(placing, acts[0, rows], ((0,), (0,))).astype(BF16)
        grads = dot(placing, grad_out[0, rows], ((0,), (0,)))
        grads = (grads * slot_gain[:, None]).astype(BF16)
        tokens = across(tokens)
        rows_in.append([tokens, swap(tokens)])
        grads = across(grads)
        rows_grad.append([grads, swap(grads)])

    for b in range(MB):
        part_out, part_input = [], []
        hiddens.append([])
        gate_grads.append([])
        up_grads.append([])
        for tokens, grads in zip(rows_in[b], rows_grad[b]):
            pre_gate = dot(tokens, gate_weight, ((1,), (0,)))
            pre_up = dot(tokens, up_weight, ((1,), (0,)))
            sigma = jax.nn.sigmoid(pre_gate)
            active = pre_gate * sigma
            hidden = (active * pre_up).astype(BF16)
            part_out.append(dot(hidden, down_weight, ((1,), (0,))).astype(BF16))
            hidden_grad = dot(grads, down_weight, ((1,), (1,)))
            gate_grad = (
                hidden_grad * pre_up * sigma * (1.0 + pre_gate * (1.0 - sigma))
            ).astype(BF16)
            up_grad = (hidden_grad * active).astype(BF16)
            part_input.append(
                (
                    dot(gate_grad, gate_weight, ((1,), (1,)))
                    + dot(up_grad, up_weight, ((1,), (1,)))
                ).astype(BF16)
            )
            hiddens[b].append(hidden)
            gate_grads[b].append(gate_grad)
            up_grads[b].append(up_grad)
        back = []
        for own, other in (part_out, part_input):
            both = (own.astype(F32) + swap(other).astype(F32)).astype(BF16)
            back.append(across(both))
        placing, weighting = routes[b]
        outs.append(
            lax.dot_general(
                weighting,
                back[0].astype(F32),
                (((1,), (0,)), ((), ())),
                precision=lax.Precision.HIGHEST,
                preferred_element_type=F32,
            ).astype(BF16)
        )
        inputs.append(dot(placing, back[1], ((1,), (0,))).astype(BF16))

    rank_index = lax.axis_index("pipe")
    rank_count = lax.axis_size("pipe")
    mirror = [(p, rank_count - 1 - p) for p in range(rank_count)]
    kept_half = (rank_index >= rank_count // 2).astype(jnp.int32)

    def joined(parts):
        return jnp.concatenate([part for batch in parts for part in batch], axis=0)

    def halves(units):
        return (
            lax.dynamic_slice_in_dim(units, kept_half * half_units, half_units, 1),
            lax.dynamic_slice_in_dim(units, (1 - kept_half) * half_units, half_units, 1),
        )

    all_in = joined(rows_in)
    all_grad = joined(rows_grad)
    keep_hidden, send_hidden = halves(joined(hiddens))
    keep_gate, send_gate = halves(joined(gate_grads))
    keep_up, send_up = halves(joined(up_grads))
    rows_dims = ((0,), (0,))
    sent = [
        lax.ppermute(dot(a, b, rows_dims).astype(BF16), "pipe", mirror)
        for a, b in ((send_hidden, all_grad), (all_in, send_gate), (all_in, send_up))
    ]
    kept = [
        dot(a, b, rows_dims).astype(BF16)
        for a, b in ((keep_hidden, all_grad), (all_in, keep_gate), (all_in, keep_up))
    ]
    grad_down, grad_gate, grad_up = [
        (own.astype(F32) + other.astype(F32)).astype(BF16)[None] for own, other in zip(kept, sent)
    ]
    out_acts = jnp.concatenate(outs, axis=0)[None]
    grad_acts = jnp.concatenate(inputs, axis=0)[None]
    return out_acts, grad_acts, grad_gate, grad_up, grad_down


def solution(mesh):
    tokens = P("pipe", "expert", None)
    columns = P("pipe", None, "expert")
    return jax.shard_map(
        on_device,
        mesh=mesh,
        in_specs=(tokens, tokens, tokens, tokens, columns, columns, tokens),
        out_specs=(tokens, tokens, columns, columns, tokens),
        check_vma=False,
    )
```

time: 730 us -> 379 us (0.52); the launches traced: 716 us -> 378 us
  waiting for transfers between devices: 447 us -> 225 us
  starting transfers between devices: 129 us -> 41.1 us
  local copies, waits for them, and re-layouts: 30.6 us -> 10.4 us
  other arithmetic: 20.3 us -> 6.78 us
    all_to_all x14 -> x8, waiting for transfers between devices: 447 us -> 172 us  [across(): lax.all_to_all(blocks.reshape(chips, capacity, width), 'expert', split_ax...]
    all_to_all x14 -> x8, starting transfers between devices: 129 us -> 36 us  [across(): lax.all_to_all(blocks.reshape(chips, capacity, width), 'expert', split_ax...]
    ppermute x0 -> x11, waiting for transfers between devices: none -> 53.1 us  [the longest x3 53 us: on_device(): lax.ppermute(dot(a, b, rows_dims).astype(BF16), 'pipe', mirror)]
    broadcast_in_dim x4 -> x0, local copies, waits for them, and re-layouts: 10.8 us -> none  [the longest x2 7.29 us: on_device(): jnp.repeat(slot_grads.reshape(expert_count, capacity, model_width), 2, ax...]
    broadcast_in_dim x5 -> x2, other arithmetic: 11.1 us -> 1.97 us  [the longest x1 0.99 us: on_device(): out_acts = jnp.concatenate(outs, axis=0)[None]]
    dot_general x26 -> x38, matrix products: 87.9 us -> 93.1 us  [the longest x36 88.8 us: dot(): return lax.dot_general(a, b, (dims, ((), ())), preferred_element_type=F32)]
  transfers between devices with their start and end apart: 14 -> 19, of which waited for: 14 -> 10; matrix products, arithmetic and copies ran while one was open for 13% -> 24% of each run, Pallas kernels for 0% -> 0%
where the time goes in v1:
time: 379 us; the launch traced here: 378 us
  waiting for transfers between devices  225 us (59%)
  matrix products  93.1 us (25%)
  starting transfers between devices  41.1 us (11%)
  local copies, waits for them, and re-layouts  10.4 us (3%)
  other arithmetic  6.78 us (2%)
    all_to_all x8, waiting for transfers between devices, across(): lax.all_to_all(blocks.reshape(chips, capacity, width), 'expert', split_ax...  172 us
    dot_general x36, matrix products, dot(): return lax.dot_general(a, b, (dims, ((), ())), preferred_element_type=F32)  88.8 us
    ppermute x3, waiting for transfers between devices, on_device(): lax.ppermute(dot(a, b, rows_dims).astype(BF16), 'pipe', mirror)  53 us
    all_to_all x8, starting transfers between devices, across(): lax.all_to_all(blocks.reshape(chips, capacity, width), 'expert', split_ax...  36 us
    unnamed x86, local copies, waits for them, and re-layouts  7.85 us
  transfers between devices with their start and end apart: 19, of which 10 were waited for; matrix products, arithmetic and copies ran while one was open for 24% of the time, Pallas kernels for 0%

profile of v1, /device:TPU:0, one launch (start us, length us, event | category | flops | bytes accessed | tf_op | source)
XLA Modules:
  0.0 377.9 jit_solution(979129887682600344)
XLA Ops:
  5.7 2.7 fusion.9
  8.4 7.3 %all-to-all-start.4 = ((bf16[8,24,3584]{2,1,0:T(8,128)(2,1)}), bf16[8,24,3584]{2,1,0:T(8,128)(2,1)S(1)}, u32[]{:S(2)}, u32[]{:S(2)}) async-start(bf16[8,24,3584]{2,1,0:T(8,128)(2,1)} %bitcast.19), calls=%async_computation.4 | async-start | bytes 2752512 | tf_op jit(solution)/shard_map/all_to_all | solution.py:42
  17.3 31.1 %all-to-all-done.4 = bf16[8,24,3584]{2,1,0:T(8,128)(2,1)S(1)} async-done(((bf16[8,24,3584]{2,1,0:T(8,128)(2,1)}), bf16[8,24,3584]{2,1,0:T(8,128)(2,1)S(1)}, u32[]{:S(2)}, u32[]{:S(2)}) %all-to-all-start.4) | async-done | bytes 1376288 | tf_op jit(solution)/shard_map/all_to_all | solution.py:42
  49.6 3.6 all-to-all-start
  54.8 31.3 %all-to-all-done = bf16[8,24,3584]{2,1,0:T(8,128)(2,1)S(1)} async-done(((bf16[8,24,3584]{2,1,0:T(8,128)(2,1)}), bf16[8,24,3584]{2,1,0:T(8,128)(2,1)S(1)}, u32[]{:S(2)}, u32[]{:S(2)}) %all-to-all-start) | async-done | bytes 1376288 | tf_op jit(solution)/shard_map/all_to_all | solution.py:42
  86.2 3.6 all-to-all-start.6
  89.8 2.6 convolution_convert_fusion.8
  92.5 30.3 %all-to-all-done.6 = bf16[8,24,3584]{2,1,0:T(8,128)(2,1)S(1)} async-done(((bf16[8,24,3584]{2,1,0:T(8,128)(2,1)}), bf16[8,24,3584]{2,1,0:T(8,128)(2,1)S(1)}, u32[]{:S(2)}, u32[]{:S(2)}) %all-to-all-start.6) | async-done | bytes 1376288 | tf_op jit(solution)/shard_map/all_to_all | solution.py:42
  123.9 3.8 all-to-all-start.2
  128.3 32.2 %all-to-all-done.2 = bf16[8,24,3584]{2,1,0:T(8,128)(2,1)S(1)} async-done(((bf16[8,24,3584]{2,1,0:T(8,128)(2,1)}), bf16[8,24,3584]{2,1,0:T(8,128)(2,1)S(1)}, u32[]{:S(2)}, u32[]{:S(2)}) %all-to-all-start.2) | async-done | bytes 1376288 | tf_op jit(solution)/shard_map/all_to_all | solution.py:42
  160.5 3.5 fusion.44
  174.6 3.5 multiply_convert_fusion.4
  182.6 3.5 multiply_convert_fusion
  189.9 4.6 %all-to-all-start.5 = ((bf16[8,24,3584]{2,1,0:T(8,128)(2,1)}), bf16[8,24,3584]{2,1,0:T(8,128)(2,1)}, u32[]{:S(2)}, u32[]{:S(2)}) async-start(bf16[8,24,3584]{2,1,0:T(8,128)(2,1)} %bitcast.163), calls=%async_computation.5 | async-start | bytes 2752512 | tf_op jit(solution)/shard_map/all_to_all | solution.py:42
  194.6 3.5 fusion.16
  207.9 20.2 %all-to-all-done.5 = bf16[8,24,3584]{2,1,0:T(8,128)(2,1)} async-done(((bf16[8,24,3584]{2,1,0:T(8,128)(2,1)}), bf16[8,24,3584]{2,1,0:T(8,128)(2,1)}, u32[]{:S(2)}, u32[]{:S(2)}) %all-to-all-start.5) | async-done | bytes 1376288 | tf_op jit(solution)/shard_map/all_to_all | solution.py:42
  228.1 4.3 %all-to-all-start.7 = ((bf16[8,24,3584]{2,1,0:T(8,128)(2,1)}), bf16[8,24,3584]{2,1,0:T(8,128)(2,1)}, u32[]{:S(2)}, u32[]{:S(2)}) async-start(bf16[8,24,3584]{2,1,0:T(8,128)(2,1)} %bitcast.26), calls=%async_computation.7 | async-start | bytes 2752512 | tf_op jit(solution)/shard_map/all_to_all | solution.py:42
  232.4 4.3 %convolution_convert_fusion.9 = bf16[192,3584]{1,0:T(8,128)(2,1)} fusion(bf16[192,512]{1,0:T(8,128)(2,1)} %get-tuple-element.13, bf16[1,512,3584]{2,1,0:T(8,128)(2,1)} %param.13), kind=kOutput, calls=%fused_computation.35 | convolution fusion | flops 705331200 | bytes 5242880 | tf_op jit(solution)/shard_map/dot_general | solution.py:14
  238.0 4.4 %convolution_convert_fusion.2 = bf16[3584,256]{1,0:T(8,128)(2,1)} fusion(bf16[768,512]{1,0:T(8,128)(2,1)S(1)} %pad_maximum_fusion.5, s32[]{:T(128)S(6)} %select_n.2, bf16[192,3584]{1,0:T(8,128)(2,1)} %copy-done.13, bf16[192,3584]{1,0:T(8,128)(2,1)S(1)} %bitcast.159, bf16[192,3584]{1,0:T(8,128)(2,1)} %collective-permute-done, bf16[192,3584]{1,0:T(8,128)(2,1)S(1)} %bitcast.152), kind=kOutput, calls=%fused_computation.13 | convolution fusion | flops 1432223744 | bytes 7733252 | tf_op jit(solution)/shard_map/dot_general | solution.py:14
  247.1 3.3 add_convert_fusion.3
  250.5 14.8 %all-to-all-done.7 = bf16[8,24,3584]{2,1,0:T(8,128)(2,1)} async-done(((bf16[8,24,3584]{2,1,0:T(8,128)(2,1)}), bf16[8,24,3584]{2,1,0:T(8,128)(2,1)}, u32[]{:S(2)}, u32[]{:S(2)}) %all-to-all-start.7) | async-done | bytes 1376288 | tf_op jit(solution)/shard_map/all_to_all | solution.py:42
  265.3 4.3 %all-to-all-start.1 = ((bf16[8,24,3584]{2,1,0:T(8,128)(2,1)}), bf16[8,24,3584]{2,1,0:T(8,128)(2,1)}, u32[]{:S(2)}, u32[]{:S(2)}) async-start(bf16[8,24,3584]{2,1,0:T(8,128)(2,1)} %bitcast.166), calls=%async_computation.1 | async-start | bytes 2752512 | tf_op jit(solution)/shard_map/all_to_all | solution.py:42
  269.6 4.8 %convolution_convert_fusion = bf16[256,3584]{1,0:T(8,128)(2,1)} fusion(bf16[192,3584]{1,0:T(8,128)(2,1)} %collective-permute-done.6, bf16[192,3584]{1,0:T(8,128)(2,1)} %bitcast.172, bf16[192,3584]{1,0:T(8,128)(2,1)} %collective-permute-done.4, bf16[192,3584]{1,0:T(8,128)(2,1)} %bitcast.168, bf16[768,512]{1,0:T(8,128)(2,1)} %pad_maximum_fusion.6, s32[]{:T(128)S(6)} %select_n.2), kind=kOutput, calls=%fused_computation.8 | convolution fusion | flops 1432223744 | bytes 7733252 | tf_op jit(solution)/shard_map/dot_general | solution.py:14
  276.8 4.1 %convolution_convert_fusion.4 = bf16[3584,256]{1,0:T(8,128)(2,1)} fusion(bf16[768,512]{1,0:T(8,128)(2,1)S(1)} %pad_maximum_fusion.4, s32[]{:T(128)S(6)} %select_n.2, bf16[192,3584]{1,0:T(8,128)(2,1)S(1)} %copy-done.14, bf16[192,3584]{1,0:T(8,128)(2,1)S(1)} %bitcast.160, bf16[192,3584]{1,0:T(8,128)(2,1)} %collective-permute-done, ...), kind=kOutput, calls=%fused_computation.18 | convolution fusion | flops 1432223744 | bytes 7733252 | tf_op jit(solution)/shard_map/dot_general | solution.py:14
  281.4 3.4 add_convert_fusion.2
  285.5 4.2 %fusion.20 = bf16[1,3584,256]{2,1,0:T(8,128)(2,1)} fusion(bf16[3584,256]{1,0:T(8,128)(2,1)} %collective-permute-done.9, bf16[768,512]{1,0:T(8,128)(2,1)S(1)} %copy-done.30, s32[]{:T(128)S(6)} %mul.200, bf16[192,3584]{1,0:T(8,128)(2,1)S(1)} %copy-done.14, bf16[192,3584]{1,0:T(8,128)(2,1)S(1)} %bitcast.161, bf16[192,3584]{1,0:T(8,128)(2,1)} %collective-permute-done, ...), kind=kOutput, calls=%fused_computation.40 | convolution fusion | flops 1435893760 | bytes 9568260 | tf_op jit(solution)/shard_map/dot_general | solution.py:14
  289.8 12.2 %all-to-all-done.1 = bf16[8,24,3584]{2,1,0:T(8,128)(2,1)} async-done(((bf16[8,24,3584]{2,1,0:T(8,128)(2,1)}), bf16[8,24,3584]{2,1,0:T(8,128)(2,1)}, u32[]{:S(2)}, u32[]{:S(2)}) %all-to-all-start.1) | async-done | bytes 1376288 | tf_op jit(solution)/shard_map/all_to_all | solution.py:42
  302.0 4.5 %all-to-all-start.3 = ((bf16[8,24,3584]{2,1,0:T(8,128)(2,1)}), bf16[8,24,3584]{2,1,0:T(8,128)(2,1)}, u32[]{:S(2)}, u32[]{:S(2)}) async-start(bf16[8,24,3584]{2,1,0:T(8,128)(2,1)} %bitcast.165), calls=%async_computation.3 | async-start | bytes 2752512 | tf_op jit(solution)/shard_map/all_to_all | solution.py:42
  306.5 18.3 %collective-permute-done.10 = bf16[256,3584]{1,0:T(8,128)(2,1)} collective-permute-done((bf16[256,3584]{1,0:T(8,128)(2,1)}, bf16[256,3584]{1,0:T(8,128)(2,1)}, u32[]{:S(2)}, u32[]{:S(2)}) %collective-permute-start.10) | collective-permute-done | bytes 1835040 | tf_op jit(solution)/shard_map/ppermute | solution.py:134
  324.9 5.0 %fusion.21 = bf16[1,256,3584]{2,1,0:T(8,128)(2,1)} fusion(bf16[256,3584]{1,0:T(8,128)(2,1)} %collective-permute-done.10, bf16[192,3584]{1,0:T(8,128)(2,1)} %collective-permute-done.6, bf16[192,3584]{1,0:T(8,128)(2,1)} %bitcast.173, bf16[192,3584]{1,0:T(8,128)(2,1)} %collective-permute-done.4, bf16[192,3584]{1,0:T(8,128)(2,1)} %bitcast.169, ...), kind=kOutput, calls=%fused_computation.41 | convolution fusion | flops 1435893760 | bytes 9568260 | tf_op jit(solution)/shard_map/dot_general | solution.py:14
  329.8 34.0 %collective-permute-done.8 = bf16[3584,256]{1,0:T(8,128)(2,1)} collective-permute-done((bf16[3584,256]{1,0:T(8,128)(2,1)}, bf16[3584,256]{1,0:T(8,128)(2,1)}, u32[]{:S(2)}, u32[]{:S(2)}) %collective-permute-start.8) | collective-permute-done | bytes 1835040 | tf_op jit(solution)/shard_map/ppermute | solution.py:134
  363.8 4.2 %fusion.19 = bf16[1,3584,256]{2,1,0:T(8,128)(2,1)} fusion(bf16[3584,256]{1,0:T(8,128)(2,1)} %collective-permute-done.8, bf16[768,512]{1,0:T(8,128)(2,1)S(1)} %copy-done.32, s32[]{:T(128)S(6)} %mul.200, bf16[192,3584]{1,0:T(8,128)(2,1)S(1)} %copy-done.15, bf16[192,3584]{1,0:T(8,128)(2,1)S(1)} %bitcast.162, bf16[192,3584]{1,0:T(8,128)(2,1)} %collective-permute-done, ...), kind=kOutput, calls=%fused_computation.39 | convolution fusion | flops 1435893760 | bytes 9568260 | tf_op jit(solution)/shard_map/dot_general | solution.py:14
  (153 shorter events, 59.2 us)
Async XLA Ops:
  1.8 13.9 %copy-start.24 = (bf16[1,128,3584]{2,1,0:T(8,128)(2,1)S(1)}, bf16[1,128,3584]{2,1,0:T(8,128)(2,1)}, u32[]{:S(2)}) copy-start(bf16[1,128,3584]{2,1,0:T(8,128)(2,1)} %param.7) | copy-start | bytes 2752516
  5.7 11.6 %copy-start.39 = (bf16[64,192]{1,0:T(8,128)(2,1)}, bf16[64,192]{1,0:T(8,128)(2,1)S(1)}, u32[]{:S(2)}) copy-start(bf16[64,192]{1,0:T(8,128)(2,1)S(1)} %get-tuple-element.29) | copy-start | bytes 73732
  5.7 84.1 %copy-start.37 = (bf16[64,192]{1,0:T(8,128)(2,1)}, bf16[64,192]{1,0:T(8,128)(2,1)S(1)}, u32[]{:S(2)}) copy-start(bf16[64,192]{1,0:T(8,128)(2,1)S(1)} %get-tuple-element.10) | copy-start | bytes 73732
  8.4 40.1 %all-to-all-start.4 = ((bf16[8,24,3584]{2,1,0:T(8,128)(2,1)}), bf16[8,24,3584]{2,1,0:T(8,128)(2,1)S(1)}, u32[]{:S(2)}, u32[]{:S(2)}) async-start(bf16[8,24,3584]{2,1,0:T(8,128)(2,1)} %bitcast.19), calls=%async_computation.4 | async-start | bytes 2752512 | tf_op jit(solution)/shard_map/all_to_all | solution.py:42
  15.7 37.5 %copy-start.25 = (bf16[1,128,3584]{2,1,0:T(8,128)(2,1)S(1)}, bf16[1,128,3584]{2,1,0:T(8,128)(2,1)}, u32[]{:S(2)}) copy-start(bf16[1,128,3584]{2,1,0:T(8,128)(2,1)} %param.8) | copy-start | bytes 2752516
  49.6 36.6 %all-to-all-start = ((bf16[8,24,3584]{2,1,0:T(8,128)(2,1)}), bf16[8,24,3584]{2,1,0:T(8,128)(2,1)S(1)}, u32[]{:S(2)}, u32[]{:S(2)}) async-start(bf16[8,24,3584]{2,1,0:T(8,128)(2,1)} %bitcast.3), calls=%async_computation | async-start | bytes 2752512 | tf_op jit(solution)/shard_map/all_to_all | solution.py:42
  86.2 77.8 %copy-start.8 = (bf16[8,24,3584]{2,1,0:T(8,128)(2,1)}, bf16[8,24,3584]{2,1,0:T(8,128)(2,1)S(1)}, u32[]{:S(2)}) copy-start(bf16[8,24,3584]{2,1,0:T(8,128)(2,1)S(1)} %all-to-all-done) | copy-start | bytes 4128772
  86.2 36.6 %all-to-all-start.6 = ((bf16[8,24,3584]{2,1,0:T(8,128)(2,1)}), bf16[8,24,3584]{2,1,0:T(8,128)(2,1)S(1)}, u32[]{:S(2)}, u32[]{:S(2)}) async-start(bf16[8,24,3584]{2,1,0:T(8,128)(2,1)} %bitcast.24), calls=%async_computation.6 | async-start | bytes 2752512 | tf_op jit(solution)/shard_map/all_to_all | solution.py:42
  123.9 36.6 %all-to-all-start.2 = ((bf16[8,24,3584]{2,1,0:T(8,128)(2,1)}), bf16[8,24,3584]{2,1,0:T(8,128)(2,1)S(1)}, u32[]{:S(2)}, u32[]{:S(2)}) async-start(bf16[8,24,3584]{2,1,0:T(8,128)(2,1)} %bitcast.164), calls=%async_computation.2 | async-start | bytes 2752512 | tf_op jit(solution)/shard_map/all_to_all | solution.py:42
  127.6 46.9 %collective-permute-start.4 = (bf16[192,3584]{1,0:T(8,128)(2,1)}, bf16[192,3584]{1,0:T(8,128)(2,1)}, u32[]{:S(2)}, u32[]{:S(2)}) collective-permute-start(bf16[192,3584]{1,0:T(8,128)(2,1)} %bitcast.167), channel_id=1, source_target_pairs={{0,1},{1,0},{2,3},{3,2},{4,5},{5,4},{6,7},{7,6},{8,9},{9,8},{10,11... | collective-permute-start | bytes 4128776 | tf_op jit(solution)/shard_map/ppermute | solution.py:53
  127.7 41.7 %collective-permute-start = (bf16[192,3584]{1,0:T(8,128)(2,1)S(1)}, bf16[192,3584]{1,0:T(8,128)(2,1)}, u32[]{:S(2)}, u32[]{:S(2)}) collective-permute-start(bf16[192,3584]{1,0:T(8,128)(2,1)S(1)} %bitcast.149), channel_id=1, source_target_pairs={{0,1},{1,0},{2,3},{3,2},{4,5},{5,4},{6,7},{7,6},{8,9},{9,8},{10,11... | collective-permute-start | bytes 4128776 | tf_op jit(solution)/shard_map/ppermute | solution.py:53
  128.2 54.4 %collective-permute-start.6 = (bf16[192,3584]{1,0:T(8,128)(2,1)}, bf16[192,3584]{1,0:T(8,128)(2,1)}, u32[]{:S(2)}, u32[]{:S(2)}) collective-permute-start(bf16[192,3584]{1,0:T(8,128)(2,1)} %bitcast.171), channel_id=1, source_target_pairs={{0,1},{1,0},{2,3},{3,2},{4,5},{5,4},{6,7},{7,6},{8,9},{9,8},{10,11... | collective-permute-start | bytes 4128776 | tf_op jit(solution)/shard_map/ppermute | solution.py:53
  160.5 20.3 %collective-permute-start.2 = (bf16[192,3584]{1,0:T(8,128)(2,1)S(1)}, bf16[192,3584]{1,0:T(8,128)(2,1)S(1)}, u32[]{:S(2)}, u32[]{:S(2)}) collective-permute-start(bf16[192,3584]{1,0:T(8,128)(2,1)S(1)} %bitcast.156), channel_id=1, source_target_pairs={{0,1},{1,0},{2,3},{3,2},{4,5},{5,4},{6,7},{7,6},{8,9},{9,8},{10,11... | collective-permute-start | bytes 4128776 | tf_op jit(solution)/shard_map/ppermute | solution.py:53
  168.0 19.5 %copy-start.33 = (bf16[192,512]{1,0:T(8,128)(2,1)}, bf16[192,512]{1,0:T(8,128)(2,1)S(1)}, u32[]{:S(2)}) copy-start(bf16[192,512]{1,0:T(8,128)(2,1)S(1)} %get-tuple-element.14) | copy-start | bytes 589828
  180.7 6.7 %collective-permute-start.5 = (bf16[192,3584]{1,0:T(8,128)(2,1)S(1)}, bf16[192,3584]{1,0:T(8,128)(2,1)S(1)}, u32[]{:S(2)}, u32[]{:S(2)}) collective-permute-start(bf16[192,3584]{1,0:T(8,128)(2,1)S(1)} %fusion.12), channel_id=1, source_target_pairs={{0,1},{1,0},{2,3},{3,2},{4,5},{5,4},{6,7},{7,6},{8,9},{9,8},{10,11... | collective-permute-start | bytes 4128776 | tf_op jit(solution)/shard_map/ppermute | solution.py:53
  189.9 38.1 %all-to-all-start.5 = ((bf16[8,24,3584]{2,1,0:T(8,128)(2,1)}), bf16[8,24,3584]{2,1,0:T(8,128)(2,1)}, u32[]{:S(2)}, u32[]{:S(2)}) async-start(bf16[8,24,3584]{2,1,0:T(8,128)(2,1)} %bitcast.163), calls=%async_computation.5 | async-start | bytes 2752512 | tf_op jit(solution)/shard_map/all_to_all | solution.py:42
  198.2 7.3 %collective-permute-start.7 = (bf16[192,3584]{1,0:T(8,128)(2,1)S(1)}, bf16[192,3584]{1,0:T(8,128)(2,1)S(1)}, u32[]{:S(2)}, u32[]{:S(2)}) collective-permute-start(bf16[192,3584]{1,0:T(8,128)(2,1)S(1)} %fusion.16), channel_id=1, source_target_pairs={{0,1},{1,0},{2,3},{3,2},{4,5},{5,4},{6,7},{7,6},{8,9},{9,8},{10,11... | collective-permute-start | bytes 4128776 | tf_op jit(solution)/shard_map/ppermute | solution.py:53
  228.1 37.2 %all-to-all-start.7 = ((bf16[8,24,3584]{2,1,0:T(8,128)(2,1)}), bf16[8,24,3584]{2,1,0:T(8,128)(2,1)}, u32[]{:S(2)}, u32[]{:S(2)}) async-start(bf16[8,24,3584]{2,1,0:T(8,128)(2,1)} %bitcast.26), calls=%async_computation.7 | async-start | bytes 2752512 | tf_op jit(solution)/shard_map/all_to_all | solution.py:42
  236.6 10.5 %collective-permute-start.1 = (bf16[192,3584]{1,0:T(8,128)(2,1)}, bf16[192,3584]{1,0:T(8,128)(2,1)}, u32[]{:S(2)}, u32[]{:S(2)}) collective-permute-start(bf16[192,3584]{1,0:T(8,128)(2,1)} %convolution_convert_fusion.9), channel_id=1, source_target_pairs={{0,1},{1,0},{2,3},{3,2},{4,5},{5,4},{6,7},{7,6},{8,9},{9,8},{10,11... | collective-permute-start | bytes 4128776 | tf_op jit(solution)/shard_map/ppermute | solution.py:53
  242.4 43.1 %collective-permute-start.9 = (bf16[3584,256]{1,0:T(8,128)(2,1)}, bf16[3584,256]{1,0:T(8,128)(2,1)}, u32[]{:S(2)}, u32[]{:S(2)}) collective-permute-start(bf16[3584,256]{1,0:T(8,128)(2,1)} %convolution_convert_fusion.2), channel_id=1, source_target_pairs={{0,16},{16,0},{1,17},{17,1},{2,18},{18,2},{3,19},{19,3},{4,20},{20... | collective-permute-start | bytes 5505032 | tf_op jit(solution)/shard_map/ppermute | solution.py:134
  245.9 35.5 %collective-permute-start.3 = (bf16[192,3584]{1,0:T(8,128)(2,1)}, bf16[192,3584]{1,0:T(8,128)(2,1)}, u32[]{:S(2)}, u32[]{:S(2)}) collective-permute-start(bf16[192,3584]{1,0:T(8,128)(2,1)} %convolution_convert_fusion.6), channel_id=1, source_target_pairs={{0,1},{1,0},{2,3},{3,2},{4,5},{5,4},{6,7},{7,6},{8,9},{9,8},{10,11... | collective-permute-start | bytes 4128776 | tf_op jit(solution)/shard_map/ppermute | solution.py:53
  265.3 36.7 %all-to-all-start.1 = ((bf16[8,24,3584]{2,1,0:T(8,128)(2,1)}), bf16[8,24,3584]{2,1,0:T(8,128)(2,1)}, u32[]{:S(2)}, u32[]{:S(2)}) async-start(bf16[8,24,3584]{2,1,0:T(8,128)(2,1)} %bitcast.166), calls=%async_computation.1 | async-start | bytes 2752512 | tf_op jit(solution)/shard_map/all_to_all | solution.py:42
  269.6 6.3 %copy-start.21 = (bf16[192,512]{1,0:T(8,128)(2,1)S(1)}, bf16[192,512]{1,0:T(8,128)(2,1)}, u32[]{:S(2)}) copy-start(bf16[192,512]{1,0:T(8,128)(2,1)} %copy-done.20) | copy-start | bytes 589828
  269.6 7.2 %copy-start.14 = (bf16[192,3584]{1,0:T(8,128)(2,1)S(1)}, bf16[192,3584]{1,0:T(8,128)(2,1)}, u32[]{:S(2)}) copy-start(bf16[192,3584]{1,0:T(8,128)(2,1)} %copy-done.13) | copy-start | bytes 4128772
  274.4 50.5 %collective-permute-start.10 = (bf16[256,3584]{1,0:T(8,128)(2,1)}, bf16[256,3584]{1,0:T(8,128)(2,1)}, u32[]{:S(2)}, u32[]{:S(2)}) collective-permute-start(bf16[256,3584]{1,0:T(8,128)(2,1)} %convolution_convert_fusion), channel_id=1, source_target_pairs={{0,16},{16,0},{1,17},{17,1},{2,18},{18,2},{3,19},{19,3},{4,20},{20... | collective-permute-start | bytes 5505032 | tf_op jit(solution)/shard_map/ppermute | solution.py:134
  280.9 82.9 %collective-permute-start.8 = (bf16[3584,256]{1,0:T(8,128)(2,1)}, bf16[3584,256]{1,0:T(8,128)(2,1)}, u32[]{:S(2)}, u32[]{:S(2)}) collective-permute-start(bf16[3584,256]{1,0:T(8,128)(2,1)} %convolution_convert_fusion.4), channel_id=1, source_target_pairs={{0,16},{16,0},{1,17},{17,1},{2,18},{18,2},{3,19},{19,3},{4,20},{20... | collective-permute-start | bytes 5505032 | tf_op jit(solution)/shard_map/ppermute | solution.py:134
  289.8 35.1 %copy-start.28 = (bf16[768,512]{1,0:T(8,128)(2,1)S(1)}, bf16[768,512]{1,0:T(8,128)(2,1)}, u32[]{:S(2)}) copy-start(bf16[768,512]{1,0:T(8,128)(2,1)} %pad_maximum_fusion.6) | copy-start | bytes 2359300
  302.0 72.8 %all-to-all-start.3 = ((bf16[8,24,3584]{2,1,0:T(8,128)(2,1)}), bf16[8,24,3584]{2,1,0:T(8,128)(2,1)}, u32[]{:S(2)}, u32[]{:S(2)}) async-start(bf16[8,24,3584]{2,1,0:T(8,128)(2,1)} %bitcast.165), calls=%async_computation.3 | async-start | bytes 2752512 | tf_op jit(solution)/shard_map/all_to_all | solution.py:42
  306.5 57.3 %copy-start.15 = (bf16[192,3584]{1,0:T(8,128)(2,1)S(1)}, bf16[192,3584]{1,0:T(8,128)(2,1)}, u32[]{:S(2)}) copy-start(bf16[192,3584]{1,0:T(8,128)(2,1)} %copy-done.13) | copy-start | bytes 4128772
  306.5 57.3 %copy-start.32 = (bf16[768,512]{1,0:T(8,128)(2,1)S(1)}, bf16[768,512]{1,0:T(8,128)(2,1)}, u32[]{:S(2)}) copy-start(bf16[768,512]{1,0:T(8,128)(2,1)} %copy-done.31) | copy-start | bytes 2359300
  329.8 38.2 %copy-start.40 = (bf16[64,192]{1,0:T(8,128)(2,1)S(1)}, bf16[64,192]{1,0:T(8,128)(2,1)}, u32[]{:S(2)}) copy-start(bf16[64,192]{1,0:T(8,128)(2,1)} %copy-done.39) | copy-start | bytes 73732
  329.8 40.0 %copy-start.38 = (bf16[64,192]{1,0:T(8,128)(2,1)S(1)}, bf16[64,192]{1,0:T(8,128)(2,1)}, u32[]{:S(2)}) copy-start(bf16[64,192]{1,0:T(8,128)(2,1)} %copy-done.37) | copy-start | bytes 73732
  (30 other events, 99.6 us)

commit v2 on v1

--- a/solution.py
+++ b/solution.py
@@ -14,12 +14,12 @@
     return lax.dot_general(a, b, (dims, ((), ())), preferred_element_type=F32)
 
 
-def route(ids, gain, expert_count, capacity):
+def route(ids, gain, expert_count, capacity, chip):
     flat_ids = ids.reshape(-1)
     member = (flat_ids[:, None] == jnp.arange(expert_count, dtype=jnp.int32)[None, :]).astype(jnp.int32)
     running = jnp.cumsum(member, axis=0) - 1
     slot_rank = jnp.sum(member * running, axis=1)
-    target = (flat_ids * capacity + slot_rank).reshape(ids.shape)
+    target = ((flat_ids ^ chip) * capacity + slot_rank).reshape(ids.shape)
     slots = jnp.arange(expert_count * capacity, dtype=jnp.int32)
     matches = (target[:, :, None] == slots[None, None, :]).astype(F32)
     placing = jnp.sum(matches, axis=1).astype(BF16)
@@ -35,19 +35,16 @@
     slot_count = chips * capacity
     width = gate_weight.shape[0]
     half_units = gate_weight.shape[1] // 2
-    same_core = [[2 * chip + core for chip in range(chips)] for core in range(2)]
+    chip = lax.axis_index("expert") // 2
     other_core = [(i, i ^ 1) for i in range(devices)]
 
     def across(blocks):
-        moved = lax.all_to_all(
-            blocks.reshape(chips, capacity, width),
-            "expert",
-            split_axis=0,
-            concat_axis=0,
-            axis_index_groups=same_core,
-            tiled=True,
-        )
-        return moved.reshape(slot_count, width)
+        pieces = [blocks[d * capacity : (d + 1) * capacity] for d in range(chips)]
+        moved = [
+            piece if d == 0 else lax.ppermute(piece, "expert", [(i, i ^ (2 * d)) for i in range(devices)])
+            for d, piece in enumerate(pieces)
+        ]
+        return jnp.concatenate(moved, axis=0)
 
     def swap(rows):
         return lax.ppermute(rows, "expert", other_core)
@@ -57,7 +54,7 @@
     for b in range(MB):
         rows = slice(b * TOK_MB, (b + 1) * TOK_MB)
         placing, weighting, slot_gain = route(
-            expert_ids[0, rows], route_weights[0, rows], chips, capacity
+            expert_ids[0, rows], route_weights[0, rows], chips, capacity, chip
         )
         routes.append((placing, weighting))
         tokens = dot(placing, acts[0, rows], ((0,), (0,))).astype(BF16)

time: 379 us -> 344 us (0.908)
  waiting for transfers between devices: 225 us -> 84.4 us
  starting transfers between devices: 41.1 us -> 147 us
  matrix products: 93.1 us -> 69.6 us
  local copies, waits for them, and re-layouts: 10.4 us -> 33.8 us
    all_to_all x8 -> x0, waiting for transfers between devices: 172 us -> none  [across(): lax.all_to_all(blocks.reshape(chips, capacity, width), 'expert', split_ax...]
    ppermute x0 -> x56, starting transfers between devices: none -> 141 us  [across(): lax.ppermute(piece, 'expert', [(i, i ^ 2 * d) for i in range(devices)])]
    ppermute x0 -> x56, waiting for transfers between devices: none -> 77.5 us  [across(): lax.ppermute(piece, 'expert', [(i, i ^ 2 * d) for i in range(devices)])]
    ppermute x3, waiting for transfers between devices: 53 us -> 6.45 us  [on_device(): lax.ppermute(dot(a, b, rows_dims).astype(BF16), 'pipe', mirror)]
    all_to_all x8 -> x0, starting transfers between devices: 36 us -> none  [across(): lax.all_to_all(blocks.reshape(chips, capacity, width), 'expert', split_ax...]
    unnamed x86 -> x94, local copies, waits for them, and re-layouts: 7.85 us -> 29.5 us
    dot_general x36, matrix products: 88.8 us -> 67.9 us  [dot(): return lax.dot_general(a, b, (dims, ((), ())), preferred_element_type=F32)]
  transfers between devices with their start and end apart: 19 -> 67, of which waited for: 10 -> 24; matrix products, arithmetic and copies ran while one was open for 24% -> 28% of each run, Pallas kernels for 0% -> 0%
where the time goes in v2:
time: 344 us; the launch traced here: 340 us
  starting transfers between devices  147 us (43%)
  waiting for transfers between devices  84.4 us (25%)
  matrix products  69.6 us (20%)
  local copies, waits for them, and re-layouts  33.8 us (10%)
  other arithmetic  3.96 us (1%)
    ppermute x56, starting transfers between devices, across(): lax.ppermute(piece, 'expert', [(i, i ^ 2 * d) for i in range(devices)])  141 us
    ppermute x56, waiting for transfers between devices, across(): lax.ppermute(piece, 'expert', [(i, i ^ 2 * d) for i in range(devices)])  77.5 us
    dot_general x36, matrix products, dot(): return lax.dot_general(a, b, (dims, ((), ())), preferred_element_type=F32)  67.9 us
    unnamed x94, local copies, waits for them, and re-layouts  29.5 us
  transfers between devices with their start and end apart: 67, of which 24 were waited for; matrix products, arithmetic and copies ran while one was open for 28% of the time, Pallas kernels for 0%

profile of v2, /device:TPU:0, one launch (start us, length us, event | category | flops | bytes accessed | tf_op | source)
XLA Modules:
  0.0 340.0 jit_solution(11491494074335467668)
XLA Ops:
  12.4 3.0 collective-permute-start.35
  21.6 3.7 %collective-permute-start.37 = (bf16[24,3584]{1,0:T(8,128)(2,1)S(1)}, bf16[24,3584]{1,0:T(8,128)(2,1)S(1)}, u32[]{:S(2)}, u32[]{:S(2)}) collective-permute-start(bf16[24,3584]{1,0:T(8,128)(2,1)S(1)} %copy-done.12), channel_id=1, source_target_pairs={{0,12},{1,13},{2,14},{3,15},{4,8},{5,9},{6,10},{7,11},{8,4},{9,5},... | collective-permute-start | bytes 516104 | tf_op jit(solution)/shard_map/ppermute | solution.py:44
  31.1 4.7 %collective-permute-start.1 = (bf16[24,3584]{1,0:T(8,128)(2,1)S(1)}, bf16[24,3584]{1,0:T(8,128)(2,1)S(1)}, u32[]{:S(2)}, u32[]{:S(2)}) collective-permute-start(bf16[24,3584]{1,0:T(8,128)(2,1)S(1)} %copy-done.9), channel_id=1, source_target_pairs={{0,4},{1,5},{2,6},{3,7},{4,0},{5,1},{6,2},{7,3},{8,12},{9,13},{10,... | collective-permute-start | bytes 516104 | tf_op jit(solution)/shard_map/ppermute | solution.py:44
  36.6 3.7 %collective-permute-done.36 = bf16[24,3584]{1,0:T(8,128)(2,1)S(1)} collective-permute-done((bf16[24,3584]{1,0:T(8,128)(2,1)}, bf16[24,3584]{1,0:T(8,128)(2,1)S(1)}, u32[]{:S(2)}, u32[]{:S(2)}) %collective-permute-start.36) | collective-permute-done | bytes 172064 | tf_op jit(solution)/shard_map/ppermute | solution.py:44
  42.3 4.5 %collective-permute-start.3 = (bf16[24,3584]{1,0:T(8,128)(2,1)S(1)}, bf16[24,3584]{1,0:T(8,128)(2,1)S(1)}, u32[]{:S(2)}, u32[]{:S(2)}) collective-permute-start(bf16[24,3584]{1,0:T(8,128)(2,1)S(1)} %copy-done.7), channel_id=1, source_target_pairs={{0,8},{1,9},{2,10},{3,11},{4,12},{5,13},{6,14},{7,15},{8,0},{9,1},... | collective-permute-start | bytes 516104 | tf_op jit(solution)/shard_map/ppermute | solution.py:44
  47.5 12.4 %collective-permute-start.4 = (bf16[24,3584]{1,0:T(8,128)(2,1)S(1)}, bf16[24,3584]{1,0:T(8,128)(2,1)S(1)}, u32[]{:S(2)}, u32[]{:S(2)}) collective-permute-start(bf16[24,3584]{1,0:T(8,128)(2,1)S(1)} %copy-done.6), channel_id=1, source_target_pairs={{0,10},{1,11},{2,8},{3,9},{4,14},{5,15},{6,12},{7,13},{8,2},{9,3},... | collective-permute-start | bytes 516104 | tf_op jit(solution)/shard_map/ppermute | solution.py:44
  61.8 4.3 %collective-permute-start.6 = (bf16[24,3584]{1,0:T(8,128)(2,1)S(1)}, bf16[24,3584]{1,0:T(8,128)(2,1)S(1)}, u32[]{:S(2)}, u32[]{:S(2)}) collective-permute-start(bf16[24,3584]{1,0:T(8,128)(2,1)S(1)} %copy-done.4), channel_id=1, source_target_pairs={{0,14},{1,15},{2,12},{3,13},{4,10},{5,11},{6,8},{7,9},{8,6},{9,7},... | collective-permute-start | bytes 516104 | tf_op jit(solution)/shard_map/ppermute | solution.py:44
  82.2 3.5 %collective-permute-start.49 = (bf16[24,3584]{1,0:T(8,128)(2,1)S(1)}, bf16[24,3584]{1,0:T(8,128)(2,1)S(1)}, u32[]{:S(2)}, u32[]{:S(2)}) collective-permute-start(bf16[24,3584]{1,0:T(8,128)(2,1)S(1)} %get-tuple-element.17), channel_id=1, source_target_pairs={{0,4},{1,5},{2,6},{3,7},{4,0},{5,1},{6,2},{7,3},{8,12},{9,13},{10,... | collective-permute-start | bytes 516104 | tf_op jit(solution)/shard_map/ppermute | solution.py:44
  86.2 4.1 %collective-permute-start.51 = (bf16[24,3584]{1,0:T(8,128)(2,1)S(1)}, bf16[24,3584]{1,0:T(8,128)(2,1)S(1)}, u32[]{:S(2)}, u32[]{:S(2)}) collective-permute-start(bf16[24,3584]{1,0:T(8,128)(2,1)S(1)} %get-tuple-element.15), channel_id=1, source_target_pairs={{0,8},{1,9},{2,10},{3,11},{4,12},{5,13},{6,14},{7,15},{8,0},{9,1},... | collective-permute-start | bytes 516104 | tf_op jit(solution)/shard_map/ppermute | solution.py:44
  107.4 6.3 %collective-permute-done.16 = bf16[24,3584]{1,0:T(8,128)(2,1)S(1)} collective-permute-done((bf16[24,3584]{1,0:T(8,128)(2,1)S(1)}, bf16[24,3584]{1,0:T(8,128)(2,1)S(1)}, u32[]{:S(2)}, u32[]{:S(2)}) %collective-permute-start.16) | collective-permute-done | bytes 172064 | tf_op jit(solution)/shard_map/ppermute | solution.py:44
  123.3 8.6 %collective-permute-done.19 = bf16[24,3584]{1,0:T(8,128)(2,1)S(1)} collective-permute-done((bf16[24,3584]{1,0:T(8,128)(2,1)S(1)}, bf16[24,3584]{1,0:T(8,128)(2,1)S(1)}, u32[]{:S(2)}, u32[]{:S(2)}) %collective-permute-start.19) | collective-permute-done | bytes 172064 | tf_op jit(solution)/shard_map/ppermute | solution.py:44
  134.5 7.0 %collective-permute-start.22 = (bf16[24,3584]{1,0:T(8,128)(2,1)S(1)}, bf16[24,3584]{1,0:T(8,128)(2,1)S(1)}, u32[]{:S(2)}, u32[]{:S(2)}) collective-permute-start(bf16[24,3584]{1,0:T(8,128)(2,1)S(1)} %get-tuple-element.30), channel_id=1, source_target_pairs={{0,14},{1,15},{2,12},{3,13},{4,10},{5,11},{6,8},{7,9},{8,6},{9,7},... | collective-permute-start | bytes 516104 | tf_op jit(solution)/shard_map/ppermute | solution.py:44
  155.9 5.8 %collective-permute-start.41 = (bf16[24,3584]{1,0:T(8,128)(2,1)S(1)}, bf16[24,3584]{1,0:T(8,128)(2,1)S(1)}, u32[]{:S(2)}, u32[]{:S(2)}) collective-permute-start(bf16[24,3584]{1,0:T(8,128)(2,1)S(1)} %get-tuple-element.53), channel_id=1, source_target_pairs={{0,2},{1,3},{2,0},{3,1},{4,6},{5,7},{6,4},{7,5},{8,10},{9,11},{10,... | collective-permute-start | bytes 516104 | tf_op jit(solution)/shard_map/ppermute | solution.py:44
  167.3 3.1 collective-permute-start.45
  173.2 5.4 %convolution_convert_fusion.2 = bf16[3584,256]{1,0:T(8,128)(2,1)} fusion(bf16[768,3584]{1,0:T(8,128)(2,1)} %constant_dynamic-update-slice_fusion.64, bf16[768,512]{1,0:T(8,128)(2,1)S(1)} %pad_maximum_fusion.1, s32[]{:T(128)S(6)} %select_n.14), kind=kOutput, calls=%fused_computation.11 | convolution fusion | flops 1410203648 | bytes 7733252 | tf_op jit(solution)/shard_map/dot_general | solution.py:14
  178.6 5.4 %convolution_convert_fusion.4 = bf16[3584,256]{1,0:T(8,128)(2,1)} fusion(bf16[768,3584]{1,0:T(8,128)(2,1)} %constant_dynamic-update-slice_fusion.64, bf16[768,512]{1,0:T(8,128)(2,1)S(1)} %pad_maximum_fusion, s32[]{:T(128)S(6)} %select_n.14), kind=kOutput, calls=%fused_computation.16 | convolution fusion | flops 1410203648 | bytes 7733252 | tf_op jit(solution)/shard_map/dot_general | solution.py:14
  184.2 11.9 %convolution_convert_fusion = bf16[256,3584]{1,0:T(8,128)(2,1)S(1)} fusion(bf16[768,3584]{1,0:T(8,128)(2,1)S(1)} %constant_dynamic-update-slice_fusion.82, bf16[768,512]{1,0:T(8,128)(2,1)S(1)} %pad_maximum_fusion.2, s32[]{:T(128)S(6)} %select_n.14), kind=kOutput, calls=%fused_computation.6 | convolution fusion | flops 1410203648 | bytes 7733252 | tf_op jit(solution)/shard_map/dot_general | solution.py:14
  196.5 3.1 collective-permute-start.47
  205.4 5.2 %collective-permute-start.12 = (bf16[24,3584]{1,0:T(8,128)(2,1)S(1)}, bf16[24,3584]{1,0:T(8,128)(2,1)S(1)}, u32[]{:S(2)}, u32[]{:S(2)}) collective-permute-start(bf16[24,3584]{1,0:T(8,128)(2,1)S(1)} %get-tuple-element.66), channel_id=1, source_target_pairs={{0,8},{1,9},{2,10},{3,11},{4,12},{5,13},{6,14},{7,15},{8,0},{9,1},... | collective-permute-start | bytes 516104 | tf_op jit(solution)/shard_map/ppermute | solution.py:44
  210.6 14.3 %collective-permute-start.13 = (bf16[24,3584]{1,0:T(8,128)(2,1)S(1)}, bf16[24,3584]{1,0:T(8,128)(2,1)S(1)}, u32[]{:S(2)}, u32[]{:S(2)}) collective-permute-start(bf16[24,3584]{1,0:T(8,128)(2,1)S(1)} %get-tuple-element.65), channel_id=1, source_target_pairs={{0,10},{1,11},{2,8},{3,9},{4,14},{5,15},{6,12},{7,13},{8,2},{9,3},... | collective-permute-start | bytes 516104 | tf_op jit(solution)/shard_map/ppermute | solution.py:44
  232.2 4.1 %collective-permute-done.13 = bf16[24,3584]{1,0:T(8,128)(2,1)S(1)} collective-permute-done((bf16[24,3584]{1,0:T(8,128)(2,1)S(1)}, bf16[24,3584]{1,0:T(8,128)(2,1)S(1)}, u32[]{:S(2)}, u32[]{:S(2)}) %collective-permute-start.13) | collective-permute-done | bytes 172064 | tf_op jit(solution)/shard_map/ppermute | solution.py:44
  253.9 6.7 %collective-permute-done.59 = bf16[24,3584]{1,0:T(8,128)(2,1)S(1)} collective-permute-done((bf16[24,3584]{1,0:T(8,128)(2,1)S(1)}, bf16[24,3584]{1,0:T(8,128)(2,1)S(1)}, u32[]{:S(2)}, u32[]{:S(2)}) %collective-permute-start.59) | collective-permute-done | bytes 172064 | tf_op jit(solution)/shard_map/ppermute | solution.py:44
  261.8 7.6 %collective-permute-done.60 = bf16[24,3584]{1,0:T(8,128)(2,1)S(1)} collective-permute-done((bf16[24,3584]{1,0:T(8,128)(2,1)S(1)}, bf16[24,3584]{1,0:T(8,128)(2,1)S(1)}, u32[]{:S(2)}, u32[]{:S(2)}) %collective-permute-start.60) | collective-permute-done | bytes 172064 | tf_op jit(solution)/shard_map/ppermute | solution.py:44
  269.4 3.0 collective-permute-start.62
  278.9 4.1 %collective-permute-done.63 = bf16[24,3584]{1,0:T(8,128)(2,1)S(1)} collective-permute-done((bf16[24,3584]{1,0:T(8,128)(2,1)S(1)}, bf16[24,3584]{1,0:T(8,128)(2,1)S(1)}, u32[]{:S(2)}, u32[]{:S(2)}) %collective-permute-start.63) | collective-permute-done | bytes 172064 | tf_op jit(solution)/shard_map/ppermute | solution.py:44
  285.7 3.8 %collective-permute-start.27 = (bf16[24,3584]{1,0:T(8,128)(2,1)S(1)}, bf16[24,3584]{1,0:T(8,128)(2,1)S(1)}, u32[]{:S(2)}, u32[]{:S(2)}) collective-permute-start(bf16[24,3584]{1,0:T(8,128)(2,1)S(1)} %get-tuple-element.75), channel_id=1, source_target_pairs={{0,6},{1,7},{2,4},{3,5},{4,2},{5,3},{6,0},{7,1},{8,14},{9,15},{10,... | collective-permute-start | bytes 516104 | tf_op jit(solution)/shard_map/ppermute | solution.py:44
  290.9 3.0 collective-permute-start.28
  297.9 9.5 %collective-permute-done.28 = bf16[24,3584]{1,0:T(8,128)(2,1)S(1)} collective-permute-done((bf16[24,3584]{1,0:T(8,128)(2,1)S(1)}, bf16[24,3584]{1,0:T(8,128)(2,1)S(1)}, u32[]{:S(2)}, u32[]{:S(2)}) %collective-permute-start.28) | collective-permute-done | bytes 172064 | tf_op jit(solution)/shard_map/ppermute | solution.py:44
  315.9 3.8 %collective-permute-done.31 = bf16[24,3584]{1,0:T(8,128)(2,1)S(1)} collective-permute-done((bf16[24,3584]{1,0:T(8,128)(2,1)S(1)}, bf16[24,3584]{1,0:T(8,128)(2,1)S(1)}, u32[]{:S(2)}, u32[]{:S(2)}) %collective-permute-start.31) | collective-permute-done | bytes 172064 | tf_op jit(solution)/shard_map/ppermute | solution.py:44
  325.9 4.5 %fusion.20 = bf16[1,3584,256]{2,1,0:T(8,128)(2,1)} fusion(bf16[768,3584]{1,0:T(8,128)(2,1)S(1)} %bitcast.142, bf16[3584,256]{1,0:T(8,128)(2,1)} %collective-permute-done.65, bf16[768,512]{1,0:T(8,128)(2,1)S(1)} %pad_maximum_fusion.1, s32[]{:T(128)S(6)} %mul.200), kind=kOutput, calls=%fused_computation.38 | convolution fusion | flops 1413873664 | bytes 9568260 | tf_op jit(solution)/shard_map/dot_general | solution.py:14
  330.4 6.4 %collective-permute-done.64 = bf16[3584,256]{1,0:T(8,128)(2,1)S(1)} collective-permute-done((bf16[3584,256]{1,0:T(8,128)(2,1)}, bf16[3584,256]{1,0:T(8,128)(2,1)S(1)}, u32[]{:S(2)}, u32[]{:S(2)}) %collective-permute-start.64) | collective-permute-done | bytes 1835040 | tf_op jit(solution)/shard_map/ppermute | solution.py:131
  336.9 3.0 fusion.19
  (269 shorter events, 158.7 us)
Async XLA Ops:
  12.4 18.8 %collective-permute-start.35 = (bf16[24,3584]{1,0:T(8,128)(2,1)}, bf16[24,3584]{1,0:T(8,128)(2,1)S(1)}, u32[]{:S(2)}, u32[]{:S(2)}) collective-permute-start(bf16[24,3584]{1,0:T(8,128)(2,1)} %get-tuple-element.24), channel_id=1, source_target_pairs={{0,8},{1,9},{2,10},{3,11},{4,12},{5,13},{6,14},{7,15},{8,0},{9,1},... | collective-permute-start | bytes 516104 | tf_op jit(solution)/shard_map/ppermute | solution.py:44
  15.3 24.9 %collective-permute-start.36 = (bf16[24,3584]{1,0:T(8,128)(2,1)}, bf16[24,3584]{1,0:T(8,128)(2,1)S(1)}, u32[]{:S(2)}, u32[]{:S(2)}) collective-permute-start(bf16[24,3584]{1,0:T(8,128)(2,1)} %get-tuple-element.23), channel_id=1, source_target_pairs={{0,10},{1,11},{2,8},{3,9},{4,14},{5,15},{6,12},{7,13},{8,2},{9,3},... | collective-permute-start | bytes 516104 | tf_op jit(solution)/shard_map/ppermute | solution.py:44
  21.6 20.7 %collective-permute-start.37 = (bf16[24,3584]{1,0:T(8,128)(2,1)S(1)}, bf16[24,3584]{1,0:T(8,128)(2,1)S(1)}, u32[]{:S(2)}, u32[]{:S(2)}) collective-permute-start(bf16[24,3584]{1,0:T(8,128)(2,1)S(1)} %copy-done.12), channel_id=1, source_target_pairs={{0,12},{1,13},{2,14},{3,15},{4,8},{5,9},{6,10},{7,11},{8,4},{9,5},... | collective-permute-start | bytes 516104 | tf_op jit(solution)/shard_map/ppermute | solution.py:44
  26.9 20.6 %collective-permute-start.38 = (bf16[24,3584]{1,0:T(8,128)(2,1)S(1)}, bf16[24,3584]{1,0:T(8,128)(2,1)S(1)}, u32[]{:S(2)}, u32[]{:S(2)}) collective-permute-start(bf16[24,3584]{1,0:T(8,128)(2,1)S(1)} %copy-done.10), channel_id=1, source_target_pairs={{0,14},{1,15},{2,12},{3,13},{4,10},{5,11},{6,8},{7,9},{8,6},{9,7},... | collective-permute-start | bytes 516104 | tf_op jit(solution)/shard_map/ppermute | solution.py:44
  28.7 31.9 %collective-permute-start = (bf16[24,3584]{1,0:T(8,128)(2,1)S(1)}, bf16[24,3584]{1,0:T(8,128)(2,1)S(1)}, u32[]{:S(2)}, u32[]{:S(2)}) collective-permute-start(bf16[24,3584]{1,0:T(8,128)(2,1)S(1)} %copy-done.11), channel_id=1, source_target_pairs={{0,2},{1,3},{2,0},{3,1},{4,6},{5,7},{6,4},{7,5},{8,10},{9,11},{10,... | collective-permute-start | bytes 516104 | tf_op jit(solution)/shard_map/ppermute | solution.py:44
  31.1 30.7 %collective-permute-start.1 = (bf16[24,3584]{1,0:T(8,128)(2,1)S(1)}, bf16[24,3584]{1,0:T(8,128)(2,1)S(1)}, u32[]{:S(2)}, u32[]{:S(2)}) collective-permute-start(bf16[24,3584]{1,0:T(8,128)(2,1)S(1)} %copy-done.9), channel_id=1, source_target_pairs={{0,4},{1,5},{2,6},{3,7},{4,0},{5,1},{6,2},{7,3},{8,12},{9,13},{10,... | collective-permute-start | bytes 516104 | tf_op jit(solution)/shard_map/ppermute | solution.py:44
  40.3 26.5 %collective-permute-start.2 = (bf16[24,3584]{1,0:T(8,128)(2,1)S(1)}, bf16[24,3584]{1,0:T(8,128)(2,1)S(1)}, u32[]{:S(2)}, u32[]{:S(2)}) collective-permute-start(bf16[24,3584]{1,0:T(8,128)(2,1)S(1)} %copy-done.8), channel_id=1, source_target_pairs={{0,6},{1,7},{2,4},{3,5},{4,2},{5,3},{6,0},{7,1},{8,14},{9,15},{10,... | collective-permute-start | bytes 516104 | tf_op jit(solution)/shard_map/ppermute | solution.py:44
  42.3 25.2 %collective-permute-start.3 = (bf16[24,3584]{1,0:T(8,128)(2,1)S(1)}, bf16[24,3584]{1,0:T(8,128)(2,1)S(1)}, u32[]{:S(2)}, u32[]{:S(2)}) collective-permute-start(bf16[24,3584]{1,0:T(8,128)(2,1)S(1)} %copy-done.7), channel_id=1, source_target_pairs={{0,8},{1,9},{2,10},{3,11},{4,12},{5,13},{6,14},{7,15},{8,0},{9,1},... | collective-permute-start | bytes 516104 | tf_op jit(solution)/shard_map/ppermute | solution.py:44
  47.5 20.7 %collective-permute-start.4 = (bf16[24,3584]{1,0:T(8,128)(2,1)S(1)}, bf16[24,3584]{1,0:T(8,128)(2,1)S(1)}, u32[]{:S(2)}, u32[]{:S(2)}) collective-permute-start(bf16[24,3584]{1,0:T(8,128)(2,1)S(1)} %copy-done.6), channel_id=1, source_target_pairs={{0,10},{1,11},{2,8},{3,9},{4,14},{5,15},{6,12},{7,13},{8,2},{9,3},... | collective-permute-start | bytes 516104 | tf_op jit(solution)/shard_map/ppermute | solution.py:44
  71.4 18.9 %collective-permute-start.7 = (bf16[192,3584]{1,0:T(8,128)(2,1)S(1)}, bf16[192,3584]{1,0:T(8,128)(2,1)S(1)}, u32[]{:S(2)}, u32[]{:S(2)}) collective-permute-start(bf16[192,3584]{1,0:T(8,128)(2,1)S(1)} %get-tuple-element.134), channel_id=1, source_target_pairs={{0,1},{1,0},{2,3},{3,2},{4,5},{5,4},{6,7},{7,6},{8,9},{9,8},{10,11... | collective-permute-start | bytes 4128776 | tf_op jit(solution)/shard_map/ppermute | solution.py:50
  79.3 20.0 %collective-permute-start.48 = (bf16[24,3584]{1,0:T(8,128)(2,1)S(1)}, bf16[24,3584]{1,0:T(8,128)(2,1)S(1)}, u32[]{:S(2)}, u32[]{:S(2)}) collective-permute-start(bf16[24,3584]{1,0:T(8,128)(2,1)S(1)} %get-tuple-element.18), channel_id=1, source_target_pairs={{0,2},{1,3},{2,0},{3,1},{4,6},{5,7},{6,4},{7,5},{8,10},{9,11},{10,... | collective-permute-start | bytes 516104 | tf_op jit(solution)/shard_map/ppermute | solution.py:44
  82.2 20.3 %collective-permute-start.49 = (bf16[24,3584]{1,0:T(8,128)(2,1)S(1)}, bf16[24,3584]{1,0:T(8,128)(2,1)S(1)}, u32[]{:S(2)}, u32[]{:S(2)}) collective-permute-start(bf16[24,3584]{1,0:T(8,128)(2,1)S(1)} %get-tuple-element.17), channel_id=1, source_target_pairs={{0,4},{1,5},{2,6},{3,7},{4,0},{5,1},{6,2},{7,3},{8,12},{9,13},{10,... | collective-permute-start | bytes 516104 | tf_op jit(solution)/shard_map/ppermute | solution.py:44
  85.6 19.9 %collective-permute-start.50 = (bf16[24,3584]{1,0:T(8,128)(2,1)S(1)}, bf16[24,3584]{1,0:T(8,128)(2,1)S(1)}, u32[]{:S(2)}, u32[]{:S(2)}) collective-permute-start(bf16[24,3584]{1,0:T(8,128)(2,1)S(1)} %get-tuple-element.16), channel_id=1, source_target_pairs={{0,6},{1,7},{2,4},{3,5},{4,2},{5,3},{6,0},{7,1},{8,14},{9,15},{10,... | collective-permute-start | bytes 516104 | tf_op jit(solution)/shard_map/ppermute | solution.py:44
  86.2 20.6 %collective-permute-start.51 = (bf16[24,3584]{1,0:T(8,128)(2,1)S(1)}, bf16[24,3584]{1,0:T(8,128)(2,1)S(1)}, u32[]{:S(2)}, u32[]{:S(2)}) collective-permute-start(bf16[24,3584]{1,0:T(8,128)(2,1)S(1)} %get-tuple-element.15), channel_id=1, source_target_pairs={{0,8},{1,9},{2,10},{3,11},{4,12},{5,13},{6,14},{7,15},{8,0},{9,1},... | collective-permute-start | bytes 516104 | tf_op jit(solution)/shard_map/ppermute | solution.py:44
  90.3 56.4 %collective-permute-start.52 = (bf16[24,3584]{1,0:T(8,128)(2,1)S(1)}, bf16[24,3584]{1,0:T(8,128)(2,1)S(1)}, u32[]{:S(2)}, u32[]{:S(2)}) collective-permute-start(bf16[24,3584]{1,0:T(8,128)(2,1)S(1)} %get-tuple-element.14), channel_id=1, source_target_pairs={{0,10},{1,11},{2,8},{3,9},{4,14},{5,15},{6,12},{7,13},{8,2},{9,3},... | collective-permute-start | bytes 516104 | tf_op jit(solution)/shard_map/ppermute | solution.py:44
  99.3 48.6 %collective-permute-start.53 = (bf16[24,3584]{1,0:T(8,128)(2,1)S(1)}, bf16[24,3584]{1,0:T(8,128)(2,1)S(1)}, u32[]{:S(2)}, u32[]{:S(2)}) collective-permute-start(bf16[24,3584]{1,0:T(8,128)(2,1)S(1)} %get-tuple-element.13), channel_id=1, source_target_pairs={{0,12},{1,13},{2,14},{3,15},{4,8},{5,9},{6,10},{7,11},{8,4},{9,5},... | collective-permute-start | bytes 516104 | tf_op jit(solution)/shard_map/ppermute | solution.py:44
  102.4 46.2 %collective-permute-start.54 = (bf16[24,3584]{1,0:T(8,128)(2,1)S(1)}, bf16[24,3584]{1,0:T(8,128)(2,1)S(1)}, u32[]{:S(2)}, u32[]{:S(2)}) collective-permute-start(bf16[24,3584]{1,0:T(8,128)(2,1)S(1)} %get-tuple-element.12), channel_id=1, source_target_pairs={{0,14},{1,15},{2,12},{3,13},{4,10},{5,11},{6,8},{7,9},{8,6},{9,7},... | collective-permute-start | bytes 516104 | tf_op jit(solution)/shard_map/ppermute | solution.py:44
  146.7 17.5 %collective-permute-start.23 = (bf16[192,3584]{1,0:T(8,128)(2,1)S(1)}, bf16[192,3584]{1,0:T(8,128)(2,1)S(1)}, u32[]{:S(2)}, u32[]{:S(2)}) collective-permute-start(bf16[192,3584]{1,0:T(8,128)(2,1)S(1)} %get-tuple-element.120), channel_id=1, source_target_pairs={{0,1},{1,0},{2,3},{3,2},{4,5},{5,4},{6,7},{7,6},{8,9},{9,8},{10,11... | collective-permute-start | bytes 4128776 | tf_op jit(solution)/shard_map/ppermute | solution.py:50
  149.3 18.0 %collective-permute-start.55 = (bf16[192,3584]{1,0:T(8,128)(2,1)}, bf16[192,3584]{1,0:T(8,128)(2,1)S(1)}, u32[]{:S(2)}, u32[]{:S(2)}) collective-permute-start(bf16[192,3584]{1,0:T(8,128)(2,1)} %get-tuple-element.92), channel_id=1, source_target_pairs={{0,1},{1,0},{2,3},{3,2},{4,5},{5,4},{6,7},{7,6},{8,9},{9,8},{10,11... | collective-permute-start | bytes 4128776 | tf_op jit(solution)/shard_map/ppermute | solution.py:50
  155.9 40.3 %collective-permute-start.41 = (bf16[24,3584]{1,0:T(8,128)(2,1)S(1)}, bf16[24,3584]{1,0:T(8,128)(2,1)S(1)}, u32[]{:S(2)}, u32[]{:S(2)}) collective-permute-start(bf16[24,3584]{1,0:T(8,128)(2,1)S(1)} %get-tuple-element.53), channel_id=1, source_target_pairs={{0,2},{1,3},{2,0},{3,1},{4,6},{5,7},{6,4},{7,5},{8,10},{9,11},{10,... | collective-permute-start | bytes 516104 | tf_op jit(solution)/shard_map/ppermute | solution.py:44
  161.7 34.9 %collective-permute-start.42 = (bf16[24,3584]{1,0:T(8,128)(2,1)S(1)}, bf16[24,3584]{1,0:T(8,128)(2,1)S(1)}, u32[]{:S(2)}, u32[]{:S(2)}) collective-permute-start(bf16[24,3584]{1,0:T(8,128)(2,1)S(1)} %get-tuple-element.52), channel_id=1, source_target_pairs={{0,4},{1,5},{2,6},{3,7},{4,0},{5,1},{6,2},{7,3},{8,12},{9,13},{10,... | collective-permute-start | bytes 516104 | tf_op jit(solution)/shard_map/ppermute | solution.py:44
  162.2 37.4 %collective-permute-start.43 = (bf16[24,3584]{1,0:T(8,128)(2,1)S(1)}, bf16[24,3584]{1,0:T(8,128)(2,1)S(1)}, u32[]{:S(2)}, u32[]{:S(2)}) collective-permute-start(bf16[24,3584]{1,0:T(8,128)(2,1)S(1)} %get-tuple-element.51), channel_id=1, source_target_pairs={{0,6},{1,7},{2,4},{3,5},{4,2},{5,3},{6,0},{7,1},{8,14},{9,15},{10,... | collective-permute-start | bytes 516104 | tf_op jit(solution)/shard_map/ppermute | solution.py:44
  164.2 37.5 %collective-permute-start.44 = (bf16[24,3584]{1,0:T(8,128)(2,1)S(1)}, bf16[24,3584]{1,0:T(8,128)(2,1)S(1)}, u32[]{:S(2)}, u32[]{:S(2)}) collective-permute-start(bf16[24,3584]{1,0:T(8,128)(2,1)S(1)} %get-tuple-element.50), channel_id=1, source_target_pairs={{0,8},{1,9},{2,10},{3,11},{4,12},{5,13},{6,14},{7,15},{8,0},{9,1},... | collective-permute-start | bytes 516104 | tf_op jit(solution)/shard_map/ppermute | solution.py:44
  167.3 34.5 %collective-permute-start.45 = (bf16[24,3584]{1,0:T(8,128)(2,1)S(1)}, bf16[24,3584]{1,0:T(8,128)(2,1)S(1)}, u32[]{:S(2)}, u32[]{:S(2)}) collective-permute-start(bf16[24,3584]{1,0:T(8,128)(2,1)S(1)} %get-tuple-element.49), channel_id=1, source_target_pairs={{0,10},{1,11},{2,8},{3,9},{4,14},{5,15},{6,12},{7,13},{8,2},{9,3},... | collective-permute-start | bytes 516104 | tf_op jit(solution)/shard_map/ppermute | solution.py:44
  199.7 25.3 %collective-permute-start.9 = (bf16[24,3584]{1,0:T(8,128)(2,1)S(1)}, bf16[24,3584]{1,0:T(8,128)(2,1)S(1)}, u32[]{:S(2)}, u32[]{:S(2)}) collective-permute-start(bf16[24,3584]{1,0:T(8,128)(2,1)S(1)} %get-tuple-element.69), channel_id=1, source_target_pairs={{0,2},{1,3},{2,0},{3,1},{4,6},{5,7},{6,4},{7,5},{8,10},{9,11},{10,... | collective-permute-start | bytes 516104 | tf_op jit(solution)/shard_map/ppermute | solution.py:44
  201.7 23.3 %collective-permute-start.10 = (bf16[24,3584]{1,0:T(8,128)(2,1)S(1)}, bf16[24,3584]{1,0:T(8,128)(2,1)S(1)}, u32[]{:S(2)}, u32[]{:S(2)}) collective-permute-start(bf16[24,3584]{1,0:T(8,128)(2,1)S(1)} %get-tuple-element.68), channel_id=1, source_target_pairs={{0,4},{1,5},{2,6},{3,7},{4,0},{5,1},{6,2},{7,3},{8,12},{9,13},{10,... | collective-permute-start | bytes 516104 | tf_op jit(solution)/shard_map/ppermute | solution.py:44
  201.8 23.3 %collective-permute-start.11 = (bf16[24,3584]{1,0:T(8,128)(2,1)S(1)}, bf16[24,3584]{1,0:T(8,128)(2,1)S(1)}, u32[]{:S(2)}, u32[]{:S(2)}) collective-permute-start(bf16[24,3584]{1,0:T(8,128)(2,1)S(1)} %get-tuple-element.67), channel_id=1, source_target_pairs={{0,6},{1,7},{2,4},{3,5},{4,2},{5,3},{6,0},{7,1},{8,14},{9,15},{10,... | collective-permute-start | bytes 516104 | tf_op jit(solution)/shard_map/ppermute | solution.py:44
  205.4 23.9 %collective-permute-start.12 = (bf16[24,3584]{1,0:T(8,128)(2,1)S(1)}, bf16[24,3584]{1,0:T(8,128)(2,1)S(1)}, u32[]{:S(2)}, u32[]{:S(2)}) collective-permute-start(bf16[24,3584]{1,0:T(8,128)(2,1)S(1)} %get-tuple-element.66), channel_id=1, source_target_pairs={{0,8},{1,9},{2,10},{3,11},{4,12},{5,13},{6,14},{7,15},{8,0},{9,1},... | collective-permute-start | bytes 516104 | tf_op jit(solution)/shard_map/ppermute | solution.py:44
  210.6 25.7 %collective-permute-start.13 = (bf16[24,3584]{1,0:T(8,128)(2,1)S(1)}, bf16[24,3584]{1,0:T(8,128)(2,1)S(1)}, u32[]{:S(2)}, u32[]{:S(2)}) collective-permute-start(bf16[24,3584]{1,0:T(8,128)(2,1)S(1)} %get-tuple-element.65), channel_id=1, source_target_pairs={{0,10},{1,11},{2,8},{3,9},{4,14},{5,15},{6,12},{7,13},{8,2},{9,3},... | collective-permute-start | bytes 516104 | tf_op jit(solution)/shard_map/ppermute | solution.py:44
  225.2 97.8 %collective-permute-start.66 = (bf16[256,3584]{1,0:T(8,128)(2,1)S(1)}, bf16[256,3584]{1,0:T(8,128)(2,1)S(1)}, u32[]{:S(2)}, u32[]{:S(2)}) collective-permute-start(bf16[256,3584]{1,0:T(8,128)(2,1)S(1)} %convolution_convert_fusion), channel_id=1, source_target_pairs={{0,16},{16,0},{1,17},{17,1},{2,18},{18,2},{3,19},{19,3},{4,20},{20... | collective-permute-start | bytes 5505032 | tf_op jit(solution)/shard_map/ppermute | solution.py:131
  229.3 96.6 %collective-permute-start.65 = (bf16[3584,256]{1,0:T(8,128)(2,1)}, bf16[3584,256]{1,0:T(8,128)(2,1)}, u32[]{:S(2)}, u32[]{:S(2)}) collective-permute-start(bf16[3584,256]{1,0:T(8,128)(2,1)} %convolution_convert_fusion.2), channel_id=1, source_target_pairs={{0,16},{16,0},{1,17},{17,1},{2,18},{18,2},{3,19},{19,3},{4,20},{20... | collective-permute-start | bytes 5505032 | tf_op jit(solution)/shard_map/ppermute | solution.py:131
  236.3 100.6 %collective-permute-start.64 = (bf16[3584,256]{1,0:T(8,128)(2,1)}, bf16[3584,256]{1,0:T(8,128)(2,1)S(1)}, u32[]{:S(2)}, u32[]{:S(2)}) collective-permute-start(bf16[3584,256]{1,0:T(8,128)(2,1)} %convolution_convert_fusion.4), channel_id=1, source_target_pairs={{0,16},{16,0},{1,17},{17,1},{2,18},{18,2},{3,19},{19,3},{4,20},{20... | collective-permute-start | bytes 5505032 | tf_op jit(solution)/shard_map/ppermute | solution.py:131
  (53 other events, 592.8 us)

commit v3 on v2

v3 whole, which is shorter than its diff:
```python
import jax
import jax.numpy as jnp
from jax import lax
from jax.sharding import PartitionSpec as P

TOPK = 2
MB = 2
TOK_MB = 64
F32 = jnp.float32
BF16 = jnp.bfloat16


def dot(a, b, dims):
    return lax.dot_general(a, b, (dims, ((), ())), preferred_element_type=F32)


def route(meta, chip, expert_count, capacity):
    ids, gain = meta[:, :TOPK].astype(jnp.int32), meta[:, TOPK:]
    flat_ids = ids.reshape(MB, TOK_MB * TOPK)
    member = (flat_ids[:, :, None] == jnp.arange(expert_count, dtype=jnp.int32)).astype(jnp.int32)
    running = jnp.cumsum(member, axis=1) - 1
    rank = jnp.sum(member * running, axis=2)
    batch = jnp.arange(MB, dtype=jnp.int32)[:, None]
    target = (((flat_ids ^ chip) * MB + batch) * capacity + rank).reshape(ids.shape)
    slots = jnp.arange(expert_count // 2 * MB * capacity, dtype=jnp.int32)
    matches = (target[:, :, None] == slots).astype(F32)
    placing = jnp.sum(matches, axis=1).astype(BF16)
    weighting = jnp.sum(matches * gain[:, :, None], axis=1)
    return placing, weighting, jnp.sum(weighting, axis=0)


def on_device(acts, grad_out, expert_ids, route_weights, w_gate, w_up, w_down):
    gate_weight, up_weight, down_weight = w_gate[0], w_up[0], w_down[0]
    devices = lax.axis_size("expert")
    chips = devices // 2
    near = chips // 2
    capacity = 3 * TOPK * TOK_MB // (2 * chips)
    piece = MB * capacity
    width = gate_weight.shape[0]
    half_units = gate_weight.shape[1] // 2
    chip = lax.axis_index("expert") // 2

    def hop(rows, distance):
        return lax.ppermute(rows, "expert", [(i, i ^ distance) for i in range(devices)])

    def far(rows):
        return hop(rows, devices // 2)

    def swap(rows):
        return hop(rows, 1)

    def near_exchange(arrays):
        moved = [[array[:piece] for array in arrays]]
        for d in range(1, near):
            sent = [array[d * piece : (d + 1) * piece] for array in arrays]
            got = hop(jnp.concatenate(sent, axis=0), 2 * d)
            moved.append([got[n * piece : (n + 1) * piece] for n in range(len(arrays))])
        return [jnp.concatenate(parts, axis=0) for parts in zip(*moved)]

    def place(placing, rows):
        return dot(placing, rows, ((0,), (0,)))

    meta = jnp.concatenate([expert_ids[0].astype(F32), route_weights[0]], axis=1)
    far_meta = far(meta)
    far_acts = far(acts[0])
    far_grads = far(grad_out[0])
    own_placing, own_weighting, own_gain = route(meta, chip, chips, capacity)
    far_placing, far_weighting, far_gain = route(far_meta, chip, chips, capacity)

    own_in = place(own_placing, acts[0]).astype(BF16)
    own_grad = (place(own_placing, grad_out[0]) * own_gain[:, None]).astype(BF16)
    own_in, own_grad = near_exchange([own_in, own_grad])
    far_in = near_exchange([place(far_placing, far_acts).astype(BF16)])[0]
    far_grad = near_exchange([(place(far_placing, far_grads) * far_gain[:, None]).astype(BF16)])[0]
    rows_in = [far_in, swap(far_in), own_in, swap(own_in)]
    rows_grad = [far_grad, swap(far_grad), own_grad, swap(own_grad)]

    hiddens, gate_grads, up_grads, part_out, part_input = [], [], [], [], []
    for tokens, grads in zip(rows_in, rows_grad):
        pre_gate = dot(tokens, gate_weight, ((1,), (0,)))
        pre_up = dot(tokens, up_weight, ((1,), (0,)))
        sigma = jax.nn.sigmoid(pre_gate)
        active = pre_gate * sigma
        hidden = (active * pre_up).astype(BF16)
        part_out.append(dot(hidden, down_weight, ((1,), (0,))).astype(BF16))
        hidden_grad = dot(grads, down_weight, ((1,), (1,)))
        gate_grad = (hidden_grad * pre_up * sigma * (1.0 + pre_gate * (1.0 - sigma))).astype(BF16)
        up_grad = (hidden_grad * active).astype(BF16)
        part_input.append(
            (
                dot(gate_grad, gate_weight, ((1,), (1,))) + dot(up_grad, up_weight, ((1,), (1,)))
            ).astype(BF16)
        )
        hiddens.append(hidden)
        gate_grads.append(gate_grad)
        up_grads.append(up_grad)

    def expert_sum(parts):
        return (parts[0].astype(F32) + swap(parts[1]).astype(F32)).astype(BF16)

    def weighted(matrix, rows):
        return lax.dot_general(
            matrix,
            rows.astype(F32),
            (((1,), (0,)), ((), ())),
            precision=lax.Precision.HIGHEST,
            preferred_element_type=F32,
        )

    far_out = near_exchange([expert_sum(part_out[:2])])[0]
    far_input = near_exchange([expert_sum(part_input[:2])])[0]
    got_out = far(weighted(far_weighting, far_out).astype(BF16))
    got_input = far(dot(far_placing, far_input, ((1,), (0,))).astype(BF16))
    own_out, own_input = near_exchange([expert_sum(part_out[2:]), expert_sum(part_input[2:])])
    out_acts = (weighted(own_weighting, own_out) + got_out.astype(F32)).astype(BF16)
    grad_acts = (dot(own_placing, own_input, ((1,), (0,))) + got_input.astype(F32)).astype(BF16)

    rank_index = lax.axis_index("pipe")
    rank_count = lax.axis_size("pipe")
    mirror = [(p, rank_count - 1 - p) for p in range(rank_count)]
    kept_half = (rank_index >= rank_count // 2).astype(jnp.int32)

    def halves(units):
        units = jnp.concatenate(units, axis=0)
        return (
            lax.dynamic_slice_in_dim(units, kept_half * half_units, half_units, 1),
            lax.dynamic_slice_in_dim(units, (1 - kept_half) * half_units, half_units, 1),
        )

    all_in = jnp.concatenate(rows_in, axis=0)
    all_grad = jnp.concatenate(rows_grad, axis=0)
    keep_hidden, send_hidden = halves(hiddens)
    keep_gate, send_gate = halves(gate_grads)
    keep_up, send_up = halves(up_grads)
    rows_dims = ((0,), (0,))
    sent = [
        lax.ppermute(dot(a, b, rows_dims).astype(BF16), "pipe", mirror)
        for a, b in ((send_hidden, all_grad), (all_in, send_gate), (all_in, send_up))
    ]
    kept = [
        dot(a, b, rows_dims).astype(BF16)
        for a, b in ((keep_hidden, all_grad), (all_in, keep_gate), (all_in, keep_up))
    ]
    grad_down, grad_gate, grad_up = [
        (own.astype(F32) + other.astype(F32)).astype(BF16)[None] for own, other in zip(kept, sent)
    ]
    return out_acts[None], grad_acts[None], grad_gate, grad_up, grad_down


def solution(mesh):
    tokens = P("pipe", "expert", None)
    columns = P("pipe", None, "expert")
    return jax.shard_map(
        on_device,
        mesh=mesh,
        in_specs=(tokens, tokens, tokens, tokens, columns, columns, tokens),
        out_specs=(tokens, tokens, columns, columns, tokens),
        check_vma=False,
    )
```

time: 344 us -> 390 us (1.13)
  waiting for transfers between devices: 84.4 us -> 261 us
  starting transfers between devices: 147 us -> 35 us
  local copies, waits for them, and re-layouts: 33.8 us -> 13.3 us
    ppermute x64 -> x31, starting transfers between devices: 142 us -> 31.3 us  [hop(): lax.ppermute(rows, 'expert', [(i, i ^ distance) for i in range(devices)])]
    ppermute x3, waiting for transfers between devices: 6.45 us -> 104 us  [on_device(): lax.ppermute(dot(a, b, rows_dims).astype(BF16), 'pipe', mirror)]
    ppermute x64 -> x31, waiting for transfers between devices: 77.9 us -> 157 us  [hop(): lax.ppermute(rows, 'expert', [(i, i ^ distance) for i in range(devices)])]
    unnamed x94 -> x27, local copies, waits for them, and re-layouts: 29.5 us -> 10.4 us
  transfers between devices with their start and end apart: 67 -> 34, of which waited for: 24 -> 15; matrix products, arithmetic and copies ran while one was open for 28% -> 21% of each run, Pallas kernels for 0% -> 0%
where the time goes in v3:
time: 390 us; the launch traced here: 385 us
  waiting for transfers between devices  261 us (67%)
  matrix products  69.1 us (18%)
  starting transfers between devices  35 us (9%)
  local copies, waits for them, and re-layouts  13.3 us (3%)
  other arithmetic  4.86 us (1%)
    ppermute x31, waiting for transfers between devices, hop(): lax.ppermute(rows, 'expert', [(i, i ^ distance) for i in range(devices)])  157 us
    ppermute x3, waiting for transfers between devices, on_device(): lax.ppermute(dot(a, b, rows_dims).astype(BF16), 'pipe', mirror)  104 us
    dot_general x36, matrix products, dot(): return lax.dot_general(a, b, (dims, ((), ())), preferred_element_type=F32)  65 us
    ppermute x31, starting transfers between devices, hop(): lax.ppermute(rows, 'expert', [(i, i ^ distance) for i in range(devices)])  31.3 us
    unnamed x27, local copies, waits for them, and re-layouts  10.4 us
  transfers between devices with their start and end apart: 34, of which 15 were waited for; matrix products, arithmetic and copies ran while one was open for 21% of the time, Pallas kernels for 0%

profile of v3, /device:TPU:0, one launch (start us, length us, event | category | flops | bytes accessed | tf_op | source)
XLA Modules:
  0.0 385.1 jit_solution(5370115310358253754)
XLA Ops:
  2.1 4.0 %collective-permute-start.10 = (f32[128,4]{0,1:T(4,128)S(1)}, f32[128,4]{0,1:T(4,128)S(1)}, u32[]{:S(2)}, u32[]{:S(2)}) collective-permute-start(f32[128,4]{0,1:T(4,128)S(1)} %pad_maximum_fusion.13), channel_id=1, source_target_pairs={{0,8},{1,9},{2,10},{3,11},{4,12},{5,13},{6,14},{7,15},{8,0},{9,1},... | collective-permute-start | bytes 6152 | tf_op jit(solution)/shard_map/ppermute | solution.py:44
  6.2 2.9 collective-permute-start.11
  12.7 1.7 convolution_convert_fusion.11
  15.0 73.1 %collective-permute-done.11 = bf16[128,3584]{1,0:T(8,128)(2,1)S(1)} collective-permute-done((bf16[128,3584]{1,0:T(8,128)(2,1)}, bf16[128,3584]{1,0:T(8,128)(2,1)S(1)}, u32[]{:S(2)}, u32[]{:S(2)}) %collective-permute-start.11) | collective-permute-done | bytes 917536 | tf_op jit(solution)/shard_map/ppermute | solution.py:44
  89.4 3.0 collective-permute-start.13
  94.6 2.0 collective-permute-start.23
  96.6 4.7 %collective-permute-done.14 = bf16[48,3584]{1,0:T(8,128)(2,1)S(1)} collective-permute-done((bf16[48,3584]{1,0:T(8,128)(2,1)S(1)}, bf16[48,3584]{1,0:T(8,128)(2,1)S(1)}, u32[]{:S(2)}, u32[]{:S(2)}) %collective-permute-start.14) | collective-permute-done | bytes 344096 | tf_op jit(solution)/shard_map/ppermute | solution.py:44
  102.9 5.9 %collective-permute-done.13 = bf16[48,3584]{1,0:T(8,128)(2,1)S(1)} collective-permute-done((bf16[48,3584]{1,0:T(8,128)(2,1)S(1)}, bf16[48,3584]{1,0:T(8,128)(2,1)S(1)}, u32[]{:S(2)}, u32[]{:S(2)}) %collective-permute-start.13) | collective-permute-done | bytes 344096 | tf_op jit(solution)/shard_map/ppermute | solution.py:44
  109.0 7.2 %collective-permute-done.24 = bf16[48,3584]{1,0:T(8,128)(2,1)S(1)} collective-permute-done((bf16[48,3584]{1,0:T(8,128)(2,1)S(1)}, bf16[48,3584]{1,0:T(8,128)(2,1)S(1)}, u32[]{:S(2)}, u32[]{:S(2)}) %collective-permute-start.24) | collective-permute-done | bytes 344096 | tf_op jit(solution)/shard_map/ppermute | solution.py:44
  116.2 5.3 %collective-permute-done.23 = bf16[48,3584]{1,0:T(8,128)(2,1)S(1)} collective-permute-done((bf16[48,3584]{1,0:T(8,128)(2,1)S(1)}, bf16[48,3584]{1,0:T(8,128)(2,1)S(1)}, u32[]{:S(2)}, u32[]{:S(2)}) %collective-permute-start.23) | collective-permute-done | bytes 344096 | tf_op jit(solution)/shard_map/ppermute | solution.py:44
  134.9 2.2 collective-permute-start.2
  142.5 1.6 fusion.14
  144.7 6.4 %collective-permute-done = bf16[96,3584]{1,0:T(8,128)(2,1)S(1)} collective-permute-done((bf16[96,3584]{1,0:T(8,128)(2,1)S(1)}, bf16[96,3584]{1,0:T(8,128)(2,1)S(1)}, u32[]{:S(2)}, u32[]{:S(2)}) %collective-permute-start) | collective-permute-done | bytes 688160 | tf_op jit(solution)/shard_map/ppermute | solution.py:44
  153.9 13.3 %collective-permute-done.2 = bf16[96,3584]{1,0:T(8,128)(2,1)S(1)} collective-permute-done((bf16[96,3584]{1,0:T(8,128)(2,1)S(1)}, bf16[96,3584]{1,0:T(8,128)(2,1)S(1)}, u32[]{:S(2)}, u32[]{:S(2)}) %collective-permute-start.2) | collective-permute-done | bytes 688160 | tf_op jit(solution)/shard_map/ppermute | solution.py:44
  174.2 1.7 collective-permute-start.18
  178.1 6.9 %collective-permute-done.19 = bf16[48,3584]{1,0:T(8,128)(2,1)S(1)} collective-permute-done((bf16[48,3584]{1,0:T(8,128)(2,1)S(1)}, bf16[48,3584]{1,0:T(8,128)(2,1)S(1)}, u32[]{:S(2)}, u32[]{:S(2)}) %collective-permute-start.19) | collective-permute-done | bytes 344096 | tf_op jit(solution)/shard_map/ppermute | solution.py:44
  186.1 6.2 %collective-permute-done.18 = bf16[48,3584]{1,0:T(8,128)(2,1)S(1)} collective-permute-done((bf16[48,3584]{1,0:T(8,128)(2,1)S(1)}, bf16[48,3584]{1,0:T(8,128)(2,1)S(1)}, u32[]{:S(2)}, u32[]{:S(2)}) %collective-permute-start.18) | collective-permute-done | bytes 344096 | tf_op jit(solution)/shard_map/ppermute | solution.py:44
  195.9 3.8 collective-permute-done.29
  201.0 10.5 %collective-permute-done.28 = bf16[48,3584]{1,0:T(8,128)(2,1)S(1)} collective-permute-done((bf16[48,3584]{1,0:T(8,128)(2,1)S(1)}, bf16[48,3584]{1,0:T(8,128)(2,1)S(1)}, u32[]{:S(2)}, u32[]{:S(2)}) %collective-permute-start.28) | collective-permute-done | bytes 344096 | tf_op jit(solution)/shard_map/ppermute | solution.py:44
  221.6 13.4 %convolution_convert_fusion.2 = bf16[3584,256]{1,0:T(8,128)(2,1)S(1)} fusion(bf16[768,3584]{1,0:T(8,128)(2,1)} %constant_dynamic-update-slice_fusion, bf16[768,512]{1,0:T(8,128)(2,1)S(1)} %pad_maximum_fusion.5, s32[]{:T(128)S(6)} %select_n.14), kind=kOutput, calls=%fused_computation.11 | convolution fusion | flops 1410203648 | bytes 7733252 | tf_op jit(solution)/shard_map/dot_general | solution.py:14
  235.2 4.2 %convolution_convert_fusion.4 = bf16[3584,256]{1,0:T(8,128)(2,1)S(1)} fusion(bf16[768,3584]{1,0:T(8,128)(2,1)} %constant_dynamic-update-slice_fusion, bf16[768,512]{1,0:T(8,128)(2,1)S(1)} %pad_maximum_fusion.4, s32[]{:T(128)S(6)} %select_n.14), kind=kOutput, calls=%fused_computation.16 | convolution fusion | flops 1410203648 | bytes 7733252 | tf_op jit(solution)/shard_map/dot_general | solution.py:14
  239.4 1.7 convolution_convert_fusion
  244.1 1.6 collective-permute-start.32
  247.4 76.0 %collective-permute-done.31 = bf16[3584,256]{1,0:T(8,128)(2,1)S(1)} collective-permute-done((bf16[3584,256]{1,0:T(8,128)(2,1)S(1)}, bf16[3584,256]{1,0:T(8,128)(2,1)S(1)}, u32[]{:S(2)}, u32[]{:S(2)}) %collective-permute-start.31) | collective-permute-done | bytes 1835040 | tf_op jit(solution)/shard_map/ppermute | solution.py:137
  323.3 5.5 %fusion.19 = bf16[1,3584,256]{2,1,0:T(8,128)(2,1)} fusion(bf16[768,3584]{1,0:T(8,128)(2,1)} %constant_dynamic-update-slice_fusion, bf16[3584,256]{1,0:T(8,128)(2,1)S(1)} %collective-permute-done.31, bf16[768,512]{1,0:T(8,128)(2,1)S(1)} %pad_maximum_fusion.4, s32[]{:T(128)S(6)} %mul.201), kind=kOutput, calls=%fused_computation.39 | convolution fusion | flops 1413873664 | bytes 9568260 | tf_op jit(solution)/shard_map/dot_general | solution.py:14
  328.8 2.0 collective-permute-start.8
  330.9 2.9 fusion.21
  333.8 27.9 %collective-permute-done.32 = bf16[3584,256]{1,0:T(8,128)(2,1)S(1)} collective-permute-done((bf16[3584,256]{1,0:T(8,128)(2,1)S(1)}, bf16[3584,256]{1,0:T(8,128)(2,1)S(1)}, u32[]{:S(2)}, u32[]{:S(2)}) %collective-permute-start.32) | collective-permute-done | bytes 1835040 | tf_op jit(solution)/shard_map/ppermute | solution.py:137
  363.1 3.0 fusion.20
  366.2 12.9 %collective-permute-done.9 = bf16[96,3584]{1,0:T(8,128)(2,1)S(1)} collective-permute-done((bf16[96,3584]{1,0:T(8,128)(2,1)S(1)}, bf16[96,3584]{1,0:T(8,128)(2,1)S(1)}, u32[]{:S(2)}, u32[]{:S(2)}) %collective-permute-start.9) | collective-permute-done | bytes 688160 | tf_op jit(solution)/shard_map/ppermute | solution.py:44
  379.2 2.5 fusion.24
  381.7 3.2 fusion.25
  (146 shorter events, 64.3 us)
Async XLA Ops:
  6.1 86.8 %collective-permute-start.21 = (bf16[128,3584]{1,0:T(8,128)(2,1)}, bf16[128,3584]{1,0:T(8,128)(2,1)S(1)}, u32[]{:S(2)}, u32[]{:S(2)}) collective-permute-start(bf16[128,3584]{1,0:T(8,128)(2,1)} %bitcast.123), channel_id=1, source_target_pairs={{0,8},{1,9},{2,10},{3,11},{4,12},{5,13},{6,14},{7,15},{8,0},{9,1},... | collective-permute-start | bytes 2752520 | tf_op jit(solution)/shard_map/ppermute | solution.py:44
  6.2 81.8 %collective-permute-start.11 = (bf16[128,3584]{1,0:T(8,128)(2,1)}, bf16[128,3584]{1,0:T(8,128)(2,1)S(1)}, u32[]{:S(2)}, u32[]{:S(2)}) collective-permute-start(bf16[128,3584]{1,0:T(8,128)(2,1)} %bitcast.122), channel_id=1, source_target_pairs={{0,8},{1,9},{2,10},{3,11},{4,12},{5,13},{6,14},{7,15},{8,0},{9,1},... | collective-permute-start | bytes 2752520 | tf_op jit(solution)/shard_map/ppermute | solution.py:44
  89.4 11.9 %collective-permute-start.14 = (bf16[48,3584]{1,0:T(8,128)(2,1)S(1)}, bf16[48,3584]{1,0:T(8,128)(2,1)S(1)}, u32[]{:S(2)}, u32[]{:S(2)}) collective-permute-start(bf16[48,3584]{1,0:T(8,128)(2,1)S(1)} %get-tuple-element.27), channel_id=1, source_target_pairs={{0,6},{1,7},{2,4},{3,5},{4,2},{5,3},{6,0},{7,1},{8,14},{9,15},{10,... | collective-permute-start | bytes 1032200 | tf_op jit(solution)/shard_map/ppermute | solution.py:44
  89.4 19.4 %collective-permute-start.13 = (bf16[48,3584]{1,0:T(8,128)(2,1)S(1)}, bf16[48,3584]{1,0:T(8,128)(2,1)S(1)}, u32[]{:S(2)}, u32[]{:S(2)}) collective-permute-start(bf16[48,3584]{1,0:T(8,128)(2,1)S(1)} %get-tuple-element.28), channel_id=1, source_target_pairs={{0,4},{1,5},{2,6},{3,7},{4,0},{5,1},{6,2},{7,3},{8,12},{9,13},{10,... | collective-permute-start | bytes 1032200 | tf_op jit(solution)/shard_map/ppermute | solution.py:44
  92.4 16.4 %collective-permute-start.12 = (bf16[48,3584]{1,0:T(8,128)(2,1)S(1)}, bf16[48,3584]{1,0:T(8,128)(2,1)S(1)}, u32[]{:S(2)}, u32[]{:S(2)}) collective-permute-start(bf16[48,3584]{1,0:T(8,128)(2,1)S(1)} %get-tuple-element.29), channel_id=1, source_target_pairs={{0,2},{1,3},{2,0},{3,1},{4,6},{5,7},{6,4},{7,5},{8,10},{9,11},{10,... | collective-permute-start | bytes 1032200 | tf_op jit(solution)/shard_map/ppermute | solution.py:44
  93.6 22.6 %collective-permute-start.24 = (bf16[48,3584]{1,0:T(8,128)(2,1)S(1)}, bf16[48,3584]{1,0:T(8,128)(2,1)S(1)}, u32[]{:S(2)}, u32[]{:S(2)}) collective-permute-start(bf16[48,3584]{1,0:T(8,128)(2,1)S(1)} %get-tuple-element.17), channel_id=1, source_target_pairs={{0,6},{1,7},{2,4},{3,5},{4,2},{5,3},{6,0},{7,1},{8,14},{9,15},{10,... | collective-permute-start | bytes 1032200 | tf_op jit(solution)/shard_map/ppermute | solution.py:44
  94.6 26.9 %collective-permute-start.23 = (bf16[48,3584]{1,0:T(8,128)(2,1)S(1)}, bf16[48,3584]{1,0:T(8,128)(2,1)S(1)}, u32[]{:S(2)}, u32[]{:S(2)}) collective-permute-start(bf16[48,3584]{1,0:T(8,128)(2,1)S(1)} %get-tuple-element.18), channel_id=1, source_target_pairs={{0,4},{1,5},{2,6},{3,7},{4,0},{5,1},{6,2},{7,3},{8,12},{9,13},{10,... | collective-permute-start | bytes 1032200 | tf_op jit(solution)/shard_map/ppermute | solution.py:44
  101.4 20.1 %collective-permute-start.22 = (bf16[48,3584]{1,0:T(8,128)(2,1)S(1)}, bf16[48,3584]{1,0:T(8,128)(2,1)S(1)}, u32[]{:S(2)}, u32[]{:S(2)}) collective-permute-start(bf16[48,3584]{1,0:T(8,128)(2,1)S(1)} %get-tuple-element.19), channel_id=1, source_target_pairs={{0,2},{1,3},{2,0},{3,1},{4,6},{5,7},{6,4},{7,5},{8,10},{9,11},{10,... | collective-permute-start | bytes 1032200 | tf_op jit(solution)/shard_map/ppermute | solution.py:44
  108.9 22.0 %collective-permute-start.15 = (bf16[192,3584]{1,0:T(8,128)(2,1)S(1)}, bf16[192,3584]{1,0:T(8,128)(2,1)S(1)}, u32[]{:S(2)}, u32[]{:S(2)}) collective-permute-start(bf16[192,3584]{1,0:T(8,128)(2,1)S(1)} %pad_maximum_fusion.2), channel_id=1, source_target_pairs={{0,1},{1,0},{2,3},{3,2},{4,5},{5,4},{6,7},{7,6},{8,9},{9,8},{10,11... | collective-permute-start | bytes 4128776 | tf_op jit(solution)/shard_map/ppermute | solution.py:44
  133.2 17.9 %collective-permute-start = (bf16[96,3584]{1,0:T(8,128)(2,1)S(1)}, bf16[96,3584]{1,0:T(8,128)(2,1)S(1)}, u32[]{:S(2)}, u32[]{:S(2)}) collective-permute-start(bf16[96,3584]{1,0:T(8,128)(2,1)S(1)} %pad_maximum_fusion.7), channel_id=1, source_target_pairs={{0,2},{1,3},{2,0},{3,1},{4,6},{5,7},{6,4},{7,5},{8,10},{9,11},{10,... | collective-permute-start | bytes 2064392 | tf_op jit(solution)/shard_map/ppermute | solution.py:44
  134.7 18.3 %collective-permute-start.1 = (bf16[96,3584]{1,0:T(8,128)(2,1)S(1)}, bf16[96,3584]{1,0:T(8,128)(2,1)S(1)}, u32[]{:S(2)}, u32[]{:S(2)}) collective-permute-start(bf16[96,3584]{1,0:T(8,128)(2,1)S(1)} %pad_maximum_fusion.8), channel_id=1, source_target_pairs={{0,4},{1,5},{2,6},{3,7},{4,0},{5,1},{6,2},{7,3},{8,12},{9,13},{10,... | collective-permute-start | bytes 2064392 | tf_op jit(solution)/shard_map/ppermute | solution.py:44
  134.9 32.3 %collective-permute-start.2 = (bf16[96,3584]{1,0:T(8,128)(2,1)S(1)}, bf16[96,3584]{1,0:T(8,128)(2,1)S(1)}, u32[]{:S(2)}, u32[]{:S(2)}) collective-permute-start(bf16[96,3584]{1,0:T(8,128)(2,1)S(1)} %pad_maximum_fusion.9), channel_id=1, source_target_pairs={{0,6},{1,7},{2,4},{3,5},{4,2},{5,3},{6,0},{7,1},{8,14},{9,15},{10,... | collective-permute-start | bytes 2064392 | tf_op jit(solution)/shard_map/ppermute | solution.py:44
  141.1 30.9 %collective-permute-start.16 = (bf16[192,3584]{1,0:T(8,128)(2,1)S(1)}, bf16[192,3584]{1,0:T(8,128)(2,1)S(1)}, u32[]{:S(2)}, u32[]{:S(2)}) collective-permute-start(bf16[192,3584]{1,0:T(8,128)(2,1)S(1)} %convolution_convert_fusion.6), channel_id=1, source_target_pairs={{0,1},{1,0},{2,3},{3,2},{4,5},{5,4},{6,7},{7,6},{8,9},{9,8},{10,11... | collective-permute-start | bytes 4128776 | tf_op jit(solution)/shard_map/ppermute | solution.py:44
  144.1 31.8 %collective-permute-start.26 = (bf16[192,3584]{1,0:T(8,128)(2,1)S(1)}, bf16[192,3584]{1,0:T(8,128)(2,1)S(1)}, u32[]{:S(2)}, u32[]{:S(2)}) collective-permute-start(bf16[192,3584]{1,0:T(8,128)(2,1)S(1)} %fusion.14), channel_id=1, source_target_pairs={{0,1},{1,0},{2,3},{3,2},{4,5},{5,4},{6,7},{7,6},{8,9},{9,8},{10,11... | collective-permute-start | bytes 4128776 | tf_op jit(solution)/shard_map/ppermute | solution.py:44
  168.1 44.7 %collective-permute-start.3 = (bf16[192,3584]{1,0:T(8,128)(2,1)S(1)}, bf16[192,3584]{1,0:T(8,128)(2,1)S(1)}, u32[]{:S(2)}, u32[]{:S(2)}) collective-permute-start(bf16[192,3584]{1,0:T(8,128)(2,1)S(1)} %pad_maximum_fusion), channel_id=1, source_target_pairs={{0,1},{1,0},{2,3},{3,2},{4,5},{5,4},{6,7},{7,6},{8,9},{9,8},{10,11... | collective-permute-start | bytes 4128776 | tf_op jit(solution)/shard_map/ppermute | solution.py:44
  168.3 45.4 %collective-permute-start.5 = (bf16[192,3584]{1,0:T(8,128)(2,1)S(1)}, bf16[192,3584]{1,0:T(8,128)(2,1)S(1)}, u32[]{:S(2)}, u32[]{:S(2)}) collective-permute-start(bf16[192,3584]{1,0:T(8,128)(2,1)S(1)} %pad_maximum_fusion.1), channel_id=1, source_target_pairs={{0,1},{1,0},{2,3},{3,2},{4,5},{5,4},{6,7},{7,6},{8,9},{9,8},{10,11... | collective-permute-start | bytes 4128776 | tf_op jit(solution)/shard_map/ppermute | solution.py:44
  173.0 11.9 %collective-permute-start.19 = (bf16[48,3584]{1,0:T(8,128)(2,1)S(1)}, bf16[48,3584]{1,0:T(8,128)(2,1)S(1)}, u32[]{:S(2)}, u32[]{:S(2)}) collective-permute-start(bf16[48,3584]{1,0:T(8,128)(2,1)S(1)} %get-tuple-element.44), channel_id=1, source_target_pairs={{0,6},{1,7},{2,4},{3,5},{4,2},{5,3},{6,0},{7,1},{8,14},{9,15},{10,... | collective-permute-start | bytes 1032200 | tf_op jit(solution)/shard_map/ppermute | solution.py:44
  174.2 18.1 %collective-permute-start.18 = (bf16[48,3584]{1,0:T(8,128)(2,1)S(1)}, bf16[48,3584]{1,0:T(8,128)(2,1)S(1)}, u32[]{:S(2)}, u32[]{:S(2)}) collective-permute-start(bf16[48,3584]{1,0:T(8,128)(2,1)S(1)} %get-tuple-element.45), channel_id=1, source_target_pairs={{0,4},{1,5},{2,6},{3,7},{4,0},{5,1},{6,2},{7,3},{8,12},{9,13},{10,... | collective-permute-start | bytes 1032200 | tf_op jit(solution)/shard_map/ppermute | solution.py:44
  175.9 16.6 %collective-permute-start.17 = (bf16[48,3584]{1,0:T(8,128)(2,1)S(1)}, bf16[48,3584]{1,0:T(8,128)(2,1)S(1)}, u32[]{:S(2)}, u32[]{:S(2)}) collective-permute-start(bf16[48,3584]{1,0:T(8,128)(2,1)S(1)} %get-tuple-element.46), channel_id=1, source_target_pairs={{0,2},{1,3},{2,0},{3,1},{4,6},{5,7},{6,4},{7,5},{8,10},{9,11},{10,... | collective-permute-start | bytes 1032200 | tf_op jit(solution)/shard_map/ppermute | solution.py:44
  185.0 14.8 %collective-permute-start.29 = (bf16[48,3584]{1,0:T(8,128)(2,1)S(1)}, bf16[48,3584]{1,0:T(8,128)(2,1)S(1)}, u32[]{:S(2)}, u32[]{:S(2)}) collective-permute-start(bf16[48,3584]{1,0:T(8,128)(2,1)S(1)} %get-tuple-element.36), channel_id=1, source_target_pairs={{0,6},{1,7},{2,4},{3,5},{4,2},{5,3},{6,0},{7,1},{8,14},{9,15},{10,... | collective-permute-start | bytes 1032200 | tf_op jit(solution)/shard_map/ppermute | solution.py:44
  192.3 19.2 %collective-permute-start.28 = (bf16[48,3584]{1,0:T(8,128)(2,1)S(1)}, bf16[48,3584]{1,0:T(8,128)(2,1)S(1)}, u32[]{:S(2)}, u32[]{:S(2)}) collective-permute-start(bf16[48,3584]{1,0:T(8,128)(2,1)S(1)} %get-tuple-element.37), channel_id=1, source_target_pairs={{0,4},{1,5},{2,6},{3,7},{4,0},{5,1},{6,2},{7,3},{8,12},{9,13},{10,... | collective-permute-start | bytes 1032200 | tf_op jit(solution)/shard_map/ppermute | solution.py:44
  192.5 18.9 %collective-permute-start.27 = (bf16[48,3584]{1,0:T(8,128)(2,1)S(1)}, bf16[48,3584]{1,0:T(8,128)(2,1)S(1)}, u32[]{:S(2)}, u32[]{:S(2)}) collective-permute-start(bf16[48,3584]{1,0:T(8,128)(2,1)S(1)} %get-tuple-element.38), channel_id=1, source_target_pairs={{0,2},{1,3},{2,0},{3,1},{4,6},{5,7},{6,4},{7,5},{8,10},{9,11},{10,... | collective-permute-start | bytes 1032200 | tf_op jit(solution)/shard_map/ppermute | solution.py:44
  199.8 181.9 %collective-permute-start.20 = (bf16[128,3584]{1,0:T(8,128)(2,1)S(1)}, bf16[128,3584]{1,0:T(8,128)(2,1)}, u32[]{:S(2)}, u32[]{:S(2)}) collective-permute-start(bf16[128,3584]{1,0:T(8,128)(2,1)S(1)} %convolution_convert_fusion.13), channel_id=1, source_target_pairs={{0,8},{1,9},{2,10},{3,11},{4,12},{5,13},{6,14},{7,15},{8,0},{9,1},... | collective-permute-start | bytes 2752520 | tf_op jit(solution)/shard_map/ppermute | solution.py:44
  212.8 166.4 %collective-permute-start.30 = (bf16[128,3584]{1,0:T(8,128)(2,1)}, bf16[128,3584]{1,0:T(8,128)(2,1)}, u32[]{:S(2)}, u32[]{:S(2)}) collective-permute-start(bf16[128,3584]{1,0:T(8,128)(2,1)} %convolution_convert_fusion.12), channel_id=1, source_target_pairs={{0,8},{1,9},{2,10},{3,11},{4,12},{5,13},{6,14},{7,15},{8,0},{9,1},... | collective-permute-start | bytes 2752520 | tf_op jit(solution)/shard_map/ppermute | solution.py:44
  218.3 24.3 %collective-permute-start.4 = (bf16[192,3584]{1,0:T(8,128)(2,1)S(1)}, bf16[192,3584]{1,0:T(8,128)(2,1)S(1)}, u32[]{:S(2)}, u32[]{:S(2)}) collective-permute-start(bf16[192,3584]{1,0:T(8,128)(2,1)S(1)} %convolution_convert_fusion.9), channel_id=1, source_target_pairs={{0,1},{1,0},{2,3},{3,2},{4,5},{5,4},{6,7},{7,6},{8,9},{9,8},{10,11... | collective-permute-start | bytes 4128776 | tf_op jit(solution)/shard_map/ppermute | solution.py:44
  219.8 24.3 %collective-permute-start.6 = (bf16[192,3584]{1,0:T(8,128)(2,1)S(1)}, bf16[192,3584]{1,0:T(8,128)(2,1)S(1)}, u32[]{:S(2)}, u32[]{:S(2)}) collective-permute-start(bf16[192,3584]{1,0:T(8,128)(2,1)S(1)} %fusion.11), channel_id=1, source_target_pairs={{0,1},{1,0},{2,3},{3,2},{4,5},{5,4},{6,7},{7,6},{8,9},{9,8},{10,11... | collective-permute-start | bytes 4128776 | tf_op jit(solution)/shard_map/ppermute | solution.py:44
  241.0 87.8 %collective-permute-start.33 = (bf16[256,3584]{1,0:T(8,128)(2,1)S(1)}, bf16[256,3584]{1,0:T(8,128)(2,1)S(1)}, u32[]{:S(2)}, u32[]{:S(2)}) collective-permute-start(bf16[256,3584]{1,0:T(8,128)(2,1)S(1)} %convolution_convert_fusion), channel_id=1, source_target_pairs={{0,16},{16,0},{1,17},{17,1},{2,18},{18,2},{3,19},{19,3},{4,20},{20... | collective-permute-start | bytes 5505032 | tf_op jit(solution)/shard_map/ppermute | solution.py:137
  242.6 80.7 %collective-permute-start.31 = (bf16[3584,256]{1,0:T(8,128)(2,1)S(1)}, bf16[3584,256]{1,0:T(8,128)(2,1)S(1)}, u32[]{:S(2)}, u32[]{:S(2)}) collective-permute-start(bf16[3584,256]{1,0:T(8,128)(2,1)S(1)} %convolution_convert_fusion.4), channel_id=1, source_target_pairs={{0,16},{16,0},{1,17},{17,1},{2,18},{18,2},{3,19},{19,3},{4,20},{20... | collective-permute-start | bytes 5505032 | tf_op jit(solution)/shard_map/ppermute | solution.py:137
  244.1 117.6 %collective-permute-start.32 = (bf16[3584,256]{1,0:T(8,128)(2,1)S(1)}, bf16[3584,256]{1,0:T(8,128)(2,1)S(1)}, u32[]{:S(2)}, u32[]{:S(2)}) collective-permute-start(bf16[3584,256]{1,0:T(8,128)(2,1)S(1)} %convolution_convert_fusion.2), channel_id=1, source_target_pairs={{0,16},{16,0},{1,17},{17,1},{2,18},{18,2},{3,19},{19,3},{4,20},{20... | collective-permute-start | bytes 5505032 | tf_op jit(solution)/shard_map/ppermute | solution.py:137
  323.3 42.8 %collective-permute-start.7 = (bf16[96,3584]{1,0:T(8,128)(2,1)S(1)}, bf16[96,3584]{1,0:T(8,128)(2,1)S(1)}, u32[]{:S(2)}, u32[]{:S(2)}) collective-permute-start(bf16[96,3584]{1,0:T(8,128)(2,1)S(1)} %pad_maximum_fusion.10), channel_id=1, source_target_pairs={{0,2},{1,3},{2,0},{3,1},{4,6},{5,7},{6,4},{7,5},{8,10},{9,11},{10,... | collective-permute-start | bytes 2064392 | tf_op jit(solution)/shard_map/ppermute | solution.py:44
  328.8 37.3 %collective-permute-start.8 = (bf16[96,3584]{1,0:T(8,128)(2,1)S(1)}, bf16[96,3584]{1,0:T(8,128)(2,1)S(1)}, u32[]{:S(2)}, u32[]{:S(2)}) collective-permute-start(bf16[96,3584]{1,0:T(8,128)(2,1)S(1)} %pad_maximum_fusion.11), channel_id=1, source_target_pairs={{0,4},{1,5},{2,6},{3,7},{4,0},{5,1},{6,2},{7,3},{8,12},{9,13},{10,... | collective-permute-start | bytes 2064392 | tf_op jit(solution)/shard_map/ppermute | solution.py:44
  361.7 17.4 %collective-permute-start.9 = (bf16[96,3584]{1,0:T(8,128)(2,1)S(1)}, bf16[96,3584]{1,0:T(8,128)(2,1)S(1)}, u32[]{:S(2)}, u32[]{:S(2)}) collective-permute-start(bf16[96,3584]{1,0:T(8,128)(2,1)S(1)} %pad_maximum_fusion.12), channel_id=1, source_target_pairs={{0,6},{1,7},{2,4},{3,5},{4,2},{5,3},{6,0},{7,1},{8,14},{9,15},{10,... | collective-permute-start | bytes 2064392 | tf_op jit(solution)/shard_map/ppermute | solution.py:44
  (8 other events, 283.9 us)

commit v4 on v3

--- a/solution.py
+++ b/solution.py
@@ -14,14 +14,14 @@
     return lax.dot_general(a, b, (dims, ((), ())), preferred_element_type=F32)
 
 
-def route(meta, chip, expert_count, capacity):
+def route(meta, half, expert_count, capacity):
     ids, gain = meta[:, :TOPK].astype(jnp.int32), meta[:, TOPK:]
     flat_ids = ids.reshape(MB, TOK_MB * TOPK)
     member = (flat_ids[:, :, None] == jnp.arange(expert_count, dtype=jnp.int32)).astype(jnp.int32)
     running = jnp.cumsum(member, axis=1) - 1
     rank = jnp.sum(member * running, axis=2)
     batch = jnp.arange(MB, dtype=jnp.int32)[:, None]
-    target = (((flat_ids ^ chip) * MB + batch) * capacity + rank).reshape(ids.shape)
+    target = (((flat_ids - half * (expert_count // 2)) * MB + batch) * capacity + rank).reshape(ids.shape)
     slots = jnp.arange(expert_count // 2 * MB * capacity, dtype=jnp.int32)
     matches = (target[:, :, None] == slots).astype(F32)
     placing = jnp.sum(matches, axis=1).astype(BF16)
@@ -38,7 +38,7 @@
     piece = MB * capacity
     width = gate_weight.shape[0]
     half_units = gate_weight.shape[1] // 2
-    chip = lax.axis_index("expert") // 2
+    half = (lax.axis_index("expert") >= devices // 2).astype(jnp.int32)
 
     def hop(rows, distance):
         return lax.ppermute(rows, "expert", [(i, i ^ distance) for i in range(devices)])
@@ -49,13 +49,24 @@
     def swap(rows):
         return hop(rows, 1)
 
-    def near_exchange(arrays):
-        moved = [[array[:piece] for array in arrays]]
-        for d in range(1, near):
-            sent = [array[d * piece : (d + 1) * piece] for array in arrays]
-            got = hop(jnp.concatenate(sent, axis=0), 2 * d)
-            moved.append([got[n * piece : (n + 1) * piece] for n in range(len(arrays))])
-        return [jnp.concatenate(parts, axis=0) for parts in zip(*moved)]
+    groups = [
+        [(half * near + member) * 2 + core for member in range(near)]
+        for half in range(2)
+        for core in range(2)
+    ]
+
+    def near_exchange(rows):
+        return lax.all_to_all(
+            rows.reshape(near, piece, width),
+            "expert",
+            split_axis=0,
+            concat_axis=0,
+            axis_index_groups=groups,
+            tiled=True,
+        ).reshape(near * piece, width)
+
+    def after(rows, *others):
+        return lax.optimization_barrier((rows, *others))[0]
 
     def place(placing, rows):
         return dot(placing, rows, ((0,), (0,)))
@@ -63,15 +74,17 @@
     meta = jnp.concatenate([expert_ids[0].astype(F32), route_weights[0]], axis=1)
     far_meta = far(meta)
     far_acts = far(acts[0])
-    far_grads = far(grad_out[0])
-    own_placing, own_weighting, own_gain = route(meta, chip, chips, capacity)
-    far_placing, far_weighting, far_gain = route(far_meta, chip, chips, capacity)
+    own_placing, own_weighting, own_gain = route(meta, half, chips, capacity)
+    far_placing, far_weighting, far_gain = route(far_meta, half, chips, capacity)
 
-    own_in = place(own_placing, acts[0]).astype(BF16)
+    own_in = near_exchange(place(own_placing, acts[0]).astype(BF16))
     own_grad = (place(own_placing, grad_out[0]) * own_gain[:, None]).astype(BF16)
-    own_in, own_grad = near_exchange([own_in, own_grad])
-    far_in = near_exchange([place(far_placing, far_acts).astype(BF16)])[0]
-    far_grad = near_exchange([(place(far_placing, far_grads) * far_gain[:, None]).astype(BF16)])[0]
+    own_grad = near_exchange(after(own_grad, own_in))
+    far_grads = far(after(grad_out[0], far_meta))
+    far_acts = after(far_acts, own_grad)
+    far_in = near_exchange(place(far_placing, far_acts).astype(BF16))
+    far_grads = after(far_grads, far_in)
+    far_grad = near_exchange((place(far_placing, far_grads) * far_gain[:, None]).astype(BF16))
     rows_in = [far_in, swap(far_in), own_in, swap(own_in)]
     rows_grad = [far_grad, swap(far_grad), own_grad, swap(own_grad)]
 
@@ -107,11 +120,12 @@
             preferred_element_type=F32,
         )
 
-    far_out = near_exchange([expert_sum(part_out[:2])])[0]
-    far_input = near_exchange([expert_sum(part_input[:2])])[0]
+    far_out = near_exchange(expert_sum(part_out[:2]))
     got_out = far(weighted(far_weighting, far_out).astype(BF16))
+    far_input = near_exchange(after(expert_sum(part_input[:2]), far_out))
     got_input = far(dot(far_placing, far_input, ((1,), (0,))).astype(BF16))
-    own_out, own_input = near_exchange([expert_sum(part_out[2:]), expert_sum(part_input[2:])])
+    own_out = near_exchange(after(expert_sum(part_out[2:]), far_input))
+    own_input = near_exchange(after(expert_sum(part_input[2:]), own_out))
     out_acts = (weighted(own_weighting, own_out) + got_out.astype(F32)).astype(BF16)
     grad_acts = (dot(own_placing, own_input, ((1,), (0,))) + got_input.astype(F32)).astype(BF16)
 
@@ -133,10 +147,10 @@
     keep_gate, send_gate = halves(gate_grads)
     keep_up, send_up = halves(up_grads)
     rows_dims = ((0,), (0,))
-    sent = [
-        lax.ppermute(dot(a, b, rows_dims).astype(BF16), "pipe", mirror)
-        for a, b in ((send_hidden, all_grad), (all_in, send_gate), (all_in, send_up))
-    ]
+    sent = []
+    for a, b in ((send_hidden, all_grad), (all_in, send_gate), (all_in, send_up)):
+        local = dot(a, b, rows_dims).astype(BF16)
+        sent.append(lax.ppermute(after(local, *sent[-1:]), "pipe", mirror))
     kept = [
         dot(a, b, rows_dims).astype(BF16)
         for a, b in ((keep_hidden, all_grad), (all_in, keep_gate), (all_in, keep_up))

time: 390 us -> 374 us (0.959)
  waiting for transfers between devices: 261 us -> 205 us
  matrix products: 69.1 us -> 105 us
  starting transfers between devices: 35 us -> 53.5 us
  local copies, waits for them, and re-layouts: 13.3 us -> 2.52 us
    ppermute x3, waiting for transfers between devices: 104 us -> 61.1 us  [on_device(): sent.append(lax.ppermute(after(local, *sent[-1:]), 'pipe', mirror))]
    ppermute x31 -> x13, waiting for transfers between devices: 157 us -> 120 us  [hop(): lax.ppermute(rows, 'expert', [(i, i ^ distance) for i in range(devices)])]
    all_to_all x0 -> x8, starting transfers between devices: none -> 34.4 us  [near_exchange(): lax.all_to_all(rows.reshape(near, piece, width), 'expert', split_axis=0,...]
    dot_general x36, matrix products: 65 us -> 98 us  [dot(): return lax.dot_general(a, b, (dims, ((), ())), preferred_element_type=F32)]
    all_to_all x0 -> x8, waiting for transfers between devices: none -> 23.9 us  [near_exchange(): lax.all_to_all(rows.reshape(near, piece, width), 'expert', split_axis=0,...]
    ppermute x31 -> x13, starting transfers between devices: 31.3 us -> 14.7 us  [hop(): lax.ppermute(rows, 'expert', [(i, i ^ distance) for i in range(devices)])]
    unnamed x27 -> x102, local copies, waits for them, and re-layouts: 10.4 us -> 1.52 us
  transfers between devices with their start and end apart: 34 -> 24, of which waited for: 15 -> 11; matrix products, arithmetic and copies ran while one was open for 21% -> 24% of each run, Pallas kernels for 0% -> 0%
where the time goes in v4:
time: 374 us; the launch traced here: 373 us
  waiting for transfers between devices  205 us (55%)
  matrix products  105 us (28%)
  starting transfers between devices  53.5 us (14%)
  other arithmetic  5.31 us (1%)
    ppermute x13, waiting for transfers between devices, hop(): lax.ppermute(rows, 'expert', [(i, i ^ distance) for i in range(devices)])  120 us
    dot_general x36, matrix products, dot(): return lax.dot_general(a, b, (dims, ((), ())), preferred_element_type=F32)  98 us
    ppermute x3, waiting for transfers between devices, on_device(): sent.append(lax.ppermute(after(local, *sent[-1:]), 'pipe', mirror))  61.1 us
    all_to_all x8, starting transfers between devices, near_exchange(): lax.all_to_all(rows.reshape(near, piece, width), 'expert', split_axis=0,...  34.4 us
    all_to_all x8, waiting for transfers between devices, near_exchange(): lax.all_to_all(rows.reshape(near, piece, width), 'expert', split_axis=0,...  23.9 us
    ppermute x13, starting transfers between devices, hop(): lax.ppermute(rows, 'expert', [(i, i ^ distance) for i in range(devices)])  14.7 us
  transfers between devices with their start and end apart: 24, of which 11 were waited for; matrix products, arithmetic and copies ran while one was open for 24% of the time, Pallas kernels for 0%

profile of v4, /device:TPU:0, one launch (start us, length us, event | category | flops | bytes accessed | tf_op | source)
XLA Modules:
  0.0 372.7 jit_solution(10180563202970550520)
XLA Ops:
  2.0 4.0 %collective-permute-start.2 = (f32[128,4]{0,1:T(4,128)S(1)}, f32[128,4]{0,1:T(4,128)S(1)}, u32[]{:S(2)}, u32[]{:S(2)}) collective-permute-start(f32[128,4]{0,1:T(4,128)S(1)} %pad_maximum_fusion.7), channel_id=1, source_target_pairs={{0,8},{1,9},{2,10},{3,11},{4,12},{5,13},{6,14},{7,15},{8,0},{9,1},... | collective-permute-start | bytes 6152 | tf_op jit(solution)/shard_map/ppermute | solution.py:44
  13.5 4.1 %all-to-all-start = ((bf16[4,48,3584]{2,1,0:T(8,128)(2,1)}), bf16[4,48,3584]{2,1,0:T(8,128)(2,1)S(1)}, u32[]{:S(2)}, u32[]{:S(2)}) async-start(bf16[4,48,3584]{2,1,0:T(8,128)(2,1)} %bitcast.3), calls=%async_computation | async-start | bytes 2752512 | tf_op jit(solution)/shard_map/all_to_all | solution.py:59
  19.2 14.4 %all-to-all-done = bf16[4,48,3584]{2,1,0:T(8,128)(2,1)S(1)} async-done(((bf16[4,48,3584]{2,1,0:T(8,128)(2,1)}), bf16[4,48,3584]{2,1,0:T(8,128)(2,1)S(1)}, u32[]{:S(2)}, u32[]{:S(2)}) %all-to-all-start) | async-done | bytes 1376288 | tf_op jit(solution)/shard_map/all_to_all | solution.py:59
  33.7 4.3 %all-to-all-start.1 = ((bf16[4,48,3584]{2,1,0:T(8,128)(2,1)}), bf16[4,48,3584]{2,1,0:T(8,128)(2,1)}, u32[]{:S(2)}, u32[]{:S(2)}) async-start(bf16[4,48,3584]{2,1,0:T(8,128)(2,1)} %bitcast.9), calls=%async_computation.1 | async-start | bytes 2752512 | tf_op jit(solution)/shard_map/all_to_all | solution.py:59
  41.3 38.6 %collective-permute-done.4 = bf16[128,3584]{1,0:T(8,128)(2,1)S(1)} collective-permute-done((bf16[128,3584]{1,0:T(8,128)(2,1)S(1)}, bf16[128,3584]{1,0:T(8,128)(2,1)S(1)}, u32[]{:S(2)}, u32[]{:S(2)}) %collective-permute-start.4) | collective-permute-done | bytes 917536 | tf_op jit(solution)/shard_map/ppermute | solution.py:44
  81.5 3.5 all-to-all-start.2
  87.9 38.8 %collective-permute-done.3 = bf16[128,3584]{1,0:T(8,128)(2,1)} collective-permute-done((bf16[128,3584]{1,0:T(8,128)(2,1)}, bf16[128,3584]{1,0:T(8,128)(2,1)}, u32[]{:S(2)}, u32[]{:S(2)}) %collective-permute-start.3) | collective-permute-done | bytes 917536 | tf_op jit(solution)/shard_map/ppermute | solution.py:44
  129.9 4.5 %all-to-all-start.3 = ((bf16[4,48,3584]{2,1,0:T(8,128)(2,1)}), bf16[4,48,3584]{2,1,0:T(8,128)(2,1)}, u32[]{:S(2)}, u32[]{:S(2)}) async-start(bf16[4,48,3584]{2,1,0:T(8,128)(2,1)} %bitcast.157), calls=%async_computation.3 | async-start | bytes 2752512 | tf_op jit(solution)/shard_map/all_to_all | solution.py:59
  134.6 3.8 %fusion.44 = f32[192,512]{1,0:T(8,128)} fusion(bf16[192,3584]{1,0:T(8,128)(2,1)S(1)} %bitcast.143, bf16[1,3584,512]{2,1,0:T(8,128)(2,1)} %param.12), kind=kOutput, calls=%fused_computation.66 | convolution fusion | flops 704643072 | bytes 5439488 | tf_op jit(solution)/shard_map/dot_general | solution.py:14
  142.8 7.3 %all-to-all-done.3 = bf16[4,48,3584]{2,1,0:T(8,128)(2,1)} async-done(((bf16[4,48,3584]{2,1,0:T(8,128)(2,1)}), bf16[4,48,3584]{2,1,0:T(8,128)(2,1)}, u32[]{:S(2)}, u32[]{:S(2)}) %all-to-all-start.3) | async-done | bytes 1376288 | tf_op jit(solution)/shard_map/all_to_all | solution.py:59
  150.0 3.5 fusion.58
  153.6 3.4 multiply_convert_fusion.2
  157.0 3.7 multiply_convert_fusion
  178.4 4.6 %all-to-all-start.4 = ((bf16[4,48,3584]{2,1,0:T(8,128)(2,1)}), bf16[4,48,3584]{2,1,0:T(8,128)(2,1)}, u32[]{:S(2)}, u32[]{:S(2)}) async-start(bf16[4,48,3584]{2,1,0:T(8,128)(2,1)} %bitcast.160), calls=%async_computation.4 | async-start | bytes 2752512 | tf_op jit(solution)/shard_map/all_to_all | solution.py:59
  183.0 3.6 fusion.11
  189.8 4.6 %convolution_convert_fusion.3 = bf16[256,3584]{1,0:T(8,128)(2,1)} fusion(bf16[192,3584]{1,0:T(8,128)(2,1)} %collective-permute-done.10, bf16[192,3584]{1,0:T(8,128)(2,1)} %bitcast.10, bf16[192,3584]{1,0:T(8,128)(2,1)S(1)} %copy-done.49, bf16[192,3584]{1,0:T(8,128)(2,1)} %bitcast.14, bf16[768,512]{1,0:T(8,128)(2,1)S(1)} %pad_maximum_fusion.5, s32[]{:T(128)S(6)} %select_n.2), kind=kOutput, calls=%fused_computation.17 | convolution fusion | flops 1432223744 | bytes 7733252 | tf_op jit(solution)/shard_map/dot_general | solution.py:14
  200.6 4.3 %all-to-all-start.5 = ((bf16[4,48,3584]{2,1,0:T(8,128)(2,1)}), bf16[4,48,3584]{2,1,0:T(8,128)(2,1)}, u32[]{:S(2)}, u32[]{:S(2)}) async-start(bf16[4,48,3584]{2,1,0:T(8,128)(2,1)} %bitcast.149), calls=%async_computation.5 | async-start | bytes 2752512 | tf_op jit(solution)/shard_map/all_to_all | solution.py:59
  211.2 4.4 %convolution_convert_fusion.4 = bf16[3584,256]{1,0:T(8,128)(2,1)} fusion(bf16[768,512]{1,0:T(8,128)(2,1)S(1)} %pad_maximum_fusion.4, s32[]{:T(128)S(6)} %select_n.2, bf16[192,3584]{1,0:T(8,128)(2,1)} %collective-permute-done, bf16[192,3584]{1,0:T(8,128)(2,1)S(1)} %bitcast.145, bf16[192,3584]{1,0:T(8,128)(2,1)} %collective-permute-done.6, ...), kind=kOutput, calls=%fused_computation.18 | convolution fusion | flops 1432223744 | bytes 7733252 | tf_op jit(solution)/shard_map/dot_general | solution.py:14
  215.7 21.3 %collective-permute-done.13 = bf16[256,3584]{1,0:T(8,128)(2,1)} collective-permute-done((bf16[256,3584]{1,0:T(8,128)(2,1)}, bf16[256,3584]{1,0:T(8,128)(2,1)}, u32[]{:S(2)}, u32[]{:S(2)}) %collective-permute-start.13) | collective-permute-done | bytes 1835040 | tf_op jit(solution)/shard_map/ppermute | solution.py:153
  241.9 4.7 %all-to-all-start.6 = ((bf16[4,48,3584]{2,1,0:T(8,128)(2,1)}), bf16[4,48,3584]{2,1,0:T(8,128)(2,1)}, u32[]{:S(2)}, u32[]{:S(2)}) async-start(bf16[4,48,3584]{2,1,0:T(8,128)(2,1)} %bitcast.159), calls=%async_computation.6 | async-start | bytes 2752512 | tf_op jit(solution)/shard_map/all_to_all | solution.py:59
  246.7 5.0 %add_convert_fusion = bf16[192,3584]{1,0:T(8,128)(2,1)} fusion(bf16[192,3584]{1,0:T(8,128)(2,1)} %collective-permute-done.11, f32[192,3584]{1,0:T(8,128)S(1)} %fusion.48, bf16[192,512]{1,0:T(8,128)(2,1)S(1)} %copy-done.34, bf16[1,3584,512]{2,1,0:T(8,128)(2,1)} %param.12), kind=kOutput, calls=%fused_computation.84 | convolution fusion | flops 708771840 | bytes 9371648 | tf_op jit(solution)/shard_map/dot_general | solution.py:14
  251.8 4.4 %convolution_convert_fusion.1 = bf16[3584,256]{1,0:T(8,128)(2,1)} fusion(bf16[768,512]{1,0:T(8,128)(2,1)S(1)} %pad_maximum_fusion.6, s32[]{:T(128)S(6)} %select_n.2, bf16[192,3584]{1,0:T(8,128)(2,1)} %collective-permute-done, bf16[192,3584]{1,0:T(8,128)(2,1)S(1)} %bitcast.146, bf16[192,3584]{1,0:T(8,128)(2,1)} %collective-permute-done.6, ...), kind=kOutput, calls=%fused_computation.12 | convolution fusion | flops 1432223744 | bytes 7733252 | tf_op jit(solution)/shard_map/dot_general | solution.py:14
  256.3 22.5 %collective-permute-done.14 = bf16[3584,256]{1,0:T(8,128)(2,1)} collective-permute-done((bf16[3584,256]{1,0:T(8,128)(2,1)}, bf16[3584,256]{1,0:T(8,128)(2,1)}, u32[]{:S(2)}, u32[]{:S(2)}) %collective-permute-start.14) | collective-permute-done | bytes 1835040 | tf_op jit(solution)/shard_map/ppermute | solution.py:153
  280.2 4.6 %fusion.21 = bf16[1,256,3584]{2,1,0:T(8,128)(2,1)} fusion(bf16[256,3584]{1,0:T(8,128)(2,1)} %collective-permute-done.13, bf16[192,3584]{1,0:T(8,128)(2,1)} %collective-permute-done.10, bf16[192,3584]{1,0:T(8,128)(2,1)} %bitcast.10, bf16[192,3584]{1,0:T(8,128)(2,1)S(1)} %copy-done.50, bf16[192,3584]{1,0:T(8,128)(2,1)} %bitcast.14, ...), kind=kOutput, calls=%fused_computation.41 | convolution fusion | flops 1435893760 | bytes 9568260 | tf_op jit(solution)/shard_map/dot_general | solution.py:14
  288.2 3.4 collective-permute-start.9
  291.6 4.3 %all-to-all-start.7 = ((bf16[4,48,3584]{2,1,0:T(8,128)(2,1)}), bf16[4,48,3584]{2,1,0:T(8,128)(2,1)}, u32[]{:S(2)}, u32[]{:S(2)}) async-start(bf16[4,48,3584]{2,1,0:T(8,128)(2,1)} %bitcast.22), calls=%async_computation.7 | async-start | bytes 2752512 | tf_op jit(solution)/shard_map/all_to_all | solution.py:59
  296.0 4.5 %fusion.19 = bf16[1,3584,256]{2,1,0:T(8,128)(2,1)} fusion(bf16[3584,256]{1,0:T(8,128)(2,1)} %collective-permute-done.14, bf16[768,512]{1,0:T(8,128)(2,1)S(1)} %copy-done.31, s32[]{:T(128)S(6)} %mul.206, bf16[192,3584]{1,0:T(8,128)(2,1)} %collective-permute-done, bf16[192,3584]{1,0:T(8,128)(2,1)S(1)} %bitcast.147, ...), kind=kOutput, calls=%fused_computation.39 | convolution fusion | flops 1435893760 | bytes 9568260 | tf_op jit(solution)/shard_map/dot_general | solution.py:14
  302.3 17.3 %collective-permute-done.15 = bf16[3584,256]{1,0:T(8,128)(2,1)} collective-permute-done((bf16[3584,256]{1,0:T(8,128)(2,1)}, bf16[3584,256]{1,0:T(8,128)(2,1)}, u32[]{:S(2)}, u32[]{:S(2)}) %collective-permute-start.15) | collective-permute-done | bytes 1835040 | tf_op jit(solution)/shard_map/ppermute | solution.py:153
  319.6 4.4 %fusion.20 = bf16[1,3584,256]{2,1,0:T(8,128)(2,1)} fusion(bf16[3584,256]{1,0:T(8,128)(2,1)} %collective-permute-done.15, bf16[768,512]{1,0:T(8,128)(2,1)S(1)} %copy-done.33, s32[]{:T(128)S(6)} %mul.206, bf16[192,3584]{1,0:T(8,128)(2,1)} %collective-permute-done, bf16[192,3584]{1,0:T(8,128)(2,1)S(1)} %bitcast.148, ...), kind=kOutput, calls=%fused_computation.40 | convolution fusion | flops 1435893760 | bytes 9568260 | tf_op jit(solution)/shard_map/dot_general | solution.py:14
  324.0 27.8 %collective-permute-done.9 = bf16[128,3584]{1,0:T(8,128)(2,1)} collective-permute-done((bf16[128,3584]{1,0:T(8,128)(2,1)}, bf16[128,3584]{1,0:T(8,128)(2,1)}, u32[]{:S(2)}, u32[]{:S(2)}) %collective-permute-start.9) | collective-permute-done | bytes 917536 | tf_op jit(solution)/shard_map/ppermute | solution.py:44
  351.8 3.5 fusion.62
  355.3 14.4 %collective-permute-done.12 = bf16[128,3584]{1,0:T(8,128)(2,1)} collective-permute-done((bf16[128,3584]{1,0:T(8,128)(2,1)S(1)}, bf16[128,3584]{1,0:T(8,128)(2,1)}, u32[]{:S(2)}, u32[]{:S(2)}) %collective-permute-start.12) | collective-permute-done | bytes 917536 | tf_op jit(solution)/shard_map/ppermute | solution.py:44
  (181 shorter events, 73.5 us)
Async XLA Ops:
  2.0 5.6 %collective-permute-start.2 = (f32[128,4]{0,1:T(4,128)S(1)}, f32[128,4]{0,1:T(4,128)S(1)}, u32[]{:S(2)}, u32[]{:S(2)}) collective-permute-start(f32[128,4]{0,1:T(4,128)S(1)} %pad_maximum_fusion.7), channel_id=1, source_target_pairs={{0,8},{1,9},{2,10},{3,11},{4,12},{5,13},{6,14},{7,15},{8,0},{9,1},... | collective-permute-start | bytes 6152 | tf_op jit(solution)/shard_map/ppermute | solution.py:44
  13.5 20.2 %all-to-all-start = ((bf16[4,48,3584]{2,1,0:T(8,128)(2,1)}), bf16[4,48,3584]{2,1,0:T(8,128)(2,1)S(1)}, u32[]{:S(2)}, u32[]{:S(2)}) async-start(bf16[4,48,3584]{2,1,0:T(8,128)(2,1)} %bitcast.3), calls=%async_computation | async-start | bytes 2752512 | tf_op jit(solution)/shard_map/all_to_all | solution.py:59
  33.7 105.2 %copy-start.10 = (bf16[4,48,3584]{2,1,0:T(8,128)(2,1)}, bf16[4,48,3584]{2,1,0:T(8,128)(2,1)S(1)}, u32[]{:S(2)}) copy-start(bf16[4,48,3584]{2,1,0:T(8,128)(2,1)S(1)} %all-to-all-done) | copy-start | bytes 4128772
  33.7 46.3 %all-to-all-start.1 = ((bf16[4,48,3584]{2,1,0:T(8,128)(2,1)}), bf16[4,48,3584]{2,1,0:T(8,128)(2,1)}, u32[]{:S(2)}, u32[]{:S(2)}) async-start(bf16[4,48,3584]{2,1,0:T(8,128)(2,1)} %bitcast.9), calls=%async_computation.1 | async-start | bytes 2752512 | tf_op jit(solution)/shard_map/all_to_all | solution.py:59
  38.0 41.9 %collective-permute-start.4 = (bf16[128,3584]{1,0:T(8,128)(2,1)S(1)}, bf16[128,3584]{1,0:T(8,128)(2,1)S(1)}, u32[]{:S(2)}, u32[]{:S(2)}) collective-permute-start(bf16[128,3584]{1,0:T(8,128)(2,1)S(1)} %bitcast.161), channel_id=1, source_target_pairs={{0,8},{1,9},{2,10},{3,11},{4,12},{5,13},{6,14},{7,15},{8,0},{9,1},... | collective-permute-start | bytes 2752520 | tf_op jit(solution)/shard_map/ppermute | solution.py:44
  41.3 88.7 %copy-start.42 = (bf16[128,192]{0,1:T(8,128)(2,1)}, bf16[128,192]{0,1:T(8,128)(2,1)S(1)}, u32[]{:S(2)}) copy-start(bf16[128,192]{0,1:T(8,128)(2,1)S(1)} %get-tuple-element.27) | copy-start | bytes 147460
  81.5 45.2 %all-to-all-start.2 = ((bf16[4,48,3584]{2,1,0:T(8,128)(2,1)}), bf16[4,48,3584]{2,1,0:T(8,128)(2,1)S(1)}, u32[]{:S(2)}, u32[]{:S(2)}) async-start(bf16[4,48,3584]{2,1,0:T(8,128)(2,1)} %bitcast.158), calls=%async_computation.2 | async-start | bytes 2752512 | tf_op jit(solution)/shard_map/all_to_all | solution.py:59
  85.1 41.6 %collective-permute-start.3 = (bf16[128,3584]{1,0:T(8,128)(2,1)}, bf16[128,3584]{1,0:T(8,128)(2,1)}, u32[]{:S(2)}, u32[]{:S(2)}) collective-permute-start(bf16[128,3584]{1,0:T(8,128)(2,1)} %bitcast.162), channel_id=1, source_target_pairs={{0,8},{1,9},{2,10},{3,11},{4,12},{5,13},{6,14},{7,15},{8,0},{9,1},... | collective-permute-start | bytes 2752520 | tf_op jit(solution)/shard_map/ppermute | solution.py:44
  126.7 46.6 %copy-start.14 = (bf16[4,48,3584]{2,1,0:T(8,128)(2,1)}, bf16[4,48,3584]{2,1,0:T(8,128)(2,1)S(1)}, u32[]{:S(2)}) copy-start(bf16[4,48,3584]{2,1,0:T(8,128)(2,1)S(1)} %all-to-all-done.2) | copy-start | bytes 4128772
  129.9 20.1 %all-to-all-start.3 = ((bf16[4,48,3584]{2,1,0:T(8,128)(2,1)}), bf16[4,48,3584]{2,1,0:T(8,128)(2,1)}, u32[]{:S(2)}, u32[]{:S(2)}) async-start(bf16[4,48,3584]{2,1,0:T(8,128)(2,1)} %bitcast.157), calls=%async_computation.3 | async-start | bytes 2752512 | tf_op jit(solution)/shard_map/all_to_all | solution.py:59
  134.5 6.1 %collective-permute-start = (bf16[192,3584]{1,0:T(8,128)(2,1)S(1)}, bf16[192,3584]{1,0:T(8,128)(2,1)}, u32[]{:S(2)}, u32[]{:S(2)}) collective-permute-start(bf16[192,3584]{1,0:T(8,128)(2,1)S(1)} %bitcast.142), channel_id=1, source_target_pairs={{0,1},{1,0},{2,3},{3,2},{4,5},{5,4},{6,7},{7,6},{8,9},{9,8},{10,11... | collective-permute-start | bytes 4128776 | tf_op jit(solution)/shard_map/ppermute | solution.py:44
  138.4 18.6 %collective-permute-start.10 = (bf16[192,3584]{1,0:T(8,128)(2,1)}, bf16[192,3584]{1,0:T(8,128)(2,1)}, u32[]{:S(2)}, u32[]{:S(2)}) collective-permute-start(bf16[192,3584]{1,0:T(8,128)(2,1)} %bitcast.10), channel_id=1, source_target_pairs={{0,1},{1,0},{2,3},{3,2},{4,5},{5,4},{6,7},{7,6},{8,9},{9,8},{10,11... | collective-permute-start | bytes 4128776 | tf_op jit(solution)/shard_map/ppermute | solution.py:44
  140.5 20.2 %collective-permute-start.6 = (bf16[192,3584]{1,0:T(8,128)(2,1)S(1)}, bf16[192,3584]{1,0:T(8,128)(2,1)}, u32[]{:S(2)}, u32[]{:S(2)}) collective-permute-start(bf16[192,3584]{1,0:T(8,128)(2,1)S(1)} %bitcast.150), channel_id=1, source_target_pairs={{0,1},{1,0},{2,3},{3,2},{4,5},{5,4},{6,7},{7,6},{8,9},{9,8},{10,11... | collective-permute-start | bytes 4128776 | tf_op jit(solution)/shard_map/ppermute | solution.py:44
  150.0 12.9 %collective-permute-start.5 = (bf16[192,3584]{1,0:T(8,128)(2,1)}, bf16[192,3584]{1,0:T(8,128)(2,1)S(1)}, u32[]{:S(2)}, u32[]{:S(2)}) collective-permute-start(bf16[192,3584]{1,0:T(8,128)(2,1)} %bitcast.14), channel_id=1, source_target_pairs={{0,1},{1,0},{2,3},{3,2},{4,5},{5,4},{6,7},{7,6},{8,9},{9,8},{10,11... | collective-permute-start | bytes 4128776 | tf_op jit(solution)/shard_map/ppermute | solution.py:44
  169.4 7.0 %collective-permute-start.8 = (bf16[192,3584]{1,0:T(8,128)(2,1)S(1)}, bf16[192,3584]{1,0:T(8,128)(2,1)S(1)}, u32[]{:S(2)}, u32[]{:S(2)}) collective-permute-start(bf16[192,3584]{1,0:T(8,128)(2,1)S(1)} %convolution_convert_fusion.6), channel_id=1, source_target_pairs={{0,1},{1,0},{2,3},{3,2},{4,5},{5,4},{6,7},{7,6},{8,9},{9,8},{10,11... | collective-permute-start | bytes 4128776 | tf_op jit(solution)/shard_map/ppermute | solution.py:44
  178.4 22.2 %all-to-all-start.4 = ((bf16[4,48,3584]{2,1,0:T(8,128)(2,1)}), bf16[4,48,3584]{2,1,0:T(8,128)(2,1)}, u32[]{:S(2)}, u32[]{:S(2)}) async-start(bf16[4,48,3584]{2,1,0:T(8,128)(2,1)} %bitcast.160), calls=%async_computation.4 | async-start | bytes 2752512 | tf_op jit(solution)/shard_map/all_to_all | solution.py:59
  186.6 9.3 %collective-permute-start.7 = (bf16[192,3584]{1,0:T(8,128)(2,1)S(1)}, bf16[192,3584]{1,0:T(8,128)(2,1)S(1)}, u32[]{:S(2)}, u32[]{:S(2)}) collective-permute-start(bf16[192,3584]{1,0:T(8,128)(2,1)S(1)} %fusion.11), channel_id=1, source_target_pairs={{0,1},{1,0},{2,3},{3,2},{4,5},{5,4},{6,7},{7,6},{8,9},{9,8},{10,11... | collective-permute-start | bytes 4128776 | tf_op jit(solution)/shard_map/ppermute | solution.py:44
  194.4 42.6 %collective-permute-start.13 = (bf16[256,3584]{1,0:T(8,128)(2,1)}, bf16[256,3584]{1,0:T(8,128)(2,1)}, u32[]{:S(2)}, u32[]{:S(2)}) collective-permute-start(bf16[256,3584]{1,0:T(8,128)(2,1)} %convolution_convert_fusion.3), channel_id=1, source_target_pairs={{0,16},{16,0},{1,17},{17,1},{2,18},{18,2},{3,19},{19,3},{4,20},{20... | collective-permute-start | bytes 5505032 | tf_op jit(solution)/shard_map/ppermute | solution.py:153
  200.6 41.3 %all-to-all-start.5 = ((bf16[4,48,3584]{2,1,0:T(8,128)(2,1)}), bf16[4,48,3584]{2,1,0:T(8,128)(2,1)}, u32[]{:S(2)}, u32[]{:S(2)}) async-start(bf16[4,48,3584]{2,1,0:T(8,128)(2,1)} %bitcast.149), calls=%async_computation.5 | async-start | bytes 2752512 | tf_op jit(solution)/shard_map/all_to_all | solution.py:59
  208.0 31.8 %collective-permute-start.1 = (bf16[192,3584]{1,0:T(8,128)(2,1)S(1)}, bf16[192,3584]{1,0:T(8,128)(2,1)S(1)}, u32[]{:S(2)}, u32[]{:S(2)}) collective-permute-start(bf16[192,3584]{1,0:T(8,128)(2,1)S(1)} %convolution_convert_fusion.9), channel_id=1, source_target_pairs={{0,1},{1,0},{2,3},{3,2},{4,5},{5,4},{6,7},{7,6},{8,9},{9,8},{10,11... | collective-permute-start | bytes 4128776 | tf_op jit(solution)/shard_map/ppermute | solution.py:44
  210.6 36.0 %collective-permute-start.11 = (bf16[192,3584]{1,0:T(8,128)(2,1)}, bf16[192,3584]{1,0:T(8,128)(2,1)}, u32[]{:S(2)}, u32[]{:S(2)}) collective-permute-start(bf16[192,3584]{1,0:T(8,128)(2,1)} %fusion.14), channel_id=1, source_target_pairs={{0,1},{1,0},{2,3},{3,2},{4,5},{5,4},{6,7},{7,6},{8,9},{9,8},{10,11... | collective-permute-start | bytes 4128776 | tf_op jit(solution)/shard_map/ppermute | solution.py:44
  237.0 41.8 %collective-permute-start.14 = (bf16[3584,256]{1,0:T(8,128)(2,1)}, bf16[3584,256]{1,0:T(8,128)(2,1)}, u32[]{:S(2)}, u32[]{:S(2)}) collective-permute-start(bf16[3584,256]{1,0:T(8,128)(2,1)} %convolution_convert_fusion.4), channel_id=1, source_target_pairs={{0,16},{16,0},{1,17},{17,1},{2,18},{18,2},{3,19},{19,3},{4,20},{20... | collective-permute-start | bytes 5505032 | tf_op jit(solution)/shard_map/ppermute | solution.py:153
  241.9 49.7 %all-to-all-start.6 = ((bf16[4,48,3584]{2,1,0:T(8,128)(2,1)}), bf16[4,48,3584]{2,1,0:T(8,128)(2,1)}, u32[]{:S(2)}, u32[]{:S(2)}) async-start(bf16[4,48,3584]{2,1,0:T(8,128)(2,1)} %bitcast.159), calls=%async_computation.6 | async-start | bytes 2752512 | tf_op jit(solution)/shard_map/all_to_all | solution.py:59
  251.8 28.4 %copy-start.29 = (bf16[768,512]{1,0:T(8,128)(2,1)S(1)}, bf16[768,512]{1,0:T(8,128)(2,1)}, u32[]{:S(2)}) copy-start(bf16[768,512]{1,0:T(8,128)(2,1)} %copy-done.28) | copy-start | bytes 2359300
  251.8 28.4 %copy-start.50 = (bf16[192,3584]{1,0:T(8,128)(2,1)S(1)}, bf16[192,3584]{1,0:T(8,128)(2,1)}, u32[]{:S(2)}) copy-start(bf16[192,3584]{1,0:T(8,128)(2,1)} %copy-done.48) | copy-start | bytes 4128772
  256.3 28.6 %copy-start.45 = (f32[128,192]{0,1:T(8,128)S(1)}, f32[128,192]{0,1:T(8,128)}, u32[]{:S(2)}) copy-start(f32[128,192]{0,1:T(8,128)} %get-tuple-element.23) | copy-start | bytes 294916
  278.8 40.8 %collective-permute-start.15 = (bf16[3584,256]{1,0:T(8,128)(2,1)}, bf16[3584,256]{1,0:T(8,128)(2,1)}, u32[]{:S(2)}, u32[]{:S(2)}) collective-permute-start(bf16[3584,256]{1,0:T(8,128)(2,1)} %convolution_convert_fusion.1), channel_id=1, source_target_pairs={{0,16},{16,0},{1,17},{17,1},{2,18},{18,2},{3,19},{19,3},{4,20},{20... | collective-permute-start | bytes 5505032 | tf_op jit(solution)/shard_map/ppermute | solution.py:153
  288.2 63.6 %collective-permute-start.9 = (bf16[128,3584]{1,0:T(8,128)(2,1)}, bf16[128,3584]{1,0:T(8,128)(2,1)}, u32[]{:S(2)}, u32[]{:S(2)}) collective-permute-start(bf16[128,3584]{1,0:T(8,128)(2,1)} %convolution_convert_fusion.13), channel_id=1, source_target_pairs={{0,8},{1,9},{2,10},{3,11},{4,12},{5,13},{6,14},{7,15},{8,0},{9,1},... | collective-permute-start | bytes 2752520 | tf_op jit(solution)/shard_map/ppermute | solution.py:44
  291.6 78.1 %all-to-all-start.7 = ((bf16[4,48,3584]{2,1,0:T(8,128)(2,1)}), bf16[4,48,3584]{2,1,0:T(8,128)(2,1)}, u32[]{:S(2)}, u32[]{:S(2)}) async-start(bf16[4,48,3584]{2,1,0:T(8,128)(2,1)} %bitcast.22), calls=%async_computation.7 | async-start | bytes 2752512 | tf_op jit(solution)/shard_map/all_to_all | solution.py:59
  302.2 49.6 %copy-start.44 = (f32[128,192]{0,1:T(8,128)S(1)}, f32[128,192]{0,1:T(8,128)}, u32[]{:S(2)}) copy-start(f32[128,192]{0,1:T(8,128)} %get-tuple-element.26) | copy-start | bytes 294916
  302.2 67.5 %collective-permute-start.12 = (bf16[128,3584]{1,0:T(8,128)(2,1)S(1)}, bf16[128,3584]{1,0:T(8,128)(2,1)}, u32[]{:S(2)}, u32[]{:S(2)}) collective-permute-start(bf16[128,3584]{1,0:T(8,128)(2,1)S(1)} %convolution_convert_fusion.12), channel_id=1, source_target_pairs={{0,8},{1,9},{2,10},{3,11},{4,12},{5,13},{6,14},{7,15},{8,0},{9,1},... | collective-permute-start | bytes 2752520 | tf_op jit(solution)/shard_map/ppermute | solution.py:44
  324.0 45.7 %copy-start.41 = (bf16[128,192]{0,1:T(8,128)(2,1)S(1)}, bf16[128,192]{0,1:T(8,128)(2,1)}, u32[]{:S(2)}) copy-start(bf16[128,192]{0,1:T(8,128)(2,1)} %copy-done.40) | copy-start | bytes 147460
  (43 other events, 289.7 us)

commit v5 on v4

v5 whole, which is shorter than its diff:
```python
import jax
import jax.numpy as jnp
from jax import lax
from jax.experimental import pallas as pl
from jax.experimental.pallas import tpu as pltpu
from jax.sharding import PartitionSpec as P

TOPK = 2
MB = 2
TOK_MB = 64
F32 = jnp.float32
BF16 = jnp.bfloat16
NN = ((1,), (0,))
NT = ((1,), (1,))
TN = ((0,), (0,))
VMEM_BYTES = 56 * 1024 * 1024


def dot(a, b, dims):
    return lax.dot_general(a, b, (dims, ((), ())), preferred_element_type=F32)


def tile_of(width):
    return 512 if width % 512 == 0 else width


def kernel_call(body, grid, in_specs, out_specs, out_shape, scratch=(), scalars=0):
    return pl.pallas_call(
        body,
        grid_spec=pltpu.PrefetchScalarGridSpec(
            num_scalar_prefetch=scalars,
            grid=grid,
            in_specs=in_specs,
            out_specs=out_specs,
            scratch_shapes=scratch,
        ),
        out_shape=out_shape,
        compiler_params=pltpu.CompilerParams(
            vmem_limit_bytes=VMEM_BYTES, dimension_semantics=("arbitrary",)
        ),
        cost_estimate=pl.CostEstimate(flops=1, bytes_accessed=1, transcendentals=0),
    )


def split3(w):
    high = w.astype(BF16)
    rest = w - high.astype(F32)
    middle = rest.astype(BF16)
    return high, middle, (rest - middle.astype(F32)).astype(BF16)


def place(placing, gain, parts):
    slots, tokens = placing.shape
    width = parts[0].shape[1]
    tile = tile_of(width)
    weighted = gain is not None

    def body(placing_ref, *refs):
        gain_ref = refs[0] if weighted else None
        part_refs, out_ref = refs[weighted:-1], refs[-1]
        rows = [ref[...] for ref in part_refs]
        rows = rows[0] if len(rows) == 1 else jnp.concatenate(rows, axis=0)
        total = dot(placing_ref[...], rows, NN)
        if weighted:
            total = total * gain_ref[...]
        out_ref[...] = total.astype(BF16)

    fixed = [placing] + ([gain] if weighted else [])
    return kernel_call(
        body,
        (width // tile,),
        [pl.BlockSpec(a.shape, lambda n: (0, 0)) for a in fixed]
        + [pl.BlockSpec((a.shape[0], tile), lambda n: (0, n)) for a in parts],
        pl.BlockSpec((slots, tile), lambda n: (0, n)),
        jax.ShapeDtypeStruct((slots, width), BF16),
    )(*fixed, *parts)


def combine(matrix, rows, parts=None):
    tokens, slots = matrix.shape
    width = rows.shape[1]
    tile = tile_of(width)

    def body(matrix_ref, rows_ref, *refs):
        rows = rows_ref[...]
        if matrix_ref.dtype == BF16:
            total = dot(matrix_ref[...], rows, NN)
        else:
            total = sum(dot(term, rows, NN) for term in split3(matrix_ref[...]))
        if parts is None:
            for b, ref in enumerate(refs):
                ref[...] = total[b * TOK_MB : (b + 1) * TOK_MB].astype(BF16)
        else:
            got = jnp.concatenate([ref[...] for ref in refs[:-1]], axis=0)
            refs[-1][...] = (total + got.astype(F32)).astype(BF16)

    part_spec = pl.BlockSpec((TOK_MB, tile), lambda n: (0, n))
    if parts is None:
        out_specs, out_shape = [part_spec] * MB, [jax.ShapeDtypeStruct((TOK_MB, width), BF16)] * MB
    else:
        out_specs = pl.BlockSpec((tokens, tile), lambda n: (0, n))
        out_shape = jax.ShapeDtypeStruct((tokens, width), BF16)
    return kernel_call(
        body,
        (width // tile,),
        [
            pl.BlockSpec((tokens, slots), lambda n: (0, 0)),
            pl.BlockSpec((slots, tile), lambda n: (0, n)),
        ]
        + [part_spec] * (0 if parts is None else MB),
        out_specs,
        out_shape,
    )(matrix, rows, *(parts or []))


def chunks(width):
    tile = tile_of(width)
    return [slice(n * tile, (n + 1) * tile) for n in range(width // tile)]


def forward(rows, gate_weight, up_weight, down_weight):
    count, width = rows[0].shape
    half_units = gate_weight.shape[1] // 2

    def body(a_ref, b_ref, gate_ref, up_ref, down_ref, pre_gate_ref, pre_up_ref, hidden_ref, out_a, out_b, acc_ref):
        step = pl.program_id(0)
        for r, (x_ref, out_ref) in enumerate(((a_ref, out_a), (b_ref, out_b))):
            here = slice(r * count, (r + 1) * count)
            pre_gate = dot(x_ref[...], gate_ref[...], NN)
            pre_up = dot(x_ref[...], up_ref[...], NN)
            pre_gate_ref[0, here] = pre_gate
            pre_up_ref[0, here] = pre_up
            hidden = (pre_gate * jax.nn.sigmoid(pre_gate) * pre_up).astype(BF16)
            hidden_ref[0, here] = hidden

            @pl.when(step == 0)
            def _():
                for cut in chunks(width):
                    acc_ref[here, cut] = dot(hidden, down_ref[:, cut], NN)

            @pl.when(step == 1)
            def _():
                for cut in chunks(width):
                    total = acc_ref[here, cut] + dot(hidden, down_ref[:, cut], NN)
                    out_ref[:, cut] = total.astype(BF16)

    whole = pl.BlockSpec((count, width), lambda n: (0, 0))
    columns = pl.BlockSpec((width, half_units), lambda n: (0, n))
    units = pl.BlockSpec((1, 2 * count, half_units), lambda n: (n, 0, 0))
    return kernel_call(
        body,
        (2,),
        [whole, whole, columns, columns, pl.BlockSpec((half_units, width), lambda n: (n, 0))],
        [units, units, units, whole, whole],
        [
            jax.ShapeDtypeStruct((2, 2 * count, half_units), F32),
            jax.ShapeDtypeStruct((2, 2 * count, half_units), F32),
            jax.ShapeDtypeStruct((2, 2 * count, half_units), BF16),
            jax.ShapeDtypeStruct((count, width), BF16),
            jax.ShapeDtypeStruct((count, width), BF16),
        ],
        [pltpu.VMEM((2 * count, width), F32)],
    )(*rows, gate_weight, up_weight, down_weight)


def backward(rows_grad, pre_gate, pre_up, gate_weight, up_weight, down_weight):
    count, width = rows_grad[0].shape
    half_units = gate_weight.shape[1] // 2

    def body(a_ref, b_ref, pre_gate_ref, pre_up_ref, gate_ref, up_ref, down_ref, units_ref, out_a, out_b, acc_ref):
        step = pl.program_id(0)
        for r, (g_ref, out_ref) in enumerate(((a_ref, out_a), (b_ref, out_b))):
            here = slice(r * count, (r + 1) * count)
            hidden_grad = dot(g_ref[...], down_ref[...], NT)
            pre_gate = pre_gate_ref[0, here]
            sigma = jax.nn.sigmoid(pre_gate)
            gate_grad = (
                hidden_grad * pre_up_ref[0, here] * sigma * (1.0 + pre_gate * (1.0 - sigma))
            ).astype(BF16)
            up_grad = (hidden_grad * (pre_gate * sigma)).astype(BF16)
            units_ref[0, here, :half_units] = gate_grad
            units_ref[0, here, half_units:] = up_grad

            @pl.when(step == 0)
            def _():
                for cut in chunks(width):
                    acc_ref[here, cut] = dot(gate_grad, gate_ref[cut], NT) + dot(
                        up_grad, up_ref[cut], NT
                    )

            @pl.when(step == 1)
            def _():
                for cut in chunks(width):
                    total = acc_ref[here, cut] + dot(gate_grad, gate_ref[cut], NT)
                    out_ref[:, cut] = (total + dot(up_grad, up_ref[cut], NT)).astype(BF16)

    whole = pl.BlockSpec((count, width), lambda n: (0, 0))
    columns = pl.BlockSpec((width, half_units), lambda n: (0, n))
    units = pl.BlockSpec((1, 2 * count, half_units), lambda n: (n, 0, 0))
    return kernel_call(
        body,
        (2,),
        [whole, whole, units, units, columns, columns, pl.BlockSpec((half_units, width), lambda n: (n, 0))],
        [pl.BlockSpec((1, 2 * count, 2 * half_units), lambda n: (n, 0, 0)), whole, whole],
        [
            jax.ShapeDtypeStruct((2, 2 * count, 2 * half_units), BF16),
            jax.ShapeDtypeStruct((count, width), BF16),
            jax.ShapeDtypeStruct((count, width), BF16),
        ],
        [pltpu.VMEM((2 * count, width), F32)],
    )(*rows_grad, pre_gate, pre_up, gate_weight, up_weight, down_weight)


def down_grad(which, hiddens, rows_grad, got=None):
    count, width = rows_grad[0].shape
    half_units = hiddens[0].shape[2]
    tile = tile_of(width)

    def body(which_ref, *refs):
        unit_refs, row_refs, rest = refs[:2], refs[2:6], refs[6:]
        total = None
        for n, row_ref in enumerate(row_refs):
            start = (n % 2) * count
            term = dot(unit_refs[n // 2][0, start : start + count], row_ref[...], TN)
            total = term if total is None else total + term
        if got is not None:
            total = total.astype(BF16).astype(F32) + rest[0][...].astype(F32)
        rest[-1][...] = total.astype(BF16)

    out_spec = pl.BlockSpec((half_units, tile), lambda n, w: (0, n))
    return kernel_call(
        body,
        (width // tile,),
        [pl.BlockSpec((1, 2 * count, half_units), lambda n, w: (w[0], 0, 0))] * 2
        + [pl.BlockSpec((count, tile), lambda n, w: (0, n))] * 4
        + [out_spec] * (got is not None),
        out_spec,
        jax.ShapeDtypeStruct((half_units, width), BF16),
        scalars=1,
    )(which, *hiddens, *rows_grad, *([] if got is None else [got]))


def gate_up_grad(which, units, rows, mirror_units, mirror_rows):
    count, width = rows[0].shape
    both = units[0].shape[2]
    half_units = both // 2
    tile = tile_of(width)

    def body(which_ref, *refs):
        unit_refs, mirror_refs, row_refs = refs[:2], refs[2:4], refs[4:12]
        gate_ref, up_ref = refs[12:]
        total = None
        for n, row_ref in enumerate(row_refs):
            start = (n % 2) * count
            here = slice(start, start + count)
            factor = unit_refs[n // 2][0, here] if n < 4 else mirror_refs[n // 2 - 2][here]
            term = dot(row_ref[...], factor, TN)
            total = term if total is None else total + term
        gate_ref[...] = total[:, :half_units].astype(BF16)
        up_ref[...] = total[:, half_units:].astype(BF16)

    out_spec = pl.BlockSpec((tile, half_units), lambda n, w: (n, 0))
    return kernel_call(
        body,
        (width // tile,),
        [pl.BlockSpec((1, 2 * count, both), lambda n, w: (w[0], 0, 0))] * 2
        + [pl.BlockSpec((2 * count, both), lambda n, w: (0, 0))] * 2
        + [pl.BlockSpec((count, tile), lambda n, w: (0, n))] * 8,
        [out_spec] * 2,
        [jax.ShapeDtypeStruct((width, half_units), BF16)] * 2,
        scalars=1,
    )(which, *units, *mirror_units, *rows, *mirror_rows)


def route(meta, half, expert_count, capacity):
    ids, gain = meta[:, :TOPK].astype(jnp.int32), meta[:, TOPK:]
    flat_ids = ids.reshape(MB, TOK_MB * TOPK)
    member = (flat_ids[:, :, None] == jnp.arange(expert_count, dtype=jnp.int32)).astype(jnp.int32)
    running = jnp.cumsum(member, axis=1) - 1
    rank = jnp.sum(member * running, axis=2)
    batch = jnp.arange(MB, dtype=jnp.int32)[:, None]
    near = expert_count // 2
    target = (((flat_ids - half * near) * MB + batch) * capacity + rank).reshape(ids.shape)
    slots = jnp.arange(near * MB * capacity, dtype=jnp.int32)
    matches = (target[:, :, None] == slots).astype(F32)
    turned = (target.T[:, None, :] == slots[:, None]).astype(F32)
    weighting = jnp.sum(matches * gain[:, :, None], axis=1)
    slot_gain = jnp.sum(turned * gain.T[:, None, :], axis=(0, 2))[:, None]
    return jnp.sum(turned, axis=0).astype(BF16), jnp.sum(matches, axis=1).astype(BF16), weighting, slot_gain


def on_device(acts, grad_out, expert_ids, route_weights, w_gate, w_up, w_down):
    weights = (w_gate[0], w_up[0], w_down[0])
    devices = lax.axis_size("expert")
    chips = devices // 2
    near = chips // 2
    capacity = 3 * TOPK * TOK_MB // (2 * chips)
    piece = MB * capacity
    width = acts.shape[2]
    half = (lax.axis_index("expert") >= devices // 2).astype(jnp.int32)
    rank_count = lax.axis_size("pipe")
    kept_half = (lax.axis_index("pipe") >= rank_count // 2).astype(jnp.int32)
    kept = kept_half.reshape(1)

    def hop(rows, distance):
        return lax.ppermute(rows, "expert", [(i, i ^ distance) for i in range(devices)])

    def far(rows):
        return hop(rows, devices // 2)

    def swap(rows):
        return hop(rows, 1)

    def mirror(rows):
        return lax.ppermute(rows, "pipe", [(p, rank_count - 1 - p) for p in range(rank_count)])

    groups = [
        [(part * near + member) * 2 + core for member in range(near)]
        for part in range(2)
        for core in range(2)
    ]

    def near_exchange(rows):
        return lax.all_to_all(
            rows.reshape(near, piece, width),
            "expert",
            split_axis=0,
            concat_axis=0,
            axis_index_groups=groups,
            tiled=True,
        ).reshape(near * piece, width)

    def tie(*arrays):
        return lax.optimization_barrier(arrays)

    def expert_sum(mine, other):
        return (mine.astype(F32) + swap(other).astype(F32)).astype(BF16)

    acts_parts = [acts[0, b * TOK_MB : (b + 1) * TOK_MB] for b in range(MB)]
    grad_parts = [grad_out[0, b * TOK_MB : (b + 1) * TOK_MB] for b in range(MB)]
    meta = jnp.concatenate([expert_ids[0].astype(F32), route_weights[0]], axis=1)
    far_meta = far(meta)
    own_placing, own_back, own_weighting, own_gain = route(meta, half, chips, capacity)
    far_placing, far_back, far_weighting, far_gain = route(far_meta, half, chips, capacity)

    own_in = place(own_placing, None, [acts[0]])
    far_acts_0 = far(acts_parts[0])
    own_in = near_exchange(own_in)
    own_grad = place(own_placing, own_gain, [grad_out[0]])
    own_in, far_acts_0, acts_1, own_grad = tie(own_in, far_acts_0, acts_parts[1], own_grad)
    far_acts_1 = far(acts_1)
    own_grad = near_exchange(own_grad)
    own_in_b = swap(own_in)
    mirror_own = mirror(own_in)
    far_in = place(far_placing, None, [far_acts_0, far_acts_1])
    far_in, own_grad, own_in_b, grads_0 = tie(far_in, own_grad, own_in_b, grad_parts[0])
    far_grads_0 = far(grads_0)
    far_in = near_exchange(far_in)
    own_pre_gate, own_pre_up, own_hidden, own_out, own_out_b = forward(
        (own_in, own_in_b), *weights
    )
    own_out = expert_sum(own_out, own_out_b)
    own_grad_b = swap(own_grad)
    far_in, far_grads_0, own_out, mirror_own, grads_1 = tie(
        far_in, far_grads_0, own_out, mirror_own, grad_parts[1]
    )
    far_grads_1 = far(grads_1)
    own_out = near_exchange(own_out)
    far_in_b = swap(far_in)
    mirror_far = mirror(far_in)
    mirror_own_b = swap(mirror_own)
    own_units, own_input, own_input_b = backward(
        (own_grad, own_grad_b), own_pre_gate, own_pre_up, *weights
    )
    far_grad = place(far_placing, far_gain, [far_grads_0, far_grads_1])
    far_grad, own_out = tie(far_grad, own_out)
    far_grad = near_exchange(far_grad)
    far_pre_gate, far_pre_up, far_hidden, far_out, far_out_b = forward(
        (far_in, far_in_b), *weights
    )
    far_out = expert_sum(far_out, far_out_b)
    own_input = expert_sum(own_input, own_input_b)
    far_grad, far_out, mirror_far, own_input = tie(far_grad, far_out, mirror_far, own_input)
    far_out = near_exchange(far_out)
    far_grad_b = swap(far_grad)
    mirror_far_b = swap(mirror_far)
    far_units, far_input, far_input_b = backward(
        (far_grad, far_grad_b), far_pre_gate, far_pre_up, *weights
    )
    far_input = expert_sum(far_input, far_input_b)
    rows_grad = (own_grad, own_grad_b, far_grad, far_grad_b)
    got_down = mirror(down_grad(1 - kept, (own_hidden, far_hidden), rows_grad))
    back_out = combine(far_weighting, far_out)
    far_input, back_out = tie(far_input, back_out)
    got_out_0 = far(back_out[0])
    far_input = near_exchange(far_input)
    far_input, got_out_0, back_out_1, own_input = tie(far_input, got_out_0, back_out[1], own_input)
    got_out_1 = far(back_out_1)
    own_input = near_exchange(own_input)
    back_input = combine(far_back, far_input)
    got_out_1, own_input, got_down, back_input, own_units, far_units = tie(
        got_out_1, own_input, got_down, back_input, own_units, far_units
    )
    got_input = [far(part) for part in back_input]
    mirror_units = [
        mirror(lax.dynamic_index_in_dim(units, 1 - kept_half, 0, keepdims=False))
        for units in (own_units, far_units)
    ]
    grad_down = down_grad(kept, (own_hidden, far_hidden), rows_grad, got_down)
    out_acts = combine(own_weighting, own_out, [got_out_0, got_out_1])
    grad_gate, grad_up = gate_up_grad(
        kept,
        (own_units, far_units),
        (own_in, own_in_b, far_in, far_in_b),
        mirror_units,
        (mirror_own, mirror_own_b, mirror_far, mirror_far_b),
    )
    grad_acts = combine(own_back, own_input, got_input)
    return out_acts[None], grad_acts[None], grad_gate[None], grad_up[None], grad_down[None]


def solution(mesh):
    tokens = P("pipe", "expert", None)
    columns = P("pipe", None, "expert")
    return jax.shard_map(
        on_device,
        mesh=mesh,
        in_specs=(tokens, tokens, tokens, tokens, columns, columns, tokens),
        out_specs=(tokens, tokens, columns, columns, tokens),
        check_vma=False,
    )
```

time: 374 us -> 385 us (1.029)
  Pallas kernels: 0 us -> 125 us
  matrix products: 105 us -> 0 us
  waiting for transfers between devices: 205 us -> 158 us
  local copies, waits for them, and re-layouts: 2.52 us -> 20.3 us
  starting transfers between devices: 53.5 us -> 64.3 us
  other arithmetic: 5.31 us -> 14 us
    pallas_call x0 -> x15, Pallas kernels: none -> 125 us  [the longest x2 28.7 us: backward(): kernel_call(body, (2,), [whole, whole, units, units, columns, columns, pl...]
    dot_general x38 -> x0, matrix products: 105 us -> none  [the longest x36 98 us: dot(): return lax.dot_general(a, b, (dims, ((), ())), preferred_element_type=F32)]
    ppermute x13 -> x19, waiting for transfers between devices: 120 us -> 70.1 us  [hop(): lax.ppermute(rows, 'expert', [(i, i ^ distance) for i in range(devices)])]
    ppermute x3 -> x5, waiting for transfers between devices: 61.1 us -> 82.2 us  [mirror(): lax.ppermute(rows, 'pipe', [(p, rank_count - 1 - p) for p in range(rank_c...]
    all_to_all x8, waiting for transfers between devices: 23.9 us -> 5.31 us  [near_exchange(): lax.all_to_all(rows.reshape(near, piece, width), 'expert', split_axis=0,...]
    convert_element_type x1 -> x4, other arithmetic: 0.01 us -> 10.3 us  [expert_sum(): return (mine.astype(F32) + swap(other).astype(F32)).astype(BF16)]
    squeeze x0 -> x4, local copies, waits for them, and re-layouts: none -> 6.69 us  [the longest x2 3.85 us: on_device(): lax.dynamic_index_in_dim(units, 1 - kept_half, 0, keepdims=False)]
    unnamed x102 -> x38, local copies, waits for them, and re-layouts: 1.52 us -> 8.11 us
  transfers between devices with their start and end apart: 24 -> 32, of which waited for: 11 -> 12; matrix products, arithmetic and copies ran while one was open for 24% -> 6% of each run, Pallas kernels for 0% -> 27%
where the time goes in v5:
time: 385 us; the launch traced here: 382 us
  waiting for transfers between devices  158 us (41%)
  Pallas kernels  125 us (32%)
  starting transfers between devices  64.3 us (17%)
  local copies, waits for them, and re-layouts  20.3 us (5%)
  other arithmetic  14 us (4%)
    ppermute x5, waiting for transfers between devices, mirror(): lax.ppermute(rows, 'pipe', [(p, rank_count - 1 - p) for p in range(rank_c...  82.2 us
    ppermute x19, waiting for transfers between devices, hop(): lax.ppermute(rows, 'expert', [(i, i ^ distance) for i in range(devices)])  70.1 us
    all_to_all x8, starting transfers between devices, near_exchange(): lax.all_to_all(rows.reshape(near, piece, width), 'expert', split_axis=0,...  37.2 us
    pallas_call x2, Pallas kernels, backward(): kernel_call(body, (2,), [whole, whole, units, units, columns, columns, pl...  28.7 us
    pallas_call x2, Pallas kernels, forward(): kernel_call(body, (2,), [whole, whole, columns, columns, pl.BlockSpec((ha...  23 us
    pallas_call x4, Pallas kernels, combine(): kernel_call(body, (width // tile,), [pl.BlockSpec((tokens, slots), lambda...  22.5 us
    pallas_call x4, Pallas kernels, place(): kernel_call(body, (width // tile,), [pl.BlockSpec(a.shape, lambda n: (0,...  21.6 us
    ppermute x19, starting transfers between devices, hop(): lax.ppermute(rows, 'expert', [(i, i ^ distance) for i in range(devices)])  20.8 us
  transfers between devices with their start and end apart: 32, of which 12 were waited for; matrix products, arithmetic and copies ran while one was open for 6% of the time, Pallas kernels for 27%

profile of v5, /device:TPU:0, one launch (start us, length us, event | category | flops | bytes accessed | tf_op | source)
XLA Modules:
  0.0 382.3 jit_solution(12763440106342908230)
XLA Ops:
  2.1 4.0 %collective-permute-start = (f32[128,4]{0,1:T(4,128)S(1)}, f32[128,4]{0,1:T(4,128)S(1)}, u32[]{:S(2)}, u32[]{:S(2)}) collective-permute-start(f32[128,4]{0,1:T(4,128)S(1)} %pad_maximum_fusion), channel_id=1, source_target_pairs={{0,8},{1,9},{2,10},{3,11},{4,12},{5,13},{6,14},{7,15},{8,0},{9,1},... | collective-permute-start | bytes 6152 | tf_op jit(solution)/shard_map/ppermute | solution.py:306
  9.3 5.4 %shard_map.110 = bf16[192,3584]{1,0:T(8,128)(2,1)} custom-call(bf16[192,128]{1,0:T(8,128)(2,1)} %get-tuple-element.120.placing_ref, bf16[128,3584]{1,0:T(8,128)(2,1)} %bitcast.79), custom_call_target="tpu_custom_call" | custom-call | flops 1 | bytes 1 | tf_op jit(solution)/shard_map/pallas_call | solution.py:69
  14.7 4.4 %all-to-all-start = ((bf16[4,48,3584]{2,1,0:T(8,128)(2,1)}), bf16[4,48,3584]{2,1,0:T(8,128)(2,1)}, u32[]{:S(2)}, u32[]{:S(2)}) async-start(bf16[4,48,3584]{2,1,0:T(8,128)(2,1)} %bitcast.78), calls=%async_computation | async-start | bytes 2752512 | tf_op jit(solution)/shard_map/all_to_all | solution.py:324
  23.7 5.5 %shard_map.111 = bf16[192,3584]{1,0:T(8,128)(2,1)} custom-call(bf16[192,128]{1,0:T(8,128)(2,1)} %get-tuple-element.120.placing_ref, f32[192,1]{1,0:T(8,128)} %copy.53.refs_0_, bf16[128,3584]{1,0:T(8,128)(2,1)} %bitcast.80), custom_call_target="tpu_custom_call" | custom-call | flops 1 | bytes 1 | tf_op jit(solution)/shard_map/pallas_call | solution.py:69
  29.1 14.3 %collective-permute-done.1.refs_0_ = bf16[64,3584]{1,0:T(8,128)(2,1)S(1)} collective-permute-done((bf16[64,3584]{1,0:T(8,128)(2,1)S(1)}, bf16[64,3584]{1,0:T(8,128)(2,1)S(1)}, u32[]{:S(2)}, u32[]{:S(2)}) %collective-permute-start.1) | collective-permute-done | bytes 458784 | tf_op jit(solution)/shard_map/ppermute | solution.py:306
  45.7 5.4 %all-to-all-start.1 = ((bf16[4,48,3584]{2,1,0:T(8,128)(2,1)}), bf16[4,48,3584]{2,1,0:T(8,128)(2,1)S(1)}, u32[]{:S(2)}, u32[]{:S(2)}) async-start(bf16[4,48,3584]{2,1,0:T(8,128)(2,1)} %bitcast.75), calls=%async_computation.1 | async-start | bytes 2752512 | tf_op jit(solution)/shard_map/all_to_all | solution.py:324
  53.9 20.0 %collective-permute-done.2.refs_1_ = bf16[64,3584]{1,0:T(8,128)(2,1)S(1)} collective-permute-done((bf16[64,3584]{1,0:T(8,128)(2,1)}, bf16[64,3584]{1,0:T(8,128)(2,1)S(1)}, u32[]{:S(2)}, u32[]{:S(2)}) %collective-permute-start.2) | collective-permute-done | bytes 458784 | tf_op jit(solution)/shard_map/ppermute | solution.py:306
  74.7 5.3 %shard_map.112 = bf16[192,3584]{1,0:T(8,128)(2,1)} custom-call(bf16[192,128]{1,0:T(8,128)(2,1)} %get-tuple-element.122.placing_ref, bf16[64,3584]{1,0:T(8,128)(2,1)} %copy-done.14, bf16[64,3584]{1,0:T(8,128)(2,1)} %copy-done.15), custom_call_target="tpu_custom_call" | custom-call | flops 1 | bytes 1 | tf_op jit(solution)/shard_map/pallas_call | solution.py:69
  81.0 11.5 %shard_map.113 = (f32[2,384,256]{2,1,0:T(8,128)}, f32[2,384,256]{2,1,0:T(8,128)}, bf16[2,384,256]{2,1,0:T(8,128)(2,1)}, bf16[192,3584]{1,0:T(8,128)(2,1)}, bf16[192,3584]{1,0:T(8,128)(2,1)}) custom-call(bf16[192,3584]{1,0:T(8,128)(2,1)} %bitcast.8.a_ref.refs_4_, bf16[192,3584]{1,0:T(8,128)(2,1)} %copy-done.6, bf16[3584,512]{1,0:T(8,128)(2,1)} %bitcast.52, ...), custom_call_target="tpu_custom_call" | custom-call | flops 1 | bytes 1 | tf_op jit(solution)/shard_map/pallas_call | solution.py:150
  92.6 5.2 %all-to-all-start.2 = ((bf16[4,48,3584]{2,1,0:T(8,128)(2,1)}), bf16[4,48,3584]{2,1,0:T(8,128)(2,1)}, u32[]{:S(2)}, u32[]{:S(2)}) async-start(bf16[4,48,3584]{2,1,0:T(8,128)(2,1)} %bitcast.17), calls=%async_computation.2 | async-start | bytes 2752512 | tf_op jit(solution)/shard_map/all_to_all | solution.py:324
  105.1 25.3 %collective-permute-done.6.refs_8_ = bf16[192,3584]{1,0:T(8,128)(2,1)} collective-permute-done((bf16[192,3584]{1,0:T(8,128)(2,1)}, bf16[192,3584]{1,0:T(8,128)(2,1)}, u32[]{:S(2)}, u32[]{:S(2)}) %collective-permute-start.6) | collective-permute-done | bytes 1376288 | tf_op jit(solution)/shard_map/ppermute | solution.py:315
  130.4 4.7 %all-to-all-start.3 = ((bf16[4,48,3584]{2,1,0:T(8,128)(2,1)}), bf16[4,48,3584]{2,1,0:T(8,128)(2,1)}, u32[]{:S(2)}, u32[]{:S(2)}) async-start(bf16[4,48,3584]{2,1,0:T(8,128)(2,1)} %bitcast.74), calls=%async_computation.3 | async-start | bytes 2752512 | tf_op jit(solution)/shard_map/all_to_all | solution.py:324
  136.1 14.3 %shard_map.116 = (bf16[2,384,512]{2,1,0:T(8,128)(2,1)}, bf16[192,3584]{1,0:T(8,128)(2,1)}, bf16[192,3584]{1,0:T(8,128)(2,1)}) custom-call(bf16[192,3584]{1,0:T(8,128)(2,1)} %bitcast.65, bf16[192,3584]{1,0:T(8,128)(2,1)} %copy-done.2, f32[2,384,256]{2,1,0:T(8,128)} %get-tuple-element.78.pre_gate_ref, f32[2,384,256]{2,1,0:T(8,128)} %get-tuple-element.79.pre_up_ref, ...), custom_call_target="tpu_custom_call" | custom-call | flops 1 | bytes 1 | tf_op jit(solution)/shard_map/pallas_call | solution.py:200
  154.8 11.5 %shard_map.115 = (f32[2,384,256]{2,1,0:T(8,128)}, f32[2,384,256]{2,1,0:T(8,128)}, bf16[2,384,256]{2,1,0:T(8,128)(2,1)}, bf16[192,3584]{1,0:T(8,128)(2,1)}, bf16[192,3584]{1,0:T(8,128)(2,1)}) custom-call(bf16[192,3584]{1,0:T(8,128)(2,1)} %bitcast.18.a_ref.refs_6_, bf16[192,3584]{1,0:T(8,128)(2,1)} %copy-done.7, bf16[3584,512]{1,0:T(8,128)(2,1)} %bitcast.54, ...), custom_call_target="tpu_custom_call" | custom-call | flops 1 | bytes 1 | tf_op jit(solution)/shard_map/pallas_call | solution.py:150
  167.2 7.1 %collective-permute-done.7.refs_2_ = bf16[64,3584]{1,0:T(8,128)(2,1)S(1)} collective-permute-done((bf16[64,3584]{1,0:T(8,128)(2,1)S(1)}, bf16[64,3584]{1,0:T(8,128)(2,1)S(1)}, u32[]{:S(2)}, u32[]{:S(2)}) %collective-permute-start.7) | collective-permute-done | bytes 458784 | tf_op jit(solution)/shard_map/ppermute | solution.py:306
  175.1 5.5 %shard_map.114 = bf16[192,3584]{1,0:T(8,128)(2,1)} custom-call(bf16[192,128]{1,0:T(8,128)(2,1)} %get-tuple-element.122.placing_ref, f32[192,1]{1,0:T(8,128)} %copy.54.refs_0_, bf16[64,3584]{1,0:T(8,128)(2,1)} %collective-permute-done.4.refs_1_, bf16[64,3584]{1,0:T(8,128)(2,1)} %copy-done.13), custom_call_target="tpu_custom_call" | custom-call | flops 1 | bytes 1 | tf_op jit(solution)/shard_map/pallas_call | solution.py:69
  180.6 3.7 all-to-all-start.4
  191.6 24.5 %collective-permute-done.10.refs_10_ = bf16[192,3584]{1,0:T(8,128)(2,1)} collective-permute-done((bf16[192,3584]{1,0:T(8,128)(2,1)}, bf16[192,3584]{1,0:T(8,128)(2,1)}, u32[]{:S(2)}, u32[]{:S(2)}) %collective-permute-start.10) | collective-permute-done | bytes 1376288 | tf_op jit(solution)/shard_map/ppermute | solution.py:315
  217.1 4.5 %all-to-all-start.5 = ((bf16[4,48,3584]{2,1,0:T(8,128)(2,1)}), bf16[4,48,3584]{2,1,0:T(8,128)(2,1)}, u32[]{:S(2)}, u32[]{:S(2)}) async-start(bf16[4,48,3584]{2,1,0:T(8,128)(2,1)} %bitcast.76), calls=%async_computation.5 | async-start | bytes 2752512 | tf_op jit(solution)/shard_map/all_to_all | solution.py:324
  222.8 14.3 %shard_map.117 = (bf16[2,384,512]{2,1,0:T(8,128)(2,1)}, bf16[192,3584]{1,0:T(8,128)(2,1)}, bf16[192,3584]{1,0:T(8,128)(2,1)}) custom-call(bf16[192,3584]{1,0:T(8,128)(2,1)} %bitcast.69, bf16[192,3584]{1,0:T(8,128)(2,1)} %copy-done.3, f32[2,384,256]{2,1,0:T(8,128)} %get-tuple-element.83.pre_gate_ref, f32[2,384,256]{2,1,0:T(8,128)} %get-tuple-element.84.pre_up_ref, ...), custom_call_target="tpu_custom_call" | custom-call | flops 1 | bytes 1 | tf_op jit(solution)/shard_map/pallas_call | solution.py:200
  238.9 5.7 %shard_map.118 = (bf16[64,3584]{1,0:T(8,128)(2,1)}, bf16[64,3584]{1,0:T(8,128)(2,1)}) custom-call(f32[128,192]{1,0:T(8,128)} %copy.55.matrix_ref, bf16[192,3584]{1,0:T(8,128)(2,1)} %bitcast.28.rows_ref), custom_call_target="tpu_custom_call" | custom-call | flops 1 | bytes 1 | tf_op jit(solution)/shard_map/pallas_call | solution.py:103
  246.0 3.7 all-to-all-start.6
  252.9 21.7 %collective-permute-done.15.refs_0_ = bf16[64,3584]{1,0:T(8,128)(2,1)} collective-permute-done((bf16[64,3584]{1,0:T(8,128)(2,1)S(1)}, bf16[64,3584]{1,0:T(8,128)(2,1)}, u32[]{:S(2)}, u32[]{:S(2)}) %collective-permute-start.15) | collective-permute-done | bytes 458784 | tf_op jit(solution)/shard_map/ppermute | solution.py:306
  277.9 5.6 %all-to-all-start.7 = ((bf16[4,48,3584]{2,1,0:T(8,128)(2,1)}), bf16[4,48,3584]{2,1,0:T(8,128)(2,1)S(1)}, u32[]{:S(2)}, u32[]{:S(2)}) async-start(bf16[4,48,3584]{2,1,0:T(8,128)(2,1)} %bitcast.31), calls=%async_computation.7 | async-start | bytes 2752512 | tf_op jit(solution)/shard_map/all_to_all | solution.py:324
  283.5 7.9 %shard_map.119 = bf16[256,3584]{1,0:T(8,128)(2,1)} custom-call(s32[1]{0:T(128)S(6)} %sub.36.which_ref, bf16[2,384,256]{2,1,0:T(8,128)(2,1)} %get-tuple-element.97.refs_0_, bf16[2,384,256]{2,1,0:T(8,128)(2,1)} %get-tuple-element.98.refs_1_, bf16[192,3584]{1,0:T(8,128)(2,1)} %bitcast.66, bf16[192,3584]{1,0:T(8,128)(2,1)} %copy-done.2, ...), custom_call_target="tpu_custom_call" | custom-call | flops 1 | bytes 1 | tf_op jit(solution)/shard_map/pallas_call | solution.py:231
  294.6 5.3 %shard_map.120 = (bf16[64,3584]{1,0:T(8,128)(2,1)}, bf16[64,3584]{1,0:T(8,128)(2,1)}) custom-call(bf16[128,192]{1,0:T(8,128)(2,1)} %copy.56.matrix_ref, bf16[192,3584]{1,0:T(8,128)(2,1)} %bitcast.73), custom_call_target="tpu_custom_call" | custom-call | flops 1 | bytes 1 | tf_op jit(solution)/shard_map/pallas_call | solution.py:103
  299.9 32.5 %collective-permute-done.17.refs_6_ = bf16[256,3584]{1,0:T(8,128)(2,1)S(1)} collective-permute-done((bf16[256,3584]{1,0:T(8,128)(2,1)}, bf16[256,3584]{1,0:T(8,128)(2,1)S(1)}, u32[]{:S(2)}, u32[]{:S(2)}) %collective-permute-start.17) | collective-permute-done | bytes 1835040 | tf_op jit(solution)/shard_map/ppermute | solution.py:315
  342.7 5.9 %shard_map.121 = bf16[128,3584]{1,0:T(8,128)(2,1)} custom-call(f32[128,192]{1,0:T(8,128)} %copy.57.matrix_ref, bf16[192,3584]{1,0:T(8,128)(2,1)} %bitcast.24.rows_ref, bf16[64,3584]{1,0:T(8,128)(2,1)} %collective-permute-done.15.refs_0_, bf16[64,3584]{1,0:T(8,128)(2,1)} %collective-permute-done.16.refs_1_), custom_call_target="tpu_custom_call" | custom-call | flops 1 | bytes 1 | tf_op jit(solution)/shard_map/pallas_call | solution.py:103
  348.6 8.3 %shard_map.124 = bf16[256,3584]{1,0:T(8,128)(2,1)} custom-call(s32[1]{0:T(128)} %bitcast.33.which_ref, bf16[2,384,256]{2,1,0:T(8,128)(2,1)} %get-tuple-element.97.refs_0_, bf16[2,384,256]{2,1,0:T(8,128)(2,1)} %get-tuple-element.98.refs_1_, bf16[192,3584]{1,0:T(8,128)(2,1)} %bitcast.67, bf16[192,3584]{1,0:T(8,128)(2,1)} %copy-done.2, ...), custom_call_target="tpu_custom_call" | custom-call | flops 1 | bytes 1 | tf_op jit(solution)/shard_map/pallas_call | solution.py:231
  356.9 13.2 %shard_map.123 = (bf16[3584,256]{1,0:T(8,128)(2,1)}, bf16[3584,256]{1,0:T(8,128)(2,1)}) custom-call(s32[1]{0:T(128)} %bitcast.33.which_ref, bf16[2,384,512]{2,1,0:T(8,128)(2,1)} %get-tuple-element.108.refs_0_, bf16[2,384,512]{2,1,0:T(8,128)(2,1)} %get-tuple-element.109.refs_1_, bf16[384,512]{1,0:T(8,128)(2,1)} %collective-permute-done.20.refs_2_, ...), custom_call_target="tpu_custom_call" | custom-call | flops 1 | bytes 1 | tf_op jit(solution)/shard_map/pallas_call | solution.py:263
  370.1 6.6 %collective-permute-done.19.refs_1_ = bf16[64,3584]{1,0:T(8,128)(2,1)} collective-permute-done((bf16[64,3584]{1,0:T(8,128)(2,1)}, bf16[64,3584]{1,0:T(8,128)(2,1)}, u32[]{:S(2)}, u32[]{:S(2)}) %collective-permute-start.19) | collective-permute-done | bytes 458784 | tf_op jit(solution)/shard_map/ppermute | solution.py:306
  376.7 5.6 %shard_map.122 = bf16[128,3584]{1,0:T(8,128)(2,1)} custom-call(bf16[128,192]{1,0:T(8,128)(2,1)} %copy.58.matrix_ref, bf16[192,3584]{1,0:T(8,128)(2,1)} %bitcast.72, bf16[64,3584]{1,0:T(8,128)(2,1)} %collective-permute-done.18.refs_0_, bf16[64,3584]{1,0:T(8,128)(2,1)} %collective-permute-done.19.refs_1_), custom_call_target="tpu_custom_call" | custom-call | flops 1 | bytes 1 | tf_op jit(solution)/shard_map/pallas_call | solution.py:103
  (122 shorter events, 63.3 us)
Async XLA Ops:
  2.1 5.6 %collective-permute-start = (f32[128,4]{0,1:T(4,128)S(1)}, f32[128,4]{0,1:T(4,128)S(1)}, u32[]{:S(2)}, u32[]{:S(2)}) collective-permute-start(f32[128,4]{0,1:T(4,128)S(1)} %pad_maximum_fusion), channel_id=1, source_target_pairs={{0,8},{1,9},{2,10},{3,11},{4,12},{5,13},{6,14},{7,15},{8,0},{9,1},... | collective-permute-start | bytes 6152 | tf_op jit(solution)/shard_map/ppermute | solution.py:306
  14.7 31.0 %all-to-all-start = ((bf16[4,48,3584]{2,1,0:T(8,128)(2,1)}), bf16[4,48,3584]{2,1,0:T(8,128)(2,1)}, u32[]{:S(2)}, u32[]{:S(2)}) async-start(bf16[4,48,3584]{2,1,0:T(8,128)(2,1)} %bitcast.78), calls=%async_computation | async-start | bytes 2752512 | tf_op jit(solution)/shard_map/all_to_all | solution.py:324
  20.0 23.4 %collective-permute-start.1 = (bf16[64,3584]{1,0:T(8,128)(2,1)S(1)}, bf16[64,3584]{1,0:T(8,128)(2,1)S(1)}, u32[]{:S(2)}, u32[]{:S(2)}) collective-permute-start(bf16[64,3584]{1,0:T(8,128)(2,1)S(1)} %get-tuple-element.126), channel_id=1, source_target_pairs={{0,8},{1,9},{2,10},{3,11},{4,12},{5,13},{6,14},{7,15},{8,0},{9,1},... | collective-permute-start | bytes 1376264 | tf_op jit(solution)/shard_map/ppermute | solution.py:306
  45.7 34.3 %all-to-all-start.1 = ((bf16[4,48,3584]{2,1,0:T(8,128)(2,1)}), bf16[4,48,3584]{2,1,0:T(8,128)(2,1)S(1)}, u32[]{:S(2)}, u32[]{:S(2)}) async-start(bf16[4,48,3584]{2,1,0:T(8,128)(2,1)} %bitcast.75), calls=%async_computation.1 | async-start | bytes 2752512 | tf_op jit(solution)/shard_map/all_to_all | solution.py:324
  51.1 28.9 %collective-permute-start.3 = (bf16[192,3584]{1,0:T(8,128)(2,1)}, bf16[192,3584]{1,0:T(8,128)(2,1)S(1)}, u32[]{:S(2)}, u32[]{:S(2)}) collective-permute-start(bf16[192,3584]{1,0:T(8,128)(2,1)} %bitcast.8.a_ref.refs_4_), channel_id=1, source_target_pairs={{0,1},{1,0},{2,3},{3,2},{4,5},{5,4},{6,7},{7,6},{8,9},{9,8},{10,11... | collective-permute-start | bytes 4128776 | tf_op jit(solution)/shard_map/ppermute | solution.py:306
  51.1 22.8 %collective-permute-start.2 = (bf16[64,3584]{1,0:T(8,128)(2,1)}, bf16[64,3584]{1,0:T(8,128)(2,1)S(1)}, u32[]{:S(2)}, u32[]{:S(2)}) collective-permute-start(bf16[64,3584]{1,0:T(8,128)(2,1)} %get-tuple-element.61), channel_id=1, source_target_pairs={{0,8},{1,9},{2,10},{3,11},{4,12},{5,13},{6,14},{7,15},{8,0},{9,1},... | collective-permute-start | bytes 1376264 | tf_op jit(solution)/shard_map/ppermute | solution.py:306
  92.5 9.5 %collective-permute-start.5 = (bf16[192,3584]{1,0:T(8,128)(2,1)}, bf16[192,3584]{1,0:T(8,128)(2,1)}, u32[]{:S(2)}, u32[]{:S(2)}) collective-permute-start(bf16[192,3584]{1,0:T(8,128)(2,1)} %get-tuple-element.68), channel_id=1, source_target_pairs={{0,1},{1,0},{2,3},{3,2},{4,5},{5,4},{6,7},{7,6},{8,9},{9,8},{10,11... | collective-permute-start | bytes 4128776 | tf_op jit(solution)/shard_map/ppermute | solution.py:306
  92.6 37.8 %all-to-all-start.2 = ((bf16[4,48,3584]{2,1,0:T(8,128)(2,1)}), bf16[4,48,3584]{2,1,0:T(8,128)(2,1)}, u32[]{:S(2)}, u32[]{:S(2)}) async-start(bf16[4,48,3584]{2,1,0:T(8,128)(2,1)} %bitcast.17), calls=%async_computation.2 | async-start | bytes 2752512 | tf_op jit(solution)/shard_map/all_to_all | solution.py:324
  97.8 32.6 %collective-permute-start.6 = (bf16[192,3584]{1,0:T(8,128)(2,1)}, bf16[192,3584]{1,0:T(8,128)(2,1)}, u32[]{:S(2)}, u32[]{:S(2)}) collective-permute-start(bf16[192,3584]{1,0:T(8,128)(2,1)} %bitcast.8.a_ref.refs_4_), channel_id=1, source_target_pairs={{0,16},{16,0},{1,17},{17,1},{2,18},{18,2},{3,19},{19,3},{4,20},{20... | collective-permute-start | bytes 4128776 | tf_op jit(solution)/shard_map/ppermute | solution.py:315
  99.0 36.1 %collective-permute-start.11 = (bf16[192,3584]{1,0:T(8,128)(2,1)S(1)}, bf16[192,3584]{1,0:T(8,128)(2,1)S(1)}, u32[]{:S(2)}, u32[]{:S(2)}) collective-permute-start(bf16[192,3584]{1,0:T(8,128)(2,1)S(1)} %bitcast.64), channel_id=1, source_target_pairs={{0,1},{1,0},{2,3},{3,2},{4,5},{5,4},{6,7},{7,6},{8,9},{9,8},{10,11... | collective-permute-start | bytes 4128776 | tf_op jit(solution)/shard_map/ppermute | solution.py:306
  99.0 31.4 %collective-permute-start.4 = (bf16[64,3584]{1,0:T(8,128)(2,1)}, bf16[64,3584]{1,0:T(8,128)(2,1)}, u32[]{:S(2)}, u32[]{:S(2)}) collective-permute-start(bf16[64,3584]{1,0:T(8,128)(2,1)} %get-tuple-element.65), channel_id=1, source_target_pairs={{0,8},{1,9},{2,10},{3,11},{4,12},{5,13},{6,14},{7,15},{8,0},{9,1},... | collective-permute-start | bytes 1376264 | tf_op jit(solution)/shard_map/ppermute | solution.py:306
  130.4 50.2 %all-to-all-start.3 = ((bf16[4,48,3584]{2,1,0:T(8,128)(2,1)}), bf16[4,48,3584]{2,1,0:T(8,128)(2,1)}, u32[]{:S(2)}, u32[]{:S(2)}) async-start(bf16[4,48,3584]{2,1,0:T(8,128)(2,1)} %bitcast.74), calls=%async_computation.3 | async-start | bytes 2752512 | tf_op jit(solution)/shard_map/all_to_all | solution.py:324
  135.0 18.7 %collective-permute-start.8 = (bf16[192,3584]{1,0:T(8,128)(2,1)}, bf16[192,3584]{1,0:T(8,128)(2,1)S(1)}, u32[]{:S(2)}, u32[]{:S(2)}) collective-permute-start(bf16[192,3584]{1,0:T(8,128)(2,1)} %bitcast.18.a_ref.refs_6_), channel_id=1, source_target_pairs={{0,1},{1,0},{2,3},{3,2},{4,5},{5,4},{6,7},{7,6},{8,9},{9,8},{10,11... | collective-permute-start | bytes 4128776 | tf_op jit(solution)/shard_map/ppermute | solution.py:306
  150.5 35.4 %collective-permute-start.12 = (bf16[192,3584]{1,0:T(8,128)(2,1)}, bf16[192,3584]{1,0:T(8,128)(2,1)}, u32[]{:S(2)}, u32[]{:S(2)}) collective-permute-start(bf16[192,3584]{1,0:T(8,128)(2,1)} %get-tuple-element.81), channel_id=1, source_target_pairs={{0,1},{1,0},{2,3},{3,2},{4,5},{5,4},{6,7},{7,6},{8,9},{9,8},{10,11... | collective-permute-start | bytes 4128776 | tf_op jit(solution)/shard_map/ppermute | solution.py:306
  151.0 23.3 %collective-permute-start.7 = (bf16[64,3584]{1,0:T(8,128)(2,1)S(1)}, bf16[64,3584]{1,0:T(8,128)(2,1)S(1)}, u32[]{:S(2)}, u32[]{:S(2)}) collective-permute-start(bf16[64,3584]{1,0:T(8,128)(2,1)S(1)} %get-tuple-element.70), channel_id=1, source_target_pairs={{0,8},{1,9},{2,10},{3,11},{4,12},{5,13},{6,14},{7,15},{8,0},{9,1},... | collective-permute-start | bytes 1376264 | tf_op jit(solution)/shard_map/ppermute | solution.py:306
  166.4 22.4 %collective-permute-start.9 = (bf16[192,3584]{1,0:T(8,128)(2,1)}, bf16[192,3584]{1,0:T(8,128)(2,1)}, u32[]{:S(2)}, u32[]{:S(2)}) collective-permute-start(bf16[192,3584]{1,0:T(8,128)(2,1)} %get-tuple-element.76), channel_id=1, source_target_pairs={{0,1},{1,0},{2,3},{3,2},{4,5},{5,4},{6,7},{7,6},{8,9},{9,8},{10,11... | collective-permute-start | bytes 4128776 | tf_op jit(solution)/shard_map/ppermute | solution.py:306
  180.6 35.5 %all-to-all-start.4 = ((bf16[4,48,3584]{2,1,0:T(8,128)(2,1)}), bf16[4,48,3584]{2,1,0:T(8,128)(2,1)S(1)}, u32[]{:S(2)}, u32[]{:S(2)}) async-start(bf16[4,48,3584]{2,1,0:T(8,128)(2,1)} %bitcast.77), calls=%async_computation.4 | async-start | bytes 2752512 | tf_op jit(solution)/shard_map/all_to_all | solution.py:324
  184.3 31.8 %collective-permute-start.10 = (bf16[192,3584]{1,0:T(8,128)(2,1)}, bf16[192,3584]{1,0:T(8,128)(2,1)}, u32[]{:S(2)}, u32[]{:S(2)}) collective-permute-start(bf16[192,3584]{1,0:T(8,128)(2,1)} %bitcast.18.a_ref.refs_6_), channel_id=1, source_target_pairs={{0,16},{16,0},{1,17},{17,1},{2,18},{18,2},{3,19},{19,3},{4,20},{20... | collective-permute-start | bytes 4128776 | tf_op jit(solution)/shard_map/ppermute | solution.py:315
  216.1 5.6 %collective-permute-start.13 = (bf16[192,3584]{1,0:T(8,128)(2,1)S(1)}, bf16[192,3584]{1,0:T(8,128)(2,1)S(1)}, u32[]{:S(2)}, u32[]{:S(2)}) collective-permute-start(bf16[192,3584]{1,0:T(8,128)(2,1)S(1)} %bitcast.68), channel_id=1, source_target_pairs={{0,1},{1,0},{2,3},{3,2},{4,5},{5,4},{6,7},{7,6},{8,9},{9,8},{10,11... | collective-permute-start | bytes 4128776 | tf_op jit(solution)/shard_map/ppermute | solution.py:306
  217.1 21.7 %all-to-all-start.5 = ((bf16[4,48,3584]{2,1,0:T(8,128)(2,1)}), bf16[4,48,3584]{2,1,0:T(8,128)(2,1)}, u32[]{:S(2)}, u32[]{:S(2)}) async-start(bf16[4,48,3584]{2,1,0:T(8,128)(2,1)} %bitcast.76), calls=%async_computation.5 | async-start | bytes 2752512 | tf_op jit(solution)/shard_map/all_to_all | solution.py:324
  237.1 7.4 %collective-permute-start.14 = (bf16[192,3584]{1,0:T(8,128)(2,1)}, bf16[192,3584]{1,0:T(8,128)(2,1)S(1)}, u32[]{:S(2)}, u32[]{:S(2)}) collective-permute-start(bf16[192,3584]{1,0:T(8,128)(2,1)} %get-tuple-element.86), channel_id=1, source_target_pairs={{0,1},{1,0},{2,3},{3,2},{4,5},{5,4},{6,7},{7,6},{8,9},{9,8},{10,11... | collective-permute-start | bytes 4128776 | tf_op jit(solution)/shard_map/ppermute | solution.py:306
  246.0 30.9 %all-to-all-start.6 = ((bf16[4,48,3584]{2,1,0:T(8,128)(2,1)}), bf16[4,48,3584]{2,1,0:T(8,128)(2,1)S(1)}, u32[]{:S(2)}, u32[]{:S(2)}) async-start(bf16[4,48,3584]{2,1,0:T(8,128)(2,1)} %bitcast.29), calls=%async_computation.6 | async-start | bytes 2752512 | tf_op jit(solution)/shard_map/all_to_all | solution.py:324
  249.6 25.0 %collective-permute-start.15 = (bf16[64,3584]{1,0:T(8,128)(2,1)S(1)}, bf16[64,3584]{1,0:T(8,128)(2,1)}, u32[]{:S(2)}, u32[]{:S(2)}) collective-permute-start(bf16[64,3584]{1,0:T(8,128)(2,1)S(1)} %copy-done.18), channel_id=1, source_target_pairs={{0,8},{1,9},{2,10},{3,11},{4,12},{5,13},{6,14},{7,15},{8,0},{9,1},... | collective-permute-start | bytes 1376264 | tf_op jit(solution)/shard_map/ppermute | solution.py:306
  277.9 54.5 %all-to-all-start.7 = ((bf16[4,48,3584]{2,1,0:T(8,128)(2,1)}), bf16[4,48,3584]{2,1,0:T(8,128)(2,1)S(1)}, u32[]{:S(2)}, u32[]{:S(2)}) async-start(bf16[4,48,3584]{2,1,0:T(8,128)(2,1)} %bitcast.31), calls=%async_computation.7 | async-start | bytes 2752512 | tf_op jit(solution)/shard_map/all_to_all | solution.py:324
  291.4 40.9 %collective-permute-start.17 = (bf16[256,3584]{1,0:T(8,128)(2,1)}, bf16[256,3584]{1,0:T(8,128)(2,1)S(1)}, u32[]{:S(2)}, u32[]{:S(2)}) collective-permute-start(bf16[256,3584]{1,0:T(8,128)(2,1)} %shard_map.119), channel_id=1, source_target_pairs={{0,16},{16,0},{1,17},{17,1},{2,18},{18,2},{3,19},{19,3},{4,20},{20... | collective-permute-start | bytes 5505032 | tf_op jit(solution)/shard_map/ppermute | solution.py:315
  292.9 47.7 %collective-permute-start.22 = (bf16[192,3584]{1,0:T(8,128)(2,1)}, bf16[192,3584]{1,0:T(8,128)(2,1)}, u32[]{:S(2)}, u32[]{:S(2)}) collective-permute-start(bf16[192,3584]{1,0:T(8,128)(2,1)} %collective-permute-done.6.refs_8_), channel_id=1, source_target_pairs={{0,1},{1,0},{2,3},{3,2},{4,5},{5,4},{6,7},{7,6},{8,9},{9,8},{10,11... | collective-permute-start | bytes 4128776 | tf_op jit(solution)/shard_map/ppermute | solution.py:306
  292.9 64.0 %collective-permute-start.23 = (bf16[192,3584]{1,0:T(8,128)(2,1)}, bf16[192,3584]{1,0:T(8,128)(2,1)}, u32[]{:S(2)}, u32[]{:S(2)}) collective-permute-start(bf16[192,3584]{1,0:T(8,128)(2,1)} %collective-permute-done.10.refs_10_), channel_id=1, source_target_pairs={{0,1},{1,0},{2,3},{3,2},{4,5},{5,4},{6,7},{7,6},{8,9},{9,8},{10,11... | collective-permute-start | bytes 4128776 | tf_op jit(solution)/shard_map/ppermute | solution.py:306
  293.4 38.9 %collective-permute-start.16 = (bf16[64,3584]{1,0:T(8,128)(2,1)}, bf16[64,3584]{1,0:T(8,128)(2,1)}, u32[]{:S(2)}, u32[]{:S(2)}) collective-permute-start(bf16[64,3584]{1,0:T(8,128)(2,1)} %get-tuple-element.95), channel_id=1, source_target_pairs={{0,8},{1,9},{2,10},{3,11},{4,12},{5,13},{6,14},{7,15},{8,0},{9,1},... | collective-permute-start | bytes 1376264 | tf_op jit(solution)/shard_map/ppermute | solution.py:306
  334.4 22.5 %collective-permute-start.20 = (bf16[384,512]{1,0:T(8,128)(2,1)}, bf16[384,512]{1,0:T(8,128)(2,1)}, u32[]{:S(2)}, u32[]{:S(2)}) collective-permute-start(bf16[384,512]{1,0:T(8,128)(2,1)} %dynamic-slice_bitcast_fusion.1), channel_id=1, source_target_pairs={{0,16},{16,0},{1,17},{17,1},{2,18},{18,2},{3,19},{19,3},{4,20},{20... | collective-permute-start | bytes 1179656 | tf_op jit(solution)/shard_map/ppermute | solution.py:315
  335.9 34.2 %collective-permute-start.18 = (bf16[64,3584]{1,0:T(8,128)(2,1)}, bf16[64,3584]{1,0:T(8,128)(2,1)}, u32[]{:S(2)}, u32[]{:S(2)}) collective-permute-start(bf16[64,3584]{1,0:T(8,128)(2,1)} %get-tuple-element.106), channel_id=1, source_target_pairs={{0,8},{1,9},{2,10},{3,11},{4,12},{5,13},{6,14},{7,15},{8,0},{9,1},... | collective-permute-start | bytes 1376264 | tf_op jit(solution)/shard_map/ppermute | solution.py:306
  336.3 40.3 %collective-permute-start.19 = (bf16[64,3584]{1,0:T(8,128)(2,1)}, bf16[64,3584]{1,0:T(8,128)(2,1)}, u32[]{:S(2)}, u32[]{:S(2)}) collective-permute-start(bf16[64,3584]{1,0:T(8,128)(2,1)} %get-tuple-element.107), channel_id=1, source_target_pairs={{0,8},{1,9},{2,10},{3,11},{4,12},{5,13},{6,14},{7,15},{8,0},{9,1},... | collective-permute-start | bytes 1376264 | tf_op jit(solution)/shard_map/ppermute | solution.py:306
  340.6 16.3 %collective-permute-start.21 = (bf16[384,512]{1,0:T(8,128)(2,1)}, bf16[384,512]{1,0:T(8,128)(2,1)}, u32[]{:S(2)}, u32[]{:S(2)}) collective-permute-start(bf16[384,512]{1,0:T(8,128)(2,1)} %dynamic-slice_bitcast_fusion), channel_id=1, source_target_pairs={{0,16},{16,0},{1,17},{17,1},{2,18},{18,2},{3,19},{19,3},{4,20},{20... | collective-permute-start | bytes 1179656 | tf_op jit(solution)/shard_map/ppermute | solution.py:315
  (19 other events, 101.7 us)

commit v6 on v5

v6 whole, which is shorter than its diff:
```python
import jax
import jax.numpy as jnp
from jax import lax
from jax.experimental import pallas as pl
from jax.experimental.pallas import tpu as pltpu
from jax.sharding import PartitionSpec as P

TOPK = 2
MB = 2
TOK_MB = 64
F32 = jnp.float32
BF16 = jnp.bfloat16
NN = ((1,), (0,))
NT = ((1,), (1,))
TN = ((0,), (0,))
VMEM_BYTES = 56 * 1024 * 1024


def dot(a, b, dims):
    return lax.dot_general(a, b, (dims, ((), ())), preferred_element_type=F32)


def tile_of(width):
    return 512 if width % 512 == 0 else width


def kernel_call(body, grid, in_specs, out_specs, out_shape, scratch=(), scalars=0):
    return pl.pallas_call(
        body,
        grid_spec=pltpu.PrefetchScalarGridSpec(
            num_scalar_prefetch=scalars,
            grid=grid,
            in_specs=in_specs,
            out_specs=out_specs,
            scratch_shapes=scratch,
        ),
        out_shape=out_shape,
        compiler_params=pltpu.CompilerParams(
            vmem_limit_bytes=VMEM_BYTES, dimension_semantics=("arbitrary",)
        ),
        cost_estimate=pl.CostEstimate(flops=1, bytes_accessed=1, transcendentals=0),
    )


def place(placing, rows, gain=None):
    slots = dot(placing, rows, NN)
    return (slots if gain is None else slots * gain).astype(BF16)


def combine(matrix, rows):
    if matrix.dtype == BF16:
        return dot(matrix, rows, NN)
    return lax.dot_general(
        matrix,
        rows.astype(F32),
        (NN, ((), ())),
        precision=lax.Precision.HIGHEST,
        preferred_element_type=F32,
    )


def chunks(width):
    tile = tile_of(width)
    return [slice(n * tile, (n + 1) * tile) for n in range(width // tile)]


def forward(rows, gate_weight, up_weight, down_weight):
    count, width = rows[0].shape
    half_units = gate_weight.shape[1] // 2

    def body(a_ref, b_ref, gate_ref, up_ref, down_ref, pre_gate_ref, pre_up_ref, hidden_ref, out_a, out_b, x_ref, acc_ref):
        step = pl.program_id(0)

        @pl.when(step == 0)
        def _():
            x_ref[:count] = a_ref[...]
            x_ref[count:] = b_ref[...]

        pre_gate = dot(x_ref[...], gate_ref[...], NN)
        pre_up = dot(x_ref[...], up_ref[...], NN)
        pre_gate_ref[0] = pre_gate
        pre_up_ref[0] = pre_up
        hidden = (pre_gate * jax.nn.sigmoid(pre_gate) * pre_up).astype(BF16)
        hidden_ref[0] = hidden

        @pl.when(step == 0)
        def _():
            for cut in chunks(width):
                acc_ref[:, cut] = dot(hidden, down_ref[:, cut], NN)

        @pl.when(step == 1)
        def _():
            for cut in chunks(width):
                total = (acc_ref[:, cut] + dot(hidden, down_ref[:, cut], NN)).astype(BF16)
                out_a[:, cut] = total[:count]
                out_b[:, cut] = total[count:]

    whole = pl.BlockSpec((count, width), lambda n: (0, 0))
    columns = pl.BlockSpec((width, half_units), lambda n: (0, n))
    units = pl.BlockSpec((1, 2 * count, half_units), lambda n: (n, 0, 0))
    return kernel_call(
        body,
        (2,),
        [whole, whole, columns, columns, pl.BlockSpec((half_units, width), lambda n: (n, 0))],
        [units, units, units, whole, whole],
        [
            jax.ShapeDtypeStruct((2, 2 * count, half_units), F32),
            jax.ShapeDtypeStruct((2, 2 * count, half_units), F32),
            jax.ShapeDtypeStruct((2, 2 * count, half_units), BF16),
            jax.ShapeDtypeStruct((count, width), BF16),
            jax.ShapeDtypeStruct((count, width), BF16),
        ],
        [pltpu.VMEM((2 * count, width), BF16), pltpu.VMEM((2 * count, width), F32)],
    )(*rows, gate_weight, up_weight, down_weight)


def backward(rows_grad, pre_gate, pre_up, gate_weight, up_weight, down_weight):
    count, width = rows_grad[0].shape
    half_units = gate_weight.shape[1] // 2

    def body(a_ref, b_ref, pre_gate_ref, pre_up_ref, gate_ref, up_ref, down_ref, units_ref, out_a, out_b, x_ref, acc_ref):
        step = pl.program_id(0)

        @pl.when(step == 0)
        def _():
            x_ref[:count] = a_ref[...]
            x_ref[count:] = b_ref[...]

        hidden_grad = dot(x_ref[...], down_ref[...], NT)
        pre_gate = pre_gate_ref[0]
        sigma = jax.nn.sigmoid(pre_gate)
        gate_grad = (
            hidden_grad * pre_up_ref[0] * sigma * (1.0 + pre_gate * (1.0 - sigma))
        ).astype(BF16)
        up_grad = (hidden_grad * (pre_gate * sigma)).astype(BF16)
        units_ref[0, :, :half_units] = gate_grad
        units_ref[0, :, half_units:] = up_grad

        @pl.when(step == 0)
        def _():
            for cut in chunks(width):
                acc_ref[:, cut] = dot(gate_grad, gate_ref[cut], NT) + dot(up_grad, up_ref[cut], NT)

        @pl.when(step == 1)
        def _():
            for cut in chunks(width):
                total = acc_ref[:, cut] + dot(gate_grad, gate_ref[cut], NT)
                total = (total + dot(up_grad, up_ref[cut], NT)).astype(BF16)
                out_a[:, cut] = total[:count]
                out_b[:, cut] = total[count:]

    whole = pl.BlockSpec((count, width), lambda n: (0, 0))
    columns = pl.BlockSpec((width, half_units), lambda n: (0, n))
    units = pl.BlockSpec((1, 2 * count, half_units), lambda n: (n, 0, 0))
    return kernel_call(
        body,
        (2,),
        [whole, whole, units, units, columns, columns, pl.BlockSpec((half_units, width), lambda n: (n, 0))],
        [pl.BlockSpec((1, 2 * count, 2 * half_units), lambda n: (n, 0, 0)), whole, whole],
        [
            jax.ShapeDtypeStruct((2, 2 * count, 2 * half_units), BF16),
            jax.ShapeDtypeStruct((count, width), BF16),
            jax.ShapeDtypeStruct((count, width), BF16),
        ],
        [pltpu.VMEM((2 * count, width), BF16), pltpu.VMEM((2 * count, width), F32)],
    )(*rows_grad, pre_gate, pre_up, gate_weight, up_weight, down_weight)


def down_grad(which, hiddens, rows_grad, got=None):
    count, width = rows_grad[0].shape
    half_units = hiddens[0].shape[2]
    tile = tile_of(width)

    def body(which_ref, *refs):
        unit_refs, row_refs, rest = refs[:2], refs[2:6], refs[6:]
        turned_ref = rest[-1]

        @pl.when(pl.program_id(0) == 0)
        def _():
            for n, unit_ref in enumerate(unit_refs):
                turned_ref[:, 2 * n * count : 2 * (n + 1) * count] = unit_ref[0].T

        rows = jnp.concatenate([ref[...] for ref in row_refs], axis=0)
        total = dot(turned_ref[...], rows, NN)
        if got is not None:
            total = total.astype(BF16).astype(F32) + rest[0][...].astype(F32)
        rest[-2][...] = total.astype(BF16)

    out_spec = pl.BlockSpec((half_units, tile), lambda n, w: (0, n))
    return kernel_call(
        body,
        (width // tile,),
        [pl.BlockSpec((1, 2 * count, half_units), lambda n, w: (w[0], 0, 0))] * 2
        + [pl.BlockSpec((count, tile), lambda n, w: (0, n))] * 4
        + [out_spec] * (got is not None),
        out_spec,
        jax.ShapeDtypeStruct((half_units, width), BF16),
        [pltpu.VMEM((half_units, 4 * count), BF16)],
        scalars=1,
    )(which, *hiddens, *rows_grad, *([] if got is None else [got]))


def gate_up_grad(which, units, rows, mirror_units, mirror_rows):
    count, width = rows[0].shape
    both = units[0].shape[2]
    half_units = both // 2
    tile = tile_of(width)

    def body(which_ref, *refs):
        unit_refs, mirror_refs, row_refs = refs[:2], refs[2:4], refs[4:12]
        gate_ref, up_ref, turned_ref = refs[12:]

        @pl.when(pl.program_id(0) == 0)
        def _():
            for n, factor in enumerate([ref[0] for ref in unit_refs] + [ref[...] for ref in mirror_refs]):
                turned_ref[:, 2 * n * count : 2 * (n + 1) * count] = factor.T

        rows = jnp.concatenate([ref[...] for ref in row_refs], axis=0)
        total = dot(turned_ref[...], rows, NN).astype(BF16).T
        gate_ref[...] = total[:, :half_units]
        up_ref[...] = total[:, half_units:]

    out_spec = pl.BlockSpec((tile, half_units), lambda n, w: (n, 0))
    return kernel_call(
        body,
        (width // tile,),
        [pl.BlockSpec((1, 2 * count, both), lambda n, w: (w[0], 0, 0))] * 2
        + [pl.BlockSpec((2 * count, both), lambda n, w: (0, 0))] * 2
        + [pl.BlockSpec((count, tile), lambda n, w: (0, n))] * 8,
        [out_spec] * 2,
        [jax.ShapeDtypeStruct((width, half_units), BF16)] * 2,
        [pltpu.VMEM((both, 8 * count), BF16)],
        scalars=1,
    )(which, *units, *mirror_units, *rows, *mirror_rows)


def route(meta, half, expert_count, capacity):
    ids, gain = meta[:, :TOPK].astype(jnp.int32), meta[:, TOPK:]
    flat_ids = ids.reshape(MB, TOK_MB * TOPK)
    member = (flat_ids[:, :, None] == jnp.arange(expert_count, dtype=jnp.int32)).astype(jnp.int32)
    running = jnp.cumsum(member, axis=1) - 1
    rank = jnp.sum(member * running, axis=2)
    batch = jnp.arange(MB, dtype=jnp.int32)[:, None]
    near = expert_count // 2
    target = (((flat_ids - half * near) * MB + batch) * capacity + rank).reshape(ids.shape)
    slots = jnp.arange(near * MB * capacity, dtype=jnp.int32)
    matches = (target[:, :, None] == slots).astype(F32)
    turned = (target.T[:, None, :] == slots[:, None]).astype(F32)
    weighting = jnp.sum(matches * gain[:, :, None], axis=1)
    slot_gain = jnp.sum(turned * gain.T[:, None, :], axis=(0, 2))[:, None]
    return jnp.sum(turned, axis=0).astype(BF16), jnp.sum(matches, axis=1).astype(BF16), weighting, slot_gain


def on_device(acts, grad_out, expert_ids, route_weights, w_gate, w_up, w_down):
    weights = (w_gate[0], w_up[0], w_down[0])
    devices = lax.axis_size("expert")
    chips = devices // 2
    near = chips // 2
    capacity = 3 * TOPK * TOK_MB // (2 * chips)
    piece = MB * capacity
    width = acts.shape[2]
    half = (lax.axis_index("expert") >= devices // 2).astype(jnp.int32)
    rank_count = lax.axis_size("pipe")
    kept_half = (lax.axis_index("pipe") >= rank_count // 2).astype(jnp.int32)
    kept = kept_half.reshape(1)

    def hop(rows, distance):
        return lax.ppermute(rows, "expert", [(i, i ^ distance) for i in range(devices)])

    def far(rows):
        return hop(rows, devices // 2)

    def swap(rows):
        return hop(rows, 1)

    def mirror(rows):
        return lax.ppermute(rows, "pipe", [(p, rank_count - 1 - p) for p in range(rank_count)])

    groups = [
        [(part * near + member) * 2 + core for member in range(near)]
        for part in range(2)
        for core in range(2)
    ]

    def near_exchange(rows):
        return lax.all_to_all(
            rows.reshape(near, piece, width),
            "expert",
            split_axis=0,
            concat_axis=0,
            axis_index_groups=groups,
            tiled=True,
        ).reshape(near * piece, width)

    def tie(*arrays):
        return lax.optimization_barrier(arrays)

    def expert_sum(mine, other):
        return (mine.astype(F32) + swap(other).astype(F32)).astype(BF16)

    acts_parts = [acts[0, b * TOK_MB : (b + 1) * TOK_MB] for b in range(MB)]
    grad_parts = [grad_out[0, b * TOK_MB : (b + 1) * TOK_MB] for b in range(MB)]
    meta = jnp.concatenate([expert_ids[0].astype(F32), route_weights[0]], axis=1)
    far_meta = far(meta)
    own_placing, own_back, own_weighting, own_gain = route(meta, half, chips, capacity)

    own_in = near_exchange(place(own_placing, acts[0]))
    far_acts_0 = far(acts_parts[0])
    acts_1, far_meta = tie(acts_parts[1], far_meta)
    far_acts_1 = far(acts_1)
    far_placing, far_back, far_weighting, far_gain = route(far_meta, half, chips, capacity)

    own_grad, own_in = tie(place(own_placing, grad_out[0], own_gain), own_in)
    own_grad = near_exchange(own_grad)
    own_in_b = swap(own_in)
    mirror_own = mirror(own_in)
    grads_0, far_acts_0 = tie(grad_parts[0], far_acts_0)
    far_grads_0 = far(grads_0)

    far_acts_1, own_grad, own_in_b = tie(far_acts_1, own_grad, own_in_b)
    far_in = near_exchange(place(far_placing, jnp.concatenate([far_acts_0, far_acts_1], axis=0)))
    grads_1, far_acts_1 = tie(grad_parts[1], far_acts_1)
    far_grads_1 = far(grads_1)
    own_grad_b = swap(own_grad)
    own_pre_gate, own_pre_up, own_hidden, own_out, own_out_b = forward((own_in, own_in_b), *weights)
    own_units, own_input, own_input_b = backward(
        (own_grad, own_grad_b), own_pre_gate, own_pre_up, *weights
    )

    far_grad = place(far_placing, jnp.concatenate([far_grads_0, far_grads_1], axis=0), far_gain)
    far_grad, far_in, own_units, own_input, own_input_b, mirror_own = tie(
        far_grad, far_in, own_units, own_input, own_input_b, mirror_own
    )
    far_in_b = swap(far_in)
    far_grad = near_exchange(far_grad)
    mirror_far = mirror(far_in)
    own_out = expert_sum(own_out, own_out_b)
    far_pre_gate, far_pre_up, far_hidden, far_out, far_out_b = forward((far_in, far_in_b), *weights)
    far_out = expert_sum(far_out, far_out_b)

    far_out, far_grad, own_out = tie(far_out, far_grad, own_out)
    far_out = near_exchange(far_out)
    far_grad_b = swap(far_grad)
    own_input = expert_sum(own_input, own_input_b)
    mirror_own_b = swap(mirror_own)
    mirror_units_own = mirror(lax.dynamic_index_in_dim(own_units, 1 - kept_half, 0, keepdims=False))
    far_units, far_input, far_input_b = backward(
        (far_grad, far_grad_b), far_pre_gate, far_pre_up, *weights
    )
    far_input = expert_sum(far_input, far_input_b)

    far_input, far_out, own_input, mirror_own_b, mirror_far, mirror_units_own = tie(
        far_input, far_out, own_input, mirror_own_b, mirror_far, mirror_units_own
    )
    back_out = combine(far_weighting, far_out).astype(BF16)
    got_out_0 = far(back_out[:TOK_MB])
    got_out_1 = far(back_out[TOK_MB:])
    far_input = near_exchange(far_input)
    mirror_units_far = mirror(lax.dynamic_index_in_dim(far_units, 1 - kept_half, 0, keepdims=False))
    rows_grad = (own_grad, own_grad_b, far_grad, far_grad_b)
    send_down = down_grad(1 - kept, (own_hidden, far_hidden), rows_grad)
    mirror_far_b = swap(mirror_far)

    send_down, mirror_units_far = tie(send_down, mirror_units_far)
    got_down = mirror(send_down)
    back_input = combine(far_back, far_input).astype(BF16)
    own_out, far_input, back_input, got_out_0, mirror_far_b, send_down = tie(
        own_out, far_input, back_input, got_out_0, mirror_far_b, send_down
    )
    own_out = near_exchange(own_out)
    got_input_0 = far(back_input[:TOK_MB])
    back_input_1, got_out_1 = tie(back_input[TOK_MB:], got_out_1)
    got_input_1 = far(back_input_1)
    own_input, own_out, got_out_1 = tie(own_input, own_out, got_out_1)
    own_input = near_exchange(own_input)
    grad_gate, grad_up = gate_up_grad(
        kept,
        (own_units, far_units),
        (own_in, own_in_b, far_in, far_in_b),
        (mirror_units_own, mirror_units_far),
        (mirror_own, mirror_own_b, mirror_far, mirror_far_b),
    )
    got_out = jnp.concatenate([got_out_0, got_out_1], axis=0).astype(F32)
    out_acts = (combine(own_weighting, own_out) + got_out).astype(BF16)
    grad_down = down_grad(kept, (own_hidden, far_hidden), rows_grad, got_down)
    got_input = jnp.concatenate([got_input_0, got_input_1], axis=0).astype(F32)
    grad_acts = (combine(own_back, own_input) + got_input).astype(BF16)
    return out_acts[None], grad_acts[None], grad_gate[None], grad_up[None], grad_down[None]


def solution(mesh):
    tokens = P("pipe", "expert", None)
    columns = P("pipe", None, "expert")
    return jax.shard_map(
        on_device,
        mesh=mesh,
        in_specs=(tokens, tokens, tokens, tokens, columns, columns, tokens),
        out_specs=(tokens, tokens, columns, columns, tokens),
        check_vma=False,
    )
```

time: 385 us -> 381 us (0.990)
  waiting for transfers between devices: 158 us -> 211 us
  Pallas kernels: 125 us -> 72.6 us
  matrix products: 0 us -> 14.7 us
  starting transfers between devices: 64.3 us -> 51.2 us
  local copies, waits for them, and re-layouts: 20.3 us -> 13.9 us
    pallas_call x8 -> x0, Pallas kernels: 44 us -> none  [the longest x4 22.5 us: combine(): kernel_call(body, (width // tile,), [pl.BlockSpec((tokens, slots), lambda...]
    all_to_all x8, waiting for transfers between devices: 5.31 us -> 45.2 us  [near_exchange(): lax.all_to_all(rows.reshape(near, piece, width), 'expert', split_axis=0,...]
    ppermute x19, waiting for transfers between devices: 70.1 us -> 99.2 us  [hop(): lax.ppermute(rows, 'expert', [(i, i ^ distance) for i in range(devices)])]
    ppermute x5, waiting for transfers between devices: 82.2 us -> 66.8 us  [mirror(): lax.ppermute(rows, 'pipe', [(p, rank_count - 1 - p) for p in range(rank_c...]
    dot_general x0 -> x8, matrix products: none -> 14.7 us  [the longest x6 11.9 us: dot(): return lax.dot_general(a, b, (dims, ((), ())), preferred_element_type=F32)]
    all_to_all x8, starting transfers between devices: 37.2 us -> 30.6 us  [near_exchange(): lax.all_to_all(rows.reshape(near, piece, width), 'expert', split_axis=0,...]
    pallas_call x2, Pallas kernels: 28.7 us -> 22.5 us  [backward(): kernel_call(body, (2,), [whole, whole, units, units, columns, columns, pl...]
    ppermute x19, starting transfers between devices: 20.8 us -> 15.3 us  [hop(): lax.ppermute(rows, 'expert', [(i, i ^ distance) for i in range(devices)])]
  transfers between devices with their start and end apart: 32 -> 32, of which waited for: 12 -> 14; matrix products, arithmetic and copies ran while one was open for 6% -> 7% of each run, Pallas kernels for 27% -> 19%
where the time goes in v6:
time: 381 us; the launch traced here: 379 us
  waiting for transfers between devices  211 us (55%)
  Pallas kernels  72.6 us (19%)
  starting transfers between devices  51.2 us (13%)
  matrix products  14.7 us (4%)
  other arithmetic  14.6 us (4%)
  local copies, waits for them, and re-layouts  13.9 us (4%)
    ppermute x19, waiting for transfers between devices, hop(): lax.ppermute(rows, 'expert', [(i, i ^ distance) for i in range(devices)])  99.2 us
    ppermute x5, waiting for transfers between devices, mirror(): lax.ppermute(rows, 'pipe', [(p, rank_count - 1 - p) for p in range(rank_c...  66.8 us
    all_to_all x8, waiting for transfers between devices, near_exchange(): lax.all_to_all(rows.reshape(near, piece, width), 'expert', split_axis=0,...  45.2 us
    all_to_all x8, starting transfers between devices, near_exchange(): lax.all_to_all(rows.reshape(near, piece, width), 'expert', split_axis=0,...  30.6 us
    pallas_call x2, Pallas kernels, backward(): kernel_call(body, (2,), [whole, whole, units, units, columns, columns, pl...  22.5 us
    pallas_call x2, Pallas kernels, forward(): kernel_call(body, (2,), [whole, whole, columns, columns, pl.BlockSpec((ha...  21.9 us
    pallas_call x2, Pallas kernels, down_grad(): kernel_call(body, (width // tile,), [pl.BlockSpec((1, 2 * count, half_uni...  15.8 us
    ppermute x19, starting transfers between devices, hop(): lax.ppermute(rows, 'expert', [(i, i ^ distance) for i in range(devices)])  15.3 us
  transfers between devices with their start and end apart: 32, of which 14 were waited for; matrix products, arithmetic and copies ran while one was open for 7% of the time, Pallas kernels for 19%

profile of v6, /device:TPU:0, one launch (start us, length us, event | category | flops | bytes accessed | tf_op | source)
XLA Modules:
  0.0 379.2 jit_solution(16758090876783287275)
XLA Ops:
  2.0 4.1 %collective-permute-start = (f32[128,4]{0,1:T(4,128)S(1)}, f32[128,4]{0,1:T(4,128)S(1)}, u32[]{:S(2)}, u32[]{:S(2)}) collective-permute-start(f32[128,4]{0,1:T(4,128)S(1)} %pad_maximum_fusion), channel_id=1, source_target_pairs={{0,8},{1,9},{2,10},{3,11},{4,12},{5,13},{6,14},{7,15},{8,0},{9,1},... | collective-permute-start | bytes 6152 | tf_op jit(solution)/shard_map/ppermute | solution.py:268
  11.9 3.9 %all-to-all-start = ((bf16[4,48,3584]{2,1,0:T(8,128)(2,1)}), bf16[4,48,3584]{2,1,0:T(8,128)(2,1)S(1)}, u32[]{:S(2)}, u32[]{:S(2)}) async-start(bf16[4,48,3584]{2,1,0:T(8,128)(2,1)} %bitcast.11), calls=%async_computation | async-start | bytes 2752512 | tf_op jit(solution)/shard_map/all_to_all | solution.py:286
  17.4 15.3 %all-to-all-done = bf16[4,48,3584]{2,1,0:T(8,128)(2,1)S(1)} async-done(((bf16[4,48,3584]{2,1,0:T(8,128)(2,1)}), bf16[4,48,3584]{2,1,0:T(8,128)(2,1)S(1)}, u32[]{:S(2)}, u32[]{:S(2)}) %all-to-all-start) | async-done | bytes 1376288 | tf_op jit(solution)/shard_map/all_to_all | solution.py:286
  32.7 3.5 all-to-all-start.1
  41.6 20.8 %collective-permute-done.1 = bf16[64,3584]{1,0:T(8,128)(2,1)S(1)} collective-permute-done((bf16[64,3584]{1,0:T(8,128)(2,1)}, bf16[64,3584]{1,0:T(8,128)(2,1)S(1)}, u32[]{:S(2)}, u32[]{:S(2)}) %collective-permute-start.1) | collective-permute-done | bytes 458784 | tf_op jit(solution)/shard_map/ppermute | solution.py:268
  62.4 17.5 %collective-permute-done.3 = bf16[64,3584]{1,0:T(8,128)(2,1)S(1)} collective-permute-done((bf16[64,3584]{1,0:T(8,128)(2,1)S(1)}, bf16[64,3584]{1,0:T(8,128)(2,1)S(1)}, u32[]{:S(2)}, u32[]{:S(2)}) %collective-permute-start.3) | collective-permute-done | bytes 458784 | tf_op jit(solution)/shard_map/ppermute | solution.py:268
  80.7 3.2 convolution_convert_fusion
  83.9 4.6 %all-to-all-start.2 = ((bf16[4,48,3584]{2,1,0:T(8,128)(2,1)}), bf16[4,48,3584]{2,1,0:T(8,128)(2,1)}, u32[]{:S(2)}, u32[]{:S(2)}) async-start(bf16[4,48,3584]{2,1,0:T(8,128)(2,1)} %bitcast.95), calls=%async_computation.2 | async-start | bytes 2752512 | tf_op jit(solution)/shard_map/all_to_all | solution.py:286
  90.3 2.9 collective-permute-start.5
  93.2 11.0 %shard_map.110 = (f32[2,384,256]{2,1,0:T(8,128)}, f32[2,384,256]{2,1,0:T(8,128)}, bf16[2,384,256]{2,1,0:T(8,128)(2,1)}, bf16[192,3584]{1,0:T(8,128)(2,1)}, bf16[192,3584]{1,0:T(8,128)(2,1)}) custom-call(bf16[192,3584]{1,0:T(8,128)(2,1)} %bitcast.90, bf16[192,3584]{1,0:T(8,128)(2,1)} %collective-permute-done.4.b_ref.refs_5_, bf16[3584,512]{1,0:T(8,128)(2,1)} %bitcast.68, ...), custom_call_target="tpu_custom_call" | custom-call | flops 1 | bytes 1 | tf_op jit(solution)/shard_map/pallas_call | solution.py:101
  104.1 10.5 %collective-permute-done.2 = bf16[64,3584]{1,0:T(8,128)(2,1)S(1)} collective-permute-done((bf16[64,3584]{1,0:T(8,128)(2,1)}, bf16[64,3584]{1,0:T(8,128)(2,1)S(1)}, u32[]{:S(2)}, u32[]{:S(2)}) %collective-permute-start.2) | collective-permute-done | bytes 458784 | tf_op jit(solution)/shard_map/ppermute | solution.py:268
  114.6 18.8 %collective-permute-done.5 = bf16[64,3584]{1,0:T(8,128)(2,1)S(1)} collective-permute-done((bf16[64,3584]{1,0:T(8,128)(2,1)S(1)}, bf16[64,3584]{1,0:T(8,128)(2,1)S(1)}, u32[]{:S(2)}, u32[]{:S(2)}) %collective-permute-start.5) | collective-permute-done | bytes 458784 | tf_op jit(solution)/shard_map/ppermute | solution.py:268
  136.2 11.3 %shard_map.111 = (bf16[2,384,512]{2,1,0:T(8,128)(2,1)}, bf16[192,3584]{1,0:T(8,128)(2,1)}, bf16[192,3584]{1,0:T(8,128)(2,1)}) custom-call(bf16[192,3584]{1,0:T(8,128)(2,1)} %bitcast.81, bf16[192,3584]{1,0:T(8,128)(2,1)} %copy-done.2, f32[2,384,256]{2,1,0:T(8,128)} %get-tuple-element.69.pre_gate_ref, f32[2,384,256]{2,1,0:T(8,128)} %get-tuple-element.70.pre_up_ref, ...), custom_call_target="tpu_custom_call" | custom-call | flops 1 | bytes 1 | tf_op jit(solution)/shard_map/pallas_call | solution.py:155
  148.1 4.0 %collective-permute-done.8.b_ref.refs_7_ = bf16[192,3584]{1,0:T(8,128)(2,1)S(1)} collective-permute-done((bf16[192,3584]{1,0:T(8,128)(2,1)}, bf16[192,3584]{1,0:T(8,128)(2,1)S(1)}, u32[]{:S(2)}, u32[]{:S(2)}) %collective-permute-start.8) | collective-permute-done | bytes 1376288 | tf_op jit(solution)/shard_map/ppermute | solution.py:268
  153.3 11.0 %shard_map.112 = (f32[2,384,256]{2,1,0:T(8,128)}, f32[2,384,256]{2,1,0:T(8,128)}, bf16[2,384,256]{2,1,0:T(8,128)(2,1)}, bf16[192,3584]{1,0:T(8,128)(2,1)}, bf16[192,3584]{1,0:T(8,128)(2,1)}) custom-call(bf16[192,3584]{1,0:T(8,128)(2,1)} %bitcast.17.a_ref.refs_6_, bf16[192,3584]{1,0:T(8,128)(2,1)} %copy-done.5, bf16[3584,512]{1,0:T(8,128)(2,1)} %bitcast.70, ...), custom_call_target="tpu_custom_call" | custom-call | flops 1 | bytes 1 | tf_op jit(solution)/shard_map/pallas_call | solution.py:101
  164.4 3.9 %all-to-all-start.3 = ((bf16[4,48,3584]{2,1,0:T(8,128)(2,1)}), bf16[4,48,3584]{2,1,0:T(8,128)(2,1)S(1)}, u32[]{:S(2)}, u32[]{:S(2)}) async-start(bf16[4,48,3584]{2,1,0:T(8,128)(2,1)} %bitcast.21), calls=%async_computation.3 | async-start | bytes 2752512 | tf_op jit(solution)/shard_map/all_to_all | solution.py:286
  171.2 2.9 add_convert_fusion.3
  174.1 12.3 %all-to-all-done.3 = bf16[4,48,3584]{2,1,0:T(8,128)(2,1)S(1)} async-done(((bf16[4,48,3584]{2,1,0:T(8,128)(2,1)}), bf16[4,48,3584]{2,1,0:T(8,128)(2,1)S(1)}, u32[]{:S(2)}, u32[]{:S(2)}) %all-to-all-start.3) | async-done | bytes 1376288 | tf_op jit(solution)/shard_map/all_to_all | solution.py:286
  186.9 4.5 %collective-permute-done.11.b_ref.refs_5_ = bf16[192,3584]{1,0:T(8,128)(2,1)S(1)} collective-permute-done((bf16[192,3584]{1,0:T(8,128)(2,1)S(1)}, bf16[192,3584]{1,0:T(8,128)(2,1)S(1)}, u32[]{:S(2)}, u32[]{:S(2)}) %collective-permute-start.11) | collective-permute-done | bytes 1376288 | tf_op jit(solution)/shard_map/ppermute | solution.py:268
  192.5 11.3 %shard_map.113 = (bf16[2,384,512]{2,1,0:T(8,128)(2,1)}, bf16[192,3584]{1,0:T(8,128)(2,1)}, bf16[192,3584]{1,0:T(8,128)(2,1)}) custom-call(bf16[192,3584]{1,0:T(8,128)(2,1)} %bitcast.85, bf16[192,3584]{1,0:T(8,128)(2,1)} %copy-done.3, f32[2,384,256]{2,1,0:T(8,128)} %get-tuple-element.81.pre_gate_ref, f32[2,384,256]{2,1,0:T(8,128)} %get-tuple-element.82.pre_up_ref, ...), custom_call_target="tpu_custom_call" | custom-call | flops 1 | bytes 1 | tf_op jit(solution)/shard_map/pallas_call | solution.py:155
  204.6 3.7 all-to-all-start.4
  212.7 2.9 add_convert_fusion.1
  215.6 29.5 %collective-permute-done.16.refs_2_ = bf16[384,512]{1,0:T(8,128)(2,1)S(1)} collective-permute-done((bf16[384,512]{1,0:T(8,128)(2,1)S(1)}, bf16[384,512]{1,0:T(8,128)(2,1)S(1)}, u32[]{:S(2)}, u32[]{:S(2)}) %collective-permute-start.16) | collective-permute-done | bytes 393248 | tf_op jit(solution)/shard_map/ppermute | solution.py:277
  245.9 3.7 all-to-all-start.5
  253.2 7.7 %shard_map.114 = bf16[256,3584]{1,0:T(8,128)(2,1)} custom-call(s32[1]{0:T(128)S(6)} %sub.37.which_ref, bf16[2,384,256]{2,1,0:T(8,128)(2,1)} %get-tuple-element.95.refs_0_, bf16[2,384,256]{2,1,0:T(8,128)(2,1)} %get-tuple-element.96.refs_1_, bf16[192,3584]{1,0:T(8,128)(2,1)} %bitcast.82, bf16[192,3584]{1,0:T(8,128)(2,1)} %copy-done.2, ...), custom_call_target="tpu_custom_call" | custom-call | flops 1 | bytes 1 | tf_op jit(solution)/shard_map/pallas_call | solution.py:190
  261.0 15.5 %all-to-all-done.5 = bf16[4,48,3584]{2,1,0:T(8,128)(2,1)S(1)} async-done(((bf16[4,48,3584]{2,1,0:T(8,128)(2,1)}), bf16[4,48,3584]{2,1,0:T(8,128)(2,1)S(1)}, u32[]{:S(2)}, u32[]{:S(2)}) %all-to-all-start.5) | async-done | bytes 1376288 | tf_op jit(solution)/shard_map/all_to_all | solution.py:286
  277.9 3.7 all-to-all-start.6
  282.7 22.9 %collective-permute-done.20 = bf16[64,3584]{1,0:T(8,128)(2,1)S(1)} collective-permute-done((bf16[64,3584]{1,0:T(8,128)(2,1)}, bf16[64,3584]{1,0:T(8,128)(2,1)S(1)}, u32[]{:S(2)}, u32[]{:S(2)}) %collective-permute-start.20) | collective-permute-done | bytes 458784 | tf_op jit(solution)/shard_map/ppermute | solution.py:268
  307.6 3.5 all-to-all-start.7
  315.2 37.2 %collective-permute-done.23.refs_6_ = bf16[256,3584]{1,0:T(8,128)(2,1)S(1)} collective-permute-done((bf16[256,3584]{1,0:T(8,128)(2,1)}, bf16[256,3584]{1,0:T(8,128)(2,1)S(1)}, u32[]{:S(2)}, u32[]{:S(2)}) %collective-permute-start.23) | collective-permute-done | bytes 1835040 | tf_op jit(solution)/shard_map/ppermute | solution.py:277
  353.6 8.1 %shard_map.116 = bf16[256,3584]{1,0:T(8,128)(2,1)} custom-call(s32[1]{0:T(128)} %bitcast.28.which_ref, bf16[2,384,256]{2,1,0:T(8,128)(2,1)} %get-tuple-element.95.refs_0_, bf16[2,384,256]{2,1,0:T(8,128)(2,1)} %get-tuple-element.96.refs_1_, bf16[192,3584]{1,0:T(8,128)(2,1)} %bitcast.83, bf16[192,3584]{1,0:T(8,128)(2,1)} %copy-done.2, ...), custom_call_target="tpu_custom_call" | custom-call | flops 1 | bytes 1 | tf_op jit(solution)/shard_map/pallas_call | solution.py:190
  361.7 12.3 %shard_map.115 = (bf16[3584,256]{1,0:T(8,128)(2,1)}, bf16[3584,256]{1,0:T(8,128)(2,1)}) custom-call(s32[1]{0:T(128)} %bitcast.28.which_ref, bf16[2,384,512]{2,1,0:T(8,128)(2,1)} %get-tuple-element.89.refs_0_, bf16[2,384,512]{2,1,0:T(8,128)(2,1)} %get-tuple-element.97.refs_1_, bf16[384,512]{1,0:T(8,128)(2,1)} %copy-done.22, ...), custom_call_target="tpu_custom_call" | custom-call | flops 1 | bytes 1 | tf_op jit(solution)/shard_map/pallas_call | solution.py:224
  (133 shorter events, 50.1 us)
Async XLA Ops:
  2.0 7.1 %collective-permute-start = (f32[128,4]{0,1:T(4,128)S(1)}, f32[128,4]{0,1:T(4,128)S(1)}, u32[]{:S(2)}, u32[]{:S(2)}) collective-permute-start(f32[128,4]{0,1:T(4,128)S(1)} %pad_maximum_fusion), channel_id=1, source_target_pairs={{0,8},{1,9},{2,10},{3,11},{4,12},{5,13},{6,14},{7,15},{8,0},{9,1},... | collective-permute-start | bytes 6152 | tf_op jit(solution)/shard_map/ppermute | solution.py:268
  11.9 20.8 %all-to-all-start = ((bf16[4,48,3584]{2,1,0:T(8,128)(2,1)}), bf16[4,48,3584]{2,1,0:T(8,128)(2,1)S(1)}, u32[]{:S(2)}, u32[]{:S(2)}) async-start(bf16[4,48,3584]{2,1,0:T(8,128)(2,1)} %bitcast.11), calls=%async_computation | async-start | bytes 2752512 | tf_op jit(solution)/shard_map/all_to_all | solution.py:286
  32.7 48.0 %all-to-all-start.1 = ((bf16[4,48,3584]{2,1,0:T(8,128)(2,1)}), bf16[4,48,3584]{2,1,0:T(8,128)(2,1)S(1)}, u32[]{:S(2)}, u32[]{:S(2)}) async-start(bf16[4,48,3584]{2,1,0:T(8,128)(2,1)} %bitcast.97), calls=%async_computation.1 | async-start | bytes 2752512 | tf_op jit(solution)/shard_map/all_to_all | solution.py:286
  36.3 44.4 %collective-permute-start.4 = (bf16[192,3584]{1,0:T(8,128)(2,1)S(1)}, bf16[192,3584]{1,0:T(8,128)(2,1)}, u32[]{:S(2)}, u32[]{:S(2)}) collective-permute-start(bf16[192,3584]{1,0:T(8,128)(2,1)S(1)} %bitcast.88), channel_id=1, source_target_pairs={{0,1},{1,0},{2,3},{3,2},{4,5},{5,4},{6,7},{7,6},{8,9},{9,8},{10,11... | collective-permute-start | bytes 4128776 | tf_op jit(solution)/shard_map/ppermute | solution.py:268
  36.3 26.0 %collective-permute-start.1 = (bf16[64,3584]{1,0:T(8,128)(2,1)}, bf16[64,3584]{1,0:T(8,128)(2,1)S(1)}, u32[]{:S(2)}, u32[]{:S(2)}) collective-permute-start(bf16[64,3584]{1,0:T(8,128)(2,1)} %get-tuple-element.125), channel_id=1, source_target_pairs={{0,8},{1,9},{2,10},{3,11},{4,12},{5,13},{6,14},{7,15},{8,0},{9,1},... | collective-permute-start | bytes 1376264 | tf_op jit(solution)/shard_map/ppermute | solution.py:268
  37.0 42.9 %collective-permute-start.3 = (bf16[64,3584]{1,0:T(8,128)(2,1)S(1)}, bf16[64,3584]{1,0:T(8,128)(2,1)S(1)}, u32[]{:S(2)}, u32[]{:S(2)}) collective-permute-start(bf16[64,3584]{1,0:T(8,128)(2,1)S(1)} %get-tuple-element.61), channel_id=1, source_target_pairs={{0,8},{1,9},{2,10},{3,11},{4,12},{5,13},{6,14},{7,15},{8,0},{9,1},... | collective-permute-start | bytes 1376264 | tf_op jit(solution)/shard_map/ppermute | solution.py:268
  83.9 63.6 %all-to-all-start.2 = ((bf16[4,48,3584]{2,1,0:T(8,128)(2,1)}), bf16[4,48,3584]{2,1,0:T(8,128)(2,1)}, u32[]{:S(2)}, u32[]{:S(2)}) async-start(bf16[4,48,3584]{2,1,0:T(8,128)(2,1)} %bitcast.95), calls=%async_computation.2 | async-start | bytes 2752512 | tf_op jit(solution)/shard_map/all_to_all | solution.py:286
  88.6 46.5 %collective-permute-start.6 = (bf16[192,3584]{1,0:T(8,128)(2,1)S(1)}, bf16[192,3584]{1,0:T(8,128)(2,1)S(1)}, u32[]{:S(2)}, u32[]{:S(2)}) collective-permute-start(bf16[192,3584]{1,0:T(8,128)(2,1)S(1)} %bitcast.80), channel_id=1, source_target_pairs={{0,1},{1,0},{2,3},{3,2},{4,5},{5,4},{6,7},{7,6},{8,9},{9,8},{10,11... | collective-permute-start | bytes 4128776 | tf_op jit(solution)/shard_map/ppermute | solution.py:268
  88.7 58.8 %collective-permute-start.7 = (bf16[192,3584]{1,0:T(8,128)(2,1)S(1)}, bf16[192,3584]{1,0:T(8,128)(2,1)}, u32[]{:S(2)}, u32[]{:S(2)}) collective-permute-start(bf16[192,3584]{1,0:T(8,128)(2,1)S(1)} %bitcast.89), channel_id=1, source_target_pairs={{0,16},{16,0},{1,17},{17,1},{2,18},{18,2},{3,19},{19,3},{4,20},{20... | collective-permute-start | bytes 4128776 | tf_op jit(solution)/shard_map/ppermute | solution.py:277
  90.2 24.4 %collective-permute-start.2 = (bf16[64,3584]{1,0:T(8,128)(2,1)}, bf16[64,3584]{1,0:T(8,128)(2,1)S(1)}, u32[]{:S(2)}, u32[]{:S(2)}) collective-permute-start(bf16[64,3584]{1,0:T(8,128)(2,1)} %get-tuple-element.60), channel_id=1, source_target_pairs={{0,8},{1,9},{2,10},{3,11},{4,12},{5,13},{6,14},{7,15},{8,0},{9,1},... | collective-permute-start | bytes 1376264 | tf_op jit(solution)/shard_map/ppermute | solution.py:268
  90.3 43.2 %collective-permute-start.5 = (bf16[64,3584]{1,0:T(8,128)(2,1)S(1)}, bf16[64,3584]{1,0:T(8,128)(2,1)S(1)}, u32[]{:S(2)}, u32[]{:S(2)}) collective-permute-start(bf16[64,3584]{1,0:T(8,128)(2,1)S(1)} %copy-done.19), channel_id=1, source_target_pairs={{0,8},{1,9},{2,10},{3,11},{4,12},{5,13},{6,14},{7,15},{8,0},{9,1},... | collective-permute-start | bytes 1376264 | tf_op jit(solution)/shard_map/ppermute | solution.py:268
  147.5 4.6 %collective-permute-start.8 = (bf16[192,3584]{1,0:T(8,128)(2,1)}, bf16[192,3584]{1,0:T(8,128)(2,1)S(1)}, u32[]{:S(2)}, u32[]{:S(2)}) collective-permute-start(bf16[192,3584]{1,0:T(8,128)(2,1)} %bitcast.17.a_ref.refs_6_), channel_id=1, source_target_pairs={{0,1},{1,0},{2,3},{3,2},{4,5},{5,4},{6,7},{7,6},{8,9},{9,8},{10,11... | collective-permute-start | bytes 4128776 | tf_op jit(solution)/shard_map/ppermute | solution.py:268
  147.6 20.8 %collective-permute-start.10 = (bf16[192,3584]{1,0:T(8,128)(2,1)}, bf16[192,3584]{1,0:T(8,128)(2,1)}, u32[]{:S(2)}, u32[]{:S(2)}) collective-permute-start(bf16[192,3584]{1,0:T(8,128)(2,1)} %get-tuple-element.79), channel_id=1, source_target_pairs={{0,1},{1,0},{2,3},{3,2},{4,5},{5,4},{6,7},{7,6},{8,9},{9,8},{10,11... | collective-permute-start | bytes 4128776 | tf_op jit(solution)/shard_map/ppermute | solution.py:268
  164.2 7.0 %collective-permute-start.9 = (bf16[192,3584]{1,0:T(8,128)(2,1)}, bf16[192,3584]{1,0:T(8,128)(2,1)}, u32[]{:S(2)}, u32[]{:S(2)}) collective-permute-start(bf16[192,3584]{1,0:T(8,128)(2,1)} %get-tuple-element.76), channel_id=1, source_target_pairs={{0,1},{1,0},{2,3},{3,2},{4,5},{5,4},{6,7},{7,6},{8,9},{9,8},{10,11... | collective-permute-start | bytes 4128776 | tf_op jit(solution)/shard_map/ppermute | solution.py:268
  164.4 22.0 %all-to-all-start.3 = ((bf16[4,48,3584]{2,1,0:T(8,128)(2,1)}), bf16[4,48,3584]{2,1,0:T(8,128)(2,1)S(1)}, u32[]{:S(2)}, u32[]{:S(2)}) async-start(bf16[4,48,3584]{2,1,0:T(8,128)(2,1)} %bitcast.21), calls=%async_computation.3 | async-start | bytes 2752512 | tf_op jit(solution)/shard_map/all_to_all | solution.py:286
  186.4 5.1 %collective-permute-start.11 = (bf16[192,3584]{1,0:T(8,128)(2,1)S(1)}, bf16[192,3584]{1,0:T(8,128)(2,1)S(1)}, u32[]{:S(2)}, u32[]{:S(2)}) collective-permute-start(bf16[192,3584]{1,0:T(8,128)(2,1)S(1)} %bitcast.84), channel_id=1, source_target_pairs={{0,1},{1,0},{2,3},{3,2},{4,5},{5,4},{6,7},{7,6},{8,9},{9,8},{10,11... | collective-permute-start | bytes 4128776 | tf_op jit(solution)/shard_map/ppermute | solution.py:268
  186.4 23.5 %collective-permute-start.13 = (bf16[192,3584]{1,0:T(8,128)(2,1)}, bf16[192,3584]{1,0:T(8,128)(2,1)}, u32[]{:S(2)}, u32[]{:S(2)}) collective-permute-start(bf16[192,3584]{1,0:T(8,128)(2,1)} %get-tuple-element.87), channel_id=1, source_target_pairs={{0,1},{1,0},{2,3},{3,2},{4,5},{5,4},{6,7},{7,6},{8,9},{9,8},{10,11... | collective-permute-start | bytes 4128776 | tf_op jit(solution)/shard_map/ppermute | solution.py:268
  203.8 8.9 %collective-permute-start.12 = (bf16[192,3584]{1,0:T(8,128)(2,1)}, bf16[192,3584]{1,0:T(8,128)(2,1)}, u32[]{:S(2)}, u32[]{:S(2)}) collective-permute-start(bf16[192,3584]{1,0:T(8,128)(2,1)} %get-tuple-element.84), channel_id=1, source_target_pairs={{0,1},{1,0},{2,3},{3,2},{4,5},{5,4},{6,7},{7,6},{8,9},{9,8},{10,11... | collective-permute-start | bytes 4128776 | tf_op jit(solution)/shard_map/ppermute | solution.py:268
  204.0 41.8 %collective-permute-start.15 = (bf16[192,3584]{1,0:T(8,128)(2,1)}, bf16[192,3584]{1,0:T(8,128)(2,1)}, u32[]{:S(2)}, u32[]{:S(2)}) collective-permute-start(bf16[192,3584]{1,0:T(8,128)(2,1)} %bitcast.17.a_ref.refs_6_), channel_id=1, source_target_pairs={{0,16},{16,0},{1,17},{17,1},{2,18},{18,2},{3,19},{19,3},{4,20},{20... | collective-permute-start | bytes 4128776 | tf_op jit(solution)/shard_map/ppermute | solution.py:277
  204.6 40.5 %collective-permute-start.14 = (bf16[192,3584]{1,0:T(8,128)(2,1)}, bf16[192,3584]{1,0:T(8,128)(2,1)}, u32[]{:S(2)}, u32[]{:S(2)}) collective-permute-start(bf16[192,3584]{1,0:T(8,128)(2,1)} %collective-permute-done.7.refs_8_), channel_id=1, source_target_pairs={{0,1},{1,0},{2,3},{3,2},{4,5},{5,4},{6,7},{7,6},{8,9},{9,8},{10,11... | collective-permute-start | bytes 4128776 | tf_op jit(solution)/shard_map/ppermute | solution.py:268
  204.6 41.2 %all-to-all-start.4 = ((bf16[4,48,3584]{2,1,0:T(8,128)(2,1)}), bf16[4,48,3584]{2,1,0:T(8,128)(2,1)S(1)}, u32[]{:S(2)}, u32[]{:S(2)}) async-start(bf16[4,48,3584]{2,1,0:T(8,128)(2,1)} %bitcast.23), calls=%async_computation.4 | async-start | bytes 2752512 | tf_op jit(solution)/shard_map/all_to_all | solution.py:286
  208.4 36.7 %collective-permute-start.16 = (bf16[384,512]{1,0:T(8,128)(2,1)S(1)}, bf16[384,512]{1,0:T(8,128)(2,1)S(1)}, u32[]{:S(2)}, u32[]{:S(2)}) collective-permute-start(bf16[384,512]{1,0:T(8,128)(2,1)S(1)} %dynamic-slice_bitcast_fusion.1), channel_id=1, source_target_pairs={{0,16},{16,0},{1,17},{17,1},{2,18},{18,2},{3,19},{19,3},{4,20},{20... | collective-permute-start | bytes 1179656 | tf_op jit(solution)/shard_map/ppermute | solution.py:277
  245.9 30.6 %all-to-all-start.5 = ((bf16[4,48,3584]{2,1,0:T(8,128)(2,1)}), bf16[4,48,3584]{2,1,0:T(8,128)(2,1)S(1)}, u32[]{:S(2)}, u32[]{:S(2)}) async-start(bf16[4,48,3584]{2,1,0:T(8,128)(2,1)} %bitcast.26), calls=%async_computation.5 | async-start | bytes 2752512 | tf_op jit(solution)/shard_map/all_to_all | solution.py:286
  250.2 10.7 %collective-permute-start.19 = (bf16[384,512]{1,0:T(8,128)(2,1)S(1)}, bf16[384,512]{1,0:T(8,128)(2,1)}, u32[]{:S(2)}, u32[]{:S(2)}) collective-permute-start(bf16[384,512]{1,0:T(8,128)(2,1)S(1)} %dynamic-slice_bitcast_fusion), channel_id=1, source_target_pairs={{0,16},{16,0},{1,17},{17,1},{2,18},{18,2},{3,19},{19,3},{4,20},{20... | collective-permute-start | bytes 1179656 | tf_op jit(solution)/shard_map/ppermute | solution.py:277
  250.8 27.0 %collective-permute-start.18 = (bf16[192,3584]{1,0:T(8,128)(2,1)}, bf16[192,3584]{1,0:T(8,128)(2,1)}, u32[]{:S(2)}, u32[]{:S(2)}) collective-permute-start(bf16[192,3584]{1,0:T(8,128)(2,1)} %collective-permute-done.15.refs_10_), channel_id=1, source_target_pairs={{0,1},{1,0},{2,3},{3,2},{4,5},{5,4},{6,7},{7,6},{8,9},{9,8},{10,11... | collective-permute-start | bytes 4128776 | tf_op jit(solution)/shard_map/ppermute | solution.py:268
  252.6 25.2 %collective-permute-start.17 = (bf16[64,3584]{1,0:T(8,128)(2,1)S(1)}, bf16[64,3584]{1,0:T(8,128)(2,1)S(1)}, u32[]{:S(2)}, u32[]{:S(2)}) collective-permute-start(bf16[64,3584]{1,0:T(8,128)(2,1)S(1)} %get-tuple-element.124), channel_id=1, source_target_pairs={{0,8},{1,9},{2,10},{3,11},{4,12},{5,13},{6,14},{7,15},{8,0},{9,1},... | collective-permute-start | bytes 1376264 | tf_op jit(solution)/shard_map/ppermute | solution.py:268
  277.9 29.8 %all-to-all-start.6 = ((bf16[4,48,3584]{2,1,0:T(8,128)(2,1)}), bf16[4,48,3584]{2,1,0:T(8,128)(2,1)S(1)}, u32[]{:S(2)}, u32[]{:S(2)}) async-start(bf16[4,48,3584]{2,1,0:T(8,128)(2,1)} %bitcast.30), calls=%async_computation.6 | async-start | bytes 2752512 | tf_op jit(solution)/shard_map/all_to_all | solution.py:286
  281.6 24.0 %collective-permute-start.20 = (bf16[64,3584]{1,0:T(8,128)(2,1)}, bf16[64,3584]{1,0:T(8,128)(2,1)S(1)}, u32[]{:S(2)}, u32[]{:S(2)}) collective-permute-start(bf16[64,3584]{1,0:T(8,128)(2,1)} %get-tuple-element.123), channel_id=1, source_target_pairs={{0,8},{1,9},{2,10},{3,11},{4,12},{5,13},{6,14},{7,15},{8,0},{9,1},... | collective-permute-start | bytes 1376264 | tf_op jit(solution)/shard_map/ppermute | solution.py:268
  307.6 69.1 %all-to-all-start.7 = ((bf16[4,48,3584]{2,1,0:T(8,128)(2,1)}), bf16[4,48,3584]{2,1,0:T(8,128)(2,1)S(1)}, u32[]{:S(2)}, u32[]{:S(2)}) async-start(bf16[4,48,3584]{2,1,0:T(8,128)(2,1)} %bitcast.33), calls=%async_computation.7 | async-start | bytes 2752512 | tf_op jit(solution)/shard_map/all_to_all | solution.py:286
  311.2 41.2 %collective-permute-start.23 = (bf16[256,3584]{1,0:T(8,128)(2,1)}, bf16[256,3584]{1,0:T(8,128)(2,1)S(1)}, u32[]{:S(2)}, u32[]{:S(2)}) collective-permute-start(bf16[256,3584]{1,0:T(8,128)(2,1)} %shard_map.114), channel_id=1, source_target_pairs={{0,16},{16,0},{1,17},{17,1},{2,18},{18,2},{3,19},{19,3},{4,20},{20... | collective-permute-start | bytes 5505032 | tf_op jit(solution)/shard_map/ppermute | solution.py:277
  312.2 63.7 %collective-permute-start.22 = (bf16[64,3584]{1,0:T(8,128)(2,1)}, bf16[64,3584]{1,0:T(8,128)(2,1)S(1)}, u32[]{:S(2)}, u32[]{:S(2)}) collective-permute-start(bf16[64,3584]{1,0:T(8,128)(2,1)} %get-tuple-element.106), channel_id=1, source_target_pairs={{0,8},{1,9},{2,10},{3,11},{4,12},{5,13},{6,14},{7,15},{8,0},{9,1},... | collective-permute-start | bytes 1376264 | tf_op jit(solution)/shard_map/ppermute | solution.py:268
  314.2 62.5 %collective-permute-start.21 = (bf16[64,3584]{1,0:T(8,128)(2,1)}, bf16[64,3584]{1,0:T(8,128)(2,1)}, u32[]{:S(2)}, u32[]{:S(2)}) collective-permute-start(bf16[64,3584]{1,0:T(8,128)(2,1)} %get-tuple-element.121), channel_id=1, source_target_pairs={{0,8},{1,9},{2,10},{3,11},{4,12},{5,13},{6,14},{7,15},{8,0},{9,1},... | collective-permute-start | bytes 1376264 | tf_op jit(solution)/shard_map/ppermute | solution.py:268
  (26 other events, 194.1 us)

commit v7 on v2

--- a/solution.py
+++ b/solution.py
@@ -127,10 +127,12 @@
     keep_gate, send_gate = halves(joined(gate_grads))
     keep_up, send_up = halves(joined(up_grads))
     rows_dims = ((0,), (0,))
-    sent = [
-        lax.ppermute(dot(a, b, rows_dims).astype(BF16), "pipe", mirror)
-        for a, b in ((send_hidden, all_grad), (all_in, send_gate), (all_in, send_up))
-    ]
+    sent = []
+    for a, b in ((send_hidden, all_grad), (all_in, send_gate), (all_in, send_up)):
+        local = dot(a, b, rows_dims).astype(BF16)
+        if sent:
+            local, sent[-1] = lax.optimization_barrier((local, sent[-1]))
+        sent.append(lax.ppermute(local, "pipe", mirror))
     kept = [
         dot(a, b, rows_dims).astype(BF16)
         for a, b in ((keep_hidden, all_grad), (all_in, keep_gate), (all_in, keep_up))

time: 344 us -> 379 us (1.10)
  waiting for transfers between devices: 84.4 us -> 137 us
  matrix products: 69.6 us -> 54.4 us
  local copies, waits for them, and re-layouts: 33.8 us -> 43.8 us
  starting transfers between devices: 147 us -> 137 us
    ppermute x3, waiting for transfers between devices: 6.45 us -> 63.4 us  [on_device(): sent.append(lax.ppermute(local, 'pipe', mirror))]
    dot_general x36, matrix products: 67.9 us -> 52.7 us  [dot(): return lax.dot_general(a, b, (dims, ((), ())), preferred_element_type=F32)]
    unnamed x94 -> x100, local copies, waits for them, and re-layouts: 29.5 us -> 39.4 us
    ppermute x56, starting transfers between devices: 141 us -> 133 us  [across(): lax.ppermute(piece, 'expert', [(i, i ^ 2 * d) for i in range(devices)])]
    ppermute x56, waiting for transfers between devices: 77.5 us -> 73.7 us  [across(): lax.ppermute(piece, 'expert', [(i, i ^ 2 * d) for i in range(devices)])]
  transfers between devices with their start and end apart: 67 -> 67, of which waited for: 24 -> 17; matrix products, arithmetic and copies ran while one was open for 28% -> 24% of each run, Pallas kernels for 0% -> 0%
where the time goes in v7:
time: 379 us; the launch traced here: 378 us
  starting transfers between devices  137 us (36%)
  waiting for transfers between devices  137 us (36%)
  matrix products  54.4 us (14%)
  local copies, waits for them, and re-layouts  43.8 us (12%)
  other arithmetic  3.97 us (1%)
    ppermute x56, starting transfers between devices, across(): lax.ppermute(piece, 'expert', [(i, i ^ 2 * d) for i in range(devices)])  133 us
    ppermute x56, waiting for transfers between devices, across(): lax.ppermute(piece, 'expert', [(i, i ^ 2 * d) for i in range(devices)])  73.7 us
    ppermute x3, waiting for transfers between devices, on_device(): sent.append(lax.ppermute(local, 'pipe', mirror))  63.4 us
    dot_general x36, matrix products, dot(): return lax.dot_general(a, b, (dims, ((), ())), preferred_element_type=F32)  52.7 us
    unnamed x100, local copies, waits for them, and re-layouts  39.4 us
  transfers between devices with their start and end apart: 67, of which 17 were waited for; matrix products, arithmetic and copies ran while one was open for 24% of the time, Pallas kernels for 0%

profile of v7, /device:TPU:0, one launch (start us, length us, event | category | flops | bytes accessed | tf_op | source)
XLA Modules:
  0.0 378.3 jit_solution(15105843636923033897)
XLA Ops:
  12.4 3.0 collective-permute-start.35
  21.6 3.6 collective-permute-start.37
  31.2 4.7 %collective-permute-start.1 = (bf16[24,3584]{1,0:T(8,128)(2,1)S(1)}, bf16[24,3584]{1,0:T(8,128)(2,1)S(1)}, u32[]{:S(2)}, u32[]{:S(2)}) collective-permute-start(bf16[24,3584]{1,0:T(8,128)(2,1)S(1)} %copy-done.9), channel_id=1, source_target_pairs={{0,4},{1,5},{2,6},{3,7},{4,0},{5,1},{6,2},{7,3},{8,12},{9,13},{10,... | collective-permute-start | bytes 516104 | tf_op jit(solution)/shard_map/ppermute | solution.py:44
  36.6 3.7 collective-permute-done.36
  42.3 4.4 %collective-permute-start.3 = (bf16[24,3584]{1,0:T(8,128)(2,1)S(1)}, bf16[24,3584]{1,0:T(8,128)(2,1)S(1)}, u32[]{:S(2)}, u32[]{:S(2)}) collective-permute-start(bf16[24,3584]{1,0:T(8,128)(2,1)S(1)} %copy-done.7), channel_id=1, source_target_pairs={{0,8},{1,9},{2,10},{3,11},{4,12},{5,13},{6,14},{7,15},{8,0},{9,1},... | collective-permute-start | bytes 516104 | tf_op jit(solution)/shard_map/ppermute | solution.py:44
  47.5 12.4 %collective-permute-start.4 = (bf16[24,3584]{1,0:T(8,128)(2,1)S(1)}, bf16[24,3584]{1,0:T(8,128)(2,1)S(1)}, u32[]{:S(2)}, u32[]{:S(2)}) collective-permute-start(bf16[24,3584]{1,0:T(8,128)(2,1)S(1)} %copy-done.6), channel_id=1, source_target_pairs={{0,10},{1,11},{2,8},{3,9},{4,14},{5,15},{6,12},{7,13},{8,2},{9,3},... | collective-permute-start | bytes 516104 | tf_op jit(solution)/shard_map/ppermute | solution.py:44
  61.8 4.3 %collective-permute-start.6 = (bf16[24,3584]{1,0:T(8,128)(2,1)S(1)}, bf16[24,3584]{1,0:T(8,128)(2,1)S(1)}, u32[]{:S(2)}, u32[]{:S(2)}) collective-permute-start(bf16[24,3584]{1,0:T(8,128)(2,1)S(1)} %copy-done.4), channel_id=1, source_target_pairs={{0,14},{1,15},{2,12},{3,13},{4,10},{5,11},{6,8},{7,9},{8,6},{9,7},... | collective-permute-start | bytes 516104 | tf_op jit(solution)/shard_map/ppermute | solution.py:44
  82.2 3.5 collective-permute-start.49
  86.2 4.1 %collective-permute-start.51 = (bf16[24,3584]{1,0:T(8,128)(2,1)S(1)}, bf16[24,3584]{1,0:T(8,128)(2,1)S(1)}, u32[]{:S(2)}, u32[]{:S(2)}) collective-permute-start(bf16[24,3584]{1,0:T(8,128)(2,1)S(1)} %get-tuple-element.23), channel_id=1, source_target_pairs={{0,8},{1,9},{2,10},{3,11},{4,12},{5,13},{6,14},{7,15},{8,0},{9,1},... | collective-permute-start | bytes 516104 | tf_op jit(solution)/shard_map/ppermute | solution.py:44
  107.4 6.3 %collective-permute-done.16 = bf16[24,3584]{1,0:T(8,128)(2,1)S(1)} collective-permute-done((bf16[24,3584]{1,0:T(8,128)(2,1)S(1)}, bf16[24,3584]{1,0:T(8,128)(2,1)S(1)}, u32[]{:S(2)}, u32[]{:S(2)}) %collective-permute-start.16) | collective-permute-done | bytes 172064 | tf_op jit(solution)/shard_map/ppermute | solution.py:44
  123.3 8.6 %collective-permute-done.19 = bf16[24,3584]{1,0:T(8,128)(2,1)S(1)} collective-permute-done((bf16[24,3584]{1,0:T(8,128)(2,1)S(1)}, bf16[24,3584]{1,0:T(8,128)(2,1)S(1)}, u32[]{:S(2)}, u32[]{:S(2)}) %collective-permute-start.19) | collective-permute-done | bytes 172064 | tf_op jit(solution)/shard_map/ppermute | solution.py:44
  134.6 7.0 %collective-permute-start.22 = (bf16[24,3584]{1,0:T(8,128)(2,1)S(1)}, bf16[24,3584]{1,0:T(8,128)(2,1)S(1)}, u32[]{:S(2)}, u32[]{:S(2)}) collective-permute-start(bf16[24,3584]{1,0:T(8,128)(2,1)S(1)} %get-tuple-element.38), channel_id=1, source_target_pairs={{0,14},{1,15},{2,12},{3,13},{4,10},{5,11},{6,8},{7,9},{8,6},{9,7},... | collective-permute-start | bytes 516104 | tf_op jit(solution)/shard_map/ppermute | solution.py:44
  155.8 5.8 %collective-permute-start.41 = (bf16[24,3584]{1,0:T(8,128)(2,1)S(1)}, bf16[24,3584]{1,0:T(8,128)(2,1)S(1)}, u32[]{:S(2)}, u32[]{:S(2)}) collective-permute-start(bf16[24,3584]{1,0:T(8,128)(2,1)S(1)} %get-tuple-element.61), channel_id=1, source_target_pairs={{0,2},{1,3},{2,0},{3,1},{4,6},{5,7},{6,4},{7,5},{8,10},{9,11},{10,... | collective-permute-start | bytes 516104 | tf_op jit(solution)/shard_map/ppermute | solution.py:44
  167.3 3.1 collective-permute-start.45
  175.2 3.1 collective-permute-start.47
  180.5 11.8 %collective-permute-done.45 = bf16[24,3584]{1,0:T(8,128)(2,1)S(1)} collective-permute-done((bf16[24,3584]{1,0:T(8,128)(2,1)S(1)}, bf16[24,3584]{1,0:T(8,128)(2,1)S(1)}, u32[]{:S(2)}, u32[]{:S(2)}) %collective-permute-start.45) | collective-permute-done | bytes 172064 | tf_op jit(solution)/shard_map/ppermute | solution.py:44
  192.3 3.1 collective-permute-start.12
  195.5 11.5 %collective-permute-start.13 = (bf16[24,3584]{1,0:T(8,128)(2,1)S(1)}, bf16[24,3584]{1,0:T(8,128)(2,1)S(1)}, u32[]{:S(2)}, u32[]{:S(2)}) collective-permute-start(bf16[24,3584]{1,0:T(8,128)(2,1)S(1)} %get-tuple-element.73), channel_id=1, source_target_pairs={{0,10},{1,11},{2,8},{3,9},{4,14},{5,15},{6,12},{7,13},{8,2},{9,3},... | collective-permute-start | bytes 516104 | tf_op jit(solution)/shard_map/ppermute | solution.py:44
  208.5 5.2 %collective-permute-start.15 = (bf16[24,3584]{1,0:T(8,128)(2,1)S(1)}, bf16[24,3584]{1,0:T(8,128)(2,1)S(1)}, u32[]{:S(2)}, u32[]{:S(2)}) collective-permute-start(bf16[24,3584]{1,0:T(8,128)(2,1)S(1)} %get-tuple-element.71), channel_id=1, source_target_pairs={{0,14},{1,15},{2,12},{3,13},{4,10},{5,11},{6,8},{7,9},{8,6},{9,7},... | collective-permute-start | bytes 516104 | tf_op jit(solution)/shard_map/ppermute | solution.py:44
  216.1 10.0 %constant_dynamic-update-slice_fusion.12 = bf16[192,3584]{1,0:T(8,128)(2,1)S(1)} fusion(bf16[192,3584]{1,0:T(8,128)(2,1)S(1)} %constant_dynamic-update-slice_fusion.13, bf16[24,3584]{1,0:T(8,128)(2,1)S(1)} %collective-permute-done.11), kind=kLoop, calls=%fused_computation.139 | loop fusion | bytes 344064
  229.6 5.8 %convolution_convert_fusion.3 = bf16[3584,256]{1,0:T(8,128)(2,1)} fusion(bf16[768,3584]{1,0:T(8,128)(2,1)} %constant_dynamic-update-slice_fusion.64, bf16[768,512]{1,0:T(8,128)(2,1)S(1)} %pad_maximum_fusion, s32[]{:T(128)S(6)} %select_n.14), kind=kOutput, calls=%fused_computation.15 | convolution fusion | flops 1410203648 | bytes 7733252 | tf_op jit(solution)/shard_map/dot_general | solution.py:14
  245.8 5.5 %collective-permute-done.58 = bf16[24,3584]{1,0:T(8,128)(2,1)S(1)} collective-permute-done((bf16[24,3584]{1,0:T(8,128)(2,1)S(1)}, bf16[24,3584]{1,0:T(8,128)(2,1)S(1)}, u32[]{:S(2)}, u32[]{:S(2)}) %collective-permute-start.58) | collective-permute-done | bytes 172064 | tf_op jit(solution)/shard_map/ppermute | solution.py:44
  252.1 3.8 collective-permute-done.59
  258.8 10.0 %collective-permute-done.61 = bf16[24,3584]{1,0:T(8,128)(2,1)S(1)} collective-permute-done((bf16[24,3584]{1,0:T(8,128)(2,1)S(1)}, bf16[24,3584]{1,0:T(8,128)(2,1)S(1)}, u32[]{:S(2)}, u32[]{:S(2)}) %collective-permute-start.61) | collective-permute-done | bytes 172064 | tf_op jit(solution)/shard_map/ppermute | solution.py:44
  268.8 4.2 %collective-permute-start.27 = (bf16[24,3584]{1,0:T(8,128)(2,1)S(1)}, bf16[24,3584]{1,0:T(8,128)(2,1)S(1)}, u32[]{:S(2)}, u32[]{:S(2)}) collective-permute-start(bf16[24,3584]{1,0:T(8,128)(2,1)S(1)} %get-tuple-element.83), channel_id=1, source_target_pairs={{0,6},{1,7},{2,4},{3,5},{4,2},{5,3},{6,0},{7,1},{8,14},{9,15},{10,... | collective-permute-start | bytes 516104 | tf_op jit(solution)/shard_map/ppermute | solution.py:44
  273.0 3.9 %collective-permute-start.28 = (bf16[24,3584]{1,0:T(8,128)(2,1)S(1)}, bf16[24,3584]{1,0:T(8,128)(2,1)S(1)}, u32[]{:S(2)}, u32[]{:S(2)}) collective-permute-start(bf16[24,3584]{1,0:T(8,128)(2,1)S(1)} %get-tuple-element.82), channel_id=1, source_target_pairs={{0,8},{1,9},{2,10},{3,11},{4,12},{5,13},{6,14},{7,15},{8,0},{9,1},... | collective-permute-start | bytes 516104 | tf_op jit(solution)/shard_map/ppermute | solution.py:44
  280.0 3.4 collective-permute-start.31
  283.5 12.7 %collective-permute-done.28 = bf16[24,3584]{1,0:T(8,128)(2,1)S(1)} collective-permute-done((bf16[24,3584]{1,0:T(8,128)(2,1)S(1)}, bf16[24,3584]{1,0:T(8,128)(2,1)S(1)}, u32[]{:S(2)}, u32[]{:S(2)}) %collective-permute-start.28) | collective-permute-done | bytes 172064 | tf_op jit(solution)/shard_map/ppermute | solution.py:44
  297.1 4.7 %collective-permute-done.29 = bf16[24,3584]{1,0:T(8,128)(2,1)S(1)} collective-permute-done((bf16[24,3584]{1,0:T(8,128)(2,1)S(1)}, bf16[24,3584]{1,0:T(8,128)(2,1)S(1)}, u32[]{:S(2)}, u32[]{:S(2)}) %collective-permute-start.29) | collective-permute-done | bytes 172064 | tf_op jit(solution)/shard_map/ppermute | solution.py:44
  303.2 33.2 %collective-permute-done.65 = bf16[3584,256]{1,0:T(8,128)(2,1)S(1)} collective-permute-done((bf16[3584,256]{1,0:T(8,128)(2,1)S(1)}, bf16[3584,256]{1,0:T(8,128)(2,1)S(1)}, u32[]{:S(2)}, u32[]{:S(2)}) %collective-permute-start.65) | collective-permute-done | bytes 1835040 | tf_op jit(solution)/shard_map/ppermute | solution.py:135
  345.0 30.2 %collective-permute-done.66 = bf16[3584,256]{1,0:T(8,128)(2,1)S(1)} collective-permute-done((bf16[3584,256]{1,0:T(8,128)(2,1)S(1)}, bf16[3584,256]{1,0:T(8,128)(2,1)S(1)}, u32[]{:S(2)}, u32[]{:S(2)}) %collective-permute-start.66) | collective-permute-done | bytes 1835040 | tf_op jit(solution)/shard_map/ppermute | solution.py:135
  375.1 3.0 fusion.20
  (276 shorter events, 137.0 us)
Async XLA Ops:
  15.3 24.9 %collective-permute-start.36 = (bf16[24,3584]{1,0:T(8,128)(2,1)}, bf16[24,3584]{1,0:T(8,128)(2,1)S(1)}, u32[]{:S(2)}, u32[]{:S(2)}) collective-permute-start(bf16[24,3584]{1,0:T(8,128)(2,1)} %get-tuple-element.31), channel_id=1, source_target_pairs={{0,10},{1,11},{2,8},{3,9},{4,14},{5,15},{6,12},{7,13},{8,2},{9,3},... | collective-permute-start | bytes 516104 | tf_op jit(solution)/shard_map/ppermute | solution.py:44
  21.6 20.7 %collective-permute-start.37 = (bf16[24,3584]{1,0:T(8,128)(2,1)S(1)}, bf16[24,3584]{1,0:T(8,128)(2,1)S(1)}, u32[]{:S(2)}, u32[]{:S(2)}) collective-permute-start(bf16[24,3584]{1,0:T(8,128)(2,1)S(1)} %copy-done.12), channel_id=1, source_target_pairs={{0,12},{1,13},{2,14},{3,15},{4,8},{5,9},{6,10},{7,11},{8,4},{9,5},... | collective-permute-start | bytes 516104 | tf_op jit(solution)/shard_map/ppermute | solution.py:44
  26.9 20.6 %collective-permute-start.38 = (bf16[24,3584]{1,0:T(8,128)(2,1)S(1)}, bf16[24,3584]{1,0:T(8,128)(2,1)S(1)}, u32[]{:S(2)}, u32[]{:S(2)}) collective-permute-start(bf16[24,3584]{1,0:T(8,128)(2,1)S(1)} %copy-done.10), channel_id=1, source_target_pairs={{0,14},{1,15},{2,12},{3,13},{4,10},{5,11},{6,8},{7,9},{8,6},{9,7},... | collective-permute-start | bytes 516104 | tf_op jit(solution)/shard_map/ppermute | solution.py:44
  28.6 32.0 %collective-permute-start = (bf16[24,3584]{1,0:T(8,128)(2,1)S(1)}, bf16[24,3584]{1,0:T(8,128)(2,1)S(1)}, u32[]{:S(2)}, u32[]{:S(2)}) collective-permute-start(bf16[24,3584]{1,0:T(8,128)(2,1)S(1)} %copy-done.11), channel_id=1, source_target_pairs={{0,2},{1,3},{2,0},{3,1},{4,6},{5,7},{6,4},{7,5},{8,10},{9,11},{10,... | collective-permute-start | bytes 516104 | tf_op jit(solution)/shard_map/ppermute | solution.py:44
  31.2 30.6 %collective-permute-start.1 = (bf16[24,3584]{1,0:T(8,128)(2,1)S(1)}, bf16[24,3584]{1,0:T(8,128)(2,1)S(1)}, u32[]{:S(2)}, u32[]{:S(2)}) collective-permute-start(bf16[24,3584]{1,0:T(8,128)(2,1)S(1)} %copy-done.9), channel_id=1, source_target_pairs={{0,4},{1,5},{2,6},{3,7},{4,0},{5,1},{6,2},{7,3},{8,12},{9,13},{10,... | collective-permute-start | bytes 516104 | tf_op jit(solution)/shard_map/ppermute | solution.py:44
  40.3 26.5 %collective-permute-start.2 = (bf16[24,3584]{1,0:T(8,128)(2,1)S(1)}, bf16[24,3584]{1,0:T(8,128)(2,1)S(1)}, u32[]{:S(2)}, u32[]{:S(2)}) collective-permute-start(bf16[24,3584]{1,0:T(8,128)(2,1)S(1)} %copy-done.8), channel_id=1, source_target_pairs={{0,6},{1,7},{2,4},{3,5},{4,2},{5,3},{6,0},{7,1},{8,14},{9,15},{10,... | collective-permute-start | bytes 516104 | tf_op jit(solution)/shard_map/ppermute | solution.py:44
  42.3 25.2 %collective-permute-start.3 = (bf16[24,3584]{1,0:T(8,128)(2,1)S(1)}, bf16[24,3584]{1,0:T(8,128)(2,1)S(1)}, u32[]{:S(2)}, u32[]{:S(2)}) collective-permute-start(bf16[24,3584]{1,0:T(8,128)(2,1)S(1)} %copy-done.7), channel_id=1, source_target_pairs={{0,8},{1,9},{2,10},{3,11},{4,12},{5,13},{6,14},{7,15},{8,0},{9,1},... | collective-permute-start | bytes 516104 | tf_op jit(solution)/shard_map/ppermute | solution.py:44
  47.5 20.7 %collective-permute-start.4 = (bf16[24,3584]{1,0:T(8,128)(2,1)S(1)}, bf16[24,3584]{1,0:T(8,128)(2,1)S(1)}, u32[]{:S(2)}, u32[]{:S(2)}) collective-permute-start(bf16[24,3584]{1,0:T(8,128)(2,1)S(1)} %copy-done.6), channel_id=1, source_target_pairs={{0,10},{1,11},{2,8},{3,9},{4,14},{5,15},{6,12},{7,13},{8,2},{9,3},... | collective-permute-start | bytes 516104 | tf_op jit(solution)/shard_map/ppermute | solution.py:44
  79.3 20.0 %collective-permute-start.48 = (bf16[24,3584]{1,0:T(8,128)(2,1)S(1)}, bf16[24,3584]{1,0:T(8,128)(2,1)S(1)}, u32[]{:S(2)}, u32[]{:S(2)}) collective-permute-start(bf16[24,3584]{1,0:T(8,128)(2,1)S(1)} %get-tuple-element.26), channel_id=1, source_target_pairs={{0,2},{1,3},{2,0},{3,1},{4,6},{5,7},{6,4},{7,5},{8,10},{9,11},{10,... | collective-permute-start | bytes 516104 | tf_op jit(solution)/shard_map/ppermute | solution.py:44
  82.2 20.3 %collective-permute-start.49 = (bf16[24,3584]{1,0:T(8,128)(2,1)S(1)}, bf16[24,3584]{1,0:T(8,128)(2,1)S(1)}, u32[]{:S(2)}, u32[]{:S(2)}) collective-permute-start(bf16[24,3584]{1,0:T(8,128)(2,1)S(1)} %get-tuple-element.25), channel_id=1, source_target_pairs={{0,4},{1,5},{2,6},{3,7},{4,0},{5,1},{6,2},{7,3},{8,12},{9,13},{10,... | collective-permute-start | bytes 516104 | tf_op jit(solution)/shard_map/ppermute | solution.py:44
  85.6 19.8 %collective-permute-start.50 = (bf16[24,3584]{1,0:T(8,128)(2,1)S(1)}, bf16[24,3584]{1,0:T(8,128)(2,1)S(1)}, u32[]{:S(2)}, u32[]{:S(2)}) collective-permute-start(bf16[24,3584]{1,0:T(8,128)(2,1)S(1)} %get-tuple-element.24), channel_id=1, source_target_pairs={{0,6},{1,7},{2,4},{3,5},{4,2},{5,3},{6,0},{7,1},{8,14},{9,15},{10,... | collective-permute-start | bytes 516104 | tf_op jit(solution)/shard_map/ppermute | solution.py:44
  86.2 20.6 %collective-permute-start.51 = (bf16[24,3584]{1,0:T(8,128)(2,1)S(1)}, bf16[24,3584]{1,0:T(8,128)(2,1)S(1)}, u32[]{:S(2)}, u32[]{:S(2)}) collective-permute-start(bf16[24,3584]{1,0:T(8,128)(2,1)S(1)} %get-tuple-element.23), channel_id=1, source_target_pairs={{0,8},{1,9},{2,10},{3,11},{4,12},{5,13},{6,14},{7,15},{8,0},{9,1},... | collective-permute-start | bytes 516104 | tf_op jit(solution)/shard_map/ppermute | solution.py:44
  90.3 56.4 %collective-permute-start.52 = (bf16[24,3584]{1,0:T(8,128)(2,1)S(1)}, bf16[24,3584]{1,0:T(8,128)(2,1)S(1)}, u32[]{:S(2)}, u32[]{:S(2)}) collective-permute-start(bf16[24,3584]{1,0:T(8,128)(2,1)S(1)} %get-tuple-element.22), channel_id=1, source_target_pairs={{0,10},{1,11},{2,8},{3,9},{4,14},{5,15},{6,12},{7,13},{8,2},{9,3},... | collective-permute-start | bytes 516104 | tf_op jit(solution)/shard_map/ppermute | solution.py:44
  99.3 48.6 %collective-permute-start.53 = (bf16[24,3584]{1,0:T(8,128)(2,1)S(1)}, bf16[24,3584]{1,0:T(8,128)(2,1)S(1)}, u32[]{:S(2)}, u32[]{:S(2)}) collective-permute-start(bf16[24,3584]{1,0:T(8,128)(2,1)S(1)} %get-tuple-element.21), channel_id=1, source_target_pairs={{0,12},{1,13},{2,14},{3,15},{4,8},{5,9},{6,10},{7,11},{8,4},{9,5},... | collective-permute-start | bytes 516104 | tf_op jit(solution)/shard_map/ppermute | solution.py:44
  102.4 46.2 %collective-permute-start.54 = (bf16[24,3584]{1,0:T(8,128)(2,1)S(1)}, bf16[24,3584]{1,0:T(8,128)(2,1)S(1)}, u32[]{:S(2)}, u32[]{:S(2)}) collective-permute-start(bf16[24,3584]{1,0:T(8,128)(2,1)S(1)} %get-tuple-element.20), channel_id=1, source_target_pairs={{0,14},{1,15},{2,12},{3,13},{4,10},{5,11},{6,8},{7,9},{8,6},{9,7},... | collective-permute-start | bytes 516104 | tf_op jit(solution)/shard_map/ppermute | solution.py:44
  167.3 25.0 %collective-permute-start.45 = (bf16[24,3584]{1,0:T(8,128)(2,1)S(1)}, bf16[24,3584]{1,0:T(8,128)(2,1)S(1)}, u32[]{:S(2)}, u32[]{:S(2)}) collective-permute-start(bf16[24,3584]{1,0:T(8,128)(2,1)S(1)} %get-tuple-element.57), channel_id=1, source_target_pairs={{0,10},{1,11},{2,8},{3,9},{4,14},{5,15},{6,12},{7,13},{8,2},{9,3},... | collective-permute-start | bytes 516104 | tf_op jit(solution)/shard_map/ppermute | solution.py:44
  175.2 20.2 %collective-permute-start.47 = (bf16[24,3584]{1,0:T(8,128)(2,1)S(1)}, bf16[24,3584]{1,0:T(8,128)(2,1)S(1)}, u32[]{:S(2)}, u32[]{:S(2)}) collective-permute-start(bf16[24,3584]{1,0:T(8,128)(2,1)S(1)} %get-tuple-element.55), channel_id=1, source_target_pairs={{0,14},{1,15},{2,12},{3,13},{4,10},{5,11},{6,8},{7,9},{8,6},{9,7},... | collective-permute-start | bytes 516104 | tf_op jit(solution)/shard_map/ppermute | solution.py:44
  178.4 28.6 %collective-permute-start.9 = (bf16[24,3584]{1,0:T(8,128)(2,1)S(1)}, bf16[24,3584]{1,0:T(8,128)(2,1)S(1)}, u32[]{:S(2)}, u32[]{:S(2)}) collective-permute-start(bf16[24,3584]{1,0:T(8,128)(2,1)S(1)} %get-tuple-element.77), channel_id=1, source_target_pairs={{0,2},{1,3},{2,0},{3,1},{4,6},{5,7},{6,4},{7,5},{8,10},{9,11},{10,... | collective-permute-start | bytes 516104 | tf_op jit(solution)/shard_map/ppermute | solution.py:44
  180.4 28.0 %collective-permute-start.10 = (bf16[24,3584]{1,0:T(8,128)(2,1)S(1)}, bf16[24,3584]{1,0:T(8,128)(2,1)S(1)}, u32[]{:S(2)}, u32[]{:S(2)}) collective-permute-start(bf16[24,3584]{1,0:T(8,128)(2,1)S(1)} %get-tuple-element.76), channel_id=1, source_target_pairs={{0,4},{1,5},{2,6},{3,7},{4,0},{5,1},{6,2},{7,3},{8,12},{9,13},{10,... | collective-permute-start | bytes 516104 | tf_op jit(solution)/shard_map/ppermute | solution.py:44
  192.3 22.3 %collective-permute-start.11 = (bf16[24,3584]{1,0:T(8,128)(2,1)S(1)}, bf16[24,3584]{1,0:T(8,128)(2,1)S(1)}, u32[]{:S(2)}, u32[]{:S(2)}) collective-permute-start(bf16[24,3584]{1,0:T(8,128)(2,1)S(1)} %get-tuple-element.75), channel_id=1, source_target_pairs={{0,6},{1,7},{2,4},{3,5},{4,2},{5,3},{6,0},{7,1},{8,14},{9,15},{10,... | collective-permute-start | bytes 516104 | tf_op jit(solution)/shard_map/ppermute | solution.py:44
  192.3 35.1 %collective-permute-start.12 = (bf16[24,3584]{1,0:T(8,128)(2,1)S(1)}, bf16[24,3584]{1,0:T(8,128)(2,1)S(1)}, u32[]{:S(2)}, u32[]{:S(2)}) collective-permute-start(bf16[24,3584]{1,0:T(8,128)(2,1)S(1)} %get-tuple-element.74), channel_id=1, source_target_pairs={{0,8},{1,9},{2,10},{3,11},{4,12},{5,13},{6,14},{7,15},{8,0},{9,1},... | collective-permute-start | bytes 516104 | tf_op jit(solution)/shard_map/ppermute | solution.py:44
  195.5 32.1 %collective-permute-start.13 = (bf16[24,3584]{1,0:T(8,128)(2,1)S(1)}, bf16[24,3584]{1,0:T(8,128)(2,1)S(1)}, u32[]{:S(2)}, u32[]{:S(2)}) collective-permute-start(bf16[24,3584]{1,0:T(8,128)(2,1)S(1)} %get-tuple-element.73), channel_id=1, source_target_pairs={{0,10},{1,11},{2,8},{3,9},{4,14},{5,15},{6,12},{7,13},{8,2},{9,3},... | collective-permute-start | bytes 516104 | tf_op jit(solution)/shard_map/ppermute | solution.py:44
  207.0 21.2 %collective-permute-start.14 = (bf16[24,3584]{1,0:T(8,128)(2,1)S(1)}, bf16[24,3584]{1,0:T(8,128)(2,1)S(1)}, u32[]{:S(2)}, u32[]{:S(2)}) collective-permute-start(bf16[24,3584]{1,0:T(8,128)(2,1)S(1)} %get-tuple-element.72), channel_id=1, source_target_pairs={{0,12},{1,13},{2,14},{3,15},{4,8},{5,9},{6,10},{7,11},{8,4},{9,5},... | collective-permute-start | bytes 516104 | tf_op jit(solution)/shard_map/ppermute | solution.py:44
  208.5 20.2 %collective-permute-start.15 = (bf16[24,3584]{1,0:T(8,128)(2,1)S(1)}, bf16[24,3584]{1,0:T(8,128)(2,1)S(1)}, u32[]{:S(2)}, u32[]{:S(2)}) collective-permute-start(bf16[24,3584]{1,0:T(8,128)(2,1)S(1)} %get-tuple-element.71), channel_id=1, source_target_pairs={{0,14},{1,15},{2,12},{3,13},{4,10},{5,11},{6,8},{7,9},{8,6},{9,7},... | collective-permute-start | bytes 516104 | tf_op jit(solution)/shard_map/ppermute | solution.py:44
  214.6 81.6 %collective-permute-start.64 = (bf16[256,3584]{1,0:T(8,128)(2,1)S(1)}, bf16[256,3584]{1,0:T(8,128)(2,1)S(1)}, u32[]{:S(2)}, u32[]{:S(2)}) collective-permute-start(bf16[256,3584]{1,0:T(8,128)(2,1)S(1)} %convolution_convert_fusion.2), channel_id=1, source_target_pairs={{0,16},{16,0},{1,17},{17,1},{2,18},{18,2},{3,19},{19,3},{4,20},{20... | collective-permute-start | bytes 5505032 | tf_op jit(solution)/shard_map/ppermute | solution.py:135
  245.0 23.8 %collective-permute-start.61 = (bf16[24,3584]{1,0:T(8,128)(2,1)S(1)}, bf16[24,3584]{1,0:T(8,128)(2,1)S(1)}, u32[]{:S(2)}, u32[]{:S(2)}) collective-permute-start(bf16[24,3584]{1,0:T(8,128)(2,1)S(1)} %get-tuple-element.65), channel_id=1, source_target_pairs={{0,10},{1,11},{2,8},{3,9},{4,14},{5,15},{6,12},{7,13},{8,2},{9,3},... | collective-permute-start | bytes 516104 | tf_op jit(solution)/shard_map/ppermute | solution.py:44
  273.0 23.1 %collective-permute-start.28 = (bf16[24,3584]{1,0:T(8,128)(2,1)S(1)}, bf16[24,3584]{1,0:T(8,128)(2,1)S(1)}, u32[]{:S(2)}, u32[]{:S(2)}) collective-permute-start(bf16[24,3584]{1,0:T(8,128)(2,1)S(1)} %get-tuple-element.82), channel_id=1, source_target_pairs={{0,8},{1,9},{2,10},{3,11},{4,12},{5,13},{6,14},{7,15},{8,0},{9,1},... | collective-permute-start | bytes 516104 | tf_op jit(solution)/shard_map/ppermute | solution.py:44
  277.0 24.8 %collective-permute-start.29 = (bf16[24,3584]{1,0:T(8,128)(2,1)S(1)}, bf16[24,3584]{1,0:T(8,128)(2,1)S(1)}, u32[]{:S(2)}, u32[]{:S(2)}) collective-permute-start(bf16[24,3584]{1,0:T(8,128)(2,1)S(1)} %get-tuple-element.81), channel_id=1, source_target_pairs={{0,10},{1,11},{2,8},{3,9},{4,14},{5,15},{6,12},{7,13},{8,2},{9,3},... | collective-permute-start | bytes 516104 | tf_op jit(solution)/shard_map/ppermute | solution.py:44
  279.4 22.3 %collective-permute-start.30 = (bf16[24,3584]{1,0:T(8,128)(2,1)S(1)}, bf16[24,3584]{1,0:T(8,128)(2,1)S(1)}, u32[]{:S(2)}, u32[]{:S(2)}) collective-permute-start(bf16[24,3584]{1,0:T(8,128)(2,1)S(1)} %get-tuple-element.80), channel_id=1, source_target_pairs={{0,12},{1,13},{2,14},{3,15},{4,8},{5,9},{6,10},{7,11},{8,4},{9,5},... | collective-permute-start | bytes 516104 | tf_op jit(solution)/shard_map/ppermute | solution.py:44
  280.0 22.2 %collective-permute-start.31 = (bf16[24,3584]{1,0:T(8,128)(2,1)S(1)}, bf16[24,3584]{1,0:T(8,128)(2,1)S(1)}, u32[]{:S(2)}, u32[]{:S(2)}) collective-permute-start(bf16[24,3584]{1,0:T(8,128)(2,1)S(1)} %get-tuple-element.79), channel_id=1, source_target_pairs={{0,14},{1,15},{2,12},{3,13},{4,10},{5,11},{6,8},{7,9},{8,6},{9,7},... | collective-permute-start | bytes 516104 | tf_op jit(solution)/shard_map/ppermute | solution.py:44
  296.2 40.2 %collective-permute-start.65 = (bf16[3584,256]{1,0:T(8,128)(2,1)S(1)}, bf16[3584,256]{1,0:T(8,128)(2,1)S(1)}, u32[]{:S(2)}, u32[]{:S(2)}) collective-permute-start(bf16[3584,256]{1,0:T(8,128)(2,1)S(1)} %copy-done.14), channel_id=1, source_target_pairs={{0,16},{16,0},{1,17},{17,1},{2,18},{18,2},{3,19},{19,3},{4,20},{20... | collective-permute-start | bytes 5505032 | tf_op jit(solution)/shard_map/ppermute | solution.py:135
  336.4 38.7 %collective-permute-start.66 = (bf16[3584,256]{1,0:T(8,128)(2,1)S(1)}, bf16[3584,256]{1,0:T(8,128)(2,1)S(1)}, u32[]{:S(2)}, u32[]{:S(2)}) collective-permute-start(bf16[3584,256]{1,0:T(8,128)(2,1)S(1)} %convolution_convert_fusion.4), channel_id=1, source_target_pairs={{0,16},{16,0},{1,17},{17,1},{2,18},{18,2},{3,19},{19,3},{4,20},{20... | collective-permute-start | bytes 5505032 | tf_op jit(solution)/shard_map/ppermute | solution.py:135
  (56 other events, 748.4 us)

commit v8 on v6

--- a/solution.py
+++ b/solution.py
@@ -166,7 +166,7 @@
     )(*rows_grad, pre_gate, pre_up, gate_weight, up_weight, down_weight)
 
 
-def down_grad(which, hiddens, rows_grad, got=None):
+def down_grad(which, hiddens, rows_grad):
     count, width = rows_grad[0].shape
     half_units = hiddens[0].shape[2]
     tile = tile_of(width)
@@ -182,8 +182,6 @@
 
         rows = jnp.concatenate([ref[...] for ref in row_refs], axis=0)
         total = dot(turned_ref[...], rows, NN)
-        if got is not None:
-            total = total.astype(BF16).astype(F32) + rest[0][...].astype(F32)
         rest[-2][...] = total.astype(BF16)
 
     out_spec = pl.BlockSpec((half_units, tile), lambda n, w: (0, n))
@@ -191,13 +189,12 @@
         body,
         (width // tile,),
         [pl.BlockSpec((1, 2 * count, half_units), lambda n, w: (w[0], 0, 0))] * 2
-        + [pl.BlockSpec((count, tile), lambda n, w: (0, n))] * 4
-        + [out_spec] * (got is not None),
+        + [pl.BlockSpec((count, tile), lambda n, w: (0, n))] * 4,
         out_spec,
         jax.ShapeDtypeStruct((half_units, width), BF16),
         [pltpu.VMEM((half_units, 4 * count), BF16)],
         scalars=1,
-    )(which, *hiddens, *rows_grad, *([] if got is None else [got]))
+    )(which, *hiddens, *rows_grad)
 
 
 def gate_up_grad(which, units, rows, mirror_units, mirror_rows):
@@ -284,13 +281,13 @@
 
     def near_exchange(rows):
         return lax.all_to_all(
-            rows.reshape(near, piece, width),
+            rows.reshape(near, -1, width),
             "expert",
             split_axis=0,
             concat_axis=0,
             axis_index_groups=groups,
             tiled=True,
-        ).reshape(near * piece, width)
+        ).reshape(rows.shape)
 
     def tie(*arrays):
         return lax.optimization_barrier(arrays)
@@ -298,93 +295,104 @@
     def expert_sum(mine, other):
         return (mine.astype(F32) + swap(other).astype(F32)).astype(BF16)
 
-    acts_parts = [acts[0, b * TOK_MB : (b + 1) * TOK_MB] for b in range(MB)]
-    grad_parts = [grad_out[0, b * TOK_MB : (b + 1) * TOK_MB] for b in range(MB)]
+    def both(own, other):
+        pair = [a.reshape(near, piece, width) for a in (own, other)]
+        return jnp.stack(pair, axis=1).reshape(2 * near * piece, width)
+
+    def of_set(matrix, which):
+        shaped = matrix.reshape(matrix.shape[0], near, 1, piece)
+        pair = [jnp.zeros_like(shaped), shaped] if which else [shaped, jnp.zeros_like(shaped)]
+        return jnp.concatenate(pair, axis=2).reshape(matrix.shape[0], 2 * near * piece)
+
+    first = acts.shape[1] // 4
     meta = jnp.concatenate([expert_ids[0].astype(F32), route_weights[0]], axis=1)
     far_meta = far(meta)
+    far_acts_0 = far(acts[0, :first])
     own_placing, own_back, own_weighting, own_gain = route(meta, half, chips, capacity)
-
-    own_in = near_exchange(place(own_placing, acts[0]))
-    far_acts_0 = far(acts_parts[0])
-    acts_1, far_meta = tie(acts_parts[1], far_meta)
+    own_in = place(own_placing, acts[0])
+    own_in, far_acts_0, far_meta, acts_1 = tie(own_in, far_acts_0, far_meta, acts[0, first:])
+
     far_acts_1 = far(acts_1)
+    own_in = near_exchange(own_in)
     far_placing, far_back, far_weighting, far_gain = route(far_meta, half, chips, capacity)
-
-    own_grad, own_in = tie(place(own_placing, grad_out[0], own_gain), own_in)
-    own_grad = near_exchange(own_grad)
+    far_acts_1, own_in, grads = tie(far_acts_1, own_in, grad_out[0])
+
+    far_grads = far(grads)
+    far_in = place(far_placing, jnp.concatenate([far_acts_0, far_acts_1], axis=0))
+    far_in = near_exchange(far_in)
     own_in_b = swap(own_in)
     mirror_own = mirror(own_in)
-    grads_0, far_acts_0 = tie(grad_parts[0], far_acts_0)
-    far_grads_0 = far(grads_0)
-
-    far_acts_1, own_grad, own_in_b = tie(far_acts_1, own_grad, own_in_b)
-    far_in = near_exchange(place(far_placing, jnp.concatenate([far_acts_0, far_acts_1], axis=0)))
-    grads_1, far_acts_1 = tie(grad_parts[1], far_acts_1)
-    far_grads_1 = far(grads_1)
+    far_grads, far_in, own_in_b, mirror_own = tie(far_grads, far_in, own_in_b, mirror_own)
+
+    all_grads = near_exchange(
+        both(place(own_placing, grads, own_gain), place(far_placing, far_grads, far_gain))
+    )
+    far_in_b = swap(far_in)
+    mirror_own_b = swap(mirror_own)
+    own_pre_gate, own_pre_up, own_hidden, own_out, own_out_b = forward((own_in, own_in_b), *weights)
+    far_pre_gate, far_pre_up, far_hidden, far_out, far_out_b = forward((far_in, far_in_b), *weights)
+    all_grads, mirror_own_b, own_out, own_out_b, far_out, far_out_b = tie(
+        all_grads, mirror_own_b, own_out, own_out_b, far_out, far_out_b
+    )
+
+    own_out = expert_sum(own_out, own_out_b)
+    far_out = expert_sum(far_out, far_out_b)
+    all_grads = all_grads.reshape(near, 2, piece, width)
+    own_grad = all_grads[:, 0].reshape(near * piece, width)
+    far_grad = all_grads[:, 1].reshape(near * piece, width)
+    own_out, far_out, own_grad, far_grad = tie(own_out, far_out, own_grad, far_grad)
+
+    all_out = near_exchange(both(own_out, far_out))
+    far_grad_b = swap(far_grad)
     own_grad_b = swap(own_grad)
-    own_pre_gate, own_pre_up, own_hidden, own_out, own_out_b = forward((own_in, own_in_b), *weights)
+    far_units, far_input, far_input_b = backward(
+        (far_grad, far_grad_b), far_pre_gate, far_pre_up, *weights
+    )
     own_units, own_input, own_input_b = backward(
         (own_grad, own_grad_b), own_pre_gate, own_pre_up, *weights
     )
-
-    far_grad = place(far_placing, jnp.concatenate([far_grads_0, far_grads_1], axis=0), far_gain)
-    far_grad, far_in, own_units, own_input, own_input_b, mirror_own = tie(
-        far_grad, far_in, own_units, own_input, own_input_b, mirror_own
-    )
-    far_in_b = swap(far_in)
-    far_grad = near_exchange(far_grad)
-    mirror_far = mirror(far_in)
-    own_out = expert_sum(own_out, own_out_b)
-    far_pre_gate, far_pre_up, far_hidden, far_out, far_out_b = forward((far_in, far_in_b), *weights)
-    far_out = expert_sum(far_out, far_out_b)
-
-    far_out, far_grad, own_out = tie(far_out, far_grad, own_out)
-    far_out = near_exchange(far_out)
-    far_grad_b = swap(far_grad)
+    all_out, far_units, far_input, far_input_b, own_units, own_input, own_input_b = tie(
+        all_out, far_units, far_input, far_input_b, own_units, own_input, own_input_b
+    )
+
+    far_input = expert_sum(far_input, far_input_b)
     own_input = expert_sum(own_input, own_input_b)
-    mirror_own_b = swap(mirror_own)
-    mirror_units_own = mirror(lax.dynamic_index_in_dim(own_units, 1 - kept_half, 0, keepdims=False))
-    far_units, far_input, far_input_b = backward(
-        (far_grad, far_grad_b), far_pre_gate, far_pre_up, *weights
-    )
-    far_input = expert_sum(far_input, far_input_b)
-
-    far_input, far_out, own_input, mirror_own_b, mirror_far, mirror_units_own = tie(
-        far_input, far_out, own_input, mirror_own_b, mirror_far, mirror_units_own
-    )
-    back_out = combine(far_weighting, far_out).astype(BF16)
-    got_out_0 = far(back_out[:TOK_MB])
-    got_out_1 = far(back_out[TOK_MB:])
+    far_input, own_input, all_out, far_units, own_units, mirror_far, own_grad_b = tie(
+        far_input, own_input, all_out, far_units, own_units, far_in, own_grad_b
+    )
+
+    got_out = far(combine(of_set(far_weighting, 1), all_out).astype(BF16))
     far_input = near_exchange(far_input)
-    mirror_units_far = mirror(lax.dynamic_index_in_dim(far_units, 1 - kept_half, 0, keepdims=False))
+    mirror_far = mirror(mirror_far)
+    mirror_units = [
+        mirror(lax.dynamic_index_in_dim(units, 1 - kept_half, 0, keepdims=False))
+        for units in (own_units, far_units)
+    ]
     rows_grad = (own_grad, own_grad_b, far_grad, far_grad_b)
     send_down = down_grad(1 - kept, (own_hidden, far_hidden), rows_grad)
+    keep_down = down_grad(kept, (own_hidden, far_hidden), rows_grad)
+    got_out, far_input, mirror_far, mirror_own_units, mirror_far_units, send_down, keep_down, own_input = tie(
+        got_out, far_input, mirror_far, *mirror_units, send_down, keep_down, own_input
+    )
+
+    got_input = far(combine(far_back, far_input).astype(BF16))
+    own_input = near_exchange(own_input)
+    got_down = mirror(send_down)
     mirror_far_b = swap(mirror_far)
-
-    send_down, mirror_units_far = tie(send_down, mirror_units_far)
-    got_down = mirror(send_down)
-    back_input = combine(far_back, far_input).astype(BF16)
-    own_out, far_input, back_input, got_out_0, mirror_far_b, send_down = tie(
-        own_out, far_input, back_input, got_out_0, mirror_far_b, send_down
-    )
-    own_out = near_exchange(own_out)
-    got_input_0 = far(back_input[:TOK_MB])
-    back_input_1, got_out_1 = tie(back_input[TOK_MB:], got_out_1)
-    got_input_1 = far(back_input_1)
-    own_input, own_out, got_out_1 = tie(own_input, own_out, got_out_1)
-    own_input = near_exchange(own_input)
     grad_gate, grad_up = gate_up_grad(
         kept,
         (own_units, far_units),
         (own_in, own_in_b, far_in, far_in_b),
-        (mirror_units_own, mirror_units_far),
+        (mirror_own_units, mirror_far_units),
         (mirror_own, mirror_own_b, mirror_far, mirror_far_b),
     )
-    got_out = jnp.concatenate([got_out_0, got_out_1], axis=0).astype(F32)
-    out_acts = (combine(own_weighting, own_out) + got_out).astype(BF16)
-    grad_down = down_grad(kept, (own_hidden, far_hidden), rows_grad, got_down)
-    got_input = jnp.concatenate([got_input_0, got_input_1], axis=0).astype(F32)
-    grad_acts = (combine(own_back, own_input) + got_input).astype(BF16)
+    out_acts = (combine(of_set(own_weighting, 0), all_out) + got_out.astype(F32)).astype(BF16)
+    got_input, own_input, got_down, grad_gate, grad_up, out_acts = tie(
+        got_input, own_input, got_down, grad_gate, grad_up, out_acts
+    )
+
+    grad_acts = (combine(own_back, own_input) + got_input.astype(F32)).astype(BF16)
+    grad_down = (keep_down.astype(F32) + got_down.astype(F32)).astype(BF16)
     return out_acts[None], grad_acts[None], grad_gate[None], grad_up[None], grad_down[None]
 
 

time: 381 us -> 312 us (0.82)
  waiting for transfers between devices: 211 us -> 147 us
  starting transfers between devices: 51.2 us -> 41.5 us
  matrix products: 14.7 us -> 19 us
    ppermute x5, waiting for transfers between devices: 66.8 us -> 25.1 us  [mirror(): lax.ppermute(rows, 'pipe', [(p, rank_count - 1 - p) for p in range(rank_c...]
    all_to_all x8 -> x6, waiting for transfers between devices: 45.2 us -> 12.2 us  [near_exchange(): lax.all_to_all(rows.reshape(near, -1, width), 'expert', split_axis=0, con...]
    ppermute x19 -> x16, waiting for transfers between devices: 99.2 us -> 110 us  [hop(): lax.ppermute(rows, 'expert', [(i, i ^ distance) for i in range(devices)])]
    convert_element_type x4, other arithmetic: 11.3 us -> 4.91 us  [expert_sum(): return (mine.astype(F32) + swap(other).astype(F32)).astype(BF16)]
    all_to_all x8 -> x6, starting transfers between devices: 30.6 us -> 24.5 us  [near_exchange(): lax.all_to_all(rows.reshape(near, -1, width), 'expert', split_axis=0, con...]
    ppermute x19 -> x16, starting transfers between devices: 15.3 us -> 12.1 us  [hop(): lax.ppermute(rows, 'expert', [(i, i ^ distance) for i in range(devices)])]
  transfers between devices with their start and end apart: 32 -> 27, of which waited for: 14 -> 11; matrix products, arithmetic and copies ran while one was open for 7% -> 8% of each run, Pallas kernels for 19% -> 23%
where the time goes in v8:
time: 312 us; the launch traced here: 311 us
  waiting for transfers between devices  147 us (47%)
  Pallas kernels  72.3 us (23%)
  starting transfers between devices  41.5 us (13%)
  matrix products  19 us (6%)
  local copies, waits for them, and re-layouts  15.1 us (5%)
  other arithmetic  15.1 us (5%)
    ppermute x16, waiting for transfers between devices, hop(): lax.ppermute(rows, 'expert', [(i, i ^ distance) for i in range(devices)])  110 us
    ppermute x5, waiting for transfers between devices, mirror(): lax.ppermute(rows, 'pipe', [(p, rank_count - 1 - p) for p in range(rank_c...  25.1 us
    all_to_all x6, starting transfers between devices, near_exchange(): lax.all_to_all(rows.reshape(near, -1, width), 'expert', split_axis=0, con...  24.5 us
    pallas_call x2, Pallas kernels, backward(): kernel_call(body, (2,), [whole, whole, units, units, columns, columns, pl...  22.6 us
    pallas_call x2, Pallas kernels, forward(): kernel_call(body, (2,), [whole, whole, columns, columns, pl.BlockSpec((ha...  22 us
    pallas_call x2, Pallas kernels, down_grad(): kernel_call(body, (width // tile,), [pl.BlockSpec((1, 2 * count, half_uni...  15.4 us
    dot_general x6, matrix products, dot(): return lax.dot_general(a, b, (dims, ((), ())), preferred_element_type=F32)  12.7 us
    pallas_call x1, Pallas kernels, gate_up_grad(): kernel_call(body, (width // tile,), [pl.BlockSpec((1, 2 * count, both), l...  12.3 us
  transfers between devices with their start and end apart: 27, of which 11 were waited for; matrix products, arithmetic and copies ran while one was open for 8% of the time, Pallas kernels for 23%

profile of v8, /device:TPU:0, one launch (start us, length us, event | category | flops | bytes accessed | tf_op | source)
XLA Modules:
  0.0 311.0 jit_solution(487389195010005381)
XLA Ops:
  2.1 4.0 %collective-permute-start.1 = (f32[128,4]{0,1:T(4,128)S(1)}, f32[128,4]{0,1:T(4,128)S(1)}, u32[]{:S(2)}, u32[]{:S(2)}) collective-permute-start(f32[128,4]{0,1:T(4,128)S(1)} %pad_maximum_fusion.2), channel_id=1, source_target_pairs={{0,8},{1,9},{2,10},{3,11},{4,12},{5,13},{6,14},{7,15},{8,0},{9,1},... | collective-permute-start | bytes 6152 | tf_op jit(solution)/shard_map/ppermute | solution.py:265
  11.2 8.9 %collective-permute-done = bf16[32,3584]{1,0:T(8,128)(2,1)S(1)} collective-permute-done((bf16[32,3584]{1,0:T(8,128)(2,1)S(1)}, bf16[32,3584]{1,0:T(8,128)(2,1)S(1)}, u32[]{:S(2)}, u32[]{:S(2)}) %collective-permute-start) | collective-permute-done | bytes 229408 | tf_op jit(solution)/shard_map/ppermute | solution.py:265
  20.1 3.5 %all-to-all-start = ((bf16[4,48,3584]{2,1,0:T(8,128)(2,1)}), bf16[4,48,3584]{2,1,0:T(8,128)(2,1)S(1)}, u32[]{:S(2)}, u32[]{:S(2)}) async-start(bf16[4,48,3584]{2,1,0:T(8,128)(2,1)} %bitcast.8), calls=%async_computation | async-start | bytes 2752512 | tf_op jit(solution)/shard_map/all_to_all | solution.py:283
  25.3 30.6 %collective-permute-done.2 = bf16[96,3584]{1,0:T(8,128)(2,1)S(1)} collective-permute-done((bf16[96,3584]{1,0:T(8,128)(2,1)S(1)}, bf16[96,3584]{1,0:T(8,128)(2,1)S(1)}, u32[]{:S(2)}, u32[]{:S(2)}) %collective-permute-start.2) | collective-permute-done | bytes 688160 | tf_op jit(solution)/shard_map/ppermute | solution.py:265
  57.5 3.5 %all-to-all-start.1 = ((bf16[4,48,3584]{2,1,0:T(8,128)(2,1)}), bf16[4,48,3584]{2,1,0:T(8,128)(2,1)S(1)}, u32[]{:S(2)}, u32[]{:S(2)}) async-start(bf16[4,48,3584]{2,1,0:T(8,128)(2,1)} %bitcast.113), calls=%async_computation.1 | async-start | bytes 2752512 | tf_op jit(solution)/shard_map/all_to_all | solution.py:283
  64.3 2.8 fusion
  67.1 38.8 %collective-permute-done.3 = bf16[128,3584]{1,0:T(8,128)(2,1)S(1)} collective-permute-done((bf16[128,3584]{1,0:T(8,128)(2,1)}, bf16[128,3584]{1,0:T(8,128)(2,1)S(1)}, u32[]{:S(2)}, u32[]{:S(2)}) %collective-permute-start.3) | collective-permute-done | bytes 917536 | tf_op jit(solution)/shard_map/ppermute | solution.py:265
  108.0 2.2 fusion.1
  112.0 4.6 %all-to-all-start.2 = ((bf16[4,96,3584]{2,1,0:T(8,128)(2,1)}), bf16[4,96,3584]{2,1,0:T(8,128)(2,1)}, u32[]{:S(2)}, u32[]{:S(2)}) async-start(bf16[4,96,3584]{2,1,0:T(8,128)(2,1)} %bitcast.109), calls=%async_computation.2 | async-start | bytes 5505024 | tf_op jit(solution)/shard_map/all_to_all | solution.py:283
  117.2 11.0 %shard_map.110 = (f32[2,384,256]{2,1,0:T(8,128)}, f32[2,384,256]{2,1,0:T(8,128)}, bf16[2,384,256]{2,1,0:T(8,128)(2,1)}, bf16[192,3584]{1,0:T(8,128)(2,1)}, bf16[192,3584]{1,0:T(8,128)(2,1)}) custom-call(bf16[192,3584]{1,0:T(8,128)(2,1)} %bitcast.103, bf16[192,3584]{1,0:T(8,128)(2,1)} %copy-done.6, bf16[3584,512]{1,0:T(8,128)(2,1)} %bitcast.79, ...), custom_call_target="tpu_custom_call" | custom-call | flops 1 | bytes 1 | tf_op jit(solution)/shard_map/pallas_call | solution.py:101
  129.3 11.0 %shard_map.111 = (f32[2,384,256]{2,1,0:T(8,128)}, f32[2,384,256]{2,1,0:T(8,128)}, bf16[2,384,256]{2,1,0:T(8,128)(2,1)}, bf16[192,3584]{1,0:T(8,128)(2,1)}, bf16[192,3584]{1,0:T(8,128)(2,1)}) custom-call(bf16[192,3584]{1,0:T(8,128)(2,1)} %bitcast.106, bf16[192,3584]{1,0:T(8,128)(2,1)} %copy-done.7, bf16[3584,512]{1,0:T(8,128)(2,1)} %bitcast.80, ...), custom_call_target="tpu_custom_call" | custom-call | flops 1 | bytes 1 | tf_op jit(solution)/shard_map/pallas_call | solution.py:101
  140.3 8.1 %all-to-all-done.2 = bf16[4,96,3584]{2,1,0:T(8,128)(2,1)} async-done(((bf16[4,96,3584]{2,1,0:T(8,128)(2,1)}), bf16[4,96,3584]{2,1,0:T(8,128)(2,1)}, u32[]{:S(2)}, u32[]{:S(2)}) %all-to-all-start.2) | async-done | bytes 2752544 | tf_op jit(solution)/shard_map/all_to_all | solution.py:283
  149.0 3.6 %fusion.19 = (bf16[4,1,48,3584]{3,2,1,0:T(8,128)(2,1)}, bf16[4,1,48,3584]{3,2,1,0:T(8,128)(2,1)}) fusion(bf16[4,2,48,3584]{3,2,1,0:T(8,128)(2,1)} %bitcast.25), kind=kLoop, calls=%fused_computation.61 | loop fusion | bytes 5505024 | tf_op jit(solution)/shard_map/slice | solution.py:342
  156.2 3.8 %all-to-all-start.3 = ((bf16[4,96,3584]{2,1,0:T(8,128)(2,1)}), bf16[4,96,3584]{2,1,0:T(8,128)(2,1)S(1)}, u32[]{:S(2)}, u32[]{:S(2)}) async-start(bf16[4,96,3584]{2,1,0:T(8,128)(2,1)} %bitcast.110), calls=%async_computation.3 | async-start | bytes 5505024 | tf_op jit(solution)/shard_map/all_to_all | solution.py:283
  160.7 2.8 collective-permute-done.11.b_ref.refs_3_
  164.6 11.3 %shard_map.113 = (bf16[2,384,512]{2,1,0:T(8,128)(2,1)}, bf16[192,3584]{1,0:T(8,128)(2,1)}, bf16[192,3584]{1,0:T(8,128)(2,1)}) custom-call(bf16[192,3584]{1,0:T(8,128)(2,1)} %bitcast.98, bf16[192,3584]{1,0:T(8,128)(2,1)} %copy-done.2, f32[2,384,256]{2,1,0:T(8,128)} %get-tuple-element.101.pre_gate_ref, f32[2,384,256]{2,1,0:T(8,128)} %get-tuple-element.102.pre_up_ref, ...), custom_call_target="tpu_custom_call" | custom-call | flops 1 | bytes 1 | tf_op jit(solution)/shard_map/pallas_call | solution.py:155
  177.0 11.3 %shard_map.112 = (bf16[2,384,512]{2,1,0:T(8,128)(2,1)}, bf16[192,3584]{1,0:T(8,128)(2,1)}, bf16[192,3584]{1,0:T(8,128)(2,1)}) custom-call(bf16[192,3584]{1,0:T(8,128)(2,1)} %bitcast.94, bf16[192,3584]{1,0:T(8,128)(2,1)} %copy-done.3, f32[2,384,256]{2,1,0:T(8,128)} %get-tuple-element.95.pre_gate_ref, f32[2,384,256]{2,1,0:T(8,128)} %get-tuple-element.96.pre_up_ref, ...), custom_call_target="tpu_custom_call" | custom-call | flops 1 | bytes 1 | tf_op jit(solution)/shard_map/pallas_call | solution.py:155
  188.3 4.0 %all-to-all-done.3 = bf16[4,96,3584]{2,1,0:T(8,128)(2,1)S(1)} async-done(((bf16[4,96,3584]{2,1,0:T(8,128)(2,1)}), bf16[4,96,3584]{2,1,0:T(8,128)(2,1)S(1)}, u32[]{:S(2)}, u32[]{:S(2)}) %all-to-all-start.3) | async-done | bytes 2752544 | tf_op jit(solution)/shard_map/all_to_all | solution.py:283
  192.9 2.8 collective-permute-done.13
  195.7 2.9 add_convert_fusion.1
  200.0 4.3 %all-to-all-start.4 = ((bf16[4,48,3584]{2,1,0:T(8,128)(2,1)}), bf16[4,48,3584]{2,1,0:T(8,128)(2,1)}, u32[]{:S(2)}, u32[]{:S(2)}) async-start(bf16[4,48,3584]{2,1,0:T(8,128)(2,1)} %bitcast.112), calls=%async_computation.4 | async-start | bytes 2752512 | tf_op jit(solution)/shard_map/all_to_all | solution.py:283
  205.6 2.6 convolution_convert_fusion.3
  213.1 7.7 %shard_map.115 = bf16[256,3584]{1,0:T(8,128)(2,1)} custom-call(s32[1]{0:T(128)} %bitcast.38.which_ref, bf16[2,384,256]{2,1,0:T(8,128)(2,1)} %get-tuple-element.118.refs_0_, bf16[2,384,256]{2,1,0:T(8,128)(2,1)} %get-tuple-element.119.refs_1_, bf16[192,3584]{1,0:T(8,128)(2,1)} %bitcast.99, bf16[192,3584]{1,0:T(8,128)(2,1)} %copy-done.2, ...), custom_call_target="tpu_custom_call" | custom-call | flops 1 | bytes 1 | tf_op jit(solution)/shard_map/pallas_call | solution.py:188
  220.9 7.7 %shard_map.114 = bf16[256,3584]{1,0:T(8,128)(2,1)} custom-call(s32[1]{0:T(128)S(6)} %sub.37.which_ref, bf16[2,384,256]{2,1,0:T(8,128)(2,1)} %get-tuple-element.118.refs_0_, bf16[2,384,256]{2,1,0:T(8,128)(2,1)} %get-tuple-element.119.refs_1_, bf16[192,3584]{1,0:T(8,128)(2,1)} %bitcast.100, bf16[192,3584]{1,0:T(8,128)(2,1)} %copy-done.2, ...), custom_call_target="tpu_custom_call" | custom-call | flops 1 | bytes 1 | tf_op jit(solution)/shard_map/pallas_call | solution.py:188
  228.6 17.5 %collective-permute-done.16.refs_2_ = bf16[384,512]{1,0:T(8,128)(2,1)S(1)} collective-permute-done((bf16[384,512]{1,0:T(8,128)(2,1)S(1)}, bf16[384,512]{1,0:T(8,128)(2,1)S(1)}, u32[]{:S(2)}, u32[]{:S(2)}) %collective-permute-start.16) | collective-permute-done | bytes 393248 | tf_op jit(solution)/shard_map/ppermute | solution.py:274
  246.0 7.6 %collective-permute-done.17.refs_3_ = bf16[384,512]{1,0:T(8,128)(2,1)S(1)} collective-permute-done((bf16[384,512]{1,0:T(8,128)(2,1)S(1)}, bf16[384,512]{1,0:T(8,128)(2,1)S(1)}, u32[]{:S(2)}, u32[]{:S(2)}) %collective-permute-start.17) | collective-permute-done | bytes 393248 | tf_op jit(solution)/shard_map/ppermute | solution.py:274
  253.7 4.5 %all-to-all-start.5 = ((bf16[4,48,3584]{2,1,0:T(8,128)(2,1)}), bf16[4,48,3584]{2,1,0:T(8,128)(2,1)}, u32[]{:S(2)}, u32[]{:S(2)}) async-start(bf16[4,48,3584]{2,1,0:T(8,128)(2,1)} %bitcast.111), calls=%async_computation.5 | async-start | bytes 2752512 | tf_op jit(solution)/shard_map/all_to_all | solution.py:283
  262.5 3.8 %fusion.2 = bf16[128,3584]{1,0:T(8,128)(2,1)} fusion(f32[128,384]{0,1:T(8,128)S(1)} %bitcast.121, bf16[384,3584]{1,0:T(8,128)(2,1)S(1)} %bitcast.92, bf16[128,3584]{1,0:T(8,128)(2,1)} %collective-permute-done.14), kind=kOutput, calls=%fused_computation.8 | convolution fusion | flops 2115305472 | bytes 4784128 | tf_op jit(solution)/shard_map/dot_general | solution.py:53
  267.4 12.3 %shard_map.116 = (bf16[3584,256]{1,0:T(8,128)(2,1)}, bf16[3584,256]{1,0:T(8,128)(2,1)}) custom-call(s32[1]{0:T(128)} %bitcast.38.which_ref, bf16[2,384,512]{2,1,0:T(8,128)(2,1)} %get-tuple-element.116.refs_0_, bf16[2,384,512]{2,1,0:T(8,128)(2,1)} %get-tuple-element.117.refs_1_, bf16[384,512]{1,0:T(8,128)(2,1)} %copy-done.17, bf16[384,512]{1,0:T(8,128)(2,1)} %copy-done.18, ...), custom_call_target="tpu_custom_call" | custom-call | flops 1 | bytes 1 | tf_op jit(solution)/shard_map/pallas_call | solution.py:221
  279.7 24.4 %collective-permute-done.18 = bf16[128,3584]{1,0:T(8,128)(2,1)S(1)} collective-permute-done((bf16[128,3584]{1,0:T(8,128)(2,1)S(1)}, bf16[128,3584]{1,0:T(8,128)(2,1)S(1)}, u32[]{:S(2)}, u32[]{:S(2)}) %collective-permute-start.18) | collective-permute-done | bytes 917536 | tf_op jit(solution)/shard_map/ppermute | solution.py:265
  305.0 3.2 %fusion.5 = bf16[1,256,3584]{2,1,0:T(8,128)(2,1)} fusion(bf16[256,3584]{1,0:T(8,128)(2,1)} %collective-permute-done.19, bf16[256,3584]{1,0:T(8,128)(2,1)S(1)} %copy-done.4), kind=kLoop, calls=%fused_computation.20 | loop fusion | flops 3670016 | bytes 5505024 | tf_op jit(solution)/shard_map/broadcast_in_dim | solution.py:396
  308.3 2.7 fusion.4
  (120 shorter events, 39.8 us)
Async XLA Ops:
  0.6 8.8 %copy-start.19 = (f32[1,128,2]{1,2,0:T(2,128)S(1)}, f32[1,128,2]{1,2,0:T(2,128)}, u32[]{:S(2)}) copy-start(f32[1,128,2]{1,2,0:T(2,128)} %param.10) | copy-start | bytes 3076
  0.7 8.9 %copy-start.8 = (bf16[1,128,3584]{2,1,0:T(8,128)(2,1)S(1)}, bf16[1,128,3584]{2,1,0:T(8,128)(2,1)}, u32[]{:S(2)}) copy-start(bf16[1,128,3584]{2,1,0:T(8,128)(2,1)} %param.7) | copy-start | bytes 2752516
  2.1 9.0 %collective-permute-start.1 = (f32[128,4]{0,1:T(4,128)S(1)}, f32[128,4]{0,1:T(4,128)S(1)}, u32[]{:S(2)}, u32[]{:S(2)}) collective-permute-start(f32[128,4]{0,1:T(4,128)S(1)} %pad_maximum_fusion.2), channel_id=1, source_target_pairs={{0,8},{1,9},{2,10},{3,11},{4,12},{5,13},{6,14},{7,15},{8,0},{9,1},... | collective-permute-start | bytes 6152 | tf_op jit(solution)/shard_map/ppermute | solution.py:265
  7.1 12.9 %collective-permute-start = (bf16[32,3584]{1,0:T(8,128)(2,1)S(1)}, bf16[32,3584]{1,0:T(8,128)(2,1)S(1)}, u32[]{:S(2)}, u32[]{:S(2)}) collective-permute-start(bf16[32,3584]{1,0:T(8,128)(2,1)S(1)} %slice_bitcast_fusion.1), channel_id=1, source_target_pairs={{0,8},{1,9},{2,10},{3,11},{4,12},{5,13},{6,14},{7,15},{8,0},{9,1},... | collective-permute-start | bytes 688136 | tf_op jit(solution)/shard_map/ppermute | solution.py:265
  20.1 35.9 %all-to-all-start = ((bf16[4,48,3584]{2,1,0:T(8,128)(2,1)}), bf16[4,48,3584]{2,1,0:T(8,128)(2,1)S(1)}, u32[]{:S(2)}, u32[]{:S(2)}) async-start(bf16[4,48,3584]{2,1,0:T(8,128)(2,1)} %bitcast.8), calls=%async_computation | async-start | bytes 2752512 | tf_op jit(solution)/shard_map/all_to_all | solution.py:283
  23.9 32.0 %collective-permute-start.2 = (bf16[96,3584]{1,0:T(8,128)(2,1)S(1)}, bf16[96,3584]{1,0:T(8,128)(2,1)S(1)}, u32[]{:S(2)}, u32[]{:S(2)}) collective-permute-start(bf16[96,3584]{1,0:T(8,128)(2,1)S(1)} %slice_bitcast_fusion), channel_id=1, source_target_pairs={{0,8},{1,9},{2,10},{3,11},{4,12},{5,13},{6,14},{7,15},{8,0},{9,1},... | collective-permute-start | bytes 2064392 | tf_op jit(solution)/shard_map/ppermute | solution.py:265
  57.5 50.4 %all-to-all-start.1 = ((bf16[4,48,3584]{2,1,0:T(8,128)(2,1)}), bf16[4,48,3584]{2,1,0:T(8,128)(2,1)S(1)}, u32[]{:S(2)}, u32[]{:S(2)}) async-start(bf16[4,48,3584]{2,1,0:T(8,128)(2,1)} %bitcast.113), calls=%async_computation.1 | async-start | bytes 2752512 | tf_op jit(solution)/shard_map/all_to_all | solution.py:283
  61.1 44.9 %collective-permute-start.4 = (bf16[192,3584]{1,0:T(8,128)(2,1)S(1)}, bf16[192,3584]{1,0:T(8,128)(2,1)S(1)}, u32[]{:S(2)}, u32[]{:S(2)}) collective-permute-start(bf16[192,3584]{1,0:T(8,128)(2,1)S(1)} %bitcast.101), channel_id=1, source_target_pairs={{0,1},{1,0},{2,3},{3,2},{4,5},{5,4},{6,7},{7,6},{8,9},{9,8},{10,11... | collective-permute-start | bytes 4128776 | tf_op jit(solution)/shard_map/ppermute | solution.py:265
  61.2 46.8 %collective-permute-start.5 = (bf16[192,3584]{1,0:T(8,128)(2,1)S(1)}, bf16[192,3584]{1,0:T(8,128)(2,1)}, u32[]{:S(2)}, u32[]{:S(2)}) collective-permute-start(bf16[192,3584]{1,0:T(8,128)(2,1)S(1)} %bitcast.102), channel_id=1, source_target_pairs={{0,16},{16,0},{1,17},{17,1},{2,18},{18,2},{3,19},{19,3},{4,20},{20... | collective-permute-start | bytes 4128776 | tf_op jit(solution)/shard_map/ppermute | solution.py:274
  62.7 43.2 %collective-permute-start.3 = (bf16[128,3584]{1,0:T(8,128)(2,1)}, bf16[128,3584]{1,0:T(8,128)(2,1)S(1)}, u32[]{:S(2)}, u32[]{:S(2)}) collective-permute-start(bf16[128,3584]{1,0:T(8,128)(2,1)} %bitcast.119), channel_id=1, source_target_pairs={{0,8},{1,9},{2,10},{3,11},{4,12},{5,13},{6,14},{7,15},{8,0},{9,1},... | collective-permute-start | bytes 2752520 | tf_op jit(solution)/shard_map/ppermute | solution.py:265
  112.0 36.5 %all-to-all-start.2 = ((bf16[4,96,3584]{2,1,0:T(8,128)(2,1)}), bf16[4,96,3584]{2,1,0:T(8,128)(2,1)}, u32[]{:S(2)}, u32[]{:S(2)}) async-start(bf16[4,96,3584]{2,1,0:T(8,128)(2,1)} %bitcast.109), calls=%async_computation.2 | async-start | bytes 5505024 | tf_op jit(solution)/shard_map/all_to_all | solution.py:283
  116.6 11.6 %collective-permute-start.7 = (bf16[192,3584]{1,0:T(8,128)(2,1)S(1)}, bf16[192,3584]{1,0:T(8,128)(2,1)S(1)}, u32[]{:S(2)}, u32[]{:S(2)}) collective-permute-start(bf16[192,3584]{1,0:T(8,128)(2,1)S(1)} %bitcast.105), channel_id=1, source_target_pairs={{0,1},{1,0},{2,3},{3,2},{4,5},{5,4},{6,7},{7,6},{8,9},{9,8},{10,11... | collective-permute-start | bytes 4128776 | tf_op jit(solution)/shard_map/ppermute | solution.py:265
  116.7 23.6 %collective-permute-start.6 = (bf16[192,3584]{1,0:T(8,128)(2,1)}, bf16[192,3584]{1,0:T(8,128)(2,1)}, u32[]{:S(2)}, u32[]{:S(2)}) collective-permute-start(bf16[192,3584]{1,0:T(8,128)(2,1)} %collective-permute-done.5.refs_8_), channel_id=1, source_target_pairs={{0,1},{1,0},{2,3},{3,2},{4,5},{5,4},{6,7},{7,6},{8,9},{9,8},{10,11... | collective-permute-start | bytes 4128776 | tf_op jit(solution)/shard_map/ppermute | solution.py:265
  128.2 20.3 %copy-start.21 = (bf16[192,3584]{1,0:T(8,128)(2,1)S(1)}, bf16[192,3584]{1,0:T(8,128)(2,1)}, u32[]{:S(2)}) copy-start(bf16[192,3584]{1,0:T(8,128)(2,1)} %get-tuple-element.88) | copy-start | bytes 4128772
  148.5 5.2 %collective-permute-start.9 = (bf16[192,3584]{1,0:T(8,128)(2,1)}, bf16[192,3584]{1,0:T(8,128)(2,1)S(1)}, u32[]{:S(2)}, u32[]{:S(2)}) collective-permute-start(bf16[192,3584]{1,0:T(8,128)(2,1)} %get-tuple-element.90), channel_id=1, source_target_pairs={{0,1},{1,0},{2,3},{3,2},{4,5},{5,4},{6,7},{7,6},{8,9},{9,8},{10,11... | collective-permute-start | bytes 4128776 | tf_op jit(solution)/shard_map/ppermute | solution.py:265
  148.5 5.6 %collective-permute-start.8 = (bf16[192,3584]{1,0:T(8,128)(2,1)S(1)}, bf16[192,3584]{1,0:T(8,128)(2,1)S(1)}, u32[]{:S(2)}, u32[]{:S(2)}) collective-permute-start(bf16[192,3584]{1,0:T(8,128)(2,1)S(1)} %copy-done.21), channel_id=1, source_target_pairs={{0,1},{1,0},{2,3},{3,2},{4,5},{5,4},{6,7},{7,6},{8,9},{9,8},{10,11... | collective-permute-start | bytes 4128776 | tf_op jit(solution)/shard_map/ppermute | solution.py:265
  156.2 36.1 %all-to-all-start.3 = ((bf16[4,96,3584]{2,1,0:T(8,128)(2,1)}), bf16[4,96,3584]{2,1,0:T(8,128)(2,1)S(1)}, u32[]{:S(2)}, u32[]{:S(2)}) async-start(bf16[4,96,3584]{2,1,0:T(8,128)(2,1)} %bitcast.110), calls=%async_computation.3 | async-start | bytes 5505024 | tf_op jit(solution)/shard_map/all_to_all | solution.py:283
  160.1 3.4 %collective-permute-start.11 = (bf16[192,3584]{1,0:T(8,128)(2,1)}, bf16[192,3584]{1,0:T(8,128)(2,1)S(1)}, u32[]{:S(2)}, u32[]{:S(2)}) collective-permute-start(bf16[192,3584]{1,0:T(8,128)(2,1)} %bitcast.97), channel_id=1, source_target_pairs={{0,1},{1,0},{2,3},{3,2},{4,5},{5,4},{6,7},{7,6},{8,9},{9,8},{10,11... | collective-permute-start | bytes 4128776 | tf_op jit(solution)/shard_map/ppermute | solution.py:265
  160.3 15.6 %collective-permute-start.10 = (bf16[192,3584]{1,0:T(8,128)(2,1)}, bf16[192,3584]{1,0:T(8,128)(2,1)S(1)}, u32[]{:S(2)}, u32[]{:S(2)}) collective-permute-start(bf16[192,3584]{1,0:T(8,128)(2,1)} %bitcast.93), channel_id=1, source_target_pairs={{0,1},{1,0},{2,3},{3,2},{4,5},{5,4},{6,7},{7,6},{8,9},{9,8},{10,11... | collective-permute-start | bytes 4128776 | tf_op jit(solution)/shard_map/ppermute | solution.py:265
  192.3 3.3 %collective-permute-start.13 = (bf16[192,3584]{1,0:T(8,128)(2,1)}, bf16[192,3584]{1,0:T(8,128)(2,1)S(1)}, u32[]{:S(2)}, u32[]{:S(2)}) collective-permute-start(bf16[192,3584]{1,0:T(8,128)(2,1)} %get-tuple-element.109), channel_id=1, source_target_pairs={{0,1},{1,0},{2,3},{3,2},{4,5},{5,4},{6,7},{7,6},{8,9},{9,8},{10,11... | collective-permute-start | bytes 4128776 | tf_op jit(solution)/shard_map/ppermute | solution.py:265
  192.3 6.2 %collective-permute-start.12 = (bf16[192,3584]{1,0:T(8,128)(2,1)}, bf16[192,3584]{1,0:T(8,128)(2,1)S(1)}, u32[]{:S(2)}, u32[]{:S(2)}) collective-permute-start(bf16[192,3584]{1,0:T(8,128)(2,1)} %get-tuple-element.107), channel_id=1, source_target_pairs={{0,1},{1,0},{2,3},{3,2},{4,5},{5,4},{6,7},{7,6},{8,9},{9,8},{10,11... | collective-permute-start | bytes 4128776 | tf_op jit(solution)/shard_map/ppermute | solution.py:265
  200.0 53.7 %all-to-all-start.4 = ((bf16[4,48,3584]{2,1,0:T(8,128)(2,1)}), bf16[4,48,3584]{2,1,0:T(8,128)(2,1)}, u32[]{:S(2)}, u32[]{:S(2)}) async-start(bf16[4,48,3584]{2,1,0:T(8,128)(2,1)} %bitcast.112), calls=%async_computation.4 | async-start | bytes 2752512 | tf_op jit(solution)/shard_map/all_to_all | solution.py:283
  204.3 49.4 %collective-permute-start.15 = (bf16[192,3584]{1,0:T(8,128)(2,1)}, bf16[192,3584]{1,0:T(8,128)(2,1)}, u32[]{:S(2)}, u32[]{:S(2)}) collective-permute-start(bf16[192,3584]{1,0:T(8,128)(2,1)} %bitcast.107), channel_id=1, source_target_pairs={{0,16},{16,0},{1,17},{17,1},{2,18},{18,2},{3,19},{19,3},{4,20},{20... | collective-permute-start | bytes 4128776 | tf_op jit(solution)/shard_map/ppermute | solution.py:274
  208.2 45.5 %collective-permute-start.14 = (bf16[128,3584]{1,0:T(8,128)(2,1)}, bf16[128,3584]{1,0:T(8,128)(2,1)}, u32[]{:S(2)}, u32[]{:S(2)}) collective-permute-start(bf16[128,3584]{1,0:T(8,128)(2,1)} %convolution_convert_fusion.3), channel_id=1, source_target_pairs={{0,8},{1,9},{2,10},{3,11},{4,12},{5,13},{6,14},{7,15},{8,0},{9,1},... | collective-permute-start | bytes 2752520 | tf_op jit(solution)/shard_map/ppermute | solution.py:265
  210.0 36.1 %collective-permute-start.16 = (bf16[384,512]{1,0:T(8,128)(2,1)S(1)}, bf16[384,512]{1,0:T(8,128)(2,1)S(1)}, u32[]{:S(2)}, u32[]{:S(2)}) collective-permute-start(bf16[384,512]{1,0:T(8,128)(2,1)S(1)} %dynamic-slice_bitcast_fusion.1), channel_id=1, source_target_pairs={{0,16},{16,0},{1,17},{17,1},{2,18},{18,2},{3,19},{19,3},{4,20},{20... | collective-permute-start | bytes 1179656 | tf_op jit(solution)/shard_map/ppermute | solution.py:274
  212.5 41.1 %collective-permute-start.17 = (bf16[384,512]{1,0:T(8,128)(2,1)S(1)}, bf16[384,512]{1,0:T(8,128)(2,1)S(1)}, u32[]{:S(2)}, u32[]{:S(2)}) collective-permute-start(bf16[384,512]{1,0:T(8,128)(2,1)S(1)} %dynamic-slice_bitcast_fusion), channel_id=1, source_target_pairs={{0,16},{16,0},{1,17},{17,1},{2,18},{18,2},{3,19},{19,3},{4,20},{20... | collective-permute-start | bytes 1179656 | tf_op jit(solution)/shard_map/ppermute | solution.py:274
  246.0 14.6 %copy-start.17 = (bf16[384,512]{1,0:T(8,128)(2,1)}, bf16[384,512]{1,0:T(8,128)(2,1)S(1)}, u32[]{:S(2)}) copy-start(bf16[384,512]{1,0:T(8,128)(2,1)S(1)} %collective-permute-done.16.refs_2_) | copy-start | bytes 1179652
  253.7 51.3 %all-to-all-start.5 = ((bf16[4,48,3584]{2,1,0:T(8,128)(2,1)}), bf16[4,48,3584]{2,1,0:T(8,128)(2,1)}, u32[]{:S(2)}, u32[]{:S(2)}) async-start(bf16[4,48,3584]{2,1,0:T(8,128)(2,1)} %bitcast.111), calls=%async_computation.5 | async-start | bytes 2752512 | tf_op jit(solution)/shard_map/all_to_all | solution.py:283
  258.2 46.8 %collective-permute-start.19 = (bf16[256,3584]{1,0:T(8,128)(2,1)}, bf16[256,3584]{1,0:T(8,128)(2,1)}, u32[]{:S(2)}, u32[]{:S(2)}) collective-permute-start(bf16[256,3584]{1,0:T(8,128)(2,1)} %shard_map.114), channel_id=1, source_target_pairs={{0,16},{16,0},{1,17},{17,1},{2,18},{18,2},{3,19},{19,3},{4,20},{20... | collective-permute-start | bytes 5505032 | tf_op jit(solution)/shard_map/ppermute | solution.py:274
  258.8 7.5 %collective-permute-start.20 = (bf16[192,3584]{1,0:T(8,128)(2,1)}, bf16[192,3584]{1,0:T(8,128)(2,1)S(1)}, u32[]{:S(2)}, u32[]{:S(2)}) collective-permute-start(bf16[192,3584]{1,0:T(8,128)(2,1)} %collective-permute-done.15.refs_10_), channel_id=1, source_target_pairs={{0,1},{1,0},{2,3},{3,2},{4,5},{5,4},{6,7},{7,6},{8,9},{9,8},{10,11... | collective-permute-start | bytes 4128776 | tf_op jit(solution)/shard_map/ppermute | solution.py:265
  260.6 43.4 %collective-permute-start.18 = (bf16[128,3584]{1,0:T(8,128)(2,1)S(1)}, bf16[128,3584]{1,0:T(8,128)(2,1)S(1)}, u32[]{:S(2)}, u32[]{:S(2)}) collective-permute-start(bf16[128,3584]{1,0:T(8,128)(2,1)S(1)} %convolution_convert_fusion.2), channel_id=1, source_target_pairs={{0,8},{1,9},{2,10},{3,11},{4,12},{5,13},{6,14},{7,15},{8,0},{9,1},... | collective-permute-start | bytes 2752520 | tf_op jit(solution)/shard_map/ppermute | solution.py:265
  266.3 38.7 %copy-start.4 = (bf16[256,3584]{1,0:T(8,128)(2,1)S(1)}, bf16[256,3584]{1,0:T(8,128)(2,1)}, u32[]{:S(2)}) copy-start(bf16[256,3584]{1,0:T(8,128)(2,1)} %shard_map.115) | copy-start | bytes 5505028
  (17 other events, 59.3 us)

commit v9 on v8

--- a/solution.py
+++ b/solution.py
@@ -64,8 +64,26 @@
     return [slice(n * tile, (n + 1) * tile) for n in range(width // tile)]
 
 
-def forward(rows, gate_weight, up_weight, down_weight):
-    count, width = rows[0].shape
+def row_spec(rows, tile):
+    if isinstance(rows, tuple):
+        array, which = rows
+        return pl.BlockSpec(
+            (array.shape[0], 1, array.shape[2], tile), lambda n, *w: (0, which, 0, n * (tile < array.shape[3]))
+        )
+    return pl.BlockSpec((rows.shape[0], tile), lambda n, *w: (0, n * (tile < rows.shape[1])))
+
+
+def row_array(rows):
+    return rows[0] if isinstance(rows, tuple) else rows
+
+
+def flat(ref):
+    value = ref[...]
+    return value.reshape(-1, value.shape[-1])
+
+
+def forward(count, rows, gate_weight, up_weight, down_weight):
+    width = gate_weight.shape[0]
     half_units = gate_weight.shape[1] // 2
 
     def body(a_ref, b_ref, gate_ref, up_ref, down_ref, pre_gate_ref, pre_up_ref, hidden_ref, out_a, out_b, x_ref, acc_ref):
@@ -73,8 +91,8 @@
 
         @pl.when(step == 0)
         def _():
-            x_ref[:count] = a_ref[...]
-            x_ref[count:] = b_ref[...]
+            x_ref[:count] = flat(a_ref)
+            x_ref[count:] = flat(b_ref)
 
         pre_gate = dot(x_ref[...], gate_ref[...], NN)
         pre_up = dot(x_ref[...], up_ref[...], NN)
@@ -101,7 +119,8 @@
     return kernel_call(
         body,
         (2,),
-        [whole, whole, columns, columns, pl.BlockSpec((half_units, width), lambda n: (n, 0))],
+        [row_spec(a, width) for a in rows]
+        + [columns, columns, pl.BlockSpec((half_units, width), lambda n: (n, 0))],
         [units, units, units, whole, whole],
         [
             jax.ShapeDtypeStruct((2, 2 * count, half_units), F32),
@@ -111,11 +130,11 @@
             jax.ShapeDtypeStruct((count, width), BF16),
         ],
         [pltpu.VMEM((2 * count, width), BF16), pltpu.VMEM((2 * count, width), F32)],
-    )(*rows, gate_weight, up_weight, down_weight)
-
-
-def backward(rows_grad, pre_gate, pre_up, gate_weight, up_weight, down_weight):
-    count, width = rows_grad[0].shape
+    )(*map(row_array, rows), gate_weight, up_weight, down_weight)
+
+
+def backward(count, rows_grad, pre_gate, pre_up, gate_weight, up_weight, down_weight):
+    width = gate_weight.shape[0]
     half_units = gate_weight.shape[1] // 2
 
     def body(a_ref, b_ref, pre_gate_ref, pre_up_ref, gate_ref, up_ref, down_ref, units_ref, out_a, out_b, x_ref, acc_ref):
@@ -123,8 +142,8 @@
 
         @pl.when(step == 0)
         def _():
-            x_ref[:count] = a_ref[...]
-            x_ref[count:] = b_ref[...]
+            x_ref[:count] = flat(a_ref)
+            x_ref[count:] = flat(b_ref)
 
         hidden_grad = dot(x_ref[...], down_ref[...], NT)
         pre_gate = pre_gate_ref[0]
@@ -155,7 +174,8 @@
     return kernel_call(
         body,
         (2,),
-        [whole, whole, units, units, columns, columns, pl.BlockSpec((half_units, width), lambda n: (n, 0))],
+        [row_spec(a, width) for a in rows_grad]
+        + [units, units, columns, columns, pl.BlockSpec((half_units, width), lambda n: (n, 0))],
         [pl.BlockSpec((1, 2 * count, 2 * half_units), lambda n: (n, 0, 0)), whole, whole],
         [
             jax.ShapeDtypeStruct((2, 2 * count, 2 * half_units), BF16),
@@ -163,11 +183,11 @@
             jax.ShapeDtypeStruct((count, width), BF16),
         ],
         [pltpu.VMEM((2 * count, width), BF16), pltpu.VMEM((2 * count, width), F32)],
-    )(*rows_grad, pre_gate, pre_up, gate_weight, up_weight, down_weight)
-
-
-def down_grad(which, hiddens, rows_grad):
-    count, width = rows_grad[0].shape
+    )(*map(row_array, rows_grad), pre_gate, pre_up, gate_weight, up_weight, down_weight)
+
+
+def down_grad(count, which, hiddens, rows_grad):
+    width = row_array(rows_grad[0]).shape[-1]
     half_units = hiddens[0].shape[2]
     tile = tile_of(width)
 
@@ -180,7 +200,7 @@
             for n, unit_ref in enumerate(unit_refs):
                 turned_ref[:, 2 * n * count : 2 * (n + 1) * count] = unit_ref[0].T
 
-        rows = jnp.concatenate([ref[...] for ref in row_refs], axis=0)
+        rows = jnp.concatenate([flat(ref) for ref in row_refs], axis=0)
         total = dot(turned_ref[...], rows, NN)
         rest[-2][...] = total.astype(BF16)
 
@@ -189,16 +209,16 @@
         body,
         (width // tile,),
         [pl.BlockSpec((1, 2 * count, half_units), lambda n, w: (w[0], 0, 0))] * 2
-        + [pl.BlockSpec((count, tile), lambda n, w: (0, n))] * 4,
+        + [row_spec(a, tile) for a in rows_grad],
         out_spec,
         jax.ShapeDtypeStruct((half_units, width), BF16),
         [pltpu.VMEM((half_units, 4 * count), BF16)],
         scalars=1,
-    )(which, *hiddens, *rows_grad)
-
-
-def gate_up_grad(which, units, rows, mirror_units, mirror_rows):
-    count, width = rows[0].shape
+    )(which, *hiddens, *map(row_array, rows_grad))
+
+
+def gate_up_grad(count, which, units, rows, mirror_units, mirror_rows):
+    width = row_array(rows[0]).shape[-1]
     both = units[0].shape[2]
     half_units = both // 2
     tile = tile_of(width)
@@ -212,7 +232,7 @@
             for n, factor in enumerate([ref[0] for ref in unit_refs] + [ref[...] for ref in mirror_refs]):
                 turned_ref[:, 2 * n * count : 2 * (n + 1) * count] = factor.T
 
-        rows = jnp.concatenate([ref[...] for ref in row_refs], axis=0)
+        rows = jnp.concatenate([flat(ref) for ref in row_refs], axis=0)
         total = dot(turned_ref[...], rows, NN).astype(BF16).T
         gate_ref[...] = total[:, :half_units]
         up_ref[...] = total[:, half_units:]
@@ -223,12 +243,12 @@
         (width // tile,),
         [pl.BlockSpec((1, 2 * count, both), lambda n, w: (w[0], 0, 0))] * 2
         + [pl.BlockSpec((2 * count, both), lambda n, w: (0, 0))] * 2
-        + [pl.BlockSpec((count, tile), lambda n, w: (0, n))] * 8,
+        + [row_spec(a, tile) for a in (*rows, *mirror_rows)],
         [out_spec] * 2,
         [jax.ShapeDtypeStruct((width, half_units), BF16)] * 2,
         [pltpu.VMEM((both, 8 * count), BF16)],
         scalars=1,
-    )(which, *units, *mirror_units, *rows, *mirror_rows)
+    )(which, *units, *mirror_units, *map(row_array, (*rows, *mirror_rows)))
 
 
 def route(meta, half, expert_count, capacity):
@@ -295,98 +315,107 @@
     def expert_sum(mine, other):
         return (mine.astype(F32) + swap(other).astype(F32)).astype(BF16)
 
-    def both(own, other):
-        pair = [a.reshape(near, piece, width) for a in (own, other)]
-        return jnp.stack(pair, axis=1).reshape(2 * near * piece, width)
-
     def of_set(matrix, which):
         shaped = matrix.reshape(matrix.shape[0], near, 1, piece)
         pair = [jnp.zeros_like(shaped), shaped] if which else [shaped, jnp.zeros_like(shaped)]
         return jnp.concatenate(pair, axis=2).reshape(matrix.shape[0], 2 * near * piece)
 
+    count = near * piece
     first = acts.shape[1] // 4
+    far_acts_0 = far(acts[0, :first])
     meta = jnp.concatenate([expert_ids[0].astype(F32), route_weights[0]], axis=1)
+    own_placing, own_back, own_weighting, own_gain = route(meta, half, chips, capacity)
+    both_placing = jnp.concatenate([of_set(own_placing.T, 0), of_set(own_placing.T, 1)], axis=0).T
+    both_gain = jnp.stack([jnp.ones_like(own_gain).reshape(near, piece), own_gain.reshape(near, piece)], axis=1)
+    own = place(
+        both_placing, jnp.concatenate([acts[0], grad_out[0]], axis=0), both_gain.reshape(2 * count, 1)
+    )
+    own, far_acts_0, acts_1, meta = tie(own, far_acts_0, acts[0, first:], meta)
+
+    far_acts_1 = far(acts_1)
+    own = near_exchange(own)
     far_meta = far(meta)
-    far_acts_0 = far(acts[0, :first])
-    own_placing, own_back, own_weighting, own_gain = route(meta, half, chips, capacity)
-    own_in = place(own_placing, acts[0])
-    own_in, far_acts_0, far_meta, acts_1 = tie(own_in, far_acts_0, far_meta, acts[0, first:])
-
-    far_acts_1 = far(acts_1)
-    own_in = near_exchange(own_in)
     far_placing, far_back, far_weighting, far_gain = route(far_meta, half, chips, capacity)
-    far_acts_1, own_in, grads = tie(far_acts_1, own_in, grad_out[0])
+    far_acts_1, own, far_placing, far_gain, grads = tie(
+        far_acts_1, own, far_placing, far_gain, grad_out[0]
+    )
 
     far_grads = far(grads)
     far_in = place(far_placing, jnp.concatenate([far_acts_0, far_acts_1], axis=0))
     far_in = near_exchange(far_in)
-    own_in_b = swap(own_in)
-    mirror_own = mirror(own_in)
-    far_grads, far_in, own_in_b, mirror_own = tie(far_grads, far_in, own_in_b, mirror_own)
-
-    all_grads = near_exchange(
-        both(place(own_placing, grads, own_gain), place(far_placing, far_grads, far_gain))
-    )
+    own_b = swap(own)
+    own = own.reshape(near, 2, piece, width)
+    own_b = own_b.reshape(near, 2, piece, width)
+    mirror_own = mirror(own[:, 0].reshape(count, width))
+    own_pre_gate, own_pre_up, own_hidden, own_out, own_out_b = forward(
+        count, ((own, 0), (own_b, 0)), *weights
+    )
+    own_units, own_input, own_input_b = backward(
+        count, ((own, 1), (own_b, 1)), own_pre_gate, own_pre_up, *weights
+    )
+    far_grads, far_in, mirror_own, own_out, own_out_b, own_input, own_input_b = tie(
+        far_grads, far_in, mirror_own, own_out, own_out_b, own_input, own_input_b
+    )
+
+    far_grad = near_exchange(place(far_placing, far_grads, far_gain))
     far_in_b = swap(far_in)
-    mirror_own_b = swap(mirror_own)
-    own_pre_gate, own_pre_up, own_hidden, own_out, own_out_b = forward((own_in, own_in_b), *weights)
-    far_pre_gate, far_pre_up, far_hidden, far_out, far_out_b = forward((far_in, far_in_b), *weights)
-    all_grads, mirror_own_b, own_out, own_out_b, far_out, far_out_b = tie(
-        all_grads, mirror_own_b, own_out, own_out_b, far_out, far_out_b
-    )
-
+    mirror_far = mirror(far_in)
     own_out = expert_sum(own_out, own_out_b)
+    far_pre_gate, far_pre_up, far_hidden, far_out, far_out_b = forward(
+        count, (far_in, far_in_b), *weights
+    )
+    far_grad, far_out, far_out_b, own_out, mirror_far, mirror_own = tie(
+        far_grad, far_out, far_out_b, own_out, mirror_far, mirror_own
+    )
+
     far_out = expert_sum(far_out, far_out_b)
-    all_grads = all_grads.reshape(near, 2, piece, width)
-    own_grad = all_grads[:, 0].reshape(near * piece, width)
-    far_grad = all_grads[:, 1].reshape(near * piece, width)
-    own_out, far_out, own_grad, far_grad = tie(own_out, far_out, own_grad, far_grad)
-
-    all_out = near_exchange(both(own_out, far_out))
+    far_out, far_grad, own_input, own_input_b = tie(far_out, far_grad, own_input, own_input_b)
+
+    far_out = near_exchange(far_out)
     far_grad_b = swap(far_grad)
-    own_grad_b = swap(own_grad)
+    own_input = expert_sum(own_input, own_input_b)
     far_units, far_input, far_input_b = backward(
-        (far_grad, far_grad_b), far_pre_gate, far_pre_up, *weights
-    )
-    own_units, own_input, own_input_b = backward(
-        (own_grad, own_grad_b), own_pre_gate, own_pre_up, *weights
-    )
-    all_out, far_units, far_input, far_input_b, own_units, own_input, own_input_b = tie(
-        all_out, far_units, far_input, far_input_b, own_units, own_input, own_input_b
+        count, (far_grad, far_grad_b), far_pre_gate, far_pre_up, *weights
+    )
+    far_out, far_units, far_input, far_input_b, own_input = tie(
+        far_out, far_units, far_input, far_input_b, own_input
     )
 
     far_input = expert_sum(far_input, far_input_b)
-    own_input = expert_sum(own_input, own_input_b)
-    far_input, own_input, all_out, far_units, own_units, mirror_far, own_grad_b = tie(
-        far_input, own_input, all_out, far_units, own_units, far_in, own_grad_b
-    )
-
-    got_out = far(combine(of_set(far_weighting, 1), all_out).astype(BF16))
-    far_input = near_exchange(far_input)
-    mirror_far = mirror(mirror_far)
+    back_out = combine(far_weighting, far_out).astype(BF16)
+    far_input, back_out, own_units, far_units, far_grad_b, mirror_own, mirror_far = tie(
+        far_input, back_out, own_units, far_units, far_grad_b, mirror_own, mirror_far
+    )
+
+    got_out = far(back_out)
+    back = near_exchange(
+        jnp.stack([a.reshape(near, piece, width) for a in (far_input, own_out)], axis=1).reshape(2 * count, width)
+    )
     mirror_units = [
         mirror(lax.dynamic_index_in_dim(units, 1 - kept_half, 0, keepdims=False))
         for units in (own_units, far_units)
     ]
-    rows_grad = (own_grad, own_grad_b, far_grad, far_grad_b)
-    send_down = down_grad(1 - kept, (own_hidden, far_hidden), rows_grad)
-    keep_down = down_grad(kept, (own_hidden, far_hidden), rows_grad)
-    got_out, far_input, mirror_far, mirror_own_units, mirror_far_units, send_down, keep_down, own_input = tie(
-        got_out, far_input, mirror_far, *mirror_units, send_down, keep_down, own_input
-    )
-
-    got_input = far(combine(far_back, far_input).astype(BF16))
+    mirror_own_b = swap(mirror_own)
+    mirror_far_b = swap(mirror_far)
+    rows_grad = ((own, 1), (own_b, 1), far_grad, far_grad_b)
+    send_down = down_grad(count, 1 - kept, (own_hidden, far_hidden), rows_grad)
+    keep_down = down_grad(count, kept, (own_hidden, far_hidden), rows_grad)
+    got_out, back, mirror_own_units, mirror_far_units, mirror_own_b, mirror_far_b, send_down, keep_down, own_input = tie(
+        got_out, back, *mirror_units, mirror_own_b, mirror_far_b, send_down, keep_down, own_input
+    )
+
+    got_input = far(combine(of_set(far_back, 0), back).astype(BF16))
     own_input = near_exchange(own_input)
     got_down = mirror(send_down)
-    mirror_far_b = swap(mirror_far)
     grad_gate, grad_up = gate_up_grad(
+        count,
         kept,
         (own_units, far_units),
-        (own_in, own_in_b, far_in, far_in_b),
+        ((own, 0), (own_b, 0), far_in, far_in_b),
         (mirror_own_units, mirror_far_units),
         (mirror_own, mirror_own_b, mirror_far, mirror_far_b),
     )
-    out_acts = (combine(of_set(own_weighting, 0), all_out) + got_out.astype(F32)).astype(BF16)
+    out_acts = (combine(of_set(own_weighting, 1), back) + got_out.astype(F32)).astype(BF16)
     got_input, own_input, got_down, grad_gate, grad_up, out_acts = tie(
         got_input, own_input, got_down, grad_gate, grad_up, out_acts
     )

time: 312 us -> 309 us (level)
  local copies, waits for them, and re-layouts: 15.1 us -> 10.1 us
  other arithmetic: 15.1 us -> 18.3 us
    ppermute x16 -> x15, waiting for transfers between devices: 110 us -> 120 us  [hop(): lax.ppermute(rows, 'expert', [(i, i ^ distance) for i in range(devices)])]
    ppermute x5, waiting for transfers between devices: 25.1 us -> 17.5 us  [mirror(): lax.ppermute(rows, 'pipe', [(p, rank_count - 1 - p) for p in range(rank_c...]
    all_to_all x6, waiting for transfers between devices: 12.2 us -> 6.66 us  [near_exchange(): lax.all_to_all(rows.reshape(near, -1, width), 'expert', split_axis=0, con...]
    slice x1, local copies, waits for them, and re-layouts: 3.56 us -> 0.1 us  [on_device(): mirror_own = mirror(own[:, 0].reshape(count, width))]
    unnamed x44 -> x42, local copies, waits for them, and re-layouts: 7.38 us -> 4.73 us
    dot_general x6 -> x5, matrix products: 12.7 us -> 12 us  [dot(): return lax.dot_general(a, b, (dims, ((), ())), preferred_element_type=F32)]
    ppermute x16 -> x15, starting transfers between devices: 12.1 us -> 11.6 us  [hop(): lax.ppermute(rows, 'expert', [(i, i ^ distance) for i in range(devices)])]
  transfers between devices with their start and end apart: 27 -> 26, of which waited for: 11 -> 12; matrix products, arithmetic and copies ran while one was open for 8% -> 10% of each run, Pallas kernels for 23% -> 23%
where the time goes in v9:
time: 309 us; the launch traced here: 307 us
  waiting for transfers between devices  145 us (47%)
  Pallas kernels  71 us (23%)
  starting transfers between devices  43.4 us (14%)
  matrix products  18.9 us (6%)
  other arithmetic  18.3 us (6%)
  local copies, waits for them, and re-layouts  10.1 us (3%)
    ppermute x15, waiting for transfers between devices, hop(): lax.ppermute(rows, 'expert', [(i, i ^ distance) for i in range(devices)])  120 us
    all_to_all x6, starting transfers between devices, near_exchange(): lax.all_to_all(rows.reshape(near, -1, width), 'expert', split_axis=0, con...  25.5 us
    pallas_call x2, Pallas kernels, backward(): kernel_call(body, (2,), [row_spec(a, width) for a in rows_grad] + [units,...  22.2 us
    pallas_call x2, Pallas kernels, forward(): kernel_call(body, (2,), [row_spec(a, width) for a in rows] + [columns, co...  21.5 us
    ppermute x5, waiting for transfers between devices, mirror(): lax.ppermute(rows, 'pipe', [(p, rank_count - 1 - p) for p in range(rank_c...  17.5 us
    pallas_call x2, Pallas kernels, down_grad(): kernel_call(body, (width // tile,), [pl.BlockSpec((1, 2 * count, half_uni...  15.2 us
    pallas_call x1, Pallas kernels, gate_up_grad(): kernel_call(body, (width // tile,), [pl.BlockSpec((1, 2 * count, both), l...  12.1 us
    dot_general x5, matrix products, dot(): return lax.dot_general(a, b, (dims, ((), ())), preferred_element_type=F32)  12 us
  transfers between devices with their start and end apart: 26, of which 12 were waited for; matrix products, arithmetic and copies ran while one was open for 10% of the time, Pallas kernels for 23%

profile of v9, /device:TPU:0, one launch (start us, length us, event | category | flops | bytes accessed | tf_op | source)
XLA Modules:
  0.0 307.4 jit_solution(1254026583822669947)
XLA Ops:
  1.8 4.1 %collective-permute-start = (bf16[32,3584]{1,0:T(8,128)(2,1)S(1)}, bf16[32,3584]{1,0:T(8,128)(2,1)S(1)}, u32[]{:S(2)}, u32[]{:S(2)}) collective-permute-start(bf16[32,3584]{1,0:T(8,128)(2,1)S(1)} %slice_bitcast_fusion.1), channel_id=1, source_target_pairs={{0,8},{1,9},{2,10},{3,11},{4,12},{5,13},{6,14},{7,15},{8,0},{9,1},... | collective-permute-start | bytes 688136 | tf_op jit(solution)/shard_map/ppermute | solution.py:285
  8.5 2.4 fusion
  10.9 5.5 %collective-permute-done = bf16[32,3584]{1,0:T(8,128)(2,1)S(1)} collective-permute-done((bf16[32,3584]{1,0:T(8,128)(2,1)S(1)}, bf16[32,3584]{1,0:T(8,128)(2,1)S(1)}, u32[]{:S(2)}, u32[]{:S(2)}) %collective-permute-start) | collective-permute-done | bytes 229408 | tf_op jit(solution)/shard_map/ppermute | solution.py:285
  17.1 3.7 %all-to-all-start = ((bf16[4,96,3584]{2,1,0:T(8,128)(2,1)}), bf16[4,96,3584]{2,1,0:T(8,128)(2,1)S(1)}, u32[]{:S(2)}, u32[]{:S(2)}) async-start(bf16[4,96,3584]{2,1,0:T(8,128)(2,1)} %bitcast.109), calls=%async_computation | async-start | bytes 5505024 | tf_op jit(solution)/shard_map/all_to_all | solution.py:303
  20.7 2.7 collective-permute-start.1
  23.7 28.0 %collective-permute-done.1 = f32[128,4]{0,1:T(4,128)S(1)} collective-permute-done((f32[128,4]{0,1:T(4,128)S(1)}, f32[128,4]{0,1:T(4,128)S(1)}, u32[]{:S(2)}, u32[]{:S(2)}) %collective-permute-start.1) | collective-permute-done | bytes 2080 | tf_op jit(solution)/shard_map/ppermute | solution.py:285
  55.9 9.0 %collective-permute-done.2 = bf16[96,3584]{1,0:T(8,128)(2,1)} collective-permute-done((bf16[96,3584]{1,0:T(8,128)(2,1)S(1)}, bf16[96,3584]{1,0:T(8,128)(2,1)}, u32[]{:S(2)}, u32[]{:S(2)}) %collective-permute-start.2) | collective-permute-done | bytes 688160 | tf_op jit(solution)/shard_map/ppermute | solution.py:285
  67.1 3.4 %convolution_convert_fusion = bf16[192,3584]{1,0:T(8,128)(2,1)} fusion(bf16[192,128]{1,0:T(8,128)(2,1)S(1)} %get-tuple-element.79, bf16[96,3584]{1,0:T(8,128)(2,1)} %collective-permute-done.2, bf16[32,3584]{1,0:T(8,128)(2,1)} %copy-done.15), kind=kOutput, calls=%fused_computation.4 | convolution fusion | flops 178683904 | bytes 2342912 | tf_op jit(solution)/shard_map/dot_general | solution.py:20
  70.5 5.4 %all-to-all-start.1 = ((bf16[4,48,3584]{2,1,0:T(8,128)(2,1)}), bf16[4,48,3584]{2,1,0:T(8,128)(2,1)}, u32[]{:S(2)}, u32[]{:S(2)}) async-start(bf16[4,48,3584]{2,1,0:T(8,128)(2,1)} %bitcast.106), calls=%async_computation.1 | async-start | bytes 2752512 | tf_op jit(solution)/shard_map/all_to_all | solution.py:303
  78.1 10.5 %shard_map.110 = (f32[2,384,256]{2,1,0:T(8,128)}, f32[2,384,256]{2,1,0:T(8,128)}, bf16[2,384,256]{2,1,0:T(8,128)(2,1)}, bf16[192,3584]{1,0:T(8,128)(2,1)}, bf16[192,3584]{1,0:T(8,128)(2,1)}) custom-call(bf16[4,2,48,3584]{3,2,1,0:T(8,128)(2,1)} %bitcast.80, bf16[4,2,48,3584]{3,2,1,0:T(8,128)(2,1)} %bitcast.26.b_ref.refs_3_.refs_5_, ...), custom_call_target="tpu_custom_call" | custom-call | flops 1 | bytes 1 | tf_op jit(solution)/shard_map/pallas_call | solution.py:119
  88.5 10.8 %shard_map.111 = (bf16[2,384,512]{2,1,0:T(8,128)(2,1)}, bf16[192,3584]{1,0:T(8,128)(2,1)}, bf16[192,3584]{1,0:T(8,128)(2,1)}) custom-call(bf16[4,2,48,3584]{3,2,1,0:T(8,128)(2,1)} %bitcast.81, bf16[4,2,48,3584]{3,2,1,0:T(8,128)(2,1)} %bitcast.26.b_ref.refs_3_.refs_5_, f32[2,384,256]{2,1,0:T(8,128)} %get-tuple-element.86.pre_gate_ref, ...), custom_call_target="tpu_custom_call" | custom-call | flops 1 | bytes 1 | tf_op jit(solution)/shard_map/pallas_call | solution.py:174
  99.3 20.5 %collective-permute-done.3 = bf16[128,3584]{1,0:T(8,128)(2,1)} collective-permute-done((bf16[128,3584]{1,0:T(8,128)(2,1)S(1)}, bf16[128,3584]{1,0:T(8,128)(2,1)}, u32[]{:S(2)}, u32[]{:S(2)}) %collective-permute-start.3) | collective-permute-done | bytes 917536 | tf_op jit(solution)/shard_map/ppermute | solution.py:285
  120.4 2.8 fusion.1
  123.2 3.7 %all-to-all-start.2 = ((bf16[4,48,3584]{2,1,0:T(8,128)(2,1)}), bf16[4,48,3584]{2,1,0:T(8,128)(2,1)S(1)}, u32[]{:S(2)}, u32[]{:S(2)}) async-start(bf16[4,48,3584]{2,1,0:T(8,128)(2,1)} %bitcast.31), calls=%async_computation.2 | async-start | bytes 2752512 | tf_op jit(solution)/shard_map/all_to_all | solution.py:303
  129.3 11.0 %shard_map.112 = (f32[2,384,256]{2,1,0:T(8,128)}, f32[2,384,256]{2,1,0:T(8,128)}, bf16[2,384,256]{2,1,0:T(8,128)(2,1)}, bf16[192,3584]{1,0:T(8,128)(2,1)}, bf16[192,3584]{1,0:T(8,128)(2,1)}) custom-call(bf16[192,3584]{1,0:T(8,128)(2,1)} %bitcast.23.a_ref.refs_6_, bf16[192,3584]{1,0:T(8,128)(2,1)} %copy-done.4, bf16[3584,512]{1,0:T(8,128)(2,1)} %bitcast.87, ...), custom_call_target="tpu_custom_call" | custom-call | flops 1 | bytes 1 | tf_op jit(solution)/shard_map/pallas_call | solution.py:119
  140.4 2.8 add_convert_fusion.4
  143.2 16.2 %collective-permute-done.8.refs_10_ = bf16[192,3584]{1,0:T(8,128)(2,1)} collective-permute-done((bf16[192,3584]{1,0:T(8,128)(2,1)}, bf16[192,3584]{1,0:T(8,128)(2,1)}, u32[]{:S(2)}, u32[]{:S(2)}) %collective-permute-start.8) | collective-permute-done | bytes 1376288 | tf_op jit(solution)/shard_map/ppermute | solution.py:294
  159.5 3.3 %collective-permute-done.9 = bf16[192,3584]{1,0:T(8,128)(2,1)S(1)} collective-permute-done((bf16[192,3584]{1,0:T(8,128)(2,1)}, bf16[192,3584]{1,0:T(8,128)(2,1)S(1)}, u32[]{:S(2)}, u32[]{:S(2)}) %collective-permute-start.9) | collective-permute-done | bytes 1376288 | tf_op jit(solution)/shard_map/ppermute | solution.py:285
  164.8 4.3 %all-to-all-start.3 = ((bf16[4,48,3584]{2,1,0:T(8,128)(2,1)}), bf16[4,48,3584]{2,1,0:T(8,128)(2,1)}, u32[]{:S(2)}, u32[]{:S(2)}) async-start(bf16[4,48,3584]{2,1,0:T(8,128)(2,1)} %bitcast.107), calls=%async_computation.3 | async-start | bytes 2752512 | tf_op jit(solution)/shard_map/all_to_all | solution.py:303
  170.3 11.4 %shard_map.113 = (bf16[2,384,512]{2,1,0:T(8,128)(2,1)}, bf16[192,3584]{1,0:T(8,128)(2,1)}, bf16[192,3584]{1,0:T(8,128)(2,1)}) custom-call(bf16[192,3584]{1,0:T(8,128)(2,1)} %bitcast.100, bf16[192,3584]{1,0:T(8,128)(2,1)} %copy-done.2, f32[2,384,256]{2,1,0:T(8,128)} %get-tuple-element.105.pre_gate_ref, f32[2,384,256]{2,1,0:T(8,128)} %get-tuple-element.106.pre_up_ref, ...), custom_call_target="tpu_custom_call" | custom-call | flops 1 | bytes 1 | tf_op jit(solution)/shard_map/pallas_call | solution.py:174
  181.7 2.8 add_convert_fusion.2
  187.6 3.2 %convolution_convert_fusion.2 = bf16[128,3584]{1,0:T(8,128)(2,1)} fusion(f32[128,192]{0,1:T(8,128)S(1)} %get-tuple-element.149, bf16[192,3584]{1,0:T(8,128)(2,1)} %bitcast.34), kind=kOutput, calls=%fused_computation.10 | convolution fusion | flops 1057423360 | bytes 2392064 | tf_op jit(solution)/shard_map/dot_general | solution.py:53
  194.0 3.8 %all-to-all-start.4 = ((bf16[4,96,3584]{2,1,0:T(8,128)(2,1)}), bf16[4,96,3584]{2,1,0:T(8,128)(2,1)S(1)}, u32[]{:S(2)}, u32[]{:S(2)}) async-start(bf16[4,96,3584]{2,1,0:T(8,128)(2,1)} %bitcast.103), calls=%async_computation.4 | async-start | bytes 5505024 | tf_op jit(solution)/shard_map/all_to_all | solution.py:303
  202.6 7.6 %shard_map.115 = bf16[256,3584]{1,0:T(8,128)(2,1)} custom-call(s32[1]{0:T(128)} %bitcast.43.which_ref, bf16[2,384,256]{2,1,0:T(8,128)(2,1)} %get-tuple-element.126.refs_0_, bf16[2,384,256]{2,1,0:T(8,128)(2,1)} %get-tuple-element.127.refs_1_, bf16[4,2,48,3584]{3,2,1,0:T(8,128)(2,1)} %bitcast.82, bf16[4,2,48,3584]{3,2,1,0:T(8,128)(2,1)} %bitcast.26.b_ref.refs_3_.refs_5_, ...), custom_call_target="tpu_custom_call" | custom-call | flops 1 | bytes 1 | tf_op jit(solution)/shard_map/pallas_call | solution.py:208
  210.2 7.6 %shard_map.114 = bf16[256,3584]{1,0:T(8,128)(2,1)} custom-call(s32[1]{0:T(128)S(6)} %sub.37.which_ref, bf16[2,384,256]{2,1,0:T(8,128)(2,1)} %get-tuple-element.126.refs_0_, bf16[2,384,256]{2,1,0:T(8,128)(2,1)} %get-tuple-element.127.refs_1_, bf16[4,2,48,3584]{3,2,1,0:T(8,128)(2,1)} %bitcast.83, bf16[4,2,48,3584]{3,2,1,0:T(8,128)(2,1)} %bitcast.26.b_ref.refs_3_.refs_5_, ...), custom_call_target="tpu_custom_call" | custom-call | flops 1 | bytes 1 | tf_op jit(solution)/shard_map/pallas_call | solution.py:208
  219.1 29.1 %collective-permute-done.13 = bf16[128,3584]{1,0:T(8,128)(2,1)} collective-permute-done((bf16[128,3584]{1,0:T(8,128)(2,1)}, bf16[128,3584]{1,0:T(8,128)(2,1)}, u32[]{:S(2)}, u32[]{:S(2)}) %collective-permute-start.13) | collective-permute-done | bytes 917536 | tf_op jit(solution)/shard_map/ppermute | solution.py:285
  250.2 4.5 %all-to-all-start.5 = ((bf16[4,48,3584]{2,1,0:T(8,128)(2,1)}), bf16[4,48,3584]{2,1,0:T(8,128)(2,1)}, u32[]{:S(2)}, u32[]{:S(2)}) async-start(bf16[4,48,3584]{2,1,0:T(8,128)(2,1)} %bitcast.104), calls=%async_computation.5 | async-start | bytes 2752512 | tf_op jit(solution)/shard_map/all_to_all | solution.py:303
  259.1 12.1 %shard_map.116 = (bf16[3584,256]{1,0:T(8,128)(2,1)}, bf16[3584,256]{1,0:T(8,128)(2,1)}) custom-call(s32[1]{0:T(128)} %bitcast.43.which_ref, bf16[2,384,512]{2,1,0:T(8,128)(2,1)} %get-tuple-element.122.refs_0_, bf16[2,384,512]{2,1,0:T(8,128)(2,1)} %get-tuple-element.123.refs_1_, bf16[384,512]{1,0:T(8,128)(2,1)} %copy-done.13, bf16[384,512]{1,0:T(8,128)(2,1)} %copy-done.14, ...), custom_call_target="tpu_custom_call" | custom-call | flops 1 | bytes 1 | tf_op jit(solution)/shard_map/pallas_call | solution.py:241
  271.2 3.8 %fusion.2 = bf16[128,3584]{1,0:T(8,128)(2,1)} fusion(f32[128,384]{0,1:T(8,128)S(1)} %bitcast.113, bf16[384,3584]{1,0:T(8,128)(2,1)S(1)} %bitcast.98, bf16[128,3584]{1,0:T(8,128)(2,1)} %collective-permute-done.13), kind=kOutput, calls=%fused_computation.7 | convolution fusion | flops 2115305472 | bytes 4784128 | tf_op jit(solution)/shard_map/dot_general | solution.py:53
  274.9 25.0 %collective-permute-done.18 = bf16[128,3584]{1,0:T(8,128)(2,1)S(1)} collective-permute-done((bf16[128,3584]{1,0:T(8,128)(2,1)S(1)}, bf16[128,3584]{1,0:T(8,128)(2,1)S(1)}, u32[]{:S(2)}, u32[]{:S(2)}) %collective-permute-start.18) | collective-permute-done | bytes 917536 | tf_op jit(solution)/shard_map/ppermute | solution.py:285
  300.9 3.8 %fusion.5 = bf16[1,256,3584]{2,1,0:T(8,128)(2,1)} fusion(bf16[256,3584]{1,0:T(8,128)(2,1)} %collective-permute-done.19, bf16[256,3584]{1,0:T(8,128)(2,1)} %shard_map.115), kind=kLoop, calls=%fused_computation.18 | loop fusion | flops 3670016 | bytes 5505024 | tf_op jit(solution)/shard_map/broadcast_in_dim | solution.py:425
  304.7 2.7 fusion.4
  (118 shorter events, 38.7 us)
Async XLA Ops:
  1.8 14.6 %collective-permute-start = (bf16[32,3584]{1,0:T(8,128)(2,1)S(1)}, bf16[32,3584]{1,0:T(8,128)(2,1)S(1)}, u32[]{:S(2)}, u32[]{:S(2)}) collective-permute-start(bf16[32,3584]{1,0:T(8,128)(2,1)S(1)} %slice_bitcast_fusion.1), channel_id=1, source_target_pairs={{0,8},{1,9},{2,10},{3,11},{4,12},{5,13},{6,14},{7,15},{8,0},{9,1},... | collective-permute-start | bytes 688136 | tf_op jit(solution)/shard_map/ppermute | solution.py:285
  17.1 50.0 %all-to-all-start = ((bf16[4,96,3584]{2,1,0:T(8,128)(2,1)}), bf16[4,96,3584]{2,1,0:T(8,128)(2,1)S(1)}, u32[]{:S(2)}, u32[]{:S(2)}) async-start(bf16[4,96,3584]{2,1,0:T(8,128)(2,1)} %bitcast.109), calls=%async_computation | async-start | bytes 5505024 | tf_op jit(solution)/shard_map/all_to_all | solution.py:303
  20.7 31.0 %collective-permute-start.1 = (f32[128,4]{0,1:T(4,128)S(1)}, f32[128,4]{0,1:T(4,128)S(1)}, u32[]{:S(2)}, u32[]{:S(2)}) collective-permute-start(f32[128,4]{0,1:T(4,128)S(1)} %pad_maximum_fusion.1), channel_id=1, source_target_pairs={{0,8},{1,9},{2,10},{3,11},{4,12},{5,13},{6,14},{7,15},{8,0},{9,1},... | collective-permute-start | bytes 6152 | tf_op jit(solution)/shard_map/ppermute | solution.py:285
  23.4 41.5 %collective-permute-start.2 = (bf16[96,3584]{1,0:T(8,128)(2,1)S(1)}, bf16[96,3584]{1,0:T(8,128)(2,1)}, u32[]{:S(2)}, u32[]{:S(2)}) collective-permute-start(bf16[96,3584]{1,0:T(8,128)(2,1)S(1)} %slice_bitcast_fusion), channel_id=1, source_target_pairs={{0,8},{1,9},{2,10},{3,11},{4,12},{5,13},{6,14},{7,15},{8,0},{9,1},... | collective-permute-start | bytes 2064392 | tf_op jit(solution)/shard_map/ppermute | solution.py:285
  67.1 8.8 %copy-start = (bf16[4,96,3584]{2,1,0:T(8,128)(2,1)}, bf16[4,96,3584]{2,1,0:T(8,128)(2,1)S(1)}, u32[]{:S(2)}) copy-start(bf16[4,96,3584]{2,1,0:T(8,128)(2,1)S(1)} %all-to-all-done) | copy-start | bytes 8257540
  67.1 10.9 %collective-permute-start.5 = (bf16[384,3584]{1,0:T(8,128)(2,1)S(1)}, bf16[384,3584]{1,0:T(8,128)(2,1)}, u32[]{:S(2)}, u32[]{:S(2)}) collective-permute-start(bf16[384,3584]{1,0:T(8,128)(2,1)S(1)} %bitcast.78), channel_id=1, source_target_pairs={{0,1},{1,0},{2,3},{3,2},{4,5},{5,4},{6,7},{7,6},{8,9},{9,8},{10,11... | collective-permute-start | bytes 8257544 | tf_op jit(solution)/shard_map/ppermute | solution.py:285
  70.5 49.4 %all-to-all-start.1 = ((bf16[4,48,3584]{2,1,0:T(8,128)(2,1)}), bf16[4,48,3584]{2,1,0:T(8,128)(2,1)}, u32[]{:S(2)}, u32[]{:S(2)}) async-start(bf16[4,48,3584]{2,1,0:T(8,128)(2,1)} %bitcast.106), calls=%async_computation.1 | async-start | bytes 2752512 | tf_op jit(solution)/shard_map/all_to_all | solution.py:303
  76.1 43.8 %collective-permute-start.4 = (bf16[192,3584]{1,0:T(8,128)(2,1)S(1)}, bf16[192,3584]{1,0:T(8,128)(2,1)}, u32[]{:S(2)}, u32[]{:S(2)}) collective-permute-start(bf16[192,3584]{1,0:T(8,128)(2,1)S(1)} %bitcast.110), channel_id=1, source_target_pairs={{0,16},{16,0},{1,17},{17,1},{2,18},{18,2},{3,19},{19,3},{4,20},{20... | collective-permute-start | bytes 4128776 | tf_op jit(solution)/shard_map/ppermute | solution.py:294
  77.6 42.3 %collective-permute-start.3 = (bf16[128,3584]{1,0:T(8,128)(2,1)S(1)}, bf16[128,3584]{1,0:T(8,128)(2,1)}, u32[]{:S(2)}, u32[]{:S(2)}) collective-permute-start(bf16[128,3584]{1,0:T(8,128)(2,1)S(1)} %bitcast.128), channel_id=1, source_target_pairs={{0,8},{1,9},{2,10},{3,11},{4,12},{5,13},{6,14},{7,15},{8,0},{9,1},... | collective-permute-start | bytes 2752520 | tf_op jit(solution)/shard_map/ppermute | solution.py:285
  119.9 8.4 %collective-permute-start.6 = (bf16[192,3584]{1,0:T(8,128)(2,1)}, bf16[192,3584]{1,0:T(8,128)(2,1)S(1)}, u32[]{:S(2)}, u32[]{:S(2)}) collective-permute-start(bf16[192,3584]{1,0:T(8,128)(2,1)} %bitcast.23.a_ref.refs_6_), channel_id=1, source_target_pairs={{0,1},{1,0},{2,3},{3,2},{4,5},{5,4},{6,7},{7,6},{8,9},{9,8},{10,11... | collective-permute-start | bytes 4128776 | tf_op jit(solution)/shard_map/ppermute | solution.py:285
  119.9 20.5 %collective-permute-start.7 = (bf16[192,3584]{1,0:T(8,128)(2,1)}, bf16[192,3584]{1,0:T(8,128)(2,1)}, u32[]{:S(2)}, u32[]{:S(2)}) collective-permute-start(bf16[192,3584]{1,0:T(8,128)(2,1)} %get-tuple-element.96), channel_id=1, source_target_pairs={{0,1},{1,0},{2,3},{3,2},{4,5},{5,4},{6,7},{7,6},{8,9},{9,8},{10,11... | collective-permute-start | bytes 4128776 | tf_op jit(solution)/shard_map/ppermute | solution.py:285
  123.2 36.3 %all-to-all-start.2 = ((bf16[4,48,3584]{2,1,0:T(8,128)(2,1)}), bf16[4,48,3584]{2,1,0:T(8,128)(2,1)S(1)}, u32[]{:S(2)}, u32[]{:S(2)}) async-start(bf16[4,48,3584]{2,1,0:T(8,128)(2,1)} %bitcast.31), calls=%async_computation.2 | async-start | bytes 2752512 | tf_op jit(solution)/shard_map/all_to_all | solution.py:303
  126.9 13.5 %copy-start.7 = (bf16[192,3584]{1,0:T(8,128)(2,1)S(1)}, bf16[192,3584]{1,0:T(8,128)(2,1)}, u32[]{:S(2)}) copy-start(bf16[192,3584]{1,0:T(8,128)(2,1)} %get-tuple-element.95) | copy-start | bytes 4128772
  126.9 32.5 %collective-permute-start.8 = (bf16[192,3584]{1,0:T(8,128)(2,1)}, bf16[192,3584]{1,0:T(8,128)(2,1)}, u32[]{:S(2)}, u32[]{:S(2)}) collective-permute-start(bf16[192,3584]{1,0:T(8,128)(2,1)} %bitcast.23.a_ref.refs_6_), channel_id=1, source_target_pairs={{0,16},{16,0},{1,17},{17,1},{2,18},{18,2},{3,19},{19,3},{4,20},{20... | collective-permute-start | bytes 4128776 | tf_op jit(solution)/shard_map/ppermute | solution.py:294
  140.3 22.5 %copy-start.9 = (bf16[192,3584]{1,0:T(8,128)(2,1)S(1)}, bf16[192,3584]{1,0:T(8,128)(2,1)}, u32[]{:S(2)}) copy-start(bf16[192,3584]{1,0:T(8,128)(2,1)} %get-tuple-element.98) | copy-start | bytes 4128772
  159.5 3.3 %collective-permute-start.9 = (bf16[192,3584]{1,0:T(8,128)(2,1)}, bf16[192,3584]{1,0:T(8,128)(2,1)S(1)}, u32[]{:S(2)}, u32[]{:S(2)}) collective-permute-start(bf16[192,3584]{1,0:T(8,128)(2,1)} %get-tuple-element.99), channel_id=1, source_target_pairs={{0,1},{1,0},{2,3},{3,2},{4,5},{5,4},{6,7},{7,6},{8,9},{9,8},{10,11... | collective-permute-start | bytes 4128776 | tf_op jit(solution)/shard_map/ppermute | solution.py:285
  164.3 4.8 %collective-permute-start.10 = (bf16[192,3584]{1,0:T(8,128)(2,1)S(1)}, bf16[192,3584]{1,0:T(8,128)(2,1)S(1)}, u32[]{:S(2)}, u32[]{:S(2)}) collective-permute-start(bf16[192,3584]{1,0:T(8,128)(2,1)S(1)} %bitcast.99), channel_id=1, source_target_pairs={{0,1},{1,0},{2,3},{3,2},{4,5},{5,4},{6,7},{7,6},{8,9},{9,8},{10,11... | collective-permute-start | bytes 4128776 | tf_op jit(solution)/shard_map/ppermute | solution.py:285
  164.5 17.2 %collective-permute-start.11 = (bf16[192,3584]{1,0:T(8,128)(2,1)}, bf16[192,3584]{1,0:T(8,128)(2,1)}, u32[]{:S(2)}, u32[]{:S(2)}) collective-permute-start(bf16[192,3584]{1,0:T(8,128)(2,1)} %get-tuple-element.111), channel_id=1, source_target_pairs={{0,1},{1,0},{2,3},{3,2},{4,5},{5,4},{6,7},{7,6},{8,9},{9,8},{10,11... | collective-permute-start | bytes 4128776 | tf_op jit(solution)/shard_map/ppermute | solution.py:285
  164.8 22.1 %all-to-all-start.3 = ((bf16[4,48,3584]{2,1,0:T(8,128)(2,1)}), bf16[4,48,3584]{2,1,0:T(8,128)(2,1)}, u32[]{:S(2)}, u32[]{:S(2)}) async-start(bf16[4,48,3584]{2,1,0:T(8,128)(2,1)} %bitcast.107), calls=%async_computation.3 | async-start | bytes 2752512 | tf_op jit(solution)/shard_map/all_to_all | solution.py:303
  170.3 11.4 %copy-start.6 = (bf16[192,3584]{1,0:T(8,128)(2,1)S(1)}, bf16[192,3584]{1,0:T(8,128)(2,1)}, u32[]{:S(2)}) copy-start(bf16[192,3584]{1,0:T(8,128)(2,1)} %get-tuple-element.110) | copy-start | bytes 4128772
  187.0 3.8 %collective-permute-start.12 = (bf16[192,3584]{1,0:T(8,128)(2,1)S(1)}, bf16[192,3584]{1,0:T(8,128)(2,1)S(1)}, u32[]{:S(2)}, u32[]{:S(2)}) collective-permute-start(bf16[192,3584]{1,0:T(8,128)(2,1)S(1)} %copy-done.18), channel_id=1, source_target_pairs={{0,1},{1,0},{2,3},{3,2},{4,5},{5,4},{6,7},{7,6},{8,9},{9,8},{10,11... | collective-permute-start | bytes 4128776 | tf_op jit(solution)/shard_map/ppermute | solution.py:285
  194.0 56.3 %all-to-all-start.4 = ((bf16[4,96,3584]{2,1,0:T(8,128)(2,1)}), bf16[4,96,3584]{2,1,0:T(8,128)(2,1)S(1)}, u32[]{:S(2)}, u32[]{:S(2)}) async-start(bf16[4,96,3584]{2,1,0:T(8,128)(2,1)} %bitcast.103), calls=%async_computation.4 | async-start | bytes 5505024 | tf_op jit(solution)/shard_map/all_to_all | solution.py:303
  197.8 50.4 %collective-permute-start.16 = (bf16[192,3584]{1,0:T(8,128)(2,1)}, bf16[192,3584]{1,0:T(8,128)(2,1)}, u32[]{:S(2)}, u32[]{:S(2)}) collective-permute-start(bf16[192,3584]{1,0:T(8,128)(2,1)} %collective-permute-done.4.refs_8_), channel_id=1, source_target_pairs={{0,1},{1,0},{2,3},{3,2},{4,5},{5,4},{6,7},{7,6},{8,9},{9,8},{10,11... | collective-permute-start | bytes 4128776 | tf_op jit(solution)/shard_map/ppermute | solution.py:285
  198.3 49.8 %collective-permute-start.17 = (bf16[192,3584]{1,0:T(8,128)(2,1)}, bf16[192,3584]{1,0:T(8,128)(2,1)}, u32[]{:S(2)}, u32[]{:S(2)}) collective-permute-start(bf16[192,3584]{1,0:T(8,128)(2,1)} %collective-permute-done.8.refs_10_), channel_id=1, source_target_pairs={{0,1},{1,0},{2,3},{3,2},{4,5},{5,4},{6,7},{7,6},{8,9},{9,8},{10,11... | collective-permute-start | bytes 4128776 | tf_op jit(solution)/shard_map/ppermute | solution.py:285
  198.4 49.7 %collective-permute-start.13 = (bf16[128,3584]{1,0:T(8,128)(2,1)}, bf16[128,3584]{1,0:T(8,128)(2,1)}, u32[]{:S(2)}, u32[]{:S(2)}) collective-permute-start(bf16[128,3584]{1,0:T(8,128)(2,1)} %convolution_convert_fusion.2), channel_id=1, source_target_pairs={{0,8},{1,9},{2,10},{3,11},{4,12},{5,13},{6,14},{7,15},{8,0},{9,1},... | collective-permute-start | bytes 2752520 | tf_op jit(solution)/shard_map/ppermute | solution.py:285
  199.4 18.4 %collective-permute-start.14 = (bf16[384,512]{1,0:T(8,128)(2,1)S(1)}, bf16[384,512]{1,0:T(8,128)(2,1)S(1)}, u32[]{:S(2)}, u32[]{:S(2)}) collective-permute-start(bf16[384,512]{1,0:T(8,128)(2,1)S(1)} %dynamic-slice_bitcast_fusion.1), channel_id=1, source_target_pairs={{0,16},{16,0},{1,17},{17,1},{2,18},{18,2},{3,19},{19,3},{4,20},{20... | collective-permute-start | bytes 1179656 | tf_op jit(solution)/shard_map/ppermute | solution.py:294
  201.7 17.3 %collective-permute-start.15 = (bf16[384,512]{1,0:T(8,128)(2,1)S(1)}, bf16[384,512]{1,0:T(8,128)(2,1)S(1)}, u32[]{:S(2)}, u32[]{:S(2)}) collective-permute-start(bf16[384,512]{1,0:T(8,128)(2,1)S(1)} %dynamic-slice_bitcast_fusion), channel_id=1, source_target_pairs={{0,16},{16,0},{1,17},{17,1},{2,18},{18,2},{3,19},{19,3},{4,20},{20... | collective-permute-start | bytes 1179656 | tf_op jit(solution)/shard_map/ppermute | solution.py:294
  217.8 39.7 %copy-start.13 = (bf16[384,512]{1,0:T(8,128)(2,1)}, bf16[384,512]{1,0:T(8,128)(2,1)S(1)}, u32[]{:S(2)}) copy-start(bf16[384,512]{1,0:T(8,128)(2,1)S(1)} %collective-permute-done.14.refs_2_) | copy-start | bytes 1179652
  219.1 38.5 %copy-start.14 = (bf16[384,512]{1,0:T(8,128)(2,1)}, bf16[384,512]{1,0:T(8,128)(2,1)S(1)}, u32[]{:S(2)}) copy-start(bf16[384,512]{1,0:T(8,128)(2,1)S(1)} %collective-permute-done.15.refs_3_) | copy-start | bytes 1179652
  250.2 50.7 %all-to-all-start.5 = ((bf16[4,48,3584]{2,1,0:T(8,128)(2,1)}), bf16[4,48,3584]{2,1,0:T(8,128)(2,1)}, u32[]{:S(2)}, u32[]{:S(2)}) async-start(bf16[4,48,3584]{2,1,0:T(8,128)(2,1)} %bitcast.104), calls=%async_computation.5 | async-start | bytes 2752512 | tf_op jit(solution)/shard_map/all_to_all | solution.py:303
  254.8 46.1 %collective-permute-start.19 = (bf16[256,3584]{1,0:T(8,128)(2,1)}, bf16[256,3584]{1,0:T(8,128)(2,1)}, u32[]{:S(2)}, u32[]{:S(2)}) collective-permute-start(bf16[256,3584]{1,0:T(8,128)(2,1)} %shard_map.114), channel_id=1, source_target_pairs={{0,16},{16,0},{1,17},{17,1},{2,18},{18,2},{3,19},{19,3},{4,20},{20... | collective-permute-start | bytes 5505032 | tf_op jit(solution)/shard_map/ppermute | solution.py:294
  257.6 42.4 %collective-permute-start.18 = (bf16[128,3584]{1,0:T(8,128)(2,1)S(1)}, bf16[128,3584]{1,0:T(8,128)(2,1)S(1)}, u32[]{:S(2)}, u32[]{:S(2)}) collective-permute-start(bf16[128,3584]{1,0:T(8,128)(2,1)S(1)} %convolution_convert_fusion.1), channel_id=1, source_target_pairs={{0,8},{1,9},{2,10},{3,11},{4,12},{5,13},{6,14},{7,15},{8,0},{9,1},... | collective-permute-start | bytes 2752520 | tf_op jit(solution)/shard_map/ppermute | solution.py:285
  (15 other events, 61.9 us)

commit v10 on v9

--- a/solution.py
+++ b/solution.py
@@ -21,10 +21,10 @@
 
 
 def tile_of(width):
-    return 512 if width % 512 == 0 else width
-
-
-def kernel_call(body, grid, in_specs, out_specs, out_shape, scratch=(), scalars=0):
+    return next((n for n in (512, 256) if width % n == 0), width)
+
+
+def kernel_call(body, grid, in_specs, out_specs, out_shape, scratch=(), scalars=0, cost=1):
     return pl.pallas_call(
         body,
         grid_spec=pltpu.PrefetchScalarGridSpec(
@@ -38,13 +38,71 @@
         compiler_params=pltpu.CompilerParams(
             vmem_limit_bytes=VMEM_BYTES, dimension_semantics=("arbitrary",)
         ),
-        cost_estimate=pl.CostEstimate(flops=1, bytes_accessed=1, transcendentals=0),
+        cost_estimate=pl.CostEstimate(flops=1, bytes_accessed=cost, transcendentals=0),
     )
 
 
 def place(placing, rows, gain=None):
     slots = dot(placing, rows, NN)
     return (slots if gain is None else slots * gain).astype(BF16)
+
+
+HOP_COST = 22_000_000
+
+
+def wide_tile(width):
+    return width // 2 if width % 256 == 0 else width
+
+
+def place_far(placing, parts, gain=None):
+    slots = placing.shape[0]
+    width = parts[0].shape[1]
+    tile = wide_tile(width)
+    fixed = [placing] if gain is None else [placing, gain]
+
+    def body(placing_ref, *refs):
+        part_refs, out_ref = refs[len(fixed) - 1 : -1], refs[-1]
+        for cut in chunks(tile):
+            rows = [ref[:, cut] for ref in part_refs]
+            rows = rows[0] if len(rows) == 1 else jnp.concatenate(rows, axis=0)
+            total = dot(placing_ref[...], rows, NN)
+            if gain is not None:
+                total = total * refs[0][...]
+            out_ref[:, cut] = total.astype(BF16)
+
+    return kernel_call(
+        body,
+        (width // tile,),
+        [pl.BlockSpec(a.shape, lambda n: (0, 0)) for a in fixed]
+        + [pl.BlockSpec((a.shape[0], tile), lambda n: (0, n)) for a in parts],
+        pl.BlockSpec((slots, tile), lambda n: (0, n)),
+        jax.ShapeDtypeStruct((slots, width), BF16),
+        cost=HOP_COST,
+    )(*fixed, *parts)
+
+
+def combine_got(matrix, rows, got):
+    tokens, slots = matrix.shape
+    width = rows.shape[1]
+    tile = wide_tile(width)
+
+    def body(matrix_ref, rows_ref, got_ref, out_ref):
+        for cut in chunks(tile):
+            total = dot(matrix_ref[...], rows_ref[:, cut], NN)
+            out_ref[:, cut] = (total + got_ref[:, cut].astype(F32)).astype(BF16)
+
+    return kernel_call(
+        body,
+        (width // tile,),
+        [
+            pl.BlockSpec((tokens, slots), lambda n: (0, 0)),
+            pl.BlockSpec((slots, tile), lambda n: (0, n)),
+            pl.BlockSpec((tokens, tile), lambda n: (0, n)),
+        ],
+        pl.BlockSpec((tokens, tile), lambda n: (0, n)),
+        jax.ShapeDtypeStruct((tokens, width), BF16),
+        cost=HOP_COST,
+    )(matrix, rows, got)
 
 
 def combine(matrix, rows):
@@ -321,7 +379,7 @@
         return jnp.concatenate(pair, axis=2).reshape(matrix.shape[0], 2 * near * piece)
 
     count = near * piece
-    first = acts.shape[1] // 4
+    first = acts.shape[1] // 8
     far_acts_0 = far(acts[0, :first])
     meta = jnp.concatenate([expert_ids[0].astype(F32), route_weights[0]], axis=1)
     own_placing, own_back, own_weighting, own_gain = route(meta, half, chips, capacity)
@@ -336,12 +394,10 @@
     own = near_exchange(own)
     far_meta = far(meta)
     far_placing, far_back, far_weighting, far_gain = route(far_meta, half, chips, capacity)
-    far_acts_1, own, far_placing, far_gain, grads = tie(
-        far_acts_1, own, far_placing, far_gain, grad_out[0]
-    )
+    far_in = place_far(far_placing, [far_acts_0, far_acts_1])
+    far_in, own, far_placing, far_gain, grads = tie(far_in, own, far_placing, far_gain, grad_out[0])
 
     far_grads = far(grads)
-    far_in = place(far_placing, jnp.concatenate([far_acts_0, far_acts_1], axis=0))
     far_in = near_exchange(far_in)
     own_b = swap(own)
     own = own.reshape(near, 2, piece, width)
@@ -353,19 +409,23 @@
     own_units, own_input, own_input_b = backward(
         count, ((own, 1), (own_b, 1)), own_pre_gate, own_pre_up, *weights
     )
-    far_grads, far_in, mirror_own, own_out, own_out_b, own_input, own_input_b = tie(
-        far_grads, far_in, mirror_own, own_out, own_out_b, own_input, own_input_b
-    )
-
-    far_grad = near_exchange(place(far_placing, far_grads, far_gain))
+    far_grads, own_out, own_out_b, own_input, own_input_b = tie(
+        far_grads, own_out, own_out_b, own_input, own_input_b
+    )
+    far_grad = place_far(far_placing, [far_grads], far_gain)
+    far_grad, far_in, mirror_own, own_out, own_out_b, own_input, own_input_b = tie(
+        far_grad, far_in, mirror_own, own_out, own_out_b, own_input, own_input_b
+    )
+
+    far_grad = near_exchange(far_grad)
     far_in_b = swap(far_in)
-    mirror_far = mirror(far_in)
+    mirror_own_b = swap(mirror_own)
     own_out = expert_sum(own_out, own_out_b)
     far_pre_gate, far_pre_up, far_hidden, far_out, far_out_b = forward(
         count, (far_in, far_in_b), *weights
     )
-    far_grad, far_out, far_out_b, own_out, mirror_far, mirror_own = tie(
-        far_grad, far_out, far_out_b, own_out, mirror_far, mirror_own
+    far_grad, far_out, far_out_b, own_out, mirror_own_b = tie(
+        far_grad, far_out, far_out_b, own_out, mirror_own_b
     )
 
     far_out = expert_sum(far_out, far_out_b)
@@ -383,30 +443,30 @@
 
     far_input = expert_sum(far_input, far_input_b)
     back_out = combine(far_weighting, far_out).astype(BF16)
-    far_input, back_out, own_units, far_units, far_grad_b, mirror_own, mirror_far = tie(
-        far_input, back_out, own_units, far_units, far_grad_b, mirror_own, mirror_far
+    far_input, back_out, own_units, far_units, far_grad_b, mirror_far = tie(
+        far_input, back_out, own_units, far_units, far_grad_b, far_in
     )
 
     got_out = far(back_out)
     back = near_exchange(
-        jnp.stack([a.reshape(near, piece, width) for a in (far_input, own_out)], axis=1).reshape(2 * count, width)
+        jnp.stack([a.reshape(near, piece, width) for a in (far_input, own_input)], axis=1).reshape(2 * count, width)
     )
     mirror_units = [
         mirror(lax.dynamic_index_in_dim(units, 1 - kept_half, 0, keepdims=False))
         for units in (own_units, far_units)
     ]
-    mirror_own_b = swap(mirror_own)
-    mirror_far_b = swap(mirror_far)
+    mirror_far = mirror(mirror_far)
     rows_grad = ((own, 1), (own_b, 1), far_grad, far_grad_b)
     send_down = down_grad(count, 1 - kept, (own_hidden, far_hidden), rows_grad)
     keep_down = down_grad(count, kept, (own_hidden, far_hidden), rows_grad)
-    got_out, back, mirror_own_units, mirror_far_units, mirror_own_b, mirror_far_b, send_down, keep_down, own_input = tie(
-        got_out, back, *mirror_units, mirror_own_b, mirror_far_b, send_down, keep_down, own_input
+    got_out, back, mirror_own_units, mirror_far_units, mirror_far, send_down, keep_down, own_out = tie(
+        got_out, back, *mirror_units, mirror_far, send_down, keep_down, own_out
     )
 
     got_input = far(combine(of_set(far_back, 0), back).astype(BF16))
-    own_input = near_exchange(own_input)
+    own_out = near_exchange(own_out)
     got_down = mirror(send_down)
+    mirror_far_b = swap(mirror_far)
     grad_gate, grad_up = gate_up_grad(
         count,
         kept,
@@ -415,13 +475,12 @@
         (mirror_own_units, mirror_far_units),
         (mirror_own, mirror_own_b, mirror_far, mirror_far_b),
     )
-    out_acts = (combine(of_set(own_weighting, 1), back) + got_out.astype(F32)).astype(BF16)
-    got_input, own_input, got_down, grad_gate, grad_up, out_acts = tie(
-        got_input, own_input, got_down, grad_gate, grad_up, out_acts
-    )
-
-    grad_acts = (combine(own_back, own_input) + got_input.astype(F32)).astype(BF16)
+    out_acts = (combine(own_weighting, own_out) + got_out.astype(F32)).astype(BF16)
     grad_down = (keep_down.astype(F32) + got_down.astype(F32)).astype(BF16)
+    got_input, grad_down, grad_gate, grad_up, out_acts = tie(
+        got_input, grad_down, grad_gate, grad_up, out_acts
+    )
+    grad_acts = combine_got(of_set(own_back, 1), back, got_input)
     return out_acts[None], grad_acts[None], grad_gate[None], grad_up[None], grad_down[None]
 
 

time: 309 us -> 289 us (0.935)
  waiting for transfers between devices: 145 us -> 112 us
  local copies, waits for them, and re-layouts: 10.1 us -> 18.4 us
  Pallas kernels: 71 us -> 79.3 us
  matrix products: 18.9 us -> 10.7 us
  other arithmetic: 18.3 us -> 21.6 us
    ppermute x15, waiting for transfers between devices: 120 us -> 54.5 us  [hop(): lax.ppermute(rows, 'expert', [(i, i ^ distance) for i in range(devices)])]
    ppermute x5, waiting for transfers between devices: 17.5 us -> 49.1 us  [mirror(): lax.ppermute(rows, 'pipe', [(p, rank_count - 1 - p) for p in range(rank_c...]
    pallas_call x0 -> x3, Pallas kernels: none -> 8.36 us  [the longest x2 5.17 us: place_far(): kernel_call(body, (width // tile,), [pl.BlockSpec(a.shape, lambda n: (0,...]
    dot_general x5 -> x2, matrix products: 12 us -> 5.17 us  [dot(): return lax.dot_general(a, b, (dims, ((), ())), preferred_element_type=F32)]
    convert_element_type x0 -> x2, other arithmetic: none -> 5.48 us  [the longest x1 3.16 us: on_device(): grad_down = (keep_down.astype(F32) + got_down.astype(F32)).astype(BF16)]
    broadcast_in_dim x1 -> x0, other arithmetic: 3.79 us -> none  [on_device(): grad_down[None]]
  transfers between devices with their start and end apart: 26 -> 26, of which waited for: 12 -> 13; matrix products, arithmetic and copies ran while one was open for 10% -> 14% of each run, Pallas kernels for 23% -> 26%
where the time goes in v10:
time: 289 us; the launch traced here: 287 us
  waiting for transfers between devices  112 us (39%)
  Pallas kernels  79.3 us (27%)
  starting transfers between devices  45 us (16%)
  other arithmetic  21.6 us (7%)
  local copies, waits for them, and re-layouts  18.4 us (6%)
  matrix products  10.7 us (4%)
    ppermute x15, waiting for transfers between devices, hop(): lax.ppermute(rows, 'expert', [(i, i ^ distance) for i in range(devices)])  54.5 us
    ppermute x5, waiting for transfers between devices, mirror(): lax.ppermute(rows, 'pipe', [(p, rank_count - 1 - p) for p in range(rank_c...  49.1 us
    all_to_all x6, starting transfers between devices, near_exchange(): lax.all_to_all(rows.reshape(near, -1, width), 'expert', split_axis=0, con...  26.1 us
    pallas_call x2, Pallas kernels, backward(): kernel_call(body, (2,), [row_spec(a, width) for a in rows_grad] + [units,...  22.1 us
    pallas_call x2, Pallas kernels, forward(): kernel_call(body, (2,), [row_spec(a, width) for a in rows] + [columns, co...  21.4 us
    pallas_call x2, Pallas kernels, down_grad(): kernel_call(body, (width // tile,), [pl.BlockSpec((1, 2 * count, half_uni...  15.2 us
    ppermute x15, starting transfers between devices, hop(): lax.ppermute(rows, 'expert', [(i, i ^ distance) for i in range(devices)])  14.1 us
    pallas_call x1, Pallas kernels, gate_up_grad(): kernel_call(body, (width // tile,), [pl.BlockSpec((1, 2 * count, both), l...  12.1 us
  transfers between devices with their start and end apart: 26, of which 13 were waited for; matrix products, arithmetic and copies ran while one was open for 14% of the time, Pallas kernels for 26%

profile of v10, /device:TPU:0, one launch (start us, length us, event | category | flops | bytes accessed | tf_op | source)
XLA Modules:
  0.0 287.5 jit_solution(16002389797285017431)
XLA Ops:
  1.6 4.0 %collective-permute-start = (bf16[16,3584]{1,0:T(8,128)(2,1)S(1)}, bf16[16,3584]{1,0:T(8,128)(2,1)S(1)}, u32[]{:S(2)}, u32[]{:S(2)}) collective-permute-start(bf16[16,3584]{1,0:T(8,128)(2,1)S(1)} %slice_bitcast_fusion.1), channel_id=1, source_target_pairs={{0,8},{1,9},{2,10},{3,11},{4,12},{5,13},{6,14},{7,15},{8,0},{9,1},... | collective-permute-start | bytes 344072 | tf_op jit(solution)/shard_map/ppermute | solution.py:343
  8.9 3.6 %fusion = bf16[384,3584]{1,0:T(8,128)(2,1)} fusion(f32[384]{0:T(512)S(1)} %mul.86, bf16[128,3584]{1,0:T(8,128)(2,1)} %bitcast.10, bf16[128,3584]{1,0:T(8,128)(2,1)S(1)} %bitcast.101, bf16[128,384]{0,1:T(8,128)(2,1)S(1)} %bitcast.109, bf16[128,384]{0,1:T(8,128)(2,1)S(1)} %bitcast.108), kind=kOutput, calls=%fused_computation.1 | convolution fusion | flops 711458816 | bytes 4785664 | tf_op jit(solution)/shard_map/dot_general | solution.py:20
  13.7 3.8 %all-to-all-start = ((bf16[4,96,3584]{2,1,0:T(8,128)(2,1)}), bf16[4,96,3584]{2,1,0:T(8,128)(2,1)S(1)}, u32[]{:S(2)}, u32[]{:S(2)}) async-start(bf16[4,96,3584]{2,1,0:T(8,128)(2,1)} %bitcast.98), calls=%async_computation | async-start | bytes 5505024 | tf_op jit(solution)/shard_map/all_to_all | solution.py:361
  20.4 28.0 %collective-permute-done.1 = f32[128,4]{0,1:T(4,128)S(1)} collective-permute-done((f32[128,4]{0,1:T(4,128)}, f32[128,4]{0,1:T(4,128)S(1)}, u32[]{:S(2)}, u32[]{:S(2)}) %collective-permute-start.1) | collective-permute-done | bytes 2080 | tf_op jit(solution)/shard_map/ppermute | solution.py:343
  64.3 2.6 shard_map.110
  67.0 5.6 %all-to-all-start.1 = ((bf16[4,48,3584]{2,1,0:T(8,128)(2,1)}), bf16[4,48,3584]{2,1,0:T(8,128)(2,1)}, u32[]{:S(2)}, u32[]{:S(2)}) async-start(bf16[4,48,3584]{2,1,0:T(8,128)(2,1)} %bitcast.93), calls=%async_computation.1 | async-start | bytes 2752512 | tf_op jit(solution)/shard_map/all_to_all | solution.py:361
  78.2 10.5 %shard_map.111 = (f32[2,384,256]{2,1,0:T(8,128)}, f32[2,384,256]{2,1,0:T(8,128)}, bf16[2,384,256]{2,1,0:T(8,128)(2,1)}, bf16[192,3584]{1,0:T(8,128)(2,1)}, bf16[192,3584]{1,0:T(8,128)(2,1)}) custom-call(bf16[4,2,48,3584]{3,2,1,0:T(8,128)(2,1)} %bitcast.68, bf16[4,2,48,3584]{3,2,1,0:T(8,128)(2,1)} %bitcast.23.b_ref.refs_3_.refs_5_, ...), custom_call_target="tpu_custom_call" | custom-call | flops 1 | bytes 1 | tf_op jit(solution)/shard_map/pallas_call | solution.py:177
  88.7 10.8 %shard_map.112 = (bf16[2,384,512]{2,1,0:T(8,128)(2,1)}, bf16[192,3584]{1,0:T(8,128)(2,1)}, bf16[192,3584]{1,0:T(8,128)(2,1)}) custom-call(bf16[4,2,48,3584]{3,2,1,0:T(8,128)(2,1)} %bitcast.69, bf16[4,2,48,3584]{3,2,1,0:T(8,128)(2,1)} %bitcast.23.b_ref.refs_3_.refs_5_, f32[2,384,256]{2,1,0:T(8,128)} %get-tuple-element.87.pre_gate_ref, ...), custom_call_target="tpu_custom_call" | custom-call | flops 1 | bytes 1 | tf_op jit(solution)/shard_map/pallas_call | solution.py:232
  99.5 18.8 %collective-permute-done.3.refs_1_ = bf16[128,3584]{1,0:T(8,128)(2,1)} collective-permute-done((bf16[128,3584]{1,0:T(8,128)(2,1)}, bf16[128,3584]{1,0:T(8,128)(2,1)}, u32[]{:S(2)}, u32[]{:S(2)}) %collective-permute-start.3) | collective-permute-done | bytes 917536 | tf_op jit(solution)/shard_map/ppermute | solution.py:343
  118.3 2.6 shard_map.113
  121.5 3.7 %all-to-all-start.2 = ((bf16[4,48,3584]{2,1,0:T(8,128)(2,1)}), bf16[4,48,3584]{2,1,0:T(8,128)(2,1)S(1)}, u32[]{:S(2)}, u32[]{:S(2)}) async-start(bf16[4,48,3584]{2,1,0:T(8,128)(2,1)} %bitcast.94), calls=%async_computation.2 | async-start | bytes 2752512 | tf_op jit(solution)/shard_map/all_to_all | solution.py:361
  126.6 11.0 %shard_map.114 = (f32[2,384,256]{2,1,0:T(8,128)}, f32[2,384,256]{2,1,0:T(8,128)}, bf16[2,384,256]{2,1,0:T(8,128)(2,1)}, bf16[192,3584]{1,0:T(8,128)(2,1)}, bf16[192,3584]{1,0:T(8,128)(2,1)}) custom-call(bf16[192,3584]{1,0:T(8,128)(2,1)} %bitcast.28.a_ref.refs_6_, bf16[192,3584]{1,0:T(8,128)(2,1)} %copy-done.5, bf16[3584,512]{1,0:T(8,128)(2,1)} %bitcast.75, ...), custom_call_target="tpu_custom_call" | custom-call | flops 1 | bytes 1 | tf_op jit(solution)/shard_map/pallas_call | solution.py:177
  137.6 2.9 add_convert_fusion.4
  140.5 2.4 all-to-all-done.2
  142.9 3.3 %collective-permute-done.9 = bf16[192,3584]{1,0:T(8,128)(2,1)S(1)} collective-permute-done((bf16[192,3584]{1,0:T(8,128)(2,1)}, bf16[192,3584]{1,0:T(8,128)(2,1)S(1)}, u32[]{:S(2)}, u32[]{:S(2)}) %collective-permute-start.9) | collective-permute-done | bytes 1376288 | tf_op jit(solution)/shard_map/ppermute | solution.py:343
  148.2 4.3 %all-to-all-start.3 = ((bf16[4,48,3584]{2,1,0:T(8,128)(2,1)}), bf16[4,48,3584]{2,1,0:T(8,128)(2,1)}, u32[]{:S(2)}, u32[]{:S(2)}) async-start(bf16[4,48,3584]{2,1,0:T(8,128)(2,1)} %bitcast.95), calls=%async_computation.3 | async-start | bytes 2752512 | tf_op jit(solution)/shard_map/all_to_all | solution.py:361
  153.7 11.4 %shard_map.115 = (bf16[2,384,512]{2,1,0:T(8,128)(2,1)}, bf16[192,3584]{1,0:T(8,128)(2,1)}, bf16[192,3584]{1,0:T(8,128)(2,1)}) custom-call(bf16[192,3584]{1,0:T(8,128)(2,1)} %bitcast.88, bf16[192,3584]{1,0:T(8,128)(2,1)} %copy-done.3, f32[2,384,256]{2,1,0:T(8,128)} %get-tuple-element.111.pre_gate_ref, f32[2,384,256]{2,1,0:T(8,128)} %get-tuple-element.112.pre_up_ref, ...), custom_call_target="tpu_custom_call" | custom-call | flops 1 | bytes 1 | tf_op jit(solution)/shard_map/pallas_call | solution.py:232
  166.7 3.6 %all-to-all-done.3 = bf16[4,48,3584]{2,1,0:T(8,128)(2,1)} async-done(((bf16[4,48,3584]{2,1,0:T(8,128)(2,1)}), bf16[4,48,3584]{2,1,0:T(8,128)(2,1)}, u32[]{:S(2)}, u32[]{:S(2)}) %all-to-all-start.3) | async-done | bytes 1376288 | tf_op jit(solution)/shard_map/all_to_all | solution.py:361
  171.0 3.2 %convolution_convert_fusion.1 = bf16[128,3584]{1,0:T(8,128)(2,1)} fusion(f32[128,192]{0,1:T(8,128)S(1)} %get-tuple-element.151, bf16[192,3584]{1,0:T(8,128)(2,1)} %bitcast.33), kind=kOutput, calls=%fused_computation.3 | convolution fusion | flops 1057423360 | bytes 2392064 | tf_op jit(solution)/shard_map/dot_general | solution.py:111
  176.7 3.8 %all-to-all-start.4 = ((bf16[4,96,3584]{2,1,0:T(8,128)(2,1)}), bf16[4,96,3584]{2,1,0:T(8,128)(2,1)S(1)}, u32[]{:S(2)}, u32[]{:S(2)}) async-start(bf16[4,96,3584]{2,1,0:T(8,128)(2,1)} %bitcast.91), calls=%async_computation.4 | async-start | bytes 5505024 | tf_op jit(solution)/shard_map/all_to_all | solution.py:361
  181.1 2.5 collective-permute-start.13
  186.9 7.6 %shard_map.117 = bf16[256,3584]{1,0:T(8,128)(2,1)} custom-call(s32[1]{0:T(128)} %bitcast.40.which_ref, bf16[2,384,256]{2,1,0:T(8,128)(2,1)} %get-tuple-element.129.refs_0_, bf16[2,384,256]{2,1,0:T(8,128)(2,1)} %get-tuple-element.130.refs_1_, bf16[4,2,48,3584]{3,2,1,0:T(8,128)(2,1)} %bitcast.70, bf16[4,2,48,3584]{3,2,1,0:T(8,128)(2,1)} %bitcast.23.b_ref.refs_3_.refs_5_, ...), custom_call_target="tpu_custom_call" | custom-call | flops 1 | bytes 1 | tf_op jit(solution)/shard_map/pallas_call | solution.py:266
  194.5 7.6 %shard_map.116 = bf16[256,3584]{1,0:T(8,128)(2,1)} custom-call(s32[1]{0:T(128)S(6)} %sub.37.which_ref, bf16[2,384,256]{2,1,0:T(8,128)(2,1)} %get-tuple-element.129.refs_0_, bf16[2,384,256]{2,1,0:T(8,128)(2,1)} %get-tuple-element.130.refs_1_, bf16[4,2,48,3584]{3,2,1,0:T(8,128)(2,1)} %bitcast.71, bf16[4,2,48,3584]{3,2,1,0:T(8,128)(2,1)} %bitcast.23.b_ref.refs_3_.refs_5_, ...), custom_call_target="tpu_custom_call" | custom-call | flops 1 | bytes 1 | tf_op jit(solution)/shard_map/pallas_call | solution.py:266
  202.1 20.1 %collective-permute-done.14.refs_2_ = bf16[384,512]{1,0:T(8,128)(2,1)S(1)} collective-permute-done((bf16[384,512]{1,0:T(8,128)(2,1)S(1)}, bf16[384,512]{1,0:T(8,128)(2,1)S(1)}, u32[]{:S(2)}, u32[]{:S(2)}) %collective-permute-start.14) | collective-permute-done | bytes 393248 | tf_op jit(solution)/shard_map/ppermute | solution.py:352
  222.2 8.0 %collective-permute-done.15.refs_3_ = bf16[384,512]{1,0:T(8,128)(2,1)S(1)} collective-permute-done((bf16[384,512]{1,0:T(8,128)(2,1)S(1)}, bf16[384,512]{1,0:T(8,128)(2,1)S(1)}, u32[]{:S(2)}, u32[]{:S(2)}) %collective-permute-start.15) | collective-permute-done | bytes 393248 | tf_op jit(solution)/shard_map/ppermute | solution.py:352
  233.5 4.9 %all-to-all-start.5 = ((bf16[4,48,3584]{2,1,0:T(8,128)(2,1)}), bf16[4,48,3584]{2,1,0:T(8,128)(2,1)}, u32[]{:S(2)}, u32[]{:S(2)}) async-start(bf16[4,48,3584]{2,1,0:T(8,128)(2,1)} %bitcast.92), calls=%async_computation.5 | async-start | bytes 2752512 | tf_op jit(solution)/shard_map/all_to_all | solution.py:361
  241.9 12.1 %shard_map.118 = (bf16[3584,256]{1,0:T(8,128)(2,1)}, bf16[3584,256]{1,0:T(8,128)(2,1)}) custom-call(s32[1]{0:T(128)} %bitcast.40.which_ref, bf16[2,384,512]{2,1,0:T(8,128)(2,1)} %get-tuple-element.126.refs_0_, bf16[2,384,512]{2,1,0:T(8,128)(2,1)} %get-tuple-element.127.refs_1_, bf16[384,512]{1,0:T(8,128)(2,1)} %copy-done.12, bf16[384,512]{1,0:T(8,128)(2,1)} %copy-done.13, ...), custom_call_target="tpu_custom_call" | custom-call | flops 1 | bytes 1 | tf_op jit(solution)/shard_map/pallas_call | solution.py:299
  254.0 21.0 %collective-permute-done.18 = bf16[256,3584]{1,0:T(8,128)(2,1)} collective-permute-done((bf16[256,3584]{1,0:T(8,128)(2,1)}, bf16[256,3584]{1,0:T(8,128)(2,1)}, u32[]{:S(2)}, u32[]{:S(2)}) %collective-permute-start.18) | collective-permute-done | bytes 1835040 | tf_op jit(solution)/shard_map/ppermute | solution.py:352
  275.0 3.2 %add_convert_fusion = bf16[256,3584]{1,0:T(8,128)(2,1)} fusion(bf16[256,3584]{1,0:T(8,128)(2,1)} %collective-permute-done.18, bf16[256,3584]{1,0:T(8,128)(2,1)S(1)} %copy-done.4), kind=kLoop, calls=%fused_computation.4 | loop fusion | flops 3670016 | bytes 5505024 | tf_op jit(solution)/shard_map/convert_element_type | solution.py:479
  278.1 2.3 fusion.11
  280.4 2.3 add_convert_fusion.5
  284.3 3.2 %shard_map.119 = bf16[128,3584]{1,0:T(8,128)(2,1)} custom-call(bf16[128,384]{1,0:T(8,128)(2,1)} %copy.58.matrix_ref, bf16[384,3584]{1,0:T(8,128)(2,1)} %bitcast.86, bf16[128,3584]{1,0:T(8,128)(2,1)} %collective-permute-done.17.got_ref), custom_call_target="tpu_custom_call" | custom-call | flops 1 | bytes 22000000 | tf_op jit(solution)/shard_map/pallas_call | solution.py:94
  (134 shorter events, 51.8 us)
Async XLA Ops:
  1.6 11.4 %collective-permute-start = (bf16[16,3584]{1,0:T(8,128)(2,1)S(1)}, bf16[16,3584]{1,0:T(8,128)(2,1)S(1)}, u32[]{:S(2)}, u32[]{:S(2)}) collective-permute-start(bf16[16,3584]{1,0:T(8,128)(2,1)S(1)} %slice_bitcast_fusion.1), channel_id=1, source_target_pairs={{0,8},{1,9},{2,10},{3,11},{4,12},{5,13},{6,14},{7,15},{8,0},{9,1},... | collective-permute-start | bytes 344072 | tf_op jit(solution)/shard_map/ppermute | solution.py:343
  13.7 53.2 %all-to-all-start = ((bf16[4,96,3584]{2,1,0:T(8,128)(2,1)}), bf16[4,96,3584]{2,1,0:T(8,128)(2,1)S(1)}, u32[]{:S(2)}, u32[]{:S(2)}) async-start(bf16[4,96,3584]{2,1,0:T(8,128)(2,1)} %bitcast.98), calls=%async_computation | async-start | bytes 5505024 | tf_op jit(solution)/shard_map/all_to_all | solution.py:361
  17.5 31.0 %collective-permute-start.1 = (f32[128,4]{0,1:T(4,128)}, f32[128,4]{0,1:T(4,128)S(1)}, u32[]{:S(2)}, u32[]{:S(2)}) collective-permute-start(f32[128,4]{0,1:T(4,128)} %pad_maximum_fusion.1), channel_id=1, source_target_pairs={{0,8},{1,9},{2,10},{3,11},{4,12},{5,13},{6,14},{7,15},{8,0},{9,1},... | collective-permute-start | bytes 6152 | tf_op jit(solution)/shard_map/ppermute | solution.py:343
  18.3 46.1 %collective-permute-start.2 = (bf16[112,3584]{1,0:T(8,128)(2,1)S(1)}, bf16[112,3584]{1,0:T(8,128)(2,1)}, u32[]{:S(2)}, u32[]{:S(2)}) collective-permute-start(bf16[112,3584]{1,0:T(8,128)(2,1)S(1)} %slice_bitcast_fusion), channel_id=1, source_target_pairs={{0,8},{1,9},{2,10},{3,11},{4,12},{5,13},{6,14},{7,15},{8,0},{9,1},... | collective-permute-start | bytes 2408456 | tf_op jit(solution)/shard_map/ppermute | solution.py:343
  66.9 11.3 %collective-permute-start.4 = (bf16[384,3584]{1,0:T(8,128)(2,1)S(1)}, bf16[384,3584]{1,0:T(8,128)(2,1)}, u32[]{:S(2)}, u32[]{:S(2)}) collective-permute-start(bf16[384,3584]{1,0:T(8,128)(2,1)S(1)} %bitcast.66), channel_id=1, source_target_pairs={{0,1},{1,0},{2,3},{3,2},{4,5},{5,4},{6,7},{7,6},{8,9},{9,8},{10,11... | collective-permute-start | bytes 8257544 | tf_op jit(solution)/shard_map/ppermute | solution.py:343
  67.0 54.0 %all-to-all-start.1 = ((bf16[4,48,3584]{2,1,0:T(8,128)(2,1)}), bf16[4,48,3584]{2,1,0:T(8,128)(2,1)}, u32[]{:S(2)}, u32[]{:S(2)}) async-start(bf16[4,48,3584]{2,1,0:T(8,128)(2,1)} %bitcast.93), calls=%async_computation.1 | async-start | bytes 2752512 | tf_op jit(solution)/shard_map/all_to_all | solution.py:361
  73.7 47.2 %collective-permute-start.5 = (bf16[192,3584]{1,0:T(8,128)(2,1)}, bf16[192,3584]{1,0:T(8,128)(2,1)}, u32[]{:S(2)}, u32[]{:S(2)}) collective-permute-start(bf16[192,3584]{1,0:T(8,128)(2,1)} %bitcast.29), channel_id=1, source_target_pairs={{0,16},{16,0},{1,17},{17,1},{2,18},{18,2},{3,19},{19,3},{4,20},{20... | collective-permute-start | bytes 4128776 | tf_op jit(solution)/shard_map/ppermute | solution.py:352
  75.2 43.1 %collective-permute-start.3 = (bf16[128,3584]{1,0:T(8,128)(2,1)}, bf16[128,3584]{1,0:T(8,128)(2,1)}, u32[]{:S(2)}, u32[]{:S(2)}) collective-permute-start(bf16[128,3584]{1,0:T(8,128)(2,1)} %bitcast.10), channel_id=1, source_target_pairs={{0,8},{1,9},{2,10},{3,11},{4,12},{5,13},{6,14},{7,15},{8,0},{9,1},... | collective-permute-start | bytes 2752520 | tf_op jit(solution)/shard_map/ppermute | solution.py:343
  120.9 4.6 %collective-permute-start.6 = (bf16[192,3584]{1,0:T(8,128)(2,1)}, bf16[192,3584]{1,0:T(8,128)(2,1)S(1)}, u32[]{:S(2)}, u32[]{:S(2)}) collective-permute-start(bf16[192,3584]{1,0:T(8,128)(2,1)} %bitcast.28.a_ref.refs_6_), channel_id=1, source_target_pairs={{0,1},{1,0},{2,3},{3,2},{4,5},{5,4},{6,7},{7,6},{8,9},{9,8},{10,11... | collective-permute-start | bytes 4128776 | tf_op jit(solution)/shard_map/ppermute | solution.py:343
  121.0 16.6 %collective-permute-start.7 = (bf16[192,3584]{1,0:T(8,128)(2,1)}, bf16[192,3584]{1,0:T(8,128)(2,1)}, u32[]{:S(2)}, u32[]{:S(2)}) collective-permute-start(bf16[192,3584]{1,0:T(8,128)(2,1)} %get-tuple-element.102), channel_id=1, source_target_pairs={{0,1},{1,0},{2,3},{3,2},{4,5},{5,4},{6,7},{7,6},{8,9},{9,8},{10,11... | collective-permute-start | bytes 4128776 | tf_op jit(solution)/shard_map/ppermute | solution.py:343
  121.5 21.3 %all-to-all-start.2 = ((bf16[4,48,3584]{2,1,0:T(8,128)(2,1)}), bf16[4,48,3584]{2,1,0:T(8,128)(2,1)S(1)}, u32[]{:S(2)}, u32[]{:S(2)}) async-start(bf16[4,48,3584]{2,1,0:T(8,128)(2,1)} %bitcast.94), calls=%async_computation.2 | async-start | bytes 2752512 | tf_op jit(solution)/shard_map/all_to_all | solution.py:361
  125.2 12.4 %copy-start.8 = (bf16[192,3584]{1,0:T(8,128)(2,1)S(1)}, bf16[192,3584]{1,0:T(8,128)(2,1)}, u32[]{:S(2)}) copy-start(bf16[192,3584]{1,0:T(8,128)(2,1)} %get-tuple-element.101) | copy-start | bytes 4128772
  125.3 15.2 %collective-permute-start.8 = (bf16[192,3584]{1,0:T(8,128)(2,1)}, bf16[192,3584]{1,0:T(8,128)(2,1)}, u32[]{:S(2)}, u32[]{:S(2)}) collective-permute-start(bf16[192,3584]{1,0:T(8,128)(2,1)} %collective-permute-done.5.refs_8_), channel_id=1, source_target_pairs={{0,1},{1,0},{2,3},{3,2},{4,5},{5,4},{6,7},{7,6},{8,9},{9,8},{10,11... | collective-permute-start | bytes 4128776 | tf_op jit(solution)/shard_map/ppermute | solution.py:343
  142.9 3.3 %collective-permute-start.9 = (bf16[192,3584]{1,0:T(8,128)(2,1)}, bf16[192,3584]{1,0:T(8,128)(2,1)S(1)}, u32[]{:S(2)}, u32[]{:S(2)}) collective-permute-start(bf16[192,3584]{1,0:T(8,128)(2,1)} %get-tuple-element.105), channel_id=1, source_target_pairs={{0,1},{1,0},{2,3},{3,2},{4,5},{5,4},{6,7},{7,6},{8,9},{9,8},{10,11... | collective-permute-start | bytes 4128776 | tf_op jit(solution)/shard_map/ppermute | solution.py:343
  147.7 4.9 %collective-permute-start.10 = (bf16[192,3584]{1,0:T(8,128)(2,1)S(1)}, bf16[192,3584]{1,0:T(8,128)(2,1)S(1)}, u32[]{:S(2)}, u32[]{:S(2)}) collective-permute-start(bf16[192,3584]{1,0:T(8,128)(2,1)S(1)} %bitcast.87), channel_id=1, source_target_pairs={{0,1},{1,0},{2,3},{3,2},{4,5},{5,4},{6,7},{7,6},{8,9},{9,8},{10,11... | collective-permute-start | bytes 4128776 | tf_op jit(solution)/shard_map/ppermute | solution.py:343
  147.9 17.2 %collective-permute-start.11 = (bf16[192,3584]{1,0:T(8,128)(2,1)}, bf16[192,3584]{1,0:T(8,128)(2,1)}, u32[]{:S(2)}, u32[]{:S(2)}) collective-permute-start(bf16[192,3584]{1,0:T(8,128)(2,1)} %get-tuple-element.117), channel_id=1, source_target_pairs={{0,1},{1,0},{2,3},{3,2},{4,5},{5,4},{6,7},{7,6},{8,9},{9,8},{10,11... | collective-permute-start | bytes 4128776 | tf_op jit(solution)/shard_map/ppermute | solution.py:343
  148.2 22.1 %all-to-all-start.3 = ((bf16[4,48,3584]{2,1,0:T(8,128)(2,1)}), bf16[4,48,3584]{2,1,0:T(8,128)(2,1)}, u32[]{:S(2)}, u32[]{:S(2)}) async-start(bf16[4,48,3584]{2,1,0:T(8,128)(2,1)} %bitcast.95), calls=%async_computation.3 | async-start | bytes 2752512 | tf_op jit(solution)/shard_map/all_to_all | solution.py:361
  170.4 3.8 %collective-permute-start.12 = (bf16[192,3584]{1,0:T(8,128)(2,1)}, bf16[192,3584]{1,0:T(8,128)(2,1)S(1)}, u32[]{:S(2)}, u32[]{:S(2)}) collective-permute-start(bf16[192,3584]{1,0:T(8,128)(2,1)} %get-tuple-element.119), channel_id=1, source_target_pairs={{0,1},{1,0},{2,3},{3,2},{4,5},{5,4},{6,7},{7,6},{8,9},{9,8},{10,11... | collective-permute-start | bytes 4128776 | tf_op jit(solution)/shard_map/ppermute | solution.py:343
  176.7 56.3 %all-to-all-start.4 = ((bf16[4,96,3584]{2,1,0:T(8,128)(2,1)}), bf16[4,96,3584]{2,1,0:T(8,128)(2,1)S(1)}, u32[]{:S(2)}, u32[]{:S(2)}) async-start(bf16[4,96,3584]{2,1,0:T(8,128)(2,1)} %bitcast.91), calls=%async_computation.4 | async-start | bytes 5505024 | tf_op jit(solution)/shard_map/all_to_all | solution.py:361
  180.5 50.5 %collective-permute-start.16 = (bf16[192,3584]{1,0:T(8,128)(2,1)}, bf16[192,3584]{1,0:T(8,128)(2,1)}, u32[]{:S(2)}, u32[]{:S(2)}) collective-permute-start(bf16[192,3584]{1,0:T(8,128)(2,1)} %bitcast.28.a_ref.refs_6_), channel_id=1, source_target_pairs={{0,16},{16,0},{1,17},{17,1},{2,18},{18,2},{3,19},{19,3},{4,20},{20... | collective-permute-start | bytes 4128776 | tf_op jit(solution)/shard_map/ppermute | solution.py:352
  181.1 49.8 %collective-permute-start.13 = (bf16[128,3584]{1,0:T(8,128)(2,1)}, bf16[128,3584]{1,0:T(8,128)(2,1)}, u32[]{:S(2)}, u32[]{:S(2)}) collective-permute-start(bf16[128,3584]{1,0:T(8,128)(2,1)} %convolution_convert_fusion.1), channel_id=1, source_target_pairs={{0,8},{1,9},{2,10},{3,11},{4,12},{5,13},{6,14},{7,15},{8,0},{9,1},... | collective-permute-start | bytes 2752520 | tf_op jit(solution)/shard_map/ppermute | solution.py:343
  183.7 38.5 %collective-permute-start.14 = (bf16[384,512]{1,0:T(8,128)(2,1)S(1)}, bf16[384,512]{1,0:T(8,128)(2,1)S(1)}, u32[]{:S(2)}, u32[]{:S(2)}) collective-permute-start(bf16[384,512]{1,0:T(8,128)(2,1)S(1)} %dynamic-slice_bitcast_fusion.1), channel_id=1, source_target_pairs={{0,16},{16,0},{1,17},{17,1},{2,18},{18,2},{3,19},{19,3},{4,20},{20... | collective-permute-start | bytes 1179656 | tf_op jit(solution)/shard_map/ppermute | solution.py:352
  186.3 44.0 %collective-permute-start.15 = (bf16[384,512]{1,0:T(8,128)(2,1)S(1)}, bf16[384,512]{1,0:T(8,128)(2,1)S(1)}, u32[]{:S(2)}, u32[]{:S(2)}) collective-permute-start(bf16[384,512]{1,0:T(8,128)(2,1)S(1)} %dynamic-slice_bitcast_fusion), channel_id=1, source_target_pairs={{0,16},{16,0},{1,17},{17,1},{2,18},{18,2},{3,19},{19,3},{4,20},{20... | collective-permute-start | bytes 1179656 | tf_op jit(solution)/shard_map/ppermute | solution.py:352
  202.1 36.3 %copy-start.17 = (f32[1,128,2]{1,2,0:T(2,128)S(1)}, f32[1,128,2]{1,2,0:T(2,128)}, u32[]{:S(2)}) copy-start(f32[1,128,2]{1,2,0:T(2,128)} %param.10) | copy-start | bytes 3076
  202.1 36.3 %copy-start.19 = (s32[128,2]{0,1:T(2,128)S(1)}, s32[128,2]{0,1:T(2,128)}, u32[]{:S(2)}) copy-start(s32[128,2]{0,1:T(2,128)} %copy-done.18) | copy-start | bytes 3076
  202.1 37.1 %copy-start.14 = (bf16[128,192]{0,1:T(8,128)(2,1)S(1)}, bf16[128,192]{0,1:T(8,128)(2,1)}, u32[]{:S(2)}) copy-start(bf16[128,192]{0,1:T(8,128)(2,1)} %get-tuple-element.152) | copy-start | bytes 147460
  222.2 18.6 %copy-start.12 = (bf16[384,512]{1,0:T(8,128)(2,1)}, bf16[384,512]{1,0:T(8,128)(2,1)S(1)}, u32[]{:S(2)}) copy-start(bf16[384,512]{1,0:T(8,128)(2,1)S(1)} %collective-permute-done.14.refs_2_) | copy-start | bytes 1179652
  233.0 42.0 %collective-permute-start.18 = (bf16[256,3584]{1,0:T(8,128)(2,1)}, bf16[256,3584]{1,0:T(8,128)(2,1)}, u32[]{:S(2)}, u32[]{:S(2)}) collective-permute-start(bf16[256,3584]{1,0:T(8,128)(2,1)} %shard_map.116), channel_id=1, source_target_pairs={{0,16},{16,0},{1,17},{17,1},{2,18},{18,2},{3,19},{19,3},{4,20},{20... | collective-permute-start | bytes 5505032 | tf_op jit(solution)/shard_map/ppermute | solution.py:352
  233.5 8.4 %collective-permute-start.19 = (bf16[192,3584]{1,0:T(8,128)(2,1)}, bf16[192,3584]{1,0:T(8,128)(2,1)}, u32[]{:S(2)}, u32[]{:S(2)}) collective-permute-start(bf16[192,3584]{1,0:T(8,128)(2,1)} %collective-permute-done.16.refs_10_), channel_id=1, source_target_pairs={{0,1},{1,0},{2,3},{3,2},{4,5},{5,4},{6,7},{7,6},{8,9},{9,8},{10,11... | collective-permute-start | bytes 4128776 | tf_op jit(solution)/shard_map/ppermute | solution.py:343
  233.5 44.6 %all-to-all-start.5 = ((bf16[4,48,3584]{2,1,0:T(8,128)(2,1)}), bf16[4,48,3584]{2,1,0:T(8,128)(2,1)}, u32[]{:S(2)}, u32[]{:S(2)}) async-start(bf16[4,48,3584]{2,1,0:T(8,128)(2,1)} %bitcast.92), calls=%async_computation.5 | async-start | bytes 2752512 | tf_op jit(solution)/shard_map/all_to_all | solution.py:361
  240.8 34.1 %copy-start.4 = (bf16[256,3584]{1,0:T(8,128)(2,1)S(1)}, bf16[256,3584]{1,0:T(8,128)(2,1)}, u32[]{:S(2)}) copy-start(bf16[256,3584]{1,0:T(8,128)(2,1)} %shard_map.117) | copy-start | bytes 5505028
  240.8 43.4 %collective-permute-start.17 = (bf16[128,3584]{1,0:T(8,128)(2,1)}, bf16[128,3584]{1,0:T(8,128)(2,1)}, u32[]{:S(2)}, u32[]{:S(2)}) collective-permute-start(bf16[128,3584]{1,0:T(8,128)(2,1)} %convolution_convert_fusion), channel_id=1, source_target_pairs={{0,8},{1,9},{2,10},{3,11},{4,12},{5,13},{6,14},{7,15},{8,0},{9,1},... | collective-permute-start | bytes 2752520 | tf_op jit(solution)/shard_map/ppermute | solution.py:343
  (21 other events, 104.6 us)

commit v11 on v10

--- a/solution.py
+++ b/solution.py
@@ -47,7 +47,7 @@
     return (slots if gain is None else slots * gain).astype(BF16)
 
 
-HOP_COST = 22_000_000
+HOP_COST = 50_000_000
 
 
 def wide_tile(width):

time: 289 us -> 289 us (level)
  no operation moved by 1% of the time
where the time goes in v11:
time: 289 us; the launch traced here: 287 us
  waiting for transfers between devices  112 us (39%)
  Pallas kernels  79.3 us (27%)
  starting transfers between devices  45 us (16%)
  other arithmetic  21.6 us (7%)
  local copies, waits for them, and re-layouts  18.4 us (6%)
  matrix products  10.7 us (4%)
    ppermute x15, waiting for transfers between devices, hop(): lax.ppermute(rows, 'expert', [(i, i ^ distance) for i in range(devices)])  54.5 us
    ppermute x5, waiting for transfers between devices, mirror(): lax.ppermute(rows, 'pipe', [(p, rank_count - 1 - p) for p in range(rank_c...  49.1 us
    all_to_all x6, starting transfers between devices, near_exchange(): lax.all_to_all(rows.reshape(near, -1, width), 'expert', split_axis=0, con...  26.1 us
    pallas_call x2, Pallas kernels, backward(): kernel_call(body, (2,), [row_spec(a, width) for a in rows_grad] + [units,...  22.1 us
    pallas_call x2, Pallas kernels, forward(): kernel_call(body, (2,), [row_spec(a, width) for a in rows] + [columns, co...  21.4 us
    pallas_call x2, Pallas kernels, down_grad(): kernel_call(body, (width // tile,), [pl.BlockSpec((1, 2 * count, half_uni...  15.2 us
    ppermute x15, starting transfers between devices, hop(): lax.ppermute(rows, 'expert', [(i, i ^ distance) for i in range(devices)])  14.1 us
    pallas_call x1, Pallas kernels, gate_up_grad(): kernel_call(body, (width // tile,), [pl.BlockSpec((1, 2 * count, both), l...  12.1 us
  transfers between devices with their start and end apart: 26, of which 13 were waited for; matrix products, arithmetic and copies ran while one was open for 14% of the time, Pallas kernels for 26%

profile of v11, /device:TPU:0, one launch (start us, length us, event | category | flops | bytes accessed | tf_op | source)
XLA Modules:
  0.0 287.5 jit_solution(16002389797285017431)
XLA Ops:
  1.6 4.0 %collective-permute-start = (bf16[16,3584]{1,0:T(8,128)(2,1)S(1)}, bf16[16,3584]{1,0:T(8,128)(2,1)S(1)}, u32[]{:S(2)}, u32[]{:S(2)}) collective-permute-start(bf16[16,3584]{1,0:T(8,128)(2,1)S(1)} %slice_bitcast_fusion.1), channel_id=1, source_target_pairs={{0,8},{1,9},{2,10},{3,11},{4,12},{5,13},{6,14},{7,15},{8,0},{9,1},... | collective-permute-start | bytes 344072 | tf_op jit(solution)/shard_map/ppermute | solution.py:343
  8.9 3.6 %fusion = bf16[384,3584]{1,0:T(8,128)(2,1)} fusion(f32[384]{0:T(512)S(1)} %mul.86, bf16[128,3584]{1,0:T(8,128)(2,1)} %bitcast.10, bf16[128,3584]{1,0:T(8,128)(2,1)S(1)} %bitcast.101, bf16[128,384]{0,1:T(8,128)(2,1)S(1)} %bitcast.109, bf16[128,384]{0,1:T(8,128)(2,1)S(1)} %bitcast.108), kind=kOutput, calls=%fused_computation.1 | convolution fusion | flops 711458816 | bytes 4785664 | tf_op jit(solution)/shard_map/dot_general | solution.py:20
  13.7 3.8 %all-to-all-start = ((bf16[4,96,3584]{2,1,0:T(8,128)(2,1)}), bf16[4,96,3584]{2,1,0:T(8,128)(2,1)S(1)}, u32[]{:S(2)}, u32[]{:S(2)}) async-start(bf16[4,96,3584]{2,1,0:T(8,128)(2,1)} %bitcast.98), calls=%async_computation | async-start | bytes 5505024 | tf_op jit(solution)/shard_map/all_to_all | solution.py:361
  20.4 28.0 %collective-permute-done.1 = f32[128,4]{0,1:T(4,128)S(1)} collective-permute-done((f32[128,4]{0,1:T(4,128)}, f32[128,4]{0,1:T(4,128)S(1)}, u32[]{:S(2)}, u32[]{:S(2)}) %collective-permute-start.1) | collective-permute-done | bytes 2080 | tf_op jit(solution)/shard_map/ppermute | solution.py:343
  64.3 2.6 shard_map.110
  67.0 5.6 %all-to-all-start.1 = ((bf16[4,48,3584]{2,1,0:T(8,128)(2,1)}), bf16[4,48,3584]{2,1,0:T(8,128)(2,1)}, u32[]{:S(2)}, u32[]{:S(2)}) async-start(bf16[4,48,3584]{2,1,0:T(8,128)(2,1)} %bitcast.93), calls=%async_computation.1 | async-start | bytes 2752512 | tf_op jit(solution)/shard_map/all_to_all | solution.py:361
  78.2 10.5 %shard_map.111 = (f32[2,384,256]{2,1,0:T(8,128)}, f32[2,384,256]{2,1,0:T(8,128)}, bf16[2,384,256]{2,1,0:T(8,128)(2,1)}, bf16[192,3584]{1,0:T(8,128)(2,1)}, bf16[192,3584]{1,0:T(8,128)(2,1)}) custom-call(bf16[4,2,48,3584]{3,2,1,0:T(8,128)(2,1)} %bitcast.68, bf16[4,2,48,3584]{3,2,1,0:T(8,128)(2,1)} %bitcast.23.b_ref.refs_3_.refs_5_, ...), custom_call_target="tpu_custom_call" | custom-call | flops 1 | bytes 1 | tf_op jit(solution)/shard_map/pallas_call | solution.py:177
  88.7 10.8 %shard_map.112 = (bf16[2,384,512]{2,1,0:T(8,128)(2,1)}, bf16[192,3584]{1,0:T(8,128)(2,1)}, bf16[192,3584]{1,0:T(8,128)(2,1)}) custom-call(bf16[4,2,48,3584]{3,2,1,0:T(8,128)(2,1)} %bitcast.69, bf16[4,2,48,3584]{3,2,1,0:T(8,128)(2,1)} %bitcast.23.b_ref.refs_3_.refs_5_, f32[2,384,256]{2,1,0:T(8,128)} %get-tuple-element.87.pre_gate_ref, ...), custom_call_target="tpu_custom_call" | custom-call | flops 1 | bytes 1 | tf_op jit(solution)/shard_map/pallas_call | solution.py:232
  99.5 18.8 %collective-permute-done.3.refs_1_ = bf16[128,3584]{1,0:T(8,128)(2,1)} collective-permute-done((bf16[128,3584]{1,0:T(8,128)(2,1)}, bf16[128,3584]{1,0:T(8,128)(2,1)}, u32[]{:S(2)}, u32[]{:S(2)}) %collective-permute-start.3) | collective-permute-done | bytes 917536 | tf_op jit(solution)/shard_map/ppermute | solution.py:343
  118.3 2.6 shard_map.113
  121.5 3.7 %all-to-all-start.2 = ((bf16[4,48,3584]{2,1,0:T(8,128)(2,1)}), bf16[4,48,3584]{2,1,0:T(8,128)(2,1)S(1)}, u32[]{:S(2)}, u32[]{:S(2)}) async-start(bf16[4,48,3584]{2,1,0:T(8,128)(2,1)} %bitcast.94), calls=%async_computation.2 | async-start | bytes 2752512 | tf_op jit(solution)/shard_map/all_to_all | solution.py:361
  126.6 11.0 %shard_map.114 = (f32[2,384,256]{2,1,0:T(8,128)}, f32[2,384,256]{2,1,0:T(8,128)}, bf16[2,384,256]{2,1,0:T(8,128)(2,1)}, bf16[192,3584]{1,0:T(8,128)(2,1)}, bf16[192,3584]{1,0:T(8,128)(2,1)}) custom-call(bf16[192,3584]{1,0:T(8,128)(2,1)} %bitcast.28.a_ref.refs_6_, bf16[192,3584]{1,0:T(8,128)(2,1)} %copy-done.5, bf16[3584,512]{1,0:T(8,128)(2,1)} %bitcast.75, ...), custom_call_target="tpu_custom_call" | custom-call | flops 1 | bytes 1 | tf_op jit(solution)/shard_map/pallas_call | solution.py:177
  137.6 2.9 add_convert_fusion.4
  140.5 2.4 all-to-all-done.2
  142.9 3.3 %collective-permute-done.9 = bf16[192,3584]{1,0:T(8,128)(2,1)S(1)} collective-permute-done((bf16[192,3584]{1,0:T(8,128)(2,1)}, bf16[192,3584]{1,0:T(8,128)(2,1)S(1)}, u32[]{:S(2)}, u32[]{:S(2)}) %collective-permute-start.9) | collective-permute-done | bytes 1376288 | tf_op jit(solution)/shard_map/ppermute | solution.py:343
  148.2 4.3 %all-to-all-start.3 = ((bf16[4,48,3584]{2,1,0:T(8,128)(2,1)}), bf16[4,48,3584]{2,1,0:T(8,128)(2,1)}, u32[]{:S(2)}, u32[]{:S(2)}) async-start(bf16[4,48,3584]{2,1,0:T(8,128)(2,1)} %bitcast.95), calls=%async_computation.3 | async-start | bytes 2752512 | tf_op jit(solution)/shard_map/all_to_all | solution.py:361
  153.7 11.4 %shard_map.115 = (bf16[2,384,512]{2,1,0:T(8,128)(2,1)}, bf16[192,3584]{1,0:T(8,128)(2,1)}, bf16[192,3584]{1,0:T(8,128)(2,1)}) custom-call(bf16[192,3584]{1,0:T(8,128)(2,1)} %bitcast.88, bf16[192,3584]{1,0:T(8,128)(2,1)} %copy-done.3, f32[2,384,256]{2,1,0:T(8,128)} %get-tuple-element.111.pre_gate_ref, f32[2,384,256]{2,1,0:T(8,128)} %get-tuple-element.112.pre_up_ref, ...), custom_call_target="tpu_custom_call" | custom-call | flops 1 | bytes 1 | tf_op jit(solution)/shard_map/pallas_call | solution.py:232
  166.7 3.6 %all-to-all-done.3 = bf16[4,48,3584]{2,1,0:T(8,128)(2,1)} async-done(((bf16[4,48,3584]{2,1,0:T(8,128)(2,1)}), bf16[4,48,3584]{2,1,0:T(8,128)(2,1)}, u32[]{:S(2)}, u32[]{:S(2)}) %all-to-all-start.3) | async-done | bytes 1376288 | tf_op jit(solution)/shard_map/all_to_all | solution.py:361
  171.0 3.2 %convolution_convert_fusion.1 = bf16[128,3584]{1,0:T(8,128)(2,1)} fusion(f32[128,192]{0,1:T(8,128)S(1)} %get-tuple-element.151, bf16[192,3584]{1,0:T(8,128)(2,1)} %bitcast.33), kind=kOutput, calls=%fused_computation.3 | convolution fusion | flops 1057423360 | bytes 2392064 | tf_op jit(solution)/shard_map/dot_general | solution.py:111
  176.7 3.8 %all-to-all-start.4 = ((bf16[4,96,3584]{2,1,0:T(8,128)(2,1)}), bf16[4,96,3584]{2,1,0:T(8,128)(2,1)S(1)}, u32[]{:S(2)}, u32[]{:S(2)}) async-start(bf16[4,96,3584]{2,1,0:T(8,128)(2,1)} %bitcast.91), calls=%async_computation.4 | async-start | bytes 5505024 | tf_op jit(solution)/shard_map/all_to_all | solution.py:361
  181.1 2.5 collective-permute-start.13
  186.9 7.6 %shard_map.117 = bf16[256,3584]{1,0:T(8,128)(2,1)} custom-call(s32[1]{0:T(128)} %bitcast.40.which_ref, bf16[2,384,256]{2,1,0:T(8,128)(2,1)} %get-tuple-element.129.refs_0_, bf16[2,384,256]{2,1,0:T(8,128)(2,1)} %get-tuple-element.130.refs_1_, bf16[4,2,48,3584]{3,2,1,0:T(8,128)(2,1)} %bitcast.70, bf16[4,2,48,3584]{3,2,1,0:T(8,128)(2,1)} %bitcast.23.b_ref.refs_3_.refs_5_, ...), custom_call_target="tpu_custom_call" | custom-call | flops 1 | bytes 1 | tf_op jit(solution)/shard_map/pallas_call | solution.py:266
  194.5 7.6 %shard_map.116 = bf16[256,3584]{1,0:T(8,128)(2,1)} custom-call(s32[1]{0:T(128)S(6)} %sub.37.which_ref, bf16[2,384,256]{2,1,0:T(8,128)(2,1)} %get-tuple-element.129.refs_0_, bf16[2,384,256]{2,1,0:T(8,128)(2,1)} %get-tuple-element.130.refs_1_, bf16[4,2,48,3584]{3,2,1,0:T(8,128)(2,1)} %bitcast.71, bf16[4,2,48,3584]{3,2,1,0:T(8,128)(2,1)} %bitcast.23.b_ref.refs_3_.refs_5_, ...), custom_call_target="tpu_custom_call" | custom-call | flops 1 | bytes 1 | tf_op jit(solution)/shard_map/pallas_call | solution.py:266
  202.1 20.1 %collective-permute-done.14.refs_2_ = bf16[384,512]{1,0:T(8,128)(2,1)S(1)} collective-permute-done((bf16[384,512]{1,0:T(8,128)(2,1)S(1)}, bf16[384,512]{1,0:T(8,128)(2,1)S(1)}, u32[]{:S(2)}, u32[]{:S(2)}) %collective-permute-start.14) | collective-permute-done | bytes 393248 | tf_op jit(solution)/shard_map/ppermute | solution.py:352
  222.2 8.0 %collective-permute-done.15.refs_3_ = bf16[384,512]{1,0:T(8,128)(2,1)S(1)} collective-permute-done((bf16[384,512]{1,0:T(8,128)(2,1)S(1)}, bf16[384,512]{1,0:T(8,128)(2,1)S(1)}, u32[]{:S(2)}, u32[]{:S(2)}) %collective-permute-start.15) | collective-permute-done | bytes 393248 | tf_op jit(solution)/shard_map/ppermute | solution.py:352
  233.5 4.9 %all-to-all-start.5 = ((bf16[4,48,3584]{2,1,0:T(8,128)(2,1)}), bf16[4,48,3584]{2,1,0:T(8,128)(2,1)}, u32[]{:S(2)}, u32[]{:S(2)}) async-start(bf16[4,48,3584]{2,1,0:T(8,128)(2,1)} %bitcast.92), calls=%async_computation.5 | async-start | bytes 2752512 | tf_op jit(solution)/shard_map/all_to_all | solution.py:361
  241.9 12.1 %shard_map.118 = (bf16[3584,256]{1,0:T(8,128)(2,1)}, bf16[3584,256]{1,0:T(8,128)(2,1)}) custom-call(s32[1]{0:T(128)} %bitcast.40.which_ref, bf16[2,384,512]{2,1,0:T(8,128)(2,1)} %get-tuple-element.126.refs_0_, bf16[2,384,512]{2,1,0:T(8,128)(2,1)} %get-tuple-element.127.refs_1_, bf16[384,512]{1,0:T(8,128)(2,1)} %copy-done.12, bf16[384,512]{1,0:T(8,128)(2,1)} %copy-done.13, ...), custom_call_target="tpu_custom_call" | custom-call | flops 1 | bytes 1 | tf_op jit(solution)/shard_map/pallas_call | solution.py:299
  254.0 21.0 %collective-permute-done.18 = bf16[256,3584]{1,0:T(8,128)(2,1)} collective-permute-done((bf16[256,3584]{1,0:T(8,128)(2,1)}, bf16[256,3584]{1,0:T(8,128)(2,1)}, u32[]{:S(2)}, u32[]{:S(2)}) %collective-permute-start.18) | collective-permute-done | bytes 1835040 | tf_op jit(solution)/shard_map/ppermute | solution.py:352
  275.0 3.2 %add_convert_fusion = bf16[256,3584]{1,0:T(8,128)(2,1)} fusion(bf16[256,3584]{1,0:T(8,128)(2,1)} %collective-permute-done.18, bf16[256,3584]{1,0:T(8,128)(2,1)S(1)} %copy-done.4), kind=kLoop, calls=%fused_computation.4 | loop fusion | flops 3670016 | bytes 5505024 | tf_op jit(solution)/shard_map/convert_element_type | solution.py:479
  278.1 2.3 fusion.11
  280.4 2.3 add_convert_fusion.5
  284.3 3.2 %shard_map.119 = bf16[128,3584]{1,0:T(8,128)(2,1)} custom-call(bf16[128,384]{1,0:T(8,128)(2,1)} %copy.58.matrix_ref, bf16[384,3584]{1,0:T(8,128)(2,1)} %bitcast.86, bf16[128,3584]{1,0:T(8,128)(2,1)} %collective-permute-done.17.got_ref), custom_call_target="tpu_custom_call" | custom-call | flops 1 | bytes 50000000 | tf_op jit(solution)/shard_map/pallas_call | solution.py:94
  (134 shorter events, 51.8 us)
Async XLA Ops:
  1.6 11.4 %collective-permute-start = (bf16[16,3584]{1,0:T(8,128)(2,1)S(1)}, bf16[16,3584]{1,0:T(8,128)(2,1)S(1)}, u32[]{:S(2)}, u32[]{:S(2)}) collective-permute-start(bf16[16,3584]{1,0:T(8,128)(2,1)S(1)} %slice_bitcast_fusion.1), channel_id=1, source_target_pairs={{0,8},{1,9},{2,10},{3,11},{4,12},{5,13},{6,14},{7,15},{8,0},{9,1},... | collective-permute-start | bytes 344072 | tf_op jit(solution)/shard_map/ppermute | solution.py:343
  13.7 53.2 %all-to-all-start = ((bf16[4,96,3584]{2,1,0:T(8,128)(2,1)}), bf16[4,96,3584]{2,1,0:T(8,128)(2,1)S(1)}, u32[]{:S(2)}, u32[]{:S(2)}) async-start(bf16[4,96,3584]{2,1,0:T(8,128)(2,1)} %bitcast.98), calls=%async_computation | async-start | bytes 5505024 | tf_op jit(solution)/shard_map/all_to_all | solution.py:361
  17.5 31.0 %collective-permute-start.1 = (f32[128,4]{0,1:T(4,128)}, f32[128,4]{0,1:T(4,128)S(1)}, u32[]{:S(2)}, u32[]{:S(2)}) collective-permute-start(f32[128,4]{0,1:T(4,128)} %pad_maximum_fusion.1), channel_id=1, source_target_pairs={{0,8},{1,9},{2,10},{3,11},{4,12},{5,13},{6,14},{7,15},{8,0},{9,1},... | collective-permute-start | bytes 6152 | tf_op jit(solution)/shard_map/ppermute | solution.py:343
  18.3 46.1 %collective-permute-start.2 = (bf16[112,3584]{1,0:T(8,128)(2,1)S(1)}, bf16[112,3584]{1,0:T(8,128)(2,1)}, u32[]{:S(2)}, u32[]{:S(2)}) collective-permute-start(bf16[112,3584]{1,0:T(8,128)(2,1)S(1)} %slice_bitcast_fusion), channel_id=1, source_target_pairs={{0,8},{1,9},{2,10},{3,11},{4,12},{5,13},{6,14},{7,15},{8,0},{9,1},... | collective-permute-start | bytes 2408456 | tf_op jit(solution)/shard_map/ppermute | solution.py:343
  66.9 11.3 %collective-permute-start.4 = (bf16[384,3584]{1,0:T(8,128)(2,1)S(1)}, bf16[384,3584]{1,0:T(8,128)(2,1)}, u32[]{:S(2)}, u32[]{:S(2)}) collective-permute-start(bf16[384,3584]{1,0:T(8,128)(2,1)S(1)} %bitcast.66), channel_id=1, source_target_pairs={{0,1},{1,0},{2,3},{3,2},{4,5},{5,4},{6,7},{7,6},{8,9},{9,8},{10,11... | collective-permute-start | bytes 8257544 | tf_op jit(solution)/shard_map/ppermute | solution.py:343
  67.0 54.0 %all-to-all-start.1 = ((bf16[4,48,3584]{2,1,0:T(8,128)(2,1)}), bf16[4,48,3584]{2,1,0:T(8,128)(2,1)}, u32[]{:S(2)}, u32[]{:S(2)}) async-start(bf16[4,48,3584]{2,1,0:T(8,128)(2,1)} %bitcast.93), calls=%async_computation.1 | async-start | bytes 2752512 | tf_op jit(solution)/shard_map/all_to_all | solution.py:361
  73.7 47.2 %collective-permute-start.5 = (bf16[192,3584]{1,0:T(8,128)(2,1)}, bf16[192,3584]{1,0:T(8,128)(2,1)}, u32[]{:S(2)}, u32[]{:S(2)}) collective-permute-start(bf16[192,3584]{1,0:T(8,128)(2,1)} %bitcast.29), channel_id=1, source_target_pairs={{0,16},{16,0},{1,17},{17,1},{2,18},{18,2},{3,19},{19,3},{4,20},{20... | collective-permute-start | bytes 4128776 | tf_op jit(solution)/shard_map/ppermute | solution.py:352
  75.2 43.1 %collective-permute-start.3 = (bf16[128,3584]{1,0:T(8,128)(2,1)}, bf16[128,3584]{1,0:T(8,128)(2,1)}, u32[]{:S(2)}, u32[]{:S(2)}) collective-permute-start(bf16[128,3584]{1,0:T(8,128)(2,1)} %bitcast.10), channel_id=1, source_target_pairs={{0,8},{1,9},{2,10},{3,11},{4,12},{5,13},{6,14},{7,15},{8,0},{9,1},... | collective-permute-start | bytes 2752520 | tf_op jit(solution)/shard_map/ppermute | solution.py:343
  120.9 4.6 %collective-permute-start.6 = (bf16[192,3584]{1,0:T(8,128)(2,1)}, bf16[192,3584]{1,0:T(8,128)(2,1)S(1)}, u32[]{:S(2)}, u32[]{:S(2)}) collective-permute-start(bf16[192,3584]{1,0:T(8,128)(2,1)} %bitcast.28.a_ref.refs_6_), channel_id=1, source_target_pairs={{0,1},{1,0},{2,3},{3,2},{4,5},{5,4},{6,7},{7,6},{8,9},{9,8},{10,11... | collective-permute-start | bytes 4128776 | tf_op jit(solution)/shard_map/ppermute | solution.py:343
  121.0 16.6 %collective-permute-start.7 = (bf16[192,3584]{1,0:T(8,128)(2,1)}, bf16[192,3584]{1,0:T(8,128)(2,1)}, u32[]{:S(2)}, u32[]{:S(2)}) collective-permute-start(bf16[192,3584]{1,0:T(8,128)(2,1)} %get-tuple-element.102), channel_id=1, source_target_pairs={{0,1},{1,0},{2,3},{3,2},{4,5},{5,4},{6,7},{7,6},{8,9},{9,8},{10,11... | collective-permute-start | bytes 4128776 | tf_op jit(solution)/shard_map/ppermute | solution.py:343
  121.5 21.3 %all-to-all-start.2 = ((bf16[4,48,3584]{2,1,0:T(8,128)(2,1)}), bf16[4,48,3584]{2,1,0:T(8,128)(2,1)S(1)}, u32[]{:S(2)}, u32[]{:S(2)}) async-start(bf16[4,48,3584]{2,1,0:T(8,128)(2,1)} %bitcast.94), calls=%async_computation.2 | async-start | bytes 2752512 | tf_op jit(solution)/shard_map/all_to_all | solution.py:361
  125.2 12.4 %copy-start.8 = (bf16[192,3584]{1,0:T(8,128)(2,1)S(1)}, bf16[192,3584]{1,0:T(8,128)(2,1)}, u32[]{:S(2)}) copy-start(bf16[192,3584]{1,0:T(8,128)(2,1)} %get-tuple-element.101) | copy-start | bytes 4128772
  125.3 15.2 %collective-permute-start.8 = (bf16[192,3584]{1,0:T(8,128)(2,1)}, bf16[192,3584]{1,0:T(8,128)(2,1)}, u32[]{:S(2)}, u32[]{:S(2)}) collective-permute-start(bf16[192,3584]{1,0:T(8,128)(2,1)} %collective-permute-done.5.refs_8_), channel_id=1, source_target_pairs={{0,1},{1,0},{2,3},{3,2},{4,5},{5,4},{6,7},{7,6},{8,9},{9,8},{10,11... | collective-permute-start | bytes 4128776 | tf_op jit(solution)/shard_map/ppermute | solution.py:343
  142.9 3.3 %collective-permute-start.9 = (bf16[192,3584]{1,0:T(8,128)(2,1)}, bf16[192,3584]{1,0:T(8,128)(2,1)S(1)}, u32[]{:S(2)}, u32[]{:S(2)}) collective-permute-start(bf16[192,3584]{1,0:T(8,128)(2,1)} %get-tuple-element.105), channel_id=1, source_target_pairs={{0,1},{1,0},{2,3},{3,2},{4,5},{5,4},{6,7},{7,6},{8,9},{9,8},{10,11... | collective-permute-start | bytes 4128776 | tf_op jit(solution)/shard_map/ppermute | solution.py:343
  147.7 4.9 %collective-permute-start.10 = (bf16[192,3584]{1,0:T(8,128)(2,1)S(1)}, bf16[192,3584]{1,0:T(8,128)(2,1)S(1)}, u32[]{:S(2)}, u32[]{:S(2)}) collective-permute-start(bf16[192,3584]{1,0:T(8,128)(2,1)S(1)} %bitcast.87), channel_id=1, source_target_pairs={{0,1},{1,0},{2,3},{3,2},{4,5},{5,4},{6,7},{7,6},{8,9},{9,8},{10,11... | collective-permute-start | bytes 4128776 | tf_op jit(solution)/shard_map/ppermute | solution.py:343
  147.9 17.2 %collective-permute-start.11 = (bf16[192,3584]{1,0:T(8,128)(2,1)}, bf16[192,3584]{1,0:T(8,128)(2,1)}, u32[]{:S(2)}, u32[]{:S(2)}) collective-permute-start(bf16[192,3584]{1,0:T(8,128)(2,1)} %get-tuple-element.117), channel_id=1, source_target_pairs={{0,1},{1,0},{2,3},{3,2},{4,5},{5,4},{6,7},{7,6},{8,9},{9,8},{10,11... | collective-permute-start | bytes 4128776 | tf_op jit(solution)/shard_map/ppermute | solution.py:343
  148.2 22.1 %all-to-all-start.3 = ((bf16[4,48,3584]{2,1,0:T(8,128)(2,1)}), bf16[4,48,3584]{2,1,0:T(8,128)(2,1)}, u32[]{:S(2)}, u32[]{:S(2)}) async-start(bf16[4,48,3584]{2,1,0:T(8,128)(2,1)} %bitcast.95), calls=%async_computation.3 | async-start | bytes 2752512 | tf_op jit(solution)/shard_map/all_to_all | solution.py:361
  170.4 3.8 %collective-permute-start.12 = (bf16[192,3584]{1,0:T(8,128)(2,1)}, bf16[192,3584]{1,0:T(8,128)(2,1)S(1)}, u32[]{:S(2)}, u32[]{:S(2)}) collective-permute-start(bf16[192,3584]{1,0:T(8,128)(2,1)} %get-tuple-element.119), channel_id=1, source_target_pairs={{0,1},{1,0},{2,3},{3,2},{4,5},{5,4},{6,7},{7,6},{8,9},{9,8},{10,11... | collective-permute-start | bytes 4128776 | tf_op jit(solution)/shard_map/ppermute | solution.py:343
  176.7 56.3 %all-to-all-start.4 = ((bf16[4,96,3584]{2,1,0:T(8,128)(2,1)}), bf16[4,96,3584]{2,1,0:T(8,128)(2,1)S(1)}, u32[]{:S(2)}, u32[]{:S(2)}) async-start(bf16[4,96,3584]{2,1,0:T(8,128)(2,1)} %bitcast.91), calls=%async_computation.4 | async-start | bytes 5505024 | tf_op jit(solution)/shard_map/all_to_all | solution.py:361
  180.5 50.5 %collective-permute-start.16 = (bf16[192,3584]{1,0:T(8,128)(2,1)}, bf16[192,3584]{1,0:T(8,128)(2,1)}, u32[]{:S(2)}, u32[]{:S(2)}) collective-permute-start(bf16[192,3584]{1,0:T(8,128)(2,1)} %bitcast.28.a_ref.refs_6_), channel_id=1, source_target_pairs={{0,16},{16,0},{1,17},{17,1},{2,18},{18,2},{3,19},{19,3},{4,20},{20... | collective-permute-start | bytes 4128776 | tf_op jit(solution)/shard_map/ppermute | solution.py:352
  181.1 49.8 %collective-permute-start.13 = (bf16[128,3584]{1,0:T(8,128)(2,1)}, bf16[128,3584]{1,0:T(8,128)(2,1)}, u32[]{:S(2)}, u32[]{:S(2)}) collective-permute-start(bf16[128,3584]{1,0:T(8,128)(2,1)} %convolution_convert_fusion.1), channel_id=1, source_target_pairs={{0,8},{1,9},{2,10},{3,11},{4,12},{5,13},{6,14},{7,15},{8,0},{9,1},... | collective-permute-start | bytes 2752520 | tf_op jit(solution)/shard_map/ppermute | solution.py:343
  183.7 38.5 %collective-permute-start.14 = (bf16[384,512]{1,0:T(8,128)(2,1)S(1)}, bf16[384,512]{1,0:T(8,128)(2,1)S(1)}, u32[]{:S(2)}, u32[]{:S(2)}) collective-permute-start(bf16[384,512]{1,0:T(8,128)(2,1)S(1)} %dynamic-slice_bitcast_fusion.1), channel_id=1, source_target_pairs={{0,16},{16,0},{1,17},{17,1},{2,18},{18,2},{3,19},{19,3},{4,20},{20... | collective-permute-start | bytes 1179656 | tf_op jit(solution)/shard_map/ppermute | solution.py:352
  186.3 44.0 %collective-permute-start.15 = (bf16[384,512]{1,0:T(8,128)(2,1)S(1)}, bf16[384,512]{1,0:T(8,128)(2,1)S(1)}, u32[]{:S(2)}, u32[]{:S(2)}) collective-permute-start(bf16[384,512]{1,0:T(8,128)(2,1)S(1)} %dynamic-slice_bitcast_fusion), channel_id=1, source_target_pairs={{0,16},{16,0},{1,17},{17,1},{2,18},{18,2},{3,19},{19,3},{4,20},{20... | collective-permute-start | bytes 1179656 | tf_op jit(solution)/shard_map/ppermute | solution.py:352
  202.1 36.3 %copy-start.17 = (f32[1,128,2]{1,2,0:T(2,128)S(1)}, f32[1,128,2]{1,2,0:T(2,128)}, u32[]{:S(2)}) copy-start(f32[1,128,2]{1,2,0:T(2,128)} %param.10) | copy-start | bytes 3076
  202.1 36.3 %copy-start.19 = (s32[128,2]{0,1:T(2,128)S(1)}, s32[128,2]{0,1:T(2,128)}, u32[]{:S(2)}) copy-start(s32[128,2]{0,1:T(2,128)} %copy-done.18) | copy-start | bytes 3076
  202.1 37.1 %copy-start.14 = (bf16[128,192]{0,1:T(8,128)(2,1)S(1)}, bf16[128,192]{0,1:T(8,128)(2,1)}, u32[]{:S(2)}) copy-start(bf16[128,192]{0,1:T(8,128)(2,1)} %get-tuple-element.152) | copy-start | bytes 147460
  222.2 18.6 %copy-start.12 = (bf16[384,512]{1,0:T(8,128)(2,1)}, bf16[384,512]{1,0:T(8,128)(2,1)S(1)}, u32[]{:S(2)}) copy-start(bf16[384,512]{1,0:T(8,128)(2,1)S(1)} %collective-permute-done.14.refs_2_) | copy-start | bytes 1179652
  233.0 42.0 %collective-permute-start.18 = (bf16[256,3584]{1,0:T(8,128)(2,1)}, bf16[256,3584]{1,0:T(8,128)(2,1)}, u32[]{:S(2)}, u32[]{:S(2)}) collective-permute-start(bf16[256,3584]{1,0:T(8,128)(2,1)} %shard_map.116), channel_id=1, source_target_pairs={{0,16},{16,0},{1,17},{17,1},{2,18},{18,2},{3,19},{19,3},{4,20},{20... | collective-permute-start | bytes 5505032 | tf_op jit(solution)/shard_map/ppermute | solution.py:352
  233.5 8.4 %collective-permute-start.19 = (bf16[192,3584]{1,0:T(8,128)(2,1)}, bf16[192,3584]{1,0:T(8,128)(2,1)}, u32[]{:S(2)}, u32[]{:S(2)}) collective-permute-start(bf16[192,3584]{1,0:T(8,128)(2,1)} %collective-permute-done.16.refs_10_), channel_id=1, source_target_pairs={{0,1},{1,0},{2,3},{3,2},{4,5},{5,4},{6,7},{7,6},{8,9},{9,8},{10,11... | collective-permute-start | bytes 4128776 | tf_op jit(solution)/shard_map/ppermute | solution.py:343
  233.5 44.6 %all-to-all-start.5 = ((bf16[4,48,3584]{2,1,0:T(8,128)(2,1)}), bf16[4,48,3584]{2,1,0:T(8,128)(2,1)}, u32[]{:S(2)}, u32[]{:S(2)}) async-start(bf16[4,48,3584]{2,1,0:T(8,128)(2,1)} %bitcast.92), calls=%async_computation.5 | async-start | bytes 2752512 | tf_op jit(solution)/shard_map/all_to_all | solution.py:361
  240.8 34.1 %copy-start.4 = (bf16[256,3584]{1,0:T(8,128)(2,1)S(1)}, bf16[256,3584]{1,0:T(8,128)(2,1)}, u32[]{:S(2)}) copy-start(bf16[256,3584]{1,0:T(8,128)(2,1)} %shard_map.117) | copy-start | bytes 5505028
  240.8 43.4 %collective-permute-start.17 = (bf16[128,3584]{1,0:T(8,128)(2,1)}, bf16[128,3584]{1,0:T(8,128)(2,1)}, u32[]{:S(2)}, u32[]{:S(2)}) collective-permute-start(bf16[128,3584]{1,0:T(8,128)(2,1)} %convolution_convert_fusion), channel_id=1, source_target_pairs={{0,8},{1,9},{2,10},{3,11},{4,12},{5,13},{6,14},{7,15},{8,0},{9,1},... | collective-permute-start | bytes 2752520 | tf_op jit(solution)/shard_map/ppermute | solution.py:343
  (21 other events, 104.6 us)

commit v12 on v11

--- a/solution.py
+++ b/solution.py
@@ -13,7 +13,7 @@
 NN = ((1,), (0,))
 NT = ((1,), (1,))
 TN = ((0,), (0,))
-VMEM_BYTES = 56 * 1024 * 1024
+VMEM_BYTES = 30 * 1024 * 1024
 
 
 def dot(a, b, dims):
@@ -379,30 +379,31 @@
         return jnp.concatenate(pair, axis=2).reshape(matrix.shape[0], 2 * near * piece)
 
     count = near * piece
-    first = acts.shape[1] // 8
-    far_acts_0 = far(acts[0, :first])
     meta = jnp.concatenate([expert_ids[0].astype(F32), route_weights[0]], axis=1)
+    far_meta = far(meta)
     own_placing, own_back, own_weighting, own_gain = route(meta, half, chips, capacity)
     both_placing = jnp.concatenate([of_set(own_placing.T, 0), of_set(own_placing.T, 1)], axis=0).T
     both_gain = jnp.stack([jnp.ones_like(own_gain).reshape(near, piece), own_gain.reshape(near, piece)], axis=1)
     own = place(
         both_placing, jnp.concatenate([acts[0], grad_out[0]], axis=0), both_gain.reshape(2 * count, 1)
     )
-    own, far_acts_0, acts_1, meta = tie(own, far_acts_0, acts[0, first:], meta)
-
-    far_acts_1 = far(acts_1)
+    own, far_meta, tokens = tie(own, far_meta, acts[0])
+
+    far_acts = far(tokens)
     own = near_exchange(own)
-    far_meta = far(meta)
     far_placing, far_back, far_weighting, far_gain = route(far_meta, half, chips, capacity)
-    far_in = place_far(far_placing, [far_acts_0, far_acts_1])
-    far_in, own, far_placing, far_gain, grads = tie(far_in, own, far_placing, far_gain, grad_out[0])
+    own = own.reshape(near, 2, piece, width)
+    own_in = own[:, 0].reshape(count, width)
+    far_acts, own, own_in, far_placing, far_gain, grads = tie(
+        far_acts, own, own_in, far_placing, far_gain, grad_out[0]
+    )
+    far_in = place_far(far_placing, [far_acts])
+    far_in, own, own_in, grads = tie(far_in, own, own_in, grads)
 
     far_grads = far(grads)
     far_in = near_exchange(far_in)
     own_b = swap(own)
-    own = own.reshape(near, 2, piece, width)
-    own_b = own_b.reshape(near, 2, piece, width)
-    mirror_own = mirror(own[:, 0].reshape(count, width))
+    mirror_own = mirror(own_in)
     own_pre_gate, own_pre_up, own_hidden, own_out, own_out_b = forward(
         count, ((own, 0), (own_b, 0)), *weights
     )

time: 289 us -> 307 us (1.062)
  local copies, waits for them, and re-layouts: 18.4 us -> 43.9 us
  Pallas kernels: 79.3 us -> 60.9 us
  waiting for transfers between devices: 112 us -> 128 us
  starting transfers between devices: 45 us -> 38.3 us
    all_to_all x6, waiting for transfers between devices: 8 us -> 52.3 us  [near_exchange(): lax.all_to_all(rows.reshape(near, -1, width), 'expert', split_axis=0, con...]
    unnamed x54 -> x94, local copies, waits for them, and re-layouts: 4.11 us -> 34.7 us
    ppermute x15 -> x14, waiting for transfers between devices: 54.5 us -> 28 us  [hop(): lax.ppermute(rows, 'expert', [(i, i ^ distance) for i in range(devices)])]
    pallas_call x2, Pallas kernels: 21.4 us -> 14.2 us  [forward(): kernel_call(body, (2,), [row_spec(a, width) for a in rows] + [columns, co...]
    ppermute x15 -> x14, starting transfers between devices: 14.1 us -> 7.42 us  [hop(): lax.ppermute(rows, 'expert', [(i, i ^ distance) for i in range(devices)])]
    pallas_call x2, Pallas kernels: 22.1 us -> 15.6 us  [backward(): kernel_call(body, (2,), [row_spec(a, width) for a in rows_grad] + [units,...]
    convert_element_type x4, other arithmetic: 6.46 us -> 9.66 us  [expert_sum(): return (mine.astype(F32) + swap(other).astype(F32)).astype(BF16)]
  transfers between devices with their start and end apart: 26 -> 25, of which waited for: 13 -> 8; matrix products, arithmetic and copies ran while one was open for 14% -> 12% of each run, Pallas kernels for 26% -> 18%
where the time goes in v12:
time: 307 us; the launch traced here: 305 us
  waiting for transfers between devices  128 us (42%)
  Pallas kernels  60.9 us (20%)
  local copies, waits for them, and re-layouts  43.9 us (14%)
  starting transfers between devices  38.3 us (12%)
  other arithmetic  20.7 us (7%)
  matrix products  12.8 us (4%)
    all_to_all x6, waiting for transfers between devices, near_exchange(): lax.all_to_all(rows.reshape(near, -1, width), 'expert', split_axis=0, con...  52.3 us
    ppermute x5, waiting for transfers between devices, mirror(): lax.ppermute(rows, 'pipe', [(p, rank_count - 1 - p) for p in range(rank_c...  47.6 us
    unnamed x94, local copies, waits for them, and re-layouts  34.7 us
    ppermute x14, waiting for transfers between devices, hop(): lax.ppermute(rows, 'expert', [(i, i ^ distance) for i in range(devices)])  28 us
    all_to_all x6, starting transfers between devices, near_exchange(): lax.all_to_all(rows.reshape(near, -1, width), 'expert', split_axis=0, con...  26 us
    pallas_call x2, Pallas kernels, backward(): kernel_call(body, (2,), [row_spec(a, width) for a in rows_grad] + [units,...  15.6 us
    pallas_call x2, Pallas kernels, forward(): kernel_call(body, (2,), [row_spec(a, width) for a in rows] + [columns, co...  14.2 us
    pallas_call x2, Pallas kernels, down_grad(): kernel_call(body, (width // tile,), [pl.BlockSpec((1, 2 * count, half_uni...  13.2 us
  transfers between devices with their start and end apart: 25, of which 8 were waited for; matrix products, arithmetic and copies ran while one was open for 12% of the time, Pallas kernels for 18%

profile of v12, /device:TPU:0, one launch (start us, length us, event | category | flops | bytes accessed | tf_op | source)
XLA Modules:
  0.0 305.5 jit_solution(11971467426311404041)
XLA Ops:
  2.0 4.0 %collective-permute-start = (f32[128,4]{0,1:T(4,128)S(1)}, f32[128,4]{0,1:T(4,128)S(1)}, u32[]{:S(2)}, u32[]{:S(2)}) collective-permute-start(f32[128,4]{0,1:T(4,128)S(1)} %pad_maximum_fusion.1), channel_id=1, source_target_pairs={{0,8},{1,9},{2,10},{3,11},{4,12},{5,13},{6,14},{7,15},{8,0},{9,1},... | collective-permute-start | bytes 6152 | tf_op jit(solution)/shard_map/ppermute | solution.py:343
  8.8 3.9 %fusion = bf16[384,3584]{1,0:T(8,128)(2,1)} fusion(f32[384]{0:T(512)S(1)} %mul.86, bf16[128,3584]{1,0:T(8,128)(2,1)} %bitcast.108, bf16[128,3584]{1,0:T(8,128)(2,1)} %bitcast.106, bf16[128,384]{0,1:T(8,128)(2,1)S(1)} %bitcast.97, bf16[128,384]{0,1:T(8,128)(2,1)S(1)} %bitcast.96), kind=kOutput, calls=%fused_computation.1 | convolution fusion | flops 711458816 | bytes 4785664 | tf_op jit(solution)/shard_map/dot_general | solution.py:20
  12.7 3.8 %all-to-all-start = ((bf16[4,96,3584]{2,1,0:T(8,128)(2,1)}), bf16[4,96,3584]{2,1,0:T(8,128)(2,1)S(1)}, u32[]{:S(2)}, u32[]{:S(2)}) async-start(bf16[4,96,3584]{2,1,0:T(8,128)(2,1)} %bitcast.86), calls=%async_computation | async-start | bytes 5505024 | tf_op jit(solution)/shard_map/all_to_all | solution.py:361
  17.9 49.9 %all-to-all-done = bf16[4,96,3584]{2,1,0:T(8,128)(2,1)S(1)} async-done(((bf16[4,96,3584]{2,1,0:T(8,128)(2,1)}), bf16[4,96,3584]{2,1,0:T(8,128)(2,1)S(1)}, u32[]{:S(2)}, u32[]{:S(2)}) %all-to-all-start) | async-done | bytes 2752544 | tf_op jit(solution)/shard_map/all_to_all | solution.py:361
  71.9 4.3 %all-to-all-start.1 = ((bf16[4,48,3584]{2,1,0:T(8,128)(2,1)}), bf16[4,48,3584]{2,1,0:T(8,128)(2,1)}, u32[]{:S(2)}, u32[]{:S(2)}) async-start(bf16[4,48,3584]{2,1,0:T(8,128)(2,1)} %bitcast.80), calls=%async_computation.1 | async-start | bytes 2752512 | tf_op jit(solution)/shard_map/all_to_all | solution.py:361
  84.8 6.9 %shard_map.111 = (f32[2,384,256]{2,1,0:T(8,128)S(1)}, f32[2,384,256]{2,1,0:T(8,128)S(1)}, bf16[2,384,256]{2,1,0:T(8,128)(2,1)S(1)}, bf16[192,3584]{1,0:T(8,128)(2,1)S(1)}, bf16[192,3584]{1,0:T(8,128)(2,1)S(1)}) custom-call(bf16[4,2,48,3584]{3,2,1,0:T(8,128)(2,1)S(1)} %bitcast.62, bf16[4,2,48,3584]{3,2,1,0:T(8,128)(2,1)} %collective-permute-done.3.b_ref.refs_3_.refs_5_, ...), custom_call_target="tpu_custom_call" | custom-call | flops 1 | bytes 1 | tf_op jit(solution)/shard_map/pallas_call | solution.py:177
  94.6 8.1 %shard_map.112 = (bf16[2,384,512]{2,1,0:T(8,128)(2,1)S(1)}, bf16[192,3584]{1,0:T(8,128)(2,1)S(1)}, bf16[192,3584]{1,0:T(8,128)(2,1)}) custom-call(bf16[4,2,48,3584]{3,2,1,0:T(8,128)(2,1)S(1)} %bitcast.63, bf16[4,2,48,3584]{3,2,1,0:T(8,128)(2,1)} %collective-permute-done.3.b_ref.refs_3_.refs_5_, f32[2,384,256]{2,1,0:T(8,128)S(1)} %get-tuple-element.94.pre_gate_ref, ...), custom_call_target="tpu_custom_call" | custom-call | flops 1 | bytes 1 | tf_op jit(solution)/shard_map/pallas_call | solution.py:232
  102.8 18.4 %collective-permute-done.2.refs_1_ = bf16[128,3584]{1,0:T(8,128)(2,1)} collective-permute-done((bf16[128,3584]{1,0:T(8,128)(2,1)}, bf16[128,3584]{1,0:T(8,128)(2,1)}, u32[]{:S(2)}, u32[]{:S(2)}) %collective-permute-start.2) | collective-permute-done | bytes 917536 | tf_op jit(solution)/shard_map/ppermute | solution.py:343
  124.7 4.5 %all-to-all-start.2 = ((bf16[4,48,3584]{2,1,0:T(8,128)(2,1)}), bf16[4,48,3584]{2,1,0:T(8,128)(2,1)}, u32[]{:S(2)}, u32[]{:S(2)}) async-start(bf16[4,48,3584]{2,1,0:T(8,128)(2,1)} %bitcast.79), calls=%async_computation.2 | async-start | bytes 2752512 | tf_op jit(solution)/shard_map/all_to_all | solution.py:361
  135.5 7.3 %shard_map.114 = (f32[2,384,256]{2,1,0:T(8,128)S(1)}, f32[2,384,256]{2,1,0:T(8,128)S(1)}, bf16[2,384,256]{2,1,0:T(8,128)(2,1)S(1)}, bf16[192,3584]{1,0:T(8,128)(2,1)S(1)}, bf16[192,3584]{1,0:T(8,128)(2,1)S(1)}) custom-call(bf16[192,3584]{1,0:T(8,128)(2,1)} %bitcast.25.a_ref.refs_6_, bf16[192,3584]{1,0:T(8,128)(2,1)} %collective-permute-done.5.b_ref.refs_7_, ...), custom_call_target="tpu_custom_call" | custom-call | flops 1 | bytes 1 | tf_op jit(solution)/shard_map/pallas_call | solution.py:177
  143.9 3.8 %add_convert_fusion.4 = bf16[192,3584]{1,0:T(8,128)(2,1)} fusion(bf16[192,3584]{1,0:T(8,128)(2,1)} %collective-permute-done.6, bf16[192,3584]{1,0:T(8,128)(2,1)S(1)} %copy-done.23), kind=kLoop, calls=%fused_computation.9 | loop fusion | flops 2752512 | bytes 4128768 | tf_op jit(solution)/shard_map/convert_element_type | solution.py:374
  149.2 3.0 collective-permute-done.8
  152.2 2.8 add_convert_fusion.3
  155.5 4.3 %all-to-all-start.3 = ((bf16[4,48,3584]{2,1,0:T(8,128)(2,1)}), bf16[4,48,3584]{2,1,0:T(8,128)(2,1)}, u32[]{:S(2)}, u32[]{:S(2)}) async-start(bf16[4,48,3584]{2,1,0:T(8,128)(2,1)} %bitcast.83), calls=%async_computation.3 | async-start | bytes 2752512 | tf_op jit(solution)/shard_map/all_to_all | solution.py:361
  168.2 7.5 %shard_map.115 = (bf16[2,384,512]{2,1,0:T(8,128)(2,1)S(1)}, bf16[192,3584]{1,0:T(8,128)(2,1)S(1)}, bf16[192,3584]{1,0:T(8,128)(2,1)S(1)}) custom-call(bf16[192,3584]{1,0:T(8,128)(2,1)} %bitcast.27.a_ref.refs_4_, bf16[192,3584]{1,0:T(8,128)(2,1)} %collective-permute-done.9.b_ref.refs_5_, f32[2,384,256]{2,1,0:T(8,128)S(1)} %copy-done.30, ...), custom_call_target="tpu_custom_call" | custom-call | flops 1 | bytes 1 | tf_op jit(solution)/shard_map/pallas_call | solution.py:232
  178.8 2.7 add_convert_fusion.2
  182.6 3.2 %convolution_convert_fusion.1 = bf16[128,3584]{1,0:T(8,128)(2,1)} fusion(f32[128,192]{0,1:T(8,128)S(1)} %get-tuple-element.159, bf16[192,3584]{1,0:T(8,128)(2,1)} %bitcast.29), kind=kOutput, calls=%fused_computation.3 | convolution fusion | flops 1057423360 | bytes 2392064 | tf_op jit(solution)/shard_map/dot_general | solution.py:111
  189.1 4.6 %all-to-all-start.4 = ((bf16[4,96,3584]{2,1,0:T(8,128)(2,1)}), bf16[4,96,3584]{2,1,0:T(8,128)(2,1)}, u32[]{:S(2)}, u32[]{:S(2)}) async-start(bf16[4,96,3584]{2,1,0:T(8,128)(2,1)} %bitcast.81), calls=%async_computation.4 | async-start | bytes 5505024 | tf_op jit(solution)/shard_map/all_to_all | solution.py:361
  197.5 6.3 %shard_map.117 = bf16[256,3584]{1,0:T(8,128)(2,1)S(1)} custom-call(s32[1]{0:T(128)} %bitcast.36.which_ref, bf16[2,384,256]{2,1,0:T(8,128)(2,1)S(1)} %copy-done.17, bf16[2,384,256]{2,1,0:T(8,128)(2,1)S(1)} %copy-done.19, bf16[4,2,48,3584]{3,2,1,0:T(8,128)(2,1)S(1)} %bitcast.64, bf16[4,2,48,3584]{3,2,1,0:T(8,128)(2,1)} %collective-permute-done.3.b_ref.refs_3_.refs_5_, ...), custom_call_target="tpu_custom_call" | custom-call | flops 1 | bytes 1 | tf_op jit(solution)/shard_map/pallas_call | solution.py:266
  203.8 6.9 %shard_map.116 = bf16[256,3584]{1,0:T(8,128)(2,1)S(1)} custom-call(s32[1]{0:T(128)S(6)} %sub.37.which_ref, bf16[2,384,256]{2,1,0:T(8,128)(2,1)S(1)} %copy-done.17, bf16[2,384,256]{2,1,0:T(8,128)(2,1)S(1)} %copy-done.19, bf16[4,2,48,3584]{3,2,1,0:T(8,128)(2,1)S(1)} %bitcast.65, bf16[4,2,48,3584]{3,2,1,0:T(8,128)(2,1)} %collective-permute-done.3.b_ref.refs_3_.refs_5_, ...), custom_call_target="tpu_custom_call" | custom-call | flops 1 | bytes 1 | tf_op jit(solution)/shard_map/pallas_call | solution.py:266
  212.0 23.5 %collective-permute-done.13.refs_2_ = bf16[384,512]{1,0:T(8,128)(2,1)S(1)} collective-permute-done((bf16[384,512]{1,0:T(8,128)(2,1)S(1)}, bf16[384,512]{1,0:T(8,128)(2,1)S(1)}, u32[]{:S(2)}, u32[]{:S(2)}) %collective-permute-start.13) | collective-permute-done | bytes 393248 | tf_op jit(solution)/shard_map/ppermute | solution.py:352
  236.2 6.9 %collective-permute-done.14.refs_3_ = bf16[384,512]{1,0:T(8,128)(2,1)S(1)} collective-permute-done((bf16[384,512]{1,0:T(8,128)(2,1)S(1)}, bf16[384,512]{1,0:T(8,128)(2,1)S(1)}, u32[]{:S(2)}, u32[]{:S(2)}) %collective-permute-start.14) | collective-permute-done | bytes 393248 | tf_op jit(solution)/shard_map/ppermute | solution.py:352
  243.8 2.3 all-to-all-done.4
  246.7 4.5 %all-to-all-start.5 = ((bf16[4,48,3584]{2,1,0:T(8,128)(2,1)}), bf16[4,48,3584]{2,1,0:T(8,128)(2,1)}, u32[]{:S(2)}, u32[]{:S(2)}) async-start(bf16[4,48,3584]{2,1,0:T(8,128)(2,1)} %bitcast.82), calls=%async_computation.5 | async-start | bytes 2752512 | tf_op jit(solution)/shard_map/all_to_all | solution.py:361
  255.1 3.5 %convolution_convert_fusion = bf16[128,3584]{1,0:T(8,128)(2,1)} fusion(bf16[128,384]{0,1:T(8,128)(2,1)S(1)} %bitcast.92, bf16[384,3584]{1,0:T(8,128)(2,1)} %bitcast.33.rows_ref), kind=kOutput, calls=%fused_computation.2 | convolution fusion | flops 352780288 | bytes 3768320 | tf_op jit(solution)/shard_map/dot_general | solution.py:20
  259.6 11.2 %shard_map.118 = (bf16[3584,256]{1,0:T(8,128)(2,1)}, bf16[3584,256]{1,0:T(8,128)(2,1)}) custom-call(s32[1]{0:T(128)} %bitcast.36.which_ref, bf16[2,384,512]{2,1,0:T(8,128)(2,1)S(1)} %get-tuple-element.134.refs_0_, bf16[2,384,512]{2,1,0:T(8,128)(2,1)S(1)} %copy-done.15, bf16[384,512]{1,0:T(8,128)(2,1)S(1)} %copy-done.38, bf16[384,512]{1,0:T(8,128)(2,1)S(1)} %copy-done.40, ...), custom_call_target="tpu_custom_call" | custom-call | flops 1 | bytes 1 | tf_op jit(solution)/shard_map/pallas_call | solution.py:299
  270.8 17.2 %collective-permute-done.17 = bf16[256,3584]{1,0:T(8,128)(2,1)} collective-permute-done((bf16[256,3584]{1,0:T(8,128)(2,1)}, bf16[256,3584]{1,0:T(8,128)(2,1)}, u32[]{:S(2)}, u32[]{:S(2)}) %collective-permute-start.17) | collective-permute-done | bytes 1835040 | tf_op jit(solution)/shard_map/ppermute | solution.py:352
  288.0 3.2 %add_convert_fusion = bf16[256,3584]{1,0:T(8,128)(2,1)} fusion(bf16[256,3584]{1,0:T(8,128)(2,1)} %collective-permute-done.17, bf16[256,3584]{1,0:T(8,128)(2,1)S(1)} %copy-done.10), kind=kLoop, calls=%fused_computation.4 | loop fusion | flops 3670016 | bytes 5505024 | tf_op jit(solution)/shard_map/convert_element_type | solution.py:480
  291.2 2.3 fusion.11
  293.5 2.3 add_convert_fusion.5
  295.7 6.6 %collective-permute-done.16.got_ref = bf16[128,3584]{1,0:T(8,128)(2,1)} collective-permute-done((bf16[128,3584]{1,0:T(8,128)(2,1)}, bf16[128,3584]{1,0:T(8,128)(2,1)}, u32[]{:S(2)}, u32[]{:S(2)}) %collective-permute-start.16) | collective-permute-done | bytes 917536 | tf_op jit(solution)/shard_map/ppermute | solution.py:343
  302.3 3.2 %shard_map.119 = bf16[128,3584]{1,0:T(8,128)(2,1)} custom-call(bf16[128,384]{1,0:T(8,128)(2,1)S(1)} %copy-done.36, bf16[384,3584]{1,0:T(8,128)(2,1)} %bitcast.33.rows_ref, bf16[128,3584]{1,0:T(8,128)(2,1)} %collective-permute-done.16.got_ref), custom_call_target="tpu_custom_call" | custom-call | flops 1 | bytes 50000000 | tf_op jit(solution)/shard_map/pallas_call | solution.py:94
  (170 shorter events, 61.6 us)
Async XLA Ops:
  2.0 10.7 %collective-permute-start = (f32[128,4]{0,1:T(4,128)S(1)}, f32[128,4]{0,1:T(4,128)S(1)}, u32[]{:S(2)}, u32[]{:S(2)}) collective-permute-start(f32[128,4]{0,1:T(4,128)S(1)} %pad_maximum_fusion.1), channel_id=1, source_target_pairs={{0,8},{1,9},{2,10},{3,11},{4,12},{5,13},{6,14},{7,15},{8,0},{9,1},... | collective-permute-start | bytes 6152 | tf_op jit(solution)/shard_map/ppermute | solution.py:343
  12.7 55.2 %all-to-all-start = ((bf16[4,96,3584]{2,1,0:T(8,128)(2,1)}), bf16[4,96,3584]{2,1,0:T(8,128)(2,1)S(1)}, u32[]{:S(2)}, u32[]{:S(2)}) async-start(bf16[4,96,3584]{2,1,0:T(8,128)(2,1)} %bitcast.86), calls=%async_computation | async-start | bytes 5505024 | tf_op jit(solution)/shard_map/all_to_all | solution.py:361
  16.5 52.6 %collective-permute-start.1 = (bf16[128,3584]{1,0:T(8,128)(2,1)}, bf16[128,3584]{1,0:T(8,128)(2,1)}, u32[]{:S(2)}, u32[]{:S(2)}) collective-permute-start(bf16[128,3584]{1,0:T(8,128)(2,1)} %bitcast.107), channel_id=1, source_target_pairs={{0,8},{1,9},{2,10},{3,11},{4,12},{5,13},{6,14},{7,15},{8,0},{9,1},... | collective-permute-start | bytes 2752520 | tf_op jit(solution)/shard_map/ppermute | solution.py:343
  17.9 52.9 %copy-start.33 = (bf16[192,128]{1,0:T(8,128)(2,1)}, bf16[192,128]{1,0:T(8,128)(2,1)S(1)}, u32[]{:S(2)}) copy-start(bf16[192,128]{1,0:T(8,128)(2,1)S(1)} %get-tuple-element.84.placing_ref) | copy-start | bytes 147460
  71.9 6.8 %collective-permute-start.3 = (bf16[4,2,48,3584]{3,2,1,0:T(8,128)(2,1)S(1)}, bf16[4,2,48,3584]{3,2,1,0:T(8,128)(2,1)}, u32[]{:S(2)}, u32[]{:S(2)}) collective-permute-start(bf16[4,2,48,3584]{3,2,1,0:T(8,128)(2,1)S(1)} %bitcast.61), channel_id=1, source_target_pairs={{0,1},{1,0},{2,3},{3,2},{4,5},{5,4},{6,7},{7,6},{8,9},{9,8},{10,11... | collective-permute-start | bytes 8257544 | tf_op jit(solution)/shard_map/ppermute | solution.py:343
  71.9 52.3 %all-to-all-start.1 = ((bf16[4,48,3584]{2,1,0:T(8,128)(2,1)}), bf16[4,48,3584]{2,1,0:T(8,128)(2,1)}, u32[]{:S(2)}, u32[]{:S(2)}) async-start(bf16[4,48,3584]{2,1,0:T(8,128)(2,1)} %bitcast.80), calls=%async_computation.1 | async-start | bytes 2752512 | tf_op jit(solution)/shard_map/all_to_all | solution.py:361
  76.2 48.0 %collective-permute-start.4 = (bf16[192,3584]{1,0:T(8,128)(2,1)}, bf16[192,3584]{1,0:T(8,128)(2,1)}, u32[]{:S(2)}, u32[]{:S(2)}) collective-permute-start(bf16[192,3584]{1,0:T(8,128)(2,1)} %bitcast.88), channel_id=1, source_target_pairs={{0,16},{16,0},{1,17},{17,1},{2,18},{18,2},{3,19},{19,3},{4,20},{20... | collective-permute-start | bytes 4128776 | tf_op jit(solution)/shard_map/ppermute | solution.py:352
  77.8 43.4 %collective-permute-start.2 = (bf16[128,3584]{1,0:T(8,128)(2,1)}, bf16[128,3584]{1,0:T(8,128)(2,1)}, u32[]{:S(2)}, u32[]{:S(2)}) collective-permute-start(bf16[128,3584]{1,0:T(8,128)(2,1)} %bitcast.109), channel_id=1, source_target_pairs={{0,8},{1,9},{2,10},{3,11},{4,12},{5,13},{6,14},{7,15},{8,0},{9,1},... | collective-permute-start | bytes 2752520 | tf_op jit(solution)/shard_map/ppermute | solution.py:343
  94.6 26.6 %copy-start.34 = (bf16[192,128]{1,0:T(8,128)(2,1)S(1)}, bf16[192,128]{1,0:T(8,128)(2,1)}, u32[]{:S(2)}) copy-start(bf16[192,128]{1,0:T(8,128)(2,1)} %copy-done.33) | copy-start | bytes 147460
  94.6 26.6 %copy-start.35 = (f32[192,1]{1,0:T(8,128)S(1)}, f32[192,1]{1,0:T(8,128)}, u32[]{:S(2)}) copy-start(f32[192,1]{1,0:T(8,128)} %copy.57.refs_0_) | copy-start | bytes 2308
  102.8 20.3 %copy-start.20 = (bf16[192,3584]{1,0:T(8,128)(2,1)}, bf16[192,3584]{1,0:T(8,128)(2,1)S(1)}, u32[]{:S(2)}) copy-start(bf16[192,3584]{1,0:T(8,128)(2,1)S(1)} %get-tuple-element.124) | copy-start | bytes 4128772
  124.2 5.1 %collective-permute-start.5 = (bf16[192,3584]{1,0:T(8,128)(2,1)}, bf16[192,3584]{1,0:T(8,128)(2,1)}, u32[]{:S(2)}, u32[]{:S(2)}) collective-permute-start(bf16[192,3584]{1,0:T(8,128)(2,1)} %bitcast.25.a_ref.refs_6_), channel_id=1, source_target_pairs={{0,1},{1,0},{2,3},{3,2},{4,5},{5,4},{6,7},{7,6},{8,9},{9,8},{10,11... | collective-permute-start | bytes 4128776 | tf_op jit(solution)/shard_map/ppermute | solution.py:343
  124.2 19.7 %collective-permute-start.6 = (bf16[192,3584]{1,0:T(8,128)(2,1)}, bf16[192,3584]{1,0:T(8,128)(2,1)}, u32[]{:S(2)}, u32[]{:S(2)}) collective-permute-start(bf16[192,3584]{1,0:T(8,128)(2,1)} %copy-done.41), channel_id=1, source_target_pairs={{0,1},{1,0},{2,3},{3,2},{4,5},{5,4},{6,7},{7,6},{8,9},{9,8},{10,11... | collective-permute-start | bytes 4128776 | tf_op jit(solution)/shard_map/ppermute | solution.py:343
  124.7 24.1 %all-to-all-start.2 = ((bf16[4,48,3584]{2,1,0:T(8,128)(2,1)}), bf16[4,48,3584]{2,1,0:T(8,128)(2,1)}, u32[]{:S(2)}, u32[]{:S(2)}) async-start(bf16[4,48,3584]{2,1,0:T(8,128)(2,1)} %bitcast.79), calls=%async_computation.2 | async-start | bytes 2752512 | tf_op jit(solution)/shard_map/all_to_all | solution.py:361
  129.2 18.5 %collective-permute-start.7 = (bf16[192,3584]{1,0:T(8,128)(2,1)}, bf16[192,3584]{1,0:T(8,128)(2,1)S(1)}, u32[]{:S(2)}, u32[]{:S(2)}) collective-permute-start(bf16[192,3584]{1,0:T(8,128)(2,1)} %collective-permute-done.4.refs_8_), channel_id=1, source_target_pairs={{0,1},{1,0},{2,3},{3,2},{4,5},{5,4},{6,7},{7,6},{8,9},{9,8},{10,11... | collective-permute-start | bytes 4128776 | tf_op jit(solution)/shard_map/ppermute | solution.py:343
  148.8 3.4 %collective-permute-start.8 = (bf16[192,3584]{1,0:T(8,128)(2,1)}, bf16[192,3584]{1,0:T(8,128)(2,1)S(1)}, u32[]{:S(2)}, u32[]{:S(2)}) collective-permute-start(bf16[192,3584]{1,0:T(8,128)(2,1)} %copy-done.43), channel_id=1, source_target_pairs={{0,1},{1,0},{2,3},{3,2},{4,5},{5,4},{6,7},{7,6},{8,9},{9,8},{10,11... | collective-permute-start | bytes 4128776 | tf_op jit(solution)/shard_map/ppermute | solution.py:343
  155.0 4.8 %collective-permute-start.9 = (bf16[192,3584]{1,0:T(8,128)(2,1)}, bf16[192,3584]{1,0:T(8,128)(2,1)}, u32[]{:S(2)}, u32[]{:S(2)}) collective-permute-start(bf16[192,3584]{1,0:T(8,128)(2,1)} %bitcast.27.a_ref.refs_4_), channel_id=1, source_target_pairs={{0,1},{1,0},{2,3},{3,2},{4,5},{5,4},{6,7},{7,6},{8,9},{9,8},{10,11... | collective-permute-start | bytes 4128776 | tf_op jit(solution)/shard_map/ppermute | solution.py:343
  155.4 23.4 %collective-permute-start.10 = (bf16[192,3584]{1,0:T(8,128)(2,1)}, bf16[192,3584]{1,0:T(8,128)(2,1)}, u32[]{:S(2)}, u32[]{:S(2)}) collective-permute-start(bf16[192,3584]{1,0:T(8,128)(2,1)} %get-tuple-element.125), channel_id=1, source_target_pairs={{0,1},{1,0},{2,3},{3,2},{4,5},{5,4},{6,7},{7,6},{8,9},{9,8},{10,11... | collective-permute-start | bytes 4128776 | tf_op jit(solution)/shard_map/ppermute | solution.py:343
  155.5 26.0 %all-to-all-start.3 = ((bf16[4,48,3584]{2,1,0:T(8,128)(2,1)}), bf16[4,48,3584]{2,1,0:T(8,128)(2,1)}, u32[]{:S(2)}, u32[]{:S(2)}) async-start(bf16[4,48,3584]{2,1,0:T(8,128)(2,1)} %bitcast.83), calls=%async_computation.3 | async-start | bytes 2752512 | tf_op jit(solution)/shard_map/all_to_all | solution.py:361
  181.5 4.2 %collective-permute-start.11 = (bf16[192,3584]{1,0:T(8,128)(2,1)}, bf16[192,3584]{1,0:T(8,128)(2,1)S(1)}, u32[]{:S(2)}, u32[]{:S(2)}) collective-permute-start(bf16[192,3584]{1,0:T(8,128)(2,1)} %copy-done.42), channel_id=1, source_target_pairs={{0,1},{1,0},{2,3},{3,2},{4,5},{5,4},{6,7},{7,6},{8,9},{9,8},{10,11... | collective-permute-start | bytes 4128776 | tf_op jit(solution)/shard_map/ppermute | solution.py:343
  189.1 57.0 %all-to-all-start.4 = ((bf16[4,96,3584]{2,1,0:T(8,128)(2,1)}), bf16[4,96,3584]{2,1,0:T(8,128)(2,1)}, u32[]{:S(2)}, u32[]{:S(2)}) async-start(bf16[4,96,3584]{2,1,0:T(8,128)(2,1)} %bitcast.81), calls=%async_computation.4 | async-start | bytes 5505024 | tf_op jit(solution)/shard_map/all_to_all | solution.py:361
  193.7 50.1 %collective-permute-start.15 = (bf16[192,3584]{1,0:T(8,128)(2,1)}, bf16[192,3584]{1,0:T(8,128)(2,1)}, u32[]{:S(2)}, u32[]{:S(2)}) collective-permute-start(bf16[192,3584]{1,0:T(8,128)(2,1)} %bitcast.25.a_ref.refs_6_), channel_id=1, source_target_pairs={{0,16},{16,0},{1,17},{17,1},{2,18},{18,2},{3,19},{19,3},{4,20},{20... | collective-permute-start | bytes 4128776 | tf_op jit(solution)/shard_map/ppermute | solution.py:352
  194.3 49.5 %collective-permute-start.12 = (bf16[128,3584]{1,0:T(8,128)(2,1)}, bf16[128,3584]{1,0:T(8,128)(2,1)}, u32[]{:S(2)}, u32[]{:S(2)}) collective-permute-start(bf16[128,3584]{1,0:T(8,128)(2,1)} %convolution_convert_fusion.1), channel_id=1, source_target_pairs={{0,8},{1,9},{2,10},{3,11},{4,12},{5,13},{6,14},{7,15},{8,0},{9,1},... | collective-permute-start | bytes 2752520 | tf_op jit(solution)/shard_map/ppermute | solution.py:343
  194.4 41.1 %collective-permute-start.13 = (bf16[384,512]{1,0:T(8,128)(2,1)S(1)}, bf16[384,512]{1,0:T(8,128)(2,1)S(1)}, u32[]{:S(2)}, u32[]{:S(2)}) collective-permute-start(bf16[384,512]{1,0:T(8,128)(2,1)S(1)} %dynamic-slice_bitcast_fusion.1), channel_id=1, source_target_pairs={{0,16},{16,0},{1,17},{17,1},{2,18},{18,2},{3,19},{19,3},{4,20},{20... | collective-permute-start | bytes 1179656 | tf_op jit(solution)/shard_map/ppermute | solution.py:352
  196.9 46.1 %collective-permute-start.14 = (bf16[384,512]{1,0:T(8,128)(2,1)S(1)}, bf16[384,512]{1,0:T(8,128)(2,1)S(1)}, u32[]{:S(2)}, u32[]{:S(2)}) collective-permute-start(bf16[384,512]{1,0:T(8,128)(2,1)S(1)} %dynamic-slice_bitcast_fusion), channel_id=1, source_target_pairs={{0,16},{16,0},{1,17},{17,1},{2,18},{18,2},{3,19},{19,3},{4,20},{20... | collective-permute-start | bytes 1179656 | tf_op jit(solution)/shard_map/ppermute | solution.py:352
  212.0 39.3 %copy-start.46 = (f32[1,128,2]{1,2,0:T(2,128)S(1)}, f32[1,128,2]{1,2,0:T(2,128)}, u32[]{:S(2)}) copy-start(f32[1,128,2]{1,2,0:T(2,128)} %param.10) | copy-start | bytes 3076
  246.2 41.8 %collective-permute-start.17 = (bf16[256,3584]{1,0:T(8,128)(2,1)}, bf16[256,3584]{1,0:T(8,128)(2,1)}, u32[]{:S(2)}, u32[]{:S(2)}) collective-permute-start(bf16[256,3584]{1,0:T(8,128)(2,1)} %copy-done.13), channel_id=1, source_target_pairs={{0,16},{16,0},{1,17},{17,1},{2,18},{18,2},{3,19},{19,3},{4,20},{20... | collective-permute-start | bytes 5505032 | tf_op jit(solution)/shard_map/ppermute | solution.py:352
  246.7 12.8 %collective-permute-start.18 = (bf16[192,3584]{1,0:T(8,128)(2,1)}, bf16[192,3584]{1,0:T(8,128)(2,1)}, u32[]{:S(2)}, u32[]{:S(2)}) collective-permute-start(bf16[192,3584]{1,0:T(8,128)(2,1)} %collective-permute-done.15.refs_10_), channel_id=1, source_target_pairs={{0,1},{1,0},{2,3},{3,2},{4,5},{5,4},{6,7},{7,6},{8,9},{9,8},{10,11... | collective-permute-start | bytes 4128776 | tf_op jit(solution)/shard_map/ppermute | solution.py:343
  246.7 44.5 %all-to-all-start.5 = ((bf16[4,48,3584]{2,1,0:T(8,128)(2,1)}), bf16[4,48,3584]{2,1,0:T(8,128)(2,1)}, u32[]{:S(2)}, u32[]{:S(2)}) async-start(bf16[4,48,3584]{2,1,0:T(8,128)(2,1)} %bitcast.82), calls=%async_computation.5 | async-start | bytes 2752512 | tf_op jit(solution)/shard_map/all_to_all | solution.py:361
  258.6 29.4 %copy-start.10 = (bf16[256,3584]{1,0:T(8,128)(2,1)S(1)}, bf16[256,3584]{1,0:T(8,128)(2,1)}, u32[]{:S(2)}) copy-start(bf16[256,3584]{1,0:T(8,128)(2,1)} %copy-done.9) | copy-start | bytes 5505028
  258.6 43.7 %collective-permute-start.16 = (bf16[128,3584]{1,0:T(8,128)(2,1)}, bf16[128,3584]{1,0:T(8,128)(2,1)}, u32[]{:S(2)}, u32[]{:S(2)}) collective-permute-start(bf16[128,3584]{1,0:T(8,128)(2,1)} %convolution_convert_fusion), channel_id=1, source_target_pairs={{0,8},{1,9},{2,10},{3,11},{4,12},{5,13},{6,14},{7,15},{8,0},{9,1},... | collective-permute-start | bytes 2752520 | tf_op jit(solution)/shard_map/ppermute | solution.py:343
  270.8 20.4 %copy-start.45 = (f32[128,192]{0,1:T(8,128)S(1)}, f32[128,192]{0,1:T(8,128)}, u32[]{:S(2)}) copy-start(f32[128,192]{0,1:T(8,128)} %get-tuple-element.158) | copy-start | bytes 294916
  (40 other events, 113.7 us)

commit v13 on v10

--- a/solution.py
+++ b/solution.py
@@ -140,108 +140,102 @@
     return value.reshape(-1, value.shape[-1])
 
 
-def forward(count, rows, gate_weight, up_weight, down_weight):
-    width = gate_weight.shape[0]
-    half_units = gate_weight.shape[1] // 2
-
-    def body(a_ref, b_ref, gate_ref, up_ref, down_ref, pre_gate_ref, pre_up_ref, hidden_ref, out_a, out_b, x_ref, acc_ref):
+def weight_specs(width, half_units):
+    mine, other = (lambda n: jnp.minimum(n, 1)), (lambda n: jnp.maximum(n - 2, 0))
+    specs = []
+    for at in (mine, other):
+        columns = pl.BlockSpec((width, half_units), lambda n, at=at: (0, at(n)))
+        specs += [columns, columns, pl.BlockSpec((half_units, width), lambda n, at=at: (at(n), 0))]
+    return specs
+
+
+def forward(count, rows, weights):
+    width = weights[0].shape[0]
+    half_units = weights[0].shape[1] // 2
+
+    def body(x_ref, *refs):
+        pre_gate_ref, pre_up_ref, hidden_ref, out_ref, acc_ref = refs[6:]
         step = pl.program_id(0)
 
-        @pl.when(step == 0)
+        def quarter(gate_ref, up_ref, down_ref):
+            x = flat(x_ref)
+            pre_gate = dot(x, gate_ref[...], NN)
+            pre_up = dot(x, up_ref[...], NN)
+            pre_gate_ref[0] = pre_gate
+            pre_up_ref[0] = pre_up
+            hidden = (pre_gate * jax.nn.sigmoid(pre_gate) * pre_up).astype(BF16)
+            hidden_ref[0] = hidden
+            for cut in chunks(width):
+                term = dot(hidden, down_ref[:, cut], NN)
+                acc_ref[:, cut] = jnp.where(step == 0, term, acc_ref[:, cut] + term)
+
+        pl.when(step < 2)(lambda: quarter(*refs[:3]))
+        pl.when(step >= 2)(lambda: quarter(*refs[3:6]))
+
+        @pl.when(step == 3)
         def _():
-            x_ref[:count] = flat(a_ref)
-            x_ref[count:] = flat(b_ref)
-
-        pre_gate = dot(x_ref[...], gate_ref[...], NN)
-        pre_up = dot(x_ref[...], up_ref[...], NN)
-        pre_gate_ref[0] = pre_gate
-        pre_up_ref[0] = pre_up
-        hidden = (pre_gate * jax.nn.sigmoid(pre_gate) * pre_up).astype(BF16)
-        hidden_ref[0] = hidden
-
-        @pl.when(step == 0)
-        def _():
-            for cut in chunks(width):
-                acc_ref[:, cut] = dot(hidden, down_ref[:, cut], NN)
-
-        @pl.when(step == 1)
-        def _():
-            for cut in chunks(width):
-                total = (acc_ref[:, cut] + dot(hidden, down_ref[:, cut], NN)).astype(BF16)
-                out_a[:, cut] = total[:count]
-                out_b[:, cut] = total[count:]
-
-    whole = pl.BlockSpec((count, width), lambda n: (0, 0))
-    columns = pl.BlockSpec((width, half_units), lambda n: (0, n))
-    units = pl.BlockSpec((1, 2 * count, half_units), lambda n: (n, 0, 0))
-    return kernel_call(
-        body,
-        (2,),
-        [row_spec(a, width) for a in rows]
-        + [columns, columns, pl.BlockSpec((half_units, width), lambda n: (n, 0))],
-        [units, units, units, whole, whole],
+            out_ref[...] = acc_ref[...].astype(BF16)
+
+    units = pl.BlockSpec((1, count, half_units), lambda n: (n, 0, 0))
+    return kernel_call(
+        body,
+        (4,),
+        [row_spec(rows, width)] + weight_specs(width, half_units),
+        [units, units, units, pl.BlockSpec((count, width), lambda n: (0, 0))],
         [
-            jax.ShapeDtypeStruct((2, 2 * count, half_units), F32),
-            jax.ShapeDtypeStruct((2, 2 * count, half_units), F32),
-            jax.ShapeDtypeStruct((2, 2 * count, half_units), BF16),
-            jax.ShapeDtypeStruct((count, width), BF16),
+            jax.ShapeDtypeStruct((4, count, half_units), F32),
+            jax.ShapeDtypeStruct((4, count, half_units), F32),
+            jax.ShapeDtypeStruct((4, count, half_units), BF16),
             jax.ShapeDtypeStruct((count, width), BF16),
         ],
-        [pltpu.VMEM((2 * count, width), BF16), pltpu.VMEM((2 * count, width), F32)],
-    )(*map(row_array, rows), gate_weight, up_weight, down_weight)
-
-
-def backward(count, rows_grad, pre_gate, pre_up, gate_weight, up_weight, down_weight):
-    width = gate_weight.shape[0]
-    half_units = gate_weight.shape[1] // 2
-
-    def body(a_ref, b_ref, pre_gate_ref, pre_up_ref, gate_ref, up_ref, down_ref, units_ref, out_a, out_b, x_ref, acc_ref):
+        [pltpu.VMEM((count, width), F32)],
+    )(row_array(rows), *weights)
+
+
+def backward(count, rows_grad, pre_gate, pre_up, weights):
+    width = weights[0].shape[0]
+    half_units = weights[0].shape[1] // 2
+
+    def body(x_ref, pre_gate_ref, pre_up_ref, *refs):
+        units_ref, out_ref, acc_ref = refs[6:]
         step = pl.program_id(0)
 
-        @pl.when(step == 0)
+        def quarter(gate_ref, up_ref, down_ref):
+            hidden_grad = dot(flat(x_ref), down_ref[...], NT)
+            pre_gate = pre_gate_ref[0]
+            sigma = jax.nn.sigmoid(pre_gate)
+            gate_grad = (
+                hidden_grad * pre_up_ref[0] * sigma * (1.0 + pre_gate * (1.0 - sigma))
+            ).astype(BF16)
+            up_grad = (hidden_grad * (pre_gate * sigma)).astype(BF16)
+            units_ref[0, :, :half_units] = gate_grad
+            units_ref[0, :, half_units:] = up_grad
+            for cut in chunks(width):
+                term = dot(gate_grad, gate_ref[cut], NT) + dot(up_grad, up_ref[cut], NT)
+                acc_ref[:, cut] = jnp.where(step == 0, term, acc_ref[:, cut] + term)
+
+        pl.when(step < 2)(lambda: quarter(*refs[:3]))
+        pl.when(step >= 2)(lambda: quarter(*refs[3:6]))
+
+        @pl.when(step == 3)
         def _():
-            x_ref[:count] = flat(a_ref)
-            x_ref[count:] = flat(b_ref)
-
-        hidden_grad = dot(x_ref[...], down_ref[...], NT)
-        pre_gate = pre_gate_ref[0]
-        sigma = jax.nn.sigmoid(pre_gate)
-        gate_grad = (
-            hidden_grad * pre_up_ref[0] * sigma * (1.0 + pre_gate * (1.0 - sigma))
-        ).astype(BF16)
-        up_grad = (hidden_grad * (pre_gate * sigma)).astype(BF16)
-        units_ref[0, :, :half_units] = gate_grad
-        units_ref[0, :, half_units:] = up_grad
-
-        @pl.when(step == 0)
-        def _():
-            for cut in chunks(width):
-                acc_ref[:, cut] = dot(gate_grad, gate_ref[cut], NT) + dot(up_grad, up_ref[cut], NT)
-
-        @pl.when(step == 1)
-        def _():
-            for cut in chunks(width):
-                total = acc_ref[:, cut] + dot(gate_grad, gate_ref[cut], NT)
-                total = (total + dot(up_grad, up_ref[cut], NT)).astype(BF16)
-                out_a[:, cut] = total[:count]
-                out_b[:, cut] = total[count:]
-
-    whole = pl.BlockSpec((count, width), lambda n: (0, 0))
-    columns = pl.BlockSpec((width, half_units), lambda n: (0, n))
-    units = pl.BlockSpec((1, 2 * count, half_units), lambda n: (n, 0, 0))
-    return kernel_call(
-        body,
-        (2,),
-        [row_spec(a, width) for a in rows_grad]
-        + [units, units, columns, columns, pl.BlockSpec((half_units, width), lambda n: (n, 0))],
-        [pl.BlockSpec((1, 2 * count, 2 * half_units), lambda n: (n, 0, 0)), whole, whole],
+            out_ref[...] = acc_ref[...].astype(BF16)
+
+    units = pl.BlockSpec((1, count, half_units), lambda n: (n, 0, 0))
+    return kernel_call(
+        body,
+        (4,),
+        [row_spec(rows_grad, width), units, units] + weight_specs(width, half_units),
         [
-            jax.ShapeDtypeStruct((2, 2 * count, 2 * half_units), BF16),
-            jax.ShapeDtypeStruct((count, width), BF16),
+            pl.BlockSpec((1, count, 2 * half_units), lambda n: (n, 0, 0)),
+            pl.BlockSpec((count, width), lambda n: (0, 0)),
+        ],
+        [
+            jax.ShapeDtypeStruct((4, count, 2 * half_units), BF16),
             jax.ShapeDtypeStruct((count, width), BF16),
         ],
-        [pltpu.VMEM((2 * count, width), BF16), pltpu.VMEM((2 * count, width), F32)],
-    )(*map(row_array, rows_grad), pre_gate, pre_up, gate_weight, up_weight, down_weight)
+        [pltpu.VMEM((count, width), F32)],
+    )(row_array(rows_grad), pre_gate, pre_up, *weights)
 
 
 def down_grad(count, which, hiddens, rows_grad):
@@ -250,13 +244,13 @@
     tile = tile_of(width)
 
     def body(which_ref, *refs):
-        unit_refs, row_refs, rest = refs[:2], refs[2:6], refs[6:]
+        unit_refs, row_refs, rest = refs[:4], refs[4:8], refs[8:]
         turned_ref = rest[-1]
 
         @pl.when(pl.program_id(0) == 0)
         def _():
             for n, unit_ref in enumerate(unit_refs):
-                turned_ref[:, 2 * n * count : 2 * (n + 1) * count] = unit_ref[0].T
+                turned_ref[:, n * count : (n + 1) * count] = unit_ref[0].T
 
         rows = jnp.concatenate([flat(ref) for ref in row_refs], axis=0)
         total = dot(turned_ref[...], rows, NN)
@@ -266,7 +260,7 @@
     return kernel_call(
         body,
         (width // tile,),
-        [pl.BlockSpec((1, 2 * count, half_units), lambda n, w: (w[0], 0, 0))] * 2
+        [pl.BlockSpec((1, count, half_units), lambda n, w: (w[0], 0, 0))] * 4
         + [row_spec(a, tile) for a in rows_grad],
         out_spec,
         jax.ShapeDtypeStruct((half_units, width), BF16),
@@ -282,13 +276,13 @@
     tile = tile_of(width)
 
     def body(which_ref, *refs):
-        unit_refs, mirror_refs, row_refs = refs[:2], refs[2:4], refs[4:12]
-        gate_ref, up_ref, turned_ref = refs[12:]
+        unit_refs, mirror_refs, row_refs = refs[:4], refs[4:8], refs[8:16]
+        gate_ref, up_ref, turned_ref = refs[16:]
 
         @pl.when(pl.program_id(0) == 0)
         def _():
             for n, factor in enumerate([ref[0] for ref in unit_refs] + [ref[...] for ref in mirror_refs]):
-                turned_ref[:, 2 * n * count : 2 * (n + 1) * count] = factor.T
+                turned_ref[:, n * count : (n + 1) * count] = factor.T
 
         rows = jnp.concatenate([flat(ref) for ref in row_refs], axis=0)
         total = dot(turned_ref[...], rows, NN).astype(BF16).T
@@ -299,8 +293,8 @@
     return kernel_call(
         body,
         (width // tile,),
-        [pl.BlockSpec((1, 2 * count, both), lambda n, w: (w[0], 0, 0))] * 2
-        + [pl.BlockSpec((2 * count, both), lambda n, w: (0, 0))] * 2
+        [pl.BlockSpec((1, count, both), lambda n, w: (w[0], 0, 0))] * 4
+        + [pl.BlockSpec((count, both), lambda n, w: (0, 0))] * 4
         + [row_spec(a, tile) for a in (*rows, *mirror_rows)],
         [out_spec] * 2,
         [jax.ShapeDtypeStruct((width, half_units), BF16)] * 2,
@@ -370,8 +364,8 @@
     def tie(*arrays):
         return lax.optimization_barrier(arrays)
 
-    def expert_sum(mine, other):
-        return (mine.astype(F32) + swap(other).astype(F32)).astype(BF16)
+    def for_mirror(units):
+        return lax.dynamic_index_in_dim(units, 1 - kept_half, 0, keepdims=False)
 
     def of_set(matrix, which):
         shaped = matrix.reshape(matrix.shape[0], near, 1, piece)
@@ -391,88 +385,73 @@
     own, far_acts_0, acts_1, meta = tie(own, far_acts_0, acts[0, first:], meta)
 
     far_acts_1 = far(acts_1)
-    own = near_exchange(own)
+    own = near_exchange(own).reshape(near, 2, piece, width)
+    own_in = own[:, 0].reshape(count, width)
     far_meta = far(meta)
+    other = [swap(weight) for weight in weights]
     far_placing, far_back, far_weighting, far_gain = route(far_meta, half, chips, capacity)
     far_in = place_far(far_placing, [far_acts_0, far_acts_1])
-    far_in, own, far_placing, far_gain, grads = tie(far_in, own, far_placing, far_gain, grad_out[0])
+    far_in, own, own_in, far_placing, far_gain, grads, *weights = tie(
+        far_in, own, own_in, far_placing, far_gain, grad_out[0], *weights, *other
+    )
 
     far_grads = far(grads)
     far_in = near_exchange(far_in)
     own_b = swap(own)
-    own = own.reshape(near, 2, piece, width)
-    own_b = own_b.reshape(near, 2, piece, width)
-    mirror_own = mirror(own[:, 0].reshape(count, width))
-    own_pre_gate, own_pre_up, own_hidden, own_out, own_out_b = forward(
-        count, ((own, 0), (own_b, 0)), *weights
-    )
-    own_units, own_input, own_input_b = backward(
-        count, ((own, 1), (own_b, 1)), own_pre_gate, own_pre_up, *weights
-    )
-    far_grads, own_out, own_out_b, own_input, own_input_b = tie(
-        far_grads, own_out, own_out_b, own_input, own_input_b
-    )
+    mirror_own = mirror(own_in)
+    own_pre_gate, own_pre_up, own_hidden, own_out = forward(count, (own, 0), weights)
+    own_units, own_input = backward(count, (own, 1), own_pre_gate, own_pre_up, weights)
+    far_grads, own_out, own_input = tie(far_grads, own_out, own_input)
     far_grad = place_far(far_placing, [far_grads], far_gain)
-    far_grad, far_in, mirror_own, own_out, own_out_b, own_input, own_input_b = tie(
-        far_grad, far_in, mirror_own, own_out, own_out_b, own_input, own_input_b
+    far_grad, far_in, own_b, mirror_own, own_out, own_input, own_hidden, own_units = tie(
+        far_grad, far_in, own_b, mirror_own, own_out, own_input, own_hidden, own_units
     )
 
     far_grad = near_exchange(far_grad)
     far_in_b = swap(far_in)
     mirror_own_b = swap(mirror_own)
-    own_out = expert_sum(own_out, own_out_b)
-    far_pre_gate, far_pre_up, far_hidden, far_out, far_out_b = forward(
-        count, (far_in, far_in_b), *weights
-    )
-    far_grad, far_out, far_out_b, own_out, mirror_own_b = tie(
-        far_grad, far_out, far_out_b, own_out, mirror_own_b
-    )
-
-    far_out = expert_sum(far_out, far_out_b)
-    far_out, far_grad, own_input, own_input_b = tie(far_out, far_grad, own_input, own_input_b)
+    own_hidden_b = swap(own_hidden[2:])
+    own_units_b = swap(own_units[2:])
+    far_pre_gate, far_pre_up, far_hidden, far_out = forward(count, far_in, weights)
+    far_grad, far_out, far_in_b, mirror_own_b, own_hidden_b, own_units_b, far_hidden = tie(
+        far_grad, far_out, far_in_b, mirror_own_b, own_hidden_b, own_units_b, far_hidden
+    )
 
     far_out = near_exchange(far_out)
     far_grad_b = swap(far_grad)
-    own_input = expert_sum(own_input, own_input_b)
-    far_units, far_input, far_input_b = backward(
-        count, (far_grad, far_grad_b), far_pre_gate, far_pre_up, *weights
-    )
-    far_out, far_units, far_input, far_input_b, own_input = tie(
-        far_out, far_units, far_input, far_input_b, own_input
-    )
-
-    far_input = expert_sum(far_input, far_input_b)
-    back_out = combine(far_weighting, far_out).astype(BF16)
-    far_input, back_out, own_units, far_units, far_grad_b, mirror_far = tie(
-        far_input, back_out, own_units, far_units, far_grad_b, far_in
-    )
-
-    got_out = far(back_out)
+    far_hidden_b = swap(far_hidden[2:])
+    mirror_units = [mirror(for_mirror(units)) for units in (own_units, own_units_b)]
+    far_units, far_input = backward(count, far_grad, far_pre_gate, far_pre_up, weights)
+    far_out, far_units, far_input, far_grad_b, far_hidden_b, mirror_far, *mirror_units = tie(
+        far_out, far_units, far_input, far_grad_b, far_hidden_b, far_in, *mirror_units
+    )
+
+    got_out = far(combine(far_weighting, far_out).astype(BF16))
     back = near_exchange(
         jnp.stack([a.reshape(near, piece, width) for a in (far_input, own_input)], axis=1).reshape(2 * count, width)
     )
-    mirror_units = [
-        mirror(lax.dynamic_index_in_dim(units, 1 - kept_half, 0, keepdims=False))
-        for units in (own_units, far_units)
-    ]
     mirror_far = mirror(mirror_far)
-    rows_grad = ((own, 1), (own_b, 1), far_grad, far_grad_b)
-    send_down = down_grad(count, 1 - kept, (own_hidden, far_hidden), rows_grad)
-    keep_down = down_grad(count, kept, (own_hidden, far_hidden), rows_grad)
-    got_out, back, mirror_own_units, mirror_far_units, mirror_far, send_down, keep_down, own_out = tie(
-        got_out, back, *mirror_units, mirror_far, send_down, keep_down, own_out
+    mirror_units.append(mirror(for_mirror(far_units)))
+    far_units_b = swap(far_units[2:])
+    hiddens = (own_hidden, own_hidden_b, far_hidden, far_hidden_b)
+    rows_grad = ((own, 1), (own_b.reshape(own.shape), 1), far_grad, far_grad_b)
+    send_down = down_grad(count, 1 - kept, hiddens, rows_grad)
+    keep_down = down_grad(count, kept, hiddens, rows_grad)
+    got_out, back, mirror_far, far_units_b, send_down, keep_down, own_out, *mirror_units = tie(
+        got_out, back, mirror_far, far_units_b, send_down, keep_down, own_out, *mirror_units
     )
 
     got_input = far(combine(of_set(far_back, 0), back).astype(BF16))
     own_out = near_exchange(own_out)
+    mirror_units.append(mirror(for_mirror(far_units_b)))
     got_down = mirror(send_down)
     mirror_far_b = swap(mirror_far)
     grad_gate, grad_up = gate_up_grad(
         count,
         kept,
-        (own_units, far_units),
-        ((own, 0), (own_b, 0), far_in, far_in_b),
-        (mirror_own_units, mirror_far_units),
+        (own_units, own_units_b, far_units, far_units_b),
+        ((own, 0), (own_b.reshape(own.shape), 0), far_in, far_in_b),
+        mirror_units,
         (mirror_own, mirror_own_b, mirror_far, mirror_far_b),
     )
     out_acts = (combine(own_weighting, own_out) + got_out.astype(F32)).astype(BF16)

time: 289 us -> 300 us (1.038)
  Pallas kernels: 79.3 us -> 98.4 us
  waiting for transfers between devices: 112 us -> 102 us
  other arithmetic: 21.6 us -> 15.7 us
  local copies, waits for them, and re-layouts: 18.4 us -> 23 us
  starting transfers between devices: 45 us -> 49.1 us
    pallas_call x7, Pallas kernels: 70.9 us -> 90.1 us  [the longest x2 34.6 us: backward(): kernel_call(body, (4,), [row_spec(rows_grad, width), units, units] + weig...]
    all_to_all x6, waiting for transfers between devices: 8 us -> 1.3 us  [near_exchange(): lax.all_to_all(rows.reshape(near, -1, width), 'expert', split_axis=0, con...]
    convert_element_type x4 -> x0, other arithmetic: 6.46 us -> none  [expert_sum(): return (mine.astype(F32) + swap(other).astype(F32)).astype(BF16)]
    unnamed x54 -> x70, local copies, waits for them, and re-layouts: 4.11 us -> 7.66 us
    ppermute x5 -> x7, starting transfers between devices: 4.78 us -> 7.82 us  [mirror(): lax.ppermute(rows, 'pipe', [(p, rank_count - 1 - p) for p in range(rank_c...]
    ppermute x15 -> x18, waiting for transfers between devices: 54.5 us -> 52.9 us  [hop(): lax.ppermute(rows, 'expert', [(i, i ^ distance) for i in range(devices)])]
    ppermute x5 -> x7, waiting for transfers between devices: 49.1 us -> 47.8 us  [mirror(): lax.ppermute(rows, 'pipe', [(p, rank_count - 1 - p) for p in range(rank_c...]
    ppermute x15 -> x18, starting transfers between devices: 14.1 us -> 13.7 us  [hop(): lax.ppermute(rows, 'expert', [(i, i ^ distance) for i in range(devices)])]
  transfers between devices with their start and end apart: 26 -> 31, of which waited for: 13 -> 7; matrix products, arithmetic and copies ran while one was open for 14% -> 12% of each run, Pallas kernels for 26% -> 32%
where the time goes in v13:
time: 300 us; the launch traced here: 298 us
  waiting for transfers between devices  102 us (34%)
  Pallas kernels  98.4 us (33%)
  starting transfers between devices  49.1 us (16%)
  local copies, waits for them, and re-layouts  23 us (8%)
  other arithmetic  15.7 us (5%)
  matrix products  8.76 us (3%)
    ppermute x18, waiting for transfers between devices, hop(): lax.ppermute(rows, 'expert', [(i, i ^ distance) for i in range(devices)])  52.9 us
    ppermute x7, waiting for transfers between devices, mirror(): lax.ppermute(rows, 'pipe', [(p, rank_count - 1 - p) for p in range(rank_c...  47.8 us
    pallas_call x2, Pallas kernels, backward(): kernel_call(body, (4,), [row_spec(rows_grad, width), units, units] + weig...  34.6 us
    all_to_all x6, starting transfers between devices, near_exchange(): lax.all_to_all(rows.reshape(near, -1, width), 'expert', split_axis=0, con...  27.5 us
    pallas_call x2, Pallas kernels, forward(): kernel_call(body, (4,), [row_spec(rows, width)] + weight_specs(width, hal...  27.5 us
    pallas_call x2, Pallas kernels, down_grad(): kernel_call(body, (width // tile,), [pl.BlockSpec((1, count, half_units),...  15.4 us
    ppermute x18, starting transfers between devices, hop(): lax.ppermute(rows, 'expert', [(i, i ^ distance) for i in range(devices)])  13.7 us
    pallas_call x1, Pallas kernels, gate_up_grad(): kernel_call(body, (width // tile,), [pl.BlockSpec((1, count, both), lambd...  12.5 us
  transfers between devices with their start and end apart: 31, of which 7 were waited for; matrix products, arithmetic and copies ran while one was open for 12% of the time, Pallas kernels for 32%

profile of v13, /device:TPU:0, one launch (start us, length us, event | category | flops | bytes accessed | tf_op | source)
XLA Modules:
  0.0 298.0 jit_solution(17775385032782741420)
XLA Ops:
  1.7 4.0 %collective-permute-start = (bf16[16,3584]{1,0:T(8,128)(2,1)S(1)}, bf16[16,3584]{1,0:T(8,128)(2,1)S(1)}, u32[]{:S(2)}, u32[]{:S(2)}) collective-permute-start(bf16[16,3584]{1,0:T(8,128)(2,1)S(1)} %slice_bitcast_fusion.1), channel_id=1, source_target_pairs={{0,8},{1,9},{2,10},{3,11},{4,12},{5,13},{6,14},{7,15},{8,0},{9,1},... | collective-permute-start | bytes 344072 | tf_op jit(solution)/shard_map/ppermute | solution.py:337
  8.9 2.5 fusion
  12.7 3.8 %all-to-all-start = ((bf16[4,96,3584]{2,1,0:T(8,128)(2,1)}), bf16[4,96,3584]{2,1,0:T(8,128)(2,1)S(1)}, u32[]{:S(2)}, u32[]{:S(2)}) async-start(bf16[4,96,3584]{2,1,0:T(8,128)(2,1)} %bitcast.100), calls=%async_computation | async-start | bytes 5505024 | tf_op jit(solution)/shard_map/all_to_all | solution.py:355
  17.0 1.8 collective-permute-start.1
  19.9 27.5 %collective-permute-done.1 = f32[128,4]{0,1:T(4,128)S(1)} collective-permute-done((f32[128,4]{0,1:T(4,128)}, f32[128,4]{0,1:T(4,128)S(1)}, u32[]{:S(2)}, u32[]{:S(2)}) %collective-permute-start.1) | collective-permute-done | bytes 2080 | tf_op jit(solution)/shard_map/ppermute | solution.py:337
  61.5 1.8 collective-permute-done.2.refs_1_
  63.3 2.6 shard_map.110
  67.9 6.7 %all-to-all-start.1 = ((bf16[4,48,3584]{2,1,0:T(8,128)(2,1)}), bf16[4,48,3584]{2,1,0:T(8,128)(2,1)}, u32[]{:S(2)}, u32[]{:S(2)}) async-start(bf16[4,48,3584]{2,1,0:T(8,128)(2,1)} %bitcast.99), calls=%async_computation.1 | async-start | bytes 2752512 | tf_op jit(solution)/shard_map/all_to_all | solution.py:355
  77.2 13.3 %shard_map.111 = (f32[4,192,256]{2,1,0:T(8,128)}, f32[4,192,256]{2,1,0:T(8,128)}, bf16[4,192,256]{2,1,0:T(8,128)(2,1)}, bf16[192,3584]{1,0:T(8,128)(2,1)}) custom-call(bf16[4,2,48,3584]{3,2,1,0:T(8,128)(2,1)} %bitcast.70, bf16[3584,512]{1,0:T(8,128)(2,1)} %bitcast.76, bf16[3584,512]{1,0:T(8,128)(2,1)} %bitcast.81, bf16[512,3584]{1,0:T(8,128)(2,1)} %bitcast.86, ...), custom_call_target="tpu_custom_call" | custom-call | flops 1 | bytes 1 | tf_op jit(solution)/shard_map/pallas_call | solution.py:180
  90.5 17.0 %shard_map.112 = (bf16[4,192,512]{2,1,0:T(8,128)(2,1)}, bf16[192,3584]{1,0:T(8,128)(2,1)}) custom-call(bf16[4,2,48,3584]{3,2,1,0:T(8,128)(2,1)} %bitcast.71, f32[4,192,256]{2,1,0:T(8,128)} %get-tuple-element.91.pre_gate_ref, f32[4,192,256]{2,1,0:T(8,128)} %get-tuple-element.92.pre_up_ref, bf16[3584,512]{1,0:T(8,128)(2,1)} %bitcast.77, ...), custom_call_target="tpu_custom_call" | custom-call | flops 1 | bytes 1 | tf_op jit(solution)/shard_map/pallas_call | solution.py:225
  108.3 10.2 %collective-permute-done.6.refs_1_ = bf16[128,3584]{1,0:T(8,128)(2,1)} collective-permute-done((bf16[128,3584]{1,0:T(8,128)(2,1)}, bf16[128,3584]{1,0:T(8,128)(2,1)}, u32[]{:S(2)}, u32[]{:S(2)}) %collective-permute-start.6) | collective-permute-done | bytes 917536 | tf_op jit(solution)/shard_map/ppermute | solution.py:337
  118.5 2.6 shard_map.113
  121.1 3.9 %all-to-all-start.2 = ((bf16[4,48,3584]{2,1,0:T(8,128)(2,1)}), bf16[4,48,3584]{2,1,0:T(8,128)(2,1)S(1)}, u32[]{:S(2)}, u32[]{:S(2)}) async-start(bf16[4,48,3584]{2,1,0:T(8,128)(2,1)} %bitcast.98), calls=%async_computation.2 | async-start | bytes 2752512 | tf_op jit(solution)/shard_map/all_to_all | solution.py:355
  126.3 14.2 %shard_map.114 = (f32[4,192,256]{2,1,0:T(8,128)}, f32[4,192,256]{2,1,0:T(8,128)}, bf16[4,192,256]{2,1,0:T(8,128)(2,1)}, bf16[192,3584]{1,0:T(8,128)(2,1)}) custom-call(bf16[192,3584]{1,0:T(8,128)(2,1)} %bitcast.27.x_ref.refs_10_, bf16[3584,512]{1,0:T(8,128)(2,1)} %bitcast.78, bf16[3584,512]{1,0:T(8,128)(2,1)} %bitcast.83, bf16[512,3584]{1,0:T(8,128)(2,1)} %bitcast.88, ...), custom_call_target="tpu_custom_call" | custom-call | flops 1 | bytes 1 | tf_op jit(solution)/shard_map/pallas_call | solution.py:180
  141.7 3.9 %all-to-all-start.3 = ((bf16[4,48,3584]{2,1,0:T(8,128)(2,1)}), bf16[4,48,3584]{2,1,0:T(8,128)(2,1)S(1)}, u32[]{:S(2)}, u32[]{:S(2)}) async-start(bf16[4,48,3584]{2,1,0:T(8,128)(2,1)} %bitcast.104), calls=%async_computation.3 | async-start | bytes 2752512 | tf_op jit(solution)/shard_map/all_to_all | solution.py:355
  148.9 17.6 %shard_map.115 = (bf16[4,192,512]{2,1,0:T(8,128)(2,1)}, bf16[192,3584]{1,0:T(8,128)(2,1)}) custom-call(bf16[192,3584]{1,0:T(8,128)(2,1)} %bitcast.93, f32[4,192,256]{2,1,0:T(8,128)} %get-tuple-element.110.pre_gate_ref, f32[4,192,256]{2,1,0:T(8,128)} %get-tuple-element.111.pre_up_ref, bf16[3584,512]{1,0:T(8,128)(2,1)} %bitcast.79, ...), custom_call_target="tpu_custom_call" | custom-call | flops 1 | bytes 1 | tf_op jit(solution)/shard_map/pallas_call | solution.py:225
  169.0 2.0 pad_maximum_fusion
  171.0 1.7 copy.57
  172.8 4.3 %all-to-all-start.4 = ((bf16[4,96,3584]{2,1,0:T(8,128)(2,1)}), bf16[4,96,3584]{2,1,0:T(8,128)(2,1)S(1)}, u32[]{:S(2)}, u32[]{:S(2)}) async-start(bf16[4,96,3584]{2,1,0:T(8,128)(2,1)} %bitcast.96), calls=%async_computation.4 | async-start | bytes 5505024 | tf_op jit(solution)/shard_map/all_to_all | solution.py:355
  178.3 2.3 convolution_convert_fusion.1
  180.5 1.8 collective-permute-start.17
  184.1 7.7 %shard_map.117 = bf16[256,3584]{1,0:T(8,128)(2,1)} custom-call(s32[1]{0:T(128)} %bitcast.38.which_ref, bf16[4,192,256]{2,1,0:T(8,128)(2,1)} %get-tuple-element.105.refs_0_, bf16[2,192,256]{2,1,0:T(8,128)(2,1)} %copy-done.16, bf16[4,192,256]{2,1,0:T(8,128)(2,1)} %get-tuple-element.114.refs_2_, bf16[2,192,256]{2,1,0:T(8,128)(2,1)} %copy-done.17, ...), custom_call_target="tpu_custom_call" | custom-call | flops 1 | bytes 1 | tf_op jit(solution)/shard_map/pallas_call | solution.py:260
  191.8 7.7 %shard_map.116 = bf16[256,3584]{1,0:T(8,128)(2,1)} custom-call(s32[1]{0:T(128)S(6)} %sub.39.which_ref, bf16[4,192,256]{2,1,0:T(8,128)(2,1)} %get-tuple-element.105.refs_0_, bf16[2,192,256]{2,1,0:T(8,128)(2,1)} %copy-done.16, bf16[4,192,256]{2,1,0:T(8,128)(2,1)} %get-tuple-element.114.refs_2_, bf16[2,192,256]{2,1,0:T(8,128)(2,1)} %copy-done.17, ...), custom_call_target="tpu_custom_call" | custom-call | flops 1 | bytes 1 | tf_op jit(solution)/shard_map/pallas_call | solution.py:260
  199.5 14.3 %collective-permute-done.20.refs_6_ = bf16[192,512]{1,0:T(8,128)(2,1)S(1)} collective-permute-done((bf16[192,512]{1,0:T(8,128)(2,1)S(1)}, bf16[192,512]{1,0:T(8,128)(2,1)S(1)}, u32[]{:S(2)}, u32[]{:S(2)}) %collective-permute-start.20) | collective-permute-done | bytes 196640 | tf_op jit(solution)/shard_map/ppermute | solution.py:346
  213.8 13.3 %collective-permute-done.17 = bf16[128,3584]{1,0:T(8,128)(2,1)S(1)} collective-permute-done((bf16[128,3584]{1,0:T(8,128)(2,1)S(1)}, bf16[128,3584]{1,0:T(8,128)(2,1)S(1)}, u32[]{:S(2)}, u32[]{:S(2)}) %collective-permute-start.17) | collective-permute-done | bytes 917536 | tf_op jit(solution)/shard_map/ppermute | solution.py:337
  229.8 4.9 %all-to-all-start.5 = ((bf16[4,48,3584]{2,1,0:T(8,128)(2,1)}), bf16[4,48,3584]{2,1,0:T(8,128)(2,1)}, u32[]{:S(2)}, u32[]{:S(2)}) async-start(bf16[4,48,3584]{2,1,0:T(8,128)(2,1)} %bitcast.102), calls=%async_computation.5 | async-start | bytes 2752512 | tf_op jit(solution)/shard_map/all_to_all | solution.py:355
  239.7 1.8 collective-permute-start.21
  241.5 33.5 %collective-permute-done.23.refs_7_ = bf16[192,512]{1,0:T(8,128)(2,1)S(1)} collective-permute-done((bf16[192,512]{1,0:T(8,128)(2,1)S(1)}, bf16[192,512]{1,0:T(8,128)(2,1)S(1)}, u32[]{:S(2)}, u32[]{:S(2)}) %collective-permute-start.23) | collective-permute-done | bytes 196640 | tf_op jit(solution)/shard_map/ppermute | solution.py:346
  275.7 12.5 %shard_map.118 = (bf16[3584,256]{1,0:T(8,128)(2,1)}, bf16[3584,256]{1,0:T(8,128)(2,1)}) custom-call(s32[1]{0:T(128)} %bitcast.38.which_ref, bf16[4,192,512]{2,1,0:T(8,128)(2,1)} %get-tuple-element.106.refs_0_, bf16[2,192,512]{2,1,0:T(8,128)(2,1)} %copy-done.13, bf16[4,192,512]{2,1,0:T(8,128)(2,1)} %get-tuple-element.120.refs_2_, ...), custom_call_target="tpu_custom_call" | custom-call | flops 1 | bytes 1 | tf_op jit(solution)/shard_map/pallas_call | solution.py:293
  288.2 3.2 %add_convert_fusion = bf16[256,3584]{1,0:T(8,128)(2,1)} fusion(bf16[256,3584]{1,0:T(8,128)(2,1)} %collective-permute-done.22, bf16[256,3584]{1,0:T(8,128)(2,1)S(1)} %copy-done.3), kind=kLoop, calls=%fused_computation.4 | loop fusion | flops 3670016 | bytes 5505024 | tf_op jit(solution)/shard_map/convert_element_type | solution.py:458
  291.4 2.3 fusion.11
  294.9 3.2 %shard_map.119 = bf16[128,3584]{1,0:T(8,128)(2,1)} custom-call(bf16[128,384]{1,0:T(8,128)(2,1)} %copy.58.matrix_ref, bf16[384,3584]{1,0:T(8,128)(2,1)} %bitcast.91, bf16[128,3584]{1,0:T(8,128)(2,1)} %collective-permute-done.21.got_ref), custom_call_target="tpu_custom_call" | custom-call | flops 1 | bytes 22000000 | tf_op jit(solution)/shard_map/pallas_call | solution.py:94
  (162 shorter events, 46.8 us)
Async XLA Ops:
  1.7 10.3 %collective-permute-start = (bf16[16,3584]{1,0:T(8,128)(2,1)S(1)}, bf16[16,3584]{1,0:T(8,128)(2,1)S(1)}, u32[]{:S(2)}, u32[]{:S(2)}) collective-permute-start(bf16[16,3584]{1,0:T(8,128)(2,1)S(1)} %slice_bitcast_fusion.1), channel_id=1, source_target_pairs={{0,8},{1,9},{2,10},{3,11},{4,12},{5,13},{6,14},{7,15},{8,0},{9,1},... | collective-permute-start | bytes 344072 | tf_op jit(solution)/shard_map/ppermute | solution.py:337
  12.7 53.2 %all-to-all-start = ((bf16[4,96,3584]{2,1,0:T(8,128)(2,1)}), bf16[4,96,3584]{2,1,0:T(8,128)(2,1)S(1)}, u32[]{:S(2)}, u32[]{:S(2)}) async-start(bf16[4,96,3584]{2,1,0:T(8,128)(2,1)} %bitcast.100), calls=%async_computation | async-start | bytes 5505024 | tf_op jit(solution)/shard_map/all_to_all | solution.py:355
  16.5 50.7 %collective-permute-start.3 = (bf16[3584,512]{1,0:T(8,128)(2,1)}, bf16[3584,512]{1,0:T(8,128)(2,1)}, u32[]{:S(2)}, u32[]{:S(2)}) collective-permute-start(bf16[3584,512]{1,0:T(8,128)(2,1)} %bitcast.75), channel_id=1, source_target_pairs={{0,1},{1,0},{2,3},{3,2},{4,5},{5,4},{6,7},{7,6},{8,9},{9,8},{10,11... | collective-permute-start | bytes 11010056 | tf_op jit(solution)/shard_map/ppermute | solution.py:337
  16.5 50.7 %collective-permute-start.4 = (bf16[3584,512]{1,0:T(8,128)(2,1)}, bf16[3584,512]{1,0:T(8,128)(2,1)}, u32[]{:S(2)}, u32[]{:S(2)}) collective-permute-start(bf16[3584,512]{1,0:T(8,128)(2,1)} %bitcast.80), channel_id=1, source_target_pairs={{0,1},{1,0},{2,3},{3,2},{4,5},{5,4},{6,7},{7,6},{8,9},{9,8},{10,11... | collective-permute-start | bytes 11010056 | tf_op jit(solution)/shard_map/ppermute | solution.py:337
  17.0 50.2 %collective-permute-start.5 = (bf16[512,3584]{1,0:T(8,128)(2,1)}, bf16[512,3584]{1,0:T(8,128)(2,1)}, u32[]{:S(2)}, u32[]{:S(2)}) collective-permute-start(bf16[512,3584]{1,0:T(8,128)(2,1)} %bitcast.85), channel_id=1, source_target_pairs={{0,1},{1,0},{2,3},{3,2},{4,5},{5,4},{6,7},{7,6},{8,9},{9,8},{10,11... | collective-permute-start | bytes 11010056 | tf_op jit(solution)/shard_map/ppermute | solution.py:337
  17.0 30.4 %collective-permute-start.1 = (f32[128,4]{0,1:T(4,128)}, f32[128,4]{0,1:T(4,128)S(1)}, u32[]{:S(2)}, u32[]{:S(2)}) collective-permute-start(f32[128,4]{0,1:T(4,128)} %pad_maximum_fusion.1), channel_id=1, source_target_pairs={{0,8},{1,9},{2,10},{3,11},{4,12},{5,13},{6,14},{7,15},{8,0},{9,1},... | collective-permute-start | bytes 6152 | tf_op jit(solution)/shard_map/ppermute | solution.py:337
  18.8 44.4 %collective-permute-start.2 = (bf16[112,3584]{1,0:T(8,128)(2,1)S(1)}, bf16[112,3584]{1,0:T(8,128)(2,1)}, u32[]{:S(2)}, u32[]{:S(2)}) collective-permute-start(bf16[112,3584]{1,0:T(8,128)(2,1)S(1)} %slice_bitcast_fusion), channel_id=1, source_target_pairs={{0,8},{1,9},{2,10},{3,11},{4,12},{5,13},{6,14},{7,15},{8,0},{9,1},... | collective-permute-start | bytes 2408456 | tf_op jit(solution)/shard_map/ppermute | solution.py:337
  67.2 54.0 %collective-permute-start.7 = (bf16[4,2,48,3584]{3,2,1,0:T(8,128)(2,1)S(1)}, bf16[4,2,48,3584]{3,2,1,0:T(8,128)(2,1)}, u32[]{:S(2)}, u32[]{:S(2)}) collective-permute-start(bf16[4,2,48,3584]{3,2,1,0:T(8,128)(2,1)S(1)} %bitcast.69), channel_id=1, source_target_pairs={{0,1},{1,0},{2,3},{3,2},{4,5},{5,4},{6,7},{7,6},{8,9},{9,8},{10,11... | collective-permute-start | bytes 8257544 | tf_op jit(solution)/shard_map/ppermute | solution.py:337
  67.9 53.2 %all-to-all-start.1 = ((bf16[4,48,3584]{2,1,0:T(8,128)(2,1)}), bf16[4,48,3584]{2,1,0:T(8,128)(2,1)}, u32[]{:S(2)}, u32[]{:S(2)}) async-start(bf16[4,48,3584]{2,1,0:T(8,128)(2,1)} %bitcast.99), calls=%async_computation.1 | async-start | bytes 2752512 | tf_op jit(solution)/shard_map/all_to_all | solution.py:355
  74.5 46.6 %collective-permute-start.8 = (bf16[192,3584]{1,0:T(8,128)(2,1)}, bf16[192,3584]{1,0:T(8,128)(2,1)}, u32[]{:S(2)}, u32[]{:S(2)}) collective-permute-start(bf16[192,3584]{1,0:T(8,128)(2,1)} %bitcast.105), channel_id=1, source_target_pairs={{0,16},{16,0},{1,17},{17,1},{2,18},{18,2},{3,19},{19,3},{4,20},{20... | collective-permute-start | bytes 4128776 | tf_op jit(solution)/shard_map/ppermute | solution.py:346
  76.0 42.5 %collective-permute-start.6 = (bf16[128,3584]{1,0:T(8,128)(2,1)}, bf16[128,3584]{1,0:T(8,128)(2,1)}, u32[]{:S(2)}, u32[]{:S(2)}) collective-permute-start(bf16[128,3584]{1,0:T(8,128)(2,1)} %bitcast.125), channel_id=1, source_target_pairs={{0,8},{1,9},{2,10},{3,11},{4,12},{5,13},{6,14},{7,15},{8,0},{9,1},... | collective-permute-start | bytes 2752520 | tf_op jit(solution)/shard_map/ppermute | solution.py:337
  121.1 20.5 %all-to-all-start.2 = ((bf16[4,48,3584]{2,1,0:T(8,128)(2,1)}), bf16[4,48,3584]{2,1,0:T(8,128)(2,1)S(1)}, u32[]{:S(2)}, u32[]{:S(2)}) async-start(bf16[4,48,3584]{2,1,0:T(8,128)(2,1)} %bitcast.98), calls=%async_computation.2 | async-start | bytes 2752512 | tf_op jit(solution)/shard_map/all_to_all | solution.py:355
  125.0 15.5 %collective-permute-start.10 = (bf16[192,3584]{1,0:T(8,128)(2,1)}, bf16[192,3584]{1,0:T(8,128)(2,1)S(1)}, u32[]{:S(2)}, u32[]{:S(2)}) collective-permute-start(bf16[192,3584]{1,0:T(8,128)(2,1)} %collective-permute-done.8.refs_12_), channel_id=1, source_target_pairs={{0,1},{1,0},{2,3},{3,2},{4,5},{5,4},{6,7},{7,6},{8,9},{9,8},{10,11... | collective-permute-start | bytes 4128776 | tf_op jit(solution)/shard_map/ppermute | solution.py:337
  125.1 16.6 %collective-permute-start.9 = (bf16[192,3584]{1,0:T(8,128)(2,1)}, bf16[192,3584]{1,0:T(8,128)(2,1)}, u32[]{:S(2)}, u32[]{:S(2)}) collective-permute-start(bf16[192,3584]{1,0:T(8,128)(2,1)} %bitcast.27.x_ref.refs_10_), channel_id=1, source_target_pairs={{0,1},{1,0},{2,3},{3,2},{4,5},{5,4},{6,7},{7,6},{8,9},{9,8},{10,11... | collective-permute-start | bytes 4128776 | tf_op jit(solution)/shard_map/ppermute | solution.py:337
  125.6 14.9 %collective-permute-start.12 = (bf16[2,192,512]{2,1,0:T(8,128)(2,1)S(1)}, bf16[2,192,512]{2,1,0:T(8,128)(2,1)S(1)}, u32[]{:S(2)}, u32[]{:S(2)}) collective-permute-start(bf16[2,192,512]{2,1,0:T(8,128)(2,1)S(1)} %slice.33), channel_id=1, source_target_pairs={{0,1},{1,0},{2,3},{3,2},{4,5},{5,4},{6,7},{7,6},{8,9},{9,8},{10,11... | collective-permute-start | bytes 1179656 | tf_op jit(solution)/shard_map/ppermute | solution.py:337
  125.8 14.7 %collective-permute-start.11 = (bf16[2,192,256]{2,1,0:T(8,128)(2,1)S(1)}, bf16[2,192,256]{2,1,0:T(8,128)(2,1)S(1)}, u32[]{:S(2)}, u32[]{:S(2)}) collective-permute-start(bf16[2,192,256]{2,1,0:T(8,128)(2,1)S(1)} %slice.32), channel_id=1, source_target_pairs={{0,1},{1,0},{2,3},{3,2},{4,5},{5,4},{6,7},{7,6},{8,9},{9,8},{10,11... | collective-permute-start | bytes 589832 | tf_op jit(solution)/shard_map/ppermute | solution.py:337
  141.7 26.2 %all-to-all-start.3 = ((bf16[4,48,3584]{2,1,0:T(8,128)(2,1)}), bf16[4,48,3584]{2,1,0:T(8,128)(2,1)S(1)}, u32[]{:S(2)}, u32[]{:S(2)}) async-start(bf16[4,48,3584]{2,1,0:T(8,128)(2,1)} %bitcast.104), calls=%async_computation.3 | async-start | bytes 2752512 | tf_op jit(solution)/shard_map/all_to_all | solution.py:355
  145.6 22.3 %collective-permute-start.13 = (bf16[192,3584]{1,0:T(8,128)(2,1)S(1)}, bf16[192,3584]{1,0:T(8,128)(2,1)}, u32[]{:S(2)}, u32[]{:S(2)}) collective-permute-start(bf16[192,3584]{1,0:T(8,128)(2,1)S(1)} %bitcast.92), channel_id=1, source_target_pairs={{0,1},{1,0},{2,3},{3,2},{4,5},{5,4},{6,7},{7,6},{8,9},{9,8},{10,11... | collective-permute-start | bytes 4128776 | tf_op jit(solution)/shard_map/ppermute | solution.py:337
  146.6 19.9 %collective-permute-start.15 = (bf16[192,512]{1,0:T(8,128)(2,1)S(1)}, bf16[192,512]{1,0:T(8,128)(2,1)S(1)}, u32[]{:S(2)}, u32[]{:S(2)}) collective-permute-start(bf16[192,512]{1,0:T(8,128)(2,1)S(1)} %dynamic-slice_bitcast_fusion.3), channel_id=1, source_target_pairs={{0,16},{16,0},{1,17},{17,1},{2,18},{18,2},{3,19},{19,3},{4,20},{20... | collective-permute-start | bytes 589832 | tf_op jit(solution)/shard_map/ppermute | solution.py:346
  147.2 19.3 %collective-permute-start.16 = (bf16[192,512]{1,0:T(8,128)(2,1)S(1)}, bf16[192,512]{1,0:T(8,128)(2,1)S(1)}, u32[]{:S(2)}, u32[]{:S(2)}) collective-permute-start(bf16[192,512]{1,0:T(8,128)(2,1)S(1)} %dynamic-slice_bitcast_fusion.2), channel_id=1, source_target_pairs={{0,16},{16,0},{1,17},{17,1},{2,18},{18,2},{3,19},{19,3},{4,20},{20... | collective-permute-start | bytes 589832 | tf_op jit(solution)/shard_map/ppermute | solution.py:346
  148.8 17.8 %collective-permute-start.14 = (bf16[2,192,256]{2,1,0:T(8,128)(2,1)S(1)}, bf16[2,192,256]{2,1,0:T(8,128)(2,1)S(1)}, u32[]{:S(2)}, u32[]{:S(2)}) collective-permute-start(bf16[2,192,256]{2,1,0:T(8,128)(2,1)S(1)} %slice.34), channel_id=1, source_target_pairs={{0,1},{1,0},{2,3},{3,2},{4,5},{5,4},{6,7},{7,6},{8,9},{9,8},{10,11... | collective-permute-start | bytes 589832 | tf_op jit(solution)/shard_map/ppermute | solution.py:337
  172.8 56.5 %all-to-all-start.4 = ((bf16[4,96,3584]{2,1,0:T(8,128)(2,1)}), bf16[4,96,3584]{2,1,0:T(8,128)(2,1)S(1)}, u32[]{:S(2)}, u32[]{:S(2)}) async-start(bf16[4,96,3584]{2,1,0:T(8,128)(2,1)} %bitcast.96), calls=%async_computation.4 | async-start | bytes 5505024 | tf_op jit(solution)/shard_map/all_to_all | solution.py:355
  177.1 50.9 %collective-permute-start.18 = (bf16[192,3584]{1,0:T(8,128)(2,1)}, bf16[192,3584]{1,0:T(8,128)(2,1)}, u32[]{:S(2)}, u32[]{:S(2)}) collective-permute-start(bf16[192,3584]{1,0:T(8,128)(2,1)} %bitcast.27.x_ref.refs_10_), channel_id=1, source_target_pairs={{0,16},{16,0},{1,17},{17,1},{2,18},{18,2},{3,19},{19,3},{4,20},{20... | collective-permute-start | bytes 4128776 | tf_op jit(solution)/shard_map/ppermute | solution.py:346
  180.5 46.5 %collective-permute-start.17 = (bf16[128,3584]{1,0:T(8,128)(2,1)S(1)}, bf16[128,3584]{1,0:T(8,128)(2,1)S(1)}, u32[]{:S(2)}, u32[]{:S(2)}) collective-permute-start(bf16[128,3584]{1,0:T(8,128)(2,1)S(1)} %convolution_convert_fusion.1), channel_id=1, source_target_pairs={{0,8},{1,9},{2,10},{3,11},{4,12},{5,13},{6,14},{7,15},{8,0},{9,1},... | collective-permute-start | bytes 2752520 | tf_op jit(solution)/shard_map/ppermute | solution.py:337
  182.4 31.4 %collective-permute-start.19 = (bf16[2,192,512]{2,1,0:T(8,128)(2,1)S(1)}, bf16[2,192,512]{2,1,0:T(8,128)(2,1)S(1)}, u32[]{:S(2)}, u32[]{:S(2)}) collective-permute-start(bf16[2,192,512]{2,1,0:T(8,128)(2,1)S(1)} %slice.35), channel_id=1, source_target_pairs={{0,1},{1,0},{2,3},{3,2},{4,5},{5,4},{6,7},{7,6},{8,9},{9,8},{10,11... | collective-permute-start | bytes 1179656 | tf_op jit(solution)/shard_map/ppermute | solution.py:337
  182.5 31.3 %collective-permute-start.20 = (bf16[192,512]{1,0:T(8,128)(2,1)S(1)}, bf16[192,512]{1,0:T(8,128)(2,1)S(1)}, u32[]{:S(2)}, u32[]{:S(2)}) collective-permute-start(bf16[192,512]{1,0:T(8,128)(2,1)S(1)} %dynamic-slice_bitcast_fusion.1), channel_id=1, source_target_pairs={{0,16},{16,0},{1,17},{17,1},{2,18},{18,2},{3,19},{19,3},{4,20},{20... | collective-permute-start | bytes 589832 | tf_op jit(solution)/shard_map/ppermute | solution.py:346
  213.8 61.2 %copy-start.20 = (bf16[192,512]{1,0:T(8,128)(2,1)}, bf16[192,512]{1,0:T(8,128)(2,1)S(1)}, u32[]{:S(2)}) copy-start(bf16[192,512]{1,0:T(8,128)(2,1)S(1)} %collective-permute-done.20.refs_6_) | copy-start | bytes 589828
  229.3 58.9 %collective-permute-start.22 = (bf16[256,3584]{1,0:T(8,128)(2,1)}, bf16[256,3584]{1,0:T(8,128)(2,1)}, u32[]{:S(2)}, u32[]{:S(2)}) collective-permute-start(bf16[256,3584]{1,0:T(8,128)(2,1)} %shard_map.116), channel_id=1, source_target_pairs={{0,16},{16,0},{1,17},{17,1},{2,18},{18,2},{3,19},{19,3},{4,20},{20... | collective-permute-start | bytes 5505032 | tf_op jit(solution)/shard_map/ppermute | solution.py:346
  229.8 45.2 %collective-permute-start.24 = (bf16[192,3584]{1,0:T(8,128)(2,1)}, bf16[192,3584]{1,0:T(8,128)(2,1)}, u32[]{:S(2)}, u32[]{:S(2)}) collective-permute-start(bf16[192,3584]{1,0:T(8,128)(2,1)} %collective-permute-done.18.refs_14_), channel_id=1, source_target_pairs={{0,1},{1,0},{2,3},{3,2},{4,5},{5,4},{6,7},{7,6},{8,9},{9,8},{10,11... | collective-permute-start | bytes 4128776 | tf_op jit(solution)/shard_map/ppermute | solution.py:337
  229.8 61.6 %all-to-all-start.5 = ((bf16[4,48,3584]{2,1,0:T(8,128)(2,1)}), bf16[4,48,3584]{2,1,0:T(8,128)(2,1)}, u32[]{:S(2)}, u32[]{:S(2)}) async-start(bf16[4,48,3584]{2,1,0:T(8,128)(2,1)} %bitcast.102), calls=%async_computation.5 | async-start | bytes 2752512 | tf_op jit(solution)/shard_map/all_to_all | solution.py:355
  236.4 38.6 %collective-permute-start.23 = (bf16[192,512]{1,0:T(8,128)(2,1)S(1)}, bf16[192,512]{1,0:T(8,128)(2,1)S(1)}, u32[]{:S(2)}, u32[]{:S(2)}) collective-permute-start(bf16[192,512]{1,0:T(8,128)(2,1)S(1)} %dynamic-slice_bitcast_fusion), channel_id=1, source_target_pairs={{0,16},{16,0},{1,17},{17,1},{2,18},{18,2},{3,19},{19,3},{4,20},{20... | collective-permute-start | bytes 589832 | tf_op jit(solution)/shard_map/ppermute | solution.py:346
  239.7 55.2 %collective-permute-start.21 = (bf16[128,3584]{1,0:T(8,128)(2,1)}, bf16[128,3584]{1,0:T(8,128)(2,1)}, u32[]{:S(2)}, u32[]{:S(2)}) collective-permute-start(bf16[128,3584]{1,0:T(8,128)(2,1)} %convolution_convert_fusion), channel_id=1, source_target_pairs={{0,8},{1,9},{2,10},{3,11},{4,12},{5,13},{6,14},{7,15},{8,0},{9,1},... | collective-permute-start | bytes 2752520 | tf_op jit(solution)/shard_map/ppermute | solution.py:337
  (34 other events, 282.6 us)

commit v14 on v13

--- a/solution.py
+++ b/solution.py
@@ -192,12 +192,14 @@
     )(row_array(rows), *weights)
 
 
-def backward(count, rows_grad, pre_gate, pre_up, weights):
+def backward(count, rows_grad, pre_gate, pre_up, weights, beside=None, near=1):
     width = weights[0].shape[0]
     half_units = weights[0].shape[1] // 2
 
+    piece = count // near
+
     def body(x_ref, pre_gate_ref, pre_up_ref, *refs):
-        units_ref, out_ref, acc_ref = refs[6:]
+        units_ref, out_ref, acc_ref = refs[-3:]
         step = pl.program_id(0)
 
         def quarter(gate_ref, up_ref, down_ref):
@@ -219,23 +221,36 @@
 
         @pl.when(step == 3)
         def _():
-            out_ref[...] = acc_ref[...].astype(BF16)
+            if beside is None:
+                out_ref[...] = acc_ref[...].astype(BF16)
+            else:
+                for n in range(near):
+                    here = slice(n * piece, (n + 1) * piece)
+                    out_ref[n, 0] = acc_ref[here].astype(BF16)
+                    out_ref[n, 1] = refs[6][here]
 
     units = pl.BlockSpec((1, count, half_units), lambda n: (n, 0, 0))
+    whole = pl.BlockSpec((count, width), lambda n: (0, 0))
+    out_spec, out_shape = whole, (count, width)
+    if beside is not None:
+        out_shape = (near, 2, piece, width)
+        out_spec = pl.BlockSpec(out_shape, lambda n: (0, 0, 0, 0))
     return kernel_call(
         body,
         (4,),
-        [row_spec(rows_grad, width), units, units] + weight_specs(width, half_units),
+        [row_spec(rows_grad, width), units, units]
+        + weight_specs(width, half_units)
+        + ([] if beside is None else [whole]),
         [
             pl.BlockSpec((1, count, 2 * half_units), lambda n: (n, 0, 0)),
-            pl.BlockSpec((count, width), lambda n: (0, 0)),
+            out_spec,
         ],
         [
             jax.ShapeDtypeStruct((4, count, 2 * half_units), BF16),
-            jax.ShapeDtypeStruct((count, width), BF16),
+            jax.ShapeDtypeStruct(out_shape, BF16),
         ],
         [pltpu.VMEM((count, width), F32)],
-    )(row_array(rows_grad), pre_gate, pre_up, *weights)
+    )(row_array(rows_grad), pre_gate, pre_up, *weights, *([] if beside is None else [beside]))
 
 
 def down_grad(count, which, hiddens, rows_grad):
@@ -420,38 +435,40 @@
     far_out = near_exchange(far_out)
     far_grad_b = swap(far_grad)
     far_hidden_b = swap(far_hidden[2:])
-    mirror_units = [mirror(for_mirror(units)) for units in (own_units, own_units_b)]
-    far_units, far_input = backward(count, far_grad, far_pre_gate, far_pre_up, weights)
-    far_out, far_units, far_input, far_grad_b, far_hidden_b, mirror_far, *mirror_units = tie(
-        far_out, far_units, far_input, far_grad_b, far_hidden_b, far_in, *mirror_units
+    far_units, inputs = backward(
+        count, far_grad, far_pre_gate, far_pre_up, weights, own_input, near
+    )
+    far_out, far_units, inputs, far_grad_b, far_hidden_b, mirror_far, own_units, own_units_b = tie(
+        far_out, far_units, inputs, far_grad_b, far_hidden_b, far_in, own_units, own_units_b
     )
 
     got_out = far(combine(far_weighting, far_out).astype(BF16))
-    back = near_exchange(
-        jnp.stack([a.reshape(near, piece, width) for a in (far_input, own_input)], axis=1).reshape(2 * count, width)
-    )
+    back = near_exchange(inputs.reshape(2 * count, width))
     mirror_far = mirror(mirror_far)
-    mirror_units.append(mirror(for_mirror(far_units)))
     far_units_b = swap(far_units[2:])
+    all_units = (own_units, own_units_b, far_units, far_units_b)
+    mirror_units = [
+        mirror(jnp.stack([for_mirror(units) for units in all_units[:2]])),
+        *[mirror(for_mirror(units)) for units in all_units[2:]],
+    ]
     hiddens = (own_hidden, own_hidden_b, far_hidden, far_hidden_b)
     rows_grad = ((own, 1), (own_b.reshape(own.shape), 1), far_grad, far_grad_b)
     send_down = down_grad(count, 1 - kept, hiddens, rows_grad)
     keep_down = down_grad(count, kept, hiddens, rows_grad)
-    got_out, back, mirror_far, far_units_b, send_down, keep_down, own_out, *mirror_units = tie(
-        got_out, back, mirror_far, far_units_b, send_down, keep_down, own_out, *mirror_units
+    got_out, back, mirror_far, send_down, keep_down, own_out, *mirror_units = tie(
+        got_out, back, mirror_far, send_down, keep_down, own_out, *mirror_units
     )
 
     got_input = far(combine(of_set(far_back, 0), back).astype(BF16))
     own_out = near_exchange(own_out)
-    mirror_units.append(mirror(for_mirror(far_units_b)))
     got_down = mirror(send_down)
     mirror_far_b = swap(mirror_far)
     grad_gate, grad_up = gate_up_grad(
         count,
         kept,
-        (own_units, own_units_b, far_units, far_units_b),
+        all_units,
         ((own, 0), (own_b.reshape(own.shape), 0), far_in, far_in_b),
-        mirror_units,
+        [mirror_units[0][0], mirror_units[0][1], *mirror_units[1:]],
         (mirror_own, mirror_own_b, mirror_far, mirror_far_b),
     )
     out_acts = (combine(own_weighting, own_out) + got_out.astype(F32)).astype(BF16)

time: 300 us -> 279 us (0.930)
  waiting for transfers between devices: 102 us -> 84.3 us
    ppermute x18, waiting for transfers between devices: 52.9 us -> 42.7 us  [hop(): lax.ppermute(rows, 'expert', [(i, i ^ distance) for i in range(devices)])]
    ppermute x7 -> x6, waiting for transfers between devices: 47.8 us -> 39.5 us  [mirror(): lax.ppermute(rows, 'pipe', [(p, rank_count - 1 - p) for p in range(rank_c...]
    unnamed x70 -> x64, local copies, waits for them, and re-layouts: 7.66 us -> 5.57 us
    ppermute x7 -> x6, starting transfers between devices: 7.82 us -> 6.26 us  [mirror(): lax.ppermute(rows, 'pipe', [(p, rank_count - 1 - p) for p in range(rank_c...]
  transfers between devices with their start and end apart: 31 -> 30, of which waited for: 7 -> 9; matrix products, arithmetic and copies ran while one was open for 12% -> 14% of each run, Pallas kernels for 32% -> 35%
where the time goes in v14:
time: 279 us; the launch traced here: 277 us
  Pallas kernels  99.3 us (36%)
  waiting for transfers between devices  84.3 us (30%)
  starting transfers between devices  46.9 us (17%)
  local copies, waits for them, and re-layouts  20.8 us (7%)
  other arithmetic  14.9 us (5%)
  matrix products  9.58 us (3%)
    ppermute x18, waiting for transfers between devices, hop(): lax.ppermute(rows, 'expert', [(i, i ^ distance) for i in range(devices)])  42.7 us
    ppermute x6, waiting for transfers between devices, mirror(): lax.ppermute(rows, 'pipe', [(p, rank_count - 1 - p) for p in range(rank_c...  39.5 us
    pallas_call x2, Pallas kernels, backward(): kernel_call(body, (4,), [row_spec(rows_grad, width), units, units] + weig...  35.4 us
    pallas_call x2, Pallas kernels, forward(): kernel_call(body, (4,), [row_spec(rows, width)] + weight_specs(width, hal...  27.4 us
    all_to_all x6, starting transfers between devices, near_exchange(): lax.all_to_all(rows.reshape(near, -1, width), 'expert', split_axis=0, con...  26.9 us
    pallas_call x2, Pallas kernels, down_grad(): kernel_call(body, (width // tile,), [pl.BlockSpec((1, count, half_units),...  15.5 us
    ppermute x18, starting transfers between devices, hop(): lax.ppermute(rows, 'expert', [(i, i ^ distance) for i in range(devices)])  13.7 us
    pallas_call x1, Pallas kernels, gate_up_grad(): kernel_call(body, (width // tile,), [pl.BlockSpec((1, count, both), lambd...  12.6 us
  transfers between devices with their start and end apart: 30, of which 9 were waited for; matrix products, arithmetic and copies ran while one was open for 14% of the time, Pallas kernels for 35%

profile of v14, /device:TPU:0, one launch (start us, length us, event | category | flops | bytes accessed | tf_op | source)
XLA Modules:
  0.0 276.9 jit_solution(8658333187048643497)
XLA Ops:
  1.7 4.0 %collective-permute-start = (bf16[16,3584]{1,0:T(8,128)(2,1)S(1)}, bf16[16,3584]{1,0:T(8,128)(2,1)S(1)}, u32[]{:S(2)}, u32[]{:S(2)}) collective-permute-start(bf16[16,3584]{1,0:T(8,128)(2,1)S(1)} %slice_bitcast_fusion.3), channel_id=1, source_target_pairs={{0,8},{1,9},{2,10},{3,11},{4,12},{5,13},{6,14},{7,15},{8,0},{9,1},... | collective-permute-start | bytes 344072 | tf_op jit(solution)/shard_map/ppermute | solution.py:352
  8.9 2.5 fusion
  12.7 3.8 %all-to-all-start = ((bf16[4,96,3584]{2,1,0:T(8,128)(2,1)}), bf16[4,96,3584]{2,1,0:T(8,128)(2,1)S(1)}, u32[]{:S(2)}, u32[]{:S(2)}) async-start(bf16[4,96,3584]{2,1,0:T(8,128)(2,1)} %bitcast.98), calls=%async_computation | async-start | bytes 5505024 | tf_op jit(solution)/shard_map/all_to_all | solution.py:370
  17.0 1.8 collective-permute-start.1
  19.9 27.5 %collective-permute-done.1 = f32[128,4]{0,1:T(4,128)S(1)} collective-permute-done((f32[128,4]{0,1:T(4,128)}, f32[128,4]{0,1:T(4,128)S(1)}, u32[]{:S(2)}, u32[]{:S(2)}) %collective-permute-start.1) | collective-permute-done | bytes 2080 | tf_op jit(solution)/shard_map/ppermute | solution.py:352
  61.3 2.0 collective-permute-done.2.refs_1_
  63.3 2.6 shard_map.110
  68.0 6.6 %all-to-all-start.1 = ((bf16[4,48,3584]{2,1,0:T(8,128)(2,1)}), bf16[4,48,3584]{2,1,0:T(8,128)(2,1)}, u32[]{:S(2)}, u32[]{:S(2)}) async-start(bf16[4,48,3584]{2,1,0:T(8,128)(2,1)} %bitcast.95), calls=%async_computation.1 | async-start | bytes 2752512 | tf_op jit(solution)/shard_map/all_to_all | solution.py:370
  77.4 13.3 %shard_map.111 = (f32[4,192,256]{2,1,0:T(8,128)}, f32[4,192,256]{2,1,0:T(8,128)}, bf16[4,192,256]{2,1,0:T(8,128)(2,1)}, bf16[192,3584]{1,0:T(8,128)(2,1)}) custom-call(bf16[4,2,48,3584]{3,2,1,0:T(8,128)(2,1)} %bitcast.68, bf16[3584,512]{1,0:T(8,128)(2,1)} %bitcast.74, bf16[3584,512]{1,0:T(8,128)(2,1)} %bitcast.79, bf16[512,3584]{1,0:T(8,128)(2,1)} %bitcast.84, ...), custom_call_target="tpu_custom_call" | custom-call | flops 1 | bytes 1 | tf_op jit(solution)/shard_map/pallas_call | solution.py:180
  90.6 17.0 %shard_map.112 = (bf16[4,192,512]{2,1,0:T(8,128)(2,1)}, bf16[192,3584]{1,0:T(8,128)(2,1)}) custom-call(bf16[4,2,48,3584]{3,2,1,0:T(8,128)(2,1)} %bitcast.69, f32[4,192,256]{2,1,0:T(8,128)} %get-tuple-element.90.pre_gate_ref, f32[4,192,256]{2,1,0:T(8,128)} %get-tuple-element.91.pre_up_ref, bf16[3584,512]{1,0:T(8,128)(2,1)} %bitcast.75, ...), custom_call_target="tpu_custom_call" | custom-call | flops 1 | bytes 1 | tf_op jit(solution)/shard_map/pallas_call | solution.py:238
  108.4 10.1 %collective-permute-done.6.refs_1_ = bf16[128,3584]{1,0:T(8,128)(2,1)} collective-permute-done((bf16[128,3584]{1,0:T(8,128)(2,1)}, bf16[128,3584]{1,0:T(8,128)(2,1)}, u32[]{:S(2)}, u32[]{:S(2)}) %collective-permute-start.6) | collective-permute-done | bytes 917536 | tf_op jit(solution)/shard_map/ppermute | solution.py:352
  118.5 2.6 shard_map.113
  121.2 3.9 %all-to-all-start.2 = ((bf16[4,48,3584]{2,1,0:T(8,128)(2,1)}), bf16[4,48,3584]{2,1,0:T(8,128)(2,1)S(1)}, u32[]{:S(2)}, u32[]{:S(2)}) async-start(bf16[4,48,3584]{2,1,0:T(8,128)(2,1)} %bitcast.94), calls=%async_computation.2 | async-start | bytes 2752512 | tf_op jit(solution)/shard_map/all_to_all | solution.py:370
  126.3 14.1 %shard_map.114 = (f32[4,192,256]{2,1,0:T(8,128)}, f32[4,192,256]{2,1,0:T(8,128)}, bf16[4,192,256]{2,1,0:T(8,128)(2,1)}, bf16[192,3584]{1,0:T(8,128)(2,1)}) custom-call(bf16[192,3584]{1,0:T(8,128)(2,1)} %bitcast.27.x_ref.refs_10_, bf16[3584,512]{1,0:T(8,128)(2,1)} %bitcast.76, bf16[3584,512]{1,0:T(8,128)(2,1)} %bitcast.81, bf16[512,3584]{1,0:T(8,128)(2,1)} %bitcast.86, ...), custom_call_target="tpu_custom_call" | custom-call | flops 1 | bytes 1 | tf_op jit(solution)/shard_map/pallas_call | solution.py:180
  141.8 3.9 %all-to-all-start.3 = ((bf16[4,48,3584]{2,1,0:T(8,128)(2,1)}), bf16[4,48,3584]{2,1,0:T(8,128)(2,1)S(1)}, u32[]{:S(2)}, u32[]{:S(2)}) async-start(bf16[4,48,3584]{2,1,0:T(8,128)(2,1)} %bitcast.101), calls=%async_computation.3 | async-start | bytes 2752512 | tf_op jit(solution)/shard_map/all_to_all | solution.py:370
  146.3 18.4 %shard_map.115 = (bf16[4,192,512]{2,1,0:T(8,128)(2,1)}, bf16[4,2,48,3584]{3,2,1,0:T(8,128)(2,1)}) custom-call(bf16[192,3584]{1,0:T(8,128)(2,1)} %bitcast.91, f32[4,192,256]{2,1,0:T(8,128)} %get-tuple-element.109.pre_gate_ref, f32[4,192,256]{2,1,0:T(8,128)} %get-tuple-element.110.pre_up_ref, bf16[3584,512]{1,0:T(8,128)(2,1)} %bitcast.77, ...), custom_call_target="tpu_custom_call" | custom-call | flops 1 | bytes 1 | tf_op jit(solution)/shard_map/pallas_call | solution.py:238
  166.6 4.2 %all-to-all-start.4 = ((bf16[4,96,3584]{2,1,0:T(8,128)(2,1)}), bf16[4,96,3584]{2,1,0:T(8,128)(2,1)S(1)}, u32[]{:S(2)}, u32[]{:S(2)}) async-start(bf16[4,96,3584]{2,1,0:T(8,128)(2,1)} %bitcast.97), calls=%async_computation.4 | async-start | bytes 5505024 | tf_op jit(solution)/shard_map/all_to_all | solution.py:370
  171.9 3.2 %convolution_convert_fusion.1 = bf16[128,3584]{1,0:T(8,128)(2,1)} fusion(f32[128,192]{0,1:T(8,128)S(1)} %get-tuple-element.149, bf16[192,3584]{1,0:T(8,128)(2,1)} %bitcast.96), kind=kOutput, calls=%fused_computation.3 | convolution fusion | flops 1057423360 | bytes 2392064 | tf_op jit(solution)/shard_map/dot_general | solution.py:111
  175.1 1.8 collective-permute-start.15
  183.5 7.7 %shard_map.117 = bf16[256,3584]{1,0:T(8,128)(2,1)} custom-call(s32[1]{0:T(128)} %bitcast.34.which_ref, bf16[4,192,256]{2,1,0:T(8,128)(2,1)} %get-tuple-element.104.refs_0_, bf16[2,192,256]{2,1,0:T(8,128)(2,1)} %copy-done.12, bf16[4,192,256]{2,1,0:T(8,128)(2,1)} %get-tuple-element.114.refs_2_, bf16[2,192,256]{2,1,0:T(8,128)(2,1)} %copy-done.13, ...), custom_call_target="tpu_custom_call" | custom-call | flops 1 | bytes 1 | tf_op jit(solution)/shard_map/pallas_call | solution.py:275
  191.2 7.7 %shard_map.116 = bf16[256,3584]{1,0:T(8,128)(2,1)} custom-call(s32[1]{0:T(128)S(6)} %sub.38.which_ref, bf16[4,192,256]{2,1,0:T(8,128)(2,1)} %get-tuple-element.104.refs_0_, bf16[2,192,256]{2,1,0:T(8,128)(2,1)} %copy-done.12, bf16[4,192,256]{2,1,0:T(8,128)(2,1)} %get-tuple-element.114.refs_2_, bf16[2,192,256]{2,1,0:T(8,128)(2,1)} %copy-done.13, ...), custom_call_target="tpu_custom_call" | custom-call | flops 1 | bytes 1 | tf_op jit(solution)/shard_map/pallas_call | solution.py:275
  199.0 17.7 %collective-permute-done.18.refs_6_ = bf16[192,512]{1,0:T(8,128)(2,1)S(1)} collective-permute-done((bf16[192,512]{1,0:T(8,128)(2,1)S(1)}, bf16[192,512]{1,0:T(8,128)(2,1)S(1)}, u32[]{:S(2)}, u32[]{:S(2)}) %collective-permute-start.18) | collective-permute-done | bytes 196640 | tf_op jit(solution)/shard_map/ppermute | solution.py:361
  216.7 3.0 %collective-permute-done.20.refs_7_ = bf16[192,512]{1,0:T(8,128)(2,1)S(1)} collective-permute-done((bf16[192,512]{1,0:T(8,128)(2,1)S(1)}, bf16[192,512]{1,0:T(8,128)(2,1)S(1)}, u32[]{:S(2)}, u32[]{:S(2)}) %collective-permute-start.20) | collective-permute-done | bytes 196640 | tf_op jit(solution)/shard_map/ppermute | solution.py:361
  220.4 2.1 all-to-all-done.4
  223.1 4.5 %all-to-all-start.5 = ((bf16[4,48,3584]{2,1,0:T(8,128)(2,1)}), bf16[4,48,3584]{2,1,0:T(8,128)(2,1)}, u32[]{:S(2)}, u32[]{:S(2)}) async-start(bf16[4,48,3584]{2,1,0:T(8,128)(2,1)} %bitcast.100), calls=%async_computation.5 | async-start | bytes 2752512 | tf_op jit(solution)/shard_map/all_to_all | solution.py:370
  232.2 12.6 %shard_map.118 = (bf16[3584,256]{1,0:T(8,128)(2,1)}, bf16[3584,256]{1,0:T(8,128)(2,1)}) custom-call(s32[1]{0:T(128)} %bitcast.34.which_ref, bf16[4,192,512]{2,1,0:T(8,128)(2,1)} %get-tuple-element.124.refs_0_, bf16[2,192,512]{2,1,0:T(8,128)(2,1)} %copy-done.11, bf16[4,192,512]{2,1,0:T(8,128)(2,1)} %get-tuple-element.126.refs_2_, ...), custom_call_target="tpu_custom_call" | custom-call | flops 1 | bytes 1 | tf_op jit(solution)/shard_map/pallas_call | solution.py:308
  244.9 18.8 %collective-permute-done.22 = bf16[256,3584]{1,0:T(8,128)(2,1)} collective-permute-done((bf16[256,3584]{1,0:T(8,128)(2,1)}, bf16[256,3584]{1,0:T(8,128)(2,1)}, u32[]{:S(2)}, u32[]{:S(2)}) %collective-permute-start.22) | collective-permute-done | bytes 1835040 | tf_op jit(solution)/shard_map/ppermute | solution.py:361
  263.7 3.2 %add_convert_fusion = bf16[256,3584]{1,0:T(8,128)(2,1)} fusion(bf16[256,3584]{1,0:T(8,128)(2,1)} %collective-permute-done.22, bf16[256,3584]{1,0:T(8,128)(2,1)S(1)} %copy-done.3), kind=kLoop, calls=%fused_computation.4 | loop fusion | flops 3670016 | bytes 5505024 | tf_op jit(solution)/shard_map/convert_element_type | solution.py:475
  266.9 2.3 fusion.11
  269.2 2.3 add_convert_fusion.1
  271.5 2.3 collective-permute-done.21.got_ref
  273.8 3.2 %shard_map.119 = bf16[128,3584]{1,0:T(8,128)(2,1)} custom-call(bf16[128,384]{1,0:T(8,128)(2,1)} %copy.53.matrix_ref, bf16[384,3584]{1,0:T(8,128)(2,1)} %bitcast.89, bf16[128,3584]{1,0:T(8,128)(2,1)} %collective-permute-done.21.got_ref), custom_call_target="tpu_custom_call" | custom-call | flops 1 | bytes 22000000 | tf_op jit(solution)/shard_map/pallas_call | solution.py:94
  (153 shorter events, 45.0 us)
Async XLA Ops:
  1.7 10.3 %collective-permute-start = (bf16[16,3584]{1,0:T(8,128)(2,1)S(1)}, bf16[16,3584]{1,0:T(8,128)(2,1)S(1)}, u32[]{:S(2)}, u32[]{:S(2)}) collective-permute-start(bf16[16,3584]{1,0:T(8,128)(2,1)S(1)} %slice_bitcast_fusion.3), channel_id=1, source_target_pairs={{0,8},{1,9},{2,10},{3,11},{4,12},{5,13},{6,14},{7,15},{8,0},{9,1},... | collective-permute-start | bytes 344072 | tf_op jit(solution)/shard_map/ppermute | solution.py:352
  12.7 53.2 %all-to-all-start = ((bf16[4,96,3584]{2,1,0:T(8,128)(2,1)}), bf16[4,96,3584]{2,1,0:T(8,128)(2,1)S(1)}, u32[]{:S(2)}, u32[]{:S(2)}) async-start(bf16[4,96,3584]{2,1,0:T(8,128)(2,1)} %bitcast.98), calls=%async_computation | async-start | bytes 5505024 | tf_op jit(solution)/shard_map/all_to_all | solution.py:370
  16.5 50.7 %collective-permute-start.3 = (bf16[3584,512]{1,0:T(8,128)(2,1)}, bf16[3584,512]{1,0:T(8,128)(2,1)}, u32[]{:S(2)}, u32[]{:S(2)}) collective-permute-start(bf16[3584,512]{1,0:T(8,128)(2,1)} %bitcast.73), channel_id=1, source_target_pairs={{0,1},{1,0},{2,3},{3,2},{4,5},{5,4},{6,7},{7,6},{8,9},{9,8},{10,11... | collective-permute-start | bytes 11010056 | tf_op jit(solution)/shard_map/ppermute | solution.py:352
  16.5 50.7 %collective-permute-start.4 = (bf16[3584,512]{1,0:T(8,128)(2,1)}, bf16[3584,512]{1,0:T(8,128)(2,1)}, u32[]{:S(2)}, u32[]{:S(2)}) collective-permute-start(bf16[3584,512]{1,0:T(8,128)(2,1)} %bitcast.78), channel_id=1, source_target_pairs={{0,1},{1,0},{2,3},{3,2},{4,5},{5,4},{6,7},{7,6},{8,9},{9,8},{10,11... | collective-permute-start | bytes 11010056 | tf_op jit(solution)/shard_map/ppermute | solution.py:352
  17.0 50.2 %collective-permute-start.5 = (bf16[512,3584]{1,0:T(8,128)(2,1)}, bf16[512,3584]{1,0:T(8,128)(2,1)}, u32[]{:S(2)}, u32[]{:S(2)}) collective-permute-start(bf16[512,3584]{1,0:T(8,128)(2,1)} %bitcast.83), channel_id=1, source_target_pairs={{0,1},{1,0},{2,3},{3,2},{4,5},{5,4},{6,7},{7,6},{8,9},{9,8},{10,11... | collective-permute-start | bytes 11010056 | tf_op jit(solution)/shard_map/ppermute | solution.py:352
  17.0 30.4 %collective-permute-start.1 = (f32[128,4]{0,1:T(4,128)}, f32[128,4]{0,1:T(4,128)S(1)}, u32[]{:S(2)}, u32[]{:S(2)}) collective-permute-start(f32[128,4]{0,1:T(4,128)} %pad_maximum_fusion.1), channel_id=1, source_target_pairs={{0,8},{1,9},{2,10},{3,11},{4,12},{5,13},{6,14},{7,15},{8,0},{9,1},... | collective-permute-start | bytes 6152 | tf_op jit(solution)/shard_map/ppermute | solution.py:352
  18.8 44.4 %collective-permute-start.2 = (bf16[112,3584]{1,0:T(8,128)(2,1)S(1)}, bf16[112,3584]{1,0:T(8,128)(2,1)}, u32[]{:S(2)}, u32[]{:S(2)}) collective-permute-start(bf16[112,3584]{1,0:T(8,128)(2,1)S(1)} %slice_bitcast_fusion), channel_id=1, source_target_pairs={{0,8},{1,9},{2,10},{3,11},{4,12},{5,13},{6,14},{7,15},{8,0},{9,1},... | collective-permute-start | bytes 2408456 | tf_op jit(solution)/shard_map/ppermute | solution.py:352
  67.2 53.9 %collective-permute-start.7 = (bf16[4,2,48,3584]{3,2,1,0:T(8,128)(2,1)S(1)}, bf16[4,2,48,3584]{3,2,1,0:T(8,128)(2,1)}, u32[]{:S(2)}, u32[]{:S(2)}) collective-permute-start(bf16[4,2,48,3584]{3,2,1,0:T(8,128)(2,1)S(1)} %bitcast.67), channel_id=1, source_target_pairs={{0,1},{1,0},{2,3},{3,2},{4,5},{5,4},{6,7},{7,6},{8,9},{9,8},{10,11... | collective-permute-start | bytes 8257544 | tf_op jit(solution)/shard_map/ppermute | solution.py:352
  68.0 53.1 %all-to-all-start.1 = ((bf16[4,48,3584]{2,1,0:T(8,128)(2,1)}), bf16[4,48,3584]{2,1,0:T(8,128)(2,1)}, u32[]{:S(2)}, u32[]{:S(2)}) async-start(bf16[4,48,3584]{2,1,0:T(8,128)(2,1)} %bitcast.95), calls=%async_computation.1 | async-start | bytes 2752512 | tf_op jit(solution)/shard_map/all_to_all | solution.py:370
  74.7 46.5 %collective-permute-start.8 = (bf16[192,3584]{1,0:T(8,128)(2,1)}, bf16[192,3584]{1,0:T(8,128)(2,1)}, u32[]{:S(2)}, u32[]{:S(2)}) collective-permute-start(bf16[192,3584]{1,0:T(8,128)(2,1)} %bitcast.102), channel_id=1, source_target_pairs={{0,16},{16,0},{1,17},{17,1},{2,18},{18,2},{3,19},{19,3},{4,20},{20... | collective-permute-start | bytes 4128776 | tf_op jit(solution)/shard_map/ppermute | solution.py:361
  76.1 42.4 %collective-permute-start.6 = (bf16[128,3584]{1,0:T(8,128)(2,1)}, bf16[128,3584]{1,0:T(8,128)(2,1)}, u32[]{:S(2)}, u32[]{:S(2)}) collective-permute-start(bf16[128,3584]{1,0:T(8,128)(2,1)} %bitcast.121), channel_id=1, source_target_pairs={{0,8},{1,9},{2,10},{3,11},{4,12},{5,13},{6,14},{7,15},{8,0},{9,1},... | collective-permute-start | bytes 2752520 | tf_op jit(solution)/shard_map/ppermute | solution.py:352
  121.2 20.5 %all-to-all-start.2 = ((bf16[4,48,3584]{2,1,0:T(8,128)(2,1)}), bf16[4,48,3584]{2,1,0:T(8,128)(2,1)S(1)}, u32[]{:S(2)}, u32[]{:S(2)}) async-start(bf16[4,48,3584]{2,1,0:T(8,128)(2,1)} %bitcast.94), calls=%async_computation.2 | async-start | bytes 2752512 | tf_op jit(solution)/shard_map/all_to_all | solution.py:370
  125.0 15.5 %collective-permute-start.10 = (bf16[192,3584]{1,0:T(8,128)(2,1)}, bf16[192,3584]{1,0:T(8,128)(2,1)S(1)}, u32[]{:S(2)}, u32[]{:S(2)}) collective-permute-start(bf16[192,3584]{1,0:T(8,128)(2,1)} %collective-permute-done.8.refs_12_), channel_id=1, source_target_pairs={{0,1},{1,0},{2,3},{3,2},{4,5},{5,4},{6,7},{7,6},{8,9},{9,8},{10,11... | collective-permute-start | bytes 4128776 | tf_op jit(solution)/shard_map/ppermute | solution.py:352
  125.1 16.5 %collective-permute-start.9 = (bf16[192,3584]{1,0:T(8,128)(2,1)}, bf16[192,3584]{1,0:T(8,128)(2,1)}, u32[]{:S(2)}, u32[]{:S(2)}) collective-permute-start(bf16[192,3584]{1,0:T(8,128)(2,1)} %bitcast.27.x_ref.refs_10_), channel_id=1, source_target_pairs={{0,1},{1,0},{2,3},{3,2},{4,5},{5,4},{6,7},{7,6},{8,9},{9,8},{10,11... | collective-permute-start | bytes 4128776 | tf_op jit(solution)/shard_map/ppermute | solution.py:352
  125.7 14.8 %collective-permute-start.12 = (bf16[2,192,512]{2,1,0:T(8,128)(2,1)S(1)}, bf16[2,192,512]{2,1,0:T(8,128)(2,1)S(1)}, u32[]{:S(2)}, u32[]{:S(2)}) collective-permute-start(bf16[2,192,512]{2,1,0:T(8,128)(2,1)S(1)} %slice.39), channel_id=1, source_target_pairs={{0,1},{1,0},{2,3},{3,2},{4,5},{5,4},{6,7},{7,6},{8,9},{9,8},{10,11... | collective-permute-start | bytes 1179656 | tf_op jit(solution)/shard_map/ppermute | solution.py:352
  125.8 14.7 %collective-permute-start.11 = (bf16[2,192,256]{2,1,0:T(8,128)(2,1)S(1)}, bf16[2,192,256]{2,1,0:T(8,128)(2,1)S(1)}, u32[]{:S(2)}, u32[]{:S(2)}) collective-permute-start(bf16[2,192,256]{2,1,0:T(8,128)(2,1)S(1)} %slice.38), channel_id=1, source_target_pairs={{0,1},{1,0},{2,3},{3,2},{4,5},{5,4},{6,7},{7,6},{8,9},{9,8},{10,11... | collective-permute-start | bytes 589832 | tf_op jit(solution)/shard_map/ppermute | solution.py:352
  141.8 23.7 %all-to-all-start.3 = ((bf16[4,48,3584]{2,1,0:T(8,128)(2,1)}), bf16[4,48,3584]{2,1,0:T(8,128)(2,1)S(1)}, u32[]{:S(2)}, u32[]{:S(2)}) async-start(bf16[4,48,3584]{2,1,0:T(8,128)(2,1)} %bitcast.101), calls=%async_computation.3 | async-start | bytes 2752512 | tf_op jit(solution)/shard_map/all_to_all | solution.py:370
  145.7 19.7 %collective-permute-start.13 = (bf16[192,3584]{1,0:T(8,128)(2,1)S(1)}, bf16[192,3584]{1,0:T(8,128)(2,1)}, u32[]{:S(2)}, u32[]{:S(2)}) collective-permute-start(bf16[192,3584]{1,0:T(8,128)(2,1)S(1)} %bitcast.90), channel_id=1, source_target_pairs={{0,1},{1,0},{2,3},{3,2},{4,5},{5,4},{6,7},{7,6},{8,9},{9,8},{10,11... | collective-permute-start | bytes 4128776 | tf_op jit(solution)/shard_map/ppermute | solution.py:352
  145.8 19.0 %collective-permute-start.14 = (bf16[2,192,256]{2,1,0:T(8,128)(2,1)S(1)}, bf16[2,192,256]{2,1,0:T(8,128)(2,1)S(1)}, u32[]{:S(2)}, u32[]{:S(2)}) collective-permute-start(bf16[2,192,256]{2,1,0:T(8,128)(2,1)S(1)} %slice.40), channel_id=1, source_target_pairs={{0,1},{1,0},{2,3},{3,2},{4,5},{5,4},{6,7},{7,6},{8,9},{9,8},{10,11... | collective-permute-start | bytes 589832 | tf_op jit(solution)/shard_map/ppermute | solution.py:352
  166.6 56.0 %all-to-all-start.4 = ((bf16[4,96,3584]{2,1,0:T(8,128)(2,1)}), bf16[4,96,3584]{2,1,0:T(8,128)(2,1)S(1)}, u32[]{:S(2)}, u32[]{:S(2)}) async-start(bf16[4,96,3584]{2,1,0:T(8,128)(2,1)} %bitcast.97), calls=%async_computation.4 | async-start | bytes 5505024 | tf_op jit(solution)/shard_map/all_to_all | solution.py:370
  170.7 49.7 %collective-permute-start.16 = (bf16[192,3584]{1,0:T(8,128)(2,1)}, bf16[192,3584]{1,0:T(8,128)(2,1)}, u32[]{:S(2)}, u32[]{:S(2)}) collective-permute-start(bf16[192,3584]{1,0:T(8,128)(2,1)} %bitcast.27.x_ref.refs_10_), channel_id=1, source_target_pairs={{0,16},{16,0},{1,17},{17,1},{2,18},{18,2},{3,19},{19,3},{4,20},{20... | collective-permute-start | bytes 4128776 | tf_op jit(solution)/shard_map/ppermute | solution.py:361
  175.1 45.3 %collective-permute-start.15 = (bf16[128,3584]{1,0:T(8,128)(2,1)}, bf16[128,3584]{1,0:T(8,128)(2,1)}, u32[]{:S(2)}, u32[]{:S(2)}) collective-permute-start(bf16[128,3584]{1,0:T(8,128)(2,1)} %convolution_convert_fusion.1), channel_id=1, source_target_pairs={{0,8},{1,9},{2,10},{3,11},{4,12},{5,13},{6,14},{7,15},{8,0},{9,1},... | collective-permute-start | bytes 2752520 | tf_op jit(solution)/shard_map/ppermute | solution.py:352
  177.7 3.3 %collective-permute-start.19 = (bf16[2,192,512]{2,1,0:T(8,128)(2,1)}, bf16[2,192,512]{2,1,0:T(8,128)(2,1)}, u32[]{:S(2)}, u32[]{:S(2)}) collective-permute-start(bf16[2,192,512]{2,1,0:T(8,128)(2,1)} %slice.41), channel_id=1, source_target_pairs={{0,1},{1,0},{2,3},{3,2},{4,5},{5,4},{6,7},{7,6},{8,9},{9,8},{10,11... | collective-permute-start | bytes 1179656 | tf_op jit(solution)/shard_map/ppermute | solution.py:352
  178.8 37.9 %collective-permute-start.17 = (bf16[2,192,512]{2,1,0:T(8,128)(2,1)S(1)}, bf16[2,192,512]{2,1,0:T(8,128)(2,1)S(1)}, u32[]{:S(2)}, u32[]{:S(2)}) collective-permute-start(bf16[2,192,512]{2,1,0:T(8,128)(2,1)S(1)} %pad_maximum_fusion), channel_id=1, source_target_pairs={{0,16},{16,0},{1,17},{17,1},{2,18},{18,2},{3,19},{19,3},{4,20},{20... | collective-permute-start | bytes 1179656 | tf_op jit(solution)/shard_map/ppermute | solution.py:361
  180.4 36.3 %collective-permute-start.18 = (bf16[192,512]{1,0:T(8,128)(2,1)S(1)}, bf16[192,512]{1,0:T(8,128)(2,1)S(1)}, u32[]{:S(2)}, u32[]{:S(2)}) collective-permute-start(bf16[192,512]{1,0:T(8,128)(2,1)S(1)} %dynamic-slice_bitcast_fusion.1), channel_id=1, source_target_pairs={{0,16},{16,0},{1,17},{17,1},{2,18},{18,2},{3,19},{19,3},{4,20},{20... | collective-permute-start | bytes 589832 | tf_op jit(solution)/shard_map/ppermute | solution.py:361
  181.9 37.7 %collective-permute-start.20 = (bf16[192,512]{1,0:T(8,128)(2,1)S(1)}, bf16[192,512]{1,0:T(8,128)(2,1)S(1)}, u32[]{:S(2)}, u32[]{:S(2)}) collective-permute-start(bf16[192,512]{1,0:T(8,128)(2,1)S(1)} %dynamic-slice_bitcast_fusion), channel_id=1, source_target_pairs={{0,16},{16,0},{1,17},{17,1},{2,18},{18,2},{3,19},{19,3},{4,20},{20... | collective-permute-start | bytes 589832 | tf_op jit(solution)/shard_map/ppermute | solution.py:361
  198.9 29.5 %copy-start.18 = (bf16[128,192]{0,1:T(8,128)(2,1)S(1)}, bf16[128,192]{0,1:T(8,128)(2,1)}, u32[]{:S(2)}) copy-start(bf16[128,192]{0,1:T(8,128)(2,1)} %get-tuple-element.150) | copy-start | bytes 147460
  222.5 41.2 %collective-permute-start.22 = (bf16[256,3584]{1,0:T(8,128)(2,1)}, bf16[256,3584]{1,0:T(8,128)(2,1)}, u32[]{:S(2)}, u32[]{:S(2)}) collective-permute-start(bf16[256,3584]{1,0:T(8,128)(2,1)} %shard_map.116), channel_id=1, source_target_pairs={{0,16},{16,0},{1,17},{17,1},{2,18},{18,2},{3,19},{19,3},{4,20},{20... | collective-permute-start | bytes 5505032 | tf_op jit(solution)/shard_map/ppermute | solution.py:361
  223.1 9.1 %collective-permute-start.23 = (bf16[192,3584]{1,0:T(8,128)(2,1)}, bf16[192,3584]{1,0:T(8,128)(2,1)}, u32[]{:S(2)}, u32[]{:S(2)}) collective-permute-start(bf16[192,3584]{1,0:T(8,128)(2,1)} %collective-permute-done.16.refs_14_), channel_id=1, source_target_pairs={{0,1},{1,0},{2,3},{3,2},{4,5},{5,4},{6,7},{7,6},{8,9},{9,8},{10,11... | collective-permute-start | bytes 4128776 | tf_op jit(solution)/shard_map/ppermute | solution.py:352
  223.1 43.8 %all-to-all-start.5 = ((bf16[4,48,3584]{2,1,0:T(8,128)(2,1)}), bf16[4,48,3584]{2,1,0:T(8,128)(2,1)}, u32[]{:S(2)}, u32[]{:S(2)}) async-start(bf16[4,48,3584]{2,1,0:T(8,128)(2,1)} %bitcast.100), calls=%async_computation.5 | async-start | bytes 2752512 | tf_op jit(solution)/shard_map/all_to_all | solution.py:370
  230.1 43.7 %collective-permute-start.21 = (bf16[128,3584]{1,0:T(8,128)(2,1)}, bf16[128,3584]{1,0:T(8,128)(2,1)}, u32[]{:S(2)}, u32[]{:S(2)}) collective-permute-start(bf16[128,3584]{1,0:T(8,128)(2,1)} %convolution_convert_fusion), channel_id=1, source_target_pairs={{0,8},{1,9},{2,10},{3,11},{4,12},{5,13},{6,14},{7,15},{8,0},{9,1},... | collective-permute-start | bytes 2752520 | tf_op jit(solution)/shard_map/ppermute | solution.py:352
  232.2 31.5 %copy-start.3 = (bf16[256,3584]{1,0:T(8,128)(2,1)S(1)}, bf16[256,3584]{1,0:T(8,128)(2,1)}, u32[]{:S(2)}) copy-start(bf16[256,3584]{1,0:T(8,128)(2,1)} %shard_map.117) | copy-start | bytes 5505028
  (30 other events, 198.4 us)

commit v15 on v14

--- a/solution.py
+++ b/solution.py
@@ -54,31 +54,46 @@
     return width // 2 if width % 256 == 0 else width
 
 
-def place_far(placing, parts, gain=None):
+def place_far(placing, parts, gain=None, beside=None, near=1):
     slots = placing.shape[0]
     width = parts[0].shape[1]
+    piece = slots // near
     tile = wide_tile(width)
-    fixed = [placing] if gain is None else [placing, gain]
-
-    def body(placing_ref, *refs):
-        part_refs, out_ref = refs[len(fixed) - 1 : -1], refs[-1]
+    fixed = [placing] + ([] if gain is None else [gain]) + ([] if beside is None else list(beside[:2]))
+    rows = list(parts) + ([] if beside is None else [beside[2]])
+
+    def body(*refs):
+        fixed_refs, row_refs, out_ref = refs[: len(fixed)], refs[len(fixed) : -1], refs[-1]
         for cut in chunks(tile):
-            rows = [ref[:, cut] for ref in part_refs]
-            rows = rows[0] if len(rows) == 1 else jnp.concatenate(rows, axis=0)
-            total = dot(placing_ref[...], rows, NN)
+            tokens = [ref[:, cut] for ref in row_refs[: len(parts)]]
+            tokens = tokens[0] if len(tokens) == 1 else jnp.concatenate(tokens, axis=0)
+            total = dot(fixed_refs[0][...], tokens, NN)
             if gain is not None:
-                total = total * refs[0][...]
-            out_ref[:, cut] = total.astype(BF16)
-
+                total = total * fixed_refs[1][...]
+            total = total.astype(BF16)
+            if beside is None:
+                out_ref[:, cut] = total
+            else:
+                second = dot(fixed_refs[-2][...], row_refs[-1][:, cut], NN) * fixed_refs[-1][...]
+                second = second.astype(BF16)
+                for n in range(near):
+                    here = slice(n * piece, (n + 1) * piece)
+                    out_ref[n, 0, :, cut] = total[here]
+                    out_ref[n, 1, :, cut] = second[here]
+
+    out_spec, out_shape = pl.BlockSpec((slots, tile), lambda n: (0, n)), (slots, width)
+    if beside is not None:
+        out_shape = (near, 2, piece, width)
+        out_spec = pl.BlockSpec((near, 2, piece, tile), lambda n: (0, 0, 0, n))
     return kernel_call(
         body,
         (width // tile,),
         [pl.BlockSpec(a.shape, lambda n: (0, 0)) for a in fixed]
-        + [pl.BlockSpec((a.shape[0], tile), lambda n: (0, n)) for a in parts],
-        pl.BlockSpec((slots, tile), lambda n: (0, n)),
-        jax.ShapeDtypeStruct((slots, width), BF16),
+        + [pl.BlockSpec((a.shape[0], tile), lambda n: (0, n)) for a in rows],
+        out_spec,
+        jax.ShapeDtypeStruct(out_shape, BF16),
         cost=HOP_COST,
-    )(*fixed, *parts)
+    )(*fixed, *rows)
 
 
 def combine_got(matrix, rows, got):
@@ -392,54 +407,52 @@
     far_acts_0 = far(acts[0, :first])
     meta = jnp.concatenate([expert_ids[0].astype(F32), route_weights[0]], axis=1)
     own_placing, own_back, own_weighting, own_gain = route(meta, half, chips, capacity)
-    both_placing = jnp.concatenate([of_set(own_placing.T, 0), of_set(own_placing.T, 1)], axis=0).T
-    both_gain = jnp.stack([jnp.ones_like(own_gain).reshape(near, piece), own_gain.reshape(near, piece)], axis=1)
-    own = place(
-        both_placing, jnp.concatenate([acts[0], grad_out[0]], axis=0), both_gain.reshape(2 * count, 1)
-    )
-    own, far_acts_0, acts_1, meta = tie(own, far_acts_0, acts[0, first:], meta)
+    own_in = place(own_placing, acts[0])
+    own_in, far_acts_0, acts_1, meta = tie(own_in, far_acts_0, acts[0, first:], meta)
 
     far_acts_1 = far(acts_1)
-    own = near_exchange(own).reshape(near, 2, piece, width)
-    own_in = own[:, 0].reshape(count, width)
+    own_in = near_exchange(own_in)
     far_meta = far(meta)
     other = [swap(weight) for weight in weights]
     far_placing, far_back, far_weighting, far_gain = route(far_meta, half, chips, capacity)
-    far_in = place_far(far_placing, [far_acts_0, far_acts_1])
-    far_in, own, own_in, far_placing, far_gain, grads, *weights = tie(
-        far_in, own, own_in, far_placing, far_gain, grad_out[0], *weights, *other
+    mixed = place_far(
+        far_placing, [far_acts_0, far_acts_1], None, (own_placing, own_gain, grad_out[0]), near
+    )
+    mixed, own_in, far_placing, far_gain, grads, *weights = tie(
+        mixed, own_in, far_placing, far_gain, grad_out[0], *weights, *other
     )
 
     far_grads = far(grads)
-    far_in = near_exchange(far_in)
-    own_b = swap(own)
+    mixed = near_exchange(mixed.reshape(2 * count, width)).reshape(mixed.shape)
+    own_in_b = swap(own_in)
     mirror_own = mirror(own_in)
-    own_pre_gate, own_pre_up, own_hidden, own_out = forward(count, (own, 0), weights)
-    own_units, own_input = backward(count, (own, 1), own_pre_gate, own_pre_up, weights)
-    far_grads, own_out, own_input = tie(far_grads, own_out, own_input)
+    own_pre_gate, own_pre_up, own_hidden, own_out = forward(count, own_in, weights)
+    far_pre_gate, far_pre_up, far_hidden, far_out = forward(count, (mixed, 0), weights)
+    far_grads, own_out, far_out = tie(far_grads, own_out, far_out)
     far_grad = place_far(far_placing, [far_grads], far_gain)
-    far_grad, far_in, own_b, mirror_own, own_out, own_input, own_hidden, own_units = tie(
-        far_grad, far_in, own_b, mirror_own, own_out, own_input, own_hidden, own_units
+    far_grad, mixed, own_in_b, mirror_own, own_out, far_out, own_hidden, far_hidden = tie(
+        far_grad, mixed, own_in_b, mirror_own, own_out, far_out, own_hidden, far_hidden
     )
 
     far_grad = near_exchange(far_grad)
-    far_in_b = swap(far_in)
+    mixed_b = swap(mixed)
     mirror_own_b = swap(mirror_own)
     own_hidden_b = swap(own_hidden[2:])
+    far_hidden_b = swap(far_hidden[2:])
+    far_in = mixed[:, 0].reshape(count, width)
+    own_units, own_input = backward(count, (mixed, 1), own_pre_gate, own_pre_up, weights)
+    far_grad, far_out, mixed_b, mirror_own_b, own_hidden_b, far_hidden_b, far_in, own_units, own_input = tie(
+        far_grad, far_out, mixed_b, mirror_own_b, own_hidden_b, far_hidden_b, far_in, own_units, own_input
+    )
+
+    far_out = near_exchange(far_out)
     own_units_b = swap(own_units[2:])
-    far_pre_gate, far_pre_up, far_hidden, far_out = forward(count, far_in, weights)
-    far_grad, far_out, far_in_b, mirror_own_b, own_hidden_b, own_units_b, far_hidden = tie(
-        far_grad, far_out, far_in_b, mirror_own_b, own_hidden_b, own_units_b, far_hidden
-    )
-
-    far_out = near_exchange(far_out)
     far_grad_b = swap(far_grad)
-    far_hidden_b = swap(far_hidden[2:])
     far_units, inputs = backward(
         count, far_grad, far_pre_gate, far_pre_up, weights, own_input, near
     )
-    far_out, far_units, inputs, far_grad_b, far_hidden_b, mirror_far, own_units, own_units_b = tie(
-        far_out, far_units, inputs, far_grad_b, far_hidden_b, far_in, own_units, own_units_b
+    far_out, far_units, inputs, far_grad_b, mirror_far, own_units, own_units_b = tie(
+        far_out, far_units, inputs, far_grad_b, far_in, own_units, own_units_b
     )
 
     got_out = far(combine(far_weighting, far_out).astype(BF16))
@@ -452,7 +465,7 @@
         *[mirror(for_mirror(units)) for units in all_units[2:]],
     ]
     hiddens = (own_hidden, own_hidden_b, far_hidden, far_hidden_b)
-    rows_grad = ((own, 1), (own_b.reshape(own.shape), 1), far_grad, far_grad_b)
+    rows_grad = ((mixed, 1), (mixed_b, 1), far_grad, far_grad_b)
     send_down = down_grad(count, 1 - kept, hiddens, rows_grad)
     keep_down = down_grad(count, kept, hiddens, rows_grad)
     got_out, back, mirror_far, send_down, keep_down, own_out, *mirror_units = tie(
@@ -467,7 +480,7 @@
         count,
         kept,
         all_units,
-        ((own, 0), (own_b.reshape(own.shape), 0), far_in, far_in_b),
+        (own_in, own_in_b, (mixed, 0), (mixed_b, 0)),
         [mirror_units[0][0], mirror_units[0][1], *mirror_units[1:]],
         (mirror_own, mirror_own_b, mirror_far, mirror_far_b),
     )

time: 279 us -> 295 us (1.057)
  waiting for transfers between devices: 84.3 us -> 112 us
  local copies, waits for them, and re-layouts: 20.8 us -> 15.8 us
  other arithmetic: 14.9 us -> 10 us
    all_to_all x6, waiting for transfers between devices: 2.12 us -> 34.1 us  [near_exchange(): lax.all_to_all(rows.reshape(near, -1, width), 'expert', split_axis=0, con...]
    ppermute x18, waiting for transfers between devices: 42.7 us -> 38.4 us  [hop(): lax.ppermute(rows, 'expert', [(i, i ^ distance) for i in range(devices)])]
  transfers between devices with their start and end apart: 30 -> 30, of which waited for: 9 -> 9; matrix products, arithmetic and copies ran while one was open for 14% -> 10% of each run, Pallas kernels for 35% -> 33%
where the time goes in v15:
time: 295 us; the launch traced here: 293 us
  waiting for transfers between devices  112 us (38%)
  Pallas kernels  100 us (34%)
  starting transfers between devices  45.8 us (16%)
  local copies, waits for them, and re-layouts  15.8 us (5%)
  other arithmetic  10 us (3%)
  matrix products  8.65 us (3%)
    ppermute x6, waiting for transfers between devices, mirror(): lax.ppermute(rows, 'pipe', [(p, rank_count - 1 - p) for p in range(rank_c...  39.2 us
    ppermute x18, waiting for transfers between devices, hop(): lax.ppermute(rows, 'expert', [(i, i ^ distance) for i in range(devices)])  38.4 us
    pallas_call x2, Pallas kernels, backward(): kernel_call(body, (4,), [row_spec(rows_grad, width), units, units] + weig...  35.6 us
    all_to_all x6, waiting for transfers between devices, near_exchange(): lax.all_to_all(rows.reshape(near, -1, width), 'expert', split_axis=0, con...  34.1 us
    pallas_call x2, Pallas kernels, forward(): kernel_call(body, (4,), [row_spec(rows, width)] + weight_specs(width, hal...  27.4 us
    all_to_all x6, starting transfers between devices, near_exchange(): lax.all_to_all(rows.reshape(near, -1, width), 'expert', split_axis=0, con...  24.6 us
    pallas_call x2, Pallas kernels, down_grad(): kernel_call(body, (width // tile,), [pl.BlockSpec((1, count, half_units),...  15.4 us
    ppermute x18, starting transfers between devices, hop(): lax.ppermute(rows, 'expert', [(i, i ^ distance) for i in range(devices)])  13.9 us
  transfers between devices with their start and end apart: 30, of which 9 were waited for; matrix products, arithmetic and copies ran while one was open for 10% of the time, Pallas kernels for 33%

profile of v15, /device:TPU:0, one launch (start us, length us, event | category | flops | bytes accessed | tf_op | source)
XLA Modules:
  0.0 293.3 jit_solution(7099585482490522031)
XLA Ops:
  1.6 4.0 %collective-permute-start = (bf16[16,3584]{1,0:T(8,128)(2,1)S(1)}, bf16[16,3584]{1,0:T(8,128)(2,1)S(1)}, u32[]{:S(2)}, u32[]{:S(2)}) collective-permute-start(bf16[16,3584]{1,0:T(8,128)(2,1)S(1)} %slice_bitcast_fusion.3), channel_id=1, source_target_pairs={{0,8},{1,9},{2,10},{3,11},{4,12},{5,13},{6,14},{7,15},{8,0},{9,1},... | collective-permute-start | bytes 344072 | tf_op jit(solution)/shard_map/ppermute | solution.py:367
  12.3 3.8 %all-to-all-start = ((bf16[4,48,3584]{2,1,0:T(8,128)(2,1)}), bf16[4,48,3584]{2,1,0:T(8,128)(2,1)S(1)}, u32[]{:S(2)}, u32[]{:S(2)}) async-start(bf16[4,48,3584]{2,1,0:T(8,128)(2,1)} %bitcast.12), calls=%async_computation | async-start | bytes 2752512 | tf_op jit(solution)/shard_map/all_to_all | solution.py:385
  19.8 12.4 %collective-permute-done.1 = f32[128,4]{0,1:T(4,128)S(1)} collective-permute-done((f32[128,4]{0,1:T(4,128)S(1)}, f32[128,4]{0,1:T(4,128)S(1)}, u32[]{:S(2)}, u32[]{:S(2)}) %collective-permute-start.1) | collective-permute-done | bytes 2080 | tf_op jit(solution)/shard_map/ppermute | solution.py:367
  33.9 22.0 %collective-permute-done.2.refs_4_ = bf16[112,3584]{1,0:T(8,128)(2,1)S(1)} collective-permute-done((bf16[112,3584]{1,0:T(8,128)(2,1)S(1)}, bf16[112,3584]{1,0:T(8,128)(2,1)S(1)}, u32[]{:S(2)}, u32[]{:S(2)}) %collective-permute-start.2) | collective-permute-done | bytes 802848 | tf_op jit(solution)/shard_map/ppermute | solution.py:367
  56.7 3.5 %shard_map.110 = bf16[4,2,48,3584]{3,2,1,0:T(8,128)(2,1)} custom-call(bf16[192,128]{1,0:T(8,128)(2,1)} %get-tuple-element.79.refs_0_, bf16[192,128]{1,0:T(8,128)(2,1)} %copy-done.14, f32[192,1]{1,0:T(8,128)} %copy.51.refs_2_, bf16[16,3584]{1,0:T(8,128)(2,1)} %copy-done.20, bf16[112,3584]{1,0:T(8,128)(2,1)} %copy-done.12, bf16[128,3584]{1,0:T(8,128)(2,1)} %bitcast.97), custom_call_target="tpu_custom_call" | custom-call | flops 1 | bytes 22000000 | tf_op jit(solution)/shard_map/pallas_call | solution.py:88
  61.4 3.7 %all-to-all-start.1 = ((bf16[4,96,3584]{2,1,0:T(8,128)(2,1)}), bf16[4,96,3584]{2,1,0:T(8,128)(2,1)S(1)}, u32[]{:S(2)}, u32[]{:S(2)}) async-start(bf16[4,96,3584]{2,1,0:T(8,128)(2,1)} %bitcast.90), calls=%async_computation.1 | async-start | bytes 5505024 | tf_op jit(solution)/shard_map/all_to_all | solution.py:385
  66.7 2.0 collective-permute-start.6
  68.7 14.2 %shard_map.111 = (f32[4,192,256]{2,1,0:T(8,128)}, f32[4,192,256]{2,1,0:T(8,128)}, bf16[4,192,256]{2,1,0:T(8,128)(2,1)}, bf16[192,3584]{1,0:T(8,128)(2,1)}) custom-call(bf16[192,3584]{1,0:T(8,128)(2,1)} %bitcast.88, bf16[3584,512]{1,0:T(8,128)(2,1)} %bitcast.70, bf16[3584,512]{1,0:T(8,128)(2,1)} %bitcast.75, bf16[512,3584]{1,0:T(8,128)(2,1)} %bitcast.80, ...), custom_call_target="tpu_custom_call" | custom-call | flops 1 | bytes 1 | tf_op jit(solution)/shard_map/pallas_call | solution.py:195
  83.6 32.0 %all-to-all-done.1 = bf16[4,96,3584]{2,1,0:T(8,128)(2,1)S(1)} async-done(((bf16[4,96,3584]{2,1,0:T(8,128)(2,1)}), bf16[4,96,3584]{2,1,0:T(8,128)(2,1)S(1)}, u32[]{:S(2)}, u32[]{:S(2)}) %all-to-all-start.1) | async-done | bytes 2752544 | tf_op jit(solution)/shard_map/all_to_all | solution.py:385
  115.6 1.6 copy-done
  117.2 13.3 %shard_map.112 = (f32[4,192,256]{2,1,0:T(8,128)}, f32[4,192,256]{2,1,0:T(8,128)}, bf16[4,192,256]{2,1,0:T(8,128)(2,1)}, bf16[192,3584]{1,0:T(8,128)(2,1)}) custom-call(bf16[4,2,48,3584]{3,2,1,0:T(8,128)(2,1)} %bitcast.62, bf16[3584,512]{1,0:T(8,128)(2,1)} %bitcast.71, bf16[3584,512]{1,0:T(8,128)(2,1)} %bitcast.76, bf16[512,3584]{1,0:T(8,128)(2,1)} %bitcast.81, ...), custom_call_target="tpu_custom_call" | custom-call | flops 1 | bytes 1 | tf_op jit(solution)/shard_map/pallas_call | solution.py:195
  130.5 2.6 shard_map.113
  133.2 4.6 %all-to-all-start.2 = ((bf16[4,48,3584]{2,1,0:T(8,128)(2,1)}), bf16[4,48,3584]{2,1,0:T(8,128)(2,1)}, u32[]{:S(2)}, u32[]{:S(2)}) async-start(bf16[4,48,3584]{2,1,0:T(8,128)(2,1)} %bitcast.92), calls=%async_computation.2 | async-start | bytes 2752512 | tf_op jit(solution)/shard_map/all_to_all | solution.py:385
  138.9 17.1 %shard_map.114 = (bf16[4,192,512]{2,1,0:T(8,128)(2,1)}, bf16[192,3584]{1,0:T(8,128)(2,1)}) custom-call(bf16[4,2,48,3584]{3,2,1,0:T(8,128)(2,1)} %bitcast.64, f32[4,192,256]{2,1,0:T(8,128)} %get-tuple-element.103.pre_gate_ref, f32[4,192,256]{2,1,0:T(8,128)} %get-tuple-element.104.pre_up_ref, bf16[3584,512]{1,0:T(8,128)(2,1)} %bitcast.72, ...), custom_call_target="tpu_custom_call" | custom-call | flops 1 | bytes 1 | tf_op jit(solution)/shard_map/pallas_call | solution.py:253
  157.3 3.8 %all-to-all-start.3 = ((bf16[4,48,3584]{2,1,0:T(8,128)(2,1)}), bf16[4,48,3584]{2,1,0:T(8,128)(2,1)S(1)}, u32[]{:S(2)}, u32[]{:S(2)}) async-start(bf16[4,48,3584]{2,1,0:T(8,128)(2,1)} %bitcast.24), calls=%async_computation.3 | async-start | bytes 2752512 | tf_op jit(solution)/shard_map/all_to_all | solution.py:385
  161.6 18.5 %shard_map.115 = (bf16[4,192,512]{2,1,0:T(8,128)(2,1)}, bf16[4,2,48,3584]{3,2,1,0:T(8,128)(2,1)}) custom-call(bf16[192,3584]{1,0:T(8,128)(2,1)} %bitcast.22.x_ref.refs_6_, f32[4,192,256]{2,1,0:T(8,128)} %get-tuple-element.109.pre_gate_ref, f32[4,192,256]{2,1,0:T(8,128)} %get-tuple-element.110.pre_up_ref, bf16[3584,512]{1,0:T(8,128)(2,1)} %bitcast.73, ...), custom_call_target="tpu_custom_call" | custom-call | flops 1 | bytes 1 | tf_op jit(solution)/shard_map/pallas_call | solution.py:253
  182.0 4.2 %all-to-all-start.4 = ((bf16[4,96,3584]{2,1,0:T(8,128)(2,1)}), bf16[4,96,3584]{2,1,0:T(8,128)(2,1)S(1)}, u32[]{:S(2)}, u32[]{:S(2)}) async-start(bf16[4,96,3584]{2,1,0:T(8,128)(2,1)} %bitcast.93), calls=%async_computation.4 | async-start | bytes 5505024 | tf_op jit(solution)/shard_map/all_to_all | solution.py:385
  188.3 3.2 %convolution_convert_fusion.2 = bf16[128,3584]{1,0:T(8,128)(2,1)} fusion(f32[128,192]{0,1:T(8,128)S(1)} %get-tuple-element.151, bf16[192,3584]{1,0:T(8,128)(2,1)} %bitcast.91), kind=kOutput, calls=%fused_computation.2 | convolution fusion | flops 1057423360 | bytes 2392064 | tf_op jit(solution)/shard_map/dot_general | solution.py:126
  198.3 7.7 %shard_map.117 = bf16[256,3584]{1,0:T(8,128)(2,1)} custom-call(s32[1]{0:T(128)} %bitcast.28.which_ref, bf16[4,192,256]{2,1,0:T(8,128)(2,1)} %get-tuple-element.101.refs_0_, bf16[2,192,256]{2,1,0:T(8,128)(2,1)} %copy-done.13, bf16[4,192,256]{2,1,0:T(8,128)(2,1)} %get-tuple-element.102.refs_2_, bf16[2,192,256]{2,1,0:T(8,128)(2,1)} %collective-permute-done.12.refs_3_, ...), custom_call_target="tpu_custom_call" | custom-call | flops 1 | bytes 1 | tf_op jit(solution)/shard_map/pallas_call | solution.py:290
  206.1 7.7 %shard_map.116 = bf16[256,3584]{1,0:T(8,128)(2,1)} custom-call(s32[1]{0:T(128)S(6)} %sub.38.which_ref, bf16[4,192,256]{2,1,0:T(8,128)(2,1)} %get-tuple-element.101.refs_0_, bf16[2,192,256]{2,1,0:T(8,128)(2,1)} %copy-done.13, bf16[4,192,256]{2,1,0:T(8,128)(2,1)} %get-tuple-element.102.refs_2_, bf16[2,192,256]{2,1,0:T(8,128)(2,1)} %collective-permute-done.12.refs_3_, ...), custom_call_target="tpu_custom_call" | custom-call | flops 1 | bytes 1 | tf_op jit(solution)/shard_map/pallas_call | solution.py:290
  213.8 18.3 %collective-permute-done.18.refs_6_ = bf16[192,512]{1,0:T(8,128)(2,1)S(1)} collective-permute-done((bf16[192,512]{1,0:T(8,128)(2,1)S(1)}, bf16[192,512]{1,0:T(8,128)(2,1)S(1)}, u32[]{:S(2)}, u32[]{:S(2)}) %collective-permute-start.18) | collective-permute-done | bytes 196640 | tf_op jit(solution)/shard_map/ppermute | solution.py:376
  232.1 3.0 %collective-permute-done.20.refs_7_ = bf16[192,512]{1,0:T(8,128)(2,1)S(1)} collective-permute-done((bf16[192,512]{1,0:T(8,128)(2,1)S(1)}, bf16[192,512]{1,0:T(8,128)(2,1)S(1)}, u32[]{:S(2)}, u32[]{:S(2)}) %collective-permute-start.20) | collective-permute-done | bytes 196640 | tf_op jit(solution)/shard_map/ppermute | solution.py:376
  235.8 2.1 all-to-all-done.4
  239.4 4.5 %all-to-all-start.5 = ((bf16[4,48,3584]{2,1,0:T(8,128)(2,1)}), bf16[4,48,3584]{2,1,0:T(8,128)(2,1)}, u32[]{:S(2)}, u32[]{:S(2)}) async-start(bf16[4,48,3584]{2,1,0:T(8,128)(2,1)} %bitcast.95), calls=%async_computation.5 | async-start | bytes 2752512 | tf_op jit(solution)/shard_map/all_to_all | solution.py:385
  244.8 1.6 convolution_convert_fusion.1
  248.5 12.6 %shard_map.118 = (bf16[3584,256]{1,0:T(8,128)(2,1)}, bf16[3584,256]{1,0:T(8,128)(2,1)}) custom-call(s32[1]{0:T(128)} %bitcast.28.which_ref, bf16[4,192,512]{2,1,0:T(8,128)(2,1)} %get-tuple-element.124.refs_0_, bf16[2,192,512]{2,1,0:T(8,128)(2,1)} %copy-done.11, bf16[4,192,512]{2,1,0:T(8,128)(2,1)} %get-tuple-element.126.refs_2_, ...), custom_call_target="tpu_custom_call" | custom-call | flops 1 | bytes 1 | tf_op jit(solution)/shard_map/pallas_call | solution.py:323
  261.2 17.9 %collective-permute-done.22 = bf16[256,3584]{1,0:T(8,128)(2,1)} collective-permute-done((bf16[256,3584]{1,0:T(8,128)(2,1)}, bf16[256,3584]{1,0:T(8,128)(2,1)}, u32[]{:S(2)}, u32[]{:S(2)}) %collective-permute-start.22) | collective-permute-done | bytes 1835040 | tf_op jit(solution)/shard_map/ppermute | solution.py:376
  279.1 3.2 %add_convert_fusion = bf16[256,3584]{1,0:T(8,128)(2,1)} fusion(bf16[256,3584]{1,0:T(8,128)(2,1)} %collective-permute-done.22, bf16[256,3584]{1,0:T(8,128)(2,1)S(1)} %copy-done.4), kind=kLoop, calls=%fused_computation.3 | loop fusion | flops 3670016 | bytes 5505024 | tf_op jit(solution)/shard_map/convert_element_type | solution.py:488
  282.2 2.3 fusion.3
  284.5 2.3 add_convert_fusion.1
  286.9 3.2 %collective-permute-done.21.got_ref = bf16[128,3584]{1,0:T(8,128)(2,1)} collective-permute-done((bf16[128,3584]{1,0:T(8,128)(2,1)}, bf16[128,3584]{1,0:T(8,128)(2,1)}, u32[]{:S(2)}, u32[]{:S(2)}) %collective-permute-start.21) | collective-permute-done | bytes 917536 | tf_op jit(solution)/shard_map/ppermute | solution.py:367
  290.1 3.2 %shard_map.119 = bf16[128,3584]{1,0:T(8,128)(2,1)} custom-call(bf16[128,384]{1,0:T(8,128)(2,1)} %copy.53.matrix_ref, bf16[384,3584]{1,0:T(8,128)(2,1)} %bitcast.85, bf16[128,3584]{1,0:T(8,128)(2,1)} %collective-permute-done.21.got_ref), custom_call_target="tpu_custom_call" | custom-call | flops 1 | bytes 22000000 | tf_op jit(solution)/shard_map/pallas_call | solution.py:109
  (130 shorter events, 36.2 us)
Async XLA Ops:
  1.6 10.6 %collective-permute-start = (bf16[16,3584]{1,0:T(8,128)(2,1)S(1)}, bf16[16,3584]{1,0:T(8,128)(2,1)S(1)}, u32[]{:S(2)}, u32[]{:S(2)}) collective-permute-start(bf16[16,3584]{1,0:T(8,128)(2,1)S(1)} %slice_bitcast_fusion.3), channel_id=1, source_target_pairs={{0,8},{1,9},{2,10},{3,11},{4,12},{5,13},{6,14},{7,15},{8,0},{9,1},... | collective-permute-start | bytes 344072 | tf_op jit(solution)/shard_map/ppermute | solution.py:367
  5.7 54.6 %collective-permute-start.3 = (bf16[3584,512]{1,0:T(8,128)(2,1)}, bf16[3584,512]{1,0:T(8,128)(2,1)}, u32[]{:S(2)}, u32[]{:S(2)}) collective-permute-start(bf16[3584,512]{1,0:T(8,128)(2,1)} %bitcast.69), channel_id=1, source_target_pairs={{0,1},{1,0},{2,3},{3,2},{4,5},{5,4},{6,7},{7,6},{8,9},{9,8},{10,11... | collective-permute-start | bytes 11010056 | tf_op jit(solution)/shard_map/ppermute | solution.py:367
  5.7 54.6 %collective-permute-start.4 = (bf16[3584,512]{1,0:T(8,128)(2,1)}, bf16[3584,512]{1,0:T(8,128)(2,1)}, u32[]{:S(2)}, u32[]{:S(2)}) collective-permute-start(bf16[3584,512]{1,0:T(8,128)(2,1)} %bitcast.74), channel_id=1, source_target_pairs={{0,1},{1,0},{2,3},{3,2},{4,5},{5,4},{6,7},{7,6},{8,9},{9,8},{10,11... | collective-permute-start | bytes 11010056 | tf_op jit(solution)/shard_map/ppermute | solution.py:367
  6.2 54.1 %collective-permute-start.5 = (bf16[512,3584]{1,0:T(8,128)(2,1)}, bf16[512,3584]{1,0:T(8,128)(2,1)}, u32[]{:S(2)}, u32[]{:S(2)}) collective-permute-start(bf16[512,3584]{1,0:T(8,128)(2,1)} %bitcast.79), channel_id=1, source_target_pairs={{0,1},{1,0},{2,3},{3,2},{4,5},{5,4},{6,7},{7,6},{8,9},{9,8},{10,11... | collective-permute-start | bytes 11010056 | tf_op jit(solution)/shard_map/ppermute | solution.py:367
  12.3 47.9 %all-to-all-start = ((bf16[4,48,3584]{2,1,0:T(8,128)(2,1)}), bf16[4,48,3584]{2,1,0:T(8,128)(2,1)S(1)}, u32[]{:S(2)}, u32[]{:S(2)}) async-start(bf16[4,48,3584]{2,1,0:T(8,128)(2,1)} %bitcast.12), calls=%async_computation | async-start | bytes 2752512 | tf_op jit(solution)/shard_map/all_to_all | solution.py:385
  16.1 16.1 %collective-permute-start.1 = (f32[128,4]{0,1:T(4,128)S(1)}, f32[128,4]{0,1:T(4,128)S(1)}, u32[]{:S(2)}, u32[]{:S(2)}) collective-permute-start(f32[128,4]{0,1:T(4,128)S(1)} %pad_maximum_fusion.1), channel_id=1, source_target_pairs={{0,8},{1,9},{2,10},{3,11},{4,12},{5,13},{6,14},{7,15},{8,0},{9,1},... | collective-permute-start | bytes 6152 | tf_op jit(solution)/shard_map/ppermute | solution.py:367
  18.4 37.4 %collective-permute-start.2 = (bf16[112,3584]{1,0:T(8,128)(2,1)S(1)}, bf16[112,3584]{1,0:T(8,128)(2,1)S(1)}, u32[]{:S(2)}, u32[]{:S(2)}) collective-permute-start(bf16[112,3584]{1,0:T(8,128)(2,1)S(1)} %slice_bitcast_fusion), channel_id=1, source_target_pairs={{0,8},{1,9},{2,10},{3,11},{4,12},{5,13},{6,14},{7,15},{8,0},{9,1},... | collective-permute-start | bytes 2408456 | tf_op jit(solution)/shard_map/ppermute | solution.py:367
  61.4 54.2 %all-to-all-start.1 = ((bf16[4,96,3584]{2,1,0:T(8,128)(2,1)}), bf16[4,96,3584]{2,1,0:T(8,128)(2,1)S(1)}, u32[]{:S(2)}, u32[]{:S(2)}) async-start(bf16[4,96,3584]{2,1,0:T(8,128)(2,1)} %bitcast.90), calls=%async_computation.1 | async-start | bytes 5505024 | tf_op jit(solution)/shard_map/all_to_all | solution.py:385
  65.0 68.0 %collective-permute-start.7 = (bf16[192,3584]{1,0:T(8,128)(2,1)}, bf16[192,3584]{1,0:T(8,128)(2,1)}, u32[]{:S(2)}, u32[]{:S(2)}) collective-permute-start(bf16[192,3584]{1,0:T(8,128)(2,1)} %bitcast.86), channel_id=1, source_target_pairs={{0,1},{1,0},{2,3},{3,2},{4,5},{5,4},{6,7},{7,6},{8,9},{9,8},{10,11... | collective-permute-start | bytes 4128776 | tf_op jit(solution)/shard_map/ppermute | solution.py:367
  65.1 68.0 %collective-permute-start.8 = (bf16[192,3584]{1,0:T(8,128)(2,1)}, bf16[192,3584]{1,0:T(8,128)(2,1)}, u32[]{:S(2)}, u32[]{:S(2)}) collective-permute-start(bf16[192,3584]{1,0:T(8,128)(2,1)} %bitcast.87), channel_id=1, source_target_pairs={{0,16},{16,0},{1,17},{17,1},{2,18},{18,2},{3,19},{19,3},{4,20},{20... | collective-permute-start | bytes 4128776 | tf_op jit(solution)/shard_map/ppermute | solution.py:376
  66.7 63.8 %collective-permute-start.6 = (bf16[128,3584]{1,0:T(8,128)(2,1)}, bf16[128,3584]{1,0:T(8,128)(2,1)}, u32[]{:S(2)}, u32[]{:S(2)}) collective-permute-start(bf16[128,3584]{1,0:T(8,128)(2,1)} %bitcast.98), channel_id=1, source_target_pairs={{0,8},{1,9},{2,10},{3,11},{4,12},{5,13},{6,14},{7,15},{8,0},{9,1},... | collective-permute-start | bytes 2752520 | tf_op jit(solution)/shard_map/ppermute | solution.py:367
  133.1 24.2 %collective-permute-start.9 = (bf16[4,2,48,3584]{3,2,1,0:T(8,128)(2,1)}, bf16[4,2,48,3584]{3,2,1,0:T(8,128)(2,1)}, u32[]{:S(2)}, u32[]{:S(2)}) collective-permute-start(bf16[4,2,48,3584]{3,2,1,0:T(8,128)(2,1)} %bitcast.63), channel_id=1, source_target_pairs={{0,1},{1,0},{2,3},{3,2},{4,5},{5,4},{6,7},{7,6},{8,9},{9,8},{10,11... | collective-permute-start | bytes 8257544 | tf_op jit(solution)/shard_map/ppermute | solution.py:367
  133.2 24.1 %all-to-all-start.2 = ((bf16[4,48,3584]{2,1,0:T(8,128)(2,1)}), bf16[4,48,3584]{2,1,0:T(8,128)(2,1)}, u32[]{:S(2)}, u32[]{:S(2)}) async-start(bf16[4,48,3584]{2,1,0:T(8,128)(2,1)} %bitcast.92), calls=%async_computation.2 | async-start | bytes 2752512 | tf_op jit(solution)/shard_map/all_to_all | solution.py:385
  137.8 19.4 %collective-permute-start.10 = (bf16[192,3584]{1,0:T(8,128)(2,1)}, bf16[192,3584]{1,0:T(8,128)(2,1)}, u32[]{:S(2)}, u32[]{:S(2)}) collective-permute-start(bf16[192,3584]{1,0:T(8,128)(2,1)} %collective-permute-done.8.refs_12_), channel_id=1, source_target_pairs={{0,1},{1,0},{2,3},{3,2},{4,5},{5,4},{6,7},{7,6},{8,9},{9,8},{10,11... | collective-permute-start | bytes 4128776 | tf_op jit(solution)/shard_map/ppermute | solution.py:367
  138.2 19.0 %collective-permute-start.11 = (bf16[2,192,256]{2,1,0:T(8,128)(2,1)S(1)}, bf16[2,192,256]{2,1,0:T(8,128)(2,1)S(1)}, u32[]{:S(2)}, u32[]{:S(2)}) collective-permute-start(bf16[2,192,256]{2,1,0:T(8,128)(2,1)S(1)} %slice.37), channel_id=1, source_target_pairs={{0,1},{1,0},{2,3},{3,2},{4,5},{5,4},{6,7},{7,6},{8,9},{9,8},{10,11... | collective-permute-start | bytes 589832 | tf_op jit(solution)/shard_map/ppermute | solution.py:367
  138.5 18.7 %collective-permute-start.12 = (bf16[2,192,256]{2,1,0:T(8,128)(2,1)S(1)}, bf16[2,192,256]{2,1,0:T(8,128)(2,1)}, u32[]{:S(2)}, u32[]{:S(2)}) collective-permute-start(bf16[2,192,256]{2,1,0:T(8,128)(2,1)S(1)} %slice.38), channel_id=1, source_target_pairs={{0,1},{1,0},{2,3},{3,2},{4,5},{5,4},{6,7},{7,6},{8,9},{9,8},{10,11... | collective-permute-start | bytes 589832 | tf_op jit(solution)/shard_map/ppermute | solution.py:367
  157.3 23.6 %all-to-all-start.3 = ((bf16[4,48,3584]{2,1,0:T(8,128)(2,1)}), bf16[4,48,3584]{2,1,0:T(8,128)(2,1)S(1)}, u32[]{:S(2)}, u32[]{:S(2)}) async-start(bf16[4,48,3584]{2,1,0:T(8,128)(2,1)} %bitcast.24), calls=%async_computation.3 | async-start | bytes 2752512 | tf_op jit(solution)/shard_map/all_to_all | solution.py:385
  161.0 19.8 %collective-permute-start.13 = (bf16[192,3584]{1,0:T(8,128)(2,1)}, bf16[192,3584]{1,0:T(8,128)(2,1)}, u32[]{:S(2)}, u32[]{:S(2)}) collective-permute-start(bf16[192,3584]{1,0:T(8,128)(2,1)} %bitcast.22.x_ref.refs_6_), channel_id=1, source_target_pairs={{0,1},{1,0},{2,3},{3,2},{4,5},{5,4},{6,7},{7,6},{8,9},{9,8},{10,11... | collective-permute-start | bytes 4128776 | tf_op jit(solution)/shard_map/ppermute | solution.py:367
  161.2 18.9 %collective-permute-start.14 = (bf16[2,192,512]{2,1,0:T(8,128)(2,1)S(1)}, bf16[2,192,512]{2,1,0:T(8,128)(2,1)S(1)}, u32[]{:S(2)}, u32[]{:S(2)}) collective-permute-start(bf16[2,192,512]{2,1,0:T(8,128)(2,1)S(1)} %slice.40), channel_id=1, source_target_pairs={{0,1},{1,0},{2,3},{3,2},{4,5},{5,4},{6,7},{7,6},{8,9},{9,8},{10,11... | collective-permute-start | bytes 1179656 | tf_op jit(solution)/shard_map/ppermute | solution.py:367
  182.0 56.0 %all-to-all-start.4 = ((bf16[4,96,3584]{2,1,0:T(8,128)(2,1)}), bf16[4,96,3584]{2,1,0:T(8,128)(2,1)S(1)}, u32[]{:S(2)}, u32[]{:S(2)}) async-start(bf16[4,96,3584]{2,1,0:T(8,128)(2,1)} %bitcast.93), calls=%async_computation.4 | async-start | bytes 5505024 | tf_op jit(solution)/shard_map/all_to_all | solution.py:385
  186.2 49.7 %collective-permute-start.16 = (bf16[192,3584]{1,0:T(8,128)(2,1)}, bf16[192,3584]{1,0:T(8,128)(2,1)}, u32[]{:S(2)}, u32[]{:S(2)}) collective-permute-start(bf16[192,3584]{1,0:T(8,128)(2,1)} %bitcast.96), channel_id=1, source_target_pairs={{0,16},{16,0},{1,17},{17,1},{2,18},{18,2},{3,19},{19,3},{4,20},{20... | collective-permute-start | bytes 4128776 | tf_op jit(solution)/shard_map/ppermute | solution.py:376
  191.5 44.3 %collective-permute-start.15 = (bf16[128,3584]{1,0:T(8,128)(2,1)}, bf16[128,3584]{1,0:T(8,128)(2,1)}, u32[]{:S(2)}, u32[]{:S(2)}) collective-permute-start(bf16[128,3584]{1,0:T(8,128)(2,1)} %convolution_convert_fusion.2), channel_id=1, source_target_pairs={{0,8},{1,9},{2,10},{3,11},{4,12},{5,13},{6,14},{7,15},{8,0},{9,1},... | collective-permute-start | bytes 2752520 | tf_op jit(solution)/shard_map/ppermute | solution.py:367
  193.5 3.3 %collective-permute-start.19 = (bf16[2,192,512]{2,1,0:T(8,128)(2,1)}, bf16[2,192,512]{2,1,0:T(8,128)(2,1)}, u32[]{:S(2)}, u32[]{:S(2)}) collective-permute-start(bf16[2,192,512]{2,1,0:T(8,128)(2,1)} %slice.41), channel_id=1, source_target_pairs={{0,1},{1,0},{2,3},{3,2},{4,5},{5,4},{6,7},{7,6},{8,9},{9,8},{10,11... | collective-permute-start | bytes 1179656 | tf_op jit(solution)/shard_map/ppermute | solution.py:367
  194.6 37.5 %collective-permute-start.17 = (bf16[2,192,512]{2,1,0:T(8,128)(2,1)S(1)}, bf16[2,192,512]{2,1,0:T(8,128)(2,1)S(1)}, u32[]{:S(2)}, u32[]{:S(2)}) collective-permute-start(bf16[2,192,512]{2,1,0:T(8,128)(2,1)S(1)} %pad_maximum_fusion), channel_id=1, source_target_pairs={{0,16},{16,0},{1,17},{17,1},{2,18},{18,2},{3,19},{19,3},{4,20},{20... | collective-permute-start | bytes 1179656 | tf_op jit(solution)/shard_map/ppermute | solution.py:376
  195.2 36.9 %collective-permute-start.18 = (bf16[192,512]{1,0:T(8,128)(2,1)S(1)}, bf16[192,512]{1,0:T(8,128)(2,1)S(1)}, u32[]{:S(2)}, u32[]{:S(2)}) collective-permute-start(bf16[192,512]{1,0:T(8,128)(2,1)S(1)} %dynamic-slice_bitcast_fusion.1), channel_id=1, source_target_pairs={{0,16},{16,0},{1,17},{17,1},{2,18},{18,2},{3,19},{19,3},{4,20},{20... | collective-permute-start | bytes 589832 | tf_op jit(solution)/shard_map/ppermute | solution.py:376
  197.7 37.3 %collective-permute-start.20 = (bf16[192,512]{1,0:T(8,128)(2,1)S(1)}, bf16[192,512]{1,0:T(8,128)(2,1)S(1)}, u32[]{:S(2)}, u32[]{:S(2)}) collective-permute-start(bf16[192,512]{1,0:T(8,128)(2,1)S(1)} %dynamic-slice_bitcast_fusion), channel_id=1, source_target_pairs={{0,16},{16,0},{1,17},{17,1},{2,18},{18,2},{3,19},{19,3},{4,20},{20... | collective-permute-start | bytes 589832 | tf_op jit(solution)/shard_map/ppermute | solution.py:376
  213.8 31.0 %copy-start.19 = (bf16[128,192]{0,1:T(8,128)(2,1)S(1)}, bf16[128,192]{0,1:T(8,128)(2,1)}, u32[]{:S(2)}) copy-start(bf16[128,192]{0,1:T(8,128)(2,1)} %get-tuple-element.152) | copy-start | bytes 147460
  237.9 41.2 %collective-permute-start.22 = (bf16[256,3584]{1,0:T(8,128)(2,1)}, bf16[256,3584]{1,0:T(8,128)(2,1)}, u32[]{:S(2)}, u32[]{:S(2)}) collective-permute-start(bf16[256,3584]{1,0:T(8,128)(2,1)} %shard_map.116), channel_id=1, source_target_pairs={{0,16},{16,0},{1,17},{17,1},{2,18},{18,2},{3,19},{19,3},{4,20},{20... | collective-permute-start | bytes 5505032 | tf_op jit(solution)/shard_map/ppermute | solution.py:376
  239.4 9.1 %collective-permute-start.23 = (bf16[192,3584]{1,0:T(8,128)(2,1)}, bf16[192,3584]{1,0:T(8,128)(2,1)}, u32[]{:S(2)}, u32[]{:S(2)}) collective-permute-start(bf16[192,3584]{1,0:T(8,128)(2,1)} %collective-permute-done.16.refs_14_), channel_id=1, source_target_pairs={{0,1},{1,0},{2,3},{3,2},{4,5},{5,4},{6,7},{7,6},{8,9},{9,8},{10,11... | collective-permute-start | bytes 4128776 | tf_op jit(solution)/shard_map/ppermute | solution.py:367
  239.4 42.8 %all-to-all-start.5 = ((bf16[4,48,3584]{2,1,0:T(8,128)(2,1)}), bf16[4,48,3584]{2,1,0:T(8,128)(2,1)}, u32[]{:S(2)}, u32[]{:S(2)}) async-start(bf16[4,48,3584]{2,1,0:T(8,128)(2,1)} %bitcast.95), calls=%async_computation.5 | async-start | bytes 2752512 | tf_op jit(solution)/shard_map/all_to_all | solution.py:385
  246.4 43.7 %collective-permute-start.21 = (bf16[128,3584]{1,0:T(8,128)(2,1)}, bf16[128,3584]{1,0:T(8,128)(2,1)}, u32[]{:S(2)}, u32[]{:S(2)}) collective-permute-start(bf16[128,3584]{1,0:T(8,128)(2,1)} %convolution_convert_fusion.1), channel_id=1, source_target_pairs={{0,8},{1,9},{2,10},{3,11},{4,12},{5,13},{6,14},{7,15},{8,0},{9,1},... | collective-permute-start | bytes 2752520 | tf_op jit(solution)/shard_map/ppermute | solution.py:367
  248.5 30.5 %copy-start.4 = (bf16[256,3584]{1,0:T(8,128)(2,1)S(1)}, bf16[256,3584]{1,0:T(8,128)(2,1)}, u32[]{:S(2)}) copy-start(bf16[256,3584]{1,0:T(8,128)(2,1)} %shard_map.117) | copy-start | bytes 5505028
  (20 other events, 146.8 us)

commit v16 on v14

--- a/solution.py
+++ b/solution.py
@@ -79,30 +79,6 @@
         jax.ShapeDtypeStruct((slots, width), BF16),
         cost=HOP_COST,
     )(*fixed, *parts)
-
-
-def combine_got(matrix, rows, got):
-    tokens, slots = matrix.shape
-    width = rows.shape[1]
-    tile = wide_tile(width)
-
-    def body(matrix_ref, rows_ref, got_ref, out_ref):
-        for cut in chunks(tile):
-            total = dot(matrix_ref[...], rows_ref[:, cut], NN)
-            out_ref[:, cut] = (total + got_ref[:, cut].astype(F32)).astype(BF16)
-
-    return kernel_call(
-        body,
-        (width // tile,),
-        [
-            pl.BlockSpec((tokens, slots), lambda n: (0, 0)),
-            pl.BlockSpec((slots, tile), lambda n: (0, n)),
-            pl.BlockSpec((tokens, tile), lambda n: (0, n)),
-        ],
-        pl.BlockSpec((tokens, tile), lambda n: (0, n)),
-        jax.ShapeDtypeStruct((tokens, width), BF16),
-        cost=HOP_COST,
-    )(matrix, rows, got)
 
 
 def combine(matrix, rows):
@@ -416,7 +392,15 @@
     mirror_own = mirror(own_in)
     own_pre_gate, own_pre_up, own_hidden, own_out = forward(count, (own, 0), weights)
     own_units, own_input = backward(count, (own, 1), own_pre_gate, own_pre_up, weights)
-    far_grads, own_out, own_input = tie(far_grads, own_out, own_input)
+    far_grads, own_out, own_input, far_weighting, own_weighting, far_mix, own_mix = tie(
+        far_grads,
+        own_out,
+        own_input,
+        far_weighting,
+        own_weighting,
+        of_set(far_back, 0),
+        of_set(own_back, 1),
+    )
     far_grad = place_far(far_placing, [far_grads], far_gain)
     far_grad, far_in, own_b, mirror_own, own_out, own_input, own_hidden, own_units = tie(
         far_grad, far_in, own_b, mirror_own, own_out, own_input, own_hidden, own_units
@@ -459,7 +443,7 @@
         got_out, back, mirror_far, send_down, keep_down, own_out, *mirror_units
     )
 
-    got_input = far(combine(of_set(far_back, 0), back).astype(BF16))
+    got_input = far(combine(far_mix, back).astype(BF16))
     own_out = near_exchange(own_out)
     got_down = mirror(send_down)
     mirror_far_b = swap(mirror_far)
@@ -473,10 +457,11 @@
     )
     out_acts = (combine(own_weighting, own_out) + got_out.astype(F32)).astype(BF16)
     grad_down = (keep_down.astype(F32) + got_down.astype(F32)).astype(BF16)
-    got_input, grad_down, grad_gate, grad_up, out_acts = tie(
-        got_input, grad_down, grad_gate, grad_up, out_acts
-    )
-    grad_acts = combine_got(of_set(own_back, 1), back, got_input)
+    own_part = combine(own_mix, back)
+    got_input, grad_down, grad_gate, grad_up, out_acts, own_part = tie(
+        got_input, grad_down, grad_gate, grad_up, out_acts, own_part
+    )
+    grad_acts = (own_part + got_input.astype(F32)).astype(BF16)
     return out_acts[None], grad_acts[None], grad_gate[None], grad_up[None], grad_down[None]
 
 

time: 279 us -> 277 us (level)
  matrix products: 9.58 us -> 12.9 us
  Pallas kernels: 99.3 us -> 96.1 us
  waiting for transfers between devices: 84.3 us -> 81.3 us
    pallas_call x1 -> x0, Pallas kernels: 3.19 us -> none  [combine_got(): kernel_call(body, (width // tile,), [pl.BlockSpec((tokens, slots), lambda...]
    dot_general x2 -> x3, matrix products: 4.1 us -> 6.01 us  [dot(): return lax.dot_general(a, b, (dims, ((), ())), preferred_element_type=F32)]
  transfers between devices with their start and end apart: 30 -> 30, of which waited for: 9 -> 9; matrix products, arithmetic and copies ran while one was open for 14% -> 15% of each run, Pallas kernels for 35% -> 35%
where the time goes in v16:
time: 277 us; the launch traced here: 275 us
  Pallas kernels  96.1 us (35%)
  waiting for transfers between devices  81.3 us (29%)
  starting transfers between devices  46.9 us (17%)
  local copies, waits for them, and re-layouts  21.4 us (8%)
  other arithmetic  15.5 us (6%)
  matrix products  12.9 us (5%)
    ppermute x18, waiting for transfers between devices, hop(): lax.ppermute(rows, 'expert', [(i, i ^ distance) for i in range(devices)])  40.1 us
    ppermute x6, waiting for transfers between devices, mirror(): lax.ppermute(rows, 'pipe', [(p, rank_count - 1 - p) for p in range(rank_c...  39.1 us
    pallas_call x2, Pallas kernels, backward(): kernel_call(body, (4,), [row_spec(rows_grad, width), units, units] + weig...  35.4 us
    pallas_call x2, Pallas kernels, forward(): kernel_call(body, (4,), [row_spec(rows, width)] + weight_specs(width, hal...  27.4 us
    all_to_all x6, starting transfers between devices, near_exchange(): lax.all_to_all(rows.reshape(near, -1, width), 'expert', split_axis=0, con...  26.9 us
    pallas_call x2, Pallas kernels, down_grad(): kernel_call(body, (width // tile,), [pl.BlockSpec((1, count, half_units),...  15.4 us
    ppermute x18, starting transfers between devices, hop(): lax.ppermute(rows, 'expert', [(i, i ^ distance) for i in range(devices)])  13.7 us
    pallas_call x1, Pallas kernels, gate_up_grad(): kernel_call(body, (width // tile,), [pl.BlockSpec((1, count, both), lambd...  12.6 us
  transfers between devices with their start and end apart: 30, of which 9 were waited for; matrix products, arithmetic and copies ran while one was open for 15% of the time, Pallas kernels for 35%

profile of v16, /device:TPU:0, one launch (start us, length us, event | category | flops | bytes accessed | tf_op | source)
XLA Modules:
  0.0 275.2 jit_solution(6995574692385174797)
XLA Ops:
  1.7 4.0 %collective-permute-start = (bf16[16,3584]{1,0:T(8,128)(2,1)S(1)}, bf16[16,3584]{1,0:T(8,128)(2,1)S(1)}, u32[]{:S(2)}, u32[]{:S(2)}) collective-permute-start(bf16[16,3584]{1,0:T(8,128)(2,1)S(1)} %slice_bitcast_fusion.3), channel_id=1, source_target_pairs={{0,8},{1,9},{2,10},{3,11},{4,12},{5,13},{6,14},{7,15},{8,0},{9,1},... | collective-permute-start | bytes 344072 | tf_op jit(solution)/shard_map/ppermute | solution.py:328
  9.0 2.5 fusion
  12.7 3.8 %all-to-all-start = ((bf16[4,96,3584]{2,1,0:T(8,128)(2,1)}), bf16[4,96,3584]{2,1,0:T(8,128)(2,1)S(1)}, u32[]{:S(2)}, u32[]{:S(2)}) async-start(bf16[4,96,3584]{2,1,0:T(8,128)(2,1)} %bitcast.101), calls=%async_computation | async-start | bytes 5505024 | tf_op jit(solution)/shard_map/all_to_all | solution.py:346
  17.0 1.8 collective-permute-start.1
  19.9 27.5 %collective-permute-done.1 = f32[128,4]{0,1:T(4,128)S(1)} collective-permute-done((f32[128,4]{0,1:T(4,128)}, f32[128,4]{0,1:T(4,128)S(1)}, u32[]{:S(2)}, u32[]{:S(2)}) %collective-permute-start.1) | collective-permute-done | bytes 2080 | tf_op jit(solution)/shard_map/ppermute | solution.py:328
  61.4 1.9 collective-permute-done.2.refs_1_
  63.3 2.6 shard_map.110
  68.0 6.6 %all-to-all-start.1 = ((bf16[4,48,3584]{2,1,0:T(8,128)(2,1)}), bf16[4,48,3584]{2,1,0:T(8,128)(2,1)}, u32[]{:S(2)}, u32[]{:S(2)}) async-start(bf16[4,48,3584]{2,1,0:T(8,128)(2,1)} %bitcast.97), calls=%async_computation.1 | async-start | bytes 2752512 | tf_op jit(solution)/shard_map/all_to_all | solution.py:346
  80.0 13.3 %shard_map.111 = (f32[4,192,256]{2,1,0:T(8,128)}, f32[4,192,256]{2,1,0:T(8,128)}, bf16[4,192,256]{2,1,0:T(8,128)(2,1)}, bf16[192,3584]{1,0:T(8,128)(2,1)}) custom-call(bf16[4,2,48,3584]{3,2,1,0:T(8,128)(2,1)} %bitcast.71, bf16[3584,512]{1,0:T(8,128)(2,1)} %bitcast.77, bf16[3584,512]{1,0:T(8,128)(2,1)} %bitcast.82, bf16[512,3584]{1,0:T(8,128)(2,1)} %bitcast.87, ...), custom_call_target="tpu_custom_call" | custom-call | flops 1 | bytes 1 | tf_op jit(solution)/shard_map/pallas_call | solution.py:156
  93.3 17.0 %shard_map.112 = (bf16[4,192,512]{2,1,0:T(8,128)(2,1)}, bf16[192,3584]{1,0:T(8,128)(2,1)}) custom-call(bf16[4,2,48,3584]{3,2,1,0:T(8,128)(2,1)} %bitcast.72, f32[4,192,256]{2,1,0:T(8,128)} %get-tuple-element.93.pre_gate_ref, f32[4,192,256]{2,1,0:T(8,128)} %get-tuple-element.94.pre_up_ref, bf16[3584,512]{1,0:T(8,128)(2,1)} %bitcast.78, ...), custom_call_target="tpu_custom_call" | custom-call | flops 1 | bytes 1 | tf_op jit(solution)/shard_map/pallas_call | solution.py:214
  111.1 7.5 %collective-permute-done.6.refs_1_ = bf16[128,3584]{1,0:T(8,128)(2,1)} collective-permute-done((bf16[128,3584]{1,0:T(8,128)(2,1)}, bf16[128,3584]{1,0:T(8,128)(2,1)}, u32[]{:S(2)}, u32[]{:S(2)}) %collective-permute-start.6) | collective-permute-done | bytes 917536 | tf_op jit(solution)/shard_map/ppermute | solution.py:328
  118.6 2.6 shard_map.113
  121.2 3.9 %all-to-all-start.2 = ((bf16[4,48,3584]{2,1,0:T(8,128)(2,1)}), bf16[4,48,3584]{2,1,0:T(8,128)(2,1)S(1)}, u32[]{:S(2)}, u32[]{:S(2)}) async-start(bf16[4,48,3584]{2,1,0:T(8,128)(2,1)} %bitcast.98), calls=%async_computation.2 | async-start | bytes 2752512 | tf_op jit(solution)/shard_map/all_to_all | solution.py:346
  126.4 14.1 %shard_map.114 = (f32[4,192,256]{2,1,0:T(8,128)}, f32[4,192,256]{2,1,0:T(8,128)}, bf16[4,192,256]{2,1,0:T(8,128)(2,1)}, bf16[192,3584]{1,0:T(8,128)(2,1)}) custom-call(bf16[192,3584]{1,0:T(8,128)(2,1)} %bitcast.29.x_ref.refs_10_, bf16[3584,512]{1,0:T(8,128)(2,1)} %bitcast.79, bf16[3584,512]{1,0:T(8,128)(2,1)} %bitcast.84, bf16[512,3584]{1,0:T(8,128)(2,1)} %bitcast.89, ...), custom_call_target="tpu_custom_call" | custom-call | flops 1 | bytes 1 | tf_op jit(solution)/shard_map/pallas_call | solution.py:156
  141.8 3.9 %all-to-all-start.3 = ((bf16[4,48,3584]{2,1,0:T(8,128)(2,1)}), bf16[4,48,3584]{2,1,0:T(8,128)(2,1)S(1)}, u32[]{:S(2)}, u32[]{:S(2)}) async-start(bf16[4,48,3584]{2,1,0:T(8,128)(2,1)} %bitcast.105), calls=%async_computation.3 | async-start | bytes 2752512 | tf_op jit(solution)/shard_map/all_to_all | solution.py:346
  146.3 18.4 %shard_map.115 = (bf16[4,192,512]{2,1,0:T(8,128)(2,1)}, bf16[4,2,48,3584]{3,2,1,0:T(8,128)(2,1)}) custom-call(bf16[192,3584]{1,0:T(8,128)(2,1)} %bitcast.94, f32[4,192,256]{2,1,0:T(8,128)} %get-tuple-element.116.pre_gate_ref, f32[4,192,256]{2,1,0:T(8,128)} %get-tuple-element.117.pre_up_ref, bf16[3584,512]{1,0:T(8,128)(2,1)} %bitcast.80, ...), custom_call_target="tpu_custom_call" | custom-call | flops 1 | bytes 1 | tf_op jit(solution)/shard_map/pallas_call | solution.py:214
  166.5 4.2 %all-to-all-start.4 = ((bf16[4,96,3584]{2,1,0:T(8,128)(2,1)}), bf16[4,96,3584]{2,1,0:T(8,128)(2,1)S(1)}, u32[]{:S(2)}, u32[]{:S(2)}) async-start(bf16[4,96,3584]{2,1,0:T(8,128)(2,1)} %bitcast.100), calls=%async_computation.4 | async-start | bytes 5505024 | tf_op jit(solution)/shard_map/all_to_all | solution.py:346
  171.3 3.2 %convolution_convert_fusion.1 = bf16[128,3584]{1,0:T(8,128)(2,1)} fusion(f32[128,192]{0,1:T(8,128)} %get-tuple-element.97, bf16[192,3584]{1,0:T(8,128)(2,1)} %bitcast.99), kind=kOutput, calls=%fused_computation.5 | convolution fusion | flops 1057423360 | bytes 2392064 | tf_op jit(solution)/shard_map/dot_general | solution.py:87
  174.5 1.8 collective-permute-start.15
  182.9 7.7 %shard_map.117 = bf16[256,3584]{1,0:T(8,128)(2,1)} custom-call(s32[1]{0:T(128)} %bitcast.36.which_ref, bf16[4,192,256]{2,1,0:T(8,128)(2,1)} %get-tuple-element.111.refs_0_, bf16[2,192,256]{2,1,0:T(8,128)(2,1)} %copy-done.12, bf16[4,192,256]{2,1,0:T(8,128)(2,1)} %get-tuple-element.121.refs_2_, bf16[2,192,256]{2,1,0:T(8,128)(2,1)} %copy-done.13, ...), custom_call_target="tpu_custom_call" | custom-call | flops 1 | bytes 1 | tf_op jit(solution)/shard_map/pallas_call | solution.py:251
  190.6 7.7 %shard_map.116 = bf16[256,3584]{1,0:T(8,128)(2,1)} custom-call(s32[1]{0:T(128)S(6)} %sub.38.which_ref, bf16[4,192,256]{2,1,0:T(8,128)(2,1)} %get-tuple-element.111.refs_0_, bf16[2,192,256]{2,1,0:T(8,128)(2,1)} %copy-done.12, bf16[4,192,256]{2,1,0:T(8,128)(2,1)} %get-tuple-element.121.refs_2_, bf16[2,192,256]{2,1,0:T(8,128)(2,1)} %copy-done.13, ...), custom_call_target="tpu_custom_call" | custom-call | flops 1 | bytes 1 | tf_op jit(solution)/shard_map/pallas_call | solution.py:251
  198.3 18.4 %collective-permute-done.18.refs_6_ = bf16[192,512]{1,0:T(8,128)(2,1)S(1)} collective-permute-done((bf16[192,512]{1,0:T(8,128)(2,1)S(1)}, bf16[192,512]{1,0:T(8,128)(2,1)S(1)}, u32[]{:S(2)}, u32[]{:S(2)}) %collective-permute-start.18) | collective-permute-done | bytes 196640 | tf_op jit(solution)/shard_map/ppermute | solution.py:337
  216.7 3.0 %collective-permute-done.20.refs_7_ = bf16[192,512]{1,0:T(8,128)(2,1)S(1)} collective-permute-done((bf16[192,512]{1,0:T(8,128)(2,1)S(1)}, bf16[192,512]{1,0:T(8,128)(2,1)S(1)}, u32[]{:S(2)}, u32[]{:S(2)}) %collective-permute-start.20) | collective-permute-done | bytes 196640 | tf_op jit(solution)/shard_map/ppermute | solution.py:337
  220.4 2.1 all-to-all-done.4
  223.1 4.5 %all-to-all-start.5 = ((bf16[4,48,3584]{2,1,0:T(8,128)(2,1)}), bf16[4,48,3584]{2,1,0:T(8,128)(2,1)}, u32[]{:S(2)}, u32[]{:S(2)}) async-start(bf16[4,48,3584]{2,1,0:T(8,128)(2,1)} %bitcast.103), calls=%async_computation.5 | async-start | bytes 2752512 | tf_op jit(solution)/shard_map/all_to_all | solution.py:346
  231.3 1.9 fusion.14
  233.3 12.6 %shard_map.118 = (bf16[3584,256]{1,0:T(8,128)(2,1)}, bf16[3584,256]{1,0:T(8,128)(2,1)}) custom-call(s32[1]{0:T(128)} %bitcast.36.which_ref, bf16[4,192,512]{2,1,0:T(8,128)(2,1)} %get-tuple-element.131.refs_0_, bf16[2,192,512]{2,1,0:T(8,128)(2,1)} %copy-done.11, bf16[4,192,512]{2,1,0:T(8,128)(2,1)} %get-tuple-element.133.refs_2_, ...), custom_call_target="tpu_custom_call" | custom-call | flops 1 | bytes 1 | tf_op jit(solution)/shard_map/pallas_call | solution.py:284
  245.9 17.8 %collective-permute-done.22 = bf16[256,3584]{1,0:T(8,128)(2,1)} collective-permute-done((bf16[256,3584]{1,0:T(8,128)(2,1)}, bf16[256,3584]{1,0:T(8,128)(2,1)}, u32[]{:S(2)}, u32[]{:S(2)}) %collective-permute-start.22) | collective-permute-done | bytes 1835040 | tf_op jit(solution)/shard_map/ppermute | solution.py:337
  263.7 3.2 %add_convert_fusion = bf16[256,3584]{1,0:T(8,128)(2,1)} fusion(bf16[256,3584]{1,0:T(8,128)(2,1)} %collective-permute-done.22, bf16[256,3584]{1,0:T(8,128)(2,1)S(1)} %copy-done.3), kind=kLoop, calls=%fused_computation.6 | loop fusion | flops 3670016 | bytes 5505024 | tf_op jit(solution)/shard_map/convert_element_type | solution.py:459
  266.9 3.6 %fusion.1 = bf16[128,3584]{1,0:T(8,128)(2,1)} fusion(f32[128,192]{0,1:T(8,128)S(1)} %copy-done.14, bf16[192,3584]{1,0:T(8,128)(2,1)} %bitcast.42, bf16[128,3584]{1,0:T(8,128)(2,1)} %collective-permute-done.15), kind=kOutput, calls=%fused_computation.3 | convolution fusion | flops 1058340864 | bytes 3309568 | tf_op jit(solution)/shard_map/dot_general | solution.py:87
  270.5 2.4 collective-permute-done.21
  272.9 2.3 fusion.5
  (156 shorter events, 46.2 us)
Async XLA Ops:
  1.7 10.3 %collective-permute-start = (bf16[16,3584]{1,0:T(8,128)(2,1)S(1)}, bf16[16,3584]{1,0:T(8,128)(2,1)S(1)}, u32[]{:S(2)}, u32[]{:S(2)}) collective-permute-start(bf16[16,3584]{1,0:T(8,128)(2,1)S(1)} %slice_bitcast_fusion.3), channel_id=1, source_target_pairs={{0,8},{1,9},{2,10},{3,11},{4,12},{5,13},{6,14},{7,15},{8,0},{9,1},... | collective-permute-start | bytes 344072 | tf_op jit(solution)/shard_map/ppermute | solution.py:328
  12.7 53.2 %all-to-all-start = ((bf16[4,96,3584]{2,1,0:T(8,128)(2,1)}), bf16[4,96,3584]{2,1,0:T(8,128)(2,1)S(1)}, u32[]{:S(2)}, u32[]{:S(2)}) async-start(bf16[4,96,3584]{2,1,0:T(8,128)(2,1)} %bitcast.101), calls=%async_computation | async-start | bytes 5505024 | tf_op jit(solution)/shard_map/all_to_all | solution.py:346
  16.5 50.7 %collective-permute-start.3 = (bf16[3584,512]{1,0:T(8,128)(2,1)}, bf16[3584,512]{1,0:T(8,128)(2,1)}, u32[]{:S(2)}, u32[]{:S(2)}) collective-permute-start(bf16[3584,512]{1,0:T(8,128)(2,1)} %bitcast.76), channel_id=1, source_target_pairs={{0,1},{1,0},{2,3},{3,2},{4,5},{5,4},{6,7},{7,6},{8,9},{9,8},{10,11... | collective-permute-start | bytes 11010056 | tf_op jit(solution)/shard_map/ppermute | solution.py:328
  16.5 50.7 %collective-permute-start.4 = (bf16[3584,512]{1,0:T(8,128)(2,1)}, bf16[3584,512]{1,0:T(8,128)(2,1)}, u32[]{:S(2)}, u32[]{:S(2)}) collective-permute-start(bf16[3584,512]{1,0:T(8,128)(2,1)} %bitcast.81), channel_id=1, source_target_pairs={{0,1},{1,0},{2,3},{3,2},{4,5},{5,4},{6,7},{7,6},{8,9},{9,8},{10,11... | collective-permute-start | bytes 11010056 | tf_op jit(solution)/shard_map/ppermute | solution.py:328
  17.0 50.2 %collective-permute-start.5 = (bf16[512,3584]{1,0:T(8,128)(2,1)}, bf16[512,3584]{1,0:T(8,128)(2,1)}, u32[]{:S(2)}, u32[]{:S(2)}) collective-permute-start(bf16[512,3584]{1,0:T(8,128)(2,1)} %bitcast.86), channel_id=1, source_target_pairs={{0,1},{1,0},{2,3},{3,2},{4,5},{5,4},{6,7},{7,6},{8,9},{9,8},{10,11... | collective-permute-start | bytes 11010056 | tf_op jit(solution)/shard_map/ppermute | solution.py:328
  17.0 30.4 %collective-permute-start.1 = (f32[128,4]{0,1:T(4,128)}, f32[128,4]{0,1:T(4,128)S(1)}, u32[]{:S(2)}, u32[]{:S(2)}) collective-permute-start(f32[128,4]{0,1:T(4,128)} %pad_maximum_fusion.1), channel_id=1, source_target_pairs={{0,8},{1,9},{2,10},{3,11},{4,12},{5,13},{6,14},{7,15},{8,0},{9,1},... | collective-permute-start | bytes 6152 | tf_op jit(solution)/shard_map/ppermute | solution.py:328
  18.8 44.4 %collective-permute-start.2 = (bf16[112,3584]{1,0:T(8,128)(2,1)S(1)}, bf16[112,3584]{1,0:T(8,128)(2,1)}, u32[]{:S(2)}, u32[]{:S(2)}) collective-permute-start(bf16[112,3584]{1,0:T(8,128)(2,1)S(1)} %slice_bitcast_fusion), channel_id=1, source_target_pairs={{0,8},{1,9},{2,10},{3,11},{4,12},{5,13},{6,14},{7,15},{8,0},{9,1},... | collective-permute-start | bytes 2408456 | tf_op jit(solution)/shard_map/ppermute | solution.py:328
  67.3 53.9 %collective-permute-start.7 = (bf16[4,2,48,3584]{3,2,1,0:T(8,128)(2,1)S(1)}, bf16[4,2,48,3584]{3,2,1,0:T(8,128)(2,1)}, u32[]{:S(2)}, u32[]{:S(2)}) collective-permute-start(bf16[4,2,48,3584]{3,2,1,0:T(8,128)(2,1)S(1)} %bitcast.70), channel_id=1, source_target_pairs={{0,1},{1,0},{2,3},{3,2},{4,5},{5,4},{6,7},{7,6},{8,9},{9,8},{10,11... | collective-permute-start | bytes 8257544 | tf_op jit(solution)/shard_map/ppermute | solution.py:328
  68.0 53.2 %all-to-all-start.1 = ((bf16[4,48,3584]{2,1,0:T(8,128)(2,1)}), bf16[4,48,3584]{2,1,0:T(8,128)(2,1)}, u32[]{:S(2)}, u32[]{:S(2)}) async-start(bf16[4,48,3584]{2,1,0:T(8,128)(2,1)} %bitcast.97), calls=%async_computation.1 | async-start | bytes 2752512 | tf_op jit(solution)/shard_map/all_to_all | solution.py:346
  74.6 46.5 %collective-permute-start.8 = (bf16[192,3584]{1,0:T(8,128)(2,1)}, bf16[192,3584]{1,0:T(8,128)(2,1)}, u32[]{:S(2)}, u32[]{:S(2)}) collective-permute-start(bf16[192,3584]{1,0:T(8,128)(2,1)} %bitcast.104), channel_id=1, source_target_pairs={{0,16},{16,0},{1,17},{17,1},{2,18},{18,2},{3,19},{19,3},{4,20},{20... | collective-permute-start | bytes 4128776 | tf_op jit(solution)/shard_map/ppermute | solution.py:337
  76.1 42.5 %collective-permute-start.6 = (bf16[128,3584]{1,0:T(8,128)(2,1)}, bf16[128,3584]{1,0:T(8,128)(2,1)}, u32[]{:S(2)}, u32[]{:S(2)}) collective-permute-start(bf16[128,3584]{1,0:T(8,128)(2,1)} %bitcast.123), channel_id=1, source_target_pairs={{0,8},{1,9},{2,10},{3,11},{4,12},{5,13},{6,14},{7,15},{8,0},{9,1},... | collective-permute-start | bytes 2752520 | tf_op jit(solution)/shard_map/ppermute | solution.py:328
  121.2 20.5 %all-to-all-start.2 = ((bf16[4,48,3584]{2,1,0:T(8,128)(2,1)}), bf16[4,48,3584]{2,1,0:T(8,128)(2,1)S(1)}, u32[]{:S(2)}, u32[]{:S(2)}) async-start(bf16[4,48,3584]{2,1,0:T(8,128)(2,1)} %bitcast.98), calls=%async_computation.2 | async-start | bytes 2752512 | tf_op jit(solution)/shard_map/all_to_all | solution.py:346
  125.1 15.5 %collective-permute-start.10 = (bf16[192,3584]{1,0:T(8,128)(2,1)}, bf16[192,3584]{1,0:T(8,128)(2,1)S(1)}, u32[]{:S(2)}, u32[]{:S(2)}) collective-permute-start(bf16[192,3584]{1,0:T(8,128)(2,1)} %collective-permute-done.8.refs_12_), channel_id=1, source_target_pairs={{0,1},{1,0},{2,3},{3,2},{4,5},{5,4},{6,7},{7,6},{8,9},{9,8},{10,11... | collective-permute-start | bytes 4128776 | tf_op jit(solution)/shard_map/ppermute | solution.py:328
  125.2 16.5 %collective-permute-start.9 = (bf16[192,3584]{1,0:T(8,128)(2,1)}, bf16[192,3584]{1,0:T(8,128)(2,1)}, u32[]{:S(2)}, u32[]{:S(2)}) collective-permute-start(bf16[192,3584]{1,0:T(8,128)(2,1)} %bitcast.29.x_ref.refs_10_), channel_id=1, source_target_pairs={{0,1},{1,0},{2,3},{3,2},{4,5},{5,4},{6,7},{7,6},{8,9},{9,8},{10,11... | collective-permute-start | bytes 4128776 | tf_op jit(solution)/shard_map/ppermute | solution.py:328
  125.7 14.8 %collective-permute-start.12 = (bf16[2,192,512]{2,1,0:T(8,128)(2,1)S(1)}, bf16[2,192,512]{2,1,0:T(8,128)(2,1)S(1)}, u32[]{:S(2)}, u32[]{:S(2)}) collective-permute-start(bf16[2,192,512]{2,1,0:T(8,128)(2,1)S(1)} %slice.39), channel_id=1, source_target_pairs={{0,1},{1,0},{2,3},{3,2},{4,5},{5,4},{6,7},{7,6},{8,9},{9,8},{10,11... | collective-permute-start | bytes 1179656 | tf_op jit(solution)/shard_map/ppermute | solution.py:328
  125.9 14.7 %collective-permute-start.11 = (bf16[2,192,256]{2,1,0:T(8,128)(2,1)S(1)}, bf16[2,192,256]{2,1,0:T(8,128)(2,1)S(1)}, u32[]{:S(2)}, u32[]{:S(2)}) collective-permute-start(bf16[2,192,256]{2,1,0:T(8,128)(2,1)S(1)} %slice.38), channel_id=1, source_target_pairs={{0,1},{1,0},{2,3},{3,2},{4,5},{5,4},{6,7},{7,6},{8,9},{9,8},{10,11... | collective-permute-start | bytes 589832 | tf_op jit(solution)/shard_map/ppermute | solution.py:328
  141.8 23.6 %all-to-all-start.3 = ((bf16[4,48,3584]{2,1,0:T(8,128)(2,1)}), bf16[4,48,3584]{2,1,0:T(8,128)(2,1)S(1)}, u32[]{:S(2)}, u32[]{:S(2)}) async-start(bf16[4,48,3584]{2,1,0:T(8,128)(2,1)} %bitcast.105), calls=%async_computation.3 | async-start | bytes 2752512 | tf_op jit(solution)/shard_map/all_to_all | solution.py:346
  145.7 19.7 %collective-permute-start.13 = (bf16[192,3584]{1,0:T(8,128)(2,1)S(1)}, bf16[192,3584]{1,0:T(8,128)(2,1)}, u32[]{:S(2)}, u32[]{:S(2)}) collective-permute-start(bf16[192,3584]{1,0:T(8,128)(2,1)S(1)} %bitcast.93), channel_id=1, source_target_pairs={{0,1},{1,0},{2,3},{3,2},{4,5},{5,4},{6,7},{7,6},{8,9},{9,8},{10,11... | collective-permute-start | bytes 4128776 | tf_op jit(solution)/shard_map/ppermute | solution.py:328
  145.8 19.0 %collective-permute-start.14 = (bf16[2,192,256]{2,1,0:T(8,128)(2,1)S(1)}, bf16[2,192,256]{2,1,0:T(8,128)(2,1)S(1)}, u32[]{:S(2)}, u32[]{:S(2)}) collective-permute-start(bf16[2,192,256]{2,1,0:T(8,128)(2,1)S(1)} %slice.40), channel_id=1, source_target_pairs={{0,1},{1,0},{2,3},{3,2},{4,5},{5,4},{6,7},{7,6},{8,9},{9,8},{10,11... | collective-permute-start | bytes 589832 | tf_op jit(solution)/shard_map/ppermute | solution.py:328
  166.5 56.0 %all-to-all-start.4 = ((bf16[4,96,3584]{2,1,0:T(8,128)(2,1)}), bf16[4,96,3584]{2,1,0:T(8,128)(2,1)S(1)}, u32[]{:S(2)}, u32[]{:S(2)}) async-start(bf16[4,96,3584]{2,1,0:T(8,128)(2,1)} %bitcast.100), calls=%async_computation.4 | async-start | bytes 5505024 | tf_op jit(solution)/shard_map/all_to_all | solution.py:346
  170.7 49.7 %collective-permute-start.16 = (bf16[192,3584]{1,0:T(8,128)(2,1)}, bf16[192,3584]{1,0:T(8,128)(2,1)}, u32[]{:S(2)}, u32[]{:S(2)}) collective-permute-start(bf16[192,3584]{1,0:T(8,128)(2,1)} %bitcast.29.x_ref.refs_10_), channel_id=1, source_target_pairs={{0,16},{16,0},{1,17},{17,1},{2,18},{18,2},{3,19},{19,3},{4,20},{20... | collective-permute-start | bytes 4128776 | tf_op jit(solution)/shard_map/ppermute | solution.py:337
  174.5 45.9 %collective-permute-start.15 = (bf16[128,3584]{1,0:T(8,128)(2,1)}, bf16[128,3584]{1,0:T(8,128)(2,1)}, u32[]{:S(2)}, u32[]{:S(2)}) collective-permute-start(bf16[128,3584]{1,0:T(8,128)(2,1)} %convolution_convert_fusion.1), channel_id=1, source_target_pairs={{0,8},{1,9},{2,10},{3,11},{4,12},{5,13},{6,14},{7,15},{8,0},{9,1},... | collective-permute-start | bytes 2752520 | tf_op jit(solution)/shard_map/ppermute | solution.py:328
  177.1 3.3 %collective-permute-start.19 = (bf16[2,192,512]{2,1,0:T(8,128)(2,1)}, bf16[2,192,512]{2,1,0:T(8,128)(2,1)}, u32[]{:S(2)}, u32[]{:S(2)}) collective-permute-start(bf16[2,192,512]{2,1,0:T(8,128)(2,1)} %slice.41), channel_id=1, source_target_pairs={{0,1},{1,0},{2,3},{3,2},{4,5},{5,4},{6,7},{7,6},{8,9},{9,8},{10,11... | collective-permute-start | bytes 1179656 | tf_op jit(solution)/shard_map/ppermute | solution.py:328
  178.2 38.5 %collective-permute-start.17 = (bf16[2,192,512]{2,1,0:T(8,128)(2,1)S(1)}, bf16[2,192,512]{2,1,0:T(8,128)(2,1)S(1)}, u32[]{:S(2)}, u32[]{:S(2)}) collective-permute-start(bf16[2,192,512]{2,1,0:T(8,128)(2,1)S(1)} %pad_maximum_fusion), channel_id=1, source_target_pairs={{0,16},{16,0},{1,17},{17,1},{2,18},{18,2},{3,19},{19,3},{4,20},{20... | collective-permute-start | bytes 1179656 | tf_op jit(solution)/shard_map/ppermute | solution.py:337
  179.8 36.9 %collective-permute-start.18 = (bf16[192,512]{1,0:T(8,128)(2,1)S(1)}, bf16[192,512]{1,0:T(8,128)(2,1)S(1)}, u32[]{:S(2)}, u32[]{:S(2)}) collective-permute-start(bf16[192,512]{1,0:T(8,128)(2,1)S(1)} %dynamic-slice_bitcast_fusion.1), channel_id=1, source_target_pairs={{0,16},{16,0},{1,17},{17,1},{2,18},{18,2},{3,19},{19,3},{4,20},{20... | collective-permute-start | bytes 589832 | tf_op jit(solution)/shard_map/ppermute | solution.py:337
  181.3 38.3 %collective-permute-start.20 = (bf16[192,512]{1,0:T(8,128)(2,1)S(1)}, bf16[192,512]{1,0:T(8,128)(2,1)S(1)}, u32[]{:S(2)}, u32[]{:S(2)}) collective-permute-start(bf16[192,512]{1,0:T(8,128)(2,1)S(1)} %dynamic-slice_bitcast_fusion), channel_id=1, source_target_pairs={{0,16},{16,0},{1,17},{17,1},{2,18},{18,2},{3,19},{19,3},{4,20},{20... | collective-permute-start | bytes 589832 | tf_op jit(solution)/shard_map/ppermute | solution.py:337
  198.3 29.3 %copy-start.18 = (bf16[128,4,2,48]{0,3,2,1:T(8,128)(2,1)S(1)}, bf16[128,4,2,48]{0,3,2,1:T(8,128)(2,1)}, u32[]{:S(2)}) copy-start(bf16[128,4,2,48]{0,3,2,1:T(8,128)(2,1)} %concatenate.26) | copy-start | bytes 294916
  222.5 41.2 %collective-permute-start.22 = (bf16[256,3584]{1,0:T(8,128)(2,1)}, bf16[256,3584]{1,0:T(8,128)(2,1)}, u32[]{:S(2)}, u32[]{:S(2)}) collective-permute-start(bf16[256,3584]{1,0:T(8,128)(2,1)} %shard_map.116), channel_id=1, source_target_pairs={{0,16},{16,0},{1,17},{17,1},{2,18},{18,2},{3,19},{19,3},{4,20},{20... | collective-permute-start | bytes 5505032 | tf_op jit(solution)/shard_map/ppermute | solution.py:337
  223.1 10.2 %collective-permute-start.23 = (bf16[192,3584]{1,0:T(8,128)(2,1)}, bf16[192,3584]{1,0:T(8,128)(2,1)}, u32[]{:S(2)}, u32[]{:S(2)}) collective-permute-start(bf16[192,3584]{1,0:T(8,128)(2,1)} %collective-permute-done.16.refs_14_), channel_id=1, source_target_pairs={{0,1},{1,0},{2,3},{3,2},{4,5},{5,4},{6,7},{7,6},{8,9},{9,8},{10,11... | collective-permute-start | bytes 4128776 | tf_op jit(solution)/shard_map/ppermute | solution.py:328
  223.1 43.8 %all-to-all-start.5 = ((bf16[4,48,3584]{2,1,0:T(8,128)(2,1)}), bf16[4,48,3584]{2,1,0:T(8,128)(2,1)}, u32[]{:S(2)}, u32[]{:S(2)}) async-start(bf16[4,48,3584]{2,1,0:T(8,128)(2,1)} %bitcast.103), calls=%async_computation.5 | async-start | bytes 2752512 | tf_op jit(solution)/shard_map/all_to_all | solution.py:346
  229.2 43.7 %collective-permute-start.21 = (bf16[128,3584]{1,0:T(8,128)(2,1)}, bf16[128,3584]{1,0:T(8,128)(2,1)}, u32[]{:S(2)}, u32[]{:S(2)}) collective-permute-start(bf16[128,3584]{1,0:T(8,128)(2,1)} %convolution_convert_fusion), channel_id=1, source_target_pairs={{0,8},{1,9},{2,10},{3,11},{4,12},{5,13},{6,14},{7,15},{8,0},{9,1},... | collective-permute-start | bytes 2752520 | tf_op jit(solution)/shard_map/ppermute | solution.py:328
  233.3 30.4 %copy-start.3 = (bf16[256,3584]{1,0:T(8,128)(2,1)S(1)}, bf16[256,3584]{1,0:T(8,128)(2,1)}, u32[]{:S(2)}) copy-start(bf16[256,3584]{1,0:T(8,128)(2,1)} %shard_map.117) | copy-start | bytes 5505028
  (32 other events, 195.3 us)

commit v17 on v16

--- a/solution.py
+++ b/solution.py
@@ -13,7 +13,7 @@
 NN = ((1,), (0,))
 NT = ((1,), (1,))
 TN = ((0,), (0,))
-VMEM_BYTES = 56 * 1024 * 1024
+VMEM_BYTES = 61 * 1024 * 1024
 
 
 def dot(a, b, dims):
@@ -88,7 +88,7 @@
         matrix,
         rows.astype(F32),
         (NN, ((), ())),
-        precision=lax.Precision.HIGHEST,
+        precision=lax.Precision.HIGH,
         preferred_element_type=F32,
     )
 

time: 277 us -> 276 us (level)
  waiting for transfers between devices: 81.3 us -> 92 us
  other arithmetic: 15.5 us -> 8.68 us
  local copies, waits for them, and re-layouts: 21.4 us -> 18.1 us
    ppermute x18, waiting for transfers between devices: 40.1 us -> 53.6 us  [hop(): lax.ppermute(rows, 'expert', [(i, i ^ distance) for i in range(devices)])]
    ppermute x6, waiting for transfers between devices: 39.1 us -> 36 us  [mirror(): lax.ppermute(rows, 'pipe', [(p, rank_count - 1 - p) for p in range(rank_c...]
  transfers between devices with their start and end apart: 30 -> 30, of which waited for: 9 -> 10; matrix products, arithmetic and copies ran while one was open for 15% -> 12% of each run, Pallas kernels for 35% -> 35%
where the time goes in v17:
time: 276 us; the launch traced here: 275 us
  Pallas kernels  96.1 us (35%)
  waiting for transfers between devices  92 us (33%)
  starting transfers between devices  46.3 us (17%)
  local copies, waits for them, and re-layouts  18.1 us (7%)
  matrix products  12.4 us (4%)
  other arithmetic  8.68 us (3%)
    ppermute x18, waiting for transfers between devices, hop(): lax.ppermute(rows, 'expert', [(i, i ^ distance) for i in range(devices)])  53.6 us
    ppermute x6, waiting for transfers between devices, mirror(): lax.ppermute(rows, 'pipe', [(p, rank_count - 1 - p) for p in range(rank_c...  36 us
    pallas_call x2, Pallas kernels, backward(): kernel_call(body, (4,), [row_spec(rows_grad, width), units, units] + weig...  35.4 us
    pallas_call x2, Pallas kernels, forward(): kernel_call(body, (4,), [row_spec(rows, width)] + weight_specs(width, hal...  27.4 us
    all_to_all x6, starting transfers between devices, near_exchange(): lax.all_to_all(rows.reshape(near, -1, width), 'expert', split_axis=0, con...  27.1 us
    pallas_call x2, Pallas kernels, down_grad(): kernel_call(body, (width // tile,), [pl.BlockSpec((1, count, half_units),...  15.4 us
    ppermute x18, starting transfers between devices, hop(): lax.ppermute(rows, 'expert', [(i, i ^ distance) for i in range(devices)])  13.1 us
    pallas_call x1, Pallas kernels, gate_up_grad(): kernel_call(body, (width // tile,), [pl.BlockSpec((1, count, both), lambd...  12.6 us
  transfers between devices with their start and end apart: 30, of which 10 were waited for; matrix products, arithmetic and copies ran while one was open for 12% of the time, Pallas kernels for 35%

profile of v17, /device:TPU:0, one launch (start us, length us, event | category | flops | bytes accessed | tf_op | source)
XLA Modules:
  0.0 274.5 jit_solution(5896556577260168336)
XLA Ops:
  1.7 4.0 %collective-permute-start = (bf16[16,3584]{1,0:T(8,128)(2,1)S(1)}, bf16[16,3584]{1,0:T(8,128)(2,1)S(1)}, u32[]{:S(2)}, u32[]{:S(2)}) collective-permute-start(bf16[16,3584]{1,0:T(8,128)(2,1)S(1)} %slice_bitcast_fusion.3), channel_id=1, source_target_pairs={{0,8},{1,9},{2,10},{3,11},{4,12},{5,13},{6,14},{7,15},{8,0},{9,1},... | collective-permute-start | bytes 344072 | tf_op jit(solution)/shard_map/ppermute | solution.py:328
  5.7 2.1 slice_bitcast_fusion
  9.3 2.5 fusion
  12.4 3.8 %all-to-all-start = ((bf16[4,96,3584]{2,1,0:T(8,128)(2,1)}), bf16[4,96,3584]{2,1,0:T(8,128)(2,1)S(1)}, u32[]{:S(2)}, u32[]{:S(2)}) async-start(bf16[4,96,3584]{2,1,0:T(8,128)(2,1)} %bitcast.101), calls=%async_computation | async-start | bytes 5505024 | tf_op jit(solution)/shard_map/all_to_all | solution.py:346
  16.8 2.1 collective-permute-start.1
  19.7 27.5 %collective-permute-done.1 = f32[128,4]{0,1:T(4,128)S(1)} collective-permute-done((f32[128,4]{0,1:T(4,128)S(1)}, f32[128,4]{0,1:T(4,128)S(1)}, u32[]{:S(2)}, u32[]{:S(2)}) %collective-permute-start.1) | collective-permute-done | bytes 2080 | tf_op jit(solution)/shard_map/ppermute | solution.py:328
  48.8 14.3 %collective-permute-done.2.refs_1_ = bf16[112,3584]{1,0:T(8,128)(2,1)} collective-permute-done((bf16[112,3584]{1,0:T(8,128)(2,1)}, bf16[112,3584]{1,0:T(8,128)(2,1)}, u32[]{:S(2)}, u32[]{:S(2)}) %collective-permute-start.2) | collective-permute-done | bytes 802848 | tf_op jit(solution)/shard_map/ppermute | solution.py:328
  63.1 2.6 shard_map.110
  67.8 6.8 %all-to-all-start.1 = ((bf16[4,48,3584]{2,1,0:T(8,128)(2,1)}), bf16[4,48,3584]{2,1,0:T(8,128)(2,1)}, u32[]{:S(2)}, u32[]{:S(2)}) async-start(bf16[4,48,3584]{2,1,0:T(8,128)(2,1)} %bitcast.97), calls=%async_computation.1 | async-start | bytes 2752512 | tf_op jit(solution)/shard_map/all_to_all | solution.py:346
  79.1 13.3 %shard_map.111 = (f32[4,192,256]{2,1,0:T(8,128)}, f32[4,192,256]{2,1,0:T(8,128)}, bf16[4,192,256]{2,1,0:T(8,128)(2,1)}, bf16[192,3584]{1,0:T(8,128)(2,1)}) custom-call(bf16[4,2,48,3584]{3,2,1,0:T(8,128)(2,1)} %bitcast.71, bf16[3584,512]{1,0:T(8,128)(2,1)} %bitcast.77, bf16[3584,512]{1,0:T(8,128)(2,1)} %bitcast.82, bf16[512,3584]{1,0:T(8,128)(2,1)} %bitcast.87, ...), custom_call_target="tpu_custom_call" | custom-call | flops 1 | bytes 1 | tf_op jit(solution)/shard_map/pallas_call | solution.py:156
  92.3 17.0 %shard_map.112 = (bf16[4,192,512]{2,1,0:T(8,128)(2,1)}, bf16[192,3584]{1,0:T(8,128)(2,1)}) custom-call(bf16[4,2,48,3584]{3,2,1,0:T(8,128)(2,1)} %bitcast.72, f32[4,192,256]{2,1,0:T(8,128)} %get-tuple-element.93.pre_gate_ref, f32[4,192,256]{2,1,0:T(8,128)} %get-tuple-element.94.pre_up_ref, bf16[3584,512]{1,0:T(8,128)(2,1)} %bitcast.78, ...), custom_call_target="tpu_custom_call" | custom-call | flops 1 | bytes 1 | tf_op jit(solution)/shard_map/pallas_call | solution.py:214
  110.1 8.4 %collective-permute-done.6.refs_1_ = bf16[128,3584]{1,0:T(8,128)(2,1)} collective-permute-done((bf16[128,3584]{1,0:T(8,128)(2,1)}, bf16[128,3584]{1,0:T(8,128)(2,1)}, u32[]{:S(2)}, u32[]{:S(2)}) %collective-permute-start.6) | collective-permute-done | bytes 917536 | tf_op jit(solution)/shard_map/ppermute | solution.py:328
  118.5 2.6 shard_map.113
  121.1 3.9 %all-to-all-start.2 = ((bf16[4,48,3584]{2,1,0:T(8,128)(2,1)}), bf16[4,48,3584]{2,1,0:T(8,128)(2,1)S(1)}, u32[]{:S(2)}, u32[]{:S(2)}) async-start(bf16[4,48,3584]{2,1,0:T(8,128)(2,1)} %bitcast.98), calls=%async_computation.2 | async-start | bytes 2752512 | tf_op jit(solution)/shard_map/all_to_all | solution.py:346
  126.3 14.1 %shard_map.114 = (f32[4,192,256]{2,1,0:T(8,128)}, f32[4,192,256]{2,1,0:T(8,128)}, bf16[4,192,256]{2,1,0:T(8,128)(2,1)}, bf16[192,3584]{1,0:T(8,128)(2,1)}) custom-call(bf16[192,3584]{1,0:T(8,128)(2,1)} %bitcast.29.x_ref.refs_10_, bf16[3584,512]{1,0:T(8,128)(2,1)} %bitcast.79, bf16[3584,512]{1,0:T(8,128)(2,1)} %bitcast.84, bf16[512,3584]{1,0:T(8,128)(2,1)} %bitcast.89, ...), custom_call_target="tpu_custom_call" | custom-call | flops 1 | bytes 1 | tf_op jit(solution)/shard_map/pallas_call | solution.py:156
  141.2 3.9 %all-to-all-start.3 = ((bf16[4,48,3584]{2,1,0:T(8,128)(2,1)}), bf16[4,48,3584]{2,1,0:T(8,128)(2,1)S(1)}, u32[]{:S(2)}, u32[]{:S(2)}) async-start(bf16[4,48,3584]{2,1,0:T(8,128)(2,1)} %bitcast.105), calls=%async_computation.3 | async-start | bytes 2752512 | tf_op jit(solution)/shard_map/all_to_all | solution.py:346
  146.4 18.5 %shard_map.115 = (bf16[4,192,512]{2,1,0:T(8,128)(2,1)}, bf16[4,2,48,3584]{3,2,1,0:T(8,128)(2,1)}) custom-call(bf16[192,3584]{1,0:T(8,128)(2,1)} %bitcast.94, f32[4,192,256]{2,1,0:T(8,128)} %get-tuple-element.116.pre_gate_ref, f32[4,192,256]{2,1,0:T(8,128)} %get-tuple-element.117.pre_up_ref, bf16[3584,512]{1,0:T(8,128)(2,1)} %bitcast.80, ...), custom_call_target="tpu_custom_call" | custom-call | flops 1 | bytes 1 | tf_op jit(solution)/shard_map/pallas_call | solution.py:214
  165.9 4.2 %all-to-all-start.4 = ((bf16[4,96,3584]{2,1,0:T(8,128)(2,1)}), bf16[4,96,3584]{2,1,0:T(8,128)(2,1)S(1)}, u32[]{:S(2)}, u32[]{:S(2)}) async-start(bf16[4,96,3584]{2,1,0:T(8,128)(2,1)} %bitcast.100), calls=%async_computation.4 | async-start | bytes 5505024 | tf_op jit(solution)/shard_map/all_to_all | solution.py:346
  170.7 3.0 %convolution_convert_fusion.1 = bf16[128,3584]{1,0:T(8,128)(2,1)} fusion(f32[128,192]{0,1:T(8,128)S(1)} %copy-done.13, bf16[192,3584]{1,0:T(8,128)(2,1)} %bitcast.99), kind=kOutput, calls=%fused_computation.5 | convolution fusion | flops 528941056 | bytes 2392064 | tf_op jit(solution)/shard_map/dot_general | solution.py:87
  184.4 7.7 %shard_map.117 = bf16[256,3584]{1,0:T(8,128)(2,1)} custom-call(s32[1]{0:T(128)} %bitcast.36.which_ref, bf16[4,192,256]{2,1,0:T(8,128)(2,1)} %get-tuple-element.111.refs_0_, bf16[2,192,256]{2,1,0:T(8,128)(2,1)} %copy-done.12, bf16[4,192,256]{2,1,0:T(8,128)(2,1)} %get-tuple-element.121.refs_2_, bf16[2,192,256]{2,1,0:T(8,128)(2,1)} %collective-permute-done.14.refs_3_, ...), custom_call_target="tpu_custom_call" | custom-call | flops 1 | bytes 1 | tf_op jit(solution)/shard_map/pallas_call | solution.py:251
  192.1 7.7 %shard_map.116 = bf16[256,3584]{1,0:T(8,128)(2,1)} custom-call(s32[1]{0:T(128)S(6)} %sub.38.which_ref, bf16[4,192,256]{2,1,0:T(8,128)(2,1)} %get-tuple-element.111.refs_0_, bf16[2,192,256]{2,1,0:T(8,128)(2,1)} %copy-done.12, bf16[4,192,256]{2,1,0:T(8,128)(2,1)} %get-tuple-element.121.refs_2_, bf16[2,192,256]{2,1,0:T(8,128)(2,1)} %collective-permute-done.14.refs_3_, ...), custom_call_target="tpu_custom_call" | custom-call | flops 1 | bytes 1 | tf_op jit(solution)/shard_map/pallas_call | solution.py:251
  199.8 16.3 %collective-permute-done.18.refs_6_ = bf16[192,512]{1,0:T(8,128)(2,1)} collective-permute-done((bf16[192,512]{1,0:T(8,128)(2,1)}, bf16[192,512]{1,0:T(8,128)(2,1)}, u32[]{:S(2)}, u32[]{:S(2)}) %collective-permute-start.18) | collective-permute-done | bytes 196640 | tf_op jit(solution)/shard_map/ppermute | solution.py:337
  216.2 2.9 %collective-permute-done.20.refs_7_ = bf16[192,512]{1,0:T(8,128)(2,1)} collective-permute-done((bf16[192,512]{1,0:T(8,128)(2,1)}, bf16[192,512]{1,0:T(8,128)(2,1)}, u32[]{:S(2)}, u32[]{:S(2)}) %collective-permute-start.20) | collective-permute-done | bytes 196640 | tf_op jit(solution)/shard_map/ppermute | solution.py:337
  219.8 2.1 all-to-all-done.4
  222.4 4.5 %all-to-all-start.5 = ((bf16[4,48,3584]{2,1,0:T(8,128)(2,1)}), bf16[4,48,3584]{2,1,0:T(8,128)(2,1)}, u32[]{:S(2)}, u32[]{:S(2)}) async-start(bf16[4,48,3584]{2,1,0:T(8,128)(2,1)} %bitcast.103), calls=%async_computation.5 | async-start | bytes 2752512 | tf_op jit(solution)/shard_map/all_to_all | solution.py:346
  231.7 1.9 fusion.14
  233.6 12.6 %shard_map.118 = (bf16[3584,256]{1,0:T(8,128)(2,1)}, bf16[3584,256]{1,0:T(8,128)(2,1)}) custom-call(s32[1]{0:T(128)} %bitcast.36.which_ref, bf16[4,192,512]{2,1,0:T(8,128)(2,1)} %get-tuple-element.131.refs_0_, bf16[2,192,512]{2,1,0:T(8,128)(2,1)} %copy-done.11, bf16[4,192,512]{2,1,0:T(8,128)(2,1)} %get-tuple-element.133.refs_2_, ...), custom_call_target="tpu_custom_call" | custom-call | flops 1 | bytes 1 | tf_op jit(solution)/shard_map/pallas_call | solution.py:284
  246.2 16.8 %collective-permute-done.22 = bf16[256,3584]{1,0:T(8,128)(2,1)} collective-permute-done((bf16[256,3584]{1,0:T(8,128)(2,1)}, bf16[256,3584]{1,0:T(8,128)(2,1)}, u32[]{:S(2)}, u32[]{:S(2)}) %collective-permute-start.22) | collective-permute-done | bytes 1835040 | tf_op jit(solution)/shard_map/ppermute | solution.py:337
  263.0 3.2 %add_convert_fusion = bf16[256,3584]{1,0:T(8,128)(2,1)} fusion(bf16[256,3584]{1,0:T(8,128)(2,1)} %collective-permute-done.22, bf16[256,3584]{1,0:T(8,128)(2,1)S(1)} %copy-done.3), kind=kLoop, calls=%fused_computation.6 | loop fusion | flops 3670016 | bytes 5505024 | tf_op jit(solution)/shard_map/convert_element_type | solution.py:459
  266.2 3.4 %fusion.1 = bf16[128,3584]{1,0:T(8,128)(2,1)} fusion(f32[128,192]{0,1:T(8,128)S(1)} %get-tuple-element.145, bf16[192,3584]{1,0:T(8,128)(2,1)} %bitcast.42, bf16[128,3584]{1,0:T(8,128)(2,1)} %collective-permute-done.15), kind=kOutput, calls=%fused_computation.3 | convolution fusion | flops 529858560 | bytes 3309568 | tf_op jit(solution)/shard_map/dot_general | solution.py:87
  269.6 2.7 collective-permute-done.21
  272.3 2.3 fusion.5
  (128 shorter events, 34.9 us)
Async XLA Ops:
  1.7 10.1 %collective-permute-start = (bf16[16,3584]{1,0:T(8,128)(2,1)S(1)}, bf16[16,3584]{1,0:T(8,128)(2,1)S(1)}, u32[]{:S(2)}, u32[]{:S(2)}) collective-permute-start(bf16[16,3584]{1,0:T(8,128)(2,1)S(1)} %slice_bitcast_fusion.3), channel_id=1, source_target_pairs={{0,8},{1,9},{2,10},{3,11},{4,12},{5,13},{6,14},{7,15},{8,0},{9,1},... | collective-permute-start | bytes 344072 | tf_op jit(solution)/shard_map/ppermute | solution.py:328
  12.4 53.3 %all-to-all-start = ((bf16[4,96,3584]{2,1,0:T(8,128)(2,1)}), bf16[4,96,3584]{2,1,0:T(8,128)(2,1)S(1)}, u32[]{:S(2)}, u32[]{:S(2)}) async-start(bf16[4,96,3584]{2,1,0:T(8,128)(2,1)} %bitcast.101), calls=%async_computation | async-start | bytes 5505024 | tf_op jit(solution)/shard_map/all_to_all | solution.py:346
  16.2 50.8 %collective-permute-start.3 = (bf16[3584,512]{1,0:T(8,128)(2,1)}, bf16[3584,512]{1,0:T(8,128)(2,1)}, u32[]{:S(2)}, u32[]{:S(2)}) collective-permute-start(bf16[3584,512]{1,0:T(8,128)(2,1)} %bitcast.76), channel_id=1, source_target_pairs={{0,1},{1,0},{2,3},{3,2},{4,5},{5,4},{6,7},{7,6},{8,9},{9,8},{10,11... | collective-permute-start | bytes 11010056 | tf_op jit(solution)/shard_map/ppermute | solution.py:328
  16.2 50.8 %collective-permute-start.4 = (bf16[3584,512]{1,0:T(8,128)(2,1)}, bf16[3584,512]{1,0:T(8,128)(2,1)}, u32[]{:S(2)}, u32[]{:S(2)}) collective-permute-start(bf16[3584,512]{1,0:T(8,128)(2,1)} %bitcast.81), channel_id=1, source_target_pairs={{0,1},{1,0},{2,3},{3,2},{4,5},{5,4},{6,7},{7,6},{8,9},{9,8},{10,11... | collective-permute-start | bytes 11010056 | tf_op jit(solution)/shard_map/ppermute | solution.py:328
  16.7 50.3 %collective-permute-start.5 = (bf16[512,3584]{1,0:T(8,128)(2,1)}, bf16[512,3584]{1,0:T(8,128)(2,1)}, u32[]{:S(2)}, u32[]{:S(2)}) collective-permute-start(bf16[512,3584]{1,0:T(8,128)(2,1)} %bitcast.86), channel_id=1, source_target_pairs={{0,1},{1,0},{2,3},{3,2},{4,5},{5,4},{6,7},{7,6},{8,9},{9,8},{10,11... | collective-permute-start | bytes 11010056 | tf_op jit(solution)/shard_map/ppermute | solution.py:328
  16.8 30.4 %collective-permute-start.1 = (f32[128,4]{0,1:T(4,128)S(1)}, f32[128,4]{0,1:T(4,128)S(1)}, u32[]{:S(2)}, u32[]{:S(2)}) collective-permute-start(f32[128,4]{0,1:T(4,128)S(1)} %pad_maximum_fusion.1), channel_id=1, source_target_pairs={{0,8},{1,9},{2,10},{3,11},{4,12},{5,13},{6,14},{7,15},{8,0},{9,1},... | collective-permute-start | bytes 6152 | tf_op jit(solution)/shard_map/ppermute | solution.py:328
  18.8 44.3 %collective-permute-start.2 = (bf16[112,3584]{1,0:T(8,128)(2,1)}, bf16[112,3584]{1,0:T(8,128)(2,1)}, u32[]{:S(2)}, u32[]{:S(2)}) collective-permute-start(bf16[112,3584]{1,0:T(8,128)(2,1)} %slice_bitcast_fusion), channel_id=1, source_target_pairs={{0,8},{1,9},{2,10},{3,11},{4,12},{5,13},{6,14},{7,15},{8,0},{9,1},... | collective-permute-start | bytes 2408456 | tf_op jit(solution)/shard_map/ppermute | solution.py:328
  67.0 54.1 %collective-permute-start.7 = (bf16[4,2,48,3584]{3,2,1,0:T(8,128)(2,1)S(1)}, bf16[4,2,48,3584]{3,2,1,0:T(8,128)(2,1)}, u32[]{:S(2)}, u32[]{:S(2)}) collective-permute-start(bf16[4,2,48,3584]{3,2,1,0:T(8,128)(2,1)S(1)} %bitcast.70), channel_id=1, source_target_pairs={{0,1},{1,0},{2,3},{3,2},{4,5},{5,4},{6,7},{7,6},{8,9},{9,8},{10,11... | collective-permute-start | bytes 8257544 | tf_op jit(solution)/shard_map/ppermute | solution.py:328
  67.8 53.3 %all-to-all-start.1 = ((bf16[4,48,3584]{2,1,0:T(8,128)(2,1)}), bf16[4,48,3584]{2,1,0:T(8,128)(2,1)}, u32[]{:S(2)}, u32[]{:S(2)}) async-start(bf16[4,48,3584]{2,1,0:T(8,128)(2,1)} %bitcast.97), calls=%async_computation.1 | async-start | bytes 2752512 | tf_op jit(solution)/shard_map/all_to_all | solution.py:346
  74.6 46.5 %collective-permute-start.8 = (bf16[192,3584]{1,0:T(8,128)(2,1)}, bf16[192,3584]{1,0:T(8,128)(2,1)}, u32[]{:S(2)}, u32[]{:S(2)}) collective-permute-start(bf16[192,3584]{1,0:T(8,128)(2,1)} %bitcast.104), channel_id=1, source_target_pairs={{0,16},{16,0},{1,17},{17,1},{2,18},{18,2},{3,19},{19,3},{4,20},{20... | collective-permute-start | bytes 4128776 | tf_op jit(solution)/shard_map/ppermute | solution.py:337
  76.1 42.4 %collective-permute-start.6 = (bf16[128,3584]{1,0:T(8,128)(2,1)}, bf16[128,3584]{1,0:T(8,128)(2,1)}, u32[]{:S(2)}, u32[]{:S(2)}) collective-permute-start(bf16[128,3584]{1,0:T(8,128)(2,1)} %bitcast.123), channel_id=1, source_target_pairs={{0,8},{1,9},{2,10},{3,11},{4,12},{5,13},{6,14},{7,15},{8,0},{9,1},... | collective-permute-start | bytes 2752520 | tf_op jit(solution)/shard_map/ppermute | solution.py:328
  121.1 19.6 %all-to-all-start.2 = ((bf16[4,48,3584]{2,1,0:T(8,128)(2,1)}), bf16[4,48,3584]{2,1,0:T(8,128)(2,1)S(1)}, u32[]{:S(2)}, u32[]{:S(2)}) async-start(bf16[4,48,3584]{2,1,0:T(8,128)(2,1)} %bitcast.98), calls=%async_computation.2 | async-start | bytes 2752512 | tf_op jit(solution)/shard_map/all_to_all | solution.py:346
  125.0 15.5 %collective-permute-start.10 = (bf16[192,3584]{1,0:T(8,128)(2,1)}, bf16[192,3584]{1,0:T(8,128)(2,1)}, u32[]{:S(2)}, u32[]{:S(2)}) collective-permute-start(bf16[192,3584]{1,0:T(8,128)(2,1)} %collective-permute-done.8.refs_12_), channel_id=1, source_target_pairs={{0,1},{1,0},{2,3},{3,2},{4,5},{5,4},{6,7},{7,6},{8,9},{9,8},{10,11... | collective-permute-start | bytes 4128776 | tf_op jit(solution)/shard_map/ppermute | solution.py:328
  125.1 15.4 %collective-permute-start.9 = (bf16[192,3584]{1,0:T(8,128)(2,1)}, bf16[192,3584]{1,0:T(8,128)(2,1)}, u32[]{:S(2)}, u32[]{:S(2)}) collective-permute-start(bf16[192,3584]{1,0:T(8,128)(2,1)} %bitcast.29.x_ref.refs_10_), channel_id=1, source_target_pairs={{0,1},{1,0},{2,3},{3,2},{4,5},{5,4},{6,7},{7,6},{8,9},{9,8},{10,11... | collective-permute-start | bytes 4128776 | tf_op jit(solution)/shard_map/ppermute | solution.py:328
  125.6 14.8 %collective-permute-start.12 = (bf16[2,192,512]{2,1,0:T(8,128)(2,1)S(1)}, bf16[2,192,512]{2,1,0:T(8,128)(2,1)S(1)}, u32[]{:S(2)}, u32[]{:S(2)}) collective-permute-start(bf16[2,192,512]{2,1,0:T(8,128)(2,1)S(1)} %slice.39), channel_id=1, source_target_pairs={{0,1},{1,0},{2,3},{3,2},{4,5},{5,4},{6,7},{7,6},{8,9},{9,8},{10,11... | collective-permute-start | bytes 1179656 | tf_op jit(solution)/shard_map/ppermute | solution.py:328
  125.8 14.7 %collective-permute-start.11 = (bf16[2,192,256]{2,1,0:T(8,128)(2,1)S(1)}, bf16[2,192,256]{2,1,0:T(8,128)(2,1)S(1)}, u32[]{:S(2)}, u32[]{:S(2)}) collective-permute-start(bf16[2,192,256]{2,1,0:T(8,128)(2,1)S(1)} %slice.38), channel_id=1, source_target_pairs={{0,1},{1,0},{2,3},{3,2},{4,5},{5,4},{6,7},{7,6},{8,9},{9,8},{10,11... | collective-permute-start | bytes 589832 | tf_op jit(solution)/shard_map/ppermute | solution.py:328
  141.2 23.6 %all-to-all-start.3 = ((bf16[4,48,3584]{2,1,0:T(8,128)(2,1)}), bf16[4,48,3584]{2,1,0:T(8,128)(2,1)S(1)}, u32[]{:S(2)}, u32[]{:S(2)}) async-start(bf16[4,48,3584]{2,1,0:T(8,128)(2,1)} %bitcast.105), calls=%async_computation.3 | async-start | bytes 2752512 | tf_op jit(solution)/shard_map/all_to_all | solution.py:346
  145.1 19.7 %collective-permute-start.13 = (bf16[192,3584]{1,0:T(8,128)(2,1)S(1)}, bf16[192,3584]{1,0:T(8,128)(2,1)}, u32[]{:S(2)}, u32[]{:S(2)}) collective-permute-start(bf16[192,3584]{1,0:T(8,128)(2,1)S(1)} %bitcast.93), channel_id=1, source_target_pairs={{0,1},{1,0},{2,3},{3,2},{4,5},{5,4},{6,7},{7,6},{8,9},{9,8},{10,11... | collective-permute-start | bytes 4128776 | tf_op jit(solution)/shard_map/ppermute | solution.py:328
  145.9 19.0 %collective-permute-start.14 = (bf16[2,192,256]{2,1,0:T(8,128)(2,1)}, bf16[2,192,256]{2,1,0:T(8,128)(2,1)}, u32[]{:S(2)}, u32[]{:S(2)}) collective-permute-start(bf16[2,192,256]{2,1,0:T(8,128)(2,1)} %slice.40), channel_id=1, source_target_pairs={{0,1},{1,0},{2,3},{3,2},{4,5},{5,4},{6,7},{7,6},{8,9},{9,8},{10,11... | collective-permute-start | bytes 589832 | tf_op jit(solution)/shard_map/ppermute | solution.py:328
  165.9 55.9 %all-to-all-start.4 = ((bf16[4,96,3584]{2,1,0:T(8,128)(2,1)}), bf16[4,96,3584]{2,1,0:T(8,128)(2,1)S(1)}, u32[]{:S(2)}, u32[]{:S(2)}) async-start(bf16[4,96,3584]{2,1,0:T(8,128)(2,1)} %bitcast.100), calls=%async_computation.4 | async-start | bytes 5505024 | tf_op jit(solution)/shard_map/all_to_all | solution.py:346
  170.1 49.6 %collective-permute-start.16 = (bf16[192,3584]{1,0:T(8,128)(2,1)}, bf16[192,3584]{1,0:T(8,128)(2,1)}, u32[]{:S(2)}, u32[]{:S(2)}) collective-permute-start(bf16[192,3584]{1,0:T(8,128)(2,1)} %bitcast.29.x_ref.refs_10_), channel_id=1, source_target_pairs={{0,16},{16,0},{1,17},{17,1},{2,18},{18,2},{3,19},{19,3},{4,20},{20... | collective-permute-start | bytes 4128776 | tf_op jit(solution)/shard_map/ppermute | solution.py:337
  173.6 46.1 %collective-permute-start.15 = (bf16[128,3584]{1,0:T(8,128)(2,1)}, bf16[128,3584]{1,0:T(8,128)(2,1)}, u32[]{:S(2)}, u32[]{:S(2)}) collective-permute-start(bf16[128,3584]{1,0:T(8,128)(2,1)} %convolution_convert_fusion.1), channel_id=1, source_target_pairs={{0,8},{1,9},{2,10},{3,11},{4,12},{5,13},{6,14},{7,15},{8,0},{9,1},... | collective-permute-start | bytes 2752520 | tf_op jit(solution)/shard_map/ppermute | solution.py:328
  175.9 5.5 %collective-permute-start.19 = (bf16[2,192,512]{2,1,0:T(8,128)(2,1)}, bf16[2,192,512]{2,1,0:T(8,128)(2,1)S(1)}, u32[]{:S(2)}, u32[]{:S(2)}) collective-permute-start(bf16[2,192,512]{2,1,0:T(8,128)(2,1)} %slice.41), channel_id=1, source_target_pairs={{0,1},{1,0},{2,3},{3,2},{4,5},{5,4},{6,7},{7,6},{8,9},{9,8},{10,11... | collective-permute-start | bytes 1179656 | tf_op jit(solution)/shard_map/ppermute | solution.py:328
  177.8 38.4 %collective-permute-start.17 = (bf16[2,192,512]{2,1,0:T(8,128)(2,1)}, bf16[2,192,512]{2,1,0:T(8,128)(2,1)}, u32[]{:S(2)}, u32[]{:S(2)}) collective-permute-start(bf16[2,192,512]{2,1,0:T(8,128)(2,1)} %pad_maximum_fusion), channel_id=1, source_target_pairs={{0,16},{16,0},{1,17},{17,1},{2,18},{18,2},{3,19},{19,3},{4,20},{20... | collective-permute-start | bytes 1179656 | tf_op jit(solution)/shard_map/ppermute | solution.py:337
  180.9 35.3 %collective-permute-start.18 = (bf16[192,512]{1,0:T(8,128)(2,1)}, bf16[192,512]{1,0:T(8,128)(2,1)}, u32[]{:S(2)}, u32[]{:S(2)}) collective-permute-start(bf16[192,512]{1,0:T(8,128)(2,1)} %dynamic-slice_bitcast_fusion.1), channel_id=1, source_target_pairs={{0,16},{16,0},{1,17},{17,1},{2,18},{18,2},{3,19},{19,3},{4,20},{20... | collective-permute-start | bytes 589832 | tf_op jit(solution)/shard_map/ppermute | solution.py:337
  182.9 36.2 %collective-permute-start.20 = (bf16[192,512]{1,0:T(8,128)(2,1)}, bf16[192,512]{1,0:T(8,128)(2,1)}, u32[]{:S(2)}, u32[]{:S(2)}) collective-permute-start(bf16[192,512]{1,0:T(8,128)(2,1)} %dynamic-slice_bitcast_fusion), channel_id=1, source_target_pairs={{0,16},{16,0},{1,17},{17,1},{2,18},{18,2},{3,19},{19,3},{4,20},{20... | collective-permute-start | bytes 589832 | tf_op jit(solution)/shard_map/ppermute | solution.py:337
  199.8 27.1 %copy-start.15 = (bf16[128,4,2,48]{0,3,2,1:T(8,128)(2,1)S(1)}, bf16[128,4,2,48]{0,3,2,1:T(8,128)(2,1)}, u32[]{:S(2)}) copy-start(bf16[128,4,2,48]{0,3,2,1:T(8,128)(2,1)} %concatenate.26) | copy-start | bytes 294916
  221.9 41.1 %collective-permute-start.22 = (bf16[256,3584]{1,0:T(8,128)(2,1)}, bf16[256,3584]{1,0:T(8,128)(2,1)}, u32[]{:S(2)}, u32[]{:S(2)}) collective-permute-start(bf16[256,3584]{1,0:T(8,128)(2,1)} %shard_map.116), channel_id=1, source_target_pairs={{0,16},{16,0},{1,17},{17,1},{2,18},{18,2},{3,19},{19,3},{4,20},{20... | collective-permute-start | bytes 5505032 | tf_op jit(solution)/shard_map/ppermute | solution.py:337
  222.4 11.2 %collective-permute-start.23 = (bf16[192,3584]{1,0:T(8,128)(2,1)}, bf16[192,3584]{1,0:T(8,128)(2,1)}, u32[]{:S(2)}, u32[]{:S(2)}) collective-permute-start(bf16[192,3584]{1,0:T(8,128)(2,1)} %collective-permute-done.16.refs_14_), channel_id=1, source_target_pairs={{0,1},{1,0},{2,3},{3,2},{4,5},{5,4},{6,7},{7,6},{8,9},{9,8},{10,11... | collective-permute-start | bytes 4128776 | tf_op jit(solution)/shard_map/ppermute | solution.py:328
  222.4 43.8 %all-to-all-start.5 = ((bf16[4,48,3584]{2,1,0:T(8,128)(2,1)}), bf16[4,48,3584]{2,1,0:T(8,128)(2,1)}, u32[]{:S(2)}, u32[]{:S(2)}) async-start(bf16[4,48,3584]{2,1,0:T(8,128)(2,1)} %bitcast.103), calls=%async_computation.5 | async-start | bytes 2752512 | tf_op jit(solution)/shard_map/all_to_all | solution.py:346
  228.6 43.7 %collective-permute-start.21 = (bf16[128,3584]{1,0:T(8,128)(2,1)}, bf16[128,3584]{1,0:T(8,128)(2,1)}, u32[]{:S(2)}, u32[]{:S(2)}) collective-permute-start(bf16[128,3584]{1,0:T(8,128)(2,1)} %convolution_convert_fusion), channel_id=1, source_target_pairs={{0,8},{1,9},{2,10},{3,11},{4,12},{5,13},{6,14},{7,15},{8,0},{9,1},... | collective-permute-start | bytes 2752520 | tf_op jit(solution)/shard_map/ppermute | solution.py:328
  233.6 29.4 %copy-start.3 = (bf16[256,3584]{1,0:T(8,128)(2,1)S(1)}, bf16[256,3584]{1,0:T(8,128)(2,1)}, u32[]{:S(2)}) copy-start(bf16[256,3584]{1,0:T(8,128)(2,1)} %shard_map.117) | copy-start | bytes 5505028
  (18 other events, 103.4 us)

commit v18 on v16

--- a/solution.py
+++ b/solution.py
@@ -133,7 +133,10 @@
         pre_gate_ref, pre_up_ref, hidden_ref, out_ref, acc_ref = refs[6:]
         step = pl.program_id(0)
 
-        def quarter(gate_ref, up_ref, down_ref):
+        def finish(cut, total):
+            out_ref[:, cut] = total.astype(BF16)
+
+        def quarter(last, gate_ref, up_ref, down_ref):
             x = flat(x_ref)
             pre_gate = dot(x, gate_ref[...], NN)
             pre_up = dot(x, up_ref[...], NN)
@@ -143,14 +146,14 @@
             hidden_ref[0] = hidden
             for cut in chunks(width):
                 term = dot(hidden, down_ref[:, cut], NN)
-                acc_ref[:, cut] = jnp.where(step == 0, term, acc_ref[:, cut] + term)
-
-        pl.when(step < 2)(lambda: quarter(*refs[:3]))
-        pl.when(step >= 2)(lambda: quarter(*refs[3:6]))
-
-        @pl.when(step == 3)
-        def _():
-            out_ref[...] = acc_ref[...].astype(BF16)
+                if last:
+                    finish(cut, acc_ref[:, cut] + term)
+                else:
+                    acc_ref[:, cut] = jnp.where(step == 0, term, acc_ref[:, cut] + term)
+
+        pl.when(step < 2)(lambda: quarter(False, *refs[:3]))
+        pl.when(step == 2)(lambda: quarter(False, *refs[3:6]))
+        pl.when(step == 3)(lambda: quarter(True, *refs[3:6]))
 
     units = pl.BlockSpec((1, count, half_units), lambda n: (n, 0, 0))
     return kernel_call(
@@ -178,7 +181,15 @@
         units_ref, out_ref, acc_ref = refs[-3:]
         step = pl.program_id(0)
 
-        def quarter(gate_ref, up_ref, down_ref):
+        def finish(cut, total):
+            total = total.astype(BF16)
+            if beside is None:
+                out_ref[:, cut] = total
+            else:
+                for n in range(near):
+                    out_ref[n, 0, :, cut] = total[n * piece : (n + 1) * piece]
+
+        def quarter(last, gate_ref, up_ref, down_ref):
             hidden_grad = dot(flat(x_ref), down_ref[...], NT)
             pre_gate = pre_gate_ref[0]
             sigma = jax.nn.sigmoid(pre_gate)
@@ -190,20 +201,21 @@
             units_ref[0, :, half_units:] = up_grad
             for cut in chunks(width):
                 term = dot(gate_grad, gate_ref[cut], NT) + dot(up_grad, up_ref[cut], NT)
-                acc_ref[:, cut] = jnp.where(step == 0, term, acc_ref[:, cut] + term)
-
-        pl.when(step < 2)(lambda: quarter(*refs[:3]))
-        pl.when(step >= 2)(lambda: quarter(*refs[3:6]))
-
-        @pl.when(step == 3)
-        def _():
-            if beside is None:
-                out_ref[...] = acc_ref[...].astype(BF16)
-            else:
+                if last:
+                    finish(cut, acc_ref[:, cut] + term)
+                else:
+                    acc_ref[:, cut] = jnp.where(step == 0, term, acc_ref[:, cut] + term)
+
+        pl.when(step < 2)(lambda: quarter(False, *refs[:3]))
+        pl.when(step == 2)(lambda: quarter(False, *refs[3:6]))
+        pl.when(step == 3)(lambda: quarter(True, *refs[3:6]))
+
+        if beside is not None:
+
+            @pl.when(step == 3)
+            def _():
                 for n in range(near):
-                    here = slice(n * piece, (n + 1) * piece)
-                    out_ref[n, 0] = acc_ref[here].astype(BF16)
-                    out_ref[n, 1] = refs[6][here]
+                    out_ref[n, 1] = refs[6][n * piece : (n + 1) * piece]
 
     units = pl.BlockSpec((1, count, half_units), lambda n: (n, 0, 0))
     whole = pl.BlockSpec((count, width), lambda n: (0, 0))

time: 277 us -> 276 us (level)
  no operation moved by 1% of the time
where the time goes in v18:
time: 276 us; the launch traced here: 275 us
  Pallas kernels  95.4 us (35%)
  waiting for transfers between devices  81.4 us (29%)
  starting transfers between devices  47.1 us (17%)
  local copies, waits for them, and re-layouts  21.4 us (8%)
  other arithmetic  15.5 us (6%)
  matrix products  12.9 us (5%)
    ppermute x18, waiting for transfers between devices, hop(): lax.ppermute(rows, 'expert', [(i, i ^ distance) for i in range(devices)])  40.2 us
    ppermute x6, waiting for transfers between devices, mirror(): lax.ppermute(rows, 'pipe', [(p, rank_count - 1 - p) for p in range(rank_c...  39.1 us
    pallas_call x2, Pallas kernels, backward(): kernel_call(body, (4,), [row_spec(rows_grad, width), units, units] + weig...  35.1 us
    pallas_call x2, Pallas kernels, forward(): kernel_call(body, (4,), [row_spec(rows, width)] + weight_specs(width, hal...  27.1 us
    all_to_all x6, starting transfers between devices, near_exchange(): lax.all_to_all(rows.reshape(near, -1, width), 'expert', split_axis=0, con...  27 us
    pallas_call x2, Pallas kernels, down_grad(): kernel_call(body, (width // tile,), [pl.BlockSpec((1, count, half_units),...  15.4 us
    ppermute x18, starting transfers between devices, hop(): lax.ppermute(rows, 'expert', [(i, i ^ distance) for i in range(devices)])  13.9 us
    pallas_call x1, Pallas kernels, gate_up_grad(): kernel_call(body, (width // tile,), [pl.BlockSpec((1, count, both), lambd...  12.6 us
  transfers between devices with their start and end apart: 30, of which 9 were waited for; matrix products, arithmetic and copies ran while one was open for 15% of the time, Pallas kernels for 35%

profile of v18, /device:TPU:0, one launch (start us, length us, event | category | flops | bytes accessed | tf_op | source)
XLA Modules:
  0.0 274.8 jit_solution(7581269441906639933)
XLA Ops:
  1.7 4.0 %collective-permute-start = (bf16[16,3584]{1,0:T(8,128)(2,1)S(1)}, bf16[16,3584]{1,0:T(8,128)(2,1)S(1)}, u32[]{:S(2)}, u32[]{:S(2)}) collective-permute-start(bf16[16,3584]{1,0:T(8,128)(2,1)S(1)} %slice_bitcast_fusion.3), channel_id=1, source_target_pairs={{0,8},{1,9},{2,10},{3,11},{4,12},{5,13},{6,14},{7,15},{8,0},{9,1},... | collective-permute-start | bytes 344072 | tf_op jit(solution)/shard_map/ppermute | solution.py:340
  9.0 2.5 fusion
  12.7 3.8 %all-to-all-start = ((bf16[4,96,3584]{2,1,0:T(8,128)(2,1)}), bf16[4,96,3584]{2,1,0:T(8,128)(2,1)S(1)}, u32[]{:S(2)}, u32[]{:S(2)}) async-start(bf16[4,96,3584]{2,1,0:T(8,128)(2,1)} %bitcast.101), calls=%async_computation | async-start | bytes 5505024 | tf_op jit(solution)/shard_map/all_to_all | solution.py:358
  17.0 1.8 collective-permute-start.1
  19.9 27.5 %collective-permute-done.1 = f32[128,4]{0,1:T(4,128)S(1)} collective-permute-done((f32[128,4]{0,1:T(4,128)}, f32[128,4]{0,1:T(4,128)S(1)}, u32[]{:S(2)}, u32[]{:S(2)}) %collective-permute-start.1) | collective-permute-done | bytes 2080 | tf_op jit(solution)/shard_map/ppermute | solution.py:340
  61.4 1.9 collective-permute-done.2.refs_1_
  63.3 2.6 shard_map.110
  68.0 6.6 %all-to-all-start.1 = ((bf16[4,48,3584]{2,1,0:T(8,128)(2,1)}), bf16[4,48,3584]{2,1,0:T(8,128)(2,1)}, u32[]{:S(2)}, u32[]{:S(2)}) async-start(bf16[4,48,3584]{2,1,0:T(8,128)(2,1)} %bitcast.97), calls=%async_computation.1 | async-start | bytes 2752512 | tf_op jit(solution)/shard_map/all_to_all | solution.py:358
  80.2 13.1 %shard_map.111 = (f32[4,192,256]{2,1,0:T(8,128)}, f32[4,192,256]{2,1,0:T(8,128)}, bf16[4,192,256]{2,1,0:T(8,128)(2,1)}, bf16[192,3584]{1,0:T(8,128)(2,1)}) custom-call(bf16[4,2,48,3584]{3,2,1,0:T(8,128)(2,1)} %bitcast.71, bf16[3584,512]{1,0:T(8,128)(2,1)} %bitcast.77, bf16[3584,512]{1,0:T(8,128)(2,1)} %bitcast.82, bf16[512,3584]{1,0:T(8,128)(2,1)} %bitcast.87, ...), custom_call_target="tpu_custom_call" | custom-call | flops 1 | bytes 1 | tf_op jit(solution)/shard_map/pallas_call | solution.py:159
  93.3 16.9 %shard_map.112 = (bf16[4,192,512]{2,1,0:T(8,128)(2,1)}, bf16[192,3584]{1,0:T(8,128)(2,1)}) custom-call(bf16[4,2,48,3584]{3,2,1,0:T(8,128)(2,1)} %bitcast.72, f32[4,192,256]{2,1,0:T(8,128)} %get-tuple-element.93.pre_gate_ref, f32[4,192,256]{2,1,0:T(8,128)} %get-tuple-element.94.pre_up_ref, bf16[3584,512]{1,0:T(8,128)(2,1)} %bitcast.78, ...), custom_call_target="tpu_custom_call" | custom-call | flops 1 | bytes 1 | tf_op jit(solution)/shard_map/pallas_call | solution.py:226
  111.0 7.6 %collective-permute-done.6.refs_1_ = bf16[128,3584]{1,0:T(8,128)(2,1)} collective-permute-done((bf16[128,3584]{1,0:T(8,128)(2,1)}, bf16[128,3584]{1,0:T(8,128)(2,1)}, u32[]{:S(2)}, u32[]{:S(2)}) %collective-permute-start.6) | collective-permute-done | bytes 917536 | tf_op jit(solution)/shard_map/ppermute | solution.py:340
  118.6 2.6 shard_map.113
  121.2 3.9 %all-to-all-start.2 = ((bf16[4,48,3584]{2,1,0:T(8,128)(2,1)}), bf16[4,48,3584]{2,1,0:T(8,128)(2,1)S(1)}, u32[]{:S(2)}, u32[]{:S(2)}) async-start(bf16[4,48,3584]{2,1,0:T(8,128)(2,1)} %bitcast.98), calls=%async_computation.2 | async-start | bytes 2752512 | tf_op jit(solution)/shard_map/all_to_all | solution.py:358
  126.4 14.0 %shard_map.114 = (f32[4,192,256]{2,1,0:T(8,128)}, f32[4,192,256]{2,1,0:T(8,128)}, bf16[4,192,256]{2,1,0:T(8,128)(2,1)}, bf16[192,3584]{1,0:T(8,128)(2,1)}) custom-call(bf16[192,3584]{1,0:T(8,128)(2,1)} %bitcast.29.x_ref.refs_10_, bf16[3584,512]{1,0:T(8,128)(2,1)} %bitcast.79, bf16[3584,512]{1,0:T(8,128)(2,1)} %bitcast.84, bf16[512,3584]{1,0:T(8,128)(2,1)} %bitcast.89, ...), custom_call_target="tpu_custom_call" | custom-call | flops 1 | bytes 1 | tf_op jit(solution)/shard_map/pallas_call | solution.py:159
  141.7 3.9 %all-to-all-start.3 = ((bf16[4,48,3584]{2,1,0:T(8,128)(2,1)}), bf16[4,48,3584]{2,1,0:T(8,128)(2,1)S(1)}, u32[]{:S(2)}, u32[]{:S(2)}) async-start(bf16[4,48,3584]{2,1,0:T(8,128)(2,1)} %bitcast.105), calls=%async_computation.3 | async-start | bytes 2752512 | tf_op jit(solution)/shard_map/all_to_all | solution.py:358
  146.2 18.2 %shard_map.115 = (bf16[4,192,512]{2,1,0:T(8,128)(2,1)}, bf16[4,2,48,3584]{3,2,1,0:T(8,128)(2,1)}) custom-call(bf16[192,3584]{1,0:T(8,128)(2,1)} %bitcast.94, f32[4,192,256]{2,1,0:T(8,128)} %get-tuple-element.116.pre_gate_ref, f32[4,192,256]{2,1,0:T(8,128)} %get-tuple-element.117.pre_up_ref, bf16[3584,512]{1,0:T(8,128)(2,1)} %bitcast.80, ...), custom_call_target="tpu_custom_call" | custom-call | flops 1 | bytes 1 | tf_op jit(solution)/shard_map/pallas_call | solution.py:226
  166.2 4.2 %all-to-all-start.4 = ((bf16[4,96,3584]{2,1,0:T(8,128)(2,1)}), bf16[4,96,3584]{2,1,0:T(8,128)(2,1)S(1)}, u32[]{:S(2)}, u32[]{:S(2)}) async-start(bf16[4,96,3584]{2,1,0:T(8,128)(2,1)} %bitcast.100), calls=%async_computation.4 | async-start | bytes 5505024 | tf_op jit(solution)/shard_map/all_to_all | solution.py:358
  170.9 3.2 %convolution_convert_fusion.1 = bf16[128,3584]{1,0:T(8,128)(2,1)} fusion(f32[128,192]{0,1:T(8,128)} %get-tuple-element.97, bf16[192,3584]{1,0:T(8,128)(2,1)} %bitcast.99), kind=kOutput, calls=%fused_computation.5 | convolution fusion | flops 1057423360 | bytes 2392064 | tf_op jit(solution)/shard_map/dot_general | solution.py:87
  174.2 1.8 collective-permute-start.15
  182.5 7.7 %shard_map.117 = bf16[256,3584]{1,0:T(8,128)(2,1)} custom-call(s32[1]{0:T(128)} %bitcast.36.which_ref, bf16[4,192,256]{2,1,0:T(8,128)(2,1)} %get-tuple-element.111.refs_0_, bf16[2,192,256]{2,1,0:T(8,128)(2,1)} %copy-done.12, bf16[4,192,256]{2,1,0:T(8,128)(2,1)} %get-tuple-element.121.refs_2_, bf16[2,192,256]{2,1,0:T(8,128)(2,1)} %copy-done.13, ...), custom_call_target="tpu_custom_call" | custom-call | flops 1 | bytes 1 | tf_op jit(solution)/shard_map/pallas_call | solution.py:263
  190.2 7.7 %shard_map.116 = bf16[256,3584]{1,0:T(8,128)(2,1)} custom-call(s32[1]{0:T(128)S(6)} %sub.38.which_ref, bf16[4,192,256]{2,1,0:T(8,128)(2,1)} %get-tuple-element.111.refs_0_, bf16[2,192,256]{2,1,0:T(8,128)(2,1)} %copy-done.12, bf16[4,192,256]{2,1,0:T(8,128)(2,1)} %get-tuple-element.121.refs_2_, bf16[2,192,256]{2,1,0:T(8,128)(2,1)} %copy-done.13, ...), custom_call_target="tpu_custom_call" | custom-call | flops 1 | bytes 1 | tf_op jit(solution)/shard_map/pallas_call | solution.py:263
  198.0 18.4 %collective-permute-done.18.refs_6_ = bf16[192,512]{1,0:T(8,128)(2,1)S(1)} collective-permute-done((bf16[192,512]{1,0:T(8,128)(2,1)S(1)}, bf16[192,512]{1,0:T(8,128)(2,1)S(1)}, u32[]{:S(2)}, u32[]{:S(2)}) %collective-permute-start.18) | collective-permute-done | bytes 196640 | tf_op jit(solution)/shard_map/ppermute | solution.py:349
  216.3 3.0 %collective-permute-done.20.refs_7_ = bf16[192,512]{1,0:T(8,128)(2,1)S(1)} collective-permute-done((bf16[192,512]{1,0:T(8,128)(2,1)S(1)}, bf16[192,512]{1,0:T(8,128)(2,1)S(1)}, u32[]{:S(2)}, u32[]{:S(2)}) %collective-permute-start.20) | collective-permute-done | bytes 196640 | tf_op jit(solution)/shard_map/ppermute | solution.py:349
  220.1 2.1 all-to-all-done.4
  222.7 4.6 %all-to-all-start.5 = ((bf16[4,48,3584]{2,1,0:T(8,128)(2,1)}), bf16[4,48,3584]{2,1,0:T(8,128)(2,1)}, u32[]{:S(2)}, u32[]{:S(2)}) async-start(bf16[4,48,3584]{2,1,0:T(8,128)(2,1)} %bitcast.103), calls=%async_computation.5 | async-start | bytes 2752512 | tf_op jit(solution)/shard_map/all_to_all | solution.py:358
  231.0 1.9 fusion.14
  233.0 12.6 %shard_map.118 = (bf16[3584,256]{1,0:T(8,128)(2,1)}, bf16[3584,256]{1,0:T(8,128)(2,1)}) custom-call(s32[1]{0:T(128)} %bitcast.36.which_ref, bf16[4,192,512]{2,1,0:T(8,128)(2,1)} %get-tuple-element.131.refs_0_, bf16[2,192,512]{2,1,0:T(8,128)(2,1)} %copy-done.11, bf16[4,192,512]{2,1,0:T(8,128)(2,1)} %get-tuple-element.133.refs_2_, ...), custom_call_target="tpu_custom_call" | custom-call | flops 1 | bytes 1 | tf_op jit(solution)/shard_map/pallas_call | solution.py:296
  245.6 17.7 %collective-permute-done.22 = bf16[256,3584]{1,0:T(8,128)(2,1)} collective-permute-done((bf16[256,3584]{1,0:T(8,128)(2,1)}, bf16[256,3584]{1,0:T(8,128)(2,1)}, u32[]{:S(2)}, u32[]{:S(2)}) %collective-permute-start.22) | collective-permute-done | bytes 1835040 | tf_op jit(solution)/shard_map/ppermute | solution.py:349
  263.3 3.2 %add_convert_fusion = bf16[256,3584]{1,0:T(8,128)(2,1)} fusion(bf16[256,3584]{1,0:T(8,128)(2,1)} %collective-permute-done.22, bf16[256,3584]{1,0:T(8,128)(2,1)S(1)} %copy-done.3), kind=kLoop, calls=%fused_computation.6 | loop fusion | flops 3670016 | bytes 5505024 | tf_op jit(solution)/shard_map/convert_element_type | solution.py:471
  266.5 3.6 %fusion.1 = bf16[128,3584]{1,0:T(8,128)(2,1)} fusion(f32[128,192]{0,1:T(8,128)S(1)} %copy-done.14, bf16[192,3584]{1,0:T(8,128)(2,1)} %bitcast.42, bf16[128,3584]{1,0:T(8,128)(2,1)} %collective-permute-done.15), kind=kOutput, calls=%fused_computation.3 | convolution fusion | flops 1058340864 | bytes 3309568 | tf_op jit(solution)/shard_map/dot_general | solution.py:87
  270.1 2.4 collective-permute-done.21
  272.6 2.3 fusion.5
  (156 shorter events, 46.4 us)
Async XLA Ops:
  1.7 10.3 %collective-permute-start = (bf16[16,3584]{1,0:T(8,128)(2,1)S(1)}, bf16[16,3584]{1,0:T(8,128)(2,1)S(1)}, u32[]{:S(2)}, u32[]{:S(2)}) collective-permute-start(bf16[16,3584]{1,0:T(8,128)(2,1)S(1)} %slice_bitcast_fusion.3), channel_id=1, source_target_pairs={{0,8},{1,9},{2,10},{3,11},{4,12},{5,13},{6,14},{7,15},{8,0},{9,1},... | collective-permute-start | bytes 344072 | tf_op jit(solution)/shard_map/ppermute | solution.py:340
  12.7 53.2 %all-to-all-start = ((bf16[4,96,3584]{2,1,0:T(8,128)(2,1)}), bf16[4,96,3584]{2,1,0:T(8,128)(2,1)S(1)}, u32[]{:S(2)}, u32[]{:S(2)}) async-start(bf16[4,96,3584]{2,1,0:T(8,128)(2,1)} %bitcast.101), calls=%async_computation | async-start | bytes 5505024 | tf_op jit(solution)/shard_map/all_to_all | solution.py:358
  16.5 50.7 %collective-permute-start.3 = (bf16[3584,512]{1,0:T(8,128)(2,1)}, bf16[3584,512]{1,0:T(8,128)(2,1)}, u32[]{:S(2)}, u32[]{:S(2)}) collective-permute-start(bf16[3584,512]{1,0:T(8,128)(2,1)} %bitcast.76), channel_id=1, source_target_pairs={{0,1},{1,0},{2,3},{3,2},{4,5},{5,4},{6,7},{7,6},{8,9},{9,8},{10,11... | collective-permute-start | bytes 11010056 | tf_op jit(solution)/shard_map/ppermute | solution.py:340
  16.5 50.7 %collective-permute-start.4 = (bf16[3584,512]{1,0:T(8,128)(2,1)}, bf16[3584,512]{1,0:T(8,128)(2,1)}, u32[]{:S(2)}, u32[]{:S(2)}) collective-permute-start(bf16[3584,512]{1,0:T(8,128)(2,1)} %bitcast.81), channel_id=1, source_target_pairs={{0,1},{1,0},{2,3},{3,2},{4,5},{5,4},{6,7},{7,6},{8,9},{9,8},{10,11... | collective-permute-start | bytes 11010056 | tf_op jit(solution)/shard_map/ppermute | solution.py:340
  17.0 50.2 %collective-permute-start.5 = (bf16[512,3584]{1,0:T(8,128)(2,1)}, bf16[512,3584]{1,0:T(8,128)(2,1)}, u32[]{:S(2)}, u32[]{:S(2)}) collective-permute-start(bf16[512,3584]{1,0:T(8,128)(2,1)} %bitcast.86), channel_id=1, source_target_pairs={{0,1},{1,0},{2,3},{3,2},{4,5},{5,4},{6,7},{7,6},{8,9},{9,8},{10,11... | collective-permute-start | bytes 11010056 | tf_op jit(solution)/shard_map/ppermute | solution.py:340
  17.0 30.4 %collective-permute-start.1 = (f32[128,4]{0,1:T(4,128)}, f32[128,4]{0,1:T(4,128)S(1)}, u32[]{:S(2)}, u32[]{:S(2)}) collective-permute-start(f32[128,4]{0,1:T(4,128)} %pad_maximum_fusion.1), channel_id=1, source_target_pairs={{0,8},{1,9},{2,10},{3,11},{4,12},{5,13},{6,14},{7,15},{8,0},{9,1},... | collective-permute-start | bytes 6152 | tf_op jit(solution)/shard_map/ppermute | solution.py:340
  18.8 44.4 %collective-permute-start.2 = (bf16[112,3584]{1,0:T(8,128)(2,1)S(1)}, bf16[112,3584]{1,0:T(8,128)(2,1)}, u32[]{:S(2)}, u32[]{:S(2)}) collective-permute-start(bf16[112,3584]{1,0:T(8,128)(2,1)S(1)} %slice_bitcast_fusion), channel_id=1, source_target_pairs={{0,8},{1,9},{2,10},{3,11},{4,12},{5,13},{6,14},{7,15},{8,0},{9,1},... | collective-permute-start | bytes 2408456 | tf_op jit(solution)/shard_map/ppermute | solution.py:340
  67.3 53.9 %collective-permute-start.7 = (bf16[4,2,48,3584]{3,2,1,0:T(8,128)(2,1)S(1)}, bf16[4,2,48,3584]{3,2,1,0:T(8,128)(2,1)}, u32[]{:S(2)}, u32[]{:S(2)}) collective-permute-start(bf16[4,2,48,3584]{3,2,1,0:T(8,128)(2,1)S(1)} %bitcast.70), channel_id=1, source_target_pairs={{0,1},{1,0},{2,3},{3,2},{4,5},{5,4},{6,7},{7,6},{8,9},{9,8},{10,11... | collective-permute-start | bytes 8257544 | tf_op jit(solution)/shard_map/ppermute | solution.py:340
  68.0 53.2 %all-to-all-start.1 = ((bf16[4,48,3584]{2,1,0:T(8,128)(2,1)}), bf16[4,48,3584]{2,1,0:T(8,128)(2,1)}, u32[]{:S(2)}, u32[]{:S(2)}) async-start(bf16[4,48,3584]{2,1,0:T(8,128)(2,1)} %bitcast.97), calls=%async_computation.1 | async-start | bytes 2752512 | tf_op jit(solution)/shard_map/all_to_all | solution.py:358
  74.6 46.5 %collective-permute-start.8 = (bf16[192,3584]{1,0:T(8,128)(2,1)}, bf16[192,3584]{1,0:T(8,128)(2,1)}, u32[]{:S(2)}, u32[]{:S(2)}) collective-permute-start(bf16[192,3584]{1,0:T(8,128)(2,1)} %bitcast.104), channel_id=1, source_target_pairs={{0,16},{16,0},{1,17},{17,1},{2,18},{18,2},{3,19},{19,3},{4,20},{20... | collective-permute-start | bytes 4128776 | tf_op jit(solution)/shard_map/ppermute | solution.py:349
  76.1 42.5 %collective-permute-start.6 = (bf16[128,3584]{1,0:T(8,128)(2,1)}, bf16[128,3584]{1,0:T(8,128)(2,1)}, u32[]{:S(2)}, u32[]{:S(2)}) collective-permute-start(bf16[128,3584]{1,0:T(8,128)(2,1)} %bitcast.123), channel_id=1, source_target_pairs={{0,8},{1,9},{2,10},{3,11},{4,12},{5,13},{6,14},{7,15},{8,0},{9,1},... | collective-permute-start | bytes 2752520 | tf_op jit(solution)/shard_map/ppermute | solution.py:340
  121.2 20.4 %all-to-all-start.2 = ((bf16[4,48,3584]{2,1,0:T(8,128)(2,1)}), bf16[4,48,3584]{2,1,0:T(8,128)(2,1)S(1)}, u32[]{:S(2)}, u32[]{:S(2)}) async-start(bf16[4,48,3584]{2,1,0:T(8,128)(2,1)} %bitcast.98), calls=%async_computation.2 | async-start | bytes 2752512 | tf_op jit(solution)/shard_map/all_to_all | solution.py:358
  125.1 15.3 %collective-permute-start.10 = (bf16[192,3584]{1,0:T(8,128)(2,1)}, bf16[192,3584]{1,0:T(8,128)(2,1)S(1)}, u32[]{:S(2)}, u32[]{:S(2)}) collective-permute-start(bf16[192,3584]{1,0:T(8,128)(2,1)} %collective-permute-done.8.refs_12_), channel_id=1, source_target_pairs={{0,1},{1,0},{2,3},{3,2},{4,5},{5,4},{6,7},{7,6},{8,9},{9,8},{10,11... | collective-permute-start | bytes 4128776 | tf_op jit(solution)/shard_map/ppermute | solution.py:340
  125.2 16.4 %collective-permute-start.9 = (bf16[192,3584]{1,0:T(8,128)(2,1)}, bf16[192,3584]{1,0:T(8,128)(2,1)}, u32[]{:S(2)}, u32[]{:S(2)}) collective-permute-start(bf16[192,3584]{1,0:T(8,128)(2,1)} %bitcast.29.x_ref.refs_10_), channel_id=1, source_target_pairs={{0,1},{1,0},{2,3},{3,2},{4,5},{5,4},{6,7},{7,6},{8,9},{9,8},{10,11... | collective-permute-start | bytes 4128776 | tf_op jit(solution)/shard_map/ppermute | solution.py:340
  125.7 14.7 %collective-permute-start.12 = (bf16[2,192,512]{2,1,0:T(8,128)(2,1)S(1)}, bf16[2,192,512]{2,1,0:T(8,128)(2,1)S(1)}, u32[]{:S(2)}, u32[]{:S(2)}) collective-permute-start(bf16[2,192,512]{2,1,0:T(8,128)(2,1)S(1)} %slice.39), channel_id=1, source_target_pairs={{0,1},{1,0},{2,3},{3,2},{4,5},{5,4},{6,7},{7,6},{8,9},{9,8},{10,11... | collective-permute-start | bytes 1179656 | tf_op jit(solution)/shard_map/ppermute | solution.py:340
  125.9 14.5 %collective-permute-start.11 = (bf16[2,192,256]{2,1,0:T(8,128)(2,1)S(1)}, bf16[2,192,256]{2,1,0:T(8,128)(2,1)S(1)}, u32[]{:S(2)}, u32[]{:S(2)}) collective-permute-start(bf16[2,192,256]{2,1,0:T(8,128)(2,1)S(1)} %slice.38), channel_id=1, source_target_pairs={{0,1},{1,0},{2,3},{3,2},{4,5},{5,4},{6,7},{7,6},{8,9},{9,8},{10,11... | collective-permute-start | bytes 589832 | tf_op jit(solution)/shard_map/ppermute | solution.py:340
  141.7 23.4 %all-to-all-start.3 = ((bf16[4,48,3584]{2,1,0:T(8,128)(2,1)}), bf16[4,48,3584]{2,1,0:T(8,128)(2,1)S(1)}, u32[]{:S(2)}, u32[]{:S(2)}) async-start(bf16[4,48,3584]{2,1,0:T(8,128)(2,1)} %bitcast.105), calls=%async_computation.3 | async-start | bytes 2752512 | tf_op jit(solution)/shard_map/all_to_all | solution.py:358
  145.6 19.5 %collective-permute-start.13 = (bf16[192,3584]{1,0:T(8,128)(2,1)S(1)}, bf16[192,3584]{1,0:T(8,128)(2,1)}, u32[]{:S(2)}, u32[]{:S(2)}) collective-permute-start(bf16[192,3584]{1,0:T(8,128)(2,1)S(1)} %bitcast.93), channel_id=1, source_target_pairs={{0,1},{1,0},{2,3},{3,2},{4,5},{5,4},{6,7},{7,6},{8,9},{9,8},{10,11... | collective-permute-start | bytes 4128776 | tf_op jit(solution)/shard_map/ppermute | solution.py:340
  145.6 18.8 %collective-permute-start.14 = (bf16[2,192,256]{2,1,0:T(8,128)(2,1)S(1)}, bf16[2,192,256]{2,1,0:T(8,128)(2,1)S(1)}, u32[]{:S(2)}, u32[]{:S(2)}) collective-permute-start(bf16[2,192,256]{2,1,0:T(8,128)(2,1)S(1)} %slice.40), channel_id=1, source_target_pairs={{0,1},{1,0},{2,3},{3,2},{4,5},{5,4},{6,7},{7,6},{8,9},{9,8},{10,11... | collective-permute-start | bytes 589832 | tf_op jit(solution)/shard_map/ppermute | solution.py:340
  166.2 56.0 %all-to-all-start.4 = ((bf16[4,96,3584]{2,1,0:T(8,128)(2,1)}), bf16[4,96,3584]{2,1,0:T(8,128)(2,1)S(1)}, u32[]{:S(2)}, u32[]{:S(2)}) async-start(bf16[4,96,3584]{2,1,0:T(8,128)(2,1)} %bitcast.100), calls=%async_computation.4 | async-start | bytes 5505024 | tf_op jit(solution)/shard_map/all_to_all | solution.py:358
  170.4 49.7 %collective-permute-start.16 = (bf16[192,3584]{1,0:T(8,128)(2,1)}, bf16[192,3584]{1,0:T(8,128)(2,1)}, u32[]{:S(2)}, u32[]{:S(2)}) collective-permute-start(bf16[192,3584]{1,0:T(8,128)(2,1)} %bitcast.29.x_ref.refs_10_), channel_id=1, source_target_pairs={{0,16},{16,0},{1,17},{17,1},{2,18},{18,2},{3,19},{19,3},{4,20},{20... | collective-permute-start | bytes 4128776 | tf_op jit(solution)/shard_map/ppermute | solution.py:349
  174.2 45.9 %collective-permute-start.15 = (bf16[128,3584]{1,0:T(8,128)(2,1)}, bf16[128,3584]{1,0:T(8,128)(2,1)}, u32[]{:S(2)}, u32[]{:S(2)}) collective-permute-start(bf16[128,3584]{1,0:T(8,128)(2,1)} %convolution_convert_fusion.1), channel_id=1, source_target_pairs={{0,8},{1,9},{2,10},{3,11},{4,12},{5,13},{6,14},{7,15},{8,0},{9,1},... | collective-permute-start | bytes 2752520 | tf_op jit(solution)/shard_map/ppermute | solution.py:340
  176.7 3.3 %collective-permute-start.19 = (bf16[2,192,512]{2,1,0:T(8,128)(2,1)}, bf16[2,192,512]{2,1,0:T(8,128)(2,1)}, u32[]{:S(2)}, u32[]{:S(2)}) collective-permute-start(bf16[2,192,512]{2,1,0:T(8,128)(2,1)} %slice.41), channel_id=1, source_target_pairs={{0,1},{1,0},{2,3},{3,2},{4,5},{5,4},{6,7},{7,6},{8,9},{9,8},{10,11... | collective-permute-start | bytes 1179656 | tf_op jit(solution)/shard_map/ppermute | solution.py:340
  177.8 38.5 %collective-permute-start.17 = (bf16[2,192,512]{2,1,0:T(8,128)(2,1)S(1)}, bf16[2,192,512]{2,1,0:T(8,128)(2,1)S(1)}, u32[]{:S(2)}, u32[]{:S(2)}) collective-permute-start(bf16[2,192,512]{2,1,0:T(8,128)(2,1)S(1)} %pad_maximum_fusion), channel_id=1, source_target_pairs={{0,16},{16,0},{1,17},{17,1},{2,18},{18,2},{3,19},{19,3},{4,20},{20... | collective-permute-start | bytes 1179656 | tf_op jit(solution)/shard_map/ppermute | solution.py:349
  179.4 36.9 %collective-permute-start.18 = (bf16[192,512]{1,0:T(8,128)(2,1)S(1)}, bf16[192,512]{1,0:T(8,128)(2,1)S(1)}, u32[]{:S(2)}, u32[]{:S(2)}) collective-permute-start(bf16[192,512]{1,0:T(8,128)(2,1)S(1)} %dynamic-slice_bitcast_fusion.1), channel_id=1, source_target_pairs={{0,16},{16,0},{1,17},{17,1},{2,18},{18,2},{3,19},{19,3},{4,20},{20... | collective-permute-start | bytes 589832 | tf_op jit(solution)/shard_map/ppermute | solution.py:349
  181.0 38.3 %collective-permute-start.20 = (bf16[192,512]{1,0:T(8,128)(2,1)S(1)}, bf16[192,512]{1,0:T(8,128)(2,1)S(1)}, u32[]{:S(2)}, u32[]{:S(2)}) collective-permute-start(bf16[192,512]{1,0:T(8,128)(2,1)S(1)} %dynamic-slice_bitcast_fusion), channel_id=1, source_target_pairs={{0,16},{16,0},{1,17},{17,1},{2,18},{18,2},{3,19},{19,3},{4,20},{20... | collective-permute-start | bytes 589832 | tf_op jit(solution)/shard_map/ppermute | solution.py:349
  198.0 29.3 %copy-start.18 = (bf16[128,4,2,48]{0,3,2,1:T(8,128)(2,1)S(1)}, bf16[128,4,2,48]{0,3,2,1:T(8,128)(2,1)}, u32[]{:S(2)}) copy-start(bf16[128,4,2,48]{0,3,2,1:T(8,128)(2,1)} %concatenate.26) | copy-start | bytes 294916
  222.2 41.2 %collective-permute-start.22 = (bf16[256,3584]{1,0:T(8,128)(2,1)}, bf16[256,3584]{1,0:T(8,128)(2,1)}, u32[]{:S(2)}, u32[]{:S(2)}) collective-permute-start(bf16[256,3584]{1,0:T(8,128)(2,1)} %shard_map.116), channel_id=1, source_target_pairs={{0,16},{16,0},{1,17},{17,1},{2,18},{18,2},{3,19},{19,3},{4,20},{20... | collective-permute-start | bytes 5505032 | tf_op jit(solution)/shard_map/ppermute | solution.py:349
  222.7 10.3 %collective-permute-start.23 = (bf16[192,3584]{1,0:T(8,128)(2,1)}, bf16[192,3584]{1,0:T(8,128)(2,1)}, u32[]{:S(2)}, u32[]{:S(2)}) collective-permute-start(bf16[192,3584]{1,0:T(8,128)(2,1)} %collective-permute-done.16.refs_14_), channel_id=1, source_target_pairs={{0,1},{1,0},{2,3},{3,2},{4,5},{5,4},{6,7},{7,6},{8,9},{9,8},{10,11... | collective-permute-start | bytes 4128776 | tf_op jit(solution)/shard_map/ppermute | solution.py:340
  222.7 43.8 %all-to-all-start.5 = ((bf16[4,48,3584]{2,1,0:T(8,128)(2,1)}), bf16[4,48,3584]{2,1,0:T(8,128)(2,1)}, u32[]{:S(2)}, u32[]{:S(2)}) async-start(bf16[4,48,3584]{2,1,0:T(8,128)(2,1)} %bitcast.103), calls=%async_computation.5 | async-start | bytes 2752512 | tf_op jit(solution)/shard_map/all_to_all | solution.py:358
  228.9 43.7 %collective-permute-start.21 = (bf16[128,3584]{1,0:T(8,128)(2,1)}, bf16[128,3584]{1,0:T(8,128)(2,1)}, u32[]{:S(2)}, u32[]{:S(2)}) collective-permute-start(bf16[128,3584]{1,0:T(8,128)(2,1)} %convolution_convert_fusion), channel_id=1, source_target_pairs={{0,8},{1,9},{2,10},{3,11},{4,12},{5,13},{6,14},{7,15},{8,0},{9,1},... | collective-permute-start | bytes 2752520 | tf_op jit(solution)/shard_map/ppermute | solution.py:340
  233.0 30.4 %copy-start.3 = (bf16[256,3584]{1,0:T(8,128)(2,1)S(1)}, bf16[256,3584]{1,0:T(8,128)(2,1)}, u32[]{:S(2)}) copy-start(bf16[256,3584]{1,0:T(8,128)(2,1)} %shard_map.117) | copy-start | bytes 5505028
  (32 other events, 195.9 us)
